TPU v7x, 32 devices: a whole 2x2x4 slice. The times are simulated.
32 devices in a mesh: grp: 2 (over y), blk: 4 (over z), sub: 2 (over x), pair: 2 (over core).
Axes of the slice: x: 2, y: 2, z: 4, core: 2. Of those that a mesh axis runs over, the one named last changes fastest.
Arguments:
- queries: bfloat16 [4096, 2048], P(('grp', 'blk', 'pair', 'sub')), parts along dimension 0, may hold values from -6 to 6
- keys: bfloat16 [4096, 2048], P(('grp', 'blk', 'pair', 'sub')), parts along dimension 0, may hold values from -6 to 6
- values: bfloat16 [4096, 2048], P(('grp', 'blk', 'pair', 'sub')), parts along dimension 0, may hold values from -6 to 6
- out_grad: bfloat16 [4096, 2048], P(('grp', 'blk', 'pair', 'sub')), parts along dimension 0, may hold values from -6 to 6
- session: int32 [4096], P('grp'), parts along dimension 0, may hold values from 0 to 7, never falling along the last dimension, each value on 1 to 512 neighbouring positions
Outputs:
- grad_queries: bfloat16 [4096, 2048], P(('grp', 'blk', 'pair', 'sub')), parts along dimension 0
- grad_keys: bfloat16 [4096, 2048], P(('grp', 'blk', 'pair', 'sub')), parts along dimension 0
- grad_values: bfloat16 [4096, 2048], P(('grp', 'blk', 'pair', 'sub')), parts along dimension 0
There are 2 independent parts, one for each index of `grp`. A program takes and returns all parts, laid end to end along the dimension named above; each array names one. Nothing has to cross between parts.
Inputs may be any that keep to these rules, and one draw needn't show every extreme that they name: Session numbers never fall along the tokens; each session is 1 to 512 tokens long and one is exactly that long.
All inputs are finite; a program needn't handle non-finite values.
Results may differ from a plain program's by a relative error of at most 0.0094.
Values may be sent and summed in bfloat16 or wider, within the bound.
No kernel may reach another device: no remote copies, remote signals or barrier semaphores. Data moves between devices by JAX's collectives and lax.ppermute only.
A program may use at most 64 MiB of HBM per device.

v0:
```python
import jax
import jax.numpy as jnp
from jax import lax
from jax.sharding import PartitionSpec as P

HD = 128
CYCLE = 2


NEG_FILL = -1e30


def passed_along(value, axis, by):
    peers = lax.axis_size(axis)
    pairs = [(i, i + by) for i in range(peers) if 0 <= i + by < peers]
    return lax.ppermute(value, axis, pairs)


def times_transposed(left, right):
    return lax.dot_general(
        left, right, (((1,), (1,)), ((), ())), preferred_element_type=jnp.float32
    )


def transposed_times(left, right):
    return lax.dot_general(
        left, right, (((0,), (0,)), ((), ())), preferred_element_type=jnp.float32
    )


def plain_times(left, right):
    return jnp.dot(left, right, preferred_element_type=jnp.float32)


def score_tile(q_head, k_head, allowed):
    return jnp.where(allowed, times_transposed(q_head, k_head) * HD ** (-0.5), NEG_FILL)


def prob_tile(scores, allowed, log_total):
    prob_full = jnp.where(allowed, jnp.exp(scores - log_total), 0.0)
    return (prob_full, prob_full.astype(jnp.bfloat16))


def score_grad(g_head, v_head, prob_full, row_dot):
    grad_prob = times_transposed(g_head, v_head)
    return (prob_full * (grad_prob - row_dot)).astype(jnp.bfloat16)


def shards(queries, keys, values, out_grad, session):
    q_local, k_local, v_local, g_local = (
        lax.all_to_all(queries, "sub", split_axis=1, concat_axis=0, tiled=True),
        lax.all_to_all(keys, "sub", split_axis=1, concat_axis=0, tiled=True),
        lax.all_to_all(values, "sub", split_axis=1, concat_axis=0, tiled=True),
        lax.all_to_all(out_grad, "sub", split_axis=1, concat_axis=0, tiled=True),
    )
    block_rows = q_local.shape[0]
    local_width = q_local.shape[1]
    local_heads = local_width // HD
    score_scale = HD ** (-0.5)
    position = lax.axis_index(("blk", "pair"))
    start = position * block_rows
    q_place = start + jnp.arange(block_rows, dtype=jnp.int32)
    margin = jnp.zeros((CYCLE * block_rows,), jnp.int32)
    padded_sess = jnp.concatenate([margin, session, margin], axis=0)
    q_sess = lax.dynamic_slice_in_dim(padded_sess, start + CYCLE * block_rows, block_rows)
    k_sess = lax.dynamic_slice_in_dim(padded_sess, start, (CYCLE + 1) * block_rows)
    k_place = start - CYCLE * block_rows + jnp.arange((CYCLE + 1) * block_rows, dtype=jnp.int32)
    held = (k_local, v_local)
    k_parts = [k_local]
    v_parts = [v_local]
    for step in range(CYCLE):
        held = passed_along((held[0], held[1]), ("blk", "pair"), 1)
        k_parts.insert(0, held[0])
        v_parts.insert(0, held[1])
    k_all = jnp.concatenate(k_parts, axis=0)
    v_all = jnp.concatenate(v_parts, axis=0)
    allowed = (q_sess[:, None] == k_sess[None, :]) & (k_place[None, :] <= q_place[:, None])
    allowed = allowed & (k_place[None, :] >= 0)
    grads_q = []
    grads_k = []
    grads_v = []
    for head_index in range(local_heads):
        columns = slice(head_index * HD, (head_index + 1) * HD)
        q_head = q_local[:, columns]
        g_head = g_local[:, columns]
        k_head = k_all[:, columns]
        v_head = v_all[:, columns]
        scores = score_tile(q_head, k_head, allowed)
        row_peak = jnp.max(scores, axis=1, keepdims=True)
        log_total = row_peak + jnp.log(jnp.sum(jnp.exp(scores - row_peak), axis=1, keepdims=True))
        prob_full, prob_low = prob_tile(scores, allowed, log_total)
        output = plain_times(prob_low, v_head)
        row_dot = jnp.sum(g_head.astype(jnp.float32) * output, axis=1, keepdims=True)
        score_low = score_grad(g_head, v_head, prob_full, row_dot)
        grads_q.append(plain_times(score_low, k_head) * score_scale)
        grads_k.append(transposed_times(score_low, q_head) * score_scale)
        grads_v.append(transposed_times(prob_low, g_head))
    grad_q_all = jnp.concatenate(grads_q, axis=1).astype(jnp.bfloat16)
    grad_k_all = jnp.concatenate(grads_k, axis=1)
    grad_v_all = jnp.concatenate(grads_v, axis=1)
    carried = (grad_k_all[:block_rows], grad_v_all[:block_rows])
    for step in range(CYCLE):
        moved = passed_along((carried[0], carried[1]), ("blk", "pair"), -1)
        lower = (step + 1) * block_rows
        upper = (step + 2) * block_rows
        carried = (moved[0] + grad_k_all[lower:upper], moved[1] + grad_v_all[lower:upper])
    grad_k_total, grad_v_total = carried
    grad_k_out = grad_k_total.astype(jnp.bfloat16)
    grad_v_out = grad_v_total.astype(jnp.bfloat16)
    grad_queries, grad_keys, grad_values = (
        lax.all_to_all(grad_q_all, "sub", split_axis=0, concat_axis=1, tiled=True),
        lax.all_to_all(grad_k_out, "sub", split_axis=0, concat_axis=1, tiled=True),
        lax.all_to_all(grad_v_out, "sub", split_axis=0, concat_axis=1, tiled=True),
    )
    return (grad_queries, grad_keys, grad_values)


def solution(mesh):
    in_specs = (
        P(("grp", "blk", "pair", "sub"), None),
        P(("grp", "blk", "pair", "sub"), None),
        P(("grp", "blk", "pair", "sub"), None),
        P(("grp", "blk", "pair", "sub"), None),
        P("grp"),
    )
    out_specs = (
        P(("grp", "blk", "pair", "sub"), None),
        P(("grp", "blk", "pair", "sub"), None),
        P(("grp", "blk", "pair", "sub"), None),
    )
    return jax.shard_map(shards, mesh=mesh, in_specs=in_specs, out_specs=out_specs, check_vma=False)
```

profile of v0, /device:TPU:16, one launch (start us, length us, event | category | flops | bytes accessed | tf_op | source)
XLA Modules:
  0.0 140.5 jit_solution(6186363817421660110)
XLA Ops:
  0.6 2.1 %copy.26 = bf16[128,2048]{0,1:T(8,128)(2,1)} copy(bf16[128,2048]{1,0:T(8,128)(2,1)} %param.6) | data formatting | bytes 1048576 | tf_op args[1]
  2.7 3.5 %all-to-all-start = ((bf16[128,2,1024]{0,2,1:T(8,128)(2,1)}), bf16[128,2,1024]{0,2,1:T(8,128)(2,1)S(1)}, u32[]{:S(2)}, u32[]{:S(2)}) async-start(bf16[128,2,1024]{0,2,1:T(8,128)(2,1)} %bitcast), calls=%async_computation | async-start | bytes 1048576 | tf_op jit(solution)/shard_map/all_to_all | solution.py:52
  6.3 1.0 copy.30
  7.3 7.2 %all-to-all-done = bf16[128,2,1024]{0,2,1:T(8,128)(2,1)S(1)} async-done(((bf16[128,2,1024]{0,2,1:T(8,128)(2,1)}), bf16[128,2,1024]{0,2,1:T(8,128)(2,1)S(1)}, u32[]{:S(2)}, u32[]{:S(2)}) %all-to-all-start) | async-done | bytes 524320 | tf_op jit(solution)/shard_map/all_to_all | solution.py:52
  14.5 3.5 %all-to-all-start.2 = ((bf16[128,2,1024]{0,2,1:T(8,128)(2,1)}), bf16[128,2,1024]{0,2,1:T(8,128)(2,1)S(1)}, u32[]{:S(2)}, u32[]{:S(2)}) async-start(bf16[128,2,1024]{0,2,1:T(8,128)(2,1)} %bitcast.7), calls=%async_computation.2 | async-start | bytes 1048576 | tf_op jit(solution)/shard_map/all_to_all | solution.py:53
  18.2 1.9 %collective-permute-start = (bf16[256,1024]{1,0:T(8,128)(2,1)S(1)}, bf16[256,1024]{1,0:T(8,128)(2,1)S(1)}, u32[]{:S(2)}, u32[]{:S(2)}) collective-permute-start(bf16[256,1024]{1,0:T(8,128)(2,1)S(1)} %bitcast.143), channel_id=1, source_target_pairs={{0,1},{1,4},{4,5},{5,8},{8,9},{9,12},{12,13},{2,3},{3,6},{6,7},{7,... | collective-permute-start | bytes 1572872 | tf_op jit(solution)/shard_map/ppermute | solution.py:16
  20.2 1.0 copy.28
  21.2 4.2 %all-to-all-done.2 = bf16[128,2,1024]{0,2,1:T(8,128)(2,1)S(1)} async-done(((bf16[128,2,1024]{0,2,1:T(8,128)(2,1)}), bf16[128,2,1024]{0,2,1:T(8,128)(2,1)S(1)}, u32[]{:S(2)}, u32[]{:S(2)}) %all-to-all-start.2) | async-done | bytes 524320 | tf_op jit(solution)/shard_map/all_to_all | solution.py:53
  25.3 3.5 %all-to-all-start.1 = ((bf16[128,2,1024]{0,2,1:T(8,128)(2,1)}), bf16[128,2,1024]{0,2,1:T(8,128)(2,1)S(1)}, u32[]{:S(2)}, u32[]{:S(2)}) async-start(bf16[128,2,1024]{0,2,1:T(8,128)(2,1)} %bitcast.3), calls=%async_computation.1 | async-start | bytes 1048576 | tf_op jit(solution)/shard_map/all_to_all | solution.py:51
  28.9 1.0 copy.32
  30.1 1.9 %collective-permute-start.2 = (bf16[256,1024]{1,0:T(8,128)(2,1)S(1)}, bf16[256,1024]{1,0:T(8,128)(2,1)}, u32[]{:S(2)}, u32[]{:S(2)}) collective-permute-start(bf16[256,1024]{1,0:T(8,128)(2,1)S(1)} %bitcast.145), channel_id=1, source_target_pairs={{0,1},{1,4},{4,5},{5,8},{8,9},{9,12},{12,13},{2,3},{3,6},{6,7},{7,... | collective-permute-start | bytes 1572872 | tf_op jit(solution)/shard_map/ppermute | solution.py:16
  32.0 3.6 %collective-permute-start.1 = (bf16[256,1024]{1,0:T(8,128)(2,1)S(1)}, bf16[256,1024]{1,0:T(8,128)(2,1)}, u32[]{:S(2)}, u32[]{:S(2)}) collective-permute-start(bf16[256,1024]{1,0:T(8,128)(2,1)S(1)} %collective-permute-done), channel_id=1, source_target_pairs={{0,1},{1,4},{4,5},{5,8},{8,9},{9,12},{12,13},{2,3},{3,6},{6,7},{7,... | collective-permute-start | bytes 1572872 | tf_op jit(solution)/shard_map/ppermute | solution.py:16
  35.6 3.5 %all-to-all-start.3 = ((bf16[128,2,1024]{0,2,1:T(8,128)(2,1)}), bf16[128,2,1024]{0,2,1:T(8,128)(2,1)S(1)}, u32[]{:S(2)}, u32[]{:S(2)}) async-start(bf16[128,2,1024]{0,2,1:T(8,128)(2,1)} %bitcast.10), calls=%async_computation.3 | async-start | bytes 1048576 | tf_op jit(solution)/shard_map/all_to_all | solution.py:54
  39.6 8.3 %all-to-all-done.3 = bf16[128,2,1024]{0,2,1:T(8,128)(2,1)S(1)} async-done(((bf16[128,2,1024]{0,2,1:T(8,128)(2,1)}), bf16[128,2,1024]{0,2,1:T(8,128)(2,1)S(1)}, u32[]{:S(2)}, u32[]{:S(2)}) %all-to-all-start.3) | async-done | bytes 524320 | tf_op jit(solution)/shard_map/all_to_all | solution.py:54
  47.9 1.9 %collective-permute-start.3 = (bf16[256,1024]{1,0:T(8,128)(2,1)}, bf16[256,1024]{1,0:T(8,128)(2,1)S(1)}, u32[]{:S(2)}, u32[]{:S(2)}) collective-permute-start(bf16[256,1024]{1,0:T(8,128)(2,1)} %collective-permute-done.2), channel_id=1, source_target_pairs={{0,1},{1,4},{4,5},{5,8},{8,9},{9,12},{12,13},{2,3},{3,6},{6,7},{7,... | collective-permute-start | bytes 1572872 | tf_op jit(solution)/shard_map/ppermute | solution.py:16
  49.8 1.2 pad_maximum_fusion
  55.1 3.4 %collective-permute-done.3 = bf16[256,1024]{1,0:T(8,128)(2,1)S(1)} collective-permute-done((bf16[256,1024]{1,0:T(8,128)(2,1)}, bf16[256,1024]{1,0:T(8,128)(2,1)S(1)}, u32[]{:S(2)}, u32[]{:S(2)}) %collective-permute-start.3) | collective-permute-done | bytes 524320 | tf_op jit(solution)/shard_map/ppermute | solution.py:16
  58.6 1.2 pad_maximum_fusion.1
  60.4 1.1 fusion.32
  71.6 1.9 %collective-permute-start.6 = (f32[256,1024]{0,1:T(8,128)S(1)}, f32[256,1024]{0,1:T(8,128)S(1)}, u32[]{:S(2)}, u32[]{:S(2)}) collective-permute-start(f32[256,1024]{0,1:T(8,128)S(1)} %slice.187), channel_id=1, source_target_pairs={{1,0},{4,1},{5,4},{8,5},{9,8},{12,9},{13,12},{3,2},{6,3},{7,6},{10... | collective-permute-start | bytes 3145736 | tf_op jit(solution)/shard_map/ppermute | solution.py:16
  73.5 1.1 fusion.33
  75.2 0.9 fusion.34
  76.1 0.9 fusion.35
  77.9 0.9 fusion.36
  78.8 0.9 fusion.37
  79.7 0.9 fusion.38
  80.5 0.9 fusion.39
  82.7 2.5 %collective-permute-start.4 = (f32[256,1024]{0,1:T(8,128)S(1)}, f32[256,1024]{0,1:T(8,128)S(1)}, u32[]{:S(2)}, u32[]{:S(2)}) collective-permute-start(f32[256,1024]{0,1:T(8,128)S(1)} %slice.184), channel_id=1, source_target_pairs={{1,0},{4,1},{5,4},{8,5},{9,8},{12,9},{13,12},{3,2},{6,3},{7,6},{10... | collective-permute-start | bytes 3145736 | tf_op jit(solution)/shard_map/ppermute | solution.py:16
  86.7 0.6 constant_dynamic-update-slice_fusion.5
  88.3 0.6 constant_dynamic-update-slice_fusion.3
  89.3 1.3 slice_add_fusion.1
  90.5 1.9 %collective-permute-start.7 = (f32[256,1024]{0,1:T(8,128)}, f32[256,1024]{0,1:T(8,128)}, u32[]{:S(2)}, u32[]{:S(2)}) collective-permute-start(f32[256,1024]{0,1:T(8,128)} %slice_add_fusion.1), channel_id=1, source_target_pairs={{1,0},{4,1},{5,4},{8,5},{9,8},{12,9},{13,12},{3,2},{6,3},{7,6},{10... | collective-permute-start | bytes 3145736 | tf_op jit(solution)/shard_map/ppermute | solution.py:16
  92.5 5.0 %collective-permute-done.4 = f32[256,1024]{0,1:T(8,128)S(1)} collective-permute-done((f32[256,1024]{0,1:T(8,128)S(1)}, f32[256,1024]{0,1:T(8,128)S(1)}, u32[]{:S(2)}, u32[]{:S(2)}) %collective-permute-start.4) | collective-permute-done | bytes 1048608 | tf_op jit(solution)/shard_map/ppermute | solution.py:16
  97.4 1.1 slice_add_fusion.3
  98.6 3.8 %collective-permute-start.5 = (f32[256,1024]{0,1:T(8,128)}, f32[256,1024]{0,1:T(8,128)}, u32[]{:S(2)}, u32[]{:S(2)}) collective-permute-start(f32[256,1024]{0,1:T(8,128)} %slice_add_fusion.3), channel_id=1, source_target_pairs={{1,0},{4,1},{5,4},{8,5},{9,8},{12,9},{13,12},{3,2},{6,3},{7,6},{10... | collective-permute-start | bytes 3145736 | tf_op jit(solution)/shard_map/ppermute | solution.py:16
  102.4 0.6 constant_dynamic-update-slice_fusion.2
  104.3 0.6 constant_dynamic-update-slice_fusion
  104.9 4.2 %all-to-all-start.4 = ((bf16[2,128,1024]{2,1,0:T(8,128)(2,1)}), bf16[2,128,1024]{2,1,0:T(8,128)(2,1)}, u32[]{:S(2)}, u32[]{:S(2)}) async-start(bf16[2,128,1024]{2,1,0:T(8,128)(2,1)} %constant_dynamic-update-slice_fusion), calls=%async_computation.4 | async-start | bytes 1048576 | tf_op jit(solution)/shard_map/all_to_all | solution.py:111
  109.1 2.4 %copy_bitcast_fusion.1 = bf16[2,128,1024]{1,2,0:T(8,128)(2,1)} fusion(f32[256,1024]{0,1:T(8,128)} %collective-permute-done.7, f32[768,1024]{0,1:T(8,128)} %copy-done), kind=kLoop, calls=%fused_computation.148 | loop fusion | flops 524288 | bytes 2621440 | tf_op jit(solution)/shard_map/all_to_all | solution.py:113
  111.6 6.0 %all-to-all-done.4 = bf16[2,128,1024]{2,1,0:T(8,128)(2,1)} async-done(((bf16[2,128,1024]{2,1,0:T(8,128)(2,1)}), bf16[2,128,1024]{2,1,0:T(8,128)(2,1)}, u32[]{:S(2)}, u32[]{:S(2)}) %all-to-all-start.4) | async-done | bytes 524320 | tf_op jit(solution)/shard_map/all_to_all | solution.py:111
  117.6 4.2 %all-to-all-start.6 = ((bf16[2,128,1024]{1,2,0:T(8,128)(2,1)}), bf16[2,128,1024]{1,2,0:T(8,128)(2,1)}, u32[]{:S(2)}, u32[]{:S(2)}) async-start(bf16[2,128,1024]{1,2,0:T(8,128)(2,1)} %copy_bitcast_fusion.1), calls=%async_computation.6 | async-start | bytes 1048576 | tf_op jit(solution)/shard_map/all_to_all | solution.py:113
  121.8 2.1 %copy_bitcast_fusion.2 = bf16[2,128,1024]{1,2,0:T(8,128)(2,1)} fusion(f32[256,1024]{0,1:T(8,128)} %collective-permute-done.5, f32[768,1024]{0,1:T(8,128)S(1)} %fusion.40), kind=kLoop, calls=%fused_computation.149 | loop fusion | flops 524288 | bytes 2621440 | tf_op jit(solution)/shard_map/all_to_all | solution.py:112
  123.9 5.5 %all-to-all-done.6 = bf16[2,128,1024]{1,2,0:T(8,128)(2,1)} async-done(((bf16[2,128,1024]{1,2,0:T(8,128)(2,1)}), bf16[2,128,1024]{1,2,0:T(8,128)(2,1)}, u32[]{:S(2)}, u32[]{:S(2)}) %all-to-all-start.6) | async-done | bytes 524320 | tf_op jit(solution)/shard_map/all_to_all | solution.py:113
  129.4 3.5 %all-to-all-start.5 = ((bf16[2,128,1024]{1,2,0:T(8,128)(2,1)}), bf16[2,128,1024]{1,2,0:T(8,128)(2,1)S(1)}, u32[]{:S(2)}, u32[]{:S(2)}) async-start(bf16[2,128,1024]{1,2,0:T(8,128)(2,1)} %copy_bitcast_fusion.2), calls=%async_computation.5 | async-start | bytes 1048576 | tf_op jit(solution)/shard_map/all_to_all | solution.py:112
  132.9 1.9 %copy.42 = bf16[2,16,8,1024]{3,2,0,1:T(8,128)(2,1)} copy(bf16[2,16,8,1024]{3,2,1,0:T(8,128)(2,1)} %bitcast.48) | data formatting | bytes 1048576 | tf_op jit(solution)/shard_map/all_to_all | solution.py:111
  134.8 2.0 %copy.38 = bf16[128,2048]{1,0:T(8,128)(2,1)} copy(bf16[128,2048]{0,1:T(8,128)(2,1)} %bitcast.39) | data formatting | bytes 1048576
  136.8 2.7 %all-to-all-done.5 = bf16[2,128,1024]{1,2,0:T(8,128)(2,1)S(1)} async-done(((bf16[2,128,1024]{1,2,0:T(8,128)(2,1)}), bf16[2,128,1024]{1,2,0:T(8,128)(2,1)S(1)}, u32[]{:S(2)}, u32[]{:S(2)}) %all-to-all-start.5) | async-done | bytes 524320 | tf_op jit(solution)/shard_map/all_to_all | solution.py:112
  139.5 1.0 copy.37
  (94 shorter events, 22.6 us)
Async XLA Ops:
  0.6 5.6 %copy-start.3 = (bf16[128,2048]{1,0:T(8,128)(2,1)S(1)}, bf16[128,2048]{1,0:T(8,128)(2,1)}, u32[]{:S(2)}) copy-start(bf16[128,2048]{1,0:T(8,128)(2,1)} %param.7) | copy-start | bytes 1572868
  2.7 11.7 %all-to-all-start = ((bf16[128,2,1024]{0,2,1:T(8,128)(2,1)}), bf16[128,2,1024]{0,2,1:T(8,128)(2,1)S(1)}, u32[]{:S(2)}, u32[]{:S(2)}) async-start(bf16[128,2,1024]{0,2,1:T(8,128)(2,1)} %bitcast), calls=%async_computation | async-start | bytes 1048576 | tf_op jit(solution)/shard_map/all_to_all | solution.py:52
  6.2 13.9 %copy-start.4 = (bf16[128,2048]{1,0:T(8,128)(2,1)S(1)}, bf16[128,2048]{1,0:T(8,128)(2,1)}, u32[]{:S(2)}) copy-start(bf16[128,2048]{1,0:T(8,128)(2,1)} %param.5) | copy-start | bytes 1572868
  14.5 10.9 %all-to-all-start.2 = ((bf16[128,2,1024]{0,2,1:T(8,128)(2,1)}), bf16[128,2,1024]{0,2,1:T(8,128)(2,1)S(1)}, u32[]{:S(2)}, u32[]{:S(2)}) async-start(bf16[128,2,1024]{0,2,1:T(8,128)(2,1)} %bitcast.7), calls=%async_computation.2 | async-start | bytes 1048576 | tf_op jit(solution)/shard_map/all_to_all | solution.py:53
  18.0 10.9 %copy-start.5 = (bf16[128,2048]{1,0:T(8,128)(2,1)S(1)}, bf16[128,2048]{1,0:T(8,128)(2,1)}, u32[]{:S(2)}) copy-start(bf16[128,2048]{1,0:T(8,128)(2,1)} %param.8) | copy-start | bytes 1572868
  18.2 11.7 %copy-start.6 = (s32[2048]{0:T(1024)S(1)}, s32[2048]{0:T(1024)}, u32[]{:S(2)}) copy-start(s32[2048]{0:T(1024)} %param.9) | copy-start | bytes 24580
  18.2 13.8 %collective-permute-start = (bf16[256,1024]{1,0:T(8,128)(2,1)S(1)}, bf16[256,1024]{1,0:T(8,128)(2,1)S(1)}, u32[]{:S(2)}, u32[]{:S(2)}) collective-permute-start(bf16[256,1024]{1,0:T(8,128)(2,1)S(1)} %bitcast.143), channel_id=1, source_target_pairs={{0,1},{1,4},{4,5},{5,8},{8,9},{9,12},{12,13},{2,3},{3,6},{6,7},{7,... | collective-permute-start | bytes 1572872 | tf_op jit(solution)/shard_map/ppermute | solution.py:16
  25.3 10.3 %all-to-all-start.1 = ((bf16[128,2,1024]{0,2,1:T(8,128)(2,1)}), bf16[128,2,1024]{0,2,1:T(8,128)(2,1)S(1)}, u32[]{:S(2)}, u32[]{:S(2)}) async-start(bf16[128,2,1024]{0,2,1:T(8,128)(2,1)} %bitcast.3), calls=%async_computation.1 | async-start | bytes 1048576 | tf_op jit(solution)/shard_map/all_to_all | solution.py:51
  30.1 17.8 %collective-permute-start.2 = (bf16[256,1024]{1,0:T(8,128)(2,1)S(1)}, bf16[256,1024]{1,0:T(8,128)(2,1)}, u32[]{:S(2)}, u32[]{:S(2)}) collective-permute-start(bf16[256,1024]{1,0:T(8,128)(2,1)S(1)} %bitcast.145), channel_id=1, source_target_pairs={{0,1},{1,4},{4,5},{5,8},{8,9},{9,12},{12,13},{2,3},{3,6},{6,7},{7,... | collective-permute-start | bytes 1572872 | tf_op jit(solution)/shard_map/ppermute | solution.py:16
  32.0 17.8 %collective-permute-start.1 = (bf16[256,1024]{1,0:T(8,128)(2,1)S(1)}, bf16[256,1024]{1,0:T(8,128)(2,1)}, u32[]{:S(2)}, u32[]{:S(2)}) collective-permute-start(bf16[256,1024]{1,0:T(8,128)(2,1)S(1)} %collective-permute-done), channel_id=1, source_target_pairs={{0,1},{1,4},{4,5},{5,8},{8,9},{9,12},{12,13},{2,3},{3,6},{6,7},{7,... | collective-permute-start | bytes 1572872 | tf_op jit(solution)/shard_map/ppermute | solution.py:16
  35.6 12.2 %all-to-all-start.3 = ((bf16[128,2,1024]{0,2,1:T(8,128)(2,1)}), bf16[128,2,1024]{0,2,1:T(8,128)(2,1)S(1)}, u32[]{:S(2)}, u32[]{:S(2)}) async-start(bf16[128,2,1024]{0,2,1:T(8,128)(2,1)} %bitcast.10), calls=%async_computation.3 | async-start | bytes 1048576 | tf_op jit(solution)/shard_map/all_to_all | solution.py:54
  39.5 14.6 %copy-start.1 = (bf16[2,128,1024]{2,1,0:T(8,128)(2,1)}, bf16[2,128,1024]{2,1,0:T(8,128)(2,1)S(1)}, u32[]{:S(2)}) copy-start(bf16[2,128,1024]{2,1,0:T(8,128)(2,1)S(1)} %copy.29) | copy-start | bytes 1572868
  47.9 10.7 %collective-permute-start.3 = (bf16[256,1024]{1,0:T(8,128)(2,1)}, bf16[256,1024]{1,0:T(8,128)(2,1)S(1)}, u32[]{:S(2)}, u32[]{:S(2)}) collective-permute-start(bf16[256,1024]{1,0:T(8,128)(2,1)} %collective-permute-done.2), channel_id=1, source_target_pairs={{0,1},{1,4},{4,5},{5,8},{8,9},{9,12},{12,13},{2,3},{3,6},{6,7},{7,... | collective-permute-start | bytes 1572872 | tf_op jit(solution)/shard_map/ppermute | solution.py:16
  60.4 1.1 copy-start.2
  71.5 17.7 %copy-start = (f32[768,1024]{0,1:T(8,128)}, f32[768,1024]{0,1:T(8,128)S(1)}, u32[]{:S(2)}) copy-start(f32[768,1024]{0,1:T(8,128)S(1)} %convolution_dynamic-update-slice_fusion) | copy-start | bytes 9437188
  71.6 17.7 %collective-permute-start.6 = (f32[256,1024]{0,1:T(8,128)S(1)}, f32[256,1024]{0,1:T(8,128)S(1)}, u32[]{:S(2)}, u32[]{:S(2)}) collective-permute-start(f32[256,1024]{0,1:T(8,128)S(1)} %slice.187), channel_id=1, source_target_pairs={{1,0},{4,1},{5,4},{8,5},{9,8},{12,9},{13,12},{3,2},{6,3},{7,6},{10... | collective-permute-start | bytes 3145736 | tf_op jit(solution)/shard_map/ppermute | solution.py:16
  82.7 14.8 %collective-permute-start.4 = (f32[256,1024]{0,1:T(8,128)S(1)}, f32[256,1024]{0,1:T(8,128)S(1)}, u32[]{:S(2)}, u32[]{:S(2)}) collective-permute-start(f32[256,1024]{0,1:T(8,128)S(1)} %slice.184), channel_id=1, source_target_pairs={{1,0},{4,1},{5,4},{8,5},{9,8},{12,9},{13,12},{3,2},{6,3},{7,6},{10... | collective-permute-start | bytes 3145736 | tf_op jit(solution)/shard_map/ppermute | solution.py:16
  90.5 18.6 %collective-permute-start.7 = (f32[256,1024]{0,1:T(8,128)}, f32[256,1024]{0,1:T(8,128)}, u32[]{:S(2)}, u32[]{:S(2)}) collective-permute-start(f32[256,1024]{0,1:T(8,128)} %slice_add_fusion.1), channel_id=1, source_target_pairs={{1,0},{4,1},{5,4},{8,5},{9,8},{12,9},{13,12},{3,2},{6,3},{7,6},{10... | collective-permute-start | bytes 3145736 | tf_op jit(solution)/shard_map/ppermute | solution.py:16
  98.6 23.3 %collective-permute-start.5 = (f32[256,1024]{0,1:T(8,128)}, f32[256,1024]{0,1:T(8,128)}, u32[]{:S(2)}, u32[]{:S(2)}) collective-permute-start(f32[256,1024]{0,1:T(8,128)} %slice_add_fusion.3), channel_id=1, source_target_pairs={{1,0},{4,1},{5,4},{8,5},{9,8},{12,9},{13,12},{3,2},{6,3},{7,6},{10... | collective-permute-start | bytes 3145736 | tf_op jit(solution)/shard_map/ppermute | solution.py:16
  104.9 12.7 %all-to-all-start.4 = ((bf16[2,128,1024]{2,1,0:T(8,128)(2,1)}), bf16[2,128,1024]{2,1,0:T(8,128)(2,1)}, u32[]{:S(2)}, u32[]{:S(2)}) async-start(bf16[2,128,1024]{2,1,0:T(8,128)(2,1)} %constant_dynamic-update-slice_fusion), calls=%async_computation.4 | async-start | bytes 1048576 | tf_op jit(solution)/shard_map/all_to_all | solution.py:111
  117.6 11.8 %all-to-all-start.6 = ((bf16[2,128,1024]{1,2,0:T(8,128)(2,1)}), bf16[2,128,1024]{1,2,0:T(8,128)(2,1)}, u32[]{:S(2)}, u32[]{:S(2)}) async-start(bf16[2,128,1024]{1,2,0:T(8,128)(2,1)} %copy_bitcast_fusion.1), calls=%async_computation.6 | async-start | bytes 1048576 | tf_op jit(solution)/shard_map/all_to_all | solution.py:113
  129.4 10.1 %all-to-all-start.5 = ((bf16[2,128,1024]{1,2,0:T(8,128)(2,1)}), bf16[2,128,1024]{1,2,0:T(8,128)(2,1)S(1)}, u32[]{:S(2)}, u32[]{:S(2)}) async-start(bf16[2,128,1024]{1,2,0:T(8,128)(2,1)} %copy_bitcast_fusion.2), calls=%async_computation.5 | async-start | bytes 1048576 | tf_op jit(solution)/shard_map/all_to_all | solution.py:112
where the time goes:
time: 142 us; the launch traced here: 140 us
  starting transfers between devices  45.3 us (32%)
  waiting for transfers between devices  42.2 us (30%)
  matrix products  24.9 us (18%)
  local copies, waits for them, and re-layouts  16.1 us (11%)
  other arithmetic  10.7 us (8%)
    ppermute x8, starting transfers between devices, passed_along(): return lax.ppermute(value, axis, pairs)  19.4 us
    unnamed x27, local copies, waits for them, and re-layouts  12.6 us
    dot_general x16, matrix products, times_transposed(): lax.dot_general(left, right, (((1,), (1,)), ((), ())), preferred_element_...  10.8 us
    ppermute x8, waiting for transfers between devices, passed_along(): return lax.ppermute(value, axis, pairs)  8.44 us
    all_to_all x1, waiting for transfers between devices, shards(): lax.all_to_all(out_grad, 'sub', split_axis=1, concat_axis=0, tiled=True)  8.26 us
    dot_general x16, matrix products, plain_times(): return jnp.dot(left, right, preferred_element_type=jnp.float32)  7.44 us
    all_to_all x1, waiting for transfers between devices, shards(): lax.all_to_all(keys, 'sub', split_axis=1, concat_axis=0, tiled=True)  7.21 us
    dot_general x16, matrix products, transposed_times(): lax.dot_general(left, right, (((0,), (0,)), ((), ())), preferred_element_...  6.69 us
  transfers between devices with their start and end apart: 15, of which 8 were waited for; matrix products, arithmetic and copies ran while one was open for 25% of the time, Pallas kernels for 0%

commit v1 on v0

v1 whole, which is shorter than its diff:
```python
import math

import jax
import jax.numpy as jnp
from jax import lax
from jax.experimental import pallas as pl
from jax.experimental.pallas import tpu as pltpu
from jax.sharding import PartitionSpec as P

HD = 128
CHUNKS = 2
NEG_FILL = -1e30
LOW = jnp.bfloat16
WIDE = jnp.float32
ROOM = 48 * 1024 * 1024


def along_blocks(value, by):
    peers = lax.axis_size("blk")
    pairs = [(i, i + by) for i in range(peers) if 0 <= i + by < peers]
    return lax.ppermute(value, "blk", pairs)


def round_sub(value, by):
    peers = lax.axis_size("sub")
    return lax.ppermute(value, "sub", [(i, (i + by) % peers) for i in range(peers)])


def swapped(value):
    return lax.ppermute(value, "pair", [(0, 1), (1, 0)])


def run_moves(moves, sems):
    copies = [pltpu.make_async_copy(src, dst, sems.at[at]) for at, (src, dst) in enumerate(moves)]
    for copy in copies:
        copy.start()
    for copy in copies:
        copy.wait()


def anywhere(count):
    return [pl.BlockSpec(memory_space=pl.ANY)] * count


def call(kernel, ins, outs, scratch, name, whole=False, flops=0):
    spec = (lambda n: [pl.BlockSpec(memory_space=pltpu.VMEM)] * n) if whole else anywhere
    moved = sum(math.prod(a.shape) * a.dtype.itemsize for a in list(ins) + list(outs))
    return pl.pallas_call(
        kernel,
        out_shape=outs,
        in_specs=spec(len(ins)),
        out_specs=spec(len(outs)),
        scratch_shapes=scratch,
        name=name,
        cost_estimate=pl.CostEstimate(flops=flops, bytes_accessed=moved, transcendentals=0),
        compiler_params=pltpu.CompilerParams(vmem_limit_bytes=ROOM),
    )(*ins)


def pair_part(arrays):
    count = len(arrays)
    rows, width = arrays[0].shape
    half = width // 2

    def kernel(*refs):
        ins, out, sems = refs[:count], refs[count], refs[count + 1]
        start = pl.multiple_of((1 - lax.axis_index("pair")) * half, half)
        run_moves([(ref.at[:, pl.ds(start, half)], out.at[i]) for i, ref in enumerate(ins)], sems)

    outs = [jax.ShapeDtypeStruct((count, rows, half), LOW)]
    return call(kernel, arrays, outs, [pltpu.SemaphoreType.DMA((count,))], "pair_part")[0]


def head_parts(arrays, received, chunk):
    count = len(arrays)
    rows, width = arrays[0].shape
    half = width // 2
    peers = lax.axis_size("sub")
    part = half // peers
    cut = part // CHUNKS

    def kernel(*refs):
        ins, rec, outs, sems = refs[:count], refs[count], refs[count + 1:-1], refs[-1]
        p, s = lax.axis_index("pair"), lax.axis_index("sub")
        moves = []
        for by, out in enumerate(outs):
            base = lax.rem(s + by, peers) * part + chunk * cut
            here = pl.multiple_of(p * half + base, cut)
            there = pl.multiple_of(base, cut)
            moves += [(ref.at[:, pl.ds(here, cut)], out.at[i, p]) for i, ref in enumerate(ins)]
            moves.append((rec.at[:, :, pl.ds(there, cut)], out.at[:, 1 - p]))
        run_moves(moves, sems)

    outs = [jax.ShapeDtypeStruct((count, 2, rows, cut), LOW)] * peers
    scratch = [pltpu.SemaphoreType.DMA((peers * (count + 1),))]
    return call(kernel, list(arrays) + [received], outs, scratch, "head_parts")


def attention_grads(bias, kv, kv_earlier, qg):
    peers = len(kv)
    _, _, rows, cut = kv[0].shape
    heads = cut // HD
    strip = rows * peers
    scale = HD ** (-0.5)
    to_bits = scale / math.log(2.0)

    def kernel(*refs):
        bias_ref = refs[0]
        kv_in, early_in, qg_in = refs[1:1 + peers], refs[1 + peers:1 + 2 * peers], refs[1 + 2 * peers:1 + 3 * peers]
        outs = refs[1 + 3 * peers:1 + 6 * peers]
        early_out, kv_out, dq_out = outs[:peers], outs[peers:2 * peers], outs[2 * peers:]
        bias_held, kv_all, qg_all, grads, early_low, dq_all, sems = refs[1 + 6 * peers:]
        s = lax.axis_index("sub")
        moves = [(bias_ref, bias_held)]
        for by in range(peers):
            at = lax.rem(s - by + peers, peers)
            moves += [
                (early_in[by], kv_all.at[:, 0:2, at]),
                (kv_in[by], kv_all.at[:, 2:4, at]),
                (qg_in[by], qg_all.at[:, :, at]),
            ]
        run_moves(moves, sems)
        for head in range(heads):
            columns = pl.ds(head * HD, HD)
            for tile in range(2):
                span = 3 * strip
                q = qg_all[0, tile, :, :, columns].reshape(strip, HD)
                g = qg_all[1, tile, :, :, columns].reshape(strip, HD)
                k = kv_all[0, tile:tile + 3, :, :, columns].reshape(span, HD)
                v = kv_all[1, tile:tile + 3, :, :, columns].reshape(span, HD)
                rows_by_rows = (((1,), (1,)), ((), ()))
                scores = lax.dot_general(k, q, rows_by_rows, preferred_element_type=WIDE) * to_bits + bias_held[tile]
                peak = jnp.max(scores, axis=0, keepdims=True)
                weight = jnp.exp2(scores - peak)
                prob = weight * (1.0 / jnp.sum(weight, axis=0, keepdims=True))
                prob_low = prob.astype(LOW)
                grad_prob = lax.dot_general(v, g, rows_by_rows, preferred_element_type=WIDE)
                row_dot = jnp.sum(prob_low.astype(WIDE) * grad_prob, axis=0, keepdims=True)
                score_low = (prob * (grad_prob - row_dot)).astype(LOW)
                dq = jnp.dot(k.T, score_low, preferred_element_type=WIDE) * scale
                dq_all[tile, :, :, columns] = dq.T.astype(LOW).reshape(peers, rows, HD)
                dk = jnp.dot(score_low, q, preferred_element_type=WIDE) * scale
                dv = jnp.dot(prob_low, g, preferred_element_type=WIDE)
                for which, term in ((0, dk), (1, dv)):
                    term = term.reshape(3, peers, rows, HD)
                    if tile == 0:
                        grads[which, 0:3, :, :, columns] = term
                    else:
                        grads[which, 1:3, :, :, columns] += term[0:2]
                        grads[which, 3:4, :, :, columns] = term[2:3]
        early_low[...] = grads[:, 0:2].astype(LOW)
        moves = []
        for by in range(peers):
            at = lax.rem(s + by, peers)
            moves += [
                (early_low.at[:, :, at], early_out[by]),
                (grads.at[:, 2:4, at], kv_out[by]),
                (dq_all.at[:, at], dq_out[by]),
            ]
        run_moves(moves, sems)

    outs = (
        [jax.ShapeDtypeStruct((2, 2, rows, cut), LOW)] * peers
        + [jax.ShapeDtypeStruct((2, 2, rows, cut), WIDE)] * peers
        + [jax.ShapeDtypeStruct((2, rows, cut), LOW)] * peers
    )
    scratch = [
        pltpu.VMEM(bias.shape, WIDE),
        pltpu.VMEM((2, 4, peers, rows, cut), LOW),
        pltpu.VMEM((2, 2, peers, rows, cut), LOW),
        pltpu.VMEM((2, 4, peers, rows, cut), WIDE),
        pltpu.VMEM((2, 2, peers, rows, cut), LOW),
        pltpu.VMEM((2, peers, rows, cut), LOW),
        pltpu.SemaphoreType.DMA((1 + 3 * peers,)),
    ]
    flops = heads * 2 * 5 * 2 * strip * 3 * strip * HD
    outs = call(kernel, [bias] + list(kv) + list(kv_earlier) + list(qg), outs, scratch, "attention_grads", flops=flops)
    return outs[:peers], outs[peers:2 * peers], outs[2 * peers:]


def summed(dq, own, later):
    _, rows, cut = dq.shape

    def kernel(dq_ref, own_ref, later_ref, out):
        out[0] = dq_ref[...]
        out[1:3] = (own_ref[...] + later_ref[...].astype(WIDE)).astype(LOW)

    outs = [jax.ShapeDtypeStruct((3, 2, rows, cut), LOW)]
    return call(kernel, [dq, own, later], outs, [], "summed", whole=True)[0]


def rows_for_pair(dq, own, later, received):
    peers = len(received) + 1
    _, rows, cut = dq.shape

    def kernel(dq_ref, own_ref, later_ref, *refs):
        rec, (send, keep) = refs[:peers - 1], refs[peers - 1:]
        p, s = lax.axis_index("pair"), lax.axis_index("sub")
        for out, row in ((send, 1 - p), (keep, p)):
            out[0, s] = dq_ref[row]
            for which in range(2):
                out[1 + which, s] = (own_ref[which, row] + later_ref[which, row].astype(WIDE)).astype(LOW)
            for by in range(1, peers):
                at = lax.rem(s - by + peers, peers)
                for which in range(3):
                    out[which, at] = rec[by - 1][which, row]

    outs = [jax.ShapeDtypeStruct((3, peers, rows, cut), LOW)] * 2
    return call(kernel, [dq, own, later] + list(received), outs, [], "rows_for_pair", whole=True)


def laid_out(kept, received):
    _, peers, rows, cut = kept[0].shape
    part = cut * CHUNKS
    half = part * peers

    def kernel(*refs):
        keep, rec, outs, sems = refs[:CHUNKS], refs[CHUNKS:2 * CHUNKS], refs[2 * CHUNKS:-1], refs[-1]
        p = lax.axis_index("pair")
        moves = []
        for chunk in range(CHUNKS):
            for source, side in ((keep[chunk], p), (rec[chunk], 1 - p)):
                for at in range(peers):
                    start = pl.multiple_of(side * half + at * part + chunk * cut, cut)
                    moves += [(source.at[which, at], out.at[:, pl.ds(start, cut)]) for which, out in enumerate(outs)]
        run_moves(moves, sems)

    outs = [jax.ShapeDtypeStruct((rows, 2 * half), LOW)] * 3
    return call(kernel, list(kept) + list(received), outs, [pltpu.SemaphoreType.DMA((6 * CHUNKS * peers,))], "laid_out")


def allowed_bias(session, rows):
    peers = lax.axis_size("sub")
    strip = rows * peers
    block = 2 * strip
    start = lax.axis_index("blk") * block
    padded = jnp.concatenate([jnp.zeros((block,), jnp.int32), session])
    sess = lax.dynamic_slice_in_dim(padded, start, 2 * block)
    place = start - block + jnp.arange(2 * block, dtype=jnp.int32)
    tiles = []
    for tile in range(2):
        q_at = slice(block + tile * strip, block + (tile + 1) * strip)
        k_at = slice(tile * strip, (tile + 3) * strip)
        allowed = (sess[None, q_at] == sess[k_at, None]) & (place[k_at, None] <= place[None, q_at])
        tiles.append(jnp.where(allowed & (place[k_at, None] >= 0), 0.0, NEG_FILL))
    return jnp.stack(tiles)


def shards(queries, keys, values, out_grad, session):
    peers = lax.axis_size("sub")
    kv_pair = swapped(pair_part([keys, values]))
    qg_pair = swapped(pair_part([queries, out_grad]))
    bias = allowed_bias(session, queries.shape[0])
    kept, paired = [], []
    for chunk in range(CHUNKS):
        kv = head_parts([keys, values], kv_pair, chunk)
        kv = [kv[0]] + [round_sub(kv[by], by) for by in range(1, peers)]
        kv_earlier = [along_blocks(value, 1) for value in kv]
        qg = head_parts([queries, out_grad], qg_pair, chunk)
        qg = [qg[0]] + [round_sub(qg[by], by) for by in range(1, peers)]
        early, own, dq = attention_grads(bias, kv, kv_earlier, qg)
        later = [along_blocks(early[by], -1) for by in list(range(1, peers)) + [0]]
        received = []
        for by in range(1, peers):
            received.append(round_sub(summed(dq[by], own[by], later[by - 1]), by))
        send, keep = rows_for_pair(dq[0], own[0], later[-1], received)
        kept.append(keep)
        paired.append(swapped(send))
    return tuple(laid_out(kept, paired))


def solution(mesh):
    spread = P(("grp", "blk", "pair", "sub"), None)
    return jax.shard_map(
        shards, mesh=mesh, in_specs=(spread,) * 4 + (P("grp"),), out_specs=(spread,) * 3, check_vma=False
    )
```

time: 142 us -> 66.5 us (0.47)
  the two profiles are of different devices: /device:TPU:16 before, /device:TPU:0 now
where the time goes in v1:
time: 66.5 us; the launch traced here: 66 us
  starting transfers between devices  26.7 us (40%)
  waiting for transfers between devices  22.2 us (33%)
  Pallas kernels  11.9 us (18%)
  local copies, waits for them, and re-layouts  3.45 us (5%)
  between operations  0.93 us (1%)
  other arithmetic  0.79 us (1%)
    ppermute x8, waiting for transfers between devices, along_blocks(): return lax.ppermute(value, 'blk', pairs)  20.1 us
    ppermute x8, starting transfers between devices, along_blocks(): return lax.ppermute(value, 'blk', pairs)  19.2 us
    pallas_call x13, Pallas kernels, call(): pl.pallas_call(kernel, out_shape=outs, in_specs=spec(len(ins)), out_specs...  11.9 us
    ppermute x6, starting transfers between devices, round_sub(): lax.ppermute(value, 'sub', [(i, (i + by) % peers) for i in range(peers)])  6.48 us
    unnamed x16, local copies, waits for them, and re-layouts  3.36 us
    ppermute x4, waiting for transfers between devices, swapped(): return lax.ppermute(value, 'pair', [(0, 1), (1, 0)])  1.71 us
  transfers between devices with their start and end apart: 18, of which 7 were waited for; matrix products, arithmetic and copies ran while one was open for 1% of the time, Pallas kernels for 15%

profile of v1, /device:TPU:0, one launch (start us, length us, event | category | flops | bytes accessed | tf_op | source)
XLA Modules:
  0.0 66.0 jit_solution(14727811020469751933)
XLA Ops:
  0.6 1.0 %copy-done = bf16[128,2048]{1,0:T(8,128)(2,1)S(1)} copy-done((bf16[128,2048]{1,0:T(8,128)(2,1)S(1)}, bf16[128,2048]{1,0:T(8,128)(2,1)}, u32[]{:S(2)}) %copy-start) | copy-done | bytes 524312
  1.7 1.0 %copy-done.2 = bf16[128,2048]{1,0:T(8,128)(2,1)S(1)} copy-done((bf16[128,2048]{1,0:T(8,128)(2,1)S(1)}, bf16[128,2048]{1,0:T(8,128)(2,1)}, u32[]{:S(2)}) %copy-start.2) | copy-done | bytes 524312
  2.7 0.8 %pair_part.2 = bf16[2,128,1024]{2,1,0:T(8,128)(2,1)} custom-call(bf16[128,2048]{1,0:T(8,128)(2,1)S(1)} %copy-done, bf16[128,2048]{1,0:T(8,128)(2,1)S(1)} %copy-done.2), custom_call_target="tpu_custom_call" | custom-call | bytes 1572864 | tf_op jit(solution)/shard_map/pair_part/pallas_call | solution.py:48
  3.5 0.5 collective-permute-start
  4.1 1.0 %copy-done.5 = bf16[128,2048]{1,0:T(8,128)(2,1)S(1)} copy-done((bf16[128,2048]{1,0:T(8,128)(2,1)S(1)}, bf16[128,2048]{1,0:T(8,128)(2,1)}, u32[]{:S(2)}) %copy-start.5) | copy-done | bytes 524312
  5.1 0.1 pair_part.3
  5.2 0.4 collective-permute-start.4
  5.6 0.2 copy-done.7
  5.8 0.1 pad_dynamic-slice_fusion
  5.9 0.0 copy-start.6
  5.9 0.0 collective-permute-done.refs_2_
  5.9 0.2 head_parts.6
  6.1 2.9 %collective-permute-start.9 = (bf16[2,2,128,256]{3,2,1,0:T(8,128)(2,1)S(1)}, bf16[2,2,128,256]{3,2,1,0:T(8,128)(2,1)S(1)}, u32[]{:S(2)}, u32[]{:S(2)}) collective-permute-start(bf16[2,2,128,256]{3,2,1,0:T(8,128)(2,1)S(1)} %get-tuple-element.39), channel_id=1, source_target_pairs={{0,2},{2,0},{1,3},{3,1},{4,6},{6,4},{5,7},{7,5},{8,10},{10,8},{9,1... | collective-permute-start | bytes 786440 | tf_op jit(solution)/shard_map/ppermute | solution.py:26
  9.0 3.5 %collective-permute-start.10 = (bf16[2,2,128,256]{3,2,1,0:T(8,128)(2,1)S(1)}, bf16[2,2,128,256]{3,2,1,0:T(8,128)(2,1)S(1)}, u32[]{:S(2)}, u32[]{:S(2)}) collective-permute-start(bf16[2,2,128,256]{3,2,1,0:T(8,128)(2,1)S(1)} %get-tuple-element.38.refs_1_), channel_id=1, source_target_pairs={{0,4},{4,8},{8,12},{1,5},{5,9},{9,13},{2,6},{6,10},{10,14},{3,7},{... | collective-permute-start | bytes 786440 | tf_op jit(solution)/shard_map/ppermute | solution.py:21
  12.5 0.2 head_parts.4
  12.7 0.6 collective-permute-start.1
  13.3 0.0 collective-permute-done.4.refs_2_
  13.3 0.2 head_parts.7
  13.5 1.6 %collective-permute-start.12 = (bf16[2,2,128,256]{3,2,1,0:T(8,128)(2,1)S(1)}, bf16[2,2,128,256]{3,2,1,0:T(8,128)(2,1)S(1)}, u32[]{:S(2)}, u32[]{:S(2)}) collective-permute-start(bf16[2,2,128,256]{3,2,1,0:T(8,128)(2,1)S(1)} %get-tuple-element.41), channel_id=1, source_target_pairs={{0,2},{2,0},{1,3},{3,1},{4,6},{6,4},{5,7},{7,5},{8,10},{10,8},{9,1... | collective-permute-start | bytes 786440 | tf_op jit(solution)/shard_map/ppermute | solution.py:26
  15.0 3.5 %collective-permute-start.2 = (bf16[2,2,128,256]{3,2,1,0:T(8,128)(2,1)S(1)}, bf16[2,2,128,256]{3,2,1,0:T(8,128)(2,1)S(1)}, u32[]{:S(2)}, u32[]{:S(2)}) collective-permute-start(bf16[2,2,128,256]{3,2,1,0:T(8,128)(2,1)S(1)} %get-tuple-element.27.refs_1_), channel_id=1, source_target_pairs={{0,4},{4,8},{8,12},{1,5},{5,9},{9,13},{2,6},{6,10},{10,14},{3,7},{... | collective-permute-start | bytes 786440 | tf_op jit(solution)/shard_map/ppermute | solution.py:21
  18.5 0.2 head_parts.5
  18.7 0.6 collective-permute-start.5
  19.3 3.6 %collective-permute-start.11 = (bf16[2,2,128,256]{3,2,1,0:T(8,128)(2,1)S(1)}, bf16[2,2,128,256]{3,2,1,0:T(8,128)(2,1)S(1)}, u32[]{:S(2)}, u32[]{:S(2)}) collective-permute-start(bf16[2,2,128,256]{3,2,1,0:T(8,128)(2,1)S(1)} %collective-permute-done.9.refs_2_), channel_id=1, source_target_pairs={{0,4},{4,8},{8,12},{1,5},{5,9},{9,13},{2,6},{6,10},{10,14},{3,7},{... | collective-permute-start | bytes 786440 | tf_op jit(solution)/shard_map/ppermute | solution.py:21
  22.9 3.5 %collective-permute-start.3 = (bf16[2,2,128,256]{3,2,1,0:T(8,128)(2,1)S(1)}, bf16[2,2,128,256]{3,2,1,0:T(8,128)(2,1)S(1)}, u32[]{:S(2)}, u32[]{:S(2)}) collective-permute-start(bf16[2,2,128,256]{3,2,1,0:T(8,128)(2,1)S(1)} %collective-permute-done.1.refs_2_), channel_id=1, source_target_pairs={{0,4},{4,8},{8,12},{1,5},{5,9},{9,13},{2,6},{6,10},{10,14},{3,7},{... | collective-permute-start | bytes 786440 | tf_op jit(solution)/shard_map/ppermute | solution.py:21
  26.4 0.7 %and_select_fusion = (f32[1,768,256]{2,1,0:T(8,128)S(1)}, f32[1,768,256]{2,1,0:T(8,128)S(1)}) fusion(s32[256]{0:T(256)S(1)} %get-tuple-element.60, s32[256]{0:T(256)S(1)} %get-tuple-element.58, s32[768]{0:T(1024)S(1)} %get-tuple-element.56, s32[768]{0:T(1024)S(1)} %get-tuple-element.54, pred[768]{0:T(1024)(128)(4,1)S(1)} %get-tuple-element.52, ...), kind=kLoop, calls=%fused_computation.1 | loop fusion | flops 1966080 | bytes 1590784 | tf_op jit(solution)/shard_map/jit(_where)/select_n | solution.py:245
  27.1 0.1 pad_maximum_fusion.refs_0_
  27.2 0.4 collective-permute-done.12.refs_6_
  27.6 3.2 %collective-permute-done.11.refs_4_ = bf16[2,2,128,256]{3,2,1,0:T(8,128)(2,1)S(1)} collective-permute-done((bf16[2,2,128,256]{3,2,1,0:T(8,128)(2,1)S(1)}, bf16[2,2,128,256]{3,2,1,0:T(8,128)(2,1)S(1)}, u32[]{:S(2)}, u32[]{:S(2)}) %collective-permute-start.11) | collective-permute-done | bytes 262176 | tf_op jit(solution)/shard_map/ppermute | solution.py:21
  30.8 4.4 %attention_grads.3 = (bf16[2,2,128,256]{3,2,1,0:T(8,128)(2,1)S(1)}, bf16[2,2,128,256]{3,2,1,0:T(8,128)(2,1)S(1)}, f32[2,2,128,256]{3,2,1,0:T(8,128)S(1)}, f32[2,...) custom-call(f32[2,768,256]{2,1,0:T(8,128)S(1)} %pad_maximum_fusion.refs_0_, ...), custom_call_target="tpu_custom_call" | custom-call | flops 1006632960 | bytes 4980736 | tf_op jit(solution)/shard_map/attention_grads/pallas_call | solution.py:48
  35.3 1.3 %collective-permute-start.14 = (bf16[2,2,128,256]{3,2,1,0:T(8,128)(2,1)S(1)}, bf16[2,2,128,256]{3,2,1,0:T(8,128)(2,1)S(1)}, u32[]{:S(2)}, u32[]{:S(2)}) collective-permute-start(bf16[2,2,128,256]{3,2,1,0:T(8,128)(2,1)S(1)} %get-tuple-element.47), channel_id=1, source_target_pairs={{4,0},{8,4},{12,8},{5,1},{9,5},{13,9},{6,2},{10,6},{14,10},{7,3},{... | collective-permute-start | bytes 786440 | tf_op jit(solution)/shard_map/ppermute | solution.py:21
  36.6 4.4 %attention_grads.2 = (bf16[2,2,128,256]{3,2,1,0:T(8,128)(2,1)S(1)}, bf16[2,2,128,256]{3,2,1,0:T(8,128)(2,1)S(1)}, f32[2,2,128,256]{3,2,1,0:T(8,128)S(1)}, f32[2,...) custom-call(f32[2,768,256]{2,1,0:T(8,128)S(1)} %pad_maximum_fusion.refs_0_, ...), custom_call_target="tpu_custom_call" | custom-call | flops 1006632960 | bytes 4980736 | tf_op jit(solution)/shard_map/attention_grads/pallas_call | solution.py:48
  41.0 1.3 %collective-permute-start.7 = (bf16[2,2,128,256]{3,2,1,0:T(8,128)(2,1)S(1)}, bf16[2,2,128,256]{3,2,1,0:T(8,128)(2,1)S(1)}, u32[]{:S(2)}, u32[]{:S(2)}) collective-permute-start(bf16[2,2,128,256]{3,2,1,0:T(8,128)(2,1)S(1)} %get-tuple-element.36), channel_id=1, source_target_pairs={{4,0},{8,4},{12,8},{5,1},{9,5},{13,9},{6,2},{10,6},{14,10},{7,3},{... | collective-permute-start | bytes 786440 | tf_op jit(solution)/shard_map/ppermute | solution.py:21
  42.3 1.7 %collective-permute-done.14.later_ref = bf16[2,2,128,256]{3,2,1,0:T(8,128)(2,1)S(1)} collective-permute-done((bf16[2,2,128,256]{3,2,1,0:T(8,128)(2,1)S(1)}, bf16[2,2,128,256]{3,2,1,0:T(8,128)(2,1)S(1)}, u32[]{:S(2)}, u32[]{:S(2)}) %collective-permute-start.14) | collective-permute-done | bytes 262176 | tf_op jit(solution)/shard_map/ppermute | solution.py:21
  44.0 0.1 summed.3
  44.1 0.4 collective-permute-start.15
  44.5 5.9 %collective-permute-done.7.later_ref = bf16[2,2,128,256]{3,2,1,0:T(8,128)(2,1)S(1)} collective-permute-done((bf16[2,2,128,256]{3,2,1,0:T(8,128)(2,1)S(1)}, bf16[2,2,128,256]{3,2,1,0:T(8,128)(2,1)S(1)}, u32[]{:S(2)}, u32[]{:S(2)}) %collective-permute-start.7) | collective-permute-done | bytes 262176 | tf_op jit(solution)/shard_map/ppermute | solution.py:21
  50.4 0.1 summed.2
  50.4 0.4 collective-permute-start.8
  50.9 1.3 %collective-permute-start.13 = (bf16[2,2,128,256]{3,2,1,0:T(8,128)(2,1)S(1)}, bf16[2,2,128,256]{3,2,1,0:T(8,128)(2,1)S(1)}, u32[]{:S(2)}, u32[]{:S(2)}) collective-permute-start(bf16[2,2,128,256]{3,2,1,0:T(8,128)(2,1)S(1)} %get-tuple-element.44), channel_id=1, source_target_pairs={{4,0},{8,4},{12,8},{5,1},{9,5},{13,9},{6,2},{10,6},{14,10},{7,3},{... | collective-permute-start | bytes 786440 | tf_op jit(solution)/shard_map/ppermute | solution.py:21
  52.2 1.3 %collective-permute-start.6 = (bf16[2,2,128,256]{3,2,1,0:T(8,128)(2,1)S(1)}, bf16[2,2,128,256]{3,2,1,0:T(8,128)(2,1)S(1)}, u32[]{:S(2)}, u32[]{:S(2)}) collective-permute-start(bf16[2,2,128,256]{3,2,1,0:T(8,128)(2,1)S(1)} %get-tuple-element.33), channel_id=1, source_target_pairs={{4,0},{8,4},{12,8},{5,1},{9,5},{13,9},{6,2},{10,6},{14,10},{7,3},{... | collective-permute-start | bytes 786440 | tf_op jit(solution)/shard_map/ppermute | solution.py:21
  53.5 6.6 %collective-permute-done.13.later_ref = bf16[2,2,128,256]{3,2,1,0:T(8,128)(2,1)S(1)} collective-permute-done((bf16[2,2,128,256]{3,2,1,0:T(8,128)(2,1)S(1)}, bf16[2,2,128,256]{3,2,1,0:T(8,128)(2,1)S(1)}, u32[]{:S(2)}, u32[]{:S(2)}) %collective-permute-start.13) | collective-permute-done | bytes 262176 | tf_op jit(solution)/shard_map/ppermute | solution.py:21
  60.0 0.1 rows_for_pair.3
  60.1 0.1 collective-permute-start.17
  60.2 2.6 %collective-permute-done.6.later_ref = bf16[2,2,128,256]{3,2,1,0:T(8,128)(2,1)S(1)} collective-permute-done((bf16[2,2,128,256]{3,2,1,0:T(8,128)(2,1)S(1)}, bf16[2,2,128,256]{3,2,1,0:T(8,128)(2,1)S(1)}, u32[]{:S(2)}, u32[]{:S(2)}) %collective-permute-start.6) | collective-permute-done | bytes 262176 | tf_op jit(solution)/shard_map/ppermute | solution.py:21
  62.9 0.1 rows_for_pair.2
  62.9 0.1 collective-permute-start.16
  63.0 1.7 %collective-permute-done.16.refs_2_ = bf16[3,2,128,256]{3,2,1,0:T(8,128)(2,1)S(1)} collective-permute-done((bf16[3,2,128,256]{3,2,1,0:T(8,128)(2,1)S(1)}, bf16[3,2,128,256]{3,2,1,0:T(8,128)(2,1)S(1)}, u32[]{:S(2)}, u32[]{:S(2)}) %collective-permute-start.16) | collective-permute-done | bytes 393248 | tf_op jit(solution)/shard_map/ppermute | solution.py:30
  64.7 1.3 %laid_out.1 = (bf16[128,2048]{1,0:T(8,128)(2,1)}, bf16[128,2048]{1,0:T(8,128)(2,1)}, bf16[128,2048]{1,0:T(8,128)(2,1)}) custom-call(bf16[3,2,128,256]{3,2,1,0:T(8,128)(2,1)S(1)} %get-tuple-element.37.refs_0_, bf16[3,2,128,256]{3,2,1,0:T(8,128)(2,1)S(1)} %get-tuple-element.48.refs_1_, bf16[3,2,128,256]{3,2,1,0:T(8,128)(2,1)S(1)} %collective-permute-done.16.refs_2_, ...), custom_call_target="tpu_custom_call" | custom-call | bytes 3145728 | tf_op jit(solution)/shard_map/laid_out/pallas_call | solution.py:48
  (26 shorter events, 0.1 us)
Async XLA Ops:
  0.6 1.0 %copy-start = (bf16[128,2048]{1,0:T(8,128)(2,1)S(1)}, bf16[128,2048]{1,0:T(8,128)(2,1)}, u32[]{:S(2)}) copy-start(bf16[128,2048]{1,0:T(8,128)(2,1)} %refs_0_.10) | copy-start | bytes 1572868
  1.7 1.0 %copy-start.2 = (bf16[128,2048]{1,0:T(8,128)(2,1)S(1)}, bf16[128,2048]{1,0:T(8,128)(2,1)}, u32[]{:S(2)}) copy-start(bf16[128,2048]{1,0:T(8,128)(2,1)} %refs_1_.10) | copy-start | bytes 1572868
  2.7 1.3 %copy-start.4 = (bf16[128,2048]{1,0:T(8,128)(2,1)S(1)}, bf16[128,2048]{1,0:T(8,128)(2,1)}, u32[]{:S(2)}) copy-start(bf16[128,2048]{1,0:T(8,128)(2,1)} %refs_0_.11) | copy-start | bytes 1572868
  2.7 3.2 %copy-start.1 = (bf16[128,2048]{1,0:T(8,128)(2,1)S(1)}, bf16[128,2048]{1,0:T(8,128)(2,1)}, u32[]{:S(2)}) copy-start(bf16[128,2048]{1,0:T(8,128)(2,1)} %refs_0_.10) | copy-start | bytes 1572868
  2.7 3.2 %copy-start.3 = (bf16[128,2048]{1,0:T(8,128)(2,1)S(1)}, bf16[128,2048]{1,0:T(8,128)(2,1)}, u32[]{:S(2)}) copy-start(bf16[128,2048]{1,0:T(8,128)(2,1)} %refs_1_.10) | copy-start | bytes 1572868
  3.5 2.4 %collective-permute-start = (bf16[2,128,1024]{2,1,0:T(8,128)(2,1)}, bf16[2,128,1024]{2,1,0:T(8,128)(2,1)S(1)}, u32[]{:S(2)}, u32[]{:S(2)}) collective-permute-start(bf16[2,128,1024]{2,1,0:T(8,128)(2,1)} %pair_part.2), channel_id=1, source_target_pairs={{0,1},{1,0},{2,3},{3,2},{4,5},{5,4},{6,7},{7,6},{8,9},{9,8},{10,11... | collective-permute-start | bytes 1572872 | tf_op jit(solution)/shard_map/ppermute | solution.py:30
  4.1 1.0 %copy-start.5 = (bf16[128,2048]{1,0:T(8,128)(2,1)S(1)}, bf16[128,2048]{1,0:T(8,128)(2,1)}, u32[]{:S(2)}) copy-start(bf16[128,2048]{1,0:T(8,128)(2,1)} %refs_1_.11) | copy-start | bytes 1572868
  5.1 0.7 %copy-start.7 = (s32[2048]{0:T(1024)S(1)}, s32[2048]{0:T(1024)}, u32[]{:S(2)}) copy-start(s32[2048]{0:T(1024)} %param.9) | copy-start | bytes 24580
  5.2 8.1 %collective-permute-start.4 = (bf16[2,128,1024]{2,1,0:T(8,128)(2,1)S(1)}, bf16[2,128,1024]{2,1,0:T(8,128)(2,1)S(1)}, u32[]{:S(2)}, u32[]{:S(2)}) collective-permute-start(bf16[2,128,1024]{2,1,0:T(8,128)(2,1)S(1)} %pair_part.3), channel_id=1, source_target_pairs={{0,1},{1,0},{2,3},{3,2},{4,5},{5,4},{6,7},{7,6},{8,9},{9,8},{10,11... | collective-permute-start | bytes 1572872 | tf_op jit(solution)/shard_map/ppermute | solution.py:30
  5.9 7.4 %copy-start.6 = (bf16[128,2048]{1,0:T(8,128)(2,1)S(1)}, bf16[128,2048]{1,0:T(8,128)(2,1)}, u32[]{:S(2)}) copy-start(bf16[128,2048]{1,0:T(8,128)(2,1)} %refs_1_.11) | copy-start | bytes 1572868
  6.1 12.6 %collective-permute-start.9 = (bf16[2,2,128,256]{3,2,1,0:T(8,128)(2,1)S(1)}, bf16[2,2,128,256]{3,2,1,0:T(8,128)(2,1)S(1)}, u32[]{:S(2)}, u32[]{:S(2)}) collective-permute-start(bf16[2,2,128,256]{3,2,1,0:T(8,128)(2,1)S(1)} %get-tuple-element.39), channel_id=1, source_target_pairs={{0,2},{2,0},{1,3},{3,1},{4,6},{6,4},{5,7},{7,5},{8,10},{10,8},{9,1... | collective-permute-start | bytes 786440 | tf_op jit(solution)/shard_map/ppermute | solution.py:26
  9.0 10.3 %collective-permute-start.10 = (bf16[2,2,128,256]{3,2,1,0:T(8,128)(2,1)S(1)}, bf16[2,2,128,256]{3,2,1,0:T(8,128)(2,1)S(1)}, u32[]{:S(2)}, u32[]{:S(2)}) collective-permute-start(bf16[2,2,128,256]{3,2,1,0:T(8,128)(2,1)S(1)} %get-tuple-element.38.refs_1_), channel_id=1, source_target_pairs={{0,4},{4,8},{8,12},{1,5},{5,9},{9,13},{2,6},{6,10},{10,14},{3,7},{... | collective-permute-start | bytes 786440 | tf_op jit(solution)/shard_map/ppermute | solution.py:21
  12.7 10.2 %collective-permute-start.1 = (bf16[2,2,128,256]{3,2,1,0:T(8,128)(2,1)S(1)}, bf16[2,2,128,256]{3,2,1,0:T(8,128)(2,1)S(1)}, u32[]{:S(2)}, u32[]{:S(2)}) collective-permute-start(bf16[2,2,128,256]{3,2,1,0:T(8,128)(2,1)S(1)} %get-tuple-element.28), channel_id=1, source_target_pairs={{0,2},{2,0},{1,3},{3,1},{4,6},{6,4},{5,7},{7,5},{8,10},{10,8},{9,1... | collective-permute-start | bytes 786440 | tf_op jit(solution)/shard_map/ppermute | solution.py:26
  13.5 14.1 %collective-permute-start.12 = (bf16[2,2,128,256]{3,2,1,0:T(8,128)(2,1)S(1)}, bf16[2,2,128,256]{3,2,1,0:T(8,128)(2,1)S(1)}, u32[]{:S(2)}, u32[]{:S(2)}) collective-permute-start(bf16[2,2,128,256]{3,2,1,0:T(8,128)(2,1)S(1)} %get-tuple-element.41), channel_id=1, source_target_pairs={{0,2},{2,0},{1,3},{3,1},{4,6},{6,4},{5,7},{7,5},{8,10},{10,8},{9,1... | collective-permute-start | bytes 786440 | tf_op jit(solution)/shard_map/ppermute | solution.py:26
  15.0 21.5 %collective-permute-start.2 = (bf16[2,2,128,256]{3,2,1,0:T(8,128)(2,1)S(1)}, bf16[2,2,128,256]{3,2,1,0:T(8,128)(2,1)S(1)}, u32[]{:S(2)}, u32[]{:S(2)}) collective-permute-start(bf16[2,2,128,256]{3,2,1,0:T(8,128)(2,1)S(1)} %get-tuple-element.27.refs_1_), channel_id=1, source_target_pairs={{0,4},{4,8},{8,12},{1,5},{5,9},{9,13},{2,6},{6,10},{10,14},{3,7},{... | collective-permute-start | bytes 786440 | tf_op jit(solution)/shard_map/ppermute | solution.py:21
  18.7 17.9 %collective-permute-start.5 = (bf16[2,2,128,256]{3,2,1,0:T(8,128)(2,1)S(1)}, bf16[2,2,128,256]{3,2,1,0:T(8,128)(2,1)S(1)}, u32[]{:S(2)}, u32[]{:S(2)}) collective-permute-start(bf16[2,2,128,256]{3,2,1,0:T(8,128)(2,1)S(1)} %get-tuple-element.30), channel_id=1, source_target_pairs={{0,2},{2,0},{1,3},{3,1},{4,6},{6,4},{5,7},{7,5},{8,10},{10,8},{9,1... | collective-permute-start | bytes 786440 | tf_op jit(solution)/shard_map/ppermute | solution.py:26
  19.3 11.6 %collective-permute-start.11 = (bf16[2,2,128,256]{3,2,1,0:T(8,128)(2,1)S(1)}, bf16[2,2,128,256]{3,2,1,0:T(8,128)(2,1)S(1)}, u32[]{:S(2)}, u32[]{:S(2)}) collective-permute-start(bf16[2,2,128,256]{3,2,1,0:T(8,128)(2,1)S(1)} %collective-permute-done.9.refs_2_), channel_id=1, source_target_pairs={{0,4},{4,8},{8,12},{1,5},{5,9},{9,13},{2,6},{6,10},{10,14},{3,7},{... | collective-permute-start | bytes 786440 | tf_op jit(solution)/shard_map/ppermute | solution.py:21
  22.9 13.7 %collective-permute-start.3 = (bf16[2,2,128,256]{3,2,1,0:T(8,128)(2,1)S(1)}, bf16[2,2,128,256]{3,2,1,0:T(8,128)(2,1)S(1)}, u32[]{:S(2)}, u32[]{:S(2)}) collective-permute-start(bf16[2,2,128,256]{3,2,1,0:T(8,128)(2,1)S(1)} %collective-permute-done.1.refs_2_), channel_id=1, source_target_pairs={{0,4},{4,8},{8,12},{1,5},{5,9},{9,13},{2,6},{6,10},{10,14},{3,7},{... | collective-permute-start | bytes 786440 | tf_op jit(solution)/shard_map/ppermute | solution.py:21
  35.3 8.7 %collective-permute-start.14 = (bf16[2,2,128,256]{3,2,1,0:T(8,128)(2,1)S(1)}, bf16[2,2,128,256]{3,2,1,0:T(8,128)(2,1)S(1)}, u32[]{:S(2)}, u32[]{:S(2)}) collective-permute-start(bf16[2,2,128,256]{3,2,1,0:T(8,128)(2,1)S(1)} %get-tuple-element.47), channel_id=1, source_target_pairs={{4,0},{8,4},{12,8},{5,1},{9,5},{13,9},{6,2},{10,6},{14,10},{7,3},{... | collective-permute-start | bytes 786440 | tf_op jit(solution)/shard_map/ppermute | solution.py:21
  41.0 9.4 %collective-permute-start.7 = (bf16[2,2,128,256]{3,2,1,0:T(8,128)(2,1)S(1)}, bf16[2,2,128,256]{3,2,1,0:T(8,128)(2,1)S(1)}, u32[]{:S(2)}, u32[]{:S(2)}) collective-permute-start(bf16[2,2,128,256]{3,2,1,0:T(8,128)(2,1)S(1)} %get-tuple-element.36), channel_id=1, source_target_pairs={{4,0},{8,4},{12,8},{5,1},{9,5},{13,9},{6,2},{10,6},{14,10},{7,3},{... | collective-permute-start | bytes 786440 | tf_op jit(solution)/shard_map/ppermute | solution.py:21
  44.1 16.0 %collective-permute-start.15 = (bf16[3,2,128,256]{3,2,1,0:T(8,128)(2,1)S(1)}, bf16[3,2,128,256]{3,2,1,0:T(8,128)(2,1)S(1)}, u32[]{:S(2)}, u32[]{:S(2)}) collective-permute-start(bf16[3,2,128,256]{3,2,1,0:T(8,128)(2,1)S(1)} %summed.3), channel_id=1, source_target_pairs={{0,2},{2,0},{1,3},{3,1},{4,6},{6,4},{5,7},{7,5},{8,10},{10,8},{9,1... | collective-permute-start | bytes 1179656 | tf_op jit(solution)/shard_map/ppermute | solution.py:26
  50.4 12.4 %collective-permute-start.8 = (bf16[3,2,128,256]{3,2,1,0:T(8,128)(2,1)S(1)}, bf16[3,2,128,256]{3,2,1,0:T(8,128)(2,1)S(1)}, u32[]{:S(2)}, u32[]{:S(2)}) collective-permute-start(bf16[3,2,128,256]{3,2,1,0:T(8,128)(2,1)S(1)} %summed.2), channel_id=1, source_target_pairs={{0,2},{2,0},{1,3},{3,1},{4,6},{6,4},{5,7},{7,5},{8,10},{10,8},{9,1... | collective-permute-start | bytes 1179656 | tf_op jit(solution)/shard_map/ppermute | solution.py:26
  50.9 9.2 %collective-permute-start.13 = (bf16[2,2,128,256]{3,2,1,0:T(8,128)(2,1)S(1)}, bf16[2,2,128,256]{3,2,1,0:T(8,128)(2,1)S(1)}, u32[]{:S(2)}, u32[]{:S(2)}) collective-permute-start(bf16[2,2,128,256]{3,2,1,0:T(8,128)(2,1)S(1)} %get-tuple-element.44), channel_id=1, source_target_pairs={{4,0},{8,4},{12,8},{5,1},{9,5},{13,9},{6,2},{10,6},{14,10},{7,3},{... | collective-permute-start | bytes 786440 | tf_op jit(solution)/shard_map/ppermute | solution.py:21
  52.2 10.7 %collective-permute-start.6 = (bf16[2,2,128,256]{3,2,1,0:T(8,128)(2,1)S(1)}, bf16[2,2,128,256]{3,2,1,0:T(8,128)(2,1)S(1)}, u32[]{:S(2)}, u32[]{:S(2)}) collective-permute-start(bf16[2,2,128,256]{3,2,1,0:T(8,128)(2,1)S(1)} %get-tuple-element.33), channel_id=1, source_target_pairs={{4,0},{8,4},{12,8},{5,1},{9,5},{13,9},{6,2},{10,6},{14,10},{7,3},{... | collective-permute-start | bytes 786440 | tf_op jit(solution)/shard_map/ppermute | solution.py:21
  60.1 2.9 %collective-permute-start.17 = (bf16[3,2,128,256]{3,2,1,0:T(8,128)(2,1)S(1)}, bf16[3,2,128,256]{3,2,1,0:T(8,128)(2,1)S(1)}, u32[]{:S(2)}, u32[]{:S(2)}) collective-permute-start(bf16[3,2,128,256]{3,2,1,0:T(8,128)(2,1)S(1)} %get-tuple-element.50), channel_id=1, source_target_pairs={{0,1},{1,0},{2,3},{3,2},{4,5},{5,4},{6,7},{7,6},{8,9},{9,8},{10,11... | collective-permute-start | bytes 1179656 | tf_op jit(solution)/shard_map/ppermute | solution.py:30
  62.9 1.8 %collective-permute-start.16 = (bf16[3,2,128,256]{3,2,1,0:T(8,128)(2,1)S(1)}, bf16[3,2,128,256]{3,2,1,0:T(8,128)(2,1)S(1)}, u32[]{:S(2)}, u32[]{:S(2)}) collective-permute-start(bf16[3,2,128,256]{3,2,1,0:T(8,128)(2,1)S(1)} %get-tuple-element.49), channel_id=1, source_target_pairs={{0,1},{1,0},{2,3},{3,2},{4,5},{5,4},{6,7},{7,6},{8,9},{9,8},{10,11... | collective-permute-start | bytes 1179656 | tf_op jit(solution)/shard_map/ppermute | solution.py:30

commit v2 on v1

--- a/solution.py
+++ b/solution.py
@@ -12,7 +12,7 @@
 NEG_FILL = -1e30
 LOW = jnp.bfloat16
 WIDE = jnp.float32
-ROOM = 48 * 1024 * 1024
+MIB = 1024 * 1024
 
 
 def along_blocks(value, by):
@@ -42,7 +42,7 @@
     return [pl.BlockSpec(memory_space=pl.ANY)] * count
 
 
-def call(kernel, ins, outs, scratch, name, whole=False, flops=0):
+def call(kernel, ins, outs, scratch, name, whole=False, flops=0, room=8 * MIB):
     spec = (lambda n: [pl.BlockSpec(memory_space=pltpu.VMEM)] * n) if whole else anywhere
     moved = sum(math.prod(a.shape) * a.dtype.itemsize for a in list(ins) + list(outs))
     return pl.pallas_call(
@@ -53,25 +53,15 @@
         scratch_shapes=scratch,
         name=name,
         cost_estimate=pl.CostEstimate(flops=flops, bytes_accessed=moved, transcendentals=0),
-        compiler_params=pltpu.CompilerParams(vmem_limit_bytes=ROOM),
+        compiler_params=pltpu.CompilerParams(vmem_limit_bytes=room),
     )(*ins)
 
 
-def pair_part(arrays):
-    count = len(arrays)
-    rows, width = arrays[0].shape
-    half = width // 2
-
-    def kernel(*refs):
-        ins, out, sems = refs[:count], refs[count], refs[count + 1]
-        start = pl.multiple_of((1 - lax.axis_index("pair")) * half, half)
-        run_moves([(ref.at[:, pl.ds(start, half)], out.at[i]) for i, ref in enumerate(ins)], sems)
-
-    outs = [jax.ShapeDtypeStruct((count, rows, half), LOW)]
-    return call(kernel, arrays, outs, [pltpu.SemaphoreType.DMA((count,))], "pair_part")[0]
-
-
-def head_parts(arrays, received, chunk):
+def corner(value):
+    return value[0, 0, :16, :HD]
+
+
+def first_parts(arrays, chunk, after):
     count = len(arrays)
     rows, width = arrays[0].shape
     half = width // 2
@@ -80,20 +70,35 @@
     cut = part // CHUNKS
 
     def kernel(*refs):
-        ins, rec, outs, sems = refs[:count], refs[count], refs[count + 1:-1], refs[-1]
+        ins, outs, sems = refs[:count], refs[-3:-1], refs[-1]
+        p = lax.axis_index("pair")
+        moves = []
+        for side, out in zip((1 - p, p), outs):
+            for at in range(peers):
+                start = pl.multiple_of(side * half + at * part + chunk * cut, cut)
+                moves += [(ref.at[:, pl.ds(start, cut)], out.at[i, at]) for i, ref in enumerate(ins)]
+        run_moves(moves, sems)
+
+    outs = [jax.ShapeDtypeStruct((count, peers, rows, cut), LOW)] * 2
+    scratch = [pltpu.SemaphoreType.DMA((2 * peers * count,))]
+    return call(kernel, arrays + after, outs, scratch, "first_parts", room=(8 if after else 62) * MIB)
+
+
+def head_parts(own, received, turns, after=()):
+    count, peers, rows, cut = own.shape
+
+    def kernel(own_ref, rec_ref, *refs):
+        outs, sems = refs[len(after):-1], refs[-1]
         p, s = lax.axis_index("pair"), lax.axis_index("sub")
         moves = []
-        for by, out in enumerate(outs):
-            base = lax.rem(s + by, peers) * part + chunk * cut
-            here = pl.multiple_of(p * half + base, cut)
-            there = pl.multiple_of(base, cut)
-            moves += [(ref.at[:, pl.ds(here, cut)], out.at[i, p]) for i, ref in enumerate(ins)]
-            moves.append((rec.at[:, :, pl.ds(there, cut)], out.at[:, 1 - p]))
-        run_moves(moves, sems)
-
-    outs = [jax.ShapeDtypeStruct((count, 2, rows, cut), LOW)] * peers
-    scratch = [pltpu.SemaphoreType.DMA((peers * (count + 1),))]
-    return call(kernel, list(arrays) + [received], outs, scratch, "head_parts")
+        for by, out in zip(turns, outs):
+            at = lax.rem(s + by, peers)
+            moves += [(own_ref.at[:, at], out.at[:, p]), (rec_ref.at[:, at], out.at[:, 1 - p])]
+        run_moves(moves, sems)
+
+    outs = [jax.ShapeDtypeStruct((count, 2, rows, cut), LOW)] * len(turns)
+    scratch = [pltpu.SemaphoreType.DMA((2 * len(turns),))]
+    return call(kernel, [own, received] + list(after), outs, scratch, "head_parts")
 
 
 def attention_grads(bias, kv, kv_earlier, qg):
@@ -107,9 +112,8 @@
     def kernel(*refs):
         bias_ref = refs[0]
         kv_in, early_in, qg_in = refs[1:1 + peers], refs[1 + peers:1 + 2 * peers], refs[1 + 2 * peers:1 + 3 * peers]
-        outs = refs[1 + 3 * peers:1 + 6 * peers]
-        early_out, kv_out, dq_out = outs[:peers], outs[peers:2 * peers], outs[2 * peers:]
-        bias_held, kv_all, qg_all, grads, early_low, dq_all, sems = refs[1 + 6 * peers:]
+        early_out, kv_out, dq_out = refs[1 + 3 * peers:4 + 3 * peers]
+        bias_held, kv_all, qg_all, grads, early_low, dq_all, sems = refs[4 + 3 * peers:]
         s = lax.axis_index("sub")
         moves = [(bias_ref, bias_held)]
         for by in range(peers):
@@ -149,21 +153,13 @@
                         grads[which, 1:3, :, :, columns] += term[0:2]
                         grads[which, 3:4, :, :, columns] = term[2:3]
         early_low[...] = grads[:, 0:2].astype(LOW)
-        moves = []
-        for by in range(peers):
-            at = lax.rem(s + by, peers)
-            moves += [
-                (early_low.at[:, :, at], early_out[by]),
-                (grads.at[:, 2:4, at], kv_out[by]),
-                (dq_all.at[:, at], dq_out[by]),
-            ]
-        run_moves(moves, sems)
-
-    outs = (
-        [jax.ShapeDtypeStruct((2, 2, rows, cut), LOW)] * peers
-        + [jax.ShapeDtypeStruct((2, 2, rows, cut), WIDE)] * peers
-        + [jax.ShapeDtypeStruct((2, rows, cut), LOW)] * peers
-    )
+        run_moves([(early_low, early_out), (grads.at[:, 2:4], kv_out), (dq_all, dq_out)], sems)
+
+    outs = [
+        jax.ShapeDtypeStruct((2, 2, peers, rows, cut), LOW),
+        jax.ShapeDtypeStruct((2, 2, peers, rows, cut), WIDE),
+        jax.ShapeDtypeStruct((2, peers, rows, cut), LOW),
+    ]
     scratch = [
         pltpu.VMEM(bias.shape, WIDE),
         pltpu.VMEM((2, 4, peers, rows, cut), LOW),
@@ -174,39 +170,42 @@
         pltpu.SemaphoreType.DMA((1 + 3 * peers,)),
     ]
     flops = heads * 2 * 5 * 2 * strip * 3 * strip * HD
-    outs = call(kernel, [bias] + list(kv) + list(kv_earlier) + list(qg), outs, scratch, "attention_grads", flops=flops)
-    return outs[:peers], outs[peers:2 * peers], outs[2 * peers:]
+    ins = [bias] + list(kv) + list(kv_earlier) + list(qg)
+    return call(kernel, ins, outs, scratch, "attention_grads", flops=flops, room=44 * MIB)
 
 
 def summed(dq, own, later):
-    _, rows, cut = dq.shape
-
-    def kernel(dq_ref, own_ref, later_ref, out):
-        out[0] = dq_ref[...]
-        out[1:3] = (own_ref[...] + later_ref[...].astype(WIDE)).astype(LOW)
-
-    outs = [jax.ShapeDtypeStruct((3, 2, rows, cut), LOW)]
-    return call(kernel, [dq, own, later], outs, [], "summed", whole=True)[0]
-
-
-def rows_for_pair(dq, own, later, received):
-    peers = len(received) + 1
-    _, rows, cut = dq.shape
-
-    def kernel(dq_ref, own_ref, later_ref, *refs):
-        rec, (send, keep) = refs[:peers - 1], refs[peers - 1:]
+    _, peers, rows, cut = dq.shape
+
+    def kernel(dq_ref, own_ref, later_ref, *outs):
+        s = lax.axis_index("sub")
+        for by, out in enumerate(outs):
+            at = lax.rem(s + by, peers)
+            for row in range(2):
+                out[0, row] = dq_ref[row, at]
+                for which in range(2):
+                    total = own_ref[which, row, at] + later_ref[which, row, at].astype(WIDE)
+                    out[1 + which, row] = total.astype(LOW)
+
+    outs = [jax.ShapeDtypeStruct((3, 2, rows, cut), LOW)] * peers
+    return call(kernel, [dq, own, later], outs, [], "summed", whole=True)
+
+
+def rows_for_pair(parts):
+    peers = len(parts)
+    _, _, rows, cut = parts[0].shape
+
+    def kernel(*refs):
+        ins, (send, keep), sems = refs[:peers], refs[peers:-1], refs[-1]
         p, s = lax.axis_index("pair"), lax.axis_index("sub")
-        for out, row in ((send, 1 - p), (keep, p)):
-            out[0, s] = dq_ref[row]
-            for which in range(2):
-                out[1 + which, s] = (own_ref[which, row] + later_ref[which, row].astype(WIDE)).astype(LOW)
-            for by in range(1, peers):
-                at = lax.rem(s - by + peers, peers)
-                for which in range(3):
-                    out[which, at] = rec[by - 1][which, row]
+        moves = []
+        for by, ref in enumerate(ins):
+            at = lax.rem(s - by + peers, peers)
+            moves += [(ref.at[:, 1 - p], send.at[:, at]), (ref.at[:, p], keep.at[:, at])]
+        run_moves(moves, sems)
 
     outs = [jax.ShapeDtypeStruct((3, peers, rows, cut), LOW)] * 2
-    return call(kernel, [dq, own, later] + list(received), outs, [], "rows_for_pair", whole=True)
+    return call(kernel, parts, outs, [pltpu.SemaphoreType.DMA((2 * peers,))], "rows_for_pair")
 
 
 def laid_out(kept, received):
@@ -247,23 +246,28 @@
 
 
 def shards(queries, keys, values, out_grad, session):
-    peers = lax.axis_size("sub")
-    kv_pair = swapped(pair_part([keys, values]))
-    qg_pair = swapped(pair_part([queries, out_grad]))
+    others = range(1, lax.axis_size("sub"))
     bias = allowed_bias(session, queries.shape[0])
     kept, paired = [], []
+    kv_turn, own_turn, qg_turn, first_turn = [], [], [], []
     for chunk in range(CHUNKS):
-        kv = head_parts([keys, values], kv_pair, chunk)
-        kv = [kv[0]] + [round_sub(kv[by], by) for by in range(1, peers)]
+        send, own = first_parts([keys, values], chunk, first_turn)
+        rec = swapped(send)
+        sends = list(head_parts(own, rec, others, kv_turn))
+        kv = [round_sub(part, by) for by, part in zip(others, sends)]
+        kv_own = list(head_parts(own, rec, [0], own_turn))
+        own_earlier = [along_blocks(kv_own[0], 1)]
         kv_earlier = [along_blocks(value, 1) for value in kv]
-        qg = head_parts([queries, out_grad], qg_pair, chunk)
-        qg = [qg[0]] + [round_sub(qg[by], by) for by in range(1, peers)]
-        early, own, dq = attention_grads(bias, kv, kv_earlier, qg)
-        later = [along_blocks(early[by], -1) for by in list(range(1, peers)) + [0]]
-        received = []
-        for by in range(1, peers):
-            received.append(round_sub(summed(dq[by], own[by], later[by - 1]), by))
-        send, keep = rows_for_pair(dq[0], own[0], later[-1], received)
+        kv_turn, own_turn = kv + own_earlier, kv_earlier
+        send, own = first_parts([queries, out_grad], chunk, [corner(sends[0])])
+        rec = swapped(send)
+        sends = list(head_parts(own, rec, others, qg_turn))
+        qg = [round_sub(part, by) for by, part in zip(others, sends)]
+        qg_own = list(head_parts(own, rec, [0]))
+        qg_turn, first_turn = qg, [corner(sends[0])]
+        early, grads, dq = attention_grads(bias, kv_own + kv, own_earlier + kv_earlier, qg_own + qg)
+        parts = summed(dq, grads, along_blocks(early, -1))
+        send, keep = rows_for_pair([parts[0]] + [round_sub(parts[by], by) for by in others])
         kept.append(keep)
         paired.append(swapped(send))
     return tuple(laid_out(kept, paired))

time: 66.5 us -> 92.8 us (1.40)
  Pallas kernels: 11.9 us -> 30.5 us
  waiting for transfers between devices: 22.2 us -> 31.5 us
  local copies, waits for them, and re-layouts: 3.45 us -> 1.09 us
    pallas_call x13 -> x19, Pallas kernels: 11.9 us -> 30.5 us  [call(): pl.pallas_call(kernel, out_shape=outs, in_specs=spec(len(ins)), out_specs...]
    ppermute x6, waiting for transfers between devices: 0.44 us -> 9.39 us  [round_sub(): lax.ppermute(value, 'sub', [(i, (i + by) % peers) for i in range(peers)])]
    unnamed x16, local copies, waits for them, and re-layouts: 3.36 us -> 0.98 us
    ppermute x6, starting transfers between devices: 6.48 us -> 8.69 us  [round_sub(): lax.ppermute(value, 'sub', [(i, (i + by) % peers) for i in range(peers)])]
    ppermute x8 -> x6, starting transfers between devices: 19.2 us -> 17.7 us  [along_blocks(): return lax.ppermute(value, 'blk', pairs)]
    ppermute x4 -> x6, waiting for transfers between devices: 1.71 us -> 3.08 us  [swapped(): return lax.ppermute(value, 'pair', [(0, 1), (1, 0)])]
    ppermute x8 -> x6, waiting for transfers between devices: 20.1 us -> 19 us  [along_blocks(): return lax.ppermute(value, 'blk', pairs)]
  transfers between devices with their start and end apart: 18 -> 18, of which waited for: 7 -> 8; matrix products, arithmetic and copies ran while one was open for 1% -> 1% of each run, Pallas kernels for 15% -> 12%
where the time goes in v2:
time: 92.8 us; the launch traced here: 92.6 us
  waiting for transfers between devices  31.5 us (34%)
  Pallas kernels  30.5 us (33%)
  starting transfers between devices  27.6 us (30%)
  local copies, waits for them, and re-layouts  1.09 us (1%)
  between operations  1.06 us (1%)
    pallas_call x19, Pallas kernels, call(): pl.pallas_call(kernel, out_shape=outs, in_specs=spec(len(ins)), out_specs...  30.5 us
    ppermute x6, waiting for transfers between devices, along_blocks(): return lax.ppermute(value, 'blk', pairs)  19 us
    ppermute x6, starting transfers between devices, along_blocks(): return lax.ppermute(value, 'blk', pairs)  17.7 us
    ppermute x6, waiting for transfers between devices, round_sub(): lax.ppermute(value, 'sub', [(i, (i + by) % peers) for i in range(peers)])  9.39 us
    ppermute x6, starting transfers between devices, round_sub(): lax.ppermute(value, 'sub', [(i, (i + by) % peers) for i in range(peers)])  8.69 us
    ppermute x6, waiting for transfers between devices, swapped(): return lax.ppermute(value, 'pair', [(0, 1), (1, 0)])  3.08 us
  transfers between devices with their start and end apart: 18, of which 8 were waited for; matrix products, arithmetic and copies ran while one was open for 1% of the time, Pallas kernels for 12%

profile of v2, /device:TPU:0, one launch (start us, length us, event | category | flops | bytes accessed | tf_op | source)
XLA Modules:
  0.0 92.6 jit_solution(10491815863175571588)
XLA Ops:
  0.6 17.1 %first_parts.4 = (bf16[2,2,128,256]{3,2,1,0:T(8,128)(2,1)}, bf16[2,2,128,256]{3,2,1,0:T(8,128)(2,1)}) custom-call(bf16[128,2048]{1,0:T(8,128)(2,1)} %refs_0_.6, bf16[128,2048]{1,0:T(8,128)(2,1)} %refs_1_.6), custom_call_target="tpu_custom_call" | custom-call | bytes 1572864 | tf_op jit(solution)/shard_map/first_parts/pallas_call | solution.py:48
  17.7 0.5 collective-permute-start
  18.2 1.4 %collective-permute-done.rec_ref = bf16[2,2,128,256]{3,2,1,0:T(8,128)(2,1)S(1)} collective-permute-done((bf16[2,2,128,256]{3,2,1,0:T(8,128)(2,1)}, bf16[2,2,128,256]{3,2,1,0:T(8,128)(2,1)S(1)}, u32[]{:S(2)}, u32[]{:S(2)}) %collective-permute-start) | collective-permute-done | bytes 262176 | tf_op jit(solution)/shard_map/ppermute | solution.py:30
  19.6 0.9 %copy-done.4 = bf16[2,2,128,256]{3,2,1,0:T(8,128)(2,1)S(1)} copy-done((bf16[2,2,128,256]{3,2,1,0:T(8,128)(2,1)S(1)}, bf16[2,2,128,256]{3,2,1,0:T(8,128)(2,1)}, u32[]{:S(2)}) %copy-start.4) | copy-done | bytes 262168
  20.6 0.2 head_parts.9
  20.8 0.8 first_parts.5
  21.6 0.4 collective-permute-start.4
  22.1 2.7 %collective-permute-start.1 = (bf16[2,2,128,256]{3,2,1,0:T(8,128)(2,1)}, bf16[2,2,128,256]{3,2,1,0:T(8,128)(2,1)S(1)}, u32[]{:S(2)}, u32[]{:S(2)}) collective-permute-start(bf16[2,2,128,256]{3,2,1,0:T(8,128)(2,1)} %copy-done.6), channel_id=1, source_target_pairs={{0,2},{2,0},{1,3},{3,1},{4,6},{6,4},{5,7},{7,5},{8,10},{10,8},{9,1... | collective-permute-start | bytes 786440 | tf_op jit(solution)/shard_map/ppermute | solution.py:26
  24.8 0.2 head_parts.8.refs_1_
  25.0 3.5 %collective-permute-start.2 = (bf16[2,2,128,256]{3,2,1,0:T(8,128)(2,1)S(1)}, bf16[2,2,128,256]{3,2,1,0:T(8,128)(2,1)S(1)}, u32[]{:S(2)}, u32[]{:S(2)}) collective-permute-start(bf16[2,2,128,256]{3,2,1,0:T(8,128)(2,1)S(1)} %head_parts.8.refs_1_), channel_id=1, source_target_pairs={{0,4},{4,8},{8,12},{1,5},{5,9},{9,13},{2,6},{6,10},{10,14},{3,7},{... | collective-permute-start | bytes 786440 | tf_op jit(solution)/shard_map/ppermute | solution.py:21
  28.5 0.2 head_parts.11
  28.7 0.2 first_parts.6
  28.9 0.1 collective-permute-start.8
  29.0 0.1 pad_dynamic-slice_fusion
  29.1 0.5 collective-permute-start.5
  29.6 2.2 %collective-permute-done.1.refs_2_.refs_0_ = bf16[2,2,128,256]{3,2,1,0:T(8,128)(2,1)S(1)} collective-permute-done((bf16[2,2,128,256]{3,2,1,0:T(8,128)(2,1)}, bf16[2,2,128,256]{3,2,1,0:T(8,128)(2,1)S(1)}, u32[]{:S(2)}, u32[]{:S(2)}) %collective-permute-start.1) | collective-permute-done | bytes 262176 | tf_op jit(solution)/shard_map/ppermute | solution.py:26
  31.8 3.7 %collective-permute-start.3 = (bf16[2,2,128,256]{3,2,1,0:T(8,128)(2,1)S(1)}, bf16[2,2,128,256]{3,2,1,0:T(8,128)(2,1)S(1)}, u32[]{:S(2)}, u32[]{:S(2)}) collective-permute-start(bf16[2,2,128,256]{3,2,1,0:T(8,128)(2,1)S(1)} %collective-permute-done.1.refs_2_.refs_0_), channel_id=1, source_target_pairs={{0,4},{4,8},{8,12},{1,5},{5,9},{9,13},{2,6},{6,10},{10,14},{3,7},{... | collective-permute-start | bytes 786440 | tf_op jit(solution)/shard_map/ppermute | solution.py:21
  35.6 0.2 head_parts.13
  35.8 2.1 %collective-permute-start.9 = (bf16[2,2,128,256]{3,2,1,0:T(8,128)(2,1)S(1)}, bf16[2,2,128,256]{3,2,1,0:T(8,128)(2,1)S(1)}, u32[]{:S(2)}, u32[]{:S(2)}) collective-permute-start(bf16[2,2,128,256]{3,2,1,0:T(8,128)(2,1)S(1)} %head_parts.13), channel_id=1, source_target_pairs={{0,2},{2,0},{1,3},{3,1},{4,6},{6,4},{5,7},{7,5},{8,10},{10,8},{9,1... | collective-permute-start | bytes 786440 | tf_op jit(solution)/shard_map/ppermute | solution.py:26
  37.9 0.2 first_parts.7
  38.1 0.1 collective-permute-start.12
  38.2 2.6 %collective-permute-done.3.refs_4_.refs_0_ = bf16[2,2,128,256]{3,2,1,0:T(8,128)(2,1)S(1)} collective-permute-done((bf16[2,2,128,256]{3,2,1,0:T(8,128)(2,1)S(1)}, bf16[2,2,128,256]{3,2,1,0:T(8,128)(2,1)S(1)}, u32[]{:S(2)}, u32[]{:S(2)}) %collective-permute-start.3) | collective-permute-done | bytes 262176 | tf_op jit(solution)/shard_map/ppermute | solution.py:21
  40.8 0.2 head_parts.12.refs_1_
  41.0 4.4 %collective-permute-start.10 = (bf16[2,2,128,256]{3,2,1,0:T(8,128)(2,1)S(1)}, bf16[2,2,128,256]{3,2,1,0:T(8,128)(2,1)S(1)}, u32[]{:S(2)}, u32[]{:S(2)}) collective-permute-start(bf16[2,2,128,256]{3,2,1,0:T(8,128)(2,1)S(1)} %head_parts.12.refs_1_), channel_id=1, source_target_pairs={{0,4},{4,8},{8,12},{1,5},{5,9},{9,13},{2,6},{6,10},{10,14},{3,7},{... | collective-permute-start | bytes 786440 | tf_op jit(solution)/shard_map/ppermute | solution.py:21
  45.4 0.2 head_parts.15
  45.6 1.6 %collective-permute-start.13 = (bf16[2,2,128,256]{3,2,1,0:T(8,128)(2,1)S(1)}, bf16[2,2,128,256]{3,2,1,0:T(8,128)(2,1)S(1)}, u32[]{:S(2)}, u32[]{:S(2)}) collective-permute-start(bf16[2,2,128,256]{3,2,1,0:T(8,128)(2,1)S(1)} %head_parts.15), channel_id=1, source_target_pairs={{0,2},{2,0},{1,3},{3,1},{4,6},{6,4},{5,7},{7,5},{8,10},{10,8},{9,1... | collective-permute-start | bytes 786440 | tf_op jit(solution)/shard_map/ppermute | solution.py:26
  47.2 3.5 %collective-permute-start.11 = (bf16[2,2,128,256]{3,2,1,0:T(8,128)(2,1)S(1)}, bf16[2,2,128,256]{3,2,1,0:T(8,128)(2,1)S(1)}, u32[]{:S(2)}, u32[]{:S(2)}) collective-permute-start(bf16[2,2,128,256]{3,2,1,0:T(8,128)(2,1)S(1)} %collective-permute-done.9.refs_2_), channel_id=1, source_target_pairs={{0,4},{4,8},{8,12},{1,5},{5,9},{9,13},{2,6},{6,10},{10,14},{3,7},{... | collective-permute-start | bytes 786440 | tf_op jit(solution)/shard_map/ppermute | solution.py:21
  50.7 0.7 and_select_fusion
  51.4 0.1 pad_maximum_fusion.refs_0_
  51.5 0.2 head_parts.10.refs_5_
  51.7 4.3 %attention_grads.2 = (bf16[2,2,2,128,256]{4,3,2,1,0:T(8,128)(2,1)S(1)}, f32[2,2,2,128,256]{4,3,2,1,0:T(8,128)S(1)}, bf16[2,2,128,256]{3,2,1,0:T(8,128)(2,1)S(1)}) custom-call(f32[2,768,256]{2,1,0:T(8,128)S(1)} %pad_maximum_fusion.refs_0_, bf16[2,2,128,256]{3,2,1,0:T(8,128)(2,1)S(1)} %head_parts.8.refs_1_, ...), custom_call_target="tpu_custom_call" | custom-call | flops 1006632960 | bytes 4980736 | tf_op jit(solution)/shard_map/attention_grads/pallas_call | solution.py:48
  55.9 1.3 %collective-permute-start.6 = (bf16[2,2,2,128,256]{4,3,2,1,0:T(8,128)(2,1)S(1)}, bf16[2,2,2,128,256]{4,3,2,1,0:T(8,128)(2,1)S(1)}, u32[]{:S(2)}, u32[]{:S(2)}) collective-permute-start(bf16[2,2,2,128,256]{4,3,2,1,0:T(8,128)(2,1)S(1)} %get-tuple-element.31), channel_id=1, source_target_pairs={{4,0},{8,4},{12,8},{5,1},{9,5},{13,9},{6,2},{10,6},{14,10},{7,3},{... | collective-permute-start | bytes 1572872 | tf_op jit(solution)/shard_map/ppermute | solution.py:21
  57.2 0.2 head_parts.14.refs_5_
  57.5 4.3 %attention_grads.3 = (bf16[2,2,2,128,256]{4,3,2,1,0:T(8,128)(2,1)S(1)}, f32[2,2,2,128,256]{4,3,2,1,0:T(8,128)S(1)}, bf16[2,2,128,256]{3,2,1,0:T(8,128)(2,1)S(1)}) custom-call(f32[2,768,256]{2,1,0:T(8,128)S(1)} %pad_maximum_fusion.refs_0_, bf16[2,2,128,256]{3,2,1,0:T(8,128)(2,1)S(1)} %head_parts.12.refs_1_, ...), custom_call_target="tpu_custom_call" | custom-call | flops 1006632960 | bytes 4980736 | tf_op jit(solution)/shard_map/attention_grads/pallas_call | solution.py:48
  61.8 1.3 %collective-permute-start.14 = (bf16[2,2,2,128,256]{4,3,2,1,0:T(8,128)(2,1)S(1)}, bf16[2,2,2,128,256]{4,3,2,1,0:T(8,128)(2,1)S(1)}, u32[]{:S(2)}, u32[]{:S(2)}) collective-permute-start(bf16[2,2,2,128,256]{4,3,2,1,0:T(8,128)(2,1)S(1)} %get-tuple-element.41), channel_id=1, source_target_pairs={{4,0},{8,4},{12,8},{5,1},{9,5},{13,9},{6,2},{10,6},{14,10},{7,3},{... | collective-permute-start | bytes 1572872 | tf_op jit(solution)/shard_map/ppermute | solution.py:21
  63.1 9.6 %collective-permute-done.6.later_ref = bf16[2,2,2,128,256]{4,3,2,1,0:T(8,128)(2,1)S(1)} collective-permute-done((bf16[2,2,2,128,256]{4,3,2,1,0:T(8,128)(2,1)S(1)}, bf16[2,2,2,128,256]{4,3,2,1,0:T(8,128)(2,1)S(1)}, u32[]{:S(2)}, u32[]{:S(2)}) %collective-permute-start.6) | collective-permute-done | bytes 524320 | tf_op jit(solution)/shard_map/ppermute | solution.py:21
  72.7 0.1 summed.2
  72.8 0.6 collective-permute-start.7
  73.4 6.7 %collective-permute-done.14.later_ref = bf16[2,2,2,128,256]{4,3,2,1,0:T(8,128)(2,1)S(1)} collective-permute-done((bf16[2,2,2,128,256]{4,3,2,1,0:T(8,128)(2,1)S(1)}, bf16[2,2,2,128,256]{4,3,2,1,0:T(8,128)(2,1)S(1)}, u32[]{:S(2)}, u32[]{:S(2)}) %collective-permute-start.14) | collective-permute-done | bytes 524320 | tf_op jit(solution)/shard_map/ppermute | solution.py:21
  80.2 0.1 summed.3
  80.3 1.2 %collective-permute-start.15 = (bf16[3,2,128,256]{3,2,1,0:T(8,128)(2,1)S(1)}, bf16[3,2,128,256]{3,2,1,0:T(8,128)(2,1)S(1)}, u32[]{:S(2)}, u32[]{:S(2)}) collective-permute-start(bf16[3,2,128,256]{3,2,1,0:T(8,128)(2,1)S(1)} %get-tuple-element.43), channel_id=1, source_target_pairs={{0,2},{2,0},{1,3},{3,1},{4,6},{6,4},{5,7},{7,5},{8,10},{10,8},{9,1... | collective-permute-start | bytes 1179656 | tf_op jit(solution)/shard_map/ppermute | solution.py:26
  81.4 0.6 collective-permute-done.7.refs_1_
  82.0 0.4 rows_for_pair.2
  82.4 0.1 collective-permute-start.16
  82.4 6.6 %collective-permute-done.15.refs_1_ = bf16[3,2,128,256]{3,2,1,0:T(8,128)(2,1)S(1)} collective-permute-done((bf16[3,2,128,256]{3,2,1,0:T(8,128)(2,1)S(1)}, bf16[3,2,128,256]{3,2,1,0:T(8,128)(2,1)S(1)}, u32[]{:S(2)}, u32[]{:S(2)}) %collective-permute-start.15) | collective-permute-done | bytes 393248 | tf_op jit(solution)/shard_map/ppermute | solution.py:26
  89.1 0.4 rows_for_pair.3
  89.5 1.7 %collective-permute-done.17.refs_3_ = bf16[3,2,128,256]{3,2,1,0:T(8,128)(2,1)S(1)} collective-permute-done((bf16[3,2,128,256]{3,2,1,0:T(8,128)(2,1)S(1)}, bf16[3,2,128,256]{3,2,1,0:T(8,128)(2,1)S(1)}, u32[]{:S(2)}, u32[]{:S(2)}) %collective-permute-start.17) | collective-permute-done | bytes 393248 | tf_op jit(solution)/shard_map/ppermute | solution.py:30
  91.2 1.3 %laid_out.1 = (bf16[128,2048]{1,0:T(8,128)(2,1)}, bf16[128,2048]{1,0:T(8,128)(2,1)}, bf16[128,2048]{1,0:T(8,128)(2,1)}) custom-call(bf16[3,2,128,256]{3,2,1,0:T(8,128)(2,1)S(1)} %get-tuple-element.34.refs_0_, bf16[3,2,128,256]{3,2,1,0:T(8,128)(2,1)S(1)} %get-tuple-element.44.refs_1_, bf16[3,2,128,256]{3,2,1,0:T(8,128)(2,1)S(1)} %collective-permute-done.16.refs_2_, ...), custom_call_target="tpu_custom_call" | custom-call | bytes 3145728 | tf_op jit(solution)/shard_map/laid_out/pallas_call | solution.py:48
  (35 shorter events, 0.2 us)
Async XLA Ops:
  0.6 20.2 %copy-start.2 = (bf16[128,2048]{1,0:T(8,128)(2,1)S(1)}, bf16[128,2048]{1,0:T(8,128)(2,1)}, u32[]{:S(2)}) copy-start(bf16[128,2048]{1,0:T(8,128)(2,1)} %refs_0_.7) | copy-start | bytes 1572868
  0.6 20.2 %copy-start.3 = (bf16[128,2048]{1,0:T(8,128)(2,1)S(1)}, bf16[128,2048]{1,0:T(8,128)(2,1)}, u32[]{:S(2)}) copy-start(bf16[128,2048]{1,0:T(8,128)(2,1)} %refs_1_.7) | copy-start | bytes 1572868
  17.7 1.9 %collective-permute-start = (bf16[2,2,128,256]{3,2,1,0:T(8,128)(2,1)}, bf16[2,2,128,256]{3,2,1,0:T(8,128)(2,1)S(1)}, u32[]{:S(2)}, u32[]{:S(2)}) collective-permute-start(bf16[2,2,128,256]{3,2,1,0:T(8,128)(2,1)} %get-tuple-element.26), channel_id=1, source_target_pairs={{0,1},{1,0},{2,3},{3,2},{4,5},{5,4},{6,7},{7,6},{8,9},{9,8},{10,11... | collective-permute-start | bytes 786440 | tf_op jit(solution)/shard_map/ppermute | solution.py:30
  19.6 0.9 %copy-start.4 = (bf16[2,2,128,256]{3,2,1,0:T(8,128)(2,1)S(1)}, bf16[2,2,128,256]{3,2,1,0:T(8,128)(2,1)}, u32[]{:S(2)}) copy-start(bf16[2,2,128,256]{3,2,1,0:T(8,128)(2,1)} %get-tuple-element.25.own_ref) | copy-start | bytes 786436
  20.6 4.2 %copy-start.5 = (bf16[2,2,128,256]{3,2,1,0:T(8,128)(2,1)S(1)}, bf16[2,2,128,256]{3,2,1,0:T(8,128)(2,1)}, u32[]{:S(2)}) copy-start(bf16[2,2,128,256]{3,2,1,0:T(8,128)(2,1)} %get-tuple-element.25.own_ref) | copy-start | bytes 786436
  20.6 8.1 %copy-start = (bf16[128,2048]{1,0:T(8,128)(2,1)S(1)}, bf16[128,2048]{1,0:T(8,128)(2,1)}, u32[]{:S(2)}) copy-start(bf16[128,2048]{1,0:T(8,128)(2,1)} %refs_0_.6) | copy-start | bytes 1572868
  20.6 8.1 %copy-start.1 = (bf16[128,2048]{1,0:T(8,128)(2,1)S(1)}, bf16[128,2048]{1,0:T(8,128)(2,1)}, u32[]{:S(2)}) copy-start(bf16[128,2048]{1,0:T(8,128)(2,1)} %refs_1_.6) | copy-start | bytes 1572868
  20.8 0.8 copy-start.6
  21.6 7.4 %copy-start.7 = (s32[2048]{0:T(1024)S(1)}, s32[2048]{0:T(1024)}, u32[]{:S(2)}) copy-start(s32[2048]{0:T(1024)} %param.9) | copy-start | bytes 24580
  21.6 6.8 %collective-permute-start.4 = (bf16[2,2,128,256]{3,2,1,0:T(8,128)(2,1)}, bf16[2,2,128,256]{3,2,1,0:T(8,128)(2,1)S(1)}, u32[]{:S(2)}, u32[]{:S(2)}) collective-permute-start(bf16[2,2,128,256]{3,2,1,0:T(8,128)(2,1)} %get-tuple-element.28), channel_id=1, source_target_pairs={{0,1},{1,0},{2,3},{3,2},{4,5},{5,4},{6,7},{7,6},{8,9},{9,8},{10,11... | collective-permute-start | bytes 786440 | tf_op jit(solution)/shard_map/ppermute | solution.py:30
  22.1 9.7 %collective-permute-start.1 = (bf16[2,2,128,256]{3,2,1,0:T(8,128)(2,1)}, bf16[2,2,128,256]{3,2,1,0:T(8,128)(2,1)S(1)}, u32[]{:S(2)}, u32[]{:S(2)}) collective-permute-start(bf16[2,2,128,256]{3,2,1,0:T(8,128)(2,1)} %copy-done.6), channel_id=1, source_target_pairs={{0,2},{2,0},{1,3},{3,1},{4,6},{6,4},{5,7},{7,5},{8,10},{10,8},{9,1... | collective-permute-start | bytes 786440 | tf_op jit(solution)/shard_map/ppermute | solution.py:26
  25.0 10.6 %collective-permute-start.2 = (bf16[2,2,128,256]{3,2,1,0:T(8,128)(2,1)S(1)}, bf16[2,2,128,256]{3,2,1,0:T(8,128)(2,1)S(1)}, u32[]{:S(2)}, u32[]{:S(2)}) collective-permute-start(bf16[2,2,128,256]{3,2,1,0:T(8,128)(2,1)S(1)} %head_parts.8.refs_1_), channel_id=1, source_target_pairs={{0,4},{4,8},{8,12},{1,5},{5,9},{9,13},{2,6},{6,10},{10,14},{3,7},{... | collective-permute-start | bytes 786440 | tf_op jit(solution)/shard_map/ppermute | solution.py:21
  28.9 6.7 %collective-permute-start.8 = (bf16[2,2,128,256]{3,2,1,0:T(8,128)(2,1)S(1)}, bf16[2,2,128,256]{3,2,1,0:T(8,128)(2,1)S(1)}, u32[]{:S(2)}, u32[]{:S(2)}) collective-permute-start(bf16[2,2,128,256]{3,2,1,0:T(8,128)(2,1)S(1)} %get-tuple-element.36), channel_id=1, source_target_pairs={{0,1},{1,0},{2,3},{3,2},{4,5},{5,4},{6,7},{7,6},{8,9},{9,8},{10,11... | collective-permute-start | bytes 786440 | tf_op jit(solution)/shard_map/ppermute | solution.py:30
  29.1 16.3 %collective-permute-start.5 = (bf16[2,2,128,256]{3,2,1,0:T(8,128)(2,1)S(1)}, bf16[2,2,128,256]{3,2,1,0:T(8,128)(2,1)S(1)}, u32[]{:S(2)}, u32[]{:S(2)}) collective-permute-start(bf16[2,2,128,256]{3,2,1,0:T(8,128)(2,1)S(1)} %head_parts.11), channel_id=1, source_target_pairs={{0,2},{2,0},{1,3},{3,1},{4,6},{6,4},{5,7},{7,5},{8,10},{10,8},{9,1... | collective-permute-start | bytes 786440 | tf_op jit(solution)/shard_map/ppermute | solution.py:26
  31.8 9.0 %collective-permute-start.3 = (bf16[2,2,128,256]{3,2,1,0:T(8,128)(2,1)S(1)}, bf16[2,2,128,256]{3,2,1,0:T(8,128)(2,1)S(1)}, u32[]{:S(2)}, u32[]{:S(2)}) collective-permute-start(bf16[2,2,128,256]{3,2,1,0:T(8,128)(2,1)S(1)} %collective-permute-done.1.refs_2_.refs_0_), channel_id=1, source_target_pairs={{0,4},{4,8},{8,12},{1,5},{5,9},{9,13},{2,6},{6,10},{10,14},{3,7},{... | collective-permute-start | bytes 786440 | tf_op jit(solution)/shard_map/ppermute | solution.py:21
  35.8 11.4 %collective-permute-start.9 = (bf16[2,2,128,256]{3,2,1,0:T(8,128)(2,1)S(1)}, bf16[2,2,128,256]{3,2,1,0:T(8,128)(2,1)S(1)}, u32[]{:S(2)}, u32[]{:S(2)}) collective-permute-start(bf16[2,2,128,256]{3,2,1,0:T(8,128)(2,1)S(1)} %head_parts.13), channel_id=1, source_target_pairs={{0,2},{2,0},{1,3},{3,1},{4,6},{6,4},{5,7},{7,5},{8,10},{10,8},{9,1... | collective-permute-start | bytes 786440 | tf_op jit(solution)/shard_map/ppermute | solution.py:26
  38.1 7.3 %collective-permute-start.12 = (bf16[2,2,128,256]{3,2,1,0:T(8,128)(2,1)S(1)}, bf16[2,2,128,256]{3,2,1,0:T(8,128)(2,1)S(1)}, u32[]{:S(2)}, u32[]{:S(2)}) collective-permute-start(bf16[2,2,128,256]{3,2,1,0:T(8,128)(2,1)S(1)} %get-tuple-element.38), channel_id=1, source_target_pairs={{0,1},{1,0},{2,3},{3,2},{4,5},{5,4},{6,7},{7,6},{8,9},{9,8},{10,11... | collective-permute-start | bytes 786440 | tf_op jit(solution)/shard_map/ppermute | solution.py:30
  41.0 16.5 %collective-permute-start.10 = (bf16[2,2,128,256]{3,2,1,0:T(8,128)(2,1)S(1)}, bf16[2,2,128,256]{3,2,1,0:T(8,128)(2,1)S(1)}, u32[]{:S(2)}, u32[]{:S(2)}) collective-permute-start(bf16[2,2,128,256]{3,2,1,0:T(8,128)(2,1)S(1)} %head_parts.12.refs_1_), channel_id=1, source_target_pairs={{0,4},{4,8},{8,12},{1,5},{5,9},{9,13},{2,6},{6,10},{10,14},{3,7},{... | collective-permute-start | bytes 786440 | tf_op jit(solution)/shard_map/ppermute | solution.py:21
  45.6 11.9 %collective-permute-start.13 = (bf16[2,2,128,256]{3,2,1,0:T(8,128)(2,1)S(1)}, bf16[2,2,128,256]{3,2,1,0:T(8,128)(2,1)S(1)}, u32[]{:S(2)}, u32[]{:S(2)}) collective-permute-start(bf16[2,2,128,256]{3,2,1,0:T(8,128)(2,1)S(1)} %head_parts.15), channel_id=1, source_target_pairs={{0,2},{2,0},{1,3},{3,1},{4,6},{6,4},{5,7},{7,5},{8,10},{10,8},{9,1... | collective-permute-start | bytes 786440 | tf_op jit(solution)/shard_map/ppermute | solution.py:26
  47.2 10.3 %collective-permute-start.11 = (bf16[2,2,128,256]{3,2,1,0:T(8,128)(2,1)S(1)}, bf16[2,2,128,256]{3,2,1,0:T(8,128)(2,1)S(1)}, u32[]{:S(2)}, u32[]{:S(2)}) collective-permute-start(bf16[2,2,128,256]{3,2,1,0:T(8,128)(2,1)S(1)} %collective-permute-done.9.refs_2_), channel_id=1, source_target_pairs={{0,4},{4,8},{8,12},{1,5},{5,9},{9,13},{2,6},{6,10},{10,14},{3,7},{... | collective-permute-start | bytes 786440 | tf_op jit(solution)/shard_map/ppermute | solution.py:21
  55.9 16.8 %collective-permute-start.6 = (bf16[2,2,2,128,256]{4,3,2,1,0:T(8,128)(2,1)S(1)}, bf16[2,2,2,128,256]{4,3,2,1,0:T(8,128)(2,1)S(1)}, u32[]{:S(2)}, u32[]{:S(2)}) collective-permute-start(bf16[2,2,2,128,256]{4,3,2,1,0:T(8,128)(2,1)S(1)} %get-tuple-element.31), channel_id=1, source_target_pairs={{4,0},{8,4},{12,8},{5,1},{9,5},{13,9},{6,2},{10,6},{14,10},{7,3},{... | collective-permute-start | bytes 1572872 | tf_op jit(solution)/shard_map/ppermute | solution.py:21
  61.8 18.4 %collective-permute-start.14 = (bf16[2,2,2,128,256]{4,3,2,1,0:T(8,128)(2,1)S(1)}, bf16[2,2,2,128,256]{4,3,2,1,0:T(8,128)(2,1)S(1)}, u32[]{:S(2)}, u32[]{:S(2)}) collective-permute-start(bf16[2,2,2,128,256]{4,3,2,1,0:T(8,128)(2,1)S(1)} %get-tuple-element.41), channel_id=1, source_target_pairs={{4,0},{8,4},{12,8},{5,1},{9,5},{13,9},{6,2},{10,6},{14,10},{7,3},{... | collective-permute-start | bytes 1572872 | tf_op jit(solution)/shard_map/ppermute | solution.py:21
  72.8 9.2 %collective-permute-start.7 = (bf16[3,2,128,256]{3,2,1,0:T(8,128)(2,1)S(1)}, bf16[3,2,128,256]{3,2,1,0:T(8,128)(2,1)S(1)}, u32[]{:S(2)}, u32[]{:S(2)}) collective-permute-start(bf16[3,2,128,256]{3,2,1,0:T(8,128)(2,1)S(1)} %get-tuple-element.33), channel_id=1, source_target_pairs={{0,2},{2,0},{1,3},{3,1},{4,6},{6,4},{5,7},{7,5},{8,10},{10,8},{9,1... | collective-permute-start | bytes 1179656 | tf_op jit(solution)/shard_map/ppermute | solution.py:26
  80.3 8.8 %collective-permute-start.15 = (bf16[3,2,128,256]{3,2,1,0:T(8,128)(2,1)S(1)}, bf16[3,2,128,256]{3,2,1,0:T(8,128)(2,1)S(1)}, u32[]{:S(2)}, u32[]{:S(2)}) collective-permute-start(bf16[3,2,128,256]{3,2,1,0:T(8,128)(2,1)S(1)} %get-tuple-element.43), channel_id=1, source_target_pairs={{0,2},{2,0},{1,3},{3,1},{4,6},{6,4},{5,7},{7,5},{8,10},{10,8},{9,1... | collective-permute-start | bytes 1179656 | tf_op jit(solution)/shard_map/ppermute | solution.py:26
  82.4 7.2 %collective-permute-start.16 = (bf16[3,2,128,256]{3,2,1,0:T(8,128)(2,1)S(1)}, bf16[3,2,128,256]{3,2,1,0:T(8,128)(2,1)S(1)}, u32[]{:S(2)}, u32[]{:S(2)}) collective-permute-start(bf16[3,2,128,256]{3,2,1,0:T(8,128)(2,1)S(1)} %get-tuple-element.45), channel_id=1, source_target_pairs={{0,1},{1,0},{2,3},{3,2},{4,5},{5,4},{6,7},{7,6},{8,9},{9,8},{10,11... | collective-permute-start | bytes 1179656 | tf_op jit(solution)/shard_map/ppermute | solution.py:30
  89.4 1.8 %collective-permute-start.17 = (bf16[3,2,128,256]{3,2,1,0:T(8,128)(2,1)S(1)}, bf16[3,2,128,256]{3,2,1,0:T(8,128)(2,1)S(1)}, u32[]{:S(2)}, u32[]{:S(2)}) collective-permute-start(bf16[3,2,128,256]{3,2,1,0:T(8,128)(2,1)S(1)} %get-tuple-element.46), channel_id=1, source_target_pairs={{0,1},{1,0},{2,3},{3,2},{4,5},{5,4},{6,7},{7,6},{8,9},{9,8},{10,11... | collective-permute-start | bytes 1179656 | tf_op jit(solution)/shard_map/ppermute | solution.py:30

commit v3 on v2

v3 whole, which is shorter than its diff:
```python
import math

import jax
import jax.numpy as jnp
from jax import lax
from jax.experimental import pallas as pl
from jax.experimental.pallas import tpu as pltpu
from jax.sharding import PartitionSpec as P

HD = 128
NEG_FILL = -1e30
LOW = jnp.bfloat16
WIDE = jnp.float32
MIB = 1024 * 1024
TO_BITS = HD ** (-0.5) / math.log(2.0)
SCALE = HD ** (-0.5)
ROWS_BY_ROWS = (((1,), (1,)), ((), ()))


def chunks_of(heads):
    return [1] * heads


def neighbours(value, first):
    peers = lax.axis_size("blk")
    pairs = []
    for i in range(peers):
        other = i + 1 if (i % 2 == 0) == first else i - 1
        pairs.append((i, other if 0 <= other < peers else i))
    return lax.ppermute(value, "blk", pairs)


def from_later(value):
    peers = lax.axis_size("blk")
    return lax.ppermute(value, "blk", [(i, (i - 1) % peers) for i in range(peers)])


def round_sub(value, by):
    peers = lax.axis_size("sub")
    return lax.ppermute(value, "sub", [(i, (i + by) % peers) for i in range(peers)])


def swapped(value):
    return lax.ppermute(value, "pair", [(0, 1), (1, 0)])


def run_moves(moves, sems):
    copies = [pltpu.make_async_copy(src, dst, sems.at[at]) for at, (src, dst) in enumerate(moves)]
    for copy in copies:
        copy.start()
    for copy in copies:
        copy.wait()


def call(kernel, ins, outs, scratch, name, whole=False, flops=0, room=8 * MIB):
    spec = pl.BlockSpec(memory_space=pltpu.VMEM if whole else pl.ANY)
    moved = sum(math.prod(a.shape) * a.dtype.itemsize for a in list(ins) + list(outs))
    return list(
        pl.pallas_call(
            kernel,
            out_shape=outs,
            in_specs=[spec] * len(ins),
            out_specs=[spec] * len(outs),
            scratch_shapes=scratch,
            name=name,
            cost_estimate=pl.CostEstimate(flops=flops, bytes_accessed=moved, transcendentals=0),
            compiler_params=pltpu.CompilerParams(vmem_limit_bytes=room),
        )(*ins)
    )


def shape(*dims, dtype=LOW):
    return jax.ShapeDtypeStruct(dims, dtype)


def first_parts(arrays, low, high):
    count = len(arrays)
    rows, width = arrays[0].shape
    half = width // 2
    peers = lax.axis_size("sub")
    part = half // peers

    def kernel(*refs):
        ins, outs, sems = refs[:count], refs[count:-1], refs[-1]
        p = lax.axis_index("pair")
        moves = []
        for side, out in zip((1 - p, p), outs):
            for at in range(peers):
                start = pl.multiple_of(side * half + at * part + low, HD)
                moves += [(ref.at[:, pl.ds(start, high - low)], out.at[i, at]) for i, ref in enumerate(ins)]
        run_moves(moves, sems)

    outs = [pltpu.VMEM((count, peers, rows, high - low), LOW)] * 2
    spec = pl.BlockSpec(memory_space=pl.ANY)
    held = [pltpu.with_memory_space_constraint(array, pltpu.HBM) for array in arrays]
    return pl.pallas_call(
        kernel,
        out_shape=outs,
        in_specs=[spec] * count,
        out_specs=[spec] * 2,
        scratch_shapes=[pltpu.SemaphoreType.DMA((2 * peers * count,))],
        name="first_parts",
        compiler_params=pltpu.CompilerParams(vmem_limit_bytes=8 * MIB),
    )(*held)


def head_parts(own, paired, low, cut, after):
    count, peers, rows, _ = own.shape

    def kernel(own_ref, pair_ref, *refs):
        outs, sems = refs[len(after):-1], refs[-1]
        p, s = lax.axis_index("pair"), lax.axis_index("sub")
        columns = pl.ds(low, cut)
        moves = []
        for by, out in enumerate(outs, 1):
            at = lax.rem(s + by, peers)
            moves += [(own_ref.at[:, at, :, columns], out.at[:, p]), (pair_ref.at[:, at, :, columns], out.at[:, 1 - p])]
        run_moves(moves, sems)

    outs = [shape(count, 2, rows, cut)] * (peers - 1)
    scratch = [pltpu.SemaphoreType.DMA((2 * peers,))]
    return call(kernel, [own, paired] + after, outs, scratch, "head_parts")


def joined(own, paired, received, low, cut, after):
    count, peers, rows, _ = own.shape

    def kernel(own_ref, pair_ref, *refs):
        rec, (here, first, second), sems = refs[:peers - 1], refs[-4:-1], refs[-1]
        p, s = lax.axis_index("pair"), lax.axis_index("sub")
        odd = lax.rem(lax.axis_index("blk"), 2)
        columns = pl.ds(low, cut)
        moves = []
        for out, start, size in ((first, 2 * odd, 2), (second, 2 - 2 * odd, 2), (here, 0, 4)):
            which = pl.ds(start, size)
            moves.append((own_ref.at[which, s, :, columns], out.at[:, p, s]))
            moves.append((pair_ref.at[which, s, :, columns], out.at[:, 1 - p, s]))
            for by, ref in enumerate(rec, 1):
                moves.append((ref.at[which], out.at[:, :, lax.rem(s - by + peers, peers)]))
        run_moves(moves, sems)

    outs = [shape(count, 2, peers, rows, cut)] + [shape(2, 2, peers, rows, cut)] * 2
    scratch = [pltpu.SemaphoreType.DMA((3 * (peers + 1),))]
    return call(kernel, [own, paired] + received + after, outs, scratch, "joined")


def taken(odd, when_odd, otherwise, held, sem):
    @pl.when(odd == 1)
    def _():
        run_moves([(when_odd, held)], sem)

    @pl.when(odd == 0)
    def _():
        run_moves([(otherwise, held)], sem)


def query_grads(bias, here, first, second):
    _, _, peers, rows, cut = here.shape
    heads = cut // HD
    strip = rows * peers

    def kernel(bias_ref, here_ref, first_ref, second_ref, dq_out, kv_out, stats_out, early, sem):
        taken(lax.rem(lax.axis_index("blk"), 2), first_ref, second_ref, early, sem)
        stats_out[...] = jnp.zeros_like(stats_out)
        for head in range(heads):
            columns = pl.ds(head * HD, HD)

            def flat(ref, which, tiles):
                block = ref[which, tiles, :, :, columns]
                return block.reshape(block.shape[0] * strip, HD)

            own_terms = []
            for tile in range(2):
                before, upto, at = pl.ds(tile, 2 - tile), pl.ds(0, tile + 1), pl.ds(tile, 1)
                q, g = flat(here_ref, 2, at), flat(here_ref, 3, at)
                k = jnp.concatenate([flat(early, 0, before), flat(here_ref, 0, upto)], axis=0)
                v = jnp.concatenate([flat(early, 1, before), flat(here_ref, 1, upto)], axis=0)
                scores = lax.dot_general(k, q, ROWS_BY_ROWS, preferred_element_type=WIDE) * TO_BITS + bias_ref[tile]
                peak = jnp.max(scores, axis=0, keepdims=True)
                weight = jnp.exp2(scores - peak)
                total = jnp.sum(weight, axis=0, keepdims=True)
                prob = weight * (1.0 / total)
                prob_low = prob.astype(LOW)
                grad_prob = lax.dot_general(v, g, ROWS_BY_ROWS, preferred_element_type=WIDE)
                row_dot = jnp.sum(prob_low.astype(WIDE) * grad_prob, axis=0, keepdims=True)
                score_low = (prob * (grad_prob - row_dot)).astype(LOW)
                stats_out[head, 2 * tile:2 * tile + 1] = peak + jnp.log2(total)
                stats_out[head, 2 * tile + 1:2 * tile + 2] = row_dot
                dq = jnp.dot(k.T, score_low, preferred_element_type=WIDE) * SCALE
                dq_out[tile, :, :, columns] = dq.T.astype(LOW).reshape(peers, rows, HD)
                skip = (2 - tile) * strip
                dk = jnp.dot(score_low[skip:], q, preferred_element_type=WIDE)
                dv = jnp.dot(prob_low[skip:], g, preferred_element_type=WIDE)
                own_terms.append((dk, dv))
            for which in range(2):
                low, high = own_terms[0][which], own_terms[1][which]
                kv_out[which, 0, :, :, columns] = (low + high[:strip]).reshape(peers, rows, HD)
                kv_out[which, 1, :, :, columns] = high[strip:].reshape(peers, rows, HD)

    outs = [
        shape(2, peers, rows, cut),
        shape(2, 2, peers, rows, cut, dtype=WIDE),
        shape(heads, 8, strip, dtype=WIDE),
    ]
    scratch = [pltpu.VMEM((2, 2, peers, rows, cut), LOW), pltpu.SemaphoreType.DMA((1,))]
    flops = heads * 2 * 5 * 2 * strip * 3 * strip * HD
    ins = [bias, here, first, second]
    return call(kernel, ins, outs, scratch, "query_grads", whole=True, flops=flops, room=40 * MIB)


def key_grads(bias, here, first, second, stats, dq, own):
    _, _, peers, rows, cut = here.shape
    heads = cut // HD
    strip = rows * peers

    def kernel(bias_ref, here_ref, first_ref, second_ref, stats_ref, dq_ref, own_ref, *refs):
        outs, (later, grads, sem) = refs[:peers], refs[peers:]
        s = lax.axis_index("sub")
        taken(lax.rem(lax.axis_index("blk"), 2), second_ref, first_ref, later, sem)
        for head in range(heads):
            columns = pl.ds(head * HD, HD)

            def flat(ref, which, tiles):
                block = ref[which, tiles, :, :, columns]
                return block.reshape(block.shape[0] * strip, HD)

            terms = []
            for tile in range(2):
                span = (2 - tile) * strip
                tiles, at = pl.ds(tile, 2 - tile), pl.ds(tile, 1)
                q, g = flat(later, 0, at), flat(later, 1, at)
                k, v = flat(here_ref, 0, tiles), flat(here_ref, 1, tiles)
                scores = lax.dot_general(k, q, ROWS_BY_ROWS, preferred_element_type=WIDE) * TO_BITS
                prob = jnp.exp2(scores + bias_ref[tile, :span] - stats_ref[head, 2 * tile:2 * tile + 1])
                grad_prob = lax.dot_general(v, g, ROWS_BY_ROWS, preferred_element_type=WIDE)
                score_low = (prob * (grad_prob - stats_ref[head, 2 * tile + 1:2 * tile + 2])).astype(LOW)
                dk = jnp.dot(score_low, q, preferred_element_type=WIDE)
                dv = jnp.dot(prob.astype(LOW), g, preferred_element_type=WIDE)
                terms.append((dk, dv))
            for which in range(2):
                scale = SCALE if which == 0 else 1.0
                wide, narrow = terms[0][which], terms[1][which]
                for tile, term in ((0, wide[:strip]), (1, wide[strip:] + narrow)):
                    term = own_ref[which, tile, :, :, columns] + term.reshape(peers, rows, HD)
                    grads[which, tile, :, :, columns] = (term * scale).astype(LOW)
        for by, out in enumerate(outs):
            at = lax.rem(s + by, peers)
            for row in range(2):
                out[0, row] = dq_ref[row, at]
                for which in range(2):
                    out[1 + which, row] = grads[which, row, at]

    outs = [shape(3, 2, rows, cut)] * peers
    held = pltpu.VMEM((2, 2, peers, rows, cut), LOW)
    scratch = [held, held, pltpu.SemaphoreType.DMA((1,))]
    flops = heads * 4 * 2 * 3 * strip * strip * HD
    ins = [bias, here, first, second, stats, dq, own]
    return call(kernel, ins, outs, scratch, "key_grads", whole=True, flops=flops, room=40 * MIB)


def rows_for_pair(parts):
    peers = len(parts)
    _, _, rows, cut = parts[0].shape

    def kernel(*refs):
        ins, (send, keep), sems = refs[:peers], refs[peers:-1], refs[-1]
        p, s = lax.axis_index("pair"), lax.axis_index("sub")
        moves = []
        for by, ref in enumerate(ins):
            at = lax.rem(s - by + peers, peers)
            moves += [(ref.at[:, 1 - p], send.at[:, at]), (ref.at[:, p], keep.at[:, at])]
        run_moves(moves, sems)

    outs = [shape(3, peers, rows, cut)] * 2
    return call(kernel, parts, outs, [pltpu.SemaphoreType.DMA((2 * peers,))], "rows_for_pair")


def laid_out(kept, paired, spans):
    _, peers, rows, _ = kept[0].shape
    part = spans[-1][1]
    half = part * peers
    count = len(spans)

    def kernel(*refs):
        keep, rec, outs, sems = refs[:count], refs[count:2 * count], refs[2 * count:-1], refs[-1]
        p = lax.axis_index("pair")
        moves = []
        for mine, theirs, (low, high) in zip(keep, rec, spans):
            for source, side in ((mine, p), (theirs, 1 - p)):
                for at in range(peers):
                    columns = pl.ds(pl.multiple_of(side * half + at * part + low, HD), high - low)
                    moves += [(source.at[which, at], out.at[:, columns]) for which, out in enumerate(outs)]
        run_moves(moves, sems)

    outs = [shape(rows, 2 * half)] * 3
    return call(kernel, kept + paired, outs, [pltpu.SemaphoreType.DMA((6 * count * peers,))], "laid_out")


def allowed_bias(session, rows):
    strip = rows * lax.axis_size("sub")
    block = 2 * strip
    at_block = lax.axis_index("blk")
    margin = jnp.zeros((block,), jnp.int32)
    window = jnp.concatenate([margin, session, margin])
    sess = lax.dynamic_slice_in_dim(window, at_block * block, 3 * block)
    place = (at_block - 1) * block + jnp.arange(3 * block, dtype=jnp.int32)

    def tile_bias(q_tile, k_tile, tiles):
        q_at = slice(q_tile * strip, (q_tile + 1) * strip)
        k_at = slice(k_tile * strip, (k_tile + tiles) * strip)
        k_place, q_place = place[k_at, None], place[None, q_at]
        allowed = (sess[None, q_at] == sess[k_at, None]) & (k_place <= q_place)
        allowed = allowed & (k_place >= 0) & (q_place < session.shape[0])
        return jnp.where(allowed, 0.0, NEG_FILL)

    for_queries = jnp.stack([tile_bias(2, 0, 3), tile_bias(3, 1, 3)])
    for_keys = jnp.stack([tile_bias(4, 2, 2), tile_bias(5, 3, 2)])
    return for_queries, for_keys


def shards(queries, keys, values, out_grad, session):
    peers = lax.axis_size("sub")
    others = range(1, peers)
    arrays = [keys, values, queries, out_grad]
    part = queries.shape[1] // (2 * peers)
    spans, at = [], 0
    for heads in chunks_of(part // HD):
        spans.append((at, at + heads * HD))
        at += heads * HD
    split = spans[0][1]
    fetched = []
    for low, high in ((0, split), (split, part)):
        send, own = first_parts(arrays, low, high)
        fetched.append((low, own, swapped(send)))
    query_bias, key_bias = allowed_bias(session, queries.shape[0])
    kept, paired = [], []
    arrived, exchanged, totals = [[], []], [[], [], []], [[], []]
    for index, (low, high) in enumerate(spans):
        base, own, pair_own = fetched[min(index, 1)]
        low, cut = low - base, high - low
        sends = head_parts(own, pair_own, low, cut, arrived[index] + exchanged[index])
        received = [round_sub(value, by) for by, value in zip(others, sends)]
        arrived.append(received)
        here, first, second = joined(own, pair_own, received, low, cut, totals[index])
        first, second = neighbours(first, True), neighbours(second, False)
        exchanged.append([first, second])
        dq, grads, stats = query_grads(query_bias, here, first, second)
        totals.append([stats])
        parts = key_grads(key_bias, here, first, second, from_later(stats), dq, grads)
        send, keep = rows_for_pair([parts[0]] + [round_sub(parts[by], by) for by in others])
        kept.append(keep)
        paired.append(swapped(send))
    return tuple(laid_out(kept, paired, spans))


def solution(mesh):
    spread = P(("grp", "blk", "pair", "sub"), None)
    return jax.shard_map(
        shards, mesh=mesh, in_specs=(spread,) * 4 + (P("grp"),), out_specs=(spread,) * 3, check_vma=False
    )
```

time: 92.8 us -> 76.6 us (0.83)
  Pallas kernels: 30.5 us -> 17.7 us
  waiting for transfers between devices: 31.5 us -> 20.7 us
  starting transfers between devices: 27.6 us -> 35.2 us
  local copies, waits for them, and re-layouts: 1.09 us -> 0.04 us
    ppermute x6 -> x12, waiting for transfers between devices: 19 us -> 2.64 us  [the longest x4 2.62 us: from_later(): lax.ppermute(value, 'blk', [(i, (i - 1) % peers) for i in range(peers)])]
    pallas_call x19 -> x23, Pallas kernels: 30.5 us -> 17.7 us  [the longest x21 15 us: call(): pl.pallas_call(kernel, out_shape=outs, in_specs=[spec] * len(ins), out_sp...]
    ppermute x6 -> x8, waiting for transfers between devices: 9.39 us -> 16.6 us  [round_sub(): lax.ppermute(value, 'sub', [(i, (i + by) % peers) for i in range(peers)])]
    ppermute x6 -> x12, starting transfers between devices: 17.7 us -> 22.5 us  [the longest x8 14.3 us: neighbours(): return lax.ppermute(value, 'blk', pairs)]
    ppermute x6 -> x8, starting transfers between devices: 8.69 us -> 11.4 us  [round_sub(): lax.ppermute(value, 'sub', [(i, (i + by) % peers) for i in range(peers)])]
    ppermute x6, waiting for transfers between devices: 3.08 us -> 1.41 us  [swapped(): return lax.ppermute(value, 'pair', [(0, 1), (1, 0)])]
    unnamed x16 -> x2, local copies, waits for them, and re-layouts: 0.98 us -> 0.01 us
  transfers between devices with their start and end apart: 18 -> 26, of which waited for: 8 -> 6; matrix products, arithmetic and copies ran while one was open for 1% -> 2% of each run, Pallas kernels for 12% -> 20%
where the time goes in v3:
time: 76.6 us; the launch traced here: 76.3 us
  starting transfers between devices  35.2 us (46%)
  waiting for transfers between devices  20.7 us (27%)
  Pallas kernels  17.7 us (23%)
  other arithmetic  1.43 us (2%)
  between operations  1.21 us (2%)
    ppermute x8, waiting for transfers between devices, round_sub(): lax.ppermute(value, 'sub', [(i, (i + by) % peers) for i in range(peers)])  16.6 us
    pallas_call x21, Pallas kernels, call(): pl.pallas_call(kernel, out_shape=outs, in_specs=[spec] * len(ins), out_sp...  15 us
    ppermute x8, starting transfers between devices, neighbours(): return lax.ppermute(value, 'blk', pairs)  14.3 us
    ppermute x8, starting transfers between devices, round_sub(): lax.ppermute(value, 'sub', [(i, (i + by) % peers) for i in range(peers)])  11.4 us
    ppermute x4, starting transfers between devices, from_later(): lax.ppermute(value, 'blk', [(i, (i - 1) % peers) for i in range(peers)])  8.11 us
    pallas_call x2, Pallas kernels, first_parts(): pl.pallas_call(kernel, out_shape=outs, in_specs=[spec] * count, out_specs...  2.76 us
    ppermute x4, waiting for transfers between devices, from_later(): lax.ppermute(value, 'blk', [(i, (i - 1) % peers) for i in range(peers)])  2.62 us
  transfers between devices with their start and end apart: 26, of which 6 were waited for; matrix products, arithmetic and copies ran while one was open for 2% of the time, Pallas kernels for 20%

profile of v3, /device:TPU:0, one launch (start us, length us, event | category | flops | bytes accessed | tf_op | source)
XLA Modules:
  0.0 76.3 jit_solution(7828115273647794598)
XLA Ops:
  0.6 1.2 %first_parts.2 = (bf16[4,2,128,128]{3,2,1,0:T(8,128)(2,1)S(1)}, bf16[4,2,128,128]{3,2,1,0:T(8,128)(2,1)S(1)}) custom-call(bf16[128,2048]{1,0:T(8,128)(2,1)} %refs_0_.3, bf16[128,2048]{1,0:T(8,128)(2,1)} %refs_1_.3, bf16[128,2048]{1,0:T(8,128)(2,1)} %refs_2_.3, bf16[128,2048]{1,0:T(8,128)(2,1)} %refs_3_.3), custom_call_target="tpu_custom_call" | custom-call | tf_op jit(solution)/shard_map/first_parts/pallas_call | solution.py:96
  1.8 0.5 collective-permute-start
  2.3 1.6 %first_parts.3 = (bf16[4,2,128,384]{3,2,1,0:T(8,128)(2,1)S(1)}, bf16[4,2,128,384]{3,2,1,0:T(8,128)(2,1)S(1)}) custom-call(bf16[128,2048]{1,0:T(8,128)(2,1)} %refs_0_.3, bf16[128,2048]{1,0:T(8,128)(2,1)} %refs_1_.3, bf16[128,2048]{1,0:T(8,128)(2,1)} %refs_2_.3, bf16[128,2048]{1,0:T(8,128)(2,1)} %refs_3_.3), custom_call_target="tpu_custom_call" | custom-call | tf_op jit(solution)/shard_map/first_parts/pallas_call | solution.py:96
  4.4 3.0 %collective-permute-start.1 = (bf16[4,2,128,128]{3,2,1,0:T(8,128)(2,1)S(1)}, bf16[4,2,128,128]{3,2,1,0:T(8,128)(2,1)S(1)}, u32[]{:S(2)}, u32[]{:S(2)}) collective-permute-start(bf16[4,2,128,128]{3,2,1,0:T(8,128)(2,1)S(1)} %head_parts.4), channel_id=1, source_target_pairs={{0,2},{2,0},{1,3},{3,1},{4,6},{6,4},{5,7},{7,5},{8,10},{10,8},{9,1... | collective-permute-start | bytes 786440 | tf_op jit(solution)/shard_map/ppermute | solution.py:40
  7.4 6.5 %collective-permute-done.1.refs_0_ = bf16[4,2,128,128]{3,2,1,0:T(8,128)(2,1)S(1)} collective-permute-done((bf16[4,2,128,128]{3,2,1,0:T(8,128)(2,1)S(1)}, bf16[4,2,128,128]{3,2,1,0:T(8,128)(2,1)S(1)}, u32[]{:S(2)}, u32[]{:S(2)}) %collective-permute-start.1) | collective-permute-done | bytes 262176 | tf_op jit(solution)/shard_map/ppermute | solution.py:40
  13.9 0.4 joined.4
  14.3 1.9 %collective-permute-start.2 = (bf16[2,2,2,128,128]{4,3,2,1,0:T(8,128)(2,1)S(1)}, bf16[2,2,2,128,128]{4,3,2,1,0:T(8,128)(2,1)S(1)}, u32[]{:S(2)}, u32[]{:S(2)}) collective-permute-start(bf16[2,2,2,128,128]{4,3,2,1,0:T(8,128)(2,1)S(1)} %get-tuple-element.50), channel_id=1, source_target_pairs={{0,4},{4,0},{8,12},{12,8},{1,5},{5,1},{9,13},{13,9},{2,6},{6,2},{1... | collective-permute-start | bytes 786440 | tf_op jit(solution)/shard_map/ppermute | solution.py:30
  16.2 0.7 collective-permute-start.3
  17.0 1.6 %collective-permute-start.7 = (bf16[4,2,128,128]{3,2,1,0:T(8,128)(2,1)S(1)}, bf16[4,2,128,128]{3,2,1,0:T(8,128)(2,1)S(1)}, u32[]{:S(2)}, u32[]{:S(2)}) collective-permute-start(bf16[4,2,128,128]{3,2,1,0:T(8,128)(2,1)S(1)} %head_parts.5), channel_id=1, source_target_pairs={{0,2},{2,0},{1,3},{3,1},{4,6},{6,4},{5,7},{7,5},{8,10},{10,8},{9,1... | collective-permute-start | bytes 786440 | tf_op jit(solution)/shard_map/ppermute | solution.py:40
  18.6 0.7 and_select_fusion
  19.4 0.6 collective-permute-start.12
  20.0 6.4 %collective-permute-done.7.refs_0_ = bf16[4,2,128,128]{3,2,1,0:T(8,128)(2,1)S(1)} collective-permute-done((bf16[4,2,128,128]{3,2,1,0:T(8,128)(2,1)S(1)}, bf16[4,2,128,128]{3,2,1,0:T(8,128)(2,1)S(1)}, u32[]{:S(2)}, u32[]{:S(2)}) %collective-permute-start.7) | collective-permute-done | bytes 262176 | tf_op jit(solution)/shard_map/ppermute | solution.py:40
  26.3 0.3 joined.5
  26.6 4.4 %collective-permute-start.8 = (bf16[2,2,2,128,128]{4,3,2,1,0:T(8,128)(2,1)S(1)}, bf16[2,2,2,128,128]{4,3,2,1,0:T(8,128)(2,1)S(1)}, u32[]{:S(2)}, u32[]{:S(2)}) collective-permute-start(bf16[2,2,2,128,128]{4,3,2,1,0:T(8,128)(2,1)S(1)} %get-tuple-element.61), channel_id=1, source_target_pairs={{0,4},{4,0},{8,12},{12,8},{1,5},{5,1},{9,13},{13,9},{2,6},{6,2},{1... | collective-permute-start | bytes 786440 | tf_op jit(solution)/shard_map/ppermute | solution.py:30
  31.1 0.7 collective-permute-start.9
  31.9 1.6 %collective-permute-start.17 = (bf16[4,2,128,128]{3,2,1,0:T(8,128)(2,1)S(1)}, bf16[4,2,128,128]{3,2,1,0:T(8,128)(2,1)S(1)}, u32[]{:S(2)}, u32[]{:S(2)}) collective-permute-start(bf16[4,2,128,128]{3,2,1,0:T(8,128)(2,1)S(1)} %head_parts.7), channel_id=1, source_target_pairs={{0,2},{2,0},{1,3},{3,1},{4,6},{6,4},{5,7},{7,5},{8,10},{10,8},{9,1... | collective-permute-start | bytes 786440 | tf_op jit(solution)/shard_map/ppermute | solution.py:40
  33.6 1.9 %query_grads.4 = (bf16[2,2,128,128]{3,2,1,0:T(8,128)(2,1)S(1)}, f32[2,2,2,128,128]{4,3,2,1,0:T(8,128)S(1)}, f32[1,8,256]{2,1,0:T(8,128)S(1)}) custom-call(f32[2,768,256]{2,1,0:T(8,128)S(1)} %pad_maximum_fusion.bias_ref, bf16[4,2,2,128,128]{4,3,2,1,0:T(8,128)(2,1)S(1)} %get-tuple-element.49.here_ref, ...), custom_call_target="tpu_custom_call" | custom-call | flops 503316480 | bytes 3284992 | tf_op jit(solution)/shard_map/query_grads/pallas_call | solution.py:59
  35.5 0.3 joined.6
  35.8 1.3 %collective-permute-start.13 = (bf16[2,2,2,128,128]{4,3,2,1,0:T(8,128)(2,1)S(1)}, bf16[2,2,2,128,128]{4,3,2,1,0:T(8,128)(2,1)S(1)}, u32[]{:S(2)}, u32[]{:S(2)}) collective-permute-start(bf16[2,2,2,128,128]{4,3,2,1,0:T(8,128)(2,1)S(1)} %get-tuple-element.70), channel_id=1, source_target_pairs={{0,4},{4,0},{8,12},{12,8},{1,5},{5,1},{9,13},{13,9},{2,6},{6,2},{1... | collective-permute-start | bytes 786440 | tf_op jit(solution)/shard_map/ppermute | solution.py:30
  37.2 0.7 collective-permute-start.14
  37.9 1.9 %query_grads.5 = (bf16[2,2,128,128]{3,2,1,0:T(8,128)(2,1)S(1)}, f32[2,2,2,128,128]{4,3,2,1,0:T(8,128)S(1)}, f32[1,8,256]{2,1,0:T(8,128)S(1)}) custom-call(f32[2,768,256]{2,1,0:T(8,128)S(1)} %pad_maximum_fusion.bias_ref, bf16[4,2,2,128,128]{4,3,2,1,0:T(8,128)(2,1)S(1)} %get-tuple-element.60.here_ref, ...), custom_call_target="tpu_custom_call" | custom-call | flops 503316480 | bytes 3284992 | tf_op jit(solution)/shard_map/query_grads/pallas_call | solution.py:59
  39.8 0.3 joined.7
  40.1 4.0 %collective-permute-start.18 = (bf16[2,2,2,128,128]{4,3,2,1,0:T(8,128)(2,1)S(1)}, bf16[2,2,2,128,128]{4,3,2,1,0:T(8,128)(2,1)S(1)}, u32[]{:S(2)}, u32[]{:S(2)}) collective-permute-start(bf16[2,2,2,128,128]{4,3,2,1,0:T(8,128)(2,1)S(1)} %get-tuple-element.79), channel_id=1, source_target_pairs={{0,4},{4,0},{8,12},{12,8},{1,5},{5,1},{9,13},{13,9},{2,6},{6,2},{1... | collective-permute-start | bytes 786440 | tf_op jit(solution)/shard_map/ppermute | solution.py:30
  44.1 0.7 collective-permute-start.19
  44.8 0.5 and_select_fusion.2
  45.3 1.0 %collective-permute-start.4 = (f32[1,8,256]{2,1,0:T(8,128)S(1)}, f32[1,8,256]{2,1,0:T(8,128)S(1)}, u32[]{:S(2)}, u32[]{:S(2)}) collective-permute-start(f32[1,8,256]{2,1,0:T(8,128)S(1)} %get-tuple-element.52.refs_1_), channel_id=1, source_target_pairs={{0,12},{4,0},{8,4},{12,8},{1,13},{5,1},{9,5},{13,9},{2,14},{6,2},{... | collective-permute-start | bytes 24584 | tf_op jit(solution)/shard_map/ppermute | solution.py:35
  46.4 2.6 %collective-permute-done.4.stats_ref = f32[1,8,256]{2,1,0:T(8,128)S(1)} collective-permute-done((f32[1,8,256]{2,1,0:T(8,128)S(1)}, f32[1,8,256]{2,1,0:T(8,128)S(1)}, u32[]{:S(2)}, u32[]{:S(2)}) %collective-permute-start.4) | collective-permute-done | bytes 8224 | tf_op jit(solution)/shard_map/ppermute | solution.py:35
  49.0 0.7 key_grads.4
  49.7 1.9 %collective-permute-start.5 = (bf16[3,2,128,128]{3,2,1,0:T(8,128)(2,1)S(1)}, bf16[3,2,128,128]{3,2,1,0:T(8,128)(2,1)S(1)}, u32[]{:S(2)}, u32[]{:S(2)}) collective-permute-start(bf16[3,2,128,128]{3,2,1,0:T(8,128)(2,1)S(1)} %get-tuple-element.56), channel_id=1, source_target_pairs={{0,2},{2,0},{1,3},{3,1},{4,6},{6,4},{5,7},{7,5},{8,10},{10,8},{9,1... | collective-permute-start | bytes 589832 | tf_op jit(solution)/shard_map/ppermute | solution.py:40
  51.7 3.5 %collective-permute-start.10 = (f32[1,8,256]{2,1,0:T(8,128)S(1)}, f32[1,8,256]{2,1,0:T(8,128)S(1)}, u32[]{:S(2)}, u32[]{:S(2)}) collective-permute-start(f32[1,8,256]{2,1,0:T(8,128)S(1)} %get-tuple-element.63.refs_1_), channel_id=1, source_target_pairs={{0,12},{4,0},{8,4},{12,8},{1,13},{5,1},{9,5},{13,9},{2,14},{6,2},{... | collective-permute-start | bytes 24584 | tf_op jit(solution)/shard_map/ppermute | solution.py:35
  55.2 1.9 %query_grads.6 = (bf16[2,2,128,128]{3,2,1,0:T(8,128)(2,1)S(1)}, f32[2,2,2,128,128]{4,3,2,1,0:T(8,128)S(1)}, f32[1,8,256]{2,1,0:T(8,128)S(1)}) custom-call(f32[2,768,256]{2,1,0:T(8,128)S(1)} %pad_maximum_fusion.bias_ref, bf16[4,2,2,128,128]{4,3,2,1,0:T(8,128)(2,1)S(1)} %get-tuple-element.69.here_ref, ...), custom_call_target="tpu_custom_call" | custom-call | flops 503316480 | bytes 3284992 | tf_op jit(solution)/shard_map/query_grads/pallas_call | solution.py:59
  57.1 0.7 collective-permute-start.15
  57.8 0.7 key_grads.5
  58.6 0.3 collective-permute-start.11
  58.8 2.1 %query_grads.7 = (bf16[2,2,128,128]{3,2,1,0:T(8,128)(2,1)S(1)}, f32[2,2,2,128,128]{4,3,2,1,0:T(8,128)S(1)}, f32[1,8,256]{2,1,0:T(8,128)S(1)}) custom-call(f32[2,768,256]{2,1,0:T(8,128)S(1)} %pad_maximum_fusion.bias_ref, bf16[4,2,2,128,128]{4,3,2,1,0:T(8,128)(2,1)S(1)} %get-tuple-element.78.here_ref, ...), custom_call_target="tpu_custom_call" | custom-call | flops 503316480 | bytes 3284992 | tf_op jit(solution)/shard_map/query_grads/pallas_call | solution.py:59
  60.9 2.9 %collective-permute-start.20 = (f32[1,8,256]{2,1,0:T(8,128)S(1)}, f32[1,8,256]{2,1,0:T(8,128)S(1)}, u32[]{:S(2)}, u32[]{:S(2)}) collective-permute-start(f32[1,8,256]{2,1,0:T(8,128)S(1)} %get-tuple-element.81), channel_id=1, source_target_pairs={{0,12},{4,0},{8,4},{12,8},{1,13},{5,1},{9,5},{13,9},{2,14},{6,2},{... | collective-permute-start | bytes 24584 | tf_op jit(solution)/shard_map/ppermute | solution.py:35
  63.8 0.7 key_grads.6
  64.5 1.9 %collective-permute-start.16 = (bf16[3,2,128,128]{3,2,1,0:T(8,128)(2,1)S(1)}, bf16[3,2,128,128]{3,2,1,0:T(8,128)(2,1)S(1)}, u32[]{:S(2)}, u32[]{:S(2)}) collective-permute-start(bf16[3,2,128,128]{3,2,1,0:T(8,128)(2,1)S(1)} %get-tuple-element.76), channel_id=1, source_target_pairs={{0,2},{2,0},{1,3},{3,1},{4,6},{6,4},{5,7},{7,5},{8,10},{10,8},{9,1... | collective-permute-start | bytes 589832 | tf_op jit(solution)/shard_map/ppermute | solution.py:40
  66.4 0.7 key_grads.7
  67.2 0.6 collective-permute-start.21
  67.8 0.2 rows_for_pair.4
  68.1 0.2 rows_for_pair.5
  68.3 0.5 collective-permute-start.23
  68.8 1.4 %collective-permute-done.16.refs_1_ = bf16[3,2,128,128]{3,2,1,0:T(8,128)(2,1)S(1)} collective-permute-done((bf16[3,2,128,128]{3,2,1,0:T(8,128)(2,1)S(1)}, bf16[3,2,128,128]{3,2,1,0:T(8,128)(2,1)S(1)}, u32[]{:S(2)}, u32[]{:S(2)}) %collective-permute-start.16) | collective-permute-done | bytes 196640 | tf_op jit(solution)/shard_map/ppermute | solution.py:40
  70.5 2.4 %collective-permute-done.21.refs_1_ = bf16[3,2,128,128]{3,2,1,0:T(8,128)(2,1)S(1)} collective-permute-done((bf16[3,2,128,128]{3,2,1,0:T(8,128)(2,1)S(1)}, bf16[3,2,128,128]{3,2,1,0:T(8,128)(2,1)S(1)}, u32[]{:S(2)}, u32[]{:S(2)}) %collective-permute-start.21) | collective-permute-done | bytes 196640 | tf_op jit(solution)/shard_map/ppermute | solution.py:40
  72.9 0.2 rows_for_pair.7
  73.2 1.4 %collective-permute-done.25.refs_7_ = bf16[3,2,128,128]{3,2,1,0:T(8,128)(2,1)S(1)} collective-permute-done((bf16[3,2,128,128]{3,2,1,0:T(8,128)(2,1)S(1)}, bf16[3,2,128,128]{3,2,1,0:T(8,128)(2,1)S(1)}, u32[]{:S(2)}, u32[]{:S(2)}) %collective-permute-start.25) | collective-permute-done | bytes 196640 | tf_op jit(solution)/shard_map/ppermute | solution.py:44
  74.6 1.5 %laid_out.1 = (bf16[128,2048]{1,0:T(8,128)(2,1)}, bf16[128,2048]{1,0:T(8,128)(2,1)}, bf16[128,2048]{1,0:T(8,128)(2,1)}) custom-call(bf16[3,2,128,128]{3,2,1,0:T(8,128)(2,1)S(1)} %get-tuple-element.57.refs_0_, bf16[3,2,128,128]{3,2,1,0:T(8,128)(2,1)S(1)} %get-tuple-element.68.refs_1_, bf16[3,2,128,128]{3,2,1,0:T(8,128)(2,1)S(1)} %get-tuple-element.77.refs_2_, ...), custom_call_target="tpu_custom_call" | custom-call | bytes 3145728 | tf_op jit(solution)/shard_map/laid_out/pallas_call | solution.py:59
  (45 shorter events, 1.3 us)
Async XLA Ops:
  1.8 2.3 %copy-start = (s32[2048]{0:T(1024)S(1)}, s32[2048]{0:T(1024)}, u32[]{:S(2)}) copy-start(s32[2048]{0:T(1024)} %param.9) | copy-start | bytes 24580
  1.8 2.4 %collective-permute-start = (bf16[4,2,128,128]{3,2,1,0:T(8,128)(2,1)S(1)}, bf16[4,2,128,128]{3,2,1,0:T(8,128)(2,1)S(1)}, u32[]{:S(2)}, u32[]{:S(2)}) collective-permute-start(bf16[4,2,128,128]{3,2,1,0:T(8,128)(2,1)S(1)} %get-tuple-element.48), channel_id=1, source_target_pairs={{0,1},{1,0},{2,3},{3,2},{4,5},{5,4},{6,7},{7,6},{8,9},{9,8},{10,11... | collective-permute-start | bytes 786440 | tf_op jit(solution)/shard_map/ppermute | solution.py:44
  3.9 13.0 %collective-permute-start.6 = (bf16[4,2,128,384]{3,2,1,0:T(8,128)(2,1)S(1)}, bf16[4,2,128,384]{3,2,1,0:T(8,128)(2,1)S(1)}, u32[]{:S(2)}, u32[]{:S(2)}) collective-permute-start(bf16[4,2,128,384]{3,2,1,0:T(8,128)(2,1)S(1)} %get-tuple-element.59), channel_id=1, source_target_pairs={{0,1},{1,0},{2,3},{3,2},{4,5},{5,4},{6,7},{7,6},{8,9},{9,8},{10,11... | collective-permute-start | bytes 2359304 | tf_op jit(solution)/shard_map/ppermute | solution.py:44
  4.4 9.5 %collective-permute-start.1 = (bf16[4,2,128,128]{3,2,1,0:T(8,128)(2,1)S(1)}, bf16[4,2,128,128]{3,2,1,0:T(8,128)(2,1)S(1)}, u32[]{:S(2)}, u32[]{:S(2)}) collective-permute-start(bf16[4,2,128,128]{3,2,1,0:T(8,128)(2,1)S(1)} %head_parts.4), channel_id=1, source_target_pairs={{0,2},{2,0},{1,3},{3,1},{4,6},{6,4},{5,7},{7,5},{8,10},{10,8},{9,1... | collective-permute-start | bytes 786440 | tf_op jit(solution)/shard_map/ppermute | solution.py:40
  14.3 17.4 %collective-permute-start.2 = (bf16[2,2,2,128,128]{4,3,2,1,0:T(8,128)(2,1)S(1)}, bf16[2,2,2,128,128]{4,3,2,1,0:T(8,128)(2,1)S(1)}, u32[]{:S(2)}, u32[]{:S(2)}) collective-permute-start(bf16[2,2,2,128,128]{4,3,2,1,0:T(8,128)(2,1)S(1)} %get-tuple-element.50), channel_id=1, source_target_pairs={{0,4},{4,0},{8,12},{12,8},{1,5},{5,1},{9,13},{13,9},{2,6},{6,2},{1... | collective-permute-start | bytes 786440 | tf_op jit(solution)/shard_map/ppermute | solution.py:30
  16.2 15.5 %collective-permute-start.3 = (bf16[2,2,2,128,128]{4,3,2,1,0:T(8,128)(2,1)S(1)}, bf16[2,2,2,128,128]{4,3,2,1,0:T(8,128)(2,1)S(1)}, u32[]{:S(2)}, u32[]{:S(2)}) collective-permute-start(bf16[2,2,2,128,128]{4,3,2,1,0:T(8,128)(2,1)S(1)} %get-tuple-element.51), channel_id=1, source_target_pairs={{0,0},{4,8},{8,4},{12,12},{1,1},{5,9},{9,5},{13,13},{2,2},{6,10},{... | collective-permute-start | bytes 786440 | tf_op jit(solution)/shard_map/ppermute | solution.py:30
  17.0 9.3 %collective-permute-start.7 = (bf16[4,2,128,128]{3,2,1,0:T(8,128)(2,1)S(1)}, bf16[4,2,128,128]{3,2,1,0:T(8,128)(2,1)S(1)}, u32[]{:S(2)}, u32[]{:S(2)}) collective-permute-start(bf16[4,2,128,128]{3,2,1,0:T(8,128)(2,1)S(1)} %head_parts.5), channel_id=1, source_target_pairs={{0,2},{2,0},{1,3},{3,1},{4,6},{6,4},{5,7},{7,5},{8,10},{10,8},{9,1... | collective-permute-start | bytes 786440 | tf_op jit(solution)/shard_map/ppermute | solution.py:40
  19.4 16.1 %collective-permute-start.12 = (bf16[4,2,128,128]{3,2,1,0:T(8,128)(2,1)S(1)}, bf16[4,2,128,128]{3,2,1,0:T(8,128)(2,1)S(1)}, u32[]{:S(2)}, u32[]{:S(2)}) collective-permute-start(bf16[4,2,128,128]{3,2,1,0:T(8,128)(2,1)S(1)} %head_parts.6), channel_id=1, source_target_pairs={{0,2},{2,0},{1,3},{3,1},{4,6},{6,4},{5,7},{7,5},{8,10},{10,8},{9,1... | collective-permute-start | bytes 786440 | tf_op jit(solution)/shard_map/ppermute | solution.py:40
  26.6 11.2 %collective-permute-start.8 = (bf16[2,2,2,128,128]{4,3,2,1,0:T(8,128)(2,1)S(1)}, bf16[2,2,2,128,128]{4,3,2,1,0:T(8,128)(2,1)S(1)}, u32[]{:S(2)}, u32[]{:S(2)}) collective-permute-start(bf16[2,2,2,128,128]{4,3,2,1,0:T(8,128)(2,1)S(1)} %get-tuple-element.61), channel_id=1, source_target_pairs={{0,4},{4,0},{8,12},{12,8},{1,5},{5,1},{9,13},{13,9},{2,6},{6,2},{1... | collective-permute-start | bytes 786440 | tf_op jit(solution)/shard_map/ppermute | solution.py:30
  31.1 6.8 %collective-permute-start.9 = (bf16[2,2,2,128,128]{4,3,2,1,0:T(8,128)(2,1)S(1)}, bf16[2,2,2,128,128]{4,3,2,1,0:T(8,128)(2,1)S(1)}, u32[]{:S(2)}, u32[]{:S(2)}) collective-permute-start(bf16[2,2,2,128,128]{4,3,2,1,0:T(8,128)(2,1)S(1)} %get-tuple-element.62), channel_id=1, source_target_pairs={{0,0},{4,8},{8,4},{12,12},{1,1},{5,9},{9,5},{13,13},{2,2},{6,10},{... | collective-permute-start | bytes 786440 | tf_op jit(solution)/shard_map/ppermute | solution.py:30
  31.9 7.9 %collective-permute-start.17 = (bf16[4,2,128,128]{3,2,1,0:T(8,128)(2,1)S(1)}, bf16[4,2,128,128]{3,2,1,0:T(8,128)(2,1)S(1)}, u32[]{:S(2)}, u32[]{:S(2)}) collective-permute-start(bf16[4,2,128,128]{3,2,1,0:T(8,128)(2,1)S(1)} %head_parts.7), channel_id=1, source_target_pairs={{0,2},{2,0},{1,3},{3,1},{4,6},{6,4},{5,7},{7,5},{8,10},{10,8},{9,1... | collective-permute-start | bytes 786440 | tf_op jit(solution)/shard_map/ppermute | solution.py:40
  35.8 15.8 %collective-permute-start.13 = (bf16[2,2,2,128,128]{4,3,2,1,0:T(8,128)(2,1)S(1)}, bf16[2,2,2,128,128]{4,3,2,1,0:T(8,128)(2,1)S(1)}, u32[]{:S(2)}, u32[]{:S(2)}) collective-permute-start(bf16[2,2,2,128,128]{4,3,2,1,0:T(8,128)(2,1)S(1)} %get-tuple-element.70), channel_id=1, source_target_pairs={{0,4},{4,0},{8,12},{12,8},{1,5},{5,1},{9,13},{13,9},{2,6},{6,2},{1... | collective-permute-start | bytes 786440 | tf_op jit(solution)/shard_map/ppermute | solution.py:30
  37.2 18.0 %collective-permute-start.14 = (bf16[2,2,2,128,128]{4,3,2,1,0:T(8,128)(2,1)S(1)}, bf16[2,2,2,128,128]{4,3,2,1,0:T(8,128)(2,1)S(1)}, u32[]{:S(2)}, u32[]{:S(2)}) collective-permute-start(bf16[2,2,2,128,128]{4,3,2,1,0:T(8,128)(2,1)S(1)} %get-tuple-element.71), channel_id=1, source_target_pairs={{0,0},{4,8},{8,4},{12,12},{1,1},{5,9},{9,5},{13,13},{2,2},{6,10},{... | collective-permute-start | bytes 786440 | tf_op jit(solution)/shard_map/ppermute | solution.py:30
  40.1 18.7 %collective-permute-start.18 = (bf16[2,2,2,128,128]{4,3,2,1,0:T(8,128)(2,1)S(1)}, bf16[2,2,2,128,128]{4,3,2,1,0:T(8,128)(2,1)S(1)}, u32[]{:S(2)}, u32[]{:S(2)}) collective-permute-start(bf16[2,2,2,128,128]{4,3,2,1,0:T(8,128)(2,1)S(1)} %get-tuple-element.79), channel_id=1, source_target_pairs={{0,4},{4,0},{8,12},{12,8},{1,5},{5,1},{9,13},{13,9},{2,6},{6,2},{1... | collective-permute-start | bytes 786440 | tf_op jit(solution)/shard_map/ppermute | solution.py:30
  44.1 14.7 %collective-permute-start.19 = (bf16[2,2,2,128,128]{4,3,2,1,0:T(8,128)(2,1)S(1)}, bf16[2,2,2,128,128]{4,3,2,1,0:T(8,128)(2,1)S(1)}, u32[]{:S(2)}, u32[]{:S(2)}) collective-permute-start(bf16[2,2,2,128,128]{4,3,2,1,0:T(8,128)(2,1)S(1)} %get-tuple-element.80), channel_id=1, source_target_pairs={{0,0},{4,8},{8,4},{12,12},{1,1},{5,9},{9,5},{13,13},{2,2},{6,10},{... | collective-permute-start | bytes 786440 | tf_op jit(solution)/shard_map/ppermute | solution.py:30
  45.3 3.7 %collective-permute-start.4 = (f32[1,8,256]{2,1,0:T(8,128)S(1)}, f32[1,8,256]{2,1,0:T(8,128)S(1)}, u32[]{:S(2)}, u32[]{:S(2)}) collective-permute-start(f32[1,8,256]{2,1,0:T(8,128)S(1)} %get-tuple-element.52.refs_1_), channel_id=1, source_target_pairs={{0,12},{4,0},{8,4},{12,8},{1,13},{5,1},{9,5},{13,9},{2,14},{6,2},{... | collective-permute-start | bytes 24584 | tf_op jit(solution)/shard_map/ppermute | solution.py:35
  49.7 18.0 %collective-permute-start.5 = (bf16[3,2,128,128]{3,2,1,0:T(8,128)(2,1)S(1)}, bf16[3,2,128,128]{3,2,1,0:T(8,128)(2,1)S(1)}, u32[]{:S(2)}, u32[]{:S(2)}) collective-permute-start(bf16[3,2,128,128]{3,2,1,0:T(8,128)(2,1)S(1)} %get-tuple-element.56), channel_id=1, source_target_pairs={{0,2},{2,0},{1,3},{3,1},{4,6},{6,4},{5,7},{7,5},{8,10},{10,8},{9,1... | collective-permute-start | bytes 589832 | tf_op jit(solution)/shard_map/ppermute | solution.py:40
  51.7 6.2 %collective-permute-start.10 = (f32[1,8,256]{2,1,0:T(8,128)S(1)}, f32[1,8,256]{2,1,0:T(8,128)S(1)}, u32[]{:S(2)}, u32[]{:S(2)}) collective-permute-start(f32[1,8,256]{2,1,0:T(8,128)S(1)} %get-tuple-element.63.refs_1_), channel_id=1, source_target_pairs={{0,12},{4,0},{8,4},{12,8},{1,13},{5,1},{9,5},{13,9},{2,14},{6,2},{... | collective-permute-start | bytes 24584 | tf_op jit(solution)/shard_map/ppermute | solution.py:35
  57.1 6.7 %collective-permute-start.15 = (f32[1,8,256]{2,1,0:T(8,128)S(1)}, f32[1,8,256]{2,1,0:T(8,128)S(1)}, u32[]{:S(2)}, u32[]{:S(2)}) collective-permute-start(f32[1,8,256]{2,1,0:T(8,128)S(1)} %get-tuple-element.72), channel_id=1, source_target_pairs={{0,12},{4,0},{8,4},{12,8},{1,13},{5,1},{9,5},{13,9},{2,14},{6,2},{... | collective-permute-start | bytes 24584 | tf_op jit(solution)/shard_map/ppermute | solution.py:35
  58.6 9.5 %collective-permute-start.11 = (bf16[3,2,128,128]{3,2,1,0:T(8,128)(2,1)S(1)}, bf16[3,2,128,128]{3,2,1,0:T(8,128)(2,1)S(1)}, u32[]{:S(2)}, u32[]{:S(2)}) collective-permute-start(bf16[3,2,128,128]{3,2,1,0:T(8,128)(2,1)S(1)} %get-tuple-element.67), channel_id=1, source_target_pairs={{0,2},{2,0},{1,3},{3,1},{4,6},{6,4},{5,7},{7,5},{8,10},{10,8},{9,1... | collective-permute-start | bytes 589832 | tf_op jit(solution)/shard_map/ppermute | solution.py:40
  60.9 5.5 %collective-permute-start.20 = (f32[1,8,256]{2,1,0:T(8,128)S(1)}, f32[1,8,256]{2,1,0:T(8,128)S(1)}, u32[]{:S(2)}, u32[]{:S(2)}) collective-permute-start(f32[1,8,256]{2,1,0:T(8,128)S(1)} %get-tuple-element.81), channel_id=1, source_target_pairs={{0,12},{4,0},{8,4},{12,8},{1,13},{5,1},{9,5},{13,9},{2,14},{6,2},{... | collective-permute-start | bytes 24584 | tf_op jit(solution)/shard_map/ppermute | solution.py:35
  64.5 5.7 %collective-permute-start.16 = (bf16[3,2,128,128]{3,2,1,0:T(8,128)(2,1)S(1)}, bf16[3,2,128,128]{3,2,1,0:T(8,128)(2,1)S(1)}, u32[]{:S(2)}, u32[]{:S(2)}) collective-permute-start(bf16[3,2,128,128]{3,2,1,0:T(8,128)(2,1)S(1)} %get-tuple-element.76), channel_id=1, source_target_pairs={{0,2},{2,0},{1,3},{3,1},{4,6},{6,4},{5,7},{7,5},{8,10},{10,8},{9,1... | collective-permute-start | bytes 589832 | tf_op jit(solution)/shard_map/ppermute | solution.py:40
  67.2 5.7 %collective-permute-start.21 = (bf16[3,2,128,128]{3,2,1,0:T(8,128)(2,1)S(1)}, bf16[3,2,128,128]{3,2,1,0:T(8,128)(2,1)S(1)}, u32[]{:S(2)}, u32[]{:S(2)}) collective-permute-start(bf16[3,2,128,128]{3,2,1,0:T(8,128)(2,1)S(1)} %get-tuple-element.85), channel_id=1, source_target_pairs={{0,2},{2,0},{1,3},{3,1},{4,6},{6,4},{5,7},{7,5},{8,10},{10,8},{9,1... | collective-permute-start | bytes 589832 | tf_op jit(solution)/shard_map/ppermute | solution.py:40
  68.0 5.2 %collective-permute-start.22 = (bf16[3,2,128,128]{3,2,1,0:T(8,128)(2,1)S(1)}, bf16[3,2,128,128]{3,2,1,0:T(8,128)(2,1)S(1)}, u32[]{:S(2)}, u32[]{:S(2)}) collective-permute-start(bf16[3,2,128,128]{3,2,1,0:T(8,128)(2,1)S(1)} %get-tuple-element.87), channel_id=1, source_target_pairs={{0,1},{1,0},{2,3},{3,2},{4,5},{5,4},{6,7},{7,6},{8,9},{9,8},{10,11... | collective-permute-start | bytes 589832 | tf_op jit(solution)/shard_map/ppermute | solution.py:44
  68.3 4.9 %collective-permute-start.23 = (bf16[3,2,128,128]{3,2,1,0:T(8,128)(2,1)S(1)}, bf16[3,2,128,128]{3,2,1,0:T(8,128)(2,1)S(1)}, u32[]{:S(2)}, u32[]{:S(2)}) collective-permute-start(bf16[3,2,128,128]{3,2,1,0:T(8,128)(2,1)S(1)} %get-tuple-element.88), channel_id=1, source_target_pairs={{0,1},{1,0},{2,3},{3,2},{4,5},{5,4},{6,7},{7,6},{8,9},{9,8},{10,11... | collective-permute-start | bytes 589832 | tf_op jit(solution)/shard_map/ppermute | solution.py:44
  70.5 2.7 %collective-permute-start.24 = (bf16[3,2,128,128]{3,2,1,0:T(8,128)(2,1)S(1)}, bf16[3,2,128,128]{3,2,1,0:T(8,128)(2,1)S(1)}, u32[]{:S(2)}, u32[]{:S(2)}) collective-permute-start(bf16[3,2,128,128]{3,2,1,0:T(8,128)(2,1)S(1)} %get-tuple-element.89), channel_id=1, source_target_pairs={{0,1},{1,0},{2,3},{3,2},{4,5},{5,4},{6,7},{7,6},{8,9},{9,8},{10,11... | collective-permute-start | bytes 589832 | tf_op jit(solution)/shard_map/ppermute | solution.py:44
  73.1 1.5 %collective-permute-start.25 = (bf16[3,2,128,128]{3,2,1,0:T(8,128)(2,1)S(1)}, bf16[3,2,128,128]{3,2,1,0:T(8,128)(2,1)S(1)}, u32[]{:S(2)}, u32[]{:S(2)}) collective-permute-start(bf16[3,2,128,128]{3,2,1,0:T(8,128)(2,1)S(1)} %get-tuple-element.90), channel_id=1, source_target_pairs={{0,1},{1,0},{2,3},{3,2},{4,5},{5,4},{6,7},{7,6},{8,9},{9,8},{10,11... | collective-permute-start | bytes 589832 | tf_op jit(solution)/shard_map/ppermute | solution.py:44

commit v4 on v2

v4 whole, which is shorter than its diff:
```python
import math

import jax
import jax.numpy as jnp
from jax import lax
from jax.experimental import pallas as pl
from jax.experimental.pallas import tpu as pltpu
from jax.sharding import PartitionSpec as P

HD = 128
NEG_FILL = -1e30
LOW = jnp.bfloat16
WIDE = jnp.float32
MIB = 1024 * 1024
TO_BITS = HD ** (-0.5) / math.log(2.0)
SCALE = HD ** (-0.5)
ROWS_BY_ROWS = (((1,), (1,)), ((), ()))


def chunks_of(heads):
    return [heads // 2, heads - heads // 2]


def along_blocks(value, by):
    peers = lax.axis_size("blk")
    return lax.ppermute(value, "blk", [(i, (i + by) % peers) for i in range(peers)])


def round_sub(value, by):
    peers = lax.axis_size("sub")
    return lax.ppermute(value, "sub", [(i, (i + by) % peers) for i in range(peers)])


def swapped(value):
    return lax.ppermute(value, "pair", [(0, 1), (1, 0)])


def run_moves(moves, sems):
    copies = [pltpu.make_async_copy(src, dst, sems.at[at]) for at, (src, dst) in enumerate(moves)]
    for copy in copies:
        copy.start()
    for copy in copies:
        copy.wait()


def call(kernel, ins, outs, scratch, name, whole=False, flops=0, room=8 * MIB):
    spec = pl.BlockSpec(memory_space=pltpu.VMEM if whole else pl.ANY)
    moved = sum(math.prod(a.shape) * a.dtype.itemsize for a in list(ins) + list(outs))
    return list(
        pl.pallas_call(
            kernel,
            out_shape=outs,
            in_specs=[spec] * len(ins),
            out_specs=[spec] * len(outs),
            scratch_shapes=scratch,
            name=name,
            cost_estimate=pl.CostEstimate(flops=flops, bytes_accessed=moved, transcendentals=0),
            compiler_params=pltpu.CompilerParams(vmem_limit_bytes=room),
        )(*ins)
    )


def shape(*dims, dtype=LOW):
    return jax.ShapeDtypeStruct(dims, dtype)


def first_parts(arrays, low, high, after):
    count = len(arrays)
    rows, width = arrays[0].shape
    half = width // 2
    peers = lax.axis_size("sub")
    part = half // peers

    def kernel(*refs):
        ins, outs, sems = refs[:count], refs[-3:-1], refs[-1]
        p = lax.axis_index("pair")
        moves = []
        for side, out in zip((1 - p, p), outs):
            for at in range(peers):
                start = pl.multiple_of(side * half + at * part + low, HD)
                moves += [(ref.at[:, pl.ds(start, high - low)], out.at[i, at]) for i, ref in enumerate(ins)]
        run_moves(moves, sems)

    outs = [pltpu.VMEM((count, peers, rows, high - low), LOW)] * 2
    spec = pl.BlockSpec(memory_space=pl.ANY)
    held = [pltpu.with_memory_space_constraint(array, pltpu.HBM) for array in arrays]
    return pl.pallas_call(
        kernel,
        out_shape=outs,
        in_specs=[spec] * (count + len(after)),
        out_specs=[spec] * 2,
        scratch_shapes=[pltpu.SemaphoreType.DMA((2 * peers * count,))],
        name="first_parts",
        compiler_params=pltpu.CompilerParams(vmem_limit_bytes=8 * MIB),
    )(*held, *after)


def head_parts(own, paired, turns, after):
    count, peers, rows, cut = own.shape

    def kernel(own_ref, pair_ref, *refs):
        outs, sems = refs[len(after):-1], refs[-1]
        p, s = lax.axis_index("pair"), lax.axis_index("sub")
        moves = []
        for by, out in zip(turns, outs):
            at = lax.rem(s + by, peers)
            moves += [(own_ref.at[:, at], out.at[:, p]), (pair_ref.at[:, at], out.at[:, 1 - p])]
        run_moves(moves, sems)

    outs = [shape(count, 2, rows, cut)] * len(turns)
    scratch = [pltpu.SemaphoreType.DMA((2 * len(turns),))]
    return call(kernel, [own, paired] + after, outs, scratch, "head_parts")


def attention_grads(bias, kv, kv_earlier, qg, split):
    peers = len(kv)
    _, _, rows, cut = kv[0].shape
    heads = cut // HD
    strip = rows * peers
    early_count = peers if split else 1

    def kernel(*refs):
        bias_ref = refs[0]
        kv_in, early_in, qg_in = refs[1:1 + peers], refs[1 + peers:1 + 2 * peers], refs[1 + 2 * peers:1 + 3 * peers]
        outs = refs[1 + 3 * peers:-5]
        own_out, dq_outs, early_outs = outs[0], outs[1:1 + peers], outs[1 + peers:]
        kv_all, qg_all, early, dq_all, sems = refs[-5:]
        s = lax.axis_index("sub")
        moves = []
        for by in range(peers):
            at = lax.rem(s - by + peers, peers)
            moves += [
                (early_in[by], kv_all.at[:, 0:2, at]),
                (kv_in[by], kv_all.at[:, 2:4, at]),
                (qg_in[by], qg_all.at[:, :, at]),
            ]
        run_moves(moves, sems)
        for head in range(heads):
            columns = pl.ds(head * HD, HD)

            def flat(ref, which, tiles):
                block = ref[which, tiles, :, :, columns]
                return block.reshape(block.shape[0] * strip, HD)

            terms = []
            for tile in range(2):
                at, span = pl.ds(tile, 1), pl.ds(tile, 3)
                q, g = flat(qg_all, 0, at), flat(qg_all, 1, at)
                k, v = flat(kv_all, 0, span), flat(kv_all, 1, span)
                scores = lax.dot_general(k, q, ROWS_BY_ROWS, preferred_element_type=WIDE) * TO_BITS + bias_ref[tile]
                peak = jnp.max(scores, axis=0, keepdims=True)
                weight = jnp.exp2(scores - peak)
                prob = weight * (1.0 / jnp.sum(weight, axis=0, keepdims=True))
                prob_low = prob.astype(LOW)
                grad_prob = lax.dot_general(v, g, ROWS_BY_ROWS, preferred_element_type=WIDE)
                row_dot = jnp.sum(prob_low.astype(WIDE) * grad_prob, axis=0, keepdims=True)
                score_low = (prob * (grad_prob - row_dot)).astype(LOW)
                dq = jnp.dot(k.T, score_low, preferred_element_type=WIDE) * SCALE
                dq_all[tile, :, :, columns] = dq.T.astype(LOW).reshape(peers, rows, HD)
                dk = jnp.dot(score_low, q, preferred_element_type=WIDE) * SCALE
                dv = jnp.dot(prob_low, g, preferred_element_type=WIDE)
                terms.append((dk, dv))
            for which in range(2):
                low, high = terms[0][which], terms[1][which]
                sums = (
                    low[:strip],
                    low[strip:2 * strip] + high[:strip],
                    low[2 * strip:] + high[strip:2 * strip],
                    high[2 * strip:],
                )
                for tile, total in enumerate(sums):
                    total = total.reshape(peers, rows, HD)
                    if tile < 2:
                        early[which, tile, :, :, columns] = total.astype(LOW)
                    else:
                        own_out[which, tile - 2, :, :, columns] = total
        moves = [] if split else [(early, early_outs[0])]
        for by in range(peers):
            at = lax.rem(s + by, peers)
            moves.append((dq_all.at[:, at], dq_outs[by]))
            if split:
                moves.append((early.at[:, :, at], early_outs[by]))
        run_moves(moves, sems)

    outs = [shape(2, 2, peers, rows, cut, dtype=WIDE)] + [shape(2, rows, cut)] * peers
    outs += [shape(2, 2, rows, cut)] * peers if split else [shape(2, 2, peers, rows, cut)]
    scratch = [
        pltpu.VMEM((2, 4, peers, rows, cut), LOW),
        pltpu.VMEM((2, 2, peers, rows, cut), LOW),
        pltpu.VMEM((2, 2, peers, rows, cut), LOW),
        pltpu.VMEM((2, peers, rows, cut), LOW),
        pltpu.SemaphoreType.DMA((3 * peers,)),
    ]
    flops = heads * 2 * 5 * 2 * strip * 3 * strip * HD
    ins = [bias] + kv + kv_earlier + qg
    outs = call(kernel, ins, outs, scratch, "attention_grads", whole=True, flops=flops, room=40 * MIB)
    return outs[0], outs[1:1 + peers], outs[1 + peers:]


def summed(own, later, turns, after):
    _, _, peers, rows, cut = own.shape
    split = len(later) > 1 or later[0].ndim == 4

    def kernel(own_ref, *refs):
        later_refs, outs = refs[:len(later)], refs[len(later) + len(after):]
        s = lax.axis_index("sub")
        for place, (by, out) in enumerate(zip(turns, outs)):
            at = lax.rem(s + by, peers)
            for which in range(2):
                for row in range(2):
                    term = later_refs[place][which, row] if split else later_refs[0][which, row, at]
                    out[which, row] = (own_ref[which, row, at] + term.astype(WIDE)).astype(LOW)

    outs = [shape(2, 2, rows, cut)] * len(turns)
    return call(kernel, [own] + later + after, outs, [], "summed", whole=True)


def rows_for_pair(dq, dkv):
    peers = len(dq)
    _, rows, cut = dq[0].shape

    def kernel(*refs):
        dq_refs, dkv_refs, (send, keep), sems = refs[:peers], refs[peers:2 * peers], refs[-3:-1], refs[-1]
        p, s = lax.axis_index("pair"), lax.axis_index("sub")
        moves = []
        for by in range(peers):
            at = lax.rem(s - by + peers, peers)
            for out, row in ((send, 1 - p), (keep, p)):
                moves += [(dq_refs[by].at[row], out.at[0, at]), (dkv_refs[by].at[:, row], out.at[1:3, at])]
        run_moves(moves, sems)

    outs = [shape(3, peers, rows, cut)] * 2
    return call(kernel, dq + dkv, outs, [pltpu.SemaphoreType.DMA((4 * peers,))], "rows_for_pair")


def laid_out(kept, paired, spans):
    _, peers, rows, _ = kept[0].shape
    part = spans[-1][1]
    half = part * peers
    count = len(spans)

    def kernel(*refs):
        keep, rec, outs, sems = refs[:count], refs[count:2 * count], refs[2 * count:-1], refs[-1]
        p = lax.axis_index("pair")
        moves = []
        for mine, theirs, (low, high) in zip(keep, rec, spans):
            for source, side in ((mine, p), (theirs, 1 - p)):
                for at in range(peers):
                    columns = pl.ds(pl.multiple_of(side * half + at * part + low, HD), high - low)
                    moves += [(source.at[which, at], out.at[:, columns]) for which, out in enumerate(outs)]
        run_moves(moves, sems)

    outs = [shape(rows, 2 * half)] * 3
    return call(kernel, kept + paired, outs, [pltpu.SemaphoreType.DMA((6 * count * peers,))], "laid_out")


def allowed_bias(session, rows):
    strip = rows * lax.axis_size("sub")
    block = 2 * strip
    at_block = lax.axis_index("blk")
    window = jnp.concatenate([jnp.zeros((block,), jnp.int32), session])
    sess = lax.dynamic_slice_in_dim(window, at_block * block, 2 * block)
    place = (at_block - 1) * block + jnp.arange(2 * block, dtype=jnp.int32)

    def tile_bias(tile):
        q_at = slice(block + tile * strip, block + (tile + 1) * strip)
        k_at = slice(tile * strip, (tile + 3) * strip)
        k_place, q_place = place[k_at, None], place[None, q_at]
        allowed = (sess[None, q_at] == sess[k_at, None]) & (k_place <= q_place) & (k_place >= 0)
        return jnp.where(allowed, 0.0, NEG_FILL)

    return jnp.stack([tile_bias(0), tile_bias(1)])


def shards(queries, keys, values, out_grad, session):
    peers = lax.axis_size("sub")
    others = list(range(1, peers))
    part = queries.shape[1] // (2 * peers)
    spans, at = [], 0
    for heads in chunks_of(part // HD):
        spans.append((at, at + heads * HD))
        at += heads * HD
    bias = allowed_bias(session, queries.shape[0])
    kept, paired = [], []
    first_turn, kv_turn, own_turn, qg_turn = [], [], [], []
    for index, (low, high) in enumerate(spans):
        last = index == len(spans) - 1
        send, own = first_parts([keys, values], low, high, first_turn)
        rec = swapped(send)
        sends = head_parts(own, rec, others, kv_turn)
        kv = [round_sub(value, by) for by, value in zip(others, sends)]
        kv_own = head_parts(own, rec, [0], own_turn)
        earlier = [along_blocks(kv_own[0], 1)]
        own_turn = earlier[:]
        earlier += [along_blocks(value, 1) for value in kv]
        send, own = first_parts([queries, out_grad], low, high, [own])
        rec = swapped(send)
        sends = head_parts(own, rec, others, qg_turn)
        qg = [round_sub(value, by) for by, value in zip(others, sends)]
        qg_own = head_parts(own, rec, [0], [])
        first_turn, kv_turn, qg_turn = sends, kv, qg
        grads, dq, early = attention_grads(bias, kv_own + kv, earlier, qg_own + qg, last)
        dq = [dq[0]] + [round_sub(dq[by], by) for by in others]
        if last:
            later = [along_blocks(value, -1) for value in early]
            dkv = summed(grads, later[1:], others, dq[1:])
            dkv = summed(grads, later[:1], [0], []) + [round_sub(value, by) for by, value in zip(others, dkv)]
        else:
            dkv = summed(grads, [along_blocks(early[0], -1)], [0] + others, dq[1:])
            dkv = [dkv[0]] + [round_sub(dkv[by], by) for by in others]
        send, keep = rows_for_pair(dq, dkv)
        kept.append(keep)
        paired.append(swapped(send))
    return tuple(laid_out(kept, paired, spans))


def solution(mesh):
    spread = P(("grp", "blk", "pair", "sub"), None)
    return jax.shard_map(
        shards, mesh=mesh, in_specs=(spread,) * 4 + (P("grp"),), out_specs=(spread,) * 3, check_vma=False
    )
```

time: 92.8 us -> 77.9 us (0.84)
  Pallas kernels: 30.5 us -> 17.4 us
  waiting for transfers between devices: 31.5 us -> 20.5 us
  starting transfers between devices: 27.6 us -> 37.8 us
  local copies, waits for them, and re-layouts: 1.09 us -> 0.11 us
    pallas_call x19 -> x20, Pallas kernels: 30.5 us -> 17.4 us  [the longest x16 12.9 us: call(): pl.pallas_call(kernel, out_shape=outs, in_specs=[spec] * len(ins), out_sp...]
    ppermute x6 -> x7, waiting for transfers between devices: 19 us -> 6.68 us  [along_blocks(): lax.ppermute(value, 'blk', [(i, (i + by) % peers) for i in range(peers)])]
    ppermute x6 -> x7, starting transfers between devices: 17.7 us -> 24.8 us  [along_blocks(): lax.ppermute(value, 'blk', [(i, (i + by) % peers) for i in range(peers)])]
    ppermute x6 -> x8, starting transfers between devices: 8.69 us -> 12.1 us  [round_sub(): lax.ppermute(value, 'sub', [(i, (i + by) % peers) for i in range(peers)])]
    ppermute x6 -> x8, waiting for transfers between devices: 9.39 us -> 12.1 us  [round_sub(): lax.ppermute(value, 'sub', [(i, (i + by) % peers) for i in range(peers)])]
    ppermute x6, waiting for transfers between devices: 3.08 us -> 1.71 us  [swapped(): return lax.ppermute(value, 'pair', [(0, 1), (1, 0)])]
    unnamed x16 -> x2, local copies, waits for them, and re-layouts: 0.98 us -> 0.01 us
  transfers between devices with their start and end apart: 18 -> 21, of which waited for: 8 -> 9; matrix products, arithmetic and copies ran while one was open for 1% -> 1% of each run, Pallas kernels for 12% -> 19%
where the time goes in v4:
time: 77.9 us; the launch traced here: 77.5 us
  starting transfers between devices  37.8 us (49%)
  waiting for transfers between devices  20.5 us (26%)
  Pallas kernels  17.4 us (22%)
  between operations  0.89 us (1%)
  other arithmetic  0.79 us (1%)
    ppermute x7, starting transfers between devices, along_blocks(): lax.ppermute(value, 'blk', [(i, (i + by) % peers) for i in range(peers)])  24.8 us
    pallas_call x16, Pallas kernels, call(): pl.pallas_call(kernel, out_shape=outs, in_specs=[spec] * len(ins), out_sp...  12.9 us
    ppermute x8, waiting for transfers between devices, round_sub(): lax.ppermute(value, 'sub', [(i, (i + by) % peers) for i in range(peers)])  12.1 us
    ppermute x8, starting transfers between devices, round_sub(): lax.ppermute(value, 'sub', [(i, (i + by) % peers) for i in range(peers)])  12.1 us
    ppermute x7, waiting for transfers between devices, along_blocks(): lax.ppermute(value, 'blk', [(i, (i + by) % peers) for i in range(peers)])  6.68 us
    pallas_call x4, Pallas kernels, first_parts(): pl.pallas_call(kernel, out_shape=outs, in_specs=[spec] * (count + len(aft...  4.56 us
    ppermute x6, waiting for transfers between devices, swapped(): return lax.ppermute(value, 'pair', [(0, 1), (1, 0)])  1.71 us
  transfers between devices with their start and end apart: 21, of which 9 were waited for; matrix products, arithmetic and copies ran while one was open for 1% of the time, Pallas kernels for 19%

profile of v4, /device:TPU:0, one launch (start us, length us, event | category | flops | bytes accessed | tf_op | source)
XLA Modules:
  0.0 77.5 jit_solution(12751823280583522791)
XLA Ops:
  0.6 1.1 %first_parts.4 = (bf16[2,2,128,256]{3,2,1,0:T(8,128)(2,1)S(1)}, bf16[2,2,128,256]{3,2,1,0:T(8,128)(2,1)S(1)}) custom-call(bf16[128,2048]{1,0:T(8,128)(2,1)} %refs_0_.6, bf16[128,2048]{1,0:T(8,128)(2,1)} %refs_1_.6), custom_call_target="tpu_custom_call" | custom-call | tf_op jit(solution)/shard_map/first_parts/pallas_call | solution.py:87
  1.8 0.5 collective-permute-start
  2.3 1.1 %first_parts.5 = (bf16[2,2,128,256]{3,2,1,0:T(8,128)(2,1)S(1)}, bf16[2,2,128,256]{3,2,1,0:T(8,128)(2,1)S(1)}) custom-call(bf16[128,2048]{1,0:T(8,128)(2,1)} %refs_0_.7, bf16[128,2048]{1,0:T(8,128)(2,1)} %refs_1_.7, bf16[2,2,128,256]{3,2,1,0:T(8,128)(2,1)S(1)} %get-tuple-element.26.own_ref.refs_2_), custom_call_target="tpu_custom_call" | custom-call | tf_op jit(solution)/shard_map/first_parts/pallas_call | solution.py:87
  3.5 0.1 collective-permute-start.4
  3.6 0.1 pad_dynamic-slice_fusion
  3.7 0.2 head_parts.9
  3.9 3.0 %collective-permute-start.1 = (bf16[2,2,128,256]{3,2,1,0:T(8,128)(2,1)S(1)}, bf16[2,2,128,256]{3,2,1,0:T(8,128)(2,1)S(1)}, u32[]{:S(2)}, u32[]{:S(2)}) collective-permute-start(bf16[2,2,128,256]{3,2,1,0:T(8,128)(2,1)S(1)} %head_parts.9), channel_id=1, source_target_pairs={{0,2},{2,0},{1,3},{3,1},{4,6},{6,4},{5,7},{7,5},{8,10},{10,8},{9,1... | collective-permute-start | bytes 786440 | tf_op jit(solution)/shard_map/ppermute | solution.py:31
  6.9 0.2 head_parts.11.refs_2_
  7.1 1.1 %first_parts.6 = (bf16[2,2,128,256]{3,2,1,0:T(8,128)(2,1)S(1)}, bf16[2,2,128,256]{3,2,1,0:T(8,128)(2,1)S(1)}) custom-call(bf16[128,2048]{1,0:T(8,128)(2,1)} %refs_0_.6, bf16[128,2048]{1,0:T(8,128)(2,1)} %refs_1_.6, bf16[2,2,128,256]{3,2,1,0:T(8,128)(2,1)S(1)} %head_parts.11.refs_2_), custom_call_target="tpu_custom_call" | custom-call | tf_op jit(solution)/shard_map/first_parts/pallas_call | solution.py:87
  8.2 0.1 collective-permute-start.9
  8.3 1.1 %collective-permute-start.5 = (bf16[2,2,128,256]{3,2,1,0:T(8,128)(2,1)S(1)}, bf16[2,2,128,256]{3,2,1,0:T(8,128)(2,1)S(1)}, u32[]{:S(2)}, u32[]{:S(2)}) collective-permute-start(bf16[2,2,128,256]{3,2,1,0:T(8,128)(2,1)S(1)} %head_parts.11.refs_2_), channel_id=1, source_target_pairs={{0,2},{2,0},{1,3},{3,1},{4,6},{6,4},{5,7},{7,5},{8,10},{10,8},{9,1... | collective-permute-start | bytes 786440 | tf_op jit(solution)/shard_map/ppermute | solution.py:31
  9.5 0.2 head_parts.8.refs_1_
  9.6 1.6 %collective-permute-start.2 = (bf16[2,2,128,256]{3,2,1,0:T(8,128)(2,1)S(1)}, bf16[2,2,128,256]{3,2,1,0:T(8,128)(2,1)S(1)}, u32[]{:S(2)}, u32[]{:S(2)}) collective-permute-start(bf16[2,2,128,256]{3,2,1,0:T(8,128)(2,1)S(1)} %head_parts.8.refs_1_), channel_id=1, source_target_pairs={{0,4},{4,8},{8,12},{12,0},{1,5},{5,9},{9,13},{13,1},{2,6},{6,10},{... | collective-permute-start | bytes 786440 | tf_op jit(solution)/shard_map/ppermute | solution.py:26
  11.3 1.1 %first_parts.7 = (bf16[2,2,128,256]{3,2,1,0:T(8,128)(2,1)S(1)}, bf16[2,2,128,256]{3,2,1,0:T(8,128)(2,1)S(1)}) custom-call(bf16[128,2048]{1,0:T(8,128)(2,1)} %refs_0_.7, bf16[128,2048]{1,0:T(8,128)(2,1)} %refs_1_.7, bf16[2,2,128,256]{3,2,1,0:T(8,128)(2,1)S(1)} %get-tuple-element.37.own_ref.refs_2_), custom_call_target="tpu_custom_call" | custom-call | tf_op jit(solution)/shard_map/first_parts/pallas_call | solution.py:87
  12.5 1.5 %collective-permute-done.1.refs_2_.refs_0_ = bf16[2,2,128,256]{3,2,1,0:T(8,128)(2,1)S(1)} collective-permute-done((bf16[2,2,128,256]{3,2,1,0:T(8,128)(2,1)S(1)}, bf16[2,2,128,256]{3,2,1,0:T(8,128)(2,1)S(1)}, u32[]{:S(2)}, u32[]{:S(2)}) %collective-permute-start.1) | collective-permute-done | bytes 262176 | tf_op jit(solution)/shard_map/ppermute | solution.py:31
  14.0 0.2 head_parts.13
  14.2 2.1 %collective-permute-start.10 = (bf16[2,2,128,256]{3,2,1,0:T(8,128)(2,1)S(1)}, bf16[2,2,128,256]{3,2,1,0:T(8,128)(2,1)S(1)}, u32[]{:S(2)}, u32[]{:S(2)}) collective-permute-start(bf16[2,2,128,256]{3,2,1,0:T(8,128)(2,1)S(1)} %head_parts.13), channel_id=1, source_target_pairs={{0,2},{2,0},{1,3},{3,1},{4,6},{6,4},{5,7},{7,5},{8,10},{10,8},{9,1... | collective-permute-start | bytes 786440 | tf_op jit(solution)/shard_map/ppermute | solution.py:31
  16.3 1.6 %collective-permute-start.3 = (bf16[2,2,128,256]{3,2,1,0:T(8,128)(2,1)S(1)}, bf16[2,2,128,256]{3,2,1,0:T(8,128)(2,1)S(1)}, u32[]{:S(2)}, u32[]{:S(2)}) collective-permute-start(bf16[2,2,128,256]{3,2,1,0:T(8,128)(2,1)S(1)} %collective-permute-done.1.refs_2_.refs_0_), channel_id=1, source_target_pairs={{0,4},{4,8},{8,12},{12,0},{1,5},{5,9},{9,13},{13,1},{2,6},{6,10},{... | collective-permute-start | bytes 786440 | tf_op jit(solution)/shard_map/ppermute | solution.py:26
  17.9 0.7 and_select_fusion
  18.6 0.1 pad_maximum_fusion.refs_0_
  18.7 0.2 head_parts.10.refs_5_
  18.9 1.6 %collective-permute-done.2.refs_3_.refs_0_ = bf16[2,2,128,256]{3,2,1,0:T(8,128)(2,1)S(1)} collective-permute-done((bf16[2,2,128,256]{3,2,1,0:T(8,128)(2,1)S(1)}, bf16[2,2,128,256]{3,2,1,0:T(8,128)(2,1)S(1)}, u32[]{:S(2)}, u32[]{:S(2)}) %collective-permute-start.2) | collective-permute-done | bytes 262176 | tf_op jit(solution)/shard_map/ppermute | solution.py:26
  20.5 0.2 head_parts.12.refs_1_
  20.6 0.1 collective-permute-start.11
  20.8 0.2 head_parts.15
  21.0 1.2 %collective-permute-start.14 = (bf16[2,2,128,256]{3,2,1,0:T(8,128)(2,1)S(1)}, bf16[2,2,128,256]{3,2,1,0:T(8,128)(2,1)S(1)}, u32[]{:S(2)}, u32[]{:S(2)}) collective-permute-start(bf16[2,2,128,256]{3,2,1,0:T(8,128)(2,1)S(1)} %head_parts.15), channel_id=1, source_target_pairs={{0,2},{2,0},{1,3},{3,1},{4,6},{6,4},{5,7},{7,5},{8,10},{10,8},{9,1... | collective-permute-start | bytes 786440 | tf_op jit(solution)/shard_map/ppermute | solution.py:31
  22.1 3.1 %collective-permute-done.10.refs_2_ = bf16[2,2,128,256]{3,2,1,0:T(8,128)(2,1)S(1)} collective-permute-done((bf16[2,2,128,256]{3,2,1,0:T(8,128)(2,1)S(1)}, bf16[2,2,128,256]{3,2,1,0:T(8,128)(2,1)S(1)}, u32[]{:S(2)}, u32[]{:S(2)}) %collective-permute-start.10) | collective-permute-done | bytes 262176 | tf_op jit(solution)/shard_map/ppermute | solution.py:31
  25.2 2.1 %collective-permute-start.12 = (bf16[2,2,128,256]{3,2,1,0:T(8,128)(2,1)S(1)}, bf16[2,2,128,256]{3,2,1,0:T(8,128)(2,1)S(1)}, u32[]{:S(2)}, u32[]{:S(2)}) collective-permute-start(bf16[2,2,128,256]{3,2,1,0:T(8,128)(2,1)S(1)} %collective-permute-done.10.refs_2_), channel_id=1, source_target_pairs={{0,4},{4,8},{8,12},{12,0},{1,5},{5,9},{9,13},{13,1},{2,6},{6,10},{... | collective-permute-start | bytes 786440 | tf_op jit(solution)/shard_map/ppermute | solution.py:26
  27.4 4.2 %attention_grads.2 = (f32[2,2,2,128,256]{4,3,2,1,0:T(8,128)S(1)}, bf16[2,128,256]{2,1,0:T(8,128)(2,1)S(1)}, bf16[2,128,256]{2,1,0:T(8,128)(2,1)S(1)}, bf16[2,2,2,128,256]{4,3,2,1,0:T(8,128)(2,1)S(1)}) custom-call(f32[2,768,256]{2,1,0:T(8,128)S(1)} %pad_maximum_fusion.refs_0_, bf16[2,2,128,256]{3,2,1,0:T(8,128)(2,1)S(1)} %head_parts.8.refs_1_, ...), custom_call_target="tpu_custom_call" | custom-call | flops 1006632960 | bytes 4980736 | tf_op jit(solution)/shard_map/attention_grads/pallas_call | solution.py:50
  31.6 2.1 %collective-permute-start.7 = (bf16[2,2,2,128,256]{4,3,2,1,0:T(8,128)(2,1)S(1)}, bf16[2,2,2,128,256]{4,3,2,1,0:T(8,128)(2,1)S(1)}, u32[]{:S(2)}, u32[]{:S(2)}) collective-permute-start(bf16[2,2,2,128,256]{4,3,2,1,0:T(8,128)(2,1)S(1)} %get-tuple-element.33), channel_id=1, source_target_pairs={{0,12},{4,0},{8,4},{12,8},{1,13},{5,1},{9,5},{13,9},{2,14},{6,2},{... | collective-permute-start | bytes 1572872 | tf_op jit(solution)/shard_map/ppermute | solution.py:26
  33.7 0.2 head_parts.14.refs_5_
  33.9 4.4 %collective-permute-done.12.refs_4_ = bf16[2,2,128,256]{3,2,1,0:T(8,128)(2,1)S(1)} collective-permute-done((bf16[2,2,128,256]{3,2,1,0:T(8,128)(2,1)S(1)}, bf16[2,2,128,256]{3,2,1,0:T(8,128)(2,1)S(1)}, u32[]{:S(2)}, u32[]{:S(2)}) %collective-permute-start.12) | collective-permute-done | bytes 262176 | tf_op jit(solution)/shard_map/ppermute | solution.py:26
  38.3 4.2 %attention_grads.3 = (f32[2,2,2,128,256]{4,3,2,1,0:T(8,128)S(1)}, bf16[2,128,256]{2,1,0:T(8,128)(2,1)S(1)}, bf16[2,128,256]{2,1,0:T(8,128)(2,1)S(1)}, bf16[2,2,1...) custom-call(f32[2,768,256]{2,1,0:T(8,128)S(1)} %pad_maximum_fusion.refs_0_, ...), custom_call_target="tpu_custom_call" | custom-call | flops 1006632960 | bytes 4980736 | tf_op jit(solution)/shard_map/attention_grads/pallas_call | solution.py:50
  42.6 16.8 %collective-permute-start.17 = (bf16[2,2,128,256]{3,2,1,0:T(8,128)(2,1)S(1)}, bf16[2,2,128,256]{3,2,1,0:T(8,128)(2,1)S(1)}, u32[]{:S(2)}, u32[]{:S(2)}) collective-permute-start(bf16[2,2,128,256]{3,2,1,0:T(8,128)(2,1)S(1)} %get-tuple-element.45), channel_id=1, source_target_pairs={{0,12},{4,0},{8,4},{12,8},{1,13},{5,1},{9,5},{13,9},{2,14},{6,2},{... | collective-permute-start | bytes 786440 | tf_op jit(solution)/shard_map/ppermute | solution.py:26
  59.4 1.2 %collective-permute-start.6 = (bf16[2,128,256]{2,1,0:T(8,128)(2,1)S(1)}, bf16[2,128,256]{2,1,0:T(8,128)(2,1)S(1)}, u32[]{:S(2)}, u32[]{:S(2)}) collective-permute-start(bf16[2,128,256]{2,1,0:T(8,128)(2,1)S(1)} %get-tuple-element.31), channel_id=1, source_target_pairs={{0,2},{2,0},{1,3},{3,1},{4,6},{6,4},{5,7},{7,5},{8,10},{10,8},{9,1... | collective-permute-start | bytes 393224 | tf_op jit(solution)/shard_map/ppermute | solution.py:31
  60.6 0.8 %collective-permute-start.15 = (bf16[2,128,256]{2,1,0:T(8,128)(2,1)S(1)}, bf16[2,128,256]{2,1,0:T(8,128)(2,1)S(1)}, u32[]{:S(2)}, u32[]{:S(2)}) collective-permute-start(bf16[2,128,256]{2,1,0:T(8,128)(2,1)S(1)} %get-tuple-element.42), channel_id=1, source_target_pairs={{0,2},{2,0},{1,3},{3,1},{4,6},{6,4},{5,7},{7,5},{8,10},{10,8},{9,1... | collective-permute-start | bytes 393224 | tf_op jit(solution)/shard_map/ppermute | solution.py:31
  61.4 0.5 collective-permute-start.16
  61.9 2.5 %collective-permute-done.6.refs_1_ = bf16[2,128,256]{2,1,0:T(8,128)(2,1)S(1)} collective-permute-done((bf16[2,128,256]{2,1,0:T(8,128)(2,1)S(1)}, bf16[2,128,256]{2,1,0:T(8,128)(2,1)S(1)}, u32[]{:S(2)}, u32[]{:S(2)}) %collective-permute-start.6) | collective-permute-done | bytes 131104 | tf_op jit(solution)/shard_map/ppermute | solution.py:31
  64.3 0.1 summed.3
  64.4 1.3 %collective-permute-start.8 = (bf16[2,2,128,256]{3,2,1,0:T(8,128)(2,1)S(1)}, bf16[2,2,128,256]{3,2,1,0:T(8,128)(2,1)S(1)}, u32[]{:S(2)}, u32[]{:S(2)}) collective-permute-start(bf16[2,2,128,256]{3,2,1,0:T(8,128)(2,1)S(1)} %get-tuple-element.35), channel_id=1, source_target_pairs={{0,2},{2,0},{1,3},{3,1},{4,6},{6,4},{5,7},{7,5},{8,10},{10,8},{9,1... | collective-permute-start | bytes 786440 | tf_op jit(solution)/shard_map/ppermute | solution.py:31
  65.8 1.3 %collective-permute-start.18 = (bf16[2,2,128,256]{3,2,1,0:T(8,128)(2,1)S(1)}, bf16[2,2,128,256]{3,2,1,0:T(8,128)(2,1)S(1)}, u32[]{:S(2)}, u32[]{:S(2)}) collective-permute-start(bf16[2,2,128,256]{3,2,1,0:T(8,128)(2,1)S(1)} %summed.5), channel_id=1, source_target_pairs={{0,2},{2,0},{1,3},{3,1},{4,6},{6,4},{5,7},{7,5},{8,10},{10,8},{9,1... | collective-permute-start | bytes 786440 | tf_op jit(solution)/shard_map/ppermute | solution.py:31
  67.1 0.7 collective-permute-done.16.refs_0_
  67.8 3.0 %collective-permute-done.8.refs_3_ = bf16[2,2,128,256]{3,2,1,0:T(8,128)(2,1)S(1)} collective-permute-done((bf16[2,2,128,256]{3,2,1,0:T(8,128)(2,1)S(1)}, bf16[2,2,128,256]{3,2,1,0:T(8,128)(2,1)S(1)}, u32[]{:S(2)}, u32[]{:S(2)}) %collective-permute-start.8) | collective-permute-done | bytes 262176 | tf_op jit(solution)/shard_map/ppermute | solution.py:31
  70.9 0.7 rows_for_pair.2
  71.7 2.0 %collective-permute-done.18.refs_3_ = bf16[2,2,128,256]{3,2,1,0:T(8,128)(2,1)S(1)} collective-permute-done((bf16[2,2,128,256]{3,2,1,0:T(8,128)(2,1)S(1)}, bf16[2,2,128,256]{3,2,1,0:T(8,128)(2,1)S(1)}, u32[]{:S(2)}, u32[]{:S(2)}) %collective-permute-start.18) | collective-permute-done | bytes 262176 | tf_op jit(solution)/shard_map/ppermute | solution.py:31
  73.7 0.7 rows_for_pair.3
  74.5 1.7 %collective-permute-done.20.refs_3_ = bf16[3,2,128,256]{3,2,1,0:T(8,128)(2,1)S(1)} collective-permute-done((bf16[3,2,128,256]{3,2,1,0:T(8,128)(2,1)S(1)}, bf16[3,2,128,256]{3,2,1,0:T(8,128)(2,1)S(1)}, u32[]{:S(2)}, u32[]{:S(2)}) %collective-permute-start.20) | collective-permute-done | bytes 393248 | tf_op jit(solution)/shard_map/ppermute | solution.py:35
  76.2 1.3 %laid_out.1 = (bf16[128,2048]{1,0:T(8,128)(2,1)}, bf16[128,2048]{1,0:T(8,128)(2,1)}, bf16[128,2048]{1,0:T(8,128)(2,1)}) custom-call(bf16[3,2,128,256]{3,2,1,0:T(8,128)(2,1)S(1)} %get-tuple-element.36.refs_0_, bf16[3,2,128,256]{3,2,1,0:T(8,128)(2,1)S(1)} %get-tuple-element.46.refs_1_, bf16[3,2,128,256]{3,2,1,0:T(8,128)(2,1)S(1)} %collective-permute-done.19.refs_2_, ...), custom_call_target="tpu_custom_call" | custom-call | bytes 3145728 | tf_op jit(solution)/shard_map/laid_out/pallas_call | solution.py:50
  (25 shorter events, 0.4 us)
Async XLA Ops:
  0.6 3.0 %copy-start = (s32[2048]{0:T(1024)S(1)}, s32[2048]{0:T(1024)}, u32[]{:S(2)}) copy-start(s32[2048]{0:T(1024)} %param.9) | copy-start | bytes 24580
  1.8 1.9 %collective-permute-start = (bf16[2,2,128,256]{3,2,1,0:T(8,128)(2,1)S(1)}, bf16[2,2,128,256]{3,2,1,0:T(8,128)(2,1)S(1)}, u32[]{:S(2)}, u32[]{:S(2)}) collective-permute-start(bf16[2,2,128,256]{3,2,1,0:T(8,128)(2,1)S(1)} %get-tuple-element.27), channel_id=1, source_target_pairs={{0,1},{1,0},{2,3},{3,2},{4,5},{5,4},{6,7},{7,6},{8,9},{9,8},{10,11... | collective-permute-start | bytes 786440 | tf_op jit(solution)/shard_map/ppermute | solution.py:35
  3.5 3.4 %collective-permute-start.4 = (bf16[2,2,128,256]{3,2,1,0:T(8,128)(2,1)S(1)}, bf16[2,2,128,256]{3,2,1,0:T(8,128)(2,1)S(1)}, u32[]{:S(2)}, u32[]{:S(2)}) collective-permute-start(bf16[2,2,128,256]{3,2,1,0:T(8,128)(2,1)S(1)} %get-tuple-element.29), channel_id=1, source_target_pairs={{0,1},{1,0},{2,3},{3,2},{4,5},{5,4},{6,7},{7,6},{8,9},{9,8},{10,11... | collective-permute-start | bytes 786440 | tf_op jit(solution)/shard_map/ppermute | solution.py:35
  3.9 10.1 %collective-permute-start.1 = (bf16[2,2,128,256]{3,2,1,0:T(8,128)(2,1)S(1)}, bf16[2,2,128,256]{3,2,1,0:T(8,128)(2,1)S(1)}, u32[]{:S(2)}, u32[]{:S(2)}) collective-permute-start(bf16[2,2,128,256]{3,2,1,0:T(8,128)(2,1)S(1)} %head_parts.9), channel_id=1, source_target_pairs={{0,2},{2,0},{1,3},{3,1},{4,6},{6,4},{5,7},{7,5},{8,10},{10,8},{9,1... | collective-permute-start | bytes 786440 | tf_op jit(solution)/shard_map/ppermute | solution.py:31
  8.2 5.8 %collective-permute-start.9 = (bf16[2,2,128,256]{3,2,1,0:T(8,128)(2,1)S(1)}, bf16[2,2,128,256]{3,2,1,0:T(8,128)(2,1)S(1)}, u32[]{:S(2)}, u32[]{:S(2)}) collective-permute-start(bf16[2,2,128,256]{3,2,1,0:T(8,128)(2,1)S(1)} %get-tuple-element.38), channel_id=1, source_target_pairs={{0,1},{1,0},{2,3},{3,2},{4,5},{5,4},{6,7},{7,6},{8,9},{9,8},{10,11... | collective-permute-start | bytes 786440 | tf_op jit(solution)/shard_map/ppermute | solution.py:35
  8.3 12.4 %collective-permute-start.5 = (bf16[2,2,128,256]{3,2,1,0:T(8,128)(2,1)S(1)}, bf16[2,2,128,256]{3,2,1,0:T(8,128)(2,1)S(1)}, u32[]{:S(2)}, u32[]{:S(2)}) collective-permute-start(bf16[2,2,128,256]{3,2,1,0:T(8,128)(2,1)S(1)} %head_parts.11.refs_2_), channel_id=1, source_target_pairs={{0,2},{2,0},{1,3},{3,1},{4,6},{6,4},{5,7},{7,5},{8,10},{10,8},{9,1... | collective-permute-start | bytes 786440 | tf_op jit(solution)/shard_map/ppermute | solution.py:31
  9.6 10.8 %collective-permute-start.2 = (bf16[2,2,128,256]{3,2,1,0:T(8,128)(2,1)S(1)}, bf16[2,2,128,256]{3,2,1,0:T(8,128)(2,1)S(1)}, u32[]{:S(2)}, u32[]{:S(2)}) collective-permute-start(bf16[2,2,128,256]{3,2,1,0:T(8,128)(2,1)S(1)} %head_parts.8.refs_1_), channel_id=1, source_target_pairs={{0,4},{4,8},{8,12},{12,0},{1,5},{5,9},{9,13},{13,1},{2,6},{6,10},{... | collective-permute-start | bytes 786440 | tf_op jit(solution)/shard_map/ppermute | solution.py:26
  12.4 8.3 %collective-permute-start.13 = (bf16[2,2,128,256]{3,2,1,0:T(8,128)(2,1)S(1)}, bf16[2,2,128,256]{3,2,1,0:T(8,128)(2,1)S(1)}, u32[]{:S(2)}, u32[]{:S(2)}) collective-permute-start(bf16[2,2,128,256]{3,2,1,0:T(8,128)(2,1)S(1)} %get-tuple-element.40), channel_id=1, source_target_pairs={{0,1},{1,0},{2,3},{3,2},{4,5},{5,4},{6,7},{7,6},{8,9},{9,8},{10,11... | collective-permute-start | bytes 786440 | tf_op jit(solution)/shard_map/ppermute | solution.py:35
  14.2 11.0 %collective-permute-start.10 = (bf16[2,2,128,256]{3,2,1,0:T(8,128)(2,1)S(1)}, bf16[2,2,128,256]{3,2,1,0:T(8,128)(2,1)S(1)}, u32[]{:S(2)}, u32[]{:S(2)}) collective-permute-start(bf16[2,2,128,256]{3,2,1,0:T(8,128)(2,1)S(1)} %head_parts.13), channel_id=1, source_target_pairs={{0,2},{2,0},{1,3},{3,1},{4,6},{6,4},{5,7},{7,5},{8,10},{10,8},{9,1... | collective-permute-start | bytes 786440 | tf_op jit(solution)/shard_map/ppermute | solution.py:31
  16.3 11.1 %collective-permute-start.3 = (bf16[2,2,128,256]{3,2,1,0:T(8,128)(2,1)S(1)}, bf16[2,2,128,256]{3,2,1,0:T(8,128)(2,1)S(1)}, u32[]{:S(2)}, u32[]{:S(2)}) collective-permute-start(bf16[2,2,128,256]{3,2,1,0:T(8,128)(2,1)S(1)} %collective-permute-done.1.refs_2_.refs_0_), channel_id=1, source_target_pairs={{0,4},{4,8},{8,12},{12,0},{1,5},{5,9},{9,13},{13,1},{2,6},{6,10},{... | collective-permute-start | bytes 786440 | tf_op jit(solution)/shard_map/ppermute | solution.py:26
  20.6 13.2 %collective-permute-start.11 = (bf16[2,2,128,256]{3,2,1,0:T(8,128)(2,1)S(1)}, bf16[2,2,128,256]{3,2,1,0:T(8,128)(2,1)S(1)}, u32[]{:S(2)}, u32[]{:S(2)}) collective-permute-start(bf16[2,2,128,256]{3,2,1,0:T(8,128)(2,1)S(1)} %head_parts.12.refs_1_), channel_id=1, source_target_pairs={{0,4},{4,8},{8,12},{12,0},{1,5},{5,9},{9,13},{13,1},{2,6},{6,10},{... | collective-permute-start | bytes 786440 | tf_op jit(solution)/shard_map/ppermute | solution.py:26
  21.0 12.9 %collective-permute-start.14 = (bf16[2,2,128,256]{3,2,1,0:T(8,128)(2,1)S(1)}, bf16[2,2,128,256]{3,2,1,0:T(8,128)(2,1)S(1)}, u32[]{:S(2)}, u32[]{:S(2)}) collective-permute-start(bf16[2,2,128,256]{3,2,1,0:T(8,128)(2,1)S(1)} %head_parts.15), channel_id=1, source_target_pairs={{0,2},{2,0},{1,3},{3,1},{4,6},{6,4},{5,7},{7,5},{8,10},{10,8},{9,1... | collective-permute-start | bytes 786440 | tf_op jit(solution)/shard_map/ppermute | solution.py:31
  25.2 13.1 %collective-permute-start.12 = (bf16[2,2,128,256]{3,2,1,0:T(8,128)(2,1)S(1)}, bf16[2,2,128,256]{3,2,1,0:T(8,128)(2,1)S(1)}, u32[]{:S(2)}, u32[]{:S(2)}) collective-permute-start(bf16[2,2,128,256]{3,2,1,0:T(8,128)(2,1)S(1)} %collective-permute-done.10.refs_2_), channel_id=1, source_target_pairs={{0,4},{4,8},{8,12},{12,0},{1,5},{5,9},{9,13},{13,1},{2,6},{6,10},{... | collective-permute-start | bytes 786440 | tf_op jit(solution)/shard_map/ppermute | solution.py:26
  31.6 32.7 %collective-permute-start.7 = (bf16[2,2,2,128,256]{4,3,2,1,0:T(8,128)(2,1)S(1)}, bf16[2,2,2,128,256]{4,3,2,1,0:T(8,128)(2,1)S(1)}, u32[]{:S(2)}, u32[]{:S(2)}) collective-permute-start(bf16[2,2,2,128,256]{4,3,2,1,0:T(8,128)(2,1)S(1)} %get-tuple-element.33), channel_id=1, source_target_pairs={{0,12},{4,0},{8,4},{12,8},{1,13},{5,1},{9,5},{13,9},{2,14},{6,2},{... | collective-permute-start | bytes 1572872 | tf_op jit(solution)/shard_map/ppermute | solution.py:26
  42.6 23.2 %collective-permute-start.17 = (bf16[2,2,128,256]{3,2,1,0:T(8,128)(2,1)S(1)}, bf16[2,2,128,256]{3,2,1,0:T(8,128)(2,1)S(1)}, u32[]{:S(2)}, u32[]{:S(2)}) collective-permute-start(bf16[2,2,128,256]{3,2,1,0:T(8,128)(2,1)S(1)} %get-tuple-element.45), channel_id=1, source_target_pairs={{0,12},{4,0},{8,4},{12,8},{1,13},{5,1},{9,5},{13,9},{2,14},{6,2},{... | collective-permute-start | bytes 786440 | tf_op jit(solution)/shard_map/ppermute | solution.py:26
  59.4 5.0 %collective-permute-start.6 = (bf16[2,128,256]{2,1,0:T(8,128)(2,1)S(1)}, bf16[2,128,256]{2,1,0:T(8,128)(2,1)S(1)}, u32[]{:S(2)}, u32[]{:S(2)}) collective-permute-start(bf16[2,128,256]{2,1,0:T(8,128)(2,1)S(1)} %get-tuple-element.31), channel_id=1, source_target_pairs={{0,2},{2,0},{1,3},{3,1},{4,6},{6,4},{5,7},{7,5},{8,10},{10,8},{9,1... | collective-permute-start | bytes 393224 | tf_op jit(solution)/shard_map/ppermute | solution.py:31
  60.6 5.1 %collective-permute-start.15 = (bf16[2,128,256]{2,1,0:T(8,128)(2,1)S(1)}, bf16[2,128,256]{2,1,0:T(8,128)(2,1)S(1)}, u32[]{:S(2)}, u32[]{:S(2)}) collective-permute-start(bf16[2,128,256]{2,1,0:T(8,128)(2,1)S(1)} %get-tuple-element.42), channel_id=1, source_target_pairs={{0,2},{2,0},{1,3},{3,1},{4,6},{6,4},{5,7},{7,5},{8,10},{10,8},{9,1... | collective-permute-start | bytes 393224 | tf_op jit(solution)/shard_map/ppermute | solution.py:31
  61.4 6.4 %collective-permute-start.16 = (bf16[2,2,128,256]{3,2,1,0:T(8,128)(2,1)S(1)}, bf16[2,2,128,256]{3,2,1,0:T(8,128)(2,1)S(1)}, u32[]{:S(2)}, u32[]{:S(2)}) collective-permute-start(bf16[2,2,128,256]{3,2,1,0:T(8,128)(2,1)S(1)} %get-tuple-element.44), channel_id=1, source_target_pairs={{0,12},{4,0},{8,4},{12,8},{1,13},{5,1},{9,5},{13,9},{2,14},{6,2},{... | collective-permute-start | bytes 786440 | tf_op jit(solution)/shard_map/ppermute | solution.py:26
  64.4 6.4 %collective-permute-start.8 = (bf16[2,2,128,256]{3,2,1,0:T(8,128)(2,1)S(1)}, bf16[2,2,128,256]{3,2,1,0:T(8,128)(2,1)S(1)}, u32[]{:S(2)}, u32[]{:S(2)}) collective-permute-start(bf16[2,2,128,256]{3,2,1,0:T(8,128)(2,1)S(1)} %get-tuple-element.35), channel_id=1, source_target_pairs={{0,2},{2,0},{1,3},{3,1},{4,6},{6,4},{5,7},{7,5},{8,10},{10,8},{9,1... | collective-permute-start | bytes 786440 | tf_op jit(solution)/shard_map/ppermute | solution.py:31
  65.8 7.9 %collective-permute-start.18 = (bf16[2,2,128,256]{3,2,1,0:T(8,128)(2,1)S(1)}, bf16[2,2,128,256]{3,2,1,0:T(8,128)(2,1)S(1)}, u32[]{:S(2)}, u32[]{:S(2)}) collective-permute-start(bf16[2,2,128,256]{3,2,1,0:T(8,128)(2,1)S(1)} %summed.5), channel_id=1, source_target_pairs={{0,2},{2,0},{1,3},{3,1},{4,6},{6,4},{5,7},{7,5},{8,10},{10,8},{9,1... | collective-permute-start | bytes 786440 | tf_op jit(solution)/shard_map/ppermute | solution.py:31
  71.6 2.9 %collective-permute-start.19 = (bf16[3,2,128,256]{3,2,1,0:T(8,128)(2,1)S(1)}, bf16[3,2,128,256]{3,2,1,0:T(8,128)(2,1)S(1)}, u32[]{:S(2)}, u32[]{:S(2)}) collective-permute-start(bf16[3,2,128,256]{3,2,1,0:T(8,128)(2,1)S(1)} %get-tuple-element.47), channel_id=1, source_target_pairs={{0,1},{1,0},{2,3},{3,2},{4,5},{5,4},{6,7},{7,6},{8,9},{9,8},{10,11... | collective-permute-start | bytes 1179656 | tf_op jit(solution)/shard_map/ppermute | solution.py:35
  74.4 1.8 %collective-permute-start.20 = (bf16[3,2,128,256]{3,2,1,0:T(8,128)(2,1)S(1)}, bf16[3,2,128,256]{3,2,1,0:T(8,128)(2,1)S(1)}, u32[]{:S(2)}, u32[]{:S(2)}) collective-permute-start(bf16[3,2,128,256]{3,2,1,0:T(8,128)(2,1)S(1)} %get-tuple-element.48), channel_id=1, source_target_pairs={{0,1},{1,0},{2,3},{3,2},{4,5},{5,4},{6,7},{7,6},{8,9},{9,8},{10,11... | collective-permute-start | bytes 1179656 | tf_op jit(solution)/shard_map/ppermute | solution.py:35

commit v5 on v4

--- a/solution.py
+++ b/solution.py
@@ -21,9 +21,10 @@
     return [heads // 2, heads - heads // 2]
 
 
-def along_blocks(value, by):
+def along_blocks(value, by, ring):
     peers = lax.axis_size("blk")
-    return lax.ppermute(value, "blk", [(i, (i + by) % peers) for i in range(peers)])
+    pairs = [(i, (i + by) % peers) for i in range(peers) if ring or 0 <= i + by < peers]
+    return lax.ppermute(value, "blk", pairs)
 
 
 def round_sub(value, by):
@@ -110,6 +111,14 @@
     outs = [shape(count, 2, rows, cut)] * len(turns)
     scratch = [pltpu.SemaphoreType.DMA((2 * len(turns),))]
     return call(kernel, [own, paired] + after, outs, scratch, "head_parts")
+
+
+def relayed(value, after):
+    def kernel(value_ref, *refs):
+        run_moves([(value_ref, refs[-2])], refs[-1])
+
+    scratch = [pltpu.SemaphoreType.DMA((1,))]
+    return call(kernel, [value] + after, [shape(*value.shape)], scratch, "relayed")[0]
 
 
 def attention_grads(bias, kv, kv_earlier, qg, split):
@@ -282,7 +291,7 @@
         at += heads * HD
     bias = allowed_bias(session, queries.shape[0])
     kept, paired = [], []
-    first_turn, kv_turn, own_turn, qg_turn = [], [], [], []
+    first_turn, kv_turn, own_turn, qg_turn, last_turn = [], [], [], [], []
     for index, (low, high) in enumerate(spans):
         last = index == len(spans) - 1
         send, own = first_parts([keys, values], low, high, first_turn)
@@ -290,9 +299,12 @@
         sends = head_parts(own, rec, others, kv_turn)
         kv = [round_sub(value, by) for by, value in zip(others, sends)]
         kv_own = head_parts(own, rec, [0], own_turn)
-        earlier = [along_blocks(kv_own[0], 1)]
+        earlier = [along_blocks(kv_own[0], 1, True)]
         own_turn = earlier[:]
-        earlier += [along_blocks(value, 1) for value in kv]
+        if last:
+            earlier += [along_blocks(relayed(value, last_turn), 1, False) for value in kv]
+        else:
+            earlier += [along_blocks(value, 1, True) for value in kv]
         send, own = first_parts([queries, out_grad], low, high, [own])
         rec = swapped(send)
         sends = head_parts(own, rec, others, qg_turn)
@@ -300,13 +312,14 @@
         qg_own = head_parts(own, rec, [0], [])
         first_turn, kv_turn, qg_turn = sends, kv, qg
         grads, dq, early = attention_grads(bias, kv_own + kv, earlier, qg_own + qg, last)
+        last_turn = [dq[0]]
         dq = [dq[0]] + [round_sub(dq[by], by) for by in others]
         if last:
-            later = [along_blocks(value, -1) for value in early]
+            later = [along_blocks(value, -1, False) for value in early]
             dkv = summed(grads, later[1:], others, dq[1:])
             dkv = summed(grads, later[:1], [0], []) + [round_sub(value, by) for by, value in zip(others, dkv)]
         else:
-            dkv = summed(grads, [along_blocks(early[0], -1)], [0] + others, dq[1:])
+            dkv = summed(grads, [along_blocks(early[0], -1, False)], [0] + others, dq[1:])
             dkv = [dkv[0]] + [round_sub(dkv[by], by) for by in others]
         send, keep = rows_for_pair(dq, dkv)
         kept.append(keep)

time: 77.9 us -> 63.9 us (0.82)
  starting transfers between devices: 37.8 us -> 22.6 us
  waiting for transfers between devices: 20.5 us -> 21.6 us
    ppermute x7, starting transfers between devices: 24.8 us -> 9.13 us  [along_blocks(): return lax.ppermute(value, 'blk', pairs)]
    ppermute x7, waiting for transfers between devices: 6.68 us -> 11.4 us  [along_blocks(): return lax.ppermute(value, 'blk', pairs)]
    ppermute x8, waiting for transfers between devices: 12.1 us -> 8.43 us  [round_sub(): lax.ppermute(value, 'sub', [(i, (i + by) % peers) for i in range(peers)])]
    pallas_call x16 -> x17, Pallas kernels: 12.9 us -> 12.9 us  [call(): pl.pallas_call(kernel, out_shape=outs, in_specs=[spec] * len(ins), out_sp...]
  transfers between devices with their start and end apart: 21 -> 21, of which waited for: 9 -> 11; matrix products, arithmetic and copies ran while one was open for 1% -> 1% of each run, Pallas kernels for 19% -> 24%
where the time goes in v5:
time: 63.9 us; the launch traced here: 63.5 us
  starting transfers between devices  22.6 us (35%)
  waiting for transfers between devices  21.6 us (34%)
  Pallas kernels  17.5 us (27%)
  between operations  0.94 us (1%)
  other arithmetic  0.79 us (1%)
    pallas_call x17, Pallas kernels, call(): pl.pallas_call(kernel, out_shape=outs, in_specs=[spec] * len(ins), out_sp...  12.9 us
    ppermute x8, starting transfers between devices, round_sub(): lax.ppermute(value, 'sub', [(i, (i + by) % peers) for i in range(peers)])  12.6 us
    ppermute x7, waiting for transfers between devices, along_blocks(): return lax.ppermute(value, 'blk', pairs)  11.4 us
    ppermute x7, starting transfers between devices, along_blocks(): return lax.ppermute(value, 'blk', pairs)  9.13 us
    ppermute x8, waiting for transfers between devices, round_sub(): lax.ppermute(value, 'sub', [(i, (i + by) % peers) for i in range(peers)])  8.43 us
    pallas_call x4, Pallas kernels, first_parts(): pl.pallas_call(kernel, out_shape=outs, in_specs=[spec] * (count + len(aft...  4.56 us
    ppermute x6, waiting for transfers between devices, swapped(): return lax.ppermute(value, 'pair', [(0, 1), (1, 0)])  1.71 us
  transfers between devices with their start and end apart: 21, of which 11 were waited for; matrix products, arithmetic and copies ran while one was open for 1% of the time, Pallas kernels for 24%

profile of v5, /device:TPU:0, one launch (start us, length us, event | category | flops | bytes accessed | tf_op | source)
XLA Modules:
  0.0 63.5 jit_solution(17584623900094286904)
XLA Ops:
  0.6 1.1 %first_parts.4 = (bf16[2,2,128,256]{3,2,1,0:T(8,128)(2,1)S(1)}, bf16[2,2,128,256]{3,2,1,0:T(8,128)(2,1)S(1)}) custom-call(bf16[128,2048]{1,0:T(8,128)(2,1)} %refs_0_.6, bf16[128,2048]{1,0:T(8,128)(2,1)} %refs_1_.6), custom_call_target="tpu_custom_call" | custom-call | tf_op jit(solution)/shard_map/first_parts/pallas_call | solution.py:88
  1.8 0.5 collective-permute-start
  2.3 1.1 %first_parts.5 = (bf16[2,2,128,256]{3,2,1,0:T(8,128)(2,1)S(1)}, bf16[2,2,128,256]{3,2,1,0:T(8,128)(2,1)S(1)}) custom-call(bf16[128,2048]{1,0:T(8,128)(2,1)} %refs_0_.7, bf16[128,2048]{1,0:T(8,128)(2,1)} %refs_1_.7, bf16[2,2,128,256]{3,2,1,0:T(8,128)(2,1)S(1)} %get-tuple-element.26.own_ref.refs_2_), custom_call_target="tpu_custom_call" | custom-call | tf_op jit(solution)/shard_map/first_parts/pallas_call | solution.py:88
  3.5 0.1 collective-permute-start.4
  3.7 0.2 head_parts.9
  3.9 3.0 %collective-permute-start.1 = (bf16[2,2,128,256]{3,2,1,0:T(8,128)(2,1)S(1)}, bf16[2,2,128,256]{3,2,1,0:T(8,128)(2,1)S(1)}, u32[]{:S(2)}, u32[]{:S(2)}) collective-permute-start(bf16[2,2,128,256]{3,2,1,0:T(8,128)(2,1)S(1)} %head_parts.9), channel_id=1, source_target_pairs={{0,2},{2,0},{1,3},{3,1},{4,6},{6,4},{5,7},{7,5},{8,10},{10,8},{9,1... | collective-permute-start | bytes 786440 | tf_op jit(solution)/shard_map/ppermute | solution.py:32
  6.9 0.2 head_parts.11.refs_2_
  7.1 1.1 %first_parts.6 = (bf16[2,2,128,256]{3,2,1,0:T(8,128)(2,1)S(1)}, bf16[2,2,128,256]{3,2,1,0:T(8,128)(2,1)S(1)}) custom-call(bf16[128,2048]{1,0:T(8,128)(2,1)} %refs_0_.6, bf16[128,2048]{1,0:T(8,128)(2,1)} %refs_1_.6, bf16[2,2,128,256]{3,2,1,0:T(8,128)(2,1)S(1)} %head_parts.11.refs_2_), custom_call_target="tpu_custom_call" | custom-call | tf_op jit(solution)/shard_map/first_parts/pallas_call | solution.py:88
  8.3 1.1 %collective-permute-start.5 = (bf16[2,2,128,256]{3,2,1,0:T(8,128)(2,1)S(1)}, bf16[2,2,128,256]{3,2,1,0:T(8,128)(2,1)S(1)}, u32[]{:S(2)}, u32[]{:S(2)}) collective-permute-start(bf16[2,2,128,256]{3,2,1,0:T(8,128)(2,1)S(1)} %head_parts.11.refs_2_), channel_id=1, source_target_pairs={{0,2},{2,0},{1,3},{3,1},{4,6},{6,4},{5,7},{7,5},{8,10},{10,8},{9,1... | collective-permute-start | bytes 786440 | tf_op jit(solution)/shard_map/ppermute | solution.py:32
  9.5 0.2 head_parts.8.refs_1_
  9.6 1.6 %collective-permute-start.2 = (bf16[2,2,128,256]{3,2,1,0:T(8,128)(2,1)S(1)}, bf16[2,2,128,256]{3,2,1,0:T(8,128)(2,1)S(1)}, u32[]{:S(2)}, u32[]{:S(2)}) collective-permute-start(bf16[2,2,128,256]{3,2,1,0:T(8,128)(2,1)S(1)} %head_parts.8.refs_1_), channel_id=1, source_target_pairs={{0,4},{4,8},{8,12},{12,0},{1,5},{5,9},{9,13},{13,1},{2,6},{6,10},{... | collective-permute-start | bytes 786440 | tf_op jit(solution)/shard_map/ppermute | solution.py:27
  11.3 1.1 %first_parts.7 = (bf16[2,2,128,256]{3,2,1,0:T(8,128)(2,1)S(1)}, bf16[2,2,128,256]{3,2,1,0:T(8,128)(2,1)S(1)}) custom-call(bf16[128,2048]{1,0:T(8,128)(2,1)} %refs_0_.7, bf16[128,2048]{1,0:T(8,128)(2,1)} %refs_1_.7, bf16[2,2,128,256]{3,2,1,0:T(8,128)(2,1)S(1)} %get-tuple-element.37.own_ref.refs_2_), custom_call_target="tpu_custom_call" | custom-call | tf_op jit(solution)/shard_map/first_parts/pallas_call | solution.py:88
  12.5 1.5 %collective-permute-done.1.refs_2_.refs_0_ = bf16[2,2,128,256]{3,2,1,0:T(8,128)(2,1)S(1)} collective-permute-done((bf16[2,2,128,256]{3,2,1,0:T(8,128)(2,1)S(1)}, bf16[2,2,128,256]{3,2,1,0:T(8,128)(2,1)S(1)}, u32[]{:S(2)}, u32[]{:S(2)}) %collective-permute-start.1) | collective-permute-done | bytes 262176 | tf_op jit(solution)/shard_map/ppermute | solution.py:32
  14.0 0.2 head_parts.13
  14.2 2.1 %collective-permute-start.10 = (bf16[2,2,128,256]{3,2,1,0:T(8,128)(2,1)S(1)}, bf16[2,2,128,256]{3,2,1,0:T(8,128)(2,1)S(1)}, u32[]{:S(2)}, u32[]{:S(2)}) collective-permute-start(bf16[2,2,128,256]{3,2,1,0:T(8,128)(2,1)S(1)} %head_parts.13), channel_id=1, source_target_pairs={{0,2},{2,0},{1,3},{3,1},{4,6},{6,4},{5,7},{7,5},{8,10},{10,8},{9,1... | collective-permute-start | bytes 786440 | tf_op jit(solution)/shard_map/ppermute | solution.py:32
  16.3 1.6 %collective-permute-start.3 = (bf16[2,2,128,256]{3,2,1,0:T(8,128)(2,1)S(1)}, bf16[2,2,128,256]{3,2,1,0:T(8,128)(2,1)S(1)}, u32[]{:S(2)}, u32[]{:S(2)}) collective-permute-start(bf16[2,2,128,256]{3,2,1,0:T(8,128)(2,1)S(1)} %collective-permute-done.1.refs_2_.refs_0_), channel_id=1, source_target_pairs={{0,4},{4,8},{8,12},{12,0},{1,5},{5,9},{9,13},{13,1},{2,6},{6,10},{... | collective-permute-start | bytes 786440 | tf_op jit(solution)/shard_map/ppermute | solution.py:27
  17.9 0.7 %and_select_fusion = (f32[1,768,256]{2,1,0:T(8,128)S(1)}, f32[1,768,256]{2,1,0:T(8,128)S(1)}) fusion(s32[256]{0:T(256)S(1)} %get-tuple-element.58, s32[256]{0:T(256)S(1)} %get-tuple-element.56, s32[768]{0:T(1024)S(1)} %get-tuple-element.54, s32[768]{0:T(1024)S(1)} %get-tuple-element.52, pred[768]{0:T(1024)(128)(4,1)S(1)} %get-tuple-element.50, ...), kind=kLoop, calls=%fused_computation.1 | loop fusion | flops 1966080 | bytes 1590784 | tf_op jit(solution)/shard_map/jit(_where)/select_n | solution.py:279
  18.6 0.1 pad_maximum_fusion.refs_0_
  18.7 0.2 head_parts.10.refs_5_
  18.9 1.6 %collective-permute-done.2.refs_3_.refs_0_ = bf16[2,2,128,256]{3,2,1,0:T(8,128)(2,1)S(1)} collective-permute-done((bf16[2,2,128,256]{3,2,1,0:T(8,128)(2,1)S(1)}, bf16[2,2,128,256]{3,2,1,0:T(8,128)(2,1)S(1)}, u32[]{:S(2)}, u32[]{:S(2)}) %collective-permute-start.2) | collective-permute-done | bytes 262176 | tf_op jit(solution)/shard_map/ppermute | solution.py:27
  20.5 0.2 head_parts.12.refs_1_
  20.6 0.1 collective-permute-start.11
  20.8 0.2 head_parts.15
  21.0 1.2 %collective-permute-start.14 = (bf16[2,2,128,256]{3,2,1,0:T(8,128)(2,1)S(1)}, bf16[2,2,128,256]{3,2,1,0:T(8,128)(2,1)S(1)}, u32[]{:S(2)}, u32[]{:S(2)}) collective-permute-start(bf16[2,2,128,256]{3,2,1,0:T(8,128)(2,1)S(1)} %head_parts.15), channel_id=1, source_target_pairs={{0,2},{2,0},{1,3},{3,1},{4,6},{6,4},{5,7},{7,5},{8,10},{10,8},{9,1... | collective-permute-start | bytes 786440 | tf_op jit(solution)/shard_map/ppermute | solution.py:32
  22.1 5.0 %collective-permute-done.3.refs_4_ = bf16[2,2,128,256]{3,2,1,0:T(8,128)(2,1)S(1)} collective-permute-done((bf16[2,2,128,256]{3,2,1,0:T(8,128)(2,1)S(1)}, bf16[2,2,128,256]{3,2,1,0:T(8,128)(2,1)S(1)}, u32[]{:S(2)}, u32[]{:S(2)}) %collective-permute-start.3) | collective-permute-done | bytes 262176 | tf_op jit(solution)/shard_map/ppermute | solution.py:27
  27.1 4.2 %attention_grads.2 = (f32[2,2,2,128,256]{4,3,2,1,0:T(8,128)S(1)}, bf16[2,128,256]{2,1,0:T(8,128)(2,1)S(1)}, bf16[2,128,256]{2,1,0:T(8,128)(2,1)S(1)}, bf16[2,2,2,128,256]{4,3,2,1,0:T(8,128)(2,1)S(1)}) custom-call(f32[2,768,256]{2,1,0:T(8,128)S(1)} %pad_maximum_fusion.refs_0_, bf16[2,2,128,256]{3,2,1,0:T(8,128)(2,1)S(1)} %head_parts.8.refs_1_, ...), custom_call_target="tpu_custom_call" | custom-call | flops 1006632960 | bytes 4980736 | tf_op jit(solution)/shard_map/attention_grads/pallas_call | solution.py:51
  31.4 2.0 %collective-permute-start.12 = (bf16[2,2,128,256]{3,2,1,0:T(8,128)(2,1)S(1)}, bf16[2,2,128,256]{3,2,1,0:T(8,128)(2,1)S(1)}, u32[]{:S(2)}, u32[]{:S(2)}) collective-permute-start(bf16[2,2,128,256]{3,2,1,0:T(8,128)(2,1)S(1)} %relayed.1), channel_id=1, source_target_pairs={{0,4},{4,8},{8,12},{1,5},{5,9},{9,13},{2,6},{6,10},{10,14},{3,7},{... | collective-permute-start | bytes 786440 | tf_op jit(solution)/shard_map/ppermute | solution.py:27
  33.4 1.3 %collective-permute-start.7 = (bf16[2,2,2,128,256]{4,3,2,1,0:T(8,128)(2,1)S(1)}, bf16[2,2,2,128,256]{4,3,2,1,0:T(8,128)(2,1)S(1)}, u32[]{:S(2)}, u32[]{:S(2)}) collective-permute-start(bf16[2,2,2,128,256]{4,3,2,1,0:T(8,128)(2,1)S(1)} %get-tuple-element.33), channel_id=1, source_target_pairs={{4,0},{8,4},{12,8},{5,1},{9,5},{13,9},{6,2},{10,6},{14,10},{7,3},{... | collective-permute-start | bytes 1572872 | tf_op jit(solution)/shard_map/ppermute | solution.py:27
  34.7 0.2 head_parts.14.refs_5_
  34.9 2.3 %collective-permute-done.12.refs_4_ = bf16[2,2,128,256]{3,2,1,0:T(8,128)(2,1)S(1)} collective-permute-done((bf16[2,2,128,256]{3,2,1,0:T(8,128)(2,1)S(1)}, bf16[2,2,128,256]{3,2,1,0:T(8,128)(2,1)S(1)}, u32[]{:S(2)}, u32[]{:S(2)}) %collective-permute-start.12) | collective-permute-done | bytes 262176 | tf_op jit(solution)/shard_map/ppermute | solution.py:27
  37.2 4.2 %attention_grads.3 = (f32[2,2,2,128,256]{4,3,2,1,0:T(8,128)S(1)}, bf16[2,128,256]{2,1,0:T(8,128)(2,1)S(1)}, bf16[2,128,256]{2,1,0:T(8,128)(2,1)S(1)}, bf16[2,2,1...) custom-call(f32[2,768,256]{2,1,0:T(8,128)S(1)} %pad_maximum_fusion.refs_0_, ...), custom_call_target="tpu_custom_call" | custom-call | flops 1006632960 | bytes 4980736 | tf_op jit(solution)/shard_map/attention_grads/pallas_call | solution.py:51
  41.4 1.3 %collective-permute-start.17 = (bf16[2,2,128,256]{3,2,1,0:T(8,128)(2,1)S(1)}, bf16[2,2,128,256]{3,2,1,0:T(8,128)(2,1)S(1)}, u32[]{:S(2)}, u32[]{:S(2)}) collective-permute-start(bf16[2,2,128,256]{3,2,1,0:T(8,128)(2,1)S(1)} %get-tuple-element.45), channel_id=1, source_target_pairs={{4,0},{8,4},{12,8},{5,1},{9,5},{13,9},{6,2},{10,6},{14,10},{7,3},{... | collective-permute-start | bytes 786440 | tf_op jit(solution)/shard_map/ppermute | solution.py:27
  42.7 0.6 collective-permute-start.6
  43.3 1.5 %collective-permute-start.15 = (bf16[2,128,256]{2,1,0:T(8,128)(2,1)S(1)}, bf16[2,128,256]{2,1,0:T(8,128)(2,1)S(1)}, u32[]{:S(2)}, u32[]{:S(2)}) collective-permute-start(bf16[2,128,256]{2,1,0:T(8,128)(2,1)S(1)} %get-tuple-element.42), channel_id=1, source_target_pairs={{0,2},{2,0},{1,3},{3,1},{4,6},{6,4},{5,7},{7,5},{8,10},{10,8},{9,1... | collective-permute-start | bytes 393224 | tf_op jit(solution)/shard_map/ppermute | solution.py:32
  44.8 1.3 %collective-permute-start.16 = (bf16[2,2,128,256]{3,2,1,0:T(8,128)(2,1)S(1)}, bf16[2,2,128,256]{3,2,1,0:T(8,128)(2,1)S(1)}, u32[]{:S(2)}, u32[]{:S(2)}) collective-permute-start(bf16[2,2,128,256]{3,2,1,0:T(8,128)(2,1)S(1)} %get-tuple-element.44), channel_id=1, source_target_pairs={{4,0},{8,4},{12,8},{5,1},{9,5},{13,9},{6,2},{10,6},{14,10},{7,3},{... | collective-permute-start | bytes 786440 | tf_op jit(solution)/shard_map/ppermute | solution.py:27
  46.1 3.1 %collective-permute-done.6.refs_1_ = bf16[2,128,256]{2,1,0:T(8,128)(2,1)S(1)} collective-permute-done((bf16[2,128,256]{2,1,0:T(8,128)(2,1)S(1)}, bf16[2,128,256]{2,1,0:T(8,128)(2,1)S(1)}, u32[]{:S(2)}, u32[]{:S(2)}) %collective-permute-start.6) | collective-permute-done | bytes 131104 | tf_op jit(solution)/shard_map/ppermute | solution.py:32
  49.2 0.1 summed.3
  49.3 0.8 %collective-permute-start.8 = (bf16[2,2,128,256]{3,2,1,0:T(8,128)(2,1)S(1)}, bf16[2,2,128,256]{3,2,1,0:T(8,128)(2,1)S(1)}, u32[]{:S(2)}, u32[]{:S(2)}) collective-permute-start(bf16[2,2,128,256]{3,2,1,0:T(8,128)(2,1)S(1)} %get-tuple-element.35), channel_id=1, source_target_pairs={{0,2},{2,0},{1,3},{3,1},{4,6},{6,4},{5,7},{7,5},{8,10},{10,8},{9,1... | collective-permute-start | bytes 786440 | tf_op jit(solution)/shard_map/ppermute | solution.py:32
  50.1 0.9 %collective-permute-done.15.refs_1_ = bf16[2,128,256]{2,1,0:T(8,128)(2,1)S(1)} collective-permute-done((bf16[2,128,256]{2,1,0:T(8,128)(2,1)S(1)}, bf16[2,128,256]{2,1,0:T(8,128)(2,1)S(1)}, u32[]{:S(2)}, u32[]{:S(2)}) %collective-permute-start.15) | collective-permute-done | bytes 131104 | tf_op jit(solution)/shard_map/ppermute | solution.py:32
  51.0 2.0 %collective-permute-done.17.refs_0_ = bf16[2,2,128,256]{3,2,1,0:T(8,128)(2,1)S(1)} collective-permute-done((bf16[2,2,128,256]{3,2,1,0:T(8,128)(2,1)S(1)}, bf16[2,2,128,256]{3,2,1,0:T(8,128)(2,1)S(1)}, u32[]{:S(2)}, u32[]{:S(2)}) %collective-permute-start.17) | collective-permute-done | bytes 262176 | tf_op jit(solution)/shard_map/ppermute | solution.py:27
  53.1 2.2 %collective-permute-start.18 = (bf16[2,2,128,256]{3,2,1,0:T(8,128)(2,1)S(1)}, bf16[2,2,128,256]{3,2,1,0:T(8,128)(2,1)S(1)}, u32[]{:S(2)}, u32[]{:S(2)}) collective-permute-start(bf16[2,2,128,256]{3,2,1,0:T(8,128)(2,1)S(1)} %summed.5), channel_id=1, source_target_pairs={{0,2},{2,0},{1,3},{3,1},{4,6},{6,4},{5,7},{7,5},{8,10},{10,8},{9,1... | collective-permute-start | bytes 786440 | tf_op jit(solution)/shard_map/ppermute | solution.py:32
  55.3 0.5 collective-permute-done.16.refs_0_
  55.9 0.4 collective-permute-done.8.refs_3_
  56.3 0.7 %rows_for_pair.2 = (bf16[3,2,128,256]{3,2,1,0:T(8,128)(2,1)S(1)}, bf16[3,2,128,256]{3,2,1,0:T(8,128)(2,1)S(1)}) custom-call(bf16[2,128,256]{2,1,0:T(8,128)(2,1)S(1)} %get-tuple-element.30.refs_0_, bf16[2,128,256]{2,1,0:T(8,128)(2,1)S(1)} %collective-permute-done.6.refs_1_, bf16[2,2,128,256]{3,2,1,0:T(8,128)(2,1)S(1)} %get-tuple-element.34.refs_2_, ...), custom_call_target="tpu_custom_call" | custom-call | bytes 1572864 | tf_op jit(solution)/shard_map/rows_for_pair/pallas_call | solution.py:51
  57.1 2.6 %collective-permute-done.18.refs_3_ = bf16[2,2,128,256]{3,2,1,0:T(8,128)(2,1)S(1)} collective-permute-done((bf16[2,2,128,256]{3,2,1,0:T(8,128)(2,1)S(1)}, bf16[2,2,128,256]{3,2,1,0:T(8,128)(2,1)S(1)}, u32[]{:S(2)}, u32[]{:S(2)}) %collective-permute-start.18) | collective-permute-done | bytes 262176 | tf_op jit(solution)/shard_map/ppermute | solution.py:32
  59.7 0.7 %rows_for_pair.3 = (bf16[3,2,128,256]{3,2,1,0:T(8,128)(2,1)S(1)}, bf16[3,2,128,256]{3,2,1,0:T(8,128)(2,1)S(1)}) custom-call(bf16[2,128,256]{2,1,0:T(8,128)(2,1)S(1)} %get-tuple-element.41.refs_0_, bf16[2,128,256]{2,1,0:T(8,128)(2,1)S(1)} %collective-permute-done.15.refs_1_, bf16[2,2,128,256]{3,2,1,0:T(8,128)(2,1)S(1)} %summed.4.refs_2_, ...), custom_call_target="tpu_custom_call" | custom-call | bytes 1572864 | tf_op jit(solution)/shard_map/rows_for_pair/pallas_call | solution.py:51
  60.5 1.7 %collective-permute-done.20.refs_3_ = bf16[3,2,128,256]{3,2,1,0:T(8,128)(2,1)S(1)} collective-permute-done((bf16[3,2,128,256]{3,2,1,0:T(8,128)(2,1)S(1)}, bf16[3,2,128,256]{3,2,1,0:T(8,128)(2,1)S(1)}, u32[]{:S(2)}, u32[]{:S(2)}) %collective-permute-start.20) | collective-permute-done | bytes 393248 | tf_op jit(solution)/shard_map/ppermute | solution.py:36
  62.2 1.3 %laid_out.1 = (bf16[128,2048]{1,0:T(8,128)(2,1)}, bf16[128,2048]{1,0:T(8,128)(2,1)}, bf16[128,2048]{1,0:T(8,128)(2,1)}) custom-call(bf16[3,2,128,256]{3,2,1,0:T(8,128)(2,1)S(1)} %get-tuple-element.36.refs_0_, bf16[3,2,128,256]{3,2,1,0:T(8,128)(2,1)S(1)} %get-tuple-element.46.refs_1_, bf16[3,2,128,256]{3,2,1,0:T(8,128)(2,1)S(1)} %collective-permute-done.19.refs_2_, ...), custom_call_target="tpu_custom_call" | custom-call | bytes 3145728 | tf_op jit(solution)/shard_map/laid_out/pallas_call | solution.py:51
  (26 shorter events, 0.6 us)
Async XLA Ops:
  0.6 3.0 %copy-start = (s32[2048]{0:T(1024)S(1)}, s32[2048]{0:T(1024)}, u32[]{:S(2)}) copy-start(s32[2048]{0:T(1024)} %param.9) | copy-start | bytes 24580
  1.8 1.9 %collective-permute-start = (bf16[2,2,128,256]{3,2,1,0:T(8,128)(2,1)S(1)}, bf16[2,2,128,256]{3,2,1,0:T(8,128)(2,1)S(1)}, u32[]{:S(2)}, u32[]{:S(2)}) collective-permute-start(bf16[2,2,128,256]{3,2,1,0:T(8,128)(2,1)S(1)} %get-tuple-element.27), channel_id=1, source_target_pairs={{0,1},{1,0},{2,3},{3,2},{4,5},{5,4},{6,7},{7,6},{8,9},{9,8},{10,11... | collective-permute-start | bytes 786440 | tf_op jit(solution)/shard_map/ppermute | solution.py:36
  3.5 3.4 %collective-permute-start.4 = (bf16[2,2,128,256]{3,2,1,0:T(8,128)(2,1)S(1)}, bf16[2,2,128,256]{3,2,1,0:T(8,128)(2,1)S(1)}, u32[]{:S(2)}, u32[]{:S(2)}) collective-permute-start(bf16[2,2,128,256]{3,2,1,0:T(8,128)(2,1)S(1)} %get-tuple-element.29), channel_id=1, source_target_pairs={{0,1},{1,0},{2,3},{3,2},{4,5},{5,4},{6,7},{7,6},{8,9},{9,8},{10,11... | collective-permute-start | bytes 786440 | tf_op jit(solution)/shard_map/ppermute | solution.py:36
  3.9 10.1 %collective-permute-start.1 = (bf16[2,2,128,256]{3,2,1,0:T(8,128)(2,1)S(1)}, bf16[2,2,128,256]{3,2,1,0:T(8,128)(2,1)S(1)}, u32[]{:S(2)}, u32[]{:S(2)}) collective-permute-start(bf16[2,2,128,256]{3,2,1,0:T(8,128)(2,1)S(1)} %head_parts.9), channel_id=1, source_target_pairs={{0,2},{2,0},{1,3},{3,1},{4,6},{6,4},{5,7},{7,5},{8,10},{10,8},{9,1... | collective-permute-start | bytes 786440 | tf_op jit(solution)/shard_map/ppermute | solution.py:32
  8.2 5.8 %collective-permute-start.9 = (bf16[2,2,128,256]{3,2,1,0:T(8,128)(2,1)S(1)}, bf16[2,2,128,256]{3,2,1,0:T(8,128)(2,1)S(1)}, u32[]{:S(2)}, u32[]{:S(2)}) collective-permute-start(bf16[2,2,128,256]{3,2,1,0:T(8,128)(2,1)S(1)} %get-tuple-element.38), channel_id=1, source_target_pairs={{0,1},{1,0},{2,3},{3,2},{4,5},{5,4},{6,7},{7,6},{8,9},{9,8},{10,11... | collective-permute-start | bytes 786440 | tf_op jit(solution)/shard_map/ppermute | solution.py:36
  8.3 12.4 %collective-permute-start.5 = (bf16[2,2,128,256]{3,2,1,0:T(8,128)(2,1)S(1)}, bf16[2,2,128,256]{3,2,1,0:T(8,128)(2,1)S(1)}, u32[]{:S(2)}, u32[]{:S(2)}) collective-permute-start(bf16[2,2,128,256]{3,2,1,0:T(8,128)(2,1)S(1)} %head_parts.11.refs_2_), channel_id=1, source_target_pairs={{0,2},{2,0},{1,3},{3,1},{4,6},{6,4},{5,7},{7,5},{8,10},{10,8},{9,1... | collective-permute-start | bytes 786440 | tf_op jit(solution)/shard_map/ppermute | solution.py:32
  9.6 10.8 %collective-permute-start.2 = (bf16[2,2,128,256]{3,2,1,0:T(8,128)(2,1)S(1)}, bf16[2,2,128,256]{3,2,1,0:T(8,128)(2,1)S(1)}, u32[]{:S(2)}, u32[]{:S(2)}) collective-permute-start(bf16[2,2,128,256]{3,2,1,0:T(8,128)(2,1)S(1)} %head_parts.8.refs_1_), channel_id=1, source_target_pairs={{0,4},{4,8},{8,12},{12,0},{1,5},{5,9},{9,13},{13,1},{2,6},{6,10},{... | collective-permute-start | bytes 786440 | tf_op jit(solution)/shard_map/ppermute | solution.py:27
  12.4 8.3 %collective-permute-start.13 = (bf16[2,2,128,256]{3,2,1,0:T(8,128)(2,1)S(1)}, bf16[2,2,128,256]{3,2,1,0:T(8,128)(2,1)S(1)}, u32[]{:S(2)}, u32[]{:S(2)}) collective-permute-start(bf16[2,2,128,256]{3,2,1,0:T(8,128)(2,1)S(1)} %get-tuple-element.40), channel_id=1, source_target_pairs={{0,1},{1,0},{2,3},{3,2},{4,5},{5,4},{6,7},{7,6},{8,9},{9,8},{10,11... | collective-permute-start | bytes 786440 | tf_op jit(solution)/shard_map/ppermute | solution.py:36
  14.2 17.1 %collective-permute-start.10 = (bf16[2,2,128,256]{3,2,1,0:T(8,128)(2,1)S(1)}, bf16[2,2,128,256]{3,2,1,0:T(8,128)(2,1)S(1)}, u32[]{:S(2)}, u32[]{:S(2)}) collective-permute-start(bf16[2,2,128,256]{3,2,1,0:T(8,128)(2,1)S(1)} %head_parts.13), channel_id=1, source_target_pairs={{0,2},{2,0},{1,3},{3,1},{4,6},{6,4},{5,7},{7,5},{8,10},{10,8},{9,1... | collective-permute-start | bytes 786440 | tf_op jit(solution)/shard_map/ppermute | solution.py:32
  16.3 10.8 %collective-permute-start.3 = (bf16[2,2,128,256]{3,2,1,0:T(8,128)(2,1)S(1)}, bf16[2,2,128,256]{3,2,1,0:T(8,128)(2,1)S(1)}, u32[]{:S(2)}, u32[]{:S(2)}) collective-permute-start(bf16[2,2,128,256]{3,2,1,0:T(8,128)(2,1)S(1)} %collective-permute-done.1.refs_2_.refs_0_), channel_id=1, source_target_pairs={{0,4},{4,8},{8,12},{12,0},{1,5},{5,9},{9,13},{13,1},{2,6},{6,10},{... | collective-permute-start | bytes 786440 | tf_op jit(solution)/shard_map/ppermute | solution.py:27
  20.6 14.2 %collective-permute-start.11 = (bf16[2,2,128,256]{3,2,1,0:T(8,128)(2,1)S(1)}, bf16[2,2,128,256]{3,2,1,0:T(8,128)(2,1)S(1)}, u32[]{:S(2)}, u32[]{:S(2)}) collective-permute-start(bf16[2,2,128,256]{3,2,1,0:T(8,128)(2,1)S(1)} %head_parts.12.refs_1_), channel_id=1, source_target_pairs={{0,4},{4,8},{8,12},{12,0},{1,5},{5,9},{9,13},{13,1},{2,6},{6,10},{... | collective-permute-start | bytes 786440 | tf_op jit(solution)/shard_map/ppermute | solution.py:27
  21.0 13.9 %collective-permute-start.14 = (bf16[2,2,128,256]{3,2,1,0:T(8,128)(2,1)S(1)}, bf16[2,2,128,256]{3,2,1,0:T(8,128)(2,1)S(1)}, u32[]{:S(2)}, u32[]{:S(2)}) collective-permute-start(bf16[2,2,128,256]{3,2,1,0:T(8,128)(2,1)S(1)} %head_parts.15), channel_id=1, source_target_pairs={{0,2},{2,0},{1,3},{3,1},{4,6},{6,4},{5,7},{7,5},{8,10},{10,8},{9,1... | collective-permute-start | bytes 786440 | tf_op jit(solution)/shard_map/ppermute | solution.py:32
  31.4 5.8 %collective-permute-start.12 = (bf16[2,2,128,256]{3,2,1,0:T(8,128)(2,1)S(1)}, bf16[2,2,128,256]{3,2,1,0:T(8,128)(2,1)S(1)}, u32[]{:S(2)}, u32[]{:S(2)}) collective-permute-start(bf16[2,2,128,256]{3,2,1,0:T(8,128)(2,1)S(1)} %relayed.1), channel_id=1, source_target_pairs={{0,4},{4,8},{8,12},{1,5},{5,9},{9,13},{2,6},{6,10},{10,14},{3,7},{... | collective-permute-start | bytes 786440 | tf_op jit(solution)/shard_map/ppermute | solution.py:27
  33.4 15.9 %collective-permute-start.7 = (bf16[2,2,2,128,256]{4,3,2,1,0:T(8,128)(2,1)S(1)}, bf16[2,2,2,128,256]{4,3,2,1,0:T(8,128)(2,1)S(1)}, u32[]{:S(2)}, u32[]{:S(2)}) collective-permute-start(bf16[2,2,2,128,256]{4,3,2,1,0:T(8,128)(2,1)S(1)} %get-tuple-element.33), channel_id=1, source_target_pairs={{4,0},{8,4},{12,8},{5,1},{9,5},{13,9},{6,2},{10,6},{14,10},{7,3},{... | collective-permute-start | bytes 1572872 | tf_op jit(solution)/shard_map/ppermute | solution.py:27
  41.4 11.6 %collective-permute-start.17 = (bf16[2,2,128,256]{3,2,1,0:T(8,128)(2,1)S(1)}, bf16[2,2,128,256]{3,2,1,0:T(8,128)(2,1)S(1)}, u32[]{:S(2)}, u32[]{:S(2)}) collective-permute-start(bf16[2,2,128,256]{3,2,1,0:T(8,128)(2,1)S(1)} %get-tuple-element.45), channel_id=1, source_target_pairs={{4,0},{8,4},{12,8},{5,1},{9,5},{13,9},{6,2},{10,6},{14,10},{7,3},{... | collective-permute-start | bytes 786440 | tf_op jit(solution)/shard_map/ppermute | solution.py:27
  42.7 6.5 %collective-permute-start.6 = (bf16[2,128,256]{2,1,0:T(8,128)(2,1)S(1)}, bf16[2,128,256]{2,1,0:T(8,128)(2,1)S(1)}, u32[]{:S(2)}, u32[]{:S(2)}) collective-permute-start(bf16[2,128,256]{2,1,0:T(8,128)(2,1)S(1)} %get-tuple-element.31), channel_id=1, source_target_pairs={{0,2},{2,0},{1,3},{3,1},{4,6},{6,4},{5,7},{7,5},{8,10},{10,8},{9,1... | collective-permute-start | bytes 393224 | tf_op jit(solution)/shard_map/ppermute | solution.py:32
  43.3 7.7 %collective-permute-start.15 = (bf16[2,128,256]{2,1,0:T(8,128)(2,1)S(1)}, bf16[2,128,256]{2,1,0:T(8,128)(2,1)S(1)}, u32[]{:S(2)}, u32[]{:S(2)}) collective-permute-start(bf16[2,128,256]{2,1,0:T(8,128)(2,1)S(1)} %get-tuple-element.42), channel_id=1, source_target_pairs={{0,2},{2,0},{1,3},{3,1},{4,6},{6,4},{5,7},{7,5},{8,10},{10,8},{9,1... | collective-permute-start | bytes 393224 | tf_op jit(solution)/shard_map/ppermute | solution.py:32
  44.8 11.0 %collective-permute-start.16 = (bf16[2,2,128,256]{3,2,1,0:T(8,128)(2,1)S(1)}, bf16[2,2,128,256]{3,2,1,0:T(8,128)(2,1)S(1)}, u32[]{:S(2)}, u32[]{:S(2)}) collective-permute-start(bf16[2,2,128,256]{3,2,1,0:T(8,128)(2,1)S(1)} %get-tuple-element.44), channel_id=1, source_target_pairs={{4,0},{8,4},{12,8},{5,1},{9,5},{13,9},{6,2},{10,6},{14,10},{7,3},{... | collective-permute-start | bytes 786440 | tf_op jit(solution)/shard_map/ppermute | solution.py:27
  49.3 7.0 %collective-permute-start.8 = (bf16[2,2,128,256]{3,2,1,0:T(8,128)(2,1)S(1)}, bf16[2,2,128,256]{3,2,1,0:T(8,128)(2,1)S(1)}, u32[]{:S(2)}, u32[]{:S(2)}) collective-permute-start(bf16[2,2,128,256]{3,2,1,0:T(8,128)(2,1)S(1)} %get-tuple-element.35), channel_id=1, source_target_pairs={{0,2},{2,0},{1,3},{3,1},{4,6},{6,4},{5,7},{7,5},{8,10},{10,8},{9,1... | collective-permute-start | bytes 786440 | tf_op jit(solution)/shard_map/ppermute | solution.py:32
  53.1 6.6 %collective-permute-start.18 = (bf16[2,2,128,256]{3,2,1,0:T(8,128)(2,1)S(1)}, bf16[2,2,128,256]{3,2,1,0:T(8,128)(2,1)S(1)}, u32[]{:S(2)}, u32[]{:S(2)}) collective-permute-start(bf16[2,2,128,256]{3,2,1,0:T(8,128)(2,1)S(1)} %summed.5), channel_id=1, source_target_pairs={{0,2},{2,0},{1,3},{3,1},{4,6},{6,4},{5,7},{7,5},{8,10},{10,8},{9,1... | collective-permute-start | bytes 786440 | tf_op jit(solution)/shard_map/ppermute | solution.py:32
  57.0 3.5 %collective-permute-start.19 = (bf16[3,2,128,256]{3,2,1,0:T(8,128)(2,1)S(1)}, bf16[3,2,128,256]{3,2,1,0:T(8,128)(2,1)S(1)}, u32[]{:S(2)}, u32[]{:S(2)}) collective-permute-start(bf16[3,2,128,256]{3,2,1,0:T(8,128)(2,1)S(1)} %get-tuple-element.47), channel_id=1, source_target_pairs={{0,1},{1,0},{2,3},{3,2},{4,5},{5,4},{6,7},{7,6},{8,9},{9,8},{10,11... | collective-permute-start | bytes 1179656 | tf_op jit(solution)/shard_map/ppermute | solution.py:36
  60.4 1.8 %collective-permute-start.20 = (bf16[3,2,128,256]{3,2,1,0:T(8,128)(2,1)S(1)}, bf16[3,2,128,256]{3,2,1,0:T(8,128)(2,1)S(1)}, u32[]{:S(2)}, u32[]{:S(2)}) collective-permute-start(bf16[3,2,128,256]{3,2,1,0:T(8,128)(2,1)S(1)} %get-tuple-element.48), channel_id=1, source_target_pairs={{0,1},{1,0},{2,3},{3,2},{4,5},{5,4},{6,7},{7,6},{8,9},{9,8},{10,11... | collective-permute-start | bytes 1179656 | tf_op jit(solution)/shard_map/ppermute | solution.py:36

commit v6 on v4

--- a/solution.py
+++ b/solution.py
@@ -21,9 +21,10 @@
     return [heads // 2, heads - heads // 2]
 
 
-def along_blocks(value, by):
+def along_blocks(value, by, ring):
     peers = lax.axis_size("blk")
-    return lax.ppermute(value, "blk", [(i, (i + by) % peers) for i in range(peers)])
+    pairs = [(i, (i + by) % peers) for i in range(peers) if ring or 0 <= i + by < peers]
+    return lax.ppermute(value, "blk", pairs)
 
 
 def round_sub(value, by):
@@ -64,39 +65,45 @@
     return jax.ShapeDtypeStruct(dims, dtype)
 
 
-def first_parts(arrays, low, high, after):
-    count = len(arrays)
-    rows, width = arrays[0].shape
-    half = width // 2
-    peers = lax.axis_size("sub")
-    part = half // peers
+def first_parts(groups, after):
+    held, wanted, outs = [], [], []
+    for arrays, low, high in groups:
+        rows, width = arrays[0].shape
+        peers = lax.axis_size("sub")
+        half = width // 2
+        part = half // peers
+        wanted.append((len(held), len(arrays), low, high))
+        held += [pltpu.with_memory_space_constraint(array, pltpu.HBM) for array in arrays]
+        outs += [pltpu.VMEM((len(arrays), peers, rows, high - low), LOW)] * 2
 
     def kernel(*refs):
-        ins, outs, sems = refs[:count], refs[-3:-1], refs[-1]
+        out_refs, sems = refs[-1 - len(outs):-1], refs[-1]
         p = lax.axis_index("pair")
         moves = []
-        for side, out in zip((1 - p, p), outs):
-            for at in range(peers):
-                start = pl.multiple_of(side * half + at * part + low, HD)
-                moves += [(ref.at[:, pl.ds(start, high - low)], out.at[i, at]) for i, ref in enumerate(ins)]
-        run_moves(moves, sems)
-
-    outs = [pltpu.VMEM((count, peers, rows, high - low), LOW)] * 2
+        for group, (first, count, low, high) in enumerate(wanted):
+            for side, out in zip((1 - p, p), out_refs[2 * group:2 * group + 2]):
+                for at in range(peers):
+                    start = pl.multiple_of(side * half + at * part + low, HD)
+                    for i in range(count):
+                        moves.append((refs[first + i].at[:, pl.ds(start, high - low)], out.at[i, at]))
+        run_moves(moves, sems)
+
     spec = pl.BlockSpec(memory_space=pl.ANY)
-    held = [pltpu.with_memory_space_constraint(array, pltpu.HBM) for array in arrays]
-    return pl.pallas_call(
+    parts = pl.pallas_call(
         kernel,
         out_shape=outs,
-        in_specs=[spec] * (count + len(after)),
-        out_specs=[spec] * 2,
-        scratch_shapes=[pltpu.SemaphoreType.DMA((2 * peers * count,))],
+        in_specs=[spec] * (len(held) + len(after)),
+        out_specs=[spec] * len(outs),
+        scratch_shapes=[pltpu.SemaphoreType.DMA((2 * peers * len(held),))],
         name="first_parts",
         compiler_params=pltpu.CompilerParams(vmem_limit_bytes=8 * MIB),
     )(*held, *after)
-
-
-def head_parts(own, paired, turns, after):
-    count, peers, rows, cut = own.shape
+    return [(parts[2 * i], parts[2 * i + 1]) for i in range(len(groups))]
+
+
+def head_parts(own, paired, which, turns, after):
+    _, peers, rows, cut = own.shape
+    chosen = pl.ds(which, 2)
 
     def kernel(own_ref, pair_ref, *refs):
         outs, sems = refs[len(after):-1], refs[-1]
@@ -104,15 +111,15 @@
         moves = []
         for by, out in zip(turns, outs):
             at = lax.rem(s + by, peers)
-            moves += [(own_ref.at[:, at], out.at[:, p]), (pair_ref.at[:, at], out.at[:, 1 - p])]
-        run_moves(moves, sems)
-
-    outs = [shape(count, 2, rows, cut)] * len(turns)
+            moves += [(own_ref.at[chosen, at], out.at[:, p]), (pair_ref.at[chosen, at], out.at[:, 1 - p])]
+        run_moves(moves, sems)
+
+    outs = [shape(2, 2, rows, cut)] * len(turns)
     scratch = [pltpu.SemaphoreType.DMA((2 * len(turns),))]
     return call(kernel, [own, paired] + after, outs, scratch, "head_parts")
 
 
-def attention_grads(bias, kv, kv_earlier, qg, split):
+def attention_grads(bias, kv, kv_earlier, qg, split, after):
     peers = len(kv)
     _, _, rows, cut = kv[0].shape
     heads = cut // HD
@@ -122,7 +129,7 @@
     def kernel(*refs):
         bias_ref = refs[0]
         kv_in, early_in, qg_in = refs[1:1 + peers], refs[1 + peers:1 + 2 * peers], refs[1 + 2 * peers:1 + 3 * peers]
-        outs = refs[1 + 3 * peers:-5]
+        outs = refs[1 + 3 * peers + len(after):-5]
         own_out, dq_outs, early_outs = outs[0], outs[1:1 + peers], outs[1 + peers:]
         kv_all, qg_all, early, dq_all, sems = refs[-5:]
         s = lax.axis_index("sub")
@@ -135,33 +142,39 @@
                 (qg_in[by], qg_all.at[:, :, at]),
             ]
         run_moves(moves, sems)
-        for head in range(heads):
-            columns = pl.ds(head * HD, HD)
-
-            def flat(ref, which, tiles):
-                block = ref[which, tiles, :, :, columns]
-                return block.reshape(block.shape[0] * strip, HD)
-
-            terms = []
-            for tile in range(2):
-                at, span = pl.ds(tile, 1), pl.ds(tile, 3)
-                q, g = flat(qg_all, 0, at), flat(qg_all, 1, at)
-                k, v = flat(kv_all, 0, span), flat(kv_all, 1, span)
-                scores = lax.dot_general(k, q, ROWS_BY_ROWS, preferred_element_type=WIDE) * TO_BITS + bias_ref[tile]
-                peak = jnp.max(scores, axis=0, keepdims=True)
-                weight = jnp.exp2(scores - peak)
-                prob = weight * (1.0 / jnp.sum(weight, axis=0, keepdims=True))
-                prob_low = prob.astype(LOW)
-                grad_prob = lax.dot_general(v, g, ROWS_BY_ROWS, preferred_element_type=WIDE)
-                row_dot = jnp.sum(prob_low.astype(WIDE) * grad_prob, axis=0, keepdims=True)
-                score_low = (prob * (grad_prob - row_dot)).astype(LOW)
-                dq = jnp.dot(k.T, score_low, preferred_element_type=WIDE) * SCALE
-                dq_all[tile, :, :, columns] = dq.T.astype(LOW).reshape(peers, rows, HD)
-                dk = jnp.dot(score_low, q, preferred_element_type=WIDE) * SCALE
-                dv = jnp.dot(prob_low, g, preferred_element_type=WIDE)
-                terms.append((dk, dv))
+        strips = [(head, tile) for head in range(heads) for tile in range(2)]
+        products, terms = {}, {}
+
+        def flat(ref, which, tiles, head):
+            block = ref[which, tiles, :, :, pl.ds(head * HD, HD)]
+            return block.reshape(block.shape[0] * strip, HD)
+
+        def multiply(head, tile):
+            at, span = pl.ds(tile, 1), pl.ds(tile, 3)
+            q, g = flat(qg_all, 0, at, head), flat(qg_all, 1, at, head)
+            k, v = flat(kv_all, 0, span, head), flat(kv_all, 1, span, head)
+            scores = lax.dot_general(k, q, ROWS_BY_ROWS, preferred_element_type=WIDE)
+            grad_prob = lax.dot_general(v, g, ROWS_BY_ROWS, preferred_element_type=WIDE)
+            products[head, tile] = q, g, k, scores, grad_prob
+
+        def finish(head, tile):
+            q, g, k, scores, grad_prob = products.pop((head, tile))
+            scores = scores * TO_BITS + bias_ref[tile]
+            peak = jnp.max(scores, axis=0, keepdims=True)
+            weight = jnp.exp2(scores - peak)
+            prob = weight * (1.0 / jnp.sum(weight, axis=0, keepdims=True))
+            prob_low = prob.astype(LOW)
+            row_dot = jnp.sum(prob_low.astype(WIDE) * grad_prob, axis=0, keepdims=True)
+            score_low = (prob * (grad_prob - row_dot)).astype(LOW)
+            dq = jnp.dot(k.T, score_low, preferred_element_type=WIDE) * SCALE
+            dq_all[tile, :, :, pl.ds(head * HD, HD)] = dq.T.astype(LOW).reshape(peers, rows, HD)
+            dk = jnp.dot(score_low, q, preferred_element_type=WIDE) * SCALE
+            dv = jnp.dot(prob_low, g, preferred_element_type=WIDE)
+            terms[head, tile] = dk, dv
+
+        def gather(head):
             for which in range(2):
-                low, high = terms[0][which], terms[1][which]
+                low, high = terms[head, 0][which], terms[head, 1][which]
                 sums = (
                     low[:strip],
                     low[strip:2 * strip] + high[:strip],
@@ -171,9 +184,17 @@
                 for tile, total in enumerate(sums):
                     total = total.reshape(peers, rows, HD)
                     if tile < 2:
-                        early[which, tile, :, :, columns] = total.astype(LOW)
+                        early[which, tile, :, :, pl.ds(head * HD, HD)] = total.astype(LOW)
                     else:
-                        own_out[which, tile - 2, :, :, columns] = total
+                        own_out[which, tile - 2, :, :, pl.ds(head * HD, HD)] = total
+
+        multiply(*strips[0])
+        for at, (head, tile) in enumerate(strips):
+            if at + 1 < len(strips):
+                multiply(*strips[at + 1])
+            finish(head, tile)
+            if tile == 1:
+                gather(head)
         moves = [] if split else [(early, early_outs[0])]
         for by in range(peers):
             at = lax.rem(s + by, peers)
@@ -192,7 +213,7 @@
         pltpu.SemaphoreType.DMA((3 * peers,)),
     ]
     flops = heads * 2 * 5 * 2 * strip * 3 * strip * HD
-    ins = [bias] + kv + kv_earlier + qg
+    ins = [bias] + kv + kv_earlier + qg + after
     outs = call(kernel, ins, outs, scratch, "attention_grads", whole=True, flops=flops, room=40 * MIB)
     return outs[0], outs[1:1 + peers], outs[1 + peers:]
 
@@ -220,17 +241,17 @@
     _, rows, cut = dq[0].shape
 
     def kernel(*refs):
-        dq_refs, dkv_refs, (send, keep), sems = refs[:peers], refs[peers:2 * peers], refs[-3:-1], refs[-1]
+        dq_refs, dkv_refs, (send, keep) = refs[:peers], refs[peers:2 * peers], refs[-2:]
         p, s = lax.axis_index("pair"), lax.axis_index("sub")
-        moves = []
         for by in range(peers):
             at = lax.rem(s - by + peers, peers)
             for out, row in ((send, 1 - p), (keep, p)):
-                moves += [(dq_refs[by].at[row], out.at[0, at]), (dkv_refs[by].at[:, row], out.at[1:3, at])]
-        run_moves(moves, sems)
+                out[0, at] = dq_refs[by][row]
+                for which in range(2):
+                    out[1 + which, at] = dkv_refs[by][which, row]
 
     outs = [shape(3, peers, rows, cut)] * 2
-    return call(kernel, dq + dkv, outs, [pltpu.SemaphoreType.DMA((4 * peers,))], "rows_for_pair")
+    return call(kernel, dq + dkv, outs, [], "rows_for_pair", whole=True)
 
 
 def laid_out(kept, paired, spans):
@@ -281,32 +302,37 @@
         spans.append((at, at + heads * HD))
         at += heads * HD
     bias = allowed_bias(session, queries.shape[0])
+    (kv_send, kv_first), = first_parts([([keys, values], *spans[0])], [])
+    rest = [([queries, out_grad], *spans[0])] + [([keys, values, queries, out_grad], *span) for span in spans[1:]]
+    rest = first_parts(rest, [kv_first])
+    kv_parts = [(kv_first, swapped(kv_send), 0)]
+    qg_parts = [(rest[0][1], swapped(rest[0][0]), 0)]
+    for send, own in rest[1:]:
+        paired = swapped(send)
+        kv_parts.append((own, paired, 0))
+        qg_parts.append((own, paired, 2))
+    count = len(spans)
+    kv_sends, qg_sends, kv, qg, kv_own, own_earlier = [], [], [], [], [], []
+    for index in range(count):
+        kv_sends.append(head_parts(*kv_parts[index], others, kv[index - 1] if index else []))
+        kv.append([round_sub(value, by) for by, value in zip(others, kv_sends[index])])
+        kv_own.append(head_parts(*kv_parts[index], [0], own_earlier[index - 1:index]))
+        own_earlier.append(along_blocks(kv_own[index][0], 1, True))
+        qg_sends.append(head_parts(*qg_parts[index], others, qg[index - 1] if index else []))
+        qg.append([round_sub(value, by) for by, value in zip(others, qg_sends[index])])
     kept, paired = [], []
-    first_turn, kv_turn, own_turn, qg_turn = [], [], [], []
-    for index, (low, high) in enumerate(spans):
-        last = index == len(spans) - 1
-        send, own = first_parts([keys, values], low, high, first_turn)
-        rec = swapped(send)
-        sends = head_parts(own, rec, others, kv_turn)
-        kv = [round_sub(value, by) for by, value in zip(others, sends)]
-        kv_own = head_parts(own, rec, [0], own_turn)
-        earlier = [along_blocks(kv_own[0], 1)]
-        own_turn = earlier[:]
-        earlier += [along_blocks(value, 1) for value in kv]
-        send, own = first_parts([queries, out_grad], low, high, [own])
-        rec = swapped(send)
-        sends = head_parts(own, rec, others, qg_turn)
-        qg = [round_sub(value, by) for by, value in zip(others, sends)]
-        qg_own = head_parts(own, rec, [0], [])
-        first_turn, kv_turn, qg_turn = sends, kv, qg
-        grads, dq, early = attention_grads(bias, kv_own + kv, earlier, qg_own + qg, last)
+    for index in range(count):
+        last = index == count - 1
+        earlier = [own_earlier[index]] + [along_blocks(value, 1, not last) for value in kv[index]]
+        qg_all = head_parts(*qg_parts[index], [0], []) + qg[index]
+        grads, dq, early = attention_grads(bias, kv_own[index] + kv[index], earlier, qg_all, last, [])
         dq = [dq[0]] + [round_sub(dq[by], by) for by in others]
+        later = [along_blocks(value, -1, False) for value in early]
         if last:
-            later = [along_blocks(value, -1) for value in early]
             dkv = summed(grads, later[1:], others, dq[1:])
-            dkv = summed(grads, later[:1], [0], []) + [round_sub(value, by) for by, value in zip(others, dkv)]
+            dkv = summed(grads, later[:1], [0], dkv[:1]) + [round_sub(value, by) for by, value in zip(others, dkv)]
         else:
-            dkv = summed(grads, [along_blocks(early[0], -1)], [0] + others, dq[1:])
+            dkv = summed(grads, later, [0] + others, dq[1:])
             dkv = [dkv[0]] + [round_sub(dkv[by], by) for by in others]
         send, keep = rows_for_pair(dq, dkv)
         kept.append(keep)

time: 77.9 us -> 65.8 us (0.84)
  starting transfers between devices: 37.8 us -> 25.3 us
  waiting for transfers between devices: 20.5 us -> 25.3 us
  Pallas kernels: 17.4 us -> 13.1 us
    ppermute x7, starting transfers between devices: 24.8 us -> 12.6 us  [along_blocks(): return lax.ppermute(value, 'blk', pairs)]
    ppermute x7, waiting for transfers between devices: 6.68 us -> 10.4 us  [along_blocks(): return lax.ppermute(value, 'blk', pairs)]
    pallas_call x16, Pallas kernels: 12.9 us -> 10.3 us  [call(): pl.pallas_call(kernel, out_shape=outs, in_specs=[spec] * len(ins), out_sp...]
    pallas_call x4 -> x2, Pallas kernels: 4.56 us -> 2.78 us  [first_parts(): pl.pallas_call(kernel, out_shape=outs, in_specs=[spec] * (len(held) + len...]
    ppermute x8, waiting for transfers between devices: 12.1 us -> 13.2 us  [round_sub(): lax.ppermute(value, 'sub', [(i, (i + by) % peers) for i in range(peers)])]
    ppermute x6 -> x5, waiting for transfers between devices: 1.71 us -> 1.71 us  [swapped(): return lax.ppermute(value, 'pair', [(0, 1), (1, 0)])]
  transfers between devices with their start and end apart: 21 -> 20, of which waited for: 9 -> 8; matrix products, arithmetic and copies ran while one was open for 1% -> 1% of each run, Pallas kernels for 19% -> 16%
where the time goes in v6:
time: 65.8 us; the launch traced here: 65.5 us
  starting transfers between devices  25.3 us (38%)
  waiting for transfers between devices  25.3 us (38%)
  Pallas kernels  13.1 us (20%)
  between operations  0.9 us (1%)
  other arithmetic  0.79 us (1%)
    ppermute x8, waiting for transfers between devices, round_sub(): lax.ppermute(value, 'sub', [(i, (i + by) % peers) for i in range(peers)])  13.2 us
    ppermute x7, starting transfers between devices, along_blocks(): return lax.ppermute(value, 'blk', pairs)  12.6 us
    ppermute x8, starting transfers between devices, round_sub(): lax.ppermute(value, 'sub', [(i, (i + by) % peers) for i in range(peers)])  11.4 us
    ppermute x7, waiting for transfers between devices, along_blocks(): return lax.ppermute(value, 'blk', pairs)  10.4 us
    pallas_call x16, Pallas kernels, call(): pl.pallas_call(kernel, out_shape=outs, in_specs=[spec] * len(ins), out_sp...  10.3 us
    pallas_call x2, Pallas kernels, first_parts(): pl.pallas_call(kernel, out_shape=outs, in_specs=[spec] * (len(held) + len...  2.78 us
    ppermute x5, waiting for transfers between devices, swapped(): return lax.ppermute(value, 'pair', [(0, 1), (1, 0)])  1.71 us
  transfers between devices with their start and end apart: 20, of which 8 were waited for; matrix products, arithmetic and copies ran while one was open for 1% of the time, Pallas kernels for 16%

profile of v6, /device:TPU:0, one launch (start us, length us, event | category | flops | bytes accessed | tf_op | source)
XLA Modules:
  0.0 65.5 jit_solution(9187752441878610740)
XLA Ops:
  0.6 1.1 %first_parts.2 = (bf16[2,2,128,256]{3,2,1,0:T(8,128)(2,1)S(1)}, bf16[2,2,128,256]{3,2,1,0:T(8,128)(2,1)S(1)}) custom-call(bf16[128,2048]{1,0:T(8,128)(2,1)} %refs_2_.1, bf16[128,2048]{1,0:T(8,128)(2,1)} %refs_3_.1), custom_call_target="tpu_custom_call" | custom-call | tf_op jit(solution)/shard_map/first_parts/pallas_call | solution.py:92
  1.8 0.5 collective-permute-start
  2.3 1.6 %first_parts.3 = (bf16[2,2,128,256]{3,2,1,0:T(8,128)(2,1)S(1)}, bf16[2,2,128,256]{3,2,1,0:T(8,128)(2,1)S(1)}, bf16[4,2,128,256]{3,2,1,0:T(8,128)(2,1)S(1)}, bf16[4,2,128,256]{3,2,1,0:T(8,128)(2,1)S(1)}) custom-call(bf16[128,2048]{1,0:T(8,128)(2,1)} %refs_4_.1, bf16[128,2048]{1,0:T(8,128)(2,1)} %refs_5_.1, bf16[128,2048]{1,0:T(8,128)(2,1)} %refs_2_.1, ...), custom_call_target="tpu_custom_call" | custom-call | tf_op jit(solution)/shard_map/first_parts/pallas_call | solution.py:92
  3.9 0.1 collective-permute-start.4
  4.1 0.5 collective-permute-start.9
  4.6 0.1 pad_dynamic-slice_fusion
  4.7 0.2 head_parts.9
  4.8 2.6 %collective-permute-start.1 = (bf16[2,2,128,256]{3,2,1,0:T(8,128)(2,1)S(1)}, bf16[2,2,128,256]{3,2,1,0:T(8,128)(2,1)S(1)}, u32[]{:S(2)}, u32[]{:S(2)}) collective-permute-start(bf16[2,2,128,256]{3,2,1,0:T(8,128)(2,1)S(1)} %head_parts.9), channel_id=1, source_target_pairs={{0,2},{2,0},{1,3},{3,1},{4,6},{6,4},{5,7},{7,5},{8,10},{10,8},{9,1... | collective-permute-start | bytes 786440 | tf_op jit(solution)/shard_map/ppermute | solution.py:32
  7.5 0.2 head_parts.8.refs_1_
  7.7 1.6 %collective-permute-start.2 = (bf16[2,2,128,256]{3,2,1,0:T(8,128)(2,1)S(1)}, bf16[2,2,128,256]{3,2,1,0:T(8,128)(2,1)S(1)}, u32[]{:S(2)}, u32[]{:S(2)}) collective-permute-start(bf16[2,2,128,256]{3,2,1,0:T(8,128)(2,1)S(1)} %head_parts.8.refs_1_), channel_id=1, source_target_pairs={{0,4},{4,8},{8,12},{12,0},{1,5},{5,9},{9,13},{13,1},{2,6},{6,10},{... | collective-permute-start | bytes 786440 | tf_op jit(solution)/shard_map/ppermute | solution.py:27
  9.3 0.2 head_parts.11
  9.5 0.6 collective-permute-start.5
  10.1 4.5 %collective-permute-done.1.refs_2_.refs_0_ = bf16[2,2,128,256]{3,2,1,0:T(8,128)(2,1)S(1)} collective-permute-done((bf16[2,2,128,256]{3,2,1,0:T(8,128)(2,1)S(1)}, bf16[2,2,128,256]{3,2,1,0:T(8,128)(2,1)S(1)}, u32[]{:S(2)}, u32[]{:S(2)}) %collective-permute-start.1) | collective-permute-done | bytes 262176 | tf_op jit(solution)/shard_map/ppermute | solution.py:32
  14.6 0.2 head_parts.13
  14.8 2.0 %collective-permute-start.10 = (bf16[2,2,128,256]{3,2,1,0:T(8,128)(2,1)S(1)}, bf16[2,2,128,256]{3,2,1,0:T(8,128)(2,1)S(1)}, u32[]{:S(2)}, u32[]{:S(2)}) collective-permute-start(bf16[2,2,128,256]{3,2,1,0:T(8,128)(2,1)S(1)} %head_parts.13), channel_id=1, source_target_pairs={{0,2},{2,0},{1,3},{3,1},{4,6},{6,4},{5,7},{7,5},{8,10},{10,8},{9,1... | collective-permute-start | bytes 786440 | tf_op jit(solution)/shard_map/ppermute | solution.py:32
  16.8 1.6 %collective-permute-start.3 = (bf16[2,2,128,256]{3,2,1,0:T(8,128)(2,1)S(1)}, bf16[2,2,128,256]{3,2,1,0:T(8,128)(2,1)S(1)}, u32[]{:S(2)}, u32[]{:S(2)}) collective-permute-start(bf16[2,2,128,256]{3,2,1,0:T(8,128)(2,1)S(1)} %collective-permute-done.1.refs_2_.refs_0_), channel_id=1, source_target_pairs={{0,4},{4,8},{8,12},{12,0},{1,5},{5,9},{9,13},{13,1},{2,6},{6,10},{... | collective-permute-start | bytes 786440 | tf_op jit(solution)/shard_map/ppermute | solution.py:27
  18.4 0.7 %and_select_fusion = (f32[1,768,256]{2,1,0:T(8,128)S(1)}, f32[1,768,256]{2,1,0:T(8,128)S(1)}) fusion(s32[256]{0:T(256)S(1)} %get-tuple-element.54, s32[256]{0:T(256)S(1)} %get-tuple-element.52, s32[768]{0:T(1024)S(1)} %get-tuple-element.50, s32[768]{0:T(1024)S(1)} %get-tuple-element.48, pred[768]{0:T(1024)(128)(4,1)S(1)} %get-tuple-element.46, ...), kind=kLoop, calls=%fused_computation.1 | loop fusion | flops 1966080 | bytes 1590784 | tf_op jit(solution)/shard_map/jit(_where)/select_n | solution.py:291
  19.1 0.1 pad_maximum_fusion.refs_0_
  19.2 0.2 head_parts.10.refs_5_
  19.4 0.2 head_parts.12.refs_1_
  19.6 1.6 %collective-permute-start.11 = (bf16[2,2,128,256]{3,2,1,0:T(8,128)(2,1)S(1)}, bf16[2,2,128,256]{3,2,1,0:T(8,128)(2,1)S(1)}, u32[]{:S(2)}, u32[]{:S(2)}) collective-permute-start(bf16[2,2,128,256]{3,2,1,0:T(8,128)(2,1)S(1)} %head_parts.12.refs_1_), channel_id=1, source_target_pairs={{0,4},{4,8},{8,12},{12,0},{1,5},{5,9},{9,13},{13,1},{2,6},{6,10},{... | collective-permute-start | bytes 786440 | tf_op jit(solution)/shard_map/ppermute | solution.py:27
  21.3 0.2 head_parts.15
  21.4 1.0 %collective-permute-start.13 = (bf16[2,2,128,256]{3,2,1,0:T(8,128)(2,1)S(1)}, bf16[2,2,128,256]{3,2,1,0:T(8,128)(2,1)S(1)}, u32[]{:S(2)}, u32[]{:S(2)}) collective-permute-start(bf16[2,2,128,256]{3,2,1,0:T(8,128)(2,1)S(1)} %head_parts.15), channel_id=1, source_target_pairs={{0,2},{2,0},{1,3},{3,1},{4,6},{6,4},{5,7},{7,5},{8,10},{10,8},{9,1... | collective-permute-start | bytes 786440 | tf_op jit(solution)/shard_map/ppermute | solution.py:32
  22.4 3.4 %collective-permute-done.10.refs_2_ = bf16[2,2,128,256]{3,2,1,0:T(8,128)(2,1)S(1)} collective-permute-done((bf16[2,2,128,256]{3,2,1,0:T(8,128)(2,1)S(1)}, bf16[2,2,128,256]{3,2,1,0:T(8,128)(2,1)S(1)}, u32[]{:S(2)}, u32[]{:S(2)}) %collective-permute-start.10) | collective-permute-done | bytes 262176 | tf_op jit(solution)/shard_map/ppermute | solution.py:32
  25.9 3.9 %collective-permute-start.12 = (bf16[2,2,128,256]{3,2,1,0:T(8,128)(2,1)S(1)}, bf16[2,2,128,256]{3,2,1,0:T(8,128)(2,1)S(1)}, u32[]{:S(2)}, u32[]{:S(2)}) collective-permute-start(bf16[2,2,128,256]{3,2,1,0:T(8,128)(2,1)S(1)} %collective-permute-done.10.refs_2_), channel_id=1, source_target_pairs={{0,4},{4,8},{8,12},{1,5},{5,9},{9,13},{2,6},{6,10},{10,14},{3,7},{... | collective-permute-start | bytes 786440 | tf_op jit(solution)/shard_map/ppermute | solution.py:27
  29.8 3.6 %attention_grads.2 = (f32[2,2,2,128,256]{4,3,2,1,0:T(8,128)S(1)}, bf16[2,128,256]{2,1,0:T(8,128)(2,1)S(1)}, bf16[2,128,256]{2,1,0:T(8,128)(2,1)S(1)}, bf16[2,2,2,128,256]{4,3,2,1,0:T(8,128)(2,1)S(1)}) custom-call(f32[2,768,256]{2,1,0:T(8,128)S(1)} %pad_maximum_fusion.refs_0_, bf16[2,2,128,256]{3,2,1,0:T(8,128)(2,1)S(1)} %head_parts.8.refs_1_, ...), custom_call_target="tpu_custom_call" | custom-call | flops 1006632960 | bytes 4980736 | tf_op jit(solution)/shard_map/attention_grads/pallas_call | solution.py:51
  33.4 1.3 %collective-permute-start.7 = (bf16[2,2,2,128,256]{4,3,2,1,0:T(8,128)(2,1)S(1)}, bf16[2,2,2,128,256]{4,3,2,1,0:T(8,128)(2,1)S(1)}, u32[]{:S(2)}, u32[]{:S(2)}) collective-permute-start(bf16[2,2,2,128,256]{4,3,2,1,0:T(8,128)(2,1)S(1)} %get-tuple-element.31), channel_id=1, source_target_pairs={{4,0},{8,4},{12,8},{5,1},{9,5},{13,9},{6,2},{10,6},{14,10},{7,3},{... | collective-permute-start | bytes 1572872 | tf_op jit(solution)/shard_map/ppermute | solution.py:27
  34.7 0.2 head_parts.14.refs_5_
  34.9 3.6 %attention_grads.3 = (f32[2,2,2,128,256]{4,3,2,1,0:T(8,128)S(1)}, bf16[2,128,256]{2,1,0:T(8,128)(2,1)S(1)}, bf16[2,128,256]{2,1,0:T(8,128)(2,1)S(1)}, bf16[2,2,1...) custom-call(f32[2,768,256]{2,1,0:T(8,128)S(1)} %pad_maximum_fusion.refs_0_, ...), custom_call_target="tpu_custom_call" | custom-call | flops 1006632960 | bytes 4980736 | tf_op jit(solution)/shard_map/attention_grads/pallas_call | solution.py:51
  38.5 1.3 %collective-permute-start.16 = (bf16[2,2,128,256]{3,2,1,0:T(8,128)(2,1)S(1)}, bf16[2,2,128,256]{3,2,1,0:T(8,128)(2,1)S(1)}, u32[]{:S(2)}, u32[]{:S(2)}) collective-permute-start(bf16[2,2,128,256]{3,2,1,0:T(8,128)(2,1)S(1)} %get-tuple-element.41), channel_id=1, source_target_pairs={{4,0},{8,4},{12,8},{5,1},{9,5},{13,9},{6,2},{10,6},{14,10},{7,3},{... | collective-permute-start | bytes 786440 | tf_op jit(solution)/shard_map/ppermute | solution.py:27
  39.8 1.6 %collective-permute-start.6 = (bf16[2,128,256]{2,1,0:T(8,128)(2,1)S(1)}, bf16[2,128,256]{2,1,0:T(8,128)(2,1)S(1)}, u32[]{:S(2)}, u32[]{:S(2)}) collective-permute-start(bf16[2,128,256]{2,1,0:T(8,128)(2,1)S(1)} %get-tuple-element.29), channel_id=1, source_target_pairs={{0,2},{2,0},{1,3},{3,1},{4,6},{6,4},{5,7},{7,5},{8,10},{10,8},{9,1... | collective-permute-start | bytes 393224 | tf_op jit(solution)/shard_map/ppermute | solution.py:32
  41.4 0.5 collective-permute-start.14
  41.9 1.3 %collective-permute-start.15 = (bf16[2,2,128,256]{3,2,1,0:T(8,128)(2,1)S(1)}, bf16[2,2,128,256]{3,2,1,0:T(8,128)(2,1)S(1)}, u32[]{:S(2)}, u32[]{:S(2)}) collective-permute-start(bf16[2,2,128,256]{3,2,1,0:T(8,128)(2,1)S(1)} %get-tuple-element.40), channel_id=1, source_target_pairs={{4,0},{8,4},{12,8},{5,1},{9,5},{13,9},{6,2},{10,6},{14,10},{7,3},{... | collective-permute-start | bytes 786440 | tf_op jit(solution)/shard_map/ppermute | solution.py:27
  43.2 2.4 %collective-permute-done.6.refs_1_ = bf16[2,128,256]{2,1,0:T(8,128)(2,1)S(1)} collective-permute-done((bf16[2,128,256]{2,1,0:T(8,128)(2,1)S(1)}, bf16[2,128,256]{2,1,0:T(8,128)(2,1)S(1)}, u32[]{:S(2)}, u32[]{:S(2)}) %collective-permute-start.6) | collective-permute-done | bytes 131104 | tf_op jit(solution)/shard_map/ppermute | solution.py:32
  45.6 4.5 %collective-permute-done.7.refs_0_ = bf16[2,2,2,128,256]{4,3,2,1,0:T(8,128)(2,1)S(1)} collective-permute-done((bf16[2,2,2,128,256]{4,3,2,1,0:T(8,128)(2,1)S(1)}, bf16[2,2,2,128,256]{4,3,2,1,0:T(8,128)(2,1)S(1)}, u32[]{:S(2)}, u32[]{:S(2)}) %collective-permute-start.7) | collective-permute-done | bytes 524320 | tf_op jit(solution)/shard_map/ppermute | solution.py:27
  50.1 0.1 summed.3
  50.2 1.6 %collective-permute-start.8 = (bf16[2,2,128,256]{3,2,1,0:T(8,128)(2,1)S(1)}, bf16[2,2,128,256]{3,2,1,0:T(8,128)(2,1)S(1)}, u32[]{:S(2)}, u32[]{:S(2)}) collective-permute-start(bf16[2,2,128,256]{3,2,1,0:T(8,128)(2,1)S(1)} %get-tuple-element.33), channel_id=1, source_target_pairs={{0,2},{2,0},{1,3},{3,1},{4,6},{6,4},{5,7},{7,5},{8,10},{10,8},{9,1... | collective-permute-start | bytes 786440 | tf_op jit(solution)/shard_map/ppermute | solution.py:32
  51.8 4.0 %collective-permute-done.16.refs_0_ = bf16[2,2,128,256]{3,2,1,0:T(8,128)(2,1)S(1)} collective-permute-done((bf16[2,2,128,256]{3,2,1,0:T(8,128)(2,1)S(1)}, bf16[2,2,128,256]{3,2,1,0:T(8,128)(2,1)S(1)}, u32[]{:S(2)}, u32[]{:S(2)}) %collective-permute-start.16) | collective-permute-done | bytes 262176 | tf_op jit(solution)/shard_map/ppermute | solution.py:27
  55.8 0.1 summed.4.refs_1_
  55.8 1.6 %collective-permute-start.17 = (bf16[2,2,128,256]{3,2,1,0:T(8,128)(2,1)S(1)}, bf16[2,2,128,256]{3,2,1,0:T(8,128)(2,1)S(1)}, u32[]{:S(2)}, u32[]{:S(2)}) collective-permute-start(bf16[2,2,128,256]{3,2,1,0:T(8,128)(2,1)S(1)} %summed.4.refs_1_), channel_id=1, source_target_pairs={{0,2},{2,0},{1,3},{3,1},{4,6},{6,4},{5,7},{7,5},{8,10},{10,8},{9,1... | collective-permute-start | bytes 786440 | tf_op jit(solution)/shard_map/ppermute | solution.py:32
  57.4 1.9 %collective-permute-done.15.refs_0_ = bf16[2,2,128,256]{3,2,1,0:T(8,128)(2,1)S(1)} collective-permute-done((bf16[2,2,128,256]{3,2,1,0:T(8,128)(2,1)S(1)}, bf16[2,2,128,256]{3,2,1,0:T(8,128)(2,1)S(1)}, u32[]{:S(2)}, u32[]{:S(2)}) %collective-permute-start.15) | collective-permute-done | bytes 262176 | tf_op jit(solution)/shard_map/ppermute | solution.py:27
  59.3 0.1 rows_for_pair.2
  59.4 0.1 collective-permute-start.18
  59.5 2.8 %collective-permute-done.17.refs_3_ = bf16[2,2,128,256]{3,2,1,0:T(8,128)(2,1)S(1)} collective-permute-done((bf16[2,2,128,256]{3,2,1,0:T(8,128)(2,1)S(1)}, bf16[2,2,128,256]{3,2,1,0:T(8,128)(2,1)S(1)}, u32[]{:S(2)}, u32[]{:S(2)}) %collective-permute-start.17) | collective-permute-done | bytes 262176 | tf_op jit(solution)/shard_map/ppermute | solution.py:32
  62.3 0.1 rows_for_pair.3
  62.3 0.1 collective-permute-start.19
  62.4 1.7 %collective-permute-done.19.refs_3_ = bf16[3,2,128,256]{3,2,1,0:T(8,128)(2,1)S(1)} collective-permute-done((bf16[3,2,128,256]{3,2,1,0:T(8,128)(2,1)S(1)}, bf16[3,2,128,256]{3,2,1,0:T(8,128)(2,1)S(1)}, u32[]{:S(2)}, u32[]{:S(2)}) %collective-permute-start.19) | collective-permute-done | bytes 393248 | tf_op jit(solution)/shard_map/ppermute | solution.py:36
  64.1 1.3 %laid_out.1 = (bf16[128,2048]{1,0:T(8,128)(2,1)}, bf16[128,2048]{1,0:T(8,128)(2,1)}, bf16[128,2048]{1,0:T(8,128)(2,1)}) custom-call(bf16[3,2,128,256]{3,2,1,0:T(8,128)(2,1)S(1)} %get-tuple-element.34.refs_0_, bf16[3,2,128,256]{3,2,1,0:T(8,128)(2,1)S(1)} %get-tuple-element.42.refs_1_, bf16[3,2,128,256]{3,2,1,0:T(8,128)(2,1)S(1)} %collective-permute-done.18.refs_2_, ...), custom_call_target="tpu_custom_call" | custom-call | bytes 3145728 | tf_op jit(solution)/shard_map/laid_out/pallas_call | solution.py:51
  (21 shorter events, 0.1 us)
Async XLA Ops:
  1.8 2.9 %collective-permute-start = (bf16[2,2,128,256]{3,2,1,0:T(8,128)(2,1)S(1)}, bf16[2,2,128,256]{3,2,1,0:T(8,128)(2,1)S(1)}, u32[]{:S(2)}, u32[]{:S(2)}) collective-permute-start(bf16[2,2,128,256]{3,2,1,0:T(8,128)(2,1)S(1)} %get-tuple-element.25), channel_id=1, source_target_pairs={{0,1},{1,0},{2,3},{3,2},{4,5},{5,4},{6,7},{7,6},{8,9},{9,8},{10,11... | collective-permute-start | bytes 786440 | tf_op jit(solution)/shard_map/ppermute | solution.py:36
  2.3 2.3 %copy-start = (s32[2048]{0:T(1024)S(1)}, s32[2048]{0:T(1024)}, u32[]{:S(2)}) copy-start(s32[2048]{0:T(1024)} %param.9) | copy-start | bytes 24580
  3.9 5.3 %collective-permute-start.4 = (bf16[2,2,128,256]{3,2,1,0:T(8,128)(2,1)S(1)}, bf16[2,2,128,256]{3,2,1,0:T(8,128)(2,1)S(1)}, u32[]{:S(2)}, u32[]{:S(2)}) collective-permute-start(bf16[2,2,128,256]{3,2,1,0:T(8,128)(2,1)S(1)} %get-tuple-element.27), channel_id=1, source_target_pairs={{0,1},{1,0},{2,3},{3,2},{4,5},{5,4},{6,7},{7,6},{8,9},{9,8},{10,11... | collective-permute-start | bytes 786440 | tf_op jit(solution)/shard_map/ppermute | solution.py:36
  4.1 10.6 %collective-permute-start.9 = (bf16[4,2,128,256]{3,2,1,0:T(8,128)(2,1)S(1)}, bf16[4,2,128,256]{3,2,1,0:T(8,128)(2,1)S(1)}, u32[]{:S(2)}, u32[]{:S(2)}) collective-permute-start(bf16[4,2,128,256]{3,2,1,0:T(8,128)(2,1)S(1)} %get-tuple-element.36), channel_id=1, source_target_pairs={{0,1},{1,0},{2,3},{3,2},{4,5},{5,4},{6,7},{7,6},{8,9},{9,8},{10,11... | collective-permute-start | bytes 1572872 | tf_op jit(solution)/shard_map/ppermute | solution.py:36
  4.8 9.8 %collective-permute-start.1 = (bf16[2,2,128,256]{3,2,1,0:T(8,128)(2,1)S(1)}, bf16[2,2,128,256]{3,2,1,0:T(8,128)(2,1)S(1)}, u32[]{:S(2)}, u32[]{:S(2)}) collective-permute-start(bf16[2,2,128,256]{3,2,1,0:T(8,128)(2,1)S(1)} %head_parts.9), channel_id=1, source_target_pairs={{0,2},{2,0},{1,3},{3,1},{4,6},{6,4},{5,7},{7,5},{8,10},{10,8},{9,1... | collective-permute-start | bytes 786440 | tf_op jit(solution)/shard_map/ppermute | solution.py:32
  7.7 11.7 %collective-permute-start.2 = (bf16[2,2,128,256]{3,2,1,0:T(8,128)(2,1)S(1)}, bf16[2,2,128,256]{3,2,1,0:T(8,128)(2,1)S(1)}, u32[]{:S(2)}, u32[]{:S(2)}) collective-permute-start(bf16[2,2,128,256]{3,2,1,0:T(8,128)(2,1)S(1)} %head_parts.8.refs_1_), channel_id=1, source_target_pairs={{0,4},{4,8},{8,12},{12,0},{1,5},{5,9},{9,13},{13,1},{2,6},{6,10},{... | collective-permute-start | bytes 786440 | tf_op jit(solution)/shard_map/ppermute | solution.py:27
  9.5 11.8 %collective-permute-start.5 = (bf16[2,2,128,256]{3,2,1,0:T(8,128)(2,1)S(1)}, bf16[2,2,128,256]{3,2,1,0:T(8,128)(2,1)S(1)}, u32[]{:S(2)}, u32[]{:S(2)}) collective-permute-start(bf16[2,2,128,256]{3,2,1,0:T(8,128)(2,1)S(1)} %head_parts.11), channel_id=1, source_target_pairs={{0,2},{2,0},{1,3},{3,1},{4,6},{6,4},{5,7},{7,5},{8,10},{10,8},{9,1... | collective-permute-start | bytes 786440 | tf_op jit(solution)/shard_map/ppermute | solution.py:32
  14.8 11.0 %collective-permute-start.10 = (bf16[2,2,128,256]{3,2,1,0:T(8,128)(2,1)S(1)}, bf16[2,2,128,256]{3,2,1,0:T(8,128)(2,1)S(1)}, u32[]{:S(2)}, u32[]{:S(2)}) collective-permute-start(bf16[2,2,128,256]{3,2,1,0:T(8,128)(2,1)S(1)} %head_parts.13), channel_id=1, source_target_pairs={{0,2},{2,0},{1,3},{3,1},{4,6},{6,4},{5,7},{7,5},{8,10},{10,8},{9,1... | collective-permute-start | bytes 786440 | tf_op jit(solution)/shard_map/ppermute | solution.py:32
  16.8 13.0 %collective-permute-start.3 = (bf16[2,2,128,256]{3,2,1,0:T(8,128)(2,1)S(1)}, bf16[2,2,128,256]{3,2,1,0:T(8,128)(2,1)S(1)}, u32[]{:S(2)}, u32[]{:S(2)}) collective-permute-start(bf16[2,2,128,256]{3,2,1,0:T(8,128)(2,1)S(1)} %collective-permute-done.1.refs_2_.refs_0_), channel_id=1, source_target_pairs={{0,4},{4,8},{8,12},{12,0},{1,5},{5,9},{9,13},{13,1},{2,6},{6,10},{... | collective-permute-start | bytes 786440 | tf_op jit(solution)/shard_map/ppermute | solution.py:27
  19.6 15.3 %collective-permute-start.11 = (bf16[2,2,128,256]{3,2,1,0:T(8,128)(2,1)S(1)}, bf16[2,2,128,256]{3,2,1,0:T(8,128)(2,1)S(1)}, u32[]{:S(2)}, u32[]{:S(2)}) collective-permute-start(bf16[2,2,128,256]{3,2,1,0:T(8,128)(2,1)S(1)} %head_parts.12.refs_1_), channel_id=1, source_target_pairs={{0,4},{4,8},{8,12},{12,0},{1,5},{5,9},{9,13},{13,1},{2,6},{6,10},{... | collective-permute-start | bytes 786440 | tf_op jit(solution)/shard_map/ppermute | solution.py:27
  21.4 13.5 %collective-permute-start.13 = (bf16[2,2,128,256]{3,2,1,0:T(8,128)(2,1)S(1)}, bf16[2,2,128,256]{3,2,1,0:T(8,128)(2,1)S(1)}, u32[]{:S(2)}, u32[]{:S(2)}) collective-permute-start(bf16[2,2,128,256]{3,2,1,0:T(8,128)(2,1)S(1)} %head_parts.15), channel_id=1, source_target_pairs={{0,2},{2,0},{1,3},{3,1},{4,6},{6,4},{5,7},{7,5},{8,10},{10,8},{9,1... | collective-permute-start | bytes 786440 | tf_op jit(solution)/shard_map/ppermute | solution.py:32
  25.9 9.1 %collective-permute-start.12 = (bf16[2,2,128,256]{3,2,1,0:T(8,128)(2,1)S(1)}, bf16[2,2,128,256]{3,2,1,0:T(8,128)(2,1)S(1)}, u32[]{:S(2)}, u32[]{:S(2)}) collective-permute-start(bf16[2,2,128,256]{3,2,1,0:T(8,128)(2,1)S(1)} %collective-permute-done.10.refs_2_), channel_id=1, source_target_pairs={{0,4},{4,8},{8,12},{1,5},{5,9},{9,13},{2,6},{6,10},{10,14},{3,7},{... | collective-permute-start | bytes 786440 | tf_op jit(solution)/shard_map/ppermute | solution.py:27
  33.4 16.8 %collective-permute-start.7 = (bf16[2,2,2,128,256]{4,3,2,1,0:T(8,128)(2,1)S(1)}, bf16[2,2,2,128,256]{4,3,2,1,0:T(8,128)(2,1)S(1)}, u32[]{:S(2)}, u32[]{:S(2)}) collective-permute-start(bf16[2,2,2,128,256]{4,3,2,1,0:T(8,128)(2,1)S(1)} %get-tuple-element.31), channel_id=1, source_target_pairs={{4,0},{8,4},{12,8},{5,1},{9,5},{13,9},{6,2},{10,6},{14,10},{7,3},{... | collective-permute-start | bytes 1572872 | tf_op jit(solution)/shard_map/ppermute | solution.py:27
  38.5 17.3 %collective-permute-start.16 = (bf16[2,2,128,256]{3,2,1,0:T(8,128)(2,1)S(1)}, bf16[2,2,128,256]{3,2,1,0:T(8,128)(2,1)S(1)}, u32[]{:S(2)}, u32[]{:S(2)}) collective-permute-start(bf16[2,2,128,256]{3,2,1,0:T(8,128)(2,1)S(1)} %get-tuple-element.41), channel_id=1, source_target_pairs={{4,0},{8,4},{12,8},{5,1},{9,5},{13,9},{6,2},{10,6},{14,10},{7,3},{... | collective-permute-start | bytes 786440 | tf_op jit(solution)/shard_map/ppermute | solution.py:27
  39.8 5.8 %collective-permute-start.6 = (bf16[2,128,256]{2,1,0:T(8,128)(2,1)S(1)}, bf16[2,128,256]{2,1,0:T(8,128)(2,1)S(1)}, u32[]{:S(2)}, u32[]{:S(2)}) collective-permute-start(bf16[2,128,256]{2,1,0:T(8,128)(2,1)S(1)} %get-tuple-element.29), channel_id=1, source_target_pairs={{0,2},{2,0},{1,3},{3,1},{4,6},{6,4},{5,7},{7,5},{8,10},{10,8},{9,1... | collective-permute-start | bytes 393224 | tf_op jit(solution)/shard_map/ppermute | solution.py:32
  41.4 10.4 %collective-permute-start.14 = (bf16[2,128,256]{2,1,0:T(8,128)(2,1)S(1)}, bf16[2,128,256]{2,1,0:T(8,128)(2,1)S(1)}, u32[]{:S(2)}, u32[]{:S(2)}) collective-permute-start(bf16[2,128,256]{2,1,0:T(8,128)(2,1)S(1)} %get-tuple-element.38), channel_id=1, source_target_pairs={{0,2},{2,0},{1,3},{3,1},{4,6},{6,4},{5,7},{7,5},{8,10},{10,8},{9,1... | collective-permute-start | bytes 393224 | tf_op jit(solution)/shard_map/ppermute | solution.py:32
  41.9 17.4 %collective-permute-start.15 = (bf16[2,2,128,256]{3,2,1,0:T(8,128)(2,1)S(1)}, bf16[2,2,128,256]{3,2,1,0:T(8,128)(2,1)S(1)}, u32[]{:S(2)}, u32[]{:S(2)}) collective-permute-start(bf16[2,2,128,256]{3,2,1,0:T(8,128)(2,1)S(1)} %get-tuple-element.40), channel_id=1, source_target_pairs={{4,0},{8,4},{12,8},{5,1},{9,5},{13,9},{6,2},{10,6},{14,10},{7,3},{... | collective-permute-start | bytes 786440 | tf_op jit(solution)/shard_map/ppermute | solution.py:27
  50.2 9.1 %collective-permute-start.8 = (bf16[2,2,128,256]{3,2,1,0:T(8,128)(2,1)S(1)}, bf16[2,2,128,256]{3,2,1,0:T(8,128)(2,1)S(1)}, u32[]{:S(2)}, u32[]{:S(2)}) collective-permute-start(bf16[2,2,128,256]{3,2,1,0:T(8,128)(2,1)S(1)} %get-tuple-element.33), channel_id=1, source_target_pairs={{0,2},{2,0},{1,3},{3,1},{4,6},{6,4},{5,7},{7,5},{8,10},{10,8},{9,1... | collective-permute-start | bytes 786440 | tf_op jit(solution)/shard_map/ppermute | solution.py:32
  55.8 6.5 %collective-permute-start.17 = (bf16[2,2,128,256]{3,2,1,0:T(8,128)(2,1)S(1)}, bf16[2,2,128,256]{3,2,1,0:T(8,128)(2,1)S(1)}, u32[]{:S(2)}, u32[]{:S(2)}) collective-permute-start(bf16[2,2,128,256]{3,2,1,0:T(8,128)(2,1)S(1)} %summed.4.refs_1_), channel_id=1, source_target_pairs={{0,2},{2,0},{1,3},{3,1},{4,6},{6,4},{5,7},{7,5},{8,10},{10,8},{9,1... | collective-permute-start | bytes 786440 | tf_op jit(solution)/shard_map/ppermute | solution.py:32
  59.4 3.0 %collective-permute-start.18 = (bf16[3,2,128,256]{3,2,1,0:T(8,128)(2,1)S(1)}, bf16[3,2,128,256]{3,2,1,0:T(8,128)(2,1)S(1)}, u32[]{:S(2)}, u32[]{:S(2)}) collective-permute-start(bf16[3,2,128,256]{3,2,1,0:T(8,128)(2,1)S(1)} %get-tuple-element.43), channel_id=1, source_target_pairs={{0,1},{1,0},{2,3},{3,2},{4,5},{5,4},{6,7},{7,6},{8,9},{9,8},{10,11... | collective-permute-start | bytes 1179656 | tf_op jit(solution)/shard_map/ppermute | solution.py:36
  62.3 1.8 %collective-permute-start.19 = (bf16[3,2,128,256]{3,2,1,0:T(8,128)(2,1)S(1)}, bf16[3,2,128,256]{3,2,1,0:T(8,128)(2,1)S(1)}, u32[]{:S(2)}, u32[]{:S(2)}) collective-permute-start(bf16[3,2,128,256]{3,2,1,0:T(8,128)(2,1)S(1)} %get-tuple-element.44), channel_id=1, source_target_pairs={{0,1},{1,0},{2,3},{3,2},{4,5},{5,4},{6,7},{7,6},{8,9},{9,8},{10,11... | collective-permute-start | bytes 1179656 | tf_op jit(solution)/shard_map/ppermute | solution.py:36

commit v7 on v6

--- a/solution.py
+++ b/solution.py
@@ -21,9 +21,17 @@
     return [heads // 2, heads - heads // 2]
 
 
-def along_blocks(value, by, ring):
+def along_blocks(value, by):
     peers = lax.axis_size("blk")
-    pairs = [(i, (i + by) % peers) for i in range(peers) if ring or 0 <= i + by < peers]
+    return lax.ppermute(value, "blk", [(i, i + by) for i in range(peers) if 0 <= i + by < peers])
+
+
+def neighbours(value, first):
+    peers = lax.axis_size("blk")
+    pairs = []
+    for i in range(peers):
+        other = i + 1 if (i % 2 == 0) == first else i - 1
+        pairs.append((i, other if 0 <= other < peers else i))
     return lax.ppermute(value, "blk", pairs)
 
 
@@ -119,40 +127,85 @@
     return call(kernel, [own, paired] + after, outs, scratch, "head_parts")
 
 
-def attention_grads(bias, kv, kv_earlier, qg, split, after):
+def relayed(value, after):
+    def kernel(value_ref, *refs):
+        run_moves([(value_ref, refs[-2])], refs[-1])
+
+    scratch = [pltpu.SemaphoreType.DMA((1,))]
+    return call(kernel, [value] + after, [shape(*value.shape)], scratch, "relayed")[0]
+
+
+def near_exchange(kv_parts, qg_parts, spans):
+    _, _, rows, _ = kv_parts[0][0].shape
+    ins = [array for parts in kv_parts + qg_parts for array in parts[:2]]
+
+    def kernel(*refs):
+        outs, sems = refs[-3:-1], refs[-1]
+        p, s = lax.axis_index("pair"), lax.axis_index("sub")
+        count = len(spans)
+
+        def fill(out, parts, first):
+            moves = []
+            for chunk, (low, high) in enumerate(spans):
+                which = pl.ds(parts[chunk][2], 2)
+                for side, ref in zip((p, 1 - p), refs[2 * (first + chunk):]):
+                    moves.append((ref.at[which, s], out.at[:, side, :, pl.ds(low, high - low)]))
+            return moves
+
+        for odd, order in ((0, outs), (1, outs[::-1])):
+            @pl.when(lax.rem(lax.axis_index("blk"), 2) == odd)
+            def _():
+                run_moves(fill(order[0], kv_parts, 0) + fill(order[1], qg_parts, count), sems)
+
+    outs = [shape(2, 2, rows, spans[-1][1])] * 2
+    scratch = [pltpu.SemaphoreType.DMA((4 * len(spans),))]
+    return call(kernel, ins, outs, scratch, "near_exchange")
+
+
+def either(condition, when_true, otherwise, held, sem):
+    @pl.when(condition)
+    def _():
+        run_moves([(when_true, held)], sem)
+
+    @pl.when(jnp.logical_not(condition))
+    def _():
+        run_moves([(otherwise, held)], sem)
+
+
+def query_grads(bias, kv, near, far, qg, span):
     peers = len(kv)
     _, _, rows, cut = kv[0].shape
     heads = cut // HD
     strip = rows * peers
-    early_count = peers if split else 1
-
-    def kernel(*refs):
-        bias_ref = refs[0]
-        kv_in, early_in, qg_in = refs[1:1 + peers], refs[1 + peers:1 + 2 * peers], refs[1 + 2 * peers:1 + 3 * peers]
-        outs = refs[1 + 3 * peers + len(after):-5]
-        own_out, dq_outs, early_outs = outs[0], outs[1:1 + peers], outs[1 + peers:]
-        kv_all, qg_all, early, dq_all, sems = refs[-5:]
+
+    def kernel(*refs):
+        bias_ref, first, second = refs[:3]
+        kv_in, far_in, qg_in = refs[3:3 + peers], refs[3 + peers:2 + 2 * peers], refs[2 + 2 * peers:2 + 3 * peers]
+        own_out, stats_out, *dq_outs = refs[2 + 3 * peers:-4]
+        kv_all, qg_all, dq_all, sems = refs[-4:]
         s = lax.axis_index("sub")
+        odd = lax.rem(lax.axis_index("blk"), 2) == 1
+        columns = pl.ds(span[0], cut)
+        either(odd, first.at[:, :, :, columns], second.at[:, :, :, columns], kv_all.at[:, 0:2, s], sems)
         moves = []
         for by in range(peers):
             at = lax.rem(s - by + peers, peers)
-            moves += [
-                (early_in[by], kv_all.at[:, 0:2, at]),
-                (kv_in[by], kv_all.at[:, 2:4, at]),
-                (qg_in[by], qg_all.at[:, :, at]),
-            ]
+            moves += [(kv_in[by], kv_all.at[:, 2:4, at]), (qg_in[by], qg_all.at[:, :, at])]
+            if by:
+                moves.append((far_in[by - 1], kv_all.at[:, 0:2, at]))
         run_moves(moves, sems)
         strips = [(head, tile) for head in range(heads) for tile in range(2)]
         products, terms = {}, {}
+        stats_out[...] = jnp.zeros_like(stats_out)
 
         def flat(ref, which, tiles, head):
             block = ref[which, tiles, :, :, pl.ds(head * HD, HD)]
             return block.reshape(block.shape[0] * strip, HD)
 
         def multiply(head, tile):
-            at, span = pl.ds(tile, 1), pl.ds(tile, 3)
+            at, reach = pl.ds(tile, 1), pl.ds(tile, 3)
             q, g = flat(qg_all, 0, at, head), flat(qg_all, 1, at, head)
-            k, v = flat(kv_all, 0, span, head), flat(kv_all, 1, span, head)
+            k, v = flat(kv_all, 0, reach, head), flat(kv_all, 1, reach, head)
             scores = lax.dot_general(k, q, ROWS_BY_ROWS, preferred_element_type=WIDE)
             grad_prob = lax.dot_general(v, g, ROWS_BY_ROWS, preferred_element_type=WIDE)
             products[head, tile] = q, g, k, scores, grad_prob
@@ -162,31 +215,25 @@
             scores = scores * TO_BITS + bias_ref[tile]
             peak = jnp.max(scores, axis=0, keepdims=True)
             weight = jnp.exp2(scores - peak)
-            prob = weight * (1.0 / jnp.sum(weight, axis=0, keepdims=True))
+            total = jnp.sum(weight, axis=0, keepdims=True)
+            prob = weight * (1.0 / total)
             prob_low = prob.astype(LOW)
             row_dot = jnp.sum(prob_low.astype(WIDE) * grad_prob, axis=0, keepdims=True)
             score_low = (prob * (grad_prob - row_dot)).astype(LOW)
+            stats_out[head, 2 * tile:2 * tile + 1] = peak + jnp.log2(total)
+            stats_out[head, 2 * tile + 1:2 * tile + 2] = row_dot
             dq = jnp.dot(k.T, score_low, preferred_element_type=WIDE) * SCALE
             dq_all[tile, :, :, pl.ds(head * HD, HD)] = dq.T.astype(LOW).reshape(peers, rows, HD)
-            dk = jnp.dot(score_low, q, preferred_element_type=WIDE) * SCALE
-            dv = jnp.dot(prob_low, g, preferred_element_type=WIDE)
+            skip = (2 - tile) * strip
+            dk = jnp.dot(score_low[skip:], q, preferred_element_type=WIDE)
+            dv = jnp.dot(prob_low[skip:], g, preferred_element_type=WIDE)
             terms[head, tile] = dk, dv
 
         def gather(head):
             for which in range(2):
                 low, high = terms[head, 0][which], terms[head, 1][which]
-                sums = (
-                    low[:strip],
-                    low[strip:2 * strip] + high[:strip],
-                    low[2 * strip:] + high[strip:2 * strip],
-                    high[2 * strip:],
-                )
-                for tile, total in enumerate(sums):
-                    total = total.reshape(peers, rows, HD)
-                    if tile < 2:
-                        early[which, tile, :, :, pl.ds(head * HD, HD)] = total.astype(LOW)
-                    else:
-                        own_out[which, tile - 2, :, :, pl.ds(head * HD, HD)] = total
+                for tile, total in enumerate((low + high[:strip], high[strip:])):
+                    own_out[which, tile, :, :, pl.ds(head * HD, HD)] = total.reshape(peers, rows, HD)
 
         multiply(*strips[0])
         for at, (head, tile) in enumerate(strips):
@@ -195,45 +242,92 @@
             finish(head, tile)
             if tile == 1:
                 gather(head)
-        moves = [] if split else [(early, early_outs[0])]
-        for by in range(peers):
-            at = lax.rem(s + by, peers)
-            moves.append((dq_all.at[:, at], dq_outs[by]))
-            if split:
-                moves.append((early.at[:, :, at], early_outs[by]))
-        run_moves(moves, sems)
-
-    outs = [shape(2, 2, peers, rows, cut, dtype=WIDE)] + [shape(2, rows, cut)] * peers
-    outs += [shape(2, 2, rows, cut)] * peers if split else [shape(2, 2, peers, rows, cut)]
+        run_moves([(dq_all.at[:, lax.rem(s + by, peers)], dq_outs[by]) for by in range(peers)], sems)
+
+    outs = [shape(2, 2, peers, rows, cut, dtype=WIDE), shape(heads, 8, strip, dtype=WIDE)]
+    outs += [shape(2, rows, cut)] * peers
     scratch = [
         pltpu.VMEM((2, 4, peers, rows, cut), LOW),
-        pltpu.VMEM((2, 2, peers, rows, cut), LOW),
         pltpu.VMEM((2, 2, peers, rows, cut), LOW),
         pltpu.VMEM((2, peers, rows, cut), LOW),
         pltpu.SemaphoreType.DMA((3 * peers,)),
     ]
     flops = heads * 2 * 5 * 2 * strip * 3 * strip * HD
-    ins = [bias] + kv + kv_earlier + qg + after
-    outs = call(kernel, ins, outs, scratch, "attention_grads", whole=True, flops=flops, room=40 * MIB)
-    return outs[0], outs[1:1 + peers], outs[1 + peers:]
-
-
-def summed(own, later, turns, after):
-    _, _, peers, rows, cut = own.shape
-    split = len(later) > 1 or later[0].ndim == 4
-
-    def kernel(own_ref, *refs):
-        later_refs, outs = refs[:len(later)], refs[len(later) + len(after):]
+    ins = [bias] + near + kv + far + qg
+    outs = call(kernel, ins, outs, scratch, "query_grads", whole=True, flops=flops, room=40 * MIB)
+    return outs[0], outs[1], outs[2:]
+
+
+def key_grads(bias, kv, near, far, stats, own, span, after):
+    peers = len(kv)
+    _, _, rows, cut = kv[0].shape
+    heads = cut // HD
+    strip = rows * peers
+
+    def kernel(*refs):
+        bias_ref, first, second, stats_ref, own_ref = refs[:5]
+        kv_in, far_in = refs[5:5 + peers], refs[5 + peers:4 + 2 * peers]
+        outs = refs[4 + 2 * peers + len(after):-4]
+        kv_all, later, grads, sems = refs[-4:]
         s = lax.axis_index("sub")
-        for place, (by, out) in enumerate(zip(turns, outs)):
-            at = lax.rem(s + by, peers)
+        odd = lax.rem(lax.axis_index("blk"), 2) == 1
+        columns = pl.ds(span[0], cut)
+        either(odd, second.at[:, :, :, columns], first.at[:, :, :, columns], later.at[:, :, s], sems)
+        moves = []
+        for by in range(peers):
+            at = lax.rem(s - by + peers, peers)
+            moves.append((kv_in[by], kv_all.at[:, :, at]))
+            if by:
+                moves.append((far_in[by - 1], later.at[:, :, at]))
+        run_moves(moves, sems)
+        strips = [(head, tile) for head in range(heads) for tile in range(2)]
+        products, terms = {}, {}
+
+        def flat(ref, which, tiles, head):
+            block = ref[which, tiles, :, :, pl.ds(head * HD, HD)]
+            return block.reshape(block.shape[0] * strip, HD)
+
+        def multiply(head, tile):
+            at, reach = pl.ds(tile, 1), pl.ds(tile, 2 - tile)
+            q, g = flat(later, 0, at, head), flat(later, 1, at, head)
+            k, v = flat(kv_all, 0, reach, head), flat(kv_all, 1, reach, head)
+            scores = lax.dot_general(k, q, ROWS_BY_ROWS, preferred_element_type=WIDE)
+            grad_prob = lax.dot_general(v, g, ROWS_BY_ROWS, preferred_element_type=WIDE)
+            products[head, tile] = q, g, scores, grad_prob
+
+        def finish(head, tile):
+            q, g, scores, grad_prob = products.pop((head, tile))
+            scores = scores * TO_BITS + bias_ref[tile, :(2 - tile) * strip]
+            prob = jnp.exp2(scores - stats_ref[head, 2 * tile:2 * tile + 1])
+            score_low = (prob * (grad_prob - stats_ref[head, 2 * tile + 1:2 * tile + 2])).astype(LOW)
+            dk = jnp.dot(score_low, q, preferred_element_type=WIDE)
+            dv = jnp.dot(prob.astype(LOW), g, preferred_element_type=WIDE)
+            terms[head, tile] = dk, dv
+
+        def gather(head):
             for which in range(2):
-                for row in range(2):
-                    term = later_refs[place][which, row] if split else later_refs[0][which, row, at]
-                    out[which, row] = (own_ref[which, row, at] + term.astype(WIDE)).astype(LOW)
-
-    outs = [shape(2, 2, rows, cut)] * len(turns)
-    return call(kernel, [own] + later + after, outs, [], "summed", whole=True)
+                scale = SCALE if which == 0 else 1.0
+                wide, narrow = terms[head, 0][which], terms[head, 1][which]
+                for tile, term in ((0, wide[:strip]), (1, wide[strip:] + narrow)):
+                    here = pl.ds(head * HD, HD)
+                    term = own_ref[which, tile, :, :, here] + term.reshape(peers, rows, HD)
+                    grads[which, tile, :, :, here] = (term * scale).astype(LOW)
+
+        multiply(*strips[0])
+        for at, (head, tile) in enumerate(strips):
+            if at + 1 < len(strips):
+                multiply(*strips[at + 1])
+            finish(head, tile)
+            if tile == 1:
+                gather(head)
+        run_moves([(grads.at[:, :, lax.rem(s + by, peers)], outs[by]) for by in range(peers)], sems)
+
+    outs = [shape(2, 2, rows, cut)] * peers
+    held = pltpu.VMEM((2, 2, peers, rows, cut), LOW)
+    scratch = [held, held, held, pltpu.SemaphoreType.DMA((3 * peers,))]
+    flops = heads * 4 * 2 * 3 * strip * strip * HD
+    ins = [bias] + near + [stats, own] + kv + far + after
+    return call(kernel, ins, outs, scratch, "key_grads", whole=True, flops=flops, room=40 * MIB)
 
 
 def rows_for_pair(dq, dkv):
@@ -279,18 +373,22 @@
     strip = rows * lax.axis_size("sub")
     block = 2 * strip
     at_block = lax.axis_index("blk")
-    window = jnp.concatenate([jnp.zeros((block,), jnp.int32), session])
-    sess = lax.dynamic_slice_in_dim(window, at_block * block, 2 * block)
-    place = (at_block - 1) * block + jnp.arange(2 * block, dtype=jnp.int32)
-
-    def tile_bias(tile):
-        q_at = slice(block + tile * strip, block + (tile + 1) * strip)
-        k_at = slice(tile * strip, (tile + 3) * strip)
+    margin = jnp.zeros((block,), jnp.int32)
+    window = jnp.concatenate([margin, session, margin])
+    sess = lax.dynamic_slice_in_dim(window, at_block * block, 3 * block)
+    place = (at_block - 1) * block + jnp.arange(3 * block, dtype=jnp.int32)
+
+    def tile_bias(q_tile, k_tile, tiles):
+        q_at = slice(q_tile * strip, (q_tile + 1) * strip)
+        k_at = slice(k_tile * strip, (k_tile + tiles) * strip)
         k_place, q_place = place[k_at, None], place[None, q_at]
-        allowed = (sess[None, q_at] == sess[k_at, None]) & (k_place <= q_place) & (k_place >= 0)
+        allowed = (sess[None, q_at] == sess[k_at, None]) & (k_place <= q_place)
+        allowed = allowed & (k_place >= 0) & (q_place < session.shape[0])
         return jnp.where(allowed, 0.0, NEG_FILL)
 
-    return jnp.stack([tile_bias(0), tile_bias(1)])
+    for_queries = jnp.stack([tile_bias(2, 0, 3), tile_bias(3, 1, 3)])
+    for_keys = jnp.stack([tile_bias(4, 2, 2), tile_bias(5, 3, 2)])
+    return for_queries, for_keys
 
 
 def shards(queries, keys, values, out_grad, session):
@@ -301,7 +399,7 @@
     for heads in chunks_of(part // HD):
         spans.append((at, at + heads * HD))
         at += heads * HD
-    bias = allowed_bias(session, queries.shape[0])
+    query_bias, key_bias = allowed_bias(session, queries.shape[0])
     (kv_send, kv_first), = first_parts([([keys, values], *spans[0])], [])
     rest = [([queries, out_grad], *spans[0])] + [([keys, values, queries, out_grad], *span) for span in spans[1:]]
     rest = first_parts(rest, [kv_first])
@@ -312,28 +410,29 @@
         kv_parts.append((own, paired, 0))
         qg_parts.append((own, paired, 2))
     count = len(spans)
-    kv_sends, qg_sends, kv, qg, kv_own, own_earlier = [], [], [], [], [], []
+    near = near_exchange(kv_parts, qg_parts, spans)
+    near = [neighbours(near[0], True), neighbours(near[1], False)]
+    kv_sends, qg_sends, kv, qg = [], [], [], []
     for index in range(count):
         kv_sends.append(head_parts(*kv_parts[index], others, kv[index - 1] if index else []))
         kv.append([round_sub(value, by) for by, value in zip(others, kv_sends[index])])
-        kv_own.append(head_parts(*kv_parts[index], [0], own_earlier[index - 1:index]))
-        own_earlier.append(along_blocks(kv_own[index][0], 1, True))
         qg_sends.append(head_parts(*qg_parts[index], others, qg[index - 1] if index else []))
         qg.append([round_sub(value, by) for by, value in zip(others, qg_sends[index])])
     kept, paired = [], []
-    for index in range(count):
-        last = index == count - 1
-        earlier = [own_earlier[index]] + [along_blocks(value, 1, not last) for value in kv[index]]
+    query_turn, key_turn = [], []
+    for index, span in enumerate(spans):
+        kv_all = head_parts(*kv_parts[index], [0], []) + kv[index]
         qg_all = head_parts(*qg_parts[index], [0], []) + qg[index]
-        grads, dq, early = attention_grads(bias, kv_own[index] + kv[index], earlier, qg_all, last, [])
+        upward = [relayed(value, query_turn) if index else value for value in kv[index]]
+        downward = [relayed(value, key_turn) if index else value for value in qg[index]]
+        earlier = [along_blocks(value, 1) for value in upward]
+        later = [along_blocks(value, -1) for value in downward]
+        grads, stats, dq = query_grads(query_bias, kv_all, near, earlier, qg_all, span)
+        query_turn = [dq[0]]
         dq = [dq[0]] + [round_sub(dq[by], by) for by in others]
-        later = [along_blocks(value, -1, False) for value in early]
-        if last:
-            dkv = summed(grads, later[1:], others, dq[1:])
-            dkv = summed(grads, later[:1], [0], dkv[:1]) + [round_sub(value, by) for by, value in zip(others, dkv)]
-        else:
-            dkv = summed(grads, later, [0] + others, dq[1:])
-            dkv = [dkv[0]] + [round_sub(dkv[by], by) for by in others]
+        dkv = key_grads(key_bias, kv_all, near, later, along_blocks(stats, -1), grads, span, dq[1:])
+        key_turn = [dkv[0]]
+        dkv = [dkv[0]] + [round_sub(dkv[by], by) for by in others]
         send, keep = rows_for_pair(dq, dkv)
         kept.append(keep)
         paired.append(swapped(send))

time: 65.8 us -> 73 us (1.11)
  the two profiles are of different devices: /device:TPU:0 before, /device:TPU:29 now
where the time goes in v7:
time: 73 us; the launch traced here: 72.6 us
  starting transfers between devices  33.4 us (46%)
  waiting for transfers between devices  21.9 us (30%)
  Pallas kernels  14.9 us (20%)
  other arithmetic  1.44 us (2%)
  between operations  1 us (1%)
    ppermute x6, starting transfers between devices, along_blocks(): lax.ppermute(value, 'blk', [(i, i + by) for i in range(peers) if 0 <= i +...  15.3 us
    ppermute x8, waiting for transfers between devices, round_sub(): lax.ppermute(value, 'sub', [(i, (i + by) % peers) for i in range(peers)])  15.1 us
    pallas_call x18, Pallas kernels, call(): pl.pallas_call(kernel, out_shape=outs, in_specs=[spec] * len(ins), out_sp...  12.1 us
    ppermute x5, starting transfers between devices, swapped(): return lax.ppermute(value, 'pair', [(0, 1), (1, 0)])  9.37 us
    ppermute x8, starting transfers between devices, round_sub(): lax.ppermute(value, 'sub', [(i, (i + by) % peers) for i in range(peers)])  7.78 us
    ppermute x6, waiting for transfers between devices, along_blocks(): lax.ppermute(value, 'blk', [(i, i + by) for i in range(peers) if 0 <= i +...  5.45 us
    pallas_call x2, Pallas kernels, first_parts(): pl.pallas_call(kernel, out_shape=outs, in_specs=[spec] * (len(held) + len...  2.78 us
  transfers between devices with their start and end apart: 21, of which 9 were waited for; matrix products, arithmetic and copies ran while one was open for 2% of the time, Pallas kernels for 17%

profile of v7, /device:TPU:29, one launch (start us, length us, event | category | flops | bytes accessed | tf_op | source)
XLA Modules:
  0.0 72.6 jit_solution(7670346307980219082)
XLA Ops:
  0.6 1.1 %first_parts.2 = (bf16[2,2,128,256]{3,2,1,0:T(8,128)(2,1)S(1)}, bf16[2,2,128,256]{3,2,1,0:T(8,128)(2,1)S(1)}) custom-call(bf16[128,2048]{1,0:T(8,128)(2,1)} %refs_2_.1, bf16[128,2048]{1,0:T(8,128)(2,1)} %refs_3_.1), custom_call_target="tpu_custom_call" | custom-call | tf_op jit(solution)/shard_map/first_parts/pallas_call | solution.py:100
  1.8 0.7 %collective-permute-start = (bf16[2,2,128,256]{3,2,1,0:T(8,128)(2,1)S(1)}, bf16[2,2,128,256]{3,2,1,0:T(8,128)(2,1)S(1)}, u32[]{:S(2)}, u32[]{:S(2)}) collective-permute-start(bf16[2,2,128,256]{3,2,1,0:T(8,128)(2,1)S(1)} %get-tuple-element.28), channel_id=1, source_target_pairs={{0,1},{1,0},{2,3},{3,2},{4,5},{5,4},{6,7},{7,6},{8,9},{9,8},{10,11... | collective-permute-start | bytes 786440 | tf_op jit(solution)/shard_map/ppermute | solution.py:44
  2.5 1.6 %first_parts.3 = (bf16[2,2,128,256]{3,2,1,0:T(8,128)(2,1)S(1)}, bf16[2,2,128,256]{3,2,1,0:T(8,128)(2,1)S(1)}, bf16[4,2,128,256]{3,2,1,0:T(8,128)(2,1)S(1)}, bf16[4,2,128,256]{3,2,1,0:T(8,128)(2,1)S(1)}) custom-call(bf16[128,2048]{1,0:T(8,128)(2,1)} %refs_4_.1, bf16[128,2048]{1,0:T(8,128)(2,1)} %refs_5_.1, bf16[128,2048]{1,0:T(8,128)(2,1)} %refs_2_.1, ...), custom_call_target="tpu_custom_call" | custom-call | tf_op jit(solution)/shard_map/first_parts/pallas_call | solution.py:100
  4.3 0.5 collective-permute-start.1
  4.9 0.7 and_select_fusion
  5.6 0.2 head_parts.9
  5.8 1.3 %collective-permute-start.5 = (bf16[2,2,128,256]{3,2,1,0:T(8,128)(2,1)S(1)}, bf16[2,2,128,256]{3,2,1,0:T(8,128)(2,1)S(1)}, u32[]{:S(2)}, u32[]{:S(2)}) collective-permute-start(bf16[2,2,128,256]{3,2,1,0:T(8,128)(2,1)S(1)} %head_parts.9), channel_id=1, source_target_pairs={{0,2},{2,0},{1,3},{3,1},{4,6},{6,4},{5,7},{7,5},{8,10},{10,8},{9,1... | collective-permute-start | bytes 786440 | tf_op jit(solution)/shard_map/ppermute | solution.py:40
  7.1 0.2 near_exchange.1
  7.3 0.2 collective-permute-start.3
  7.6 0.7 collective-permute-start.4
  8.3 0.2 head_parts.11
  8.5 0.6 collective-permute-start.7
  9.1 4.7 %collective-permute-done.5.refs_4_.refs_6_.refs_0_ = bf16[2,2,128,256]{3,2,1,0:T(8,128)(2,1)S(1)} collective-permute-done((bf16[2,2,128,256]{3,2,1,0:T(8,128)(2,1)S(1)}, bf16[2,2,128,256]{3,2,1,0:T(8,128)(2,1)S(1)}, u32[]{:S(2)}, u32[]{:S(2)}) %collective-permute-start.5) | collective-permute-done | bytes 262176 | tf_op jit(solution)/shard_map/ppermute | solution.py:40
  13.8 0.2 head_parts.13
  14.0 1.3 %collective-permute-start.12 = (bf16[2,2,128,256]{3,2,1,0:T(8,128)(2,1)S(1)}, bf16[2,2,128,256]{3,2,1,0:T(8,128)(2,1)S(1)}, u32[]{:S(2)}, u32[]{:S(2)}) collective-permute-start(bf16[2,2,128,256]{3,2,1,0:T(8,128)(2,1)S(1)} %head_parts.13), channel_id=1, source_target_pairs={{0,2},{2,0},{1,3},{3,1},{4,6},{6,4},{5,7},{7,5},{8,10},{10,8},{9,1... | collective-permute-start | bytes 786440 | tf_op jit(solution)/shard_map/ppermute | solution.py:40
  15.2 1.3 %collective-permute-start.6 = (bf16[2,2,128,256]{3,2,1,0:T(8,128)(2,1)S(1)}, bf16[2,2,128,256]{3,2,1,0:T(8,128)(2,1)S(1)}, u32[]{:S(2)}, u32[]{:S(2)}) collective-permute-start(bf16[2,2,128,256]{3,2,1,0:T(8,128)(2,1)S(1)} %collective-permute-done.5.refs_4_.refs_6_.refs_0_), channel_id=1, source_target_pairs={{0,4},{4,8},{8,12},{1,5},{5,9},{9,13},{2,6},{6,10},{10,14},{3,7},{... | collective-permute-start | bytes 786440 | tf_op jit(solution)/shard_map/ppermute | solution.py:26
  16.5 0.1 pad_maximum_fusion.refs_0_
  16.7 0.2 head_parts.8.refs_3_.refs_5_
  16.9 0.2 head_parts.10.refs_6_
  17.1 2.3 %collective-permute-done.7.refs_7_.refs_0_ = bf16[2,2,128,256]{3,2,1,0:T(8,128)(2,1)S(1)} collective-permute-done((bf16[2,2,128,256]{3,2,1,0:T(8,128)(2,1)S(1)}, bf16[2,2,128,256]{3,2,1,0:T(8,128)(2,1)S(1)}, u32[]{:S(2)}, u32[]{:S(2)}) %collective-permute-start.7) | collective-permute-done | bytes 262176 | tf_op jit(solution)/shard_map/ppermute | solution.py:40
  19.4 0.2 head_parts.15
  19.6 1.3 %collective-permute-start.14 = (bf16[2,2,128,256]{3,2,1,0:T(8,128)(2,1)S(1)}, bf16[2,2,128,256]{3,2,1,0:T(8,128)(2,1)S(1)}, u32[]{:S(2)}, u32[]{:S(2)}) collective-permute-start(bf16[2,2,128,256]{3,2,1,0:T(8,128)(2,1)S(1)} %head_parts.15), channel_id=1, source_target_pairs={{0,2},{2,0},{1,3},{3,1},{4,6},{6,4},{5,7},{7,5},{8,10},{10,8},{9,1... | collective-permute-start | bytes 786440 | tf_op jit(solution)/shard_map/ppermute | solution.py:40
  20.9 5.3 %collective-permute-done.6.refs_5_ = bf16[2,2,128,256]{3,2,1,0:T(8,128)(2,1)S(1)} collective-permute-done((bf16[2,2,128,256]{3,2,1,0:T(8,128)(2,1)S(1)}, bf16[2,2,128,256]{3,2,1,0:T(8,128)(2,1)S(1)}, u32[]{:S(2)}, u32[]{:S(2)}) %collective-permute-start.6) | collective-permute-done | bytes 262176 | tf_op jit(solution)/shard_map/ppermute | solution.py:26
  26.2 4.9 %collective-permute-start.10 = (bf16[2,2,128,256]{3,2,1,0:T(8,128)(2,1)S(1)}, bf16[2,2,128,256]{3,2,1,0:T(8,128)(2,1)S(1)}, u32[]{:S(2)}, u32[]{:S(2)}) collective-permute-start(bf16[2,2,128,256]{3,2,1,0:T(8,128)(2,1)S(1)} %collective-permute-done.7.refs_7_.refs_0_), channel_id=1, source_target_pairs={{4,0},{8,4},{12,8},{5,1},{9,5},{13,9},{6,2},{10,6},{14,10},{7,3},{... | collective-permute-start | bytes 786440 | tf_op jit(solution)/shard_map/ppermute | solution.py:26
  31.2 3.2 %query_grads.2 = (f32[2,2,2,128,256]{4,3,2,1,0:T(8,128)S(1)}, f32[2,8,256]{2,1,0:T(8,128)S(1)}, bf16[2,128,256]{2,1,0:T(8,128)(2,1)S(1)}, bf16[2,128,256]{2,1,0:T(8,128)(2,1)S(1)}) custom-call(f32[2,768,256]{2,1,0:T(8,128)S(1)} %pad_maximum_fusion.refs_0_, bf16[2,2,128,512]{3,2,1,0:T(8,128)(2,1)S(1)} %collective-permute-done.3.refs_1_, ...), custom_call_target="tpu_custom_call" | custom-call | flops 1006632960 | bytes 5259264 | tf_op jit(solution)/shard_map/query_grads/pallas_call | solution.py:59
  34.5 1.3 %collective-permute-start.13 = (bf16[2,2,128,256]{3,2,1,0:T(8,128)(2,1)S(1)}, bf16[2,2,128,256]{3,2,1,0:T(8,128)(2,1)S(1)}, u32[]{:S(2)}, u32[]{:S(2)}) collective-permute-start(bf16[2,2,128,256]{3,2,1,0:T(8,128)(2,1)S(1)} %relayed.2), channel_id=1, source_target_pairs={{0,4},{4,8},{8,12},{1,5},{5,9},{9,13},{2,6},{6,10},{10,14},{3,7},{... | collective-permute-start | bytes 786440 | tf_op jit(solution)/shard_map/ppermute | solution.py:26
  35.8 0.5 and_select_fusion.2
  36.2 4.0 %collective-permute-start.9 = (f32[2,8,256]{2,1,0:T(8,128)S(1)}, f32[2,8,256]{2,1,0:T(8,128)S(1)}, u32[]{:S(2)}, u32[]{:S(2)}) collective-permute-start(f32[2,8,256]{2,1,0:T(8,128)S(1)} %get-tuple-element.37), channel_id=1, source_target_pairs={{4,0},{8,4},{12,8},{5,1},{9,5},{13,9},{6,2},{10,6},{14,10},{7,3},{... | collective-permute-start | bytes 49160 | tf_op jit(solution)/shard_map/ppermute | solution.py:26
  40.2 0.9 %collective-permute-start.8 = (bf16[2,128,256]{2,1,0:T(8,128)(2,1)S(1)}, bf16[2,128,256]{2,1,0:T(8,128)(2,1)S(1)}, u32[]{:S(2)}, u32[]{:S(2)}) collective-permute-start(bf16[2,128,256]{2,1,0:T(8,128)(2,1)S(1)} %get-tuple-element.36), channel_id=1, source_target_pairs={{0,2},{2,0},{1,3},{3,1},{4,6},{6,4},{5,7},{7,5},{8,10},{10,8},{9,1... | collective-permute-start | bytes 393224 | tf_op jit(solution)/shard_map/ppermute | solution.py:40
  41.2 3.2 %collective-permute-done.8.refs_8_.refs_1_ = bf16[2,128,256]{2,1,0:T(8,128)(2,1)S(1)} collective-permute-done((bf16[2,128,256]{2,1,0:T(8,128)(2,1)S(1)}, bf16[2,128,256]{2,1,0:T(8,128)(2,1)S(1)}, u32[]{:S(2)}, u32[]{:S(2)}) %collective-permute-start.8) | collective-permute-done | bytes 131104 | tf_op jit(solution)/shard_map/ppermute | solution.py:40
  44.4 1.2 %key_grads.2 = (bf16[2,2,128,256]{3,2,1,0:T(8,128)(2,1)S(1)}, bf16[2,2,128,256]{3,2,1,0:T(8,128)(2,1)S(1)}) custom-call(f32[2,512,256]{2,1,0:T(8,128)S(1)} %pad_maximum_fusion.1.refs_0_, bf16[2,2,128,512]{3,2,1,0:T(8,128)(2,1)S(1)} %collective-permute-done.3.refs_1_, bf16[2,2,128,512]{3,2,1,0:T(8,128)(2,1)S(1)} %collective-permute-done.4.refs_2_, ...), custom_call_target="tpu_custom_call" | custom-call | flops 402653184 | bytes 4603904 | tf_op jit(solution)/shard_map/key_grads/pallas_call | solution.py:59
  45.6 1.9 %collective-permute-start.17 = (bf16[2,2,128,256]{3,2,1,0:T(8,128)(2,1)S(1)}, bf16[2,2,128,256]{3,2,1,0:T(8,128)(2,1)S(1)}, u32[]{:S(2)}, u32[]{:S(2)}) collective-permute-start(bf16[2,2,128,256]{3,2,1,0:T(8,128)(2,1)S(1)} %relayed.3), channel_id=1, source_target_pairs={{4,0},{8,4},{12,8},{5,1},{9,5},{13,9},{6,2},{10,6},{14,10},{7,3},{... | collective-permute-start | bytes 786440 | tf_op jit(solution)/shard_map/ppermute | solution.py:26
  47.6 0.2 head_parts.12.refs_3_.refs_5_
  47.8 0.2 head_parts.14.refs_6_
  48.0 3.2 %query_grads.3 = (f32[2,2,2,128,256]{4,3,2,1,0:T(8,128)S(1)}, f32[2,8,256]{2,1,0:T(8,128)S(1)}, bf16[2,128,256]{2,1,0:T(8,128)(2,1)S(1)}, bf16[2,128,256]{2,1,0:T(8,128)(2,1)S(1)}) custom-call(f32[2,768,256]{2,1,0:T(8,128)S(1)} %pad_maximum_fusion.refs_0_, bf16[2,2,128,512]{3,2,1,0:T(8,128)(2,1)S(1)} %collective-permute-done.3.refs_1_, ...), custom_call_target="tpu_custom_call" | custom-call | flops 1006632960 | bytes 5259264 | tf_op jit(solution)/shard_map/query_grads/pallas_call | solution.py:59
  51.3 0.9 %collective-permute-start.15 = (bf16[2,128,256]{2,1,0:T(8,128)(2,1)S(1)}, bf16[2,128,256]{2,1,0:T(8,128)(2,1)S(1)}, u32[]{:S(2)}, u32[]{:S(2)}) collective-permute-start(bf16[2,128,256]{2,1,0:T(8,128)(2,1)S(1)} %get-tuple-element.43), channel_id=1, source_target_pairs={{0,2},{2,0},{1,3},{3,1},{4,6},{6,4},{5,7},{7,5},{8,10},{10,8},{9,1... | collective-permute-start | bytes 393224 | tf_op jit(solution)/shard_map/ppermute | solution.py:40
  52.1 1.9 %collective-permute-start.16 = (f32[2,8,256]{2,1,0:T(8,128)S(1)}, f32[2,8,256]{2,1,0:T(8,128)S(1)}, u32[]{:S(2)}, u32[]{:S(2)}) collective-permute-start(f32[2,8,256]{2,1,0:T(8,128)S(1)} %get-tuple-element.44), channel_id=1, source_target_pairs={{4,0},{8,4},{12,8},{5,1},{9,5},{13,9},{6,2},{10,6},{14,10},{7,3},{... | collective-permute-start | bytes 49160 | tf_op jit(solution)/shard_map/ppermute | solution.py:26
  54.0 0.7 %collective-permute-start.11 = (bf16[2,2,128,256]{3,2,1,0:T(8,128)(2,1)S(1)}, bf16[2,2,128,256]{3,2,1,0:T(8,128)(2,1)S(1)}, u32[]{:S(2)}, u32[]{:S(2)}) collective-permute-start(bf16[2,2,128,256]{3,2,1,0:T(8,128)(2,1)S(1)} %get-tuple-element.40), channel_id=1, source_target_pairs={{0,2},{2,0},{1,3},{3,1},{4,6},{6,4},{5,7},{7,5},{8,10},{10,8},{9,1... | collective-permute-start | bytes 786440 | tf_op jit(solution)/shard_map/ppermute | solution.py:40
  54.8 0.1 collective-permute-done.16.refs_3_
  54.9 0.3 collective-permute-done.15.refs_8_.refs_1_
  55.1 1.2 %key_grads.3 = (bf16[2,2,128,256]{3,2,1,0:T(8,128)(2,1)S(1)}, bf16[2,2,128,256]{3,2,1,0:T(8,128)(2,1)S(1)}) custom-call(f32[2,512,256]{2,1,0:T(8,128)S(1)} %pad_maximum_fusion.1.refs_0_, bf16[2,2,128,512]{3,2,1,0:T(8,128)(2,1)S(1)} %collective-permute-done.3.refs_1_, bf16[2,2,128,512]{3,2,1,0:T(8,128)(2,1)S(1)} %collective-permute-done.4.refs_2_, ...), custom_call_target="tpu_custom_call" | custom-call | flops 402653184 | bytes 4603904 | tf_op jit(solution)/shard_map/key_grads/pallas_call | solution.py:59
  56.3 0.9 %collective-permute-start.18 = (bf16[2,2,128,256]{3,2,1,0:T(8,128)(2,1)S(1)}, bf16[2,2,128,256]{3,2,1,0:T(8,128)(2,1)S(1)}, u32[]{:S(2)}, u32[]{:S(2)}) collective-permute-start(bf16[2,2,128,256]{3,2,1,0:T(8,128)(2,1)S(1)} %get-tuple-element.47), channel_id=1, source_target_pairs={{0,2},{2,0},{1,3},{3,1},{4,6},{6,4},{5,7},{7,5},{8,10},{10,8},{9,1... | collective-permute-start | bytes 786440 | tf_op jit(solution)/shard_map/ppermute | solution.py:40
  57.2 4.2 %collective-permute-done.11.refs_3_ = bf16[2,2,128,256]{3,2,1,0:T(8,128)(2,1)S(1)} collective-permute-done((bf16[2,2,128,256]{3,2,1,0:T(8,128)(2,1)S(1)}, bf16[2,2,128,256]{3,2,1,0:T(8,128)(2,1)S(1)}, u32[]{:S(2)}, u32[]{:S(2)}) %collective-permute-start.11) | collective-permute-done | bytes 262176 | tf_op jit(solution)/shard_map/ppermute | solution.py:40
  61.5 5.2 %collective-permute-start.19 = (bf16[3,2,128,256]{3,2,1,0:T(8,128)(2,1)S(1)}, bf16[3,2,128,256]{3,2,1,0:T(8,128)(2,1)S(1)}, u32[]{:S(2)}, u32[]{:S(2)}) collective-permute-start(bf16[3,2,128,256]{3,2,1,0:T(8,128)(2,1)S(1)} %get-tuple-element.49), channel_id=1, source_target_pairs={{0,1},{1,0},{2,3},{3,2},{4,5},{5,4},{6,7},{7,6},{8,9},{9,8},{10,11... | collective-permute-start | bytes 1179656 | tf_op jit(solution)/shard_map/ppermute | solution.py:44
  66.7 0.3 collective-permute-done.18.refs_3_
  67.1 2.8 %collective-permute-start.20 = (bf16[3,2,128,256]{3,2,1,0:T(8,128)(2,1)S(1)}, bf16[3,2,128,256]{3,2,1,0:T(8,128)(2,1)S(1)}, u32[]{:S(2)}, u32[]{:S(2)}) collective-permute-start(bf16[3,2,128,256]{3,2,1,0:T(8,128)(2,1)S(1)} %get-tuple-element.50), channel_id=1, source_target_pairs={{0,1},{1,0},{2,3},{3,2},{4,5},{5,4},{6,7},{7,6},{8,9},{9,8},{10,11... | collective-permute-start | bytes 1179656 | tf_op jit(solution)/shard_map/ppermute | solution.py:44
  69.9 1.3 %collective-permute-done.20.refs_3_ = bf16[3,2,128,256]{3,2,1,0:T(8,128)(2,1)S(1)} collective-permute-done((bf16[3,2,128,256]{3,2,1,0:T(8,128)(2,1)S(1)}, bf16[3,2,128,256]{3,2,1,0:T(8,128)(2,1)S(1)}, u32[]{:S(2)}, u32[]{:S(2)}) %collective-permute-start.20) | collective-permute-done | bytes 393248 | tf_op jit(solution)/shard_map/ppermute | solution.py:44
  71.3 1.3 %laid_out.1 = (bf16[128,2048]{1,0:T(8,128)(2,1)}, bf16[128,2048]{1,0:T(8,128)(2,1)}, bf16[128,2048]{1,0:T(8,128)(2,1)}) custom-call(bf16[3,2,128,256]{3,2,1,0:T(8,128)(2,1)S(1)} %get-tuple-element.41.refs_0_, bf16[3,2,128,256]{3,2,1,0:T(8,128)(2,1)S(1)} %get-tuple-element.48.refs_1_, bf16[3,2,128,256]{3,2,1,0:T(8,128)(2,1)S(1)} %collective-permute-done.19.refs_2_, ...), custom_call_target="tpu_custom_call" | custom-call | bytes 3145728 | tf_op jit(solution)/shard_map/laid_out/pallas_call | solution.py:59
  (32 shorter events, 0.5 us)
Async XLA Ops:
  1.8 3.8 %collective-permute-start = (bf16[2,2,128,256]{3,2,1,0:T(8,128)(2,1)S(1)}, bf16[2,2,128,256]{3,2,1,0:T(8,128)(2,1)S(1)}, u32[]{:S(2)}, u32[]{:S(2)}) collective-permute-start(bf16[2,2,128,256]{3,2,1,0:T(8,128)(2,1)S(1)} %get-tuple-element.28), channel_id=1, source_target_pairs={{0,1},{1,0},{2,3},{3,2},{4,5},{5,4},{6,7},{7,6},{8,9},{9,8},{10,11... | collective-permute-start | bytes 786440 | tf_op jit(solution)/shard_map/ppermute | solution.py:44
  2.5 2.2 %copy-start = (s32[2048]{0:T(1024)S(1)}, s32[2048]{0:T(1024)}, u32[]{:S(2)}) copy-start(s32[2048]{0:T(1024)} %param.9) | copy-start | bytes 24580
  4.2 3.0 %collective-permute-start.2 = (bf16[2,2,128,256]{3,2,1,0:T(8,128)(2,1)S(1)}, bf16[2,2,128,256]{3,2,1,0:T(8,128)(2,1)S(1)}, u32[]{:S(2)}, u32[]{:S(2)}) collective-permute-start(bf16[2,2,128,256]{3,2,1,0:T(8,128)(2,1)S(1)} %get-tuple-element.32), channel_id=1, source_target_pairs={{0,1},{1,0},{2,3},{3,2},{4,5},{5,4},{6,7},{7,6},{8,9},{9,8},{10,11... | collective-permute-start | bytes 786440 | tf_op jit(solution)/shard_map/ppermute | solution.py:44
  4.3 2.9 %collective-permute-start.1 = (bf16[4,2,128,256]{3,2,1,0:T(8,128)(2,1)S(1)}, bf16[4,2,128,256]{3,2,1,0:T(8,128)(2,1)S(1)}, u32[]{:S(2)}, u32[]{:S(2)}) collective-permute-start(bf16[4,2,128,256]{3,2,1,0:T(8,128)(2,1)S(1)} %get-tuple-element.30), channel_id=1, source_target_pairs={{0,1},{1,0},{2,3},{3,2},{4,5},{5,4},{6,7},{7,6},{8,9},{9,8},{10,11... | collective-permute-start | bytes 1572872 | tf_op jit(solution)/shard_map/ppermute | solution.py:44
  5.8 8.0 %collective-permute-start.5 = (bf16[2,2,128,256]{3,2,1,0:T(8,128)(2,1)S(1)}, bf16[2,2,128,256]{3,2,1,0:T(8,128)(2,1)S(1)}, u32[]{:S(2)}, u32[]{:S(2)}) collective-permute-start(bf16[2,2,128,256]{3,2,1,0:T(8,128)(2,1)S(1)} %head_parts.9), channel_id=1, source_target_pairs={{0,2},{2,0},{1,3},{3,1},{4,6},{6,4},{5,7},{7,5},{8,10},{10,8},{9,1... | collective-permute-start | bytes 786440 | tf_op jit(solution)/shard_map/ppermute | solution.py:40
  7.3 23.8 %collective-permute-start.3 = (bf16[2,2,128,512]{3,2,1,0:T(8,128)(2,1)S(1)}, bf16[2,2,128,512]{3,2,1,0:T(8,128)(2,1)S(1)}, u32[]{:S(2)}, u32[]{:S(2)}) collective-permute-start(bf16[2,2,128,512]{3,2,1,0:T(8,128)(2,1)S(1)} %get-tuple-element.33), channel_id=1, source_target_pairs={{0,4},{4,0},{8,12},{12,8},{1,5},{5,1},{9,13},{13,9},{2,6},{6,2},{1... | collective-permute-start | bytes 1572872 | tf_op jit(solution)/shard_map/ppermute | solution.py:35
  7.6 23.6 %collective-permute-start.4 = (bf16[2,2,128,512]{3,2,1,0:T(8,128)(2,1)S(1)}, bf16[2,2,128,512]{3,2,1,0:T(8,128)(2,1)S(1)}, u32[]{:S(2)}, u32[]{:S(2)}) collective-permute-start(bf16[2,2,128,512]{3,2,1,0:T(8,128)(2,1)S(1)} %get-tuple-element.34), channel_id=1, source_target_pairs={{0,0},{4,8},{8,4},{12,12},{1,1},{5,9},{9,5},{13,13},{2,2},{6,10},{... | collective-permute-start | bytes 1572872 | tf_op jit(solution)/shard_map/ppermute | solution.py:35
  8.5 10.9 %collective-permute-start.7 = (bf16[2,2,128,256]{3,2,1,0:T(8,128)(2,1)S(1)}, bf16[2,2,128,256]{3,2,1,0:T(8,128)(2,1)S(1)}, u32[]{:S(2)}, u32[]{:S(2)}) collective-permute-start(bf16[2,2,128,256]{3,2,1,0:T(8,128)(2,1)S(1)} %head_parts.11), channel_id=1, source_target_pairs={{0,2},{2,0},{1,3},{3,1},{4,6},{6,4},{5,7},{7,5},{8,10},{10,8},{9,1... | collective-permute-start | bytes 786440 | tf_op jit(solution)/shard_map/ppermute | solution.py:40
  14.0 20.4 %collective-permute-start.12 = (bf16[2,2,128,256]{3,2,1,0:T(8,128)(2,1)S(1)}, bf16[2,2,128,256]{3,2,1,0:T(8,128)(2,1)S(1)}, u32[]{:S(2)}, u32[]{:S(2)}) collective-permute-start(bf16[2,2,128,256]{3,2,1,0:T(8,128)(2,1)S(1)} %head_parts.13), channel_id=1, source_target_pairs={{0,2},{2,0},{1,3},{3,1},{4,6},{6,4},{5,7},{7,5},{8,10},{10,8},{9,1... | collective-permute-start | bytes 786440 | tf_op jit(solution)/shard_map/ppermute | solution.py:40
  15.2 10.9 %collective-permute-start.6 = (bf16[2,2,128,256]{3,2,1,0:T(8,128)(2,1)S(1)}, bf16[2,2,128,256]{3,2,1,0:T(8,128)(2,1)S(1)}, u32[]{:S(2)}, u32[]{:S(2)}) collective-permute-start(bf16[2,2,128,256]{3,2,1,0:T(8,128)(2,1)S(1)} %collective-permute-done.5.refs_4_.refs_6_.refs_0_), channel_id=1, source_target_pairs={{0,4},{4,8},{8,12},{1,5},{5,9},{9,13},{2,6},{6,10},{10,14},{3,7},{... | collective-permute-start | bytes 786440 | tf_op jit(solution)/shard_map/ppermute | solution.py:26
  19.6 26.0 %collective-permute-start.14 = (bf16[2,2,128,256]{3,2,1,0:T(8,128)(2,1)S(1)}, bf16[2,2,128,256]{3,2,1,0:T(8,128)(2,1)S(1)}, u32[]{:S(2)}, u32[]{:S(2)}) collective-permute-start(bf16[2,2,128,256]{3,2,1,0:T(8,128)(2,1)S(1)} %head_parts.15), channel_id=1, source_target_pairs={{0,2},{2,0},{1,3},{3,1},{4,6},{6,4},{5,7},{7,5},{8,10},{10,8},{9,1... | collective-permute-start | bytes 786440 | tf_op jit(solution)/shard_map/ppermute | solution.py:40
  26.2 15.0 %collective-permute-start.10 = (bf16[2,2,128,256]{3,2,1,0:T(8,128)(2,1)S(1)}, bf16[2,2,128,256]{3,2,1,0:T(8,128)(2,1)S(1)}, u32[]{:S(2)}, u32[]{:S(2)}) collective-permute-start(bf16[2,2,128,256]{3,2,1,0:T(8,128)(2,1)S(1)} %collective-permute-done.7.refs_7_.refs_0_), channel_id=1, source_target_pairs={{4,0},{8,4},{12,8},{5,1},{9,5},{13,9},{6,2},{10,6},{14,10},{7,3},{... | collective-permute-start | bytes 786440 | tf_op jit(solution)/shard_map/ppermute | solution.py:26
  34.5 13.6 %collective-permute-start.13 = (bf16[2,2,128,256]{3,2,1,0:T(8,128)(2,1)S(1)}, bf16[2,2,128,256]{3,2,1,0:T(8,128)(2,1)S(1)}, u32[]{:S(2)}, u32[]{:S(2)}) collective-permute-start(bf16[2,2,128,256]{3,2,1,0:T(8,128)(2,1)S(1)} %relayed.2), channel_id=1, source_target_pairs={{0,4},{4,8},{8,12},{1,5},{5,9},{9,13},{2,6},{6,10},{10,14},{3,7},{... | collective-permute-start | bytes 786440 | tf_op jit(solution)/shard_map/ppermute | solution.py:26
  36.2 4.9 %collective-permute-start.9 = (f32[2,8,256]{2,1,0:T(8,128)S(1)}, f32[2,8,256]{2,1,0:T(8,128)S(1)}, u32[]{:S(2)}, u32[]{:S(2)}) collective-permute-start(f32[2,8,256]{2,1,0:T(8,128)S(1)} %get-tuple-element.37), channel_id=1, source_target_pairs={{4,0},{8,4},{12,8},{5,1},{9,5},{13,9},{6,2},{10,6},{14,10},{7,3},{... | collective-permute-start | bytes 49160 | tf_op jit(solution)/shard_map/ppermute | solution.py:26
  40.2 4.2 %collective-permute-start.8 = (bf16[2,128,256]{2,1,0:T(8,128)(2,1)S(1)}, bf16[2,128,256]{2,1,0:T(8,128)(2,1)S(1)}, u32[]{:S(2)}, u32[]{:S(2)}) collective-permute-start(bf16[2,128,256]{2,1,0:T(8,128)(2,1)S(1)} %get-tuple-element.36), channel_id=1, source_target_pairs={{0,2},{2,0},{1,3},{3,1},{4,6},{6,4},{5,7},{7,5},{8,10},{10,8},{9,1... | collective-permute-start | bytes 393224 | tf_op jit(solution)/shard_map/ppermute | solution.py:40
  45.6 9.5 %collective-permute-start.17 = (bf16[2,2,128,256]{3,2,1,0:T(8,128)(2,1)S(1)}, bf16[2,2,128,256]{3,2,1,0:T(8,128)(2,1)S(1)}, u32[]{:S(2)}, u32[]{:S(2)}) collective-permute-start(bf16[2,2,128,256]{3,2,1,0:T(8,128)(2,1)S(1)} %relayed.3), channel_id=1, source_target_pairs={{4,0},{8,4},{12,8},{5,1},{9,5},{13,9},{6,2},{10,6},{14,10},{7,3},{... | collective-permute-start | bytes 786440 | tf_op jit(solution)/shard_map/ppermute | solution.py:26
  51.3 3.9 %collective-permute-start.15 = (bf16[2,128,256]{2,1,0:T(8,128)(2,1)S(1)}, bf16[2,128,256]{2,1,0:T(8,128)(2,1)S(1)}, u32[]{:S(2)}, u32[]{:S(2)}) collective-permute-start(bf16[2,128,256]{2,1,0:T(8,128)(2,1)S(1)} %get-tuple-element.43), channel_id=1, source_target_pairs={{0,2},{2,0},{1,3},{3,1},{4,6},{6,4},{5,7},{7,5},{8,10},{10,8},{9,1... | collective-permute-start | bytes 393224 | tf_op jit(solution)/shard_map/ppermute | solution.py:40
  52.1 2.8 %collective-permute-start.16 = (f32[2,8,256]{2,1,0:T(8,128)S(1)}, f32[2,8,256]{2,1,0:T(8,128)S(1)}, u32[]{:S(2)}, u32[]{:S(2)}) collective-permute-start(f32[2,8,256]{2,1,0:T(8,128)S(1)} %get-tuple-element.44), channel_id=1, source_target_pairs={{4,0},{8,4},{12,8},{5,1},{9,5},{13,9},{6,2},{10,6},{14,10},{7,3},{... | collective-permute-start | bytes 49160 | tf_op jit(solution)/shard_map/ppermute | solution.py:26
  54.0 7.4 %collective-permute-start.11 = (bf16[2,2,128,256]{3,2,1,0:T(8,128)(2,1)S(1)}, bf16[2,2,128,256]{3,2,1,0:T(8,128)(2,1)S(1)}, u32[]{:S(2)}, u32[]{:S(2)}) collective-permute-start(bf16[2,2,128,256]{3,2,1,0:T(8,128)(2,1)S(1)} %get-tuple-element.40), channel_id=1, source_target_pairs={{0,2},{2,0},{1,3},{3,1},{4,6},{6,4},{5,7},{7,5},{8,10},{10,8},{9,1... | collective-permute-start | bytes 786440 | tf_op jit(solution)/shard_map/ppermute | solution.py:40
  56.3 10.7 %collective-permute-start.18 = (bf16[2,2,128,256]{3,2,1,0:T(8,128)(2,1)S(1)}, bf16[2,2,128,256]{3,2,1,0:T(8,128)(2,1)S(1)}, u32[]{:S(2)}, u32[]{:S(2)}) collective-permute-start(bf16[2,2,128,256]{3,2,1,0:T(8,128)(2,1)S(1)} %get-tuple-element.47), channel_id=1, source_target_pairs={{0,2},{2,0},{1,3},{3,1},{4,6},{6,4},{5,7},{7,5},{8,10},{10,8},{9,1... | collective-permute-start | bytes 786440 | tf_op jit(solution)/shard_map/ppermute | solution.py:40
  61.5 8.5 %collective-permute-start.19 = (bf16[3,2,128,256]{3,2,1,0:T(8,128)(2,1)S(1)}, bf16[3,2,128,256]{3,2,1,0:T(8,128)(2,1)S(1)}, u32[]{:S(2)}, u32[]{:S(2)}) collective-permute-start(bf16[3,2,128,256]{3,2,1,0:T(8,128)(2,1)S(1)} %get-tuple-element.49), channel_id=1, source_target_pairs={{0,1},{1,0},{2,3},{3,2},{4,5},{5,4},{6,7},{7,6},{8,9},{9,8},{10,11... | collective-permute-start | bytes 1179656 | tf_op jit(solution)/shard_map/ppermute | solution.py:44
  67.1 4.2 %collective-permute-start.20 = (bf16[3,2,128,256]{3,2,1,0:T(8,128)(2,1)S(1)}, bf16[3,2,128,256]{3,2,1,0:T(8,128)(2,1)S(1)}, u32[]{:S(2)}, u32[]{:S(2)}) collective-permute-start(bf16[3,2,128,256]{3,2,1,0:T(8,128)(2,1)S(1)} %get-tuple-element.50), channel_id=1, source_target_pairs={{0,1},{1,0},{2,3},{3,2},{4,5},{5,4},{6,7},{7,6},{8,9},{9,8},{10,11... | collective-permute-start | bytes 1179656 | tf_op jit(solution)/shard_map/ppermute | solution.py:44

commit v8 on v6

--- a/solution.py
+++ b/solution.py
@@ -117,6 +117,14 @@
     outs = [shape(2, 2, rows, cut)] * len(turns)
     scratch = [pltpu.SemaphoreType.DMA((2 * len(turns),))]
     return call(kernel, [own, paired] + after, outs, scratch, "head_parts")
+
+
+def relayed(value, after):
+    def kernel(value_ref, *refs):
+        run_moves([(value_ref, refs[-2])], refs[-1])
+
+    scratch = [pltpu.SemaphoreType.DMA((1,))]
+    return call(kernel, [value] + after, [shape(*value.shape)], scratch, "relayed")[0]
 
 
 def attention_grads(bias, kv, kv_earlier, qg, split, after):
@@ -312,27 +320,30 @@
         kv_parts.append((own, paired, 0))
         qg_parts.append((own, paired, 2))
     count = len(spans)
-    kv_sends, qg_sends, kv, qg, kv_own, own_earlier = [], [], [], [], [], []
-    for index in range(count):
-        kv_sends.append(head_parts(*kv_parts[index], others, kv[index - 1] if index else []))
-        kv.append([round_sub(value, by) for by, value in zip(others, kv_sends[index])])
-        kv_own.append(head_parts(*kv_parts[index], [0], own_earlier[index - 1:index]))
-        own_earlier.append(along_blocks(kv_own[index][0], 1, True))
-        qg_sends.append(head_parts(*qg_parts[index], others, qg[index - 1] if index else []))
-        qg.append([round_sub(value, by) for by, value in zip(others, qg_sends[index])])
-    kept, paired = [], []
+    kv, qg, kept, paired = [], [], [], []
+    kv_turn, own_turn, far_turn = [], [], []
     for index in range(count):
         last = index == count - 1
-        earlier = [own_earlier[index]] + [along_blocks(value, 1, not last) for value in kv[index]]
-        qg_all = head_parts(*qg_parts[index], [0], []) + qg[index]
-        grads, dq, early = attention_grads(bias, kv_own[index] + kv[index], earlier, qg_all, last, [])
+        sends = head_parts(*kv_parts[index], others, kv_turn)
+        kv = [round_sub(value, by) for by, value in zip(others, sends)]
+        kv_own = head_parts(*kv_parts[index], [0], own_turn)
+        own_earlier = along_blocks(kv_own[0], 1, True)
+        sends = head_parts(*qg_parts[index], others, sends if last else kv)
+        qg = [round_sub(value, by) for by, value in zip(others, sends)]
+        forward = [relayed(value, far_turn if index else [own_earlier]) for value in kv]
+        far_earlier = [along_blocks(value, 1, not last) for value in forward]
+        kv_turn, own_turn = qg, far_earlier
+        qg_all = head_parts(*qg_parts[index], [0], []) + qg
+        grads, dq, early = attention_grads(bias, kv_own + kv, [own_earlier] + far_earlier, qg_all, last, [])
+        far_turn = [dq[0]]
         dq = [dq[0]] + [round_sub(dq[by], by) for by in others]
-        later = [along_blocks(value, -1, False) for value in early]
         if last:
-            dkv = summed(grads, later[1:], others, dq[1:])
-            dkv = summed(grads, later[:1], [0], dkv[:1]) + [round_sub(value, by) for by, value in zip(others, dkv)]
+            later = [along_blocks(value, -1, False) for value in early[1:]]
+            dkv = summed(grads, later, others, dq[1:])
+            near = along_blocks(relayed(early[0], later), -1, False)
+            dkv = summed(grads, [near], [0], []) + [round_sub(value, by) for by, value in zip(others, dkv)]
         else:
-            dkv = summed(grads, later, [0] + others, dq[1:])
+            dkv = summed(grads, [along_blocks(early[0], -1, False)], [0] + others, dq[1:])
             dkv = [dkv[0]] + [round_sub(dkv[by], by) for by in others]
         send, keep = rows_for_pair(dq, dkv)
         kept.append(keep)

time: 65.8 us -> 67.2 us (1.021)
  waiting for transfers between devices: 25.3 us -> 29.8 us
  starting transfers between devices: 25.3 us -> 21.8 us
    ppermute x7, starting transfers between devices: 12.6 us -> 8.38 us  [along_blocks(): return lax.ppermute(value, 'blk', pairs)]
    ppermute x8, waiting for transfers between devices: 13.2 us -> 17.1 us  [round_sub(): lax.ppermute(value, 'sub', [(i, (i + by) % peers) for i in range(peers)])]
    ppermute x8, starting transfers between devices: 11.4 us -> 12.2 us  [round_sub(): lax.ppermute(value, 'sub', [(i, (i + by) % peers) for i in range(peers)])]
    pallas_call x16 -> x19, Pallas kernels: 10.3 us -> 10.3 us  [call(): pl.pallas_call(kernel, out_shape=outs, in_specs=[spec] * len(ins), out_sp...]
  transfers between devices with their start and end apart: 20 -> 20, of which waited for: 8 -> 12; matrix products, arithmetic and copies ran while one was open for 1% -> 1% of each run, Pallas kernels for 16% -> 16%
where the time goes in v8:
time: 67.2 us; the launch traced here: 66.5 us
  waiting for transfers between devices  29.8 us (44%)
  starting transfers between devices  21.8 us (32%)
  Pallas kernels  13.1 us (19%)
  between operations  0.92 us (1%)
  other arithmetic  0.79 us (1%)
    ppermute x8, waiting for transfers between devices, round_sub(): lax.ppermute(value, 'sub', [(i, (i + by) % peers) for i in range(peers)])  17.1 us
    ppermute x8, starting transfers between devices, round_sub(): lax.ppermute(value, 'sub', [(i, (i + by) % peers) for i in range(peers)])  12.2 us
    ppermute x7, waiting for transfers between devices, along_blocks(): return lax.ppermute(value, 'blk', pairs)  10.9 us
    pallas_call x19, Pallas kernels, call(): pl.pallas_call(kernel, out_shape=outs, in_specs=[spec] * len(ins), out_sp...  10.3 us
    ppermute x7, starting transfers between devices, along_blocks(): return lax.ppermute(value, 'blk', pairs)  8.38 us
    pallas_call x2, Pallas kernels, first_parts(): pl.pallas_call(kernel, out_shape=outs, in_specs=[spec] * (len(held) + len...  2.78 us
    ppermute x5, waiting for transfers between devices, swapped(): return lax.ppermute(value, 'pair', [(0, 1), (1, 0)])  1.71 us
  transfers between devices with their start and end apart: 20, of which 12 were waited for; matrix products, arithmetic and copies ran while one was open for 1% of the time, Pallas kernels for 16%

profile of v8, /device:TPU:0, one launch (start us, length us, event | category | flops | bytes accessed | tf_op | source)
XLA Modules:
  0.0 66.5 jit_solution(6140018583350673426)
XLA Ops:
  0.6 1.1 %first_parts.2 = (bf16[2,2,128,256]{3,2,1,0:T(8,128)(2,1)S(1)}, bf16[2,2,128,256]{3,2,1,0:T(8,128)(2,1)S(1)}) custom-call(bf16[128,2048]{1,0:T(8,128)(2,1)} %refs_2_.1, bf16[128,2048]{1,0:T(8,128)(2,1)} %refs_3_.1), custom_call_target="tpu_custom_call" | custom-call | tf_op jit(solution)/shard_map/first_parts/pallas_call | solution.py:92
  1.8 0.5 collective-permute-start
  2.3 1.6 %first_parts.3 = (bf16[2,2,128,256]{3,2,1,0:T(8,128)(2,1)S(1)}, bf16[2,2,128,256]{3,2,1,0:T(8,128)(2,1)S(1)}, bf16[4,2,128,256]{3,2,1,0:T(8,128)(2,1)S(1)}, bf16[4,2,128,256]{3,2,1,0:T(8,128)(2,1)S(1)}) custom-call(bf16[128,2048]{1,0:T(8,128)(2,1)} %refs_4_.1, bf16[128,2048]{1,0:T(8,128)(2,1)} %refs_5_.1, bf16[128,2048]{1,0:T(8,128)(2,1)} %refs_2_.1, ...), custom_call_target="tpu_custom_call" | custom-call | tf_op jit(solution)/shard_map/first_parts/pallas_call | solution.py:92
  3.9 0.1 collective-permute-start.4
  4.1 0.5 collective-permute-start.9
  4.5 0.2 head_parts.9
  4.8 2.6 %collective-permute-start.1 = (bf16[2,2,128,256]{3,2,1,0:T(8,128)(2,1)S(1)}, bf16[2,2,128,256]{3,2,1,0:T(8,128)(2,1)S(1)}, u32[]{:S(2)}, u32[]{:S(2)}) collective-permute-start(bf16[2,2,128,256]{3,2,1,0:T(8,128)(2,1)S(1)} %head_parts.9), channel_id=1, source_target_pairs={{0,2},{2,0},{1,3},{3,1},{4,6},{6,4},{5,7},{7,5},{8,10},{10,8},{9,1... | collective-permute-start | bytes 786440 | tf_op jit(solution)/shard_map/ppermute | solution.py:32
  7.4 0.1 pad_dynamic-slice_fusion
  7.5 0.2 head_parts.8.refs_1_
  7.7 1.6 %collective-permute-start.2 = (bf16[2,2,128,256]{3,2,1,0:T(8,128)(2,1)S(1)}, bf16[2,2,128,256]{3,2,1,0:T(8,128)(2,1)S(1)}, u32[]{:S(2)}, u32[]{:S(2)}) collective-permute-start(bf16[2,2,128,256]{3,2,1,0:T(8,128)(2,1)S(1)} %head_parts.8.refs_1_), channel_id=1, source_target_pairs={{0,4},{4,8},{8,12},{12,0},{1,5},{5,9},{9,13},{13,1},{2,6},{6,10},{... | collective-permute-start | bytes 786440 | tf_op jit(solution)/shard_map/ppermute | solution.py:27
  9.3 5.0 %collective-permute-done.1.value_ref.refs_0_.refs_2_ = bf16[2,2,128,256]{3,2,1,0:T(8,128)(2,1)S(1)} collective-permute-done((bf16[2,2,128,256]{3,2,1,0:T(8,128)(2,1)S(1)}, bf16[2,2,128,256]{3,2,1,0:T(8,128)(2,1)S(1)}, u32[]{:S(2)}, u32[]{:S(2)}) %collective-permute-start.1) | collective-permute-done | bytes 262176 | tf_op jit(solution)/shard_map/ppermute | solution.py:32
  14.3 0.2 head_parts.11
  14.5 1.8 %collective-permute-start.5 = (bf16[2,2,128,256]{3,2,1,0:T(8,128)(2,1)S(1)}, bf16[2,2,128,256]{3,2,1,0:T(8,128)(2,1)S(1)}, u32[]{:S(2)}, u32[]{:S(2)}) collective-permute-start(bf16[2,2,128,256]{3,2,1,0:T(8,128)(2,1)S(1)} %head_parts.11), channel_id=1, source_target_pairs={{0,2},{2,0},{1,3},{3,1},{4,6},{6,4},{5,7},{7,5},{8,10},{10,8},{9,1... | collective-permute-start | bytes 786440 | tf_op jit(solution)/shard_map/ppermute | solution.py:32
  16.3 1.7 %collective-permute-done.2.refs_0_.refs_3_ = bf16[2,2,128,256]{3,2,1,0:T(8,128)(2,1)S(1)} collective-permute-done((bf16[2,2,128,256]{3,2,1,0:T(8,128)(2,1)S(1)}, bf16[2,2,128,256]{3,2,1,0:T(8,128)(2,1)S(1)}, u32[]{:S(2)}, u32[]{:S(2)}) %collective-permute-start.2) | collective-permute-done | bytes 262176 | tf_op jit(solution)/shard_map/ppermute | solution.py:27
  18.0 0.1 collective-permute-start.3
  18.1 4.5 %collective-permute-done.5.refs_6_.refs_0_ = bf16[2,2,128,256]{3,2,1,0:T(8,128)(2,1)S(1)} collective-permute-done((bf16[2,2,128,256]{3,2,1,0:T(8,128)(2,1)S(1)}, bf16[2,2,128,256]{3,2,1,0:T(8,128)(2,1)S(1)}, u32[]{:S(2)}, u32[]{:S(2)}) %collective-permute-start.5) | collective-permute-done | bytes 262176 | tf_op jit(solution)/shard_map/ppermute | solution.py:32
  22.6 0.2 head_parts.13.refs_0_
  22.8 1.6 %collective-permute-start.10 = (bf16[2,2,128,256]{3,2,1,0:T(8,128)(2,1)S(1)}, bf16[2,2,128,256]{3,2,1,0:T(8,128)(2,1)S(1)}, u32[]{:S(2)}, u32[]{:S(2)}) collective-permute-start(bf16[2,2,128,256]{3,2,1,0:T(8,128)(2,1)S(1)} %head_parts.13.refs_0_), channel_id=1, source_target_pairs={{0,2},{2,0},{1,3},{3,1},{4,6},{6,4},{5,7},{7,5},{8,10},{10,8},{9,1... | collective-permute-start | bytes 786440 | tf_op jit(solution)/shard_map/ppermute | solution.py:32
  24.4 0.7 %and_select_fusion = (f32[1,768,256]{2,1,0:T(8,128)S(1)}, f32[1,768,256]{2,1,0:T(8,128)S(1)}) fusion(s32[256]{0:T(256)S(1)} %get-tuple-element.54, s32[256]{0:T(256)S(1)} %get-tuple-element.52, s32[768]{0:T(1024)S(1)} %get-tuple-element.50, s32[768]{0:T(1024)S(1)} %get-tuple-element.48, pred[768]{0:T(1024)(128)(4,1)S(1)} %get-tuple-element.46, ...), kind=kLoop, calls=%fused_computation.1 | loop fusion | flops 1966080 | bytes 1590784 | tf_op jit(solution)/shard_map/jit(_where)/select_n | solution.py:299
  25.1 0.1 pad_maximum_fusion.refs_0_
  25.2 0.2 head_parts.10.refs_5_
  25.4 2.1 %collective-permute-done.3.refs_4_.refs_0_ = bf16[2,2,128,256]{3,2,1,0:T(8,128)(2,1)S(1)} collective-permute-done((bf16[2,2,128,256]{3,2,1,0:T(8,128)(2,1)S(1)}, bf16[2,2,128,256]{3,2,1,0:T(8,128)(2,1)S(1)}, u32[]{:S(2)}, u32[]{:S(2)}) %collective-permute-start.3) | collective-permute-done | bytes 262176 | tf_op jit(solution)/shard_map/ppermute | solution.py:27
  27.5 0.2 head_parts.12.refs_1_
  27.7 0.2 head_parts.15
  27.9 0.8 %collective-permute-start.13 = (bf16[2,2,128,256]{3,2,1,0:T(8,128)(2,1)S(1)}, bf16[2,2,128,256]{3,2,1,0:T(8,128)(2,1)S(1)}, u32[]{:S(2)}, u32[]{:S(2)}) collective-permute-start(bf16[2,2,128,256]{3,2,1,0:T(8,128)(2,1)S(1)} %head_parts.15), channel_id=1, source_target_pairs={{0,2},{2,0},{1,3},{3,1},{4,6},{6,4},{5,7},{7,5},{8,10},{10,8},{9,1... | collective-permute-start | bytes 786440 | tf_op jit(solution)/shard_map/ppermute | solution.py:32
  28.8 3.5 %attention_grads.2 = (f32[2,2,2,128,256]{4,3,2,1,0:T(8,128)S(1)}, bf16[2,128,256]{2,1,0:T(8,128)(2,1)S(1)}, bf16[2,128,256]{2,1,0:T(8,128)(2,1)S(1)}, bf16[2,2,2,128,256]{4,3,2,1,0:T(8,128)(2,1)S(1)}) custom-call(f32[2,768,256]{2,1,0:T(8,128)S(1)} %pad_maximum_fusion.refs_0_, bf16[2,2,128,256]{3,2,1,0:T(8,128)(2,1)S(1)} %head_parts.8.refs_1_, ...), custom_call_target="tpu_custom_call" | custom-call | flops 1006632960 | bytes 4980736 | tf_op jit(solution)/shard_map/attention_grads/pallas_call | solution.py:51
  32.4 2.8 %collective-permute-start.12 = (bf16[2,2,128,256]{3,2,1,0:T(8,128)(2,1)S(1)}, bf16[2,2,128,256]{3,2,1,0:T(8,128)(2,1)S(1)}, u32[]{:S(2)}, u32[]{:S(2)}) collective-permute-start(bf16[2,2,128,256]{3,2,1,0:T(8,128)(2,1)S(1)} %relayed.4), channel_id=1, source_target_pairs={{0,4},{4,8},{8,12},{1,5},{5,9},{9,13},{2,6},{6,10},{10,14},{3,7},{... | collective-permute-start | bytes 786440 | tf_op jit(solution)/shard_map/ppermute | solution.py:27
  35.1 1.3 %collective-permute-start.7 = (bf16[2,2,2,128,256]{4,3,2,1,0:T(8,128)(2,1)S(1)}, bf16[2,2,2,128,256]{4,3,2,1,0:T(8,128)(2,1)S(1)}, u32[]{:S(2)}, u32[]{:S(2)}) collective-permute-start(bf16[2,2,2,128,256]{4,3,2,1,0:T(8,128)(2,1)S(1)} %get-tuple-element.31), channel_id=1, source_target_pairs={{4,0},{8,4},{12,8},{5,1},{9,5},{13,9},{6,2},{10,6},{14,10},{7,3},{... | collective-permute-start | bytes 1572872 | tf_op jit(solution)/shard_map/ppermute | solution.py:27
  36.4 0.2 head_parts.14.refs_5_
  36.7 2.3 %collective-permute-done.12.refs_4_ = bf16[2,2,128,256]{3,2,1,0:T(8,128)(2,1)S(1)} collective-permute-done((bf16[2,2,128,256]{3,2,1,0:T(8,128)(2,1)S(1)}, bf16[2,2,128,256]{3,2,1,0:T(8,128)(2,1)S(1)}, u32[]{:S(2)}, u32[]{:S(2)}) %collective-permute-start.12) | collective-permute-done | bytes 262176 | tf_op jit(solution)/shard_map/ppermute | solution.py:27
  39.0 3.5 %attention_grads.3 = (f32[2,2,2,128,256]{4,3,2,1,0:T(8,128)S(1)}, bf16[2,128,256]{2,1,0:T(8,128)(2,1)S(1)}, bf16[2,128,256]{2,1,0:T(8,128)(2,1)S(1)}, bf16[2,2,1...) custom-call(f32[2,768,256]{2,1,0:T(8,128)S(1)} %pad_maximum_fusion.refs_0_, ...), custom_call_target="tpu_custom_call" | custom-call | flops 1006632960 | bytes 4980736 | tf_op jit(solution)/shard_map/attention_grads/pallas_call | solution.py:51
  42.5 1.3 %collective-permute-start.15 = (bf16[2,2,128,256]{3,2,1,0:T(8,128)(2,1)S(1)}, bf16[2,2,128,256]{3,2,1,0:T(8,128)(2,1)S(1)}, u32[]{:S(2)}, u32[]{:S(2)}) collective-permute-start(bf16[2,2,128,256]{3,2,1,0:T(8,128)(2,1)S(1)} %get-tuple-element.41), channel_id=1, source_target_pairs={{4,0},{8,4},{12,8},{5,1},{9,5},{13,9},{6,2},{10,6},{14,10},{7,3},{... | collective-permute-start | bytes 786440 | tf_op jit(solution)/shard_map/ppermute | solution.py:27
  43.8 2.1 %collective-permute-start.6 = (bf16[2,128,256]{2,1,0:T(8,128)(2,1)S(1)}, bf16[2,128,256]{2,1,0:T(8,128)(2,1)S(1)}, u32[]{:S(2)}, u32[]{:S(2)}) collective-permute-start(bf16[2,128,256]{2,1,0:T(8,128)(2,1)S(1)} %get-tuple-element.29), channel_id=1, source_target_pairs={{0,2},{2,0},{1,3},{3,1},{4,6},{6,4},{5,7},{7,5},{8,10},{10,8},{9,1... | collective-permute-start | bytes 393224 | tf_op jit(solution)/shard_map/ppermute | solution.py:32
  46.0 0.1 collective-permute-start.14
  46.0 3.9 %collective-permute-done.6.refs_1_ = bf16[2,128,256]{2,1,0:T(8,128)(2,1)S(1)} collective-permute-done((bf16[2,128,256]{2,1,0:T(8,128)(2,1)S(1)}, bf16[2,128,256]{2,1,0:T(8,128)(2,1)S(1)}, u32[]{:S(2)}, u32[]{:S(2)}) %collective-permute-start.6) | collective-permute-done | bytes 131104 | tf_op jit(solution)/shard_map/ppermute | solution.py:32
  49.9 1.4 %collective-permute-done.7.refs_0_ = bf16[2,2,2,128,256]{4,3,2,1,0:T(8,128)(2,1)S(1)} collective-permute-done((bf16[2,2,2,128,256]{4,3,2,1,0:T(8,128)(2,1)S(1)}, bf16[2,2,2,128,256]{4,3,2,1,0:T(8,128)(2,1)S(1)}, u32[]{:S(2)}, u32[]{:S(2)}) %collective-permute-start.7) | collective-permute-done | bytes 524320 | tf_op jit(solution)/shard_map/ppermute | solution.py:27
  51.3 0.1 summed.3
  51.4 1.6 %collective-permute-start.8 = (bf16[2,2,128,256]{3,2,1,0:T(8,128)(2,1)S(1)}, bf16[2,2,128,256]{3,2,1,0:T(8,128)(2,1)S(1)}, u32[]{:S(2)}, u32[]{:S(2)}) collective-permute-start(bf16[2,2,128,256]{3,2,1,0:T(8,128)(2,1)S(1)} %get-tuple-element.33), channel_id=1, source_target_pairs={{0,2},{2,0},{1,3},{3,1},{4,6},{6,4},{5,7},{7,5},{8,10},{10,8},{9,1... | collective-permute-start | bytes 786440 | tf_op jit(solution)/shard_map/ppermute | solution.py:32
  53.0 1.2 %collective-permute-done.15.refs_0_ = bf16[2,2,128,256]{3,2,1,0:T(8,128)(2,1)S(1)} collective-permute-done((bf16[2,2,128,256]{3,2,1,0:T(8,128)(2,1)S(1)}, bf16[2,2,128,256]{3,2,1,0:T(8,128)(2,1)S(1)}, u32[]{:S(2)}, u32[]{:S(2)}) %collective-permute-start.15) | collective-permute-done | bytes 262176 | tf_op jit(solution)/shard_map/ppermute | solution.py:27
  54.2 1.3 %collective-permute-start.16 = (bf16[2,2,128,256]{3,2,1,0:T(8,128)(2,1)S(1)}, bf16[2,2,128,256]{3,2,1,0:T(8,128)(2,1)S(1)}, u32[]{:S(2)}, u32[]{:S(2)}) collective-permute-start(bf16[2,2,128,256]{3,2,1,0:T(8,128)(2,1)S(1)} %relayed.5), channel_id=1, source_target_pairs={{4,0},{8,4},{12,8},{5,1},{9,5},{13,9},{6,2},{10,6},{14,10},{7,3},{... | collective-permute-start | bytes 786440 | tf_op jit(solution)/shard_map/ppermute | solution.py:27
  55.5 1.6 %collective-permute-start.17 = (bf16[2,2,128,256]{3,2,1,0:T(8,128)(2,1)S(1)}, bf16[2,2,128,256]{3,2,1,0:T(8,128)(2,1)S(1)}, u32[]{:S(2)}, u32[]{:S(2)}) collective-permute-start(bf16[2,2,128,256]{3,2,1,0:T(8,128)(2,1)S(1)} %summed.5), channel_id=1, source_target_pairs={{0,2},{2,0},{1,3},{3,1},{4,6},{6,4},{5,7},{7,5},{8,10},{10,8},{9,1... | collective-permute-start | bytes 786440 | tf_op jit(solution)/shard_map/ppermute | solution.py:32
  57.1 3.4 %collective-permute-done.8.refs_3_ = bf16[2,2,128,256]{3,2,1,0:T(8,128)(2,1)S(1)} collective-permute-done((bf16[2,2,128,256]{3,2,1,0:T(8,128)(2,1)S(1)}, bf16[2,2,128,256]{3,2,1,0:T(8,128)(2,1)S(1)}, u32[]{:S(2)}, u32[]{:S(2)}) %collective-permute-start.8) | collective-permute-done | bytes 262176 | tf_op jit(solution)/shard_map/ppermute | solution.py:32
  60.6 0.1 collective-permute-start.18
  60.7 2.3 %collective-permute-done.16.refs_0_ = bf16[2,2,128,256]{3,2,1,0:T(8,128)(2,1)S(1)} collective-permute-done((bf16[2,2,128,256]{3,2,1,0:T(8,128)(2,1)S(1)}, bf16[2,2,128,256]{3,2,1,0:T(8,128)(2,1)S(1)}, u32[]{:S(2)}, u32[]{:S(2)}) %collective-permute-start.16) | collective-permute-done | bytes 262176 | tf_op jit(solution)/shard_map/ppermute | solution.py:27
  63.1 0.3 collective-permute-done.17.refs_3_
  63.4 0.1 collective-permute-start.19
  63.5 1.7 %collective-permute-done.19.refs_3_ = bf16[3,2,128,256]{3,2,1,0:T(8,128)(2,1)S(1)} collective-permute-done((bf16[3,2,128,256]{3,2,1,0:T(8,128)(2,1)S(1)}, bf16[3,2,128,256]{3,2,1,0:T(8,128)(2,1)S(1)}, u32[]{:S(2)}, u32[]{:S(2)}) %collective-permute-start.19) | collective-permute-done | bytes 393248 | tf_op jit(solution)/shard_map/ppermute | solution.py:36
  65.2 1.3 %laid_out.1 = (bf16[128,2048]{1,0:T(8,128)(2,1)}, bf16[128,2048]{1,0:T(8,128)(2,1)}, bf16[128,2048]{1,0:T(8,128)(2,1)}) custom-call(bf16[3,2,128,256]{3,2,1,0:T(8,128)(2,1)S(1)} %get-tuple-element.34.refs_0_, bf16[3,2,128,256]{3,2,1,0:T(8,128)(2,1)S(1)} %get-tuple-element.42.refs_1_, bf16[3,2,128,256]{3,2,1,0:T(8,128)(2,1)S(1)} %collective-permute-done.18.refs_2_, ...), custom_call_target="tpu_custom_call" | custom-call | bytes 3145728 | tf_op jit(solution)/shard_map/laid_out/pallas_call | solution.py:51
  (24 shorter events, 0.4 us)
Async XLA Ops:
  1.8 2.8 %collective-permute-start = (bf16[2,2,128,256]{3,2,1,0:T(8,128)(2,1)S(1)}, bf16[2,2,128,256]{3,2,1,0:T(8,128)(2,1)S(1)}, u32[]{:S(2)}, u32[]{:S(2)}) collective-permute-start(bf16[2,2,128,256]{3,2,1,0:T(8,128)(2,1)S(1)} %get-tuple-element.25), channel_id=1, source_target_pairs={{0,1},{1,0},{2,3},{3,2},{4,5},{5,4},{6,7},{7,6},{8,9},{9,8},{10,11... | collective-permute-start | bytes 786440 | tf_op jit(solution)/shard_map/ppermute | solution.py:36
  2.3 5.1 %copy-start = (s32[2048]{0:T(1024)S(1)}, s32[2048]{0:T(1024)}, u32[]{:S(2)}) copy-start(s32[2048]{0:T(1024)} %param.9) | copy-start | bytes 24580
  3.9 5.3 %collective-permute-start.4 = (bf16[2,2,128,256]{3,2,1,0:T(8,128)(2,1)S(1)}, bf16[2,2,128,256]{3,2,1,0:T(8,128)(2,1)S(1)}, u32[]{:S(2)}, u32[]{:S(2)}) collective-permute-start(bf16[2,2,128,256]{3,2,1,0:T(8,128)(2,1)S(1)} %get-tuple-element.27), channel_id=1, source_target_pairs={{0,1},{1,0},{2,3},{3,2},{4,5},{5,4},{6,7},{7,6},{8,9},{9,8},{10,11... | collective-permute-start | bytes 786440 | tf_op jit(solution)/shard_map/ppermute | solution.py:36
  4.1 14.0 %collective-permute-start.9 = (bf16[4,2,128,256]{3,2,1,0:T(8,128)(2,1)S(1)}, bf16[4,2,128,256]{3,2,1,0:T(8,128)(2,1)S(1)}, u32[]{:S(2)}, u32[]{:S(2)}) collective-permute-start(bf16[4,2,128,256]{3,2,1,0:T(8,128)(2,1)S(1)} %get-tuple-element.36), channel_id=1, source_target_pairs={{0,1},{1,0},{2,3},{3,2},{4,5},{5,4},{6,7},{7,6},{8,9},{9,8},{10,11... | collective-permute-start | bytes 1572872 | tf_op jit(solution)/shard_map/ppermute | solution.py:36
  4.8 9.5 %collective-permute-start.1 = (bf16[2,2,128,256]{3,2,1,0:T(8,128)(2,1)S(1)}, bf16[2,2,128,256]{3,2,1,0:T(8,128)(2,1)S(1)}, u32[]{:S(2)}, u32[]{:S(2)}) collective-permute-start(bf16[2,2,128,256]{3,2,1,0:T(8,128)(2,1)S(1)} %head_parts.9), channel_id=1, source_target_pairs={{0,2},{2,0},{1,3},{3,1},{4,6},{6,4},{5,7},{7,5},{8,10},{10,8},{9,1... | collective-permute-start | bytes 786440 | tf_op jit(solution)/shard_map/ppermute | solution.py:32
  7.7 10.3 %collective-permute-start.2 = (bf16[2,2,128,256]{3,2,1,0:T(8,128)(2,1)S(1)}, bf16[2,2,128,256]{3,2,1,0:T(8,128)(2,1)S(1)}, u32[]{:S(2)}, u32[]{:S(2)}) collective-permute-start(bf16[2,2,128,256]{3,2,1,0:T(8,128)(2,1)S(1)} %head_parts.8.refs_1_), channel_id=1, source_target_pairs={{0,4},{4,8},{8,12},{12,0},{1,5},{5,9},{9,13},{13,1},{2,6},{6,10},{... | collective-permute-start | bytes 786440 | tf_op jit(solution)/shard_map/ppermute | solution.py:27
  14.5 8.1 %collective-permute-start.5 = (bf16[2,2,128,256]{3,2,1,0:T(8,128)(2,1)S(1)}, bf16[2,2,128,256]{3,2,1,0:T(8,128)(2,1)S(1)}, u32[]{:S(2)}, u32[]{:S(2)}) collective-permute-start(bf16[2,2,128,256]{3,2,1,0:T(8,128)(2,1)S(1)} %head_parts.11), channel_id=1, source_target_pairs={{0,2},{2,0},{1,3},{3,1},{4,6},{6,4},{5,7},{7,5},{8,10},{10,8},{9,1... | collective-permute-start | bytes 786440 | tf_op jit(solution)/shard_map/ppermute | solution.py:32
  18.0 9.5 %collective-permute-start.3 = (bf16[2,2,128,256]{3,2,1,0:T(8,128)(2,1)S(1)}, bf16[2,2,128,256]{3,2,1,0:T(8,128)(2,1)S(1)}, u32[]{:S(2)}, u32[]{:S(2)}) collective-permute-start(bf16[2,2,128,256]{3,2,1,0:T(8,128)(2,1)S(1)} %relayed.3), channel_id=1, source_target_pairs={{0,4},{4,8},{8,12},{12,0},{1,5},{5,9},{9,13},{13,1},{2,6},{6,10},{... | collective-permute-start | bytes 786440 | tf_op jit(solution)/shard_map/ppermute | solution.py:27
  22.8 9.5 %collective-permute-start.10 = (bf16[2,2,128,256]{3,2,1,0:T(8,128)(2,1)S(1)}, bf16[2,2,128,256]{3,2,1,0:T(8,128)(2,1)S(1)}, u32[]{:S(2)}, u32[]{:S(2)}) collective-permute-start(bf16[2,2,128,256]{3,2,1,0:T(8,128)(2,1)S(1)} %head_parts.13.refs_0_), channel_id=1, source_target_pairs={{0,2},{2,0},{1,3},{3,1},{4,6},{6,4},{5,7},{7,5},{8,10},{10,8},{9,1... | collective-permute-start | bytes 786440 | tf_op jit(solution)/shard_map/ppermute | solution.py:32
  27.6 9.0 %collective-permute-start.11 = (bf16[2,2,128,256]{3,2,1,0:T(8,128)(2,1)S(1)}, bf16[2,2,128,256]{3,2,1,0:T(8,128)(2,1)S(1)}, u32[]{:S(2)}, u32[]{:S(2)}) collective-permute-start(bf16[2,2,128,256]{3,2,1,0:T(8,128)(2,1)S(1)} %head_parts.12.refs_1_), channel_id=1, source_target_pairs={{0,4},{4,8},{8,12},{12,0},{1,5},{5,9},{9,13},{13,1},{2,6},{6,10},{... | collective-permute-start | bytes 786440 | tf_op jit(solution)/shard_map/ppermute | solution.py:27
  27.9 8.7 %collective-permute-start.13 = (bf16[2,2,128,256]{3,2,1,0:T(8,128)(2,1)S(1)}, bf16[2,2,128,256]{3,2,1,0:T(8,128)(2,1)S(1)}, u32[]{:S(2)}, u32[]{:S(2)}) collective-permute-start(bf16[2,2,128,256]{3,2,1,0:T(8,128)(2,1)S(1)} %head_parts.15), channel_id=1, source_target_pairs={{0,2},{2,0},{1,3},{3,1},{4,6},{6,4},{5,7},{7,5},{8,10},{10,8},{9,1... | collective-permute-start | bytes 786440 | tf_op jit(solution)/shard_map/ppermute | solution.py:32
  32.4 6.6 %collective-permute-start.12 = (bf16[2,2,128,256]{3,2,1,0:T(8,128)(2,1)S(1)}, bf16[2,2,128,256]{3,2,1,0:T(8,128)(2,1)S(1)}, u32[]{:S(2)}, u32[]{:S(2)}) collective-permute-start(bf16[2,2,128,256]{3,2,1,0:T(8,128)(2,1)S(1)} %relayed.4), channel_id=1, source_target_pairs={{0,4},{4,8},{8,12},{1,5},{5,9},{9,13},{2,6},{6,10},{10,14},{3,7},{... | collective-permute-start | bytes 786440 | tf_op jit(solution)/shard_map/ppermute | solution.py:27
  35.1 16.2 %collective-permute-start.7 = (bf16[2,2,2,128,256]{4,3,2,1,0:T(8,128)(2,1)S(1)}, bf16[2,2,2,128,256]{4,3,2,1,0:T(8,128)(2,1)S(1)}, u32[]{:S(2)}, u32[]{:S(2)}) collective-permute-start(bf16[2,2,2,128,256]{4,3,2,1,0:T(8,128)(2,1)S(1)} %get-tuple-element.31), channel_id=1, source_target_pairs={{4,0},{8,4},{12,8},{5,1},{9,5},{13,9},{6,2},{10,6},{14,10},{7,3},{... | collective-permute-start | bytes 1572872 | tf_op jit(solution)/shard_map/ppermute | solution.py:27
  42.5 11.6 %collective-permute-start.15 = (bf16[2,2,128,256]{3,2,1,0:T(8,128)(2,1)S(1)}, bf16[2,2,128,256]{3,2,1,0:T(8,128)(2,1)S(1)}, u32[]{:S(2)}, u32[]{:S(2)}) collective-permute-start(bf16[2,2,128,256]{3,2,1,0:T(8,128)(2,1)S(1)} %get-tuple-element.41), channel_id=1, source_target_pairs={{4,0},{8,4},{12,8},{5,1},{9,5},{13,9},{6,2},{10,6},{14,10},{7,3},{... | collective-permute-start | bytes 786440 | tf_op jit(solution)/shard_map/ppermute | solution.py:27
  43.8 6.1 %collective-permute-start.6 = (bf16[2,128,256]{2,1,0:T(8,128)(2,1)S(1)}, bf16[2,128,256]{2,1,0:T(8,128)(2,1)S(1)}, u32[]{:S(2)}, u32[]{:S(2)}) collective-permute-start(bf16[2,128,256]{2,1,0:T(8,128)(2,1)S(1)} %get-tuple-element.29), channel_id=1, source_target_pairs={{0,2},{2,0},{1,3},{3,1},{4,6},{6,4},{5,7},{7,5},{8,10},{10,8},{9,1... | collective-permute-start | bytes 393224 | tf_op jit(solution)/shard_map/ppermute | solution.py:32
  46.0 9.5 %collective-permute-start.14 = (bf16[2,128,256]{2,1,0:T(8,128)(2,1)S(1)}, bf16[2,128,256]{2,1,0:T(8,128)(2,1)S(1)}, u32[]{:S(2)}, u32[]{:S(2)}) collective-permute-start(bf16[2,128,256]{2,1,0:T(8,128)(2,1)S(1)} %get-tuple-element.38), channel_id=1, source_target_pairs={{0,2},{2,0},{1,3},{3,1},{4,6},{6,4},{5,7},{7,5},{8,10},{10,8},{9,1... | collective-permute-start | bytes 393224 | tf_op jit(solution)/shard_map/ppermute | solution.py:32
  51.4 9.1 %collective-permute-start.8 = (bf16[2,2,128,256]{3,2,1,0:T(8,128)(2,1)S(1)}, bf16[2,2,128,256]{3,2,1,0:T(8,128)(2,1)S(1)}, u32[]{:S(2)}, u32[]{:S(2)}) collective-permute-start(bf16[2,2,128,256]{3,2,1,0:T(8,128)(2,1)S(1)} %get-tuple-element.33), channel_id=1, source_target_pairs={{0,2},{2,0},{1,3},{3,1},{4,6},{6,4},{5,7},{7,5},{8,10},{10,8},{9,1... | collective-permute-start | bytes 786440 | tf_op jit(solution)/shard_map/ppermute | solution.py:32
  54.2 8.8 %collective-permute-start.16 = (bf16[2,2,128,256]{3,2,1,0:T(8,128)(2,1)S(1)}, bf16[2,2,128,256]{3,2,1,0:T(8,128)(2,1)S(1)}, u32[]{:S(2)}, u32[]{:S(2)}) collective-permute-start(bf16[2,2,128,256]{3,2,1,0:T(8,128)(2,1)S(1)} %relayed.5), channel_id=1, source_target_pairs={{4,0},{8,4},{12,8},{5,1},{9,5},{13,9},{6,2},{10,6},{14,10},{7,3},{... | collective-permute-start | bytes 786440 | tf_op jit(solution)/shard_map/ppermute | solution.py:27
  55.5 7.8 %collective-permute-start.17 = (bf16[2,2,128,256]{3,2,1,0:T(8,128)(2,1)S(1)}, bf16[2,2,128,256]{3,2,1,0:T(8,128)(2,1)S(1)}, u32[]{:S(2)}, u32[]{:S(2)}) collective-permute-start(bf16[2,2,128,256]{3,2,1,0:T(8,128)(2,1)S(1)} %summed.5), channel_id=1, source_target_pairs={{0,2},{2,0},{1,3},{3,1},{4,6},{6,4},{5,7},{7,5},{8,10},{10,8},{9,1... | collective-permute-start | bytes 786440 | tf_op jit(solution)/shard_map/ppermute | solution.py:32
  60.6 2.9 %collective-permute-start.18 = (bf16[3,2,128,256]{3,2,1,0:T(8,128)(2,1)S(1)}, bf16[3,2,128,256]{3,2,1,0:T(8,128)(2,1)S(1)}, u32[]{:S(2)}, u32[]{:S(2)}) collective-permute-start(bf16[3,2,128,256]{3,2,1,0:T(8,128)(2,1)S(1)} %get-tuple-element.43), channel_id=1, source_target_pairs={{0,1},{1,0},{2,3},{3,2},{4,5},{5,4},{6,7},{7,6},{8,9},{9,8},{10,11... | collective-permute-start | bytes 1179656 | tf_op jit(solution)/shard_map/ppermute | solution.py:36
  63.4 1.8 %collective-permute-start.19 = (bf16[3,2,128,256]{3,2,1,0:T(8,128)(2,1)S(1)}, bf16[3,2,128,256]{3,2,1,0:T(8,128)(2,1)S(1)}, u32[]{:S(2)}, u32[]{:S(2)}) collective-permute-start(bf16[3,2,128,256]{3,2,1,0:T(8,128)(2,1)S(1)} %get-tuple-element.44), channel_id=1, source_target_pairs={{0,1},{1,0},{2,3},{3,2},{4,5},{5,4},{6,7},{7,6},{8,9},{9,8},{10,11... | collective-permute-start | bytes 1179656 | tf_op jit(solution)/shard_map/ppermute | solution.py:36

commit v9 on v6

--- a/solution.py
+++ b/solution.py
@@ -117,6 +117,14 @@
     outs = [shape(2, 2, rows, cut)] * len(turns)
     scratch = [pltpu.SemaphoreType.DMA((2 * len(turns),))]
     return call(kernel, [own, paired] + after, outs, scratch, "head_parts")
+
+
+def relayed(value, after):
+    def kernel(value_ref, *refs):
+        run_moves([(value_ref, refs[-2])], refs[-1])
+
+    scratch = [pltpu.SemaphoreType.DMA((1,))]
+    return call(kernel, [value] + after, [shape(*value.shape)], scratch, "relayed")[0]
 
 
 def attention_grads(bias, kv, kv_earlier, qg, split, after):
@@ -323,16 +331,19 @@
     kept, paired = [], []
     for index in range(count):
         last = index == count - 1
-        earlier = [own_earlier[index]] + [along_blocks(value, 1, not last) for value in kv[index]]
+        forward = [relayed(value, [first_dq]) if index else value for value in kv[index]]
+        earlier = [own_earlier[index]] + [along_blocks(value, 1, not last) for value in forward]
         qg_all = head_parts(*qg_parts[index], [0], []) + qg[index]
         grads, dq, early = attention_grads(bias, kv_own[index] + kv[index], earlier, qg_all, last, [])
+        first_dq = dq[0]
         dq = [dq[0]] + [round_sub(dq[by], by) for by in others]
-        later = [along_blocks(value, -1, False) for value in early]
         if last:
-            dkv = summed(grads, later[1:], others, dq[1:])
-            dkv = summed(grads, later[:1], [0], dkv[:1]) + [round_sub(value, by) for by, value in zip(others, dkv)]
+            later = [along_blocks(value, -1, False) for value in early[1:]]
+            dkv = summed(grads, later, others, dq[1:])
+            near = along_blocks(relayed(early[0], dkv), -1, False)
+            dkv = summed(grads, [near], [0], []) + [round_sub(value, by) for by, value in zip(others, dkv)]
         else:
-            dkv = summed(grads, later, [0] + others, dq[1:])
+            dkv = summed(grads, [along_blocks(early[0], -1, False)], [0] + others, dq[1:])
             dkv = [dkv[0]] + [round_sub(dkv[by], by) for by in others]
         send, keep = rows_for_pair(dq, dkv)
         kept.append(keep)

time: 65.8 us -> 62.4 us (0.948)
  starting transfers between devices: 25.3 us -> 22.3 us
    ppermute x7, starting transfers between devices: 12.6 us -> 10.4 us  [along_blocks(): return lax.ppermute(value, 'blk', pairs)]
    ppermute x8, waiting for transfers between devices: 13.2 us -> 12.3 us  [round_sub(): lax.ppermute(value, 'sub', [(i, (i + by) % peers) for i in range(peers)])]
    ppermute x8, starting transfers between devices: 11.4 us -> 10.6 us  [round_sub(): lax.ppermute(value, 'sub', [(i, (i + by) % peers) for i in range(peers)])]
    pallas_call x16 -> x18, Pallas kernels: 10.3 us -> 10.3 us  [call(): pl.pallas_call(kernel, out_shape=outs, in_specs=[spec] * len(ins), out_sp...]
  transfers between devices with their start and end apart: 20 -> 20, of which waited for: 8 -> 10; matrix products, arithmetic and copies ran while one was open for 1% -> 1% of each run, Pallas kernels for 16% -> 17%
where the time goes in v9:
time: 62.4 us; the launch traced here: 62 us
  waiting for transfers between devices  24.9 us (40%)
  starting transfers between devices  22.3 us (36%)
  Pallas kernels  13.1 us (21%)
  between operations  0.9 us (1%)
  other arithmetic  0.79 us (1%)
    ppermute x8, waiting for transfers between devices, round_sub(): lax.ppermute(value, 'sub', [(i, (i + by) % peers) for i in range(peers)])  12.3 us
    ppermute x7, waiting for transfers between devices, along_blocks(): return lax.ppermute(value, 'blk', pairs)  10.9 us
    ppermute x8, starting transfers between devices, round_sub(): lax.ppermute(value, 'sub', [(i, (i + by) % peers) for i in range(peers)])  10.6 us
    ppermute x7, starting transfers between devices, along_blocks(): return lax.ppermute(value, 'blk', pairs)  10.4 us
    pallas_call x18, Pallas kernels, call(): pl.pallas_call(kernel, out_shape=outs, in_specs=[spec] * len(ins), out_sp...  10.3 us
    pallas_call x2, Pallas kernels, first_parts(): pl.pallas_call(kernel, out_shape=outs, in_specs=[spec] * (len(held) + len...  2.78 us
    ppermute x5, waiting for transfers between devices, swapped(): return lax.ppermute(value, 'pair', [(0, 1), (1, 0)])  1.71 us
  transfers between devices with their start and end apart: 20, of which 10 were waited for; matrix products, arithmetic and copies ran while one was open for 1% of the time, Pallas kernels for 17%

profile of v9, /device:TPU:0, one launch (start us, length us, event | category | flops | bytes accessed | tf_op | source)
XLA Modules:
  0.0 62.0 jit_solution(2853982494151915075)
XLA Ops:
  0.6 1.1 %first_parts.2 = (bf16[2,2,128,256]{3,2,1,0:T(8,128)(2,1)S(1)}, bf16[2,2,128,256]{3,2,1,0:T(8,128)(2,1)S(1)}) custom-call(bf16[128,2048]{1,0:T(8,128)(2,1)} %refs_2_.1, bf16[128,2048]{1,0:T(8,128)(2,1)} %refs_3_.1), custom_call_target="tpu_custom_call" | custom-call | tf_op jit(solution)/shard_map/first_parts/pallas_call | solution.py:92
  1.8 0.5 collective-permute-start
  2.3 1.6 %first_parts.3 = (bf16[2,2,128,256]{3,2,1,0:T(8,128)(2,1)S(1)}, bf16[2,2,128,256]{3,2,1,0:T(8,128)(2,1)S(1)}, bf16[4,2,128,256]{3,2,1,0:T(8,128)(2,1)S(1)}, bf16[4,2,128,256]{3,2,1,0:T(8,128)(2,1)S(1)}) custom-call(bf16[128,2048]{1,0:T(8,128)(2,1)} %refs_4_.1, bf16[128,2048]{1,0:T(8,128)(2,1)} %refs_5_.1, bf16[128,2048]{1,0:T(8,128)(2,1)} %refs_2_.1, ...), custom_call_target="tpu_custom_call" | custom-call | tf_op jit(solution)/shard_map/first_parts/pallas_call | solution.py:92
  3.9 0.1 collective-permute-start.4
  4.1 0.5 collective-permute-start.9
  4.6 0.1 pad_dynamic-slice_fusion
  4.7 0.2 head_parts.9
  4.8 2.6 %collective-permute-start.1 = (bf16[2,2,128,256]{3,2,1,0:T(8,128)(2,1)S(1)}, bf16[2,2,128,256]{3,2,1,0:T(8,128)(2,1)S(1)}, u32[]{:S(2)}, u32[]{:S(2)}) collective-permute-start(bf16[2,2,128,256]{3,2,1,0:T(8,128)(2,1)S(1)} %head_parts.9), channel_id=1, source_target_pairs={{0,2},{2,0},{1,3},{3,1},{4,6},{6,4},{5,7},{7,5},{8,10},{10,8},{9,1... | collective-permute-start | bytes 786440 | tf_op jit(solution)/shard_map/ppermute | solution.py:32
  7.5 0.2 head_parts.8.refs_1_
  7.7 1.6 %collective-permute-start.2 = (bf16[2,2,128,256]{3,2,1,0:T(8,128)(2,1)S(1)}, bf16[2,2,128,256]{3,2,1,0:T(8,128)(2,1)S(1)}, u32[]{:S(2)}, u32[]{:S(2)}) collective-permute-start(bf16[2,2,128,256]{3,2,1,0:T(8,128)(2,1)S(1)} %head_parts.8.refs_1_), channel_id=1, source_target_pairs={{0,4},{4,8},{8,12},{12,0},{1,5},{5,9},{9,13},{13,1},{2,6},{6,10},{... | collective-permute-start | bytes 786440 | tf_op jit(solution)/shard_map/ppermute | solution.py:27
  9.3 0.2 head_parts.11
  9.5 0.6 collective-permute-start.5
  10.1 4.5 %collective-permute-done.1.refs_2_.refs_0_ = bf16[2,2,128,256]{3,2,1,0:T(8,128)(2,1)S(1)} collective-permute-done((bf16[2,2,128,256]{3,2,1,0:T(8,128)(2,1)S(1)}, bf16[2,2,128,256]{3,2,1,0:T(8,128)(2,1)S(1)}, u32[]{:S(2)}, u32[]{:S(2)}) %collective-permute-start.1) | collective-permute-done | bytes 262176 | tf_op jit(solution)/shard_map/ppermute | solution.py:32
  14.6 0.2 head_parts.13
  14.8 2.0 %collective-permute-start.10 = (bf16[2,2,128,256]{3,2,1,0:T(8,128)(2,1)S(1)}, bf16[2,2,128,256]{3,2,1,0:T(8,128)(2,1)S(1)}, u32[]{:S(2)}, u32[]{:S(2)}) collective-permute-start(bf16[2,2,128,256]{3,2,1,0:T(8,128)(2,1)S(1)} %head_parts.13), channel_id=1, source_target_pairs={{0,2},{2,0},{1,3},{3,1},{4,6},{6,4},{5,7},{7,5},{8,10},{10,8},{9,1... | collective-permute-start | bytes 786440 | tf_op jit(solution)/shard_map/ppermute | solution.py:32
  16.8 1.6 %collective-permute-start.3 = (bf16[2,2,128,256]{3,2,1,0:T(8,128)(2,1)S(1)}, bf16[2,2,128,256]{3,2,1,0:T(8,128)(2,1)S(1)}, u32[]{:S(2)}, u32[]{:S(2)}) collective-permute-start(bf16[2,2,128,256]{3,2,1,0:T(8,128)(2,1)S(1)} %collective-permute-done.1.refs_2_.refs_0_), channel_id=1, source_target_pairs={{0,4},{4,8},{8,12},{12,0},{1,5},{5,9},{9,13},{13,1},{2,6},{6,10},{... | collective-permute-start | bytes 786440 | tf_op jit(solution)/shard_map/ppermute | solution.py:27
  18.4 0.7 %and_select_fusion = (f32[1,768,256]{2,1,0:T(8,128)S(1)}, f32[1,768,256]{2,1,0:T(8,128)S(1)}) fusion(s32[256]{0:T(256)S(1)} %get-tuple-element.54, s32[256]{0:T(256)S(1)} %get-tuple-element.52, s32[768]{0:T(1024)S(1)} %get-tuple-element.50, s32[768]{0:T(1024)S(1)} %get-tuple-element.48, pred[768]{0:T(1024)(128)(4,1)S(1)} %get-tuple-element.46, ...), kind=kLoop, calls=%fused_computation.1 | loop fusion | flops 1966080 | bytes 1590784 | tf_op jit(solution)/shard_map/jit(_where)/select_n | solution.py:299
  19.1 0.1 pad_maximum_fusion.refs_0_
  19.2 0.2 head_parts.10.refs_5_
  19.4 0.2 head_parts.12.refs_1_
  19.6 1.6 %collective-permute-start.11 = (bf16[2,2,128,256]{3,2,1,0:T(8,128)(2,1)S(1)}, bf16[2,2,128,256]{3,2,1,0:T(8,128)(2,1)S(1)}, u32[]{:S(2)}, u32[]{:S(2)}) collective-permute-start(bf16[2,2,128,256]{3,2,1,0:T(8,128)(2,1)S(1)} %head_parts.12.refs_1_), channel_id=1, source_target_pairs={{0,4},{4,8},{8,12},{12,0},{1,5},{5,9},{9,13},{13,1},{2,6},{6,10},{... | collective-permute-start | bytes 786440 | tf_op jit(solution)/shard_map/ppermute | solution.py:27
  21.3 0.2 head_parts.15
  21.4 1.0 %collective-permute-start.13 = (bf16[2,2,128,256]{3,2,1,0:T(8,128)(2,1)S(1)}, bf16[2,2,128,256]{3,2,1,0:T(8,128)(2,1)S(1)}, u32[]{:S(2)}, u32[]{:S(2)}) collective-permute-start(bf16[2,2,128,256]{3,2,1,0:T(8,128)(2,1)S(1)} %head_parts.15), channel_id=1, source_target_pairs={{0,2},{2,0},{1,3},{3,1},{4,6},{6,4},{5,7},{7,5},{8,10},{10,8},{9,1... | collective-permute-start | bytes 786440 | tf_op jit(solution)/shard_map/ppermute | solution.py:32
  22.4 5.4 %collective-permute-done.3.refs_4_ = bf16[2,2,128,256]{3,2,1,0:T(8,128)(2,1)S(1)} collective-permute-done((bf16[2,2,128,256]{3,2,1,0:T(8,128)(2,1)S(1)}, bf16[2,2,128,256]{3,2,1,0:T(8,128)(2,1)S(1)}, u32[]{:S(2)}, u32[]{:S(2)}) %collective-permute-start.3) | collective-permute-done | bytes 262176 | tf_op jit(solution)/shard_map/ppermute | solution.py:27
  27.9 3.5 %attention_grads.2 = (f32[2,2,2,128,256]{4,3,2,1,0:T(8,128)S(1)}, bf16[2,128,256]{2,1,0:T(8,128)(2,1)S(1)}, bf16[2,128,256]{2,1,0:T(8,128)(2,1)S(1)}, bf16[2,2,2,128,256]{4,3,2,1,0:T(8,128)(2,1)S(1)}) custom-call(f32[2,768,256]{2,1,0:T(8,128)S(1)} %pad_maximum_fusion.refs_0_, bf16[2,2,128,256]{3,2,1,0:T(8,128)(2,1)S(1)} %head_parts.8.refs_1_, ...), custom_call_target="tpu_custom_call" | custom-call | flops 1006632960 | bytes 4980736 | tf_op jit(solution)/shard_map/attention_grads/pallas_call | solution.py:51
  31.5 1.7 %collective-permute-start.12 = (bf16[2,2,128,256]{3,2,1,0:T(8,128)(2,1)S(1)}, bf16[2,2,128,256]{3,2,1,0:T(8,128)(2,1)S(1)}, u32[]{:S(2)}, u32[]{:S(2)}) collective-permute-start(bf16[2,2,128,256]{3,2,1,0:T(8,128)(2,1)S(1)} %relayed.2), channel_id=1, source_target_pairs={{0,4},{4,8},{8,12},{1,5},{5,9},{9,13},{2,6},{6,10},{10,14},{3,7},{... | collective-permute-start | bytes 786440 | tf_op jit(solution)/shard_map/ppermute | solution.py:27
  33.2 1.3 %collective-permute-start.7 = (bf16[2,2,2,128,256]{4,3,2,1,0:T(8,128)(2,1)S(1)}, bf16[2,2,2,128,256]{4,3,2,1,0:T(8,128)(2,1)S(1)}, u32[]{:S(2)}, u32[]{:S(2)}) collective-permute-start(bf16[2,2,2,128,256]{4,3,2,1,0:T(8,128)(2,1)S(1)} %get-tuple-element.31), channel_id=1, source_target_pairs={{4,0},{8,4},{12,8},{5,1},{9,5},{13,9},{6,2},{10,6},{14,10},{7,3},{... | collective-permute-start | bytes 1572872 | tf_op jit(solution)/shard_map/ppermute | solution.py:27
  34.5 0.2 head_parts.14.refs_5_
  34.7 2.3 %collective-permute-done.12.refs_4_ = bf16[2,2,128,256]{3,2,1,0:T(8,128)(2,1)S(1)} collective-permute-done((bf16[2,2,128,256]{3,2,1,0:T(8,128)(2,1)S(1)}, bf16[2,2,128,256]{3,2,1,0:T(8,128)(2,1)S(1)}, u32[]{:S(2)}, u32[]{:S(2)}) %collective-permute-start.12) | collective-permute-done | bytes 262176 | tf_op jit(solution)/shard_map/ppermute | solution.py:27
  37.0 3.5 %attention_grads.3 = (f32[2,2,2,128,256]{4,3,2,1,0:T(8,128)S(1)}, bf16[2,128,256]{2,1,0:T(8,128)(2,1)S(1)}, bf16[2,128,256]{2,1,0:T(8,128)(2,1)S(1)}, bf16[2,2,1...) custom-call(f32[2,768,256]{2,1,0:T(8,128)S(1)} %pad_maximum_fusion.refs_0_, ...), custom_call_target="tpu_custom_call" | custom-call | flops 1006632960 | bytes 4980736 | tf_op jit(solution)/shard_map/attention_grads/pallas_call | solution.py:51
  40.6 1.3 %collective-permute-start.15 = (bf16[2,2,128,256]{3,2,1,0:T(8,128)(2,1)S(1)}, bf16[2,2,128,256]{3,2,1,0:T(8,128)(2,1)S(1)}, u32[]{:S(2)}, u32[]{:S(2)}) collective-permute-start(bf16[2,2,128,256]{3,2,1,0:T(8,128)(2,1)S(1)} %get-tuple-element.41), channel_id=1, source_target_pairs={{4,0},{8,4},{12,8},{5,1},{9,5},{13,9},{6,2},{10,6},{14,10},{7,3},{... | collective-permute-start | bytes 786440 | tf_op jit(solution)/shard_map/ppermute | solution.py:27
  41.9 0.6 collective-permute-start.6
  42.5 1.5 %collective-permute-start.14 = (bf16[2,128,256]{2,1,0:T(8,128)(2,1)S(1)}, bf16[2,128,256]{2,1,0:T(8,128)(2,1)S(1)}, u32[]{:S(2)}, u32[]{:S(2)}) collective-permute-start(bf16[2,128,256]{2,1,0:T(8,128)(2,1)S(1)} %get-tuple-element.38), channel_id=1, source_target_pairs={{0,2},{2,0},{1,3},{3,1},{4,6},{6,4},{5,7},{7,5},{8,10},{10,8},{9,1... | collective-permute-start | bytes 393224 | tf_op jit(solution)/shard_map/ppermute | solution.py:32
  44.0 4.1 %collective-permute-done.6.refs_1_ = bf16[2,128,256]{2,1,0:T(8,128)(2,1)S(1)} collective-permute-done((bf16[2,128,256]{2,1,0:T(8,128)(2,1)S(1)}, bf16[2,128,256]{2,1,0:T(8,128)(2,1)S(1)}, u32[]{:S(2)}, u32[]{:S(2)}) %collective-permute-start.6) | collective-permute-done | bytes 131104 | tf_op jit(solution)/shard_map/ppermute | solution.py:32
  48.1 0.1 summed.3
  48.2 0.8 %collective-permute-start.8 = (bf16[2,2,128,256]{3,2,1,0:T(8,128)(2,1)S(1)}, bf16[2,2,128,256]{3,2,1,0:T(8,128)(2,1)S(1)}, u32[]{:S(2)}, u32[]{:S(2)}) collective-permute-start(bf16[2,2,128,256]{3,2,1,0:T(8,128)(2,1)S(1)} %get-tuple-element.33), channel_id=1, source_target_pairs={{0,2},{2,0},{1,3},{3,1},{4,6},{6,4},{5,7},{7,5},{8,10},{10,8},{9,1... | collective-permute-start | bytes 786440 | tf_op jit(solution)/shard_map/ppermute | solution.py:32
  49.0 0.5 collective-permute-done.14.refs_1_
  49.5 0.7 %collective-permute-done.15.refs_0_ = bf16[2,2,128,256]{3,2,1,0:T(8,128)(2,1)S(1)} collective-permute-done((bf16[2,2,128,256]{3,2,1,0:T(8,128)(2,1)S(1)}, bf16[2,2,128,256]{3,2,1,0:T(8,128)(2,1)S(1)}, u32[]{:S(2)}, u32[]{:S(2)}) %collective-permute-start.15) | collective-permute-done | bytes 262176 | tf_op jit(solution)/shard_map/ppermute | solution.py:27
  50.2 1.3 %collective-permute-start.16 = (bf16[2,2,128,256]{3,2,1,0:T(8,128)(2,1)S(1)}, bf16[2,2,128,256]{3,2,1,0:T(8,128)(2,1)S(1)}, u32[]{:S(2)}, u32[]{:S(2)}) collective-permute-start(bf16[2,2,128,256]{3,2,1,0:T(8,128)(2,1)S(1)} %relayed.3), channel_id=1, source_target_pairs={{4,0},{8,4},{12,8},{5,1},{9,5},{13,9},{6,2},{10,6},{14,10},{7,3},{... | collective-permute-start | bytes 786440 | tf_op jit(solution)/shard_map/ppermute | solution.py:27
  51.5 1.5 %collective-permute-start.17 = (bf16[2,2,128,256]{3,2,1,0:T(8,128)(2,1)S(1)}, bf16[2,2,128,256]{3,2,1,0:T(8,128)(2,1)S(1)}, u32[]{:S(2)}, u32[]{:S(2)}) collective-permute-start(bf16[2,2,128,256]{3,2,1,0:T(8,128)(2,1)S(1)} %summed.4.refs_0_), channel_id=1, source_target_pairs={{0,2},{2,0},{1,3},{3,1},{4,6},{6,4},{5,7},{7,5},{8,10},{10,8},{9,1... | collective-permute-start | bytes 786440 | tf_op jit(solution)/shard_map/ppermute | solution.py:32
  53.1 3.0 %collective-permute-done.8.refs_3_ = bf16[2,2,128,256]{3,2,1,0:T(8,128)(2,1)S(1)} collective-permute-done((bf16[2,2,128,256]{3,2,1,0:T(8,128)(2,1)S(1)}, bf16[2,2,128,256]{3,2,1,0:T(8,128)(2,1)S(1)}, u32[]{:S(2)}, u32[]{:S(2)}) %collective-permute-start.8) | collective-permute-done | bytes 262176 | tf_op jit(solution)/shard_map/ppermute | solution.py:32
  56.1 0.1 collective-permute-start.18
  56.2 2.5 %collective-permute-done.16.refs_0_ = bf16[2,2,128,256]{3,2,1,0:T(8,128)(2,1)S(1)} collective-permute-done((bf16[2,2,128,256]{3,2,1,0:T(8,128)(2,1)S(1)}, bf16[2,2,128,256]{3,2,1,0:T(8,128)(2,1)S(1)}, u32[]{:S(2)}, u32[]{:S(2)}) %collective-permute-start.16) | collective-permute-done | bytes 262176 | tf_op jit(solution)/shard_map/ppermute | solution.py:27
  58.7 0.1 collective-permute-done.17.refs_3_
  58.9 0.1 rows_for_pair.3
  58.9 0.1 collective-permute-start.19
  59.0 1.7 %collective-permute-done.19.refs_3_ = bf16[3,2,128,256]{3,2,1,0:T(8,128)(2,1)S(1)} collective-permute-done((bf16[3,2,128,256]{3,2,1,0:T(8,128)(2,1)S(1)}, bf16[3,2,128,256]{3,2,1,0:T(8,128)(2,1)S(1)}, u32[]{:S(2)}, u32[]{:S(2)}) %collective-permute-start.19) | collective-permute-done | bytes 393248 | tf_op jit(solution)/shard_map/ppermute | solution.py:36
  60.7 1.3 %laid_out.1 = (bf16[128,2048]{1,0:T(8,128)(2,1)}, bf16[128,2048]{1,0:T(8,128)(2,1)}, bf16[128,2048]{1,0:T(8,128)(2,1)}) custom-call(bf16[3,2,128,256]{3,2,1,0:T(8,128)(2,1)S(1)} %get-tuple-element.34.refs_0_, bf16[3,2,128,256]{3,2,1,0:T(8,128)(2,1)S(1)} %get-tuple-element.42.refs_1_, bf16[3,2,128,256]{3,2,1,0:T(8,128)(2,1)S(1)} %collective-permute-done.18.refs_2_, ...), custom_call_target="tpu_custom_call" | custom-call | bytes 3145728 | tf_op jit(solution)/shard_map/laid_out/pallas_call | solution.py:51
  (23 shorter events, 0.3 us)
Async XLA Ops:
  1.8 2.9 %collective-permute-start = (bf16[2,2,128,256]{3,2,1,0:T(8,128)(2,1)S(1)}, bf16[2,2,128,256]{3,2,1,0:T(8,128)(2,1)S(1)}, u32[]{:S(2)}, u32[]{:S(2)}) collective-permute-start(bf16[2,2,128,256]{3,2,1,0:T(8,128)(2,1)S(1)} %get-tuple-element.25), channel_id=1, source_target_pairs={{0,1},{1,0},{2,3},{3,2},{4,5},{5,4},{6,7},{7,6},{8,9},{9,8},{10,11... | collective-permute-start | bytes 786440 | tf_op jit(solution)/shard_map/ppermute | solution.py:36
  2.3 2.3 %copy-start = (s32[2048]{0:T(1024)S(1)}, s32[2048]{0:T(1024)}, u32[]{:S(2)}) copy-start(s32[2048]{0:T(1024)} %param.9) | copy-start | bytes 24580
  3.9 5.3 %collective-permute-start.4 = (bf16[2,2,128,256]{3,2,1,0:T(8,128)(2,1)S(1)}, bf16[2,2,128,256]{3,2,1,0:T(8,128)(2,1)S(1)}, u32[]{:S(2)}, u32[]{:S(2)}) collective-permute-start(bf16[2,2,128,256]{3,2,1,0:T(8,128)(2,1)S(1)} %get-tuple-element.27), channel_id=1, source_target_pairs={{0,1},{1,0},{2,3},{3,2},{4,5},{5,4},{6,7},{7,6},{8,9},{9,8},{10,11... | collective-permute-start | bytes 786440 | tf_op jit(solution)/shard_map/ppermute | solution.py:36
  4.1 10.6 %collective-permute-start.9 = (bf16[4,2,128,256]{3,2,1,0:T(8,128)(2,1)S(1)}, bf16[4,2,128,256]{3,2,1,0:T(8,128)(2,1)S(1)}, u32[]{:S(2)}, u32[]{:S(2)}) collective-permute-start(bf16[4,2,128,256]{3,2,1,0:T(8,128)(2,1)S(1)} %get-tuple-element.36), channel_id=1, source_target_pairs={{0,1},{1,0},{2,3},{3,2},{4,5},{5,4},{6,7},{7,6},{8,9},{9,8},{10,11... | collective-permute-start | bytes 1572872 | tf_op jit(solution)/shard_map/ppermute | solution.py:36
  4.8 9.8 %collective-permute-start.1 = (bf16[2,2,128,256]{3,2,1,0:T(8,128)(2,1)S(1)}, bf16[2,2,128,256]{3,2,1,0:T(8,128)(2,1)S(1)}, u32[]{:S(2)}, u32[]{:S(2)}) collective-permute-start(bf16[2,2,128,256]{3,2,1,0:T(8,128)(2,1)S(1)} %head_parts.9), channel_id=1, source_target_pairs={{0,2},{2,0},{1,3},{3,1},{4,6},{6,4},{5,7},{7,5},{8,10},{10,8},{9,1... | collective-permute-start | bytes 786440 | tf_op jit(solution)/shard_map/ppermute | solution.py:32
  7.7 11.7 %collective-permute-start.2 = (bf16[2,2,128,256]{3,2,1,0:T(8,128)(2,1)S(1)}, bf16[2,2,128,256]{3,2,1,0:T(8,128)(2,1)S(1)}, u32[]{:S(2)}, u32[]{:S(2)}) collective-permute-start(bf16[2,2,128,256]{3,2,1,0:T(8,128)(2,1)S(1)} %head_parts.8.refs_1_), channel_id=1, source_target_pairs={{0,4},{4,8},{8,12},{12,0},{1,5},{5,9},{9,13},{13,1},{2,6},{6,10},{... | collective-permute-start | bytes 786440 | tf_op jit(solution)/shard_map/ppermute | solution.py:27
  9.5 11.8 %collective-permute-start.5 = (bf16[2,2,128,256]{3,2,1,0:T(8,128)(2,1)S(1)}, bf16[2,2,128,256]{3,2,1,0:T(8,128)(2,1)S(1)}, u32[]{:S(2)}, u32[]{:S(2)}) collective-permute-start(bf16[2,2,128,256]{3,2,1,0:T(8,128)(2,1)S(1)} %head_parts.11), channel_id=1, source_target_pairs={{0,2},{2,0},{1,3},{3,1},{4,6},{6,4},{5,7},{7,5},{8,10},{10,8},{9,1... | collective-permute-start | bytes 786440 | tf_op jit(solution)/shard_map/ppermute | solution.py:32
  14.8 16.6 %collective-permute-start.10 = (bf16[2,2,128,256]{3,2,1,0:T(8,128)(2,1)S(1)}, bf16[2,2,128,256]{3,2,1,0:T(8,128)(2,1)S(1)}, u32[]{:S(2)}, u32[]{:S(2)}) collective-permute-start(bf16[2,2,128,256]{3,2,1,0:T(8,128)(2,1)S(1)} %head_parts.13), channel_id=1, source_target_pairs={{0,2},{2,0},{1,3},{3,1},{4,6},{6,4},{5,7},{7,5},{8,10},{10,8},{9,1... | collective-permute-start | bytes 786440 | tf_op jit(solution)/shard_map/ppermute | solution.py:32
  16.8 11.0 %collective-permute-start.3 = (bf16[2,2,128,256]{3,2,1,0:T(8,128)(2,1)S(1)}, bf16[2,2,128,256]{3,2,1,0:T(8,128)(2,1)S(1)}, u32[]{:S(2)}, u32[]{:S(2)}) collective-permute-start(bf16[2,2,128,256]{3,2,1,0:T(8,128)(2,1)S(1)} %collective-permute-done.1.refs_2_.refs_0_), channel_id=1, source_target_pairs={{0,4},{4,8},{8,12},{12,0},{1,5},{5,9},{9,13},{13,1},{2,6},{6,10},{... | collective-permute-start | bytes 786440 | tf_op jit(solution)/shard_map/ppermute | solution.py:27
  19.6 15.1 %collective-permute-start.11 = (bf16[2,2,128,256]{3,2,1,0:T(8,128)(2,1)S(1)}, bf16[2,2,128,256]{3,2,1,0:T(8,128)(2,1)S(1)}, u32[]{:S(2)}, u32[]{:S(2)}) collective-permute-start(bf16[2,2,128,256]{3,2,1,0:T(8,128)(2,1)S(1)} %head_parts.12.refs_1_), channel_id=1, source_target_pairs={{0,4},{4,8},{8,12},{12,0},{1,5},{5,9},{9,13},{13,1},{2,6},{6,10},{... | collective-permute-start | bytes 786440 | tf_op jit(solution)/shard_map/ppermute | solution.py:27
  21.4 13.2 %collective-permute-start.13 = (bf16[2,2,128,256]{3,2,1,0:T(8,128)(2,1)S(1)}, bf16[2,2,128,256]{3,2,1,0:T(8,128)(2,1)S(1)}, u32[]{:S(2)}, u32[]{:S(2)}) collective-permute-start(bf16[2,2,128,256]{3,2,1,0:T(8,128)(2,1)S(1)} %head_parts.15), channel_id=1, source_target_pairs={{0,2},{2,0},{1,3},{3,1},{4,6},{6,4},{5,7},{7,5},{8,10},{10,8},{9,1... | collective-permute-start | bytes 786440 | tf_op jit(solution)/shard_map/ppermute | solution.py:32
  31.5 5.6 %collective-permute-start.12 = (bf16[2,2,128,256]{3,2,1,0:T(8,128)(2,1)S(1)}, bf16[2,2,128,256]{3,2,1,0:T(8,128)(2,1)S(1)}, u32[]{:S(2)}, u32[]{:S(2)}) collective-permute-start(bf16[2,2,128,256]{3,2,1,0:T(8,128)(2,1)S(1)} %relayed.2), channel_id=1, source_target_pairs={{0,4},{4,8},{8,12},{1,5},{5,9},{9,13},{2,6},{6,10},{10,14},{3,7},{... | collective-permute-start | bytes 786440 | tf_op jit(solution)/shard_map/ppermute | solution.py:27
  33.2 14.9 %collective-permute-start.7 = (bf16[2,2,2,128,256]{4,3,2,1,0:T(8,128)(2,1)S(1)}, bf16[2,2,2,128,256]{4,3,2,1,0:T(8,128)(2,1)S(1)}, u32[]{:S(2)}, u32[]{:S(2)}) collective-permute-start(bf16[2,2,2,128,256]{4,3,2,1,0:T(8,128)(2,1)S(1)} %get-tuple-element.31), channel_id=1, source_target_pairs={{4,0},{8,4},{12,8},{5,1},{9,5},{13,9},{6,2},{10,6},{14,10},{7,3},{... | collective-permute-start | bytes 1572872 | tf_op jit(solution)/shard_map/ppermute | solution.py:27
  40.6 9.6 %collective-permute-start.15 = (bf16[2,2,128,256]{3,2,1,0:T(8,128)(2,1)S(1)}, bf16[2,2,128,256]{3,2,1,0:T(8,128)(2,1)S(1)}, u32[]{:S(2)}, u32[]{:S(2)}) collective-permute-start(bf16[2,2,128,256]{3,2,1,0:T(8,128)(2,1)S(1)} %get-tuple-element.41), channel_id=1, source_target_pairs={{4,0},{8,4},{12,8},{5,1},{9,5},{13,9},{6,2},{10,6},{14,10},{7,3},{... | collective-permute-start | bytes 786440 | tf_op jit(solution)/shard_map/ppermute | solution.py:27
  41.9 6.2 %collective-permute-start.6 = (bf16[2,128,256]{2,1,0:T(8,128)(2,1)S(1)}, bf16[2,128,256]{2,1,0:T(8,128)(2,1)S(1)}, u32[]{:S(2)}, u32[]{:S(2)}) collective-permute-start(bf16[2,128,256]{2,1,0:T(8,128)(2,1)S(1)} %get-tuple-element.29), channel_id=1, source_target_pairs={{0,2},{2,0},{1,3},{3,1},{4,6},{6,4},{5,7},{7,5},{8,10},{10,8},{9,1... | collective-permute-start | bytes 393224 | tf_op jit(solution)/shard_map/ppermute | solution.py:32
  42.5 7.0 %collective-permute-start.14 = (bf16[2,128,256]{2,1,0:T(8,128)(2,1)S(1)}, bf16[2,128,256]{2,1,0:T(8,128)(2,1)S(1)}, u32[]{:S(2)}, u32[]{:S(2)}) collective-permute-start(bf16[2,128,256]{2,1,0:T(8,128)(2,1)S(1)} %get-tuple-element.38), channel_id=1, source_target_pairs={{0,2},{2,0},{1,3},{3,1},{4,6},{6,4},{5,7},{7,5},{8,10},{10,8},{9,1... | collective-permute-start | bytes 393224 | tf_op jit(solution)/shard_map/ppermute | solution.py:32
  48.2 7.9 %collective-permute-start.8 = (bf16[2,2,128,256]{3,2,1,0:T(8,128)(2,1)S(1)}, bf16[2,2,128,256]{3,2,1,0:T(8,128)(2,1)S(1)}, u32[]{:S(2)}, u32[]{:S(2)}) collective-permute-start(bf16[2,2,128,256]{3,2,1,0:T(8,128)(2,1)S(1)} %get-tuple-element.33), channel_id=1, source_target_pairs={{0,2},{2,0},{1,3},{3,1},{4,6},{6,4},{5,7},{7,5},{8,10},{10,8},{9,1... | collective-permute-start | bytes 786440 | tf_op jit(solution)/shard_map/ppermute | solution.py:32
  50.2 8.4 %collective-permute-start.16 = (bf16[2,2,128,256]{3,2,1,0:T(8,128)(2,1)S(1)}, bf16[2,2,128,256]{3,2,1,0:T(8,128)(2,1)S(1)}, u32[]{:S(2)}, u32[]{:S(2)}) collective-permute-start(bf16[2,2,128,256]{3,2,1,0:T(8,128)(2,1)S(1)} %relayed.3), channel_id=1, source_target_pairs={{4,0},{8,4},{12,8},{5,1},{9,5},{13,9},{6,2},{10,6},{14,10},{7,3},{... | collective-permute-start | bytes 786440 | tf_op jit(solution)/shard_map/ppermute | solution.py:27
  51.5 7.3 %collective-permute-start.17 = (bf16[2,2,128,256]{3,2,1,0:T(8,128)(2,1)S(1)}, bf16[2,2,128,256]{3,2,1,0:T(8,128)(2,1)S(1)}, u32[]{:S(2)}, u32[]{:S(2)}) collective-permute-start(bf16[2,2,128,256]{3,2,1,0:T(8,128)(2,1)S(1)} %summed.4.refs_0_), channel_id=1, source_target_pairs={{0,2},{2,0},{1,3},{3,1},{4,6},{6,4},{5,7},{7,5},{8,10},{10,8},{9,1... | collective-permute-start | bytes 786440 | tf_op jit(solution)/shard_map/ppermute | solution.py:32
  56.1 2.9 %collective-permute-start.18 = (bf16[3,2,128,256]{3,2,1,0:T(8,128)(2,1)S(1)}, bf16[3,2,128,256]{3,2,1,0:T(8,128)(2,1)S(1)}, u32[]{:S(2)}, u32[]{:S(2)}) collective-permute-start(bf16[3,2,128,256]{3,2,1,0:T(8,128)(2,1)S(1)} %get-tuple-element.43), channel_id=1, source_target_pairs={{0,1},{1,0},{2,3},{3,2},{4,5},{5,4},{6,7},{7,6},{8,9},{9,8},{10,11... | collective-permute-start | bytes 1179656 | tf_op jit(solution)/shard_map/ppermute | solution.py:36
  58.9 1.8 %collective-permute-start.19 = (bf16[3,2,128,256]{3,2,1,0:T(8,128)(2,1)S(1)}, bf16[3,2,128,256]{3,2,1,0:T(8,128)(2,1)S(1)}, u32[]{:S(2)}, u32[]{:S(2)}) collective-permute-start(bf16[3,2,128,256]{3,2,1,0:T(8,128)(2,1)S(1)} %get-tuple-element.44), channel_id=1, source_target_pairs={{0,1},{1,0},{2,3},{3,2},{4,5},{5,4},{6,7},{7,6},{8,9},{9,8},{10,11... | collective-permute-start | bytes 1179656 | tf_op jit(solution)/shard_map/ppermute | solution.py:36

commit v10 on v6

--- a/solution.py
+++ b/solution.py
@@ -119,7 +119,26 @@
     return call(kernel, [own, paired] + after, outs, scratch, "head_parts")
 
 
-def attention_grads(bias, kv, kv_earlier, qg, split, after):
+def near_keys(kv_parts, spans):
+    _, _, rows, _ = kv_parts[0][0].shape
+    ins = [array for parts in kv_parts for array in parts[:2]]
+
+    def kernel(*refs):
+        out, sems = refs[-2:]
+        p, s = lax.axis_index("pair"), lax.axis_index("sub")
+        moves = []
+        for chunk, (low, high) in enumerate(spans):
+            which = pl.ds(kv_parts[chunk][2], 2)
+            for side, ref in zip((p, 1 - p), refs[2 * chunk:]):
+                moves.append((ref.at[which, s], out.at[:, side, :, pl.ds(low, high - low)]))
+        run_moves(moves, sems)
+
+    outs = [shape(2, 2, rows, spans[-1][1])]
+    scratch = [pltpu.SemaphoreType.DMA((2 * len(spans),))]
+    return call(kernel, ins, outs, scratch, "near_keys")[0]
+
+
+def attention_grads(bias, kv, kv_earlier, qg, split, low):
     peers = len(kv)
     _, _, rows, cut = kv[0].shape
     heads = cut // HD
@@ -129,7 +148,7 @@
     def kernel(*refs):
         bias_ref = refs[0]
         kv_in, early_in, qg_in = refs[1:1 + peers], refs[1 + peers:1 + 2 * peers], refs[1 + 2 * peers:1 + 3 * peers]
-        outs = refs[1 + 3 * peers + len(after):-5]
+        outs = refs[1 + 3 * peers:-5]
         own_out, dq_outs, early_outs = outs[0], outs[1:1 + peers], outs[1 + peers:]
         kv_all, qg_all, early, dq_all, sems = refs[-5:]
         s = lax.axis_index("sub")
@@ -137,7 +156,7 @@
         for by in range(peers):
             at = lax.rem(s - by + peers, peers)
             moves += [
-                (early_in[by], kv_all.at[:, 0:2, at]),
+                (early_in[by] if by else early_in[0].at[:, :, :, pl.ds(low, cut)], kv_all.at[:, 0:2, at]),
                 (kv_in[by], kv_all.at[:, 2:4, at]),
                 (qg_in[by], qg_all.at[:, :, at]),
             ]
@@ -213,7 +232,7 @@
         pltpu.SemaphoreType.DMA((3 * peers,)),
     ]
     flops = heads * 2 * 5 * 2 * strip * 3 * strip * HD
-    ins = [bias] + kv + kv_earlier + qg + after
+    ins = [bias] + kv + kv_earlier + qg
     outs = call(kernel, ins, outs, scratch, "attention_grads", whole=True, flops=flops, room=40 * MIB)
     return outs[0], outs[1:1 + peers], outs[1 + peers:]
 
@@ -312,27 +331,29 @@
         kv_parts.append((own, paired, 0))
         qg_parts.append((own, paired, 2))
     count = len(spans)
-    kv_sends, qg_sends, kv, qg, kv_own, own_earlier = [], [], [], [], [], []
+    near = along_blocks(near_keys(kv_parts, spans), 1, True)
+    kv, qg = [], []
     for index in range(count):
-        kv_sends.append(head_parts(*kv_parts[index], others, kv[index - 1] if index else []))
-        kv.append([round_sub(value, by) for by, value in zip(others, kv_sends[index])])
-        kv_own.append(head_parts(*kv_parts[index], [0], own_earlier[index - 1:index]))
-        own_earlier.append(along_blocks(kv_own[index][0], 1, True))
-        qg_sends.append(head_parts(*qg_parts[index], others, qg[index - 1] if index else []))
-        qg.append([round_sub(value, by) for by, value in zip(others, qg_sends[index])])
-    kept, paired = [], []
+        sends = head_parts(*kv_parts[index], others, kv[index - 2] if index > 1 else [])
+        kv.append([round_sub(value, by) for by, value in zip(others, sends)])
+    for index in range(count):
+        sends = head_parts(*qg_parts[index], others, kv[index])
+        qg.append([round_sub(value, by) for by, value in zip(others, sends)])
+    kept, paired, sums = [], [], []
     for index in range(count):
         last = index == count - 1
-        earlier = [own_earlier[index]] + [along_blocks(value, 1, not last) for value in kv[index]]
+        earlier = [near] + [along_blocks(value, 1, True) for value in kv[index]]
+        kv_all = head_parts(*kv_parts[index], [0], []) + kv[index]
         qg_all = head_parts(*qg_parts[index], [0], []) + qg[index]
-        grads, dq, early = attention_grads(bias, kv_own[index] + kv[index], earlier, qg_all, last, [])
+        grads, dq, early = attention_grads(bias, kv_all, earlier, qg_all, last, spans[index][0])
         dq = [dq[0]] + [round_sub(dq[by], by) for by in others]
         later = [along_blocks(value, -1, False) for value in early]
         if last:
-            dkv = summed(grads, later[1:], others, dq[1:])
+            dkv = summed(grads, later[1:], others, dq[1:] + sums)
             dkv = summed(grads, later[:1], [0], dkv[:1]) + [round_sub(value, by) for by, value in zip(others, dkv)]
         else:
             dkv = summed(grads, later, [0] + others, dq[1:])
+            sums = dkv[:1]
             dkv = [dkv[0]] + [round_sub(dkv[by], by) for by in others]
         send, keep = rows_for_pair(dq, dkv)
         kept.append(keep)

time: 65.8 us -> 67.6 us (1.027)
  waiting for transfers between devices: 25.3 us -> 32.6 us
  starting transfers between devices: 25.3 us -> 19.8 us
    ppermute x8, waiting for transfers between devices: 13.2 us -> 18 us  [round_sub(): lax.ppermute(value, 'sub', [(i, (i + by) % peers) for i in range(peers)])]
    ppermute x7 -> x6, starting transfers between devices: 12.6 us -> 8.91 us  [along_blocks(): return lax.ppermute(value, 'blk', pairs)]
    ppermute x7 -> x6, waiting for transfers between devices: 10.4 us -> 12.9 us  [along_blocks(): return lax.ppermute(value, 'blk', pairs)]
    ppermute x8, starting transfers between devices: 11.4 us -> 9.7 us  [round_sub(): lax.ppermute(value, 'sub', [(i, (i + by) % peers) for i in range(peers)])]
    pallas_call x16 -> x17, Pallas kernels: 10.3 us -> 10.3 us  [call(): pl.pallas_call(kernel, out_shape=outs, in_specs=[spec] * len(ins), out_sp...]
  transfers between devices with their start and end apart: 20 -> 19, of which waited for: 8 -> 9; matrix products, arithmetic and copies ran while one was open for 1% -> 1% of each run, Pallas kernels for 16% -> 16%
where the time goes in v10:
time: 67.6 us; the launch traced here: 67.3 us
  waiting for transfers between devices  32.6 us (48%)
  starting transfers between devices  19.8 us (29%)
  Pallas kernels  13.1 us (19%)
  between operations  0.86 us (1%)
  other arithmetic  0.79 us (1%)
    ppermute x8, waiting for transfers between devices, round_sub(): lax.ppermute(value, 'sub', [(i, (i + by) % peers) for i in range(peers)])  18 us
    ppermute x6, waiting for transfers between devices, along_blocks(): return lax.ppermute(value, 'blk', pairs)  12.9 us
    pallas_call x17, Pallas kernels, call(): pl.pallas_call(kernel, out_shape=outs, in_specs=[spec] * len(ins), out_sp...  10.3 us
    ppermute x8, starting transfers between devices, round_sub(): lax.ppermute(value, 'sub', [(i, (i + by) % peers) for i in range(peers)])  9.7 us
    ppermute x6, starting transfers between devices, along_blocks(): return lax.ppermute(value, 'blk', pairs)  8.91 us
    pallas_call x2, Pallas kernels, first_parts(): pl.pallas_call(kernel, out_shape=outs, in_specs=[spec] * (len(held) + len...  2.78 us
    ppermute x5, waiting for transfers between devices, swapped(): return lax.ppermute(value, 'pair', [(0, 1), (1, 0)])  1.71 us
  transfers between devices with their start and end apart: 19, of which 9 were waited for; matrix products, arithmetic and copies ran while one was open for 1% of the time, Pallas kernels for 16%

profile of v10, /device:TPU:0, one launch (start us, length us, event | category | flops | bytes accessed | tf_op | source)
XLA Modules:
  0.0 67.3 jit_solution(1444034257894388813)
XLA Ops:
  0.6 1.1 %first_parts.2 = (bf16[2,2,128,256]{3,2,1,0:T(8,128)(2,1)S(1)}, bf16[2,2,128,256]{3,2,1,0:T(8,128)(2,1)S(1)}) custom-call(bf16[128,2048]{1,0:T(8,128)(2,1)} %refs_2_.1, bf16[128,2048]{1,0:T(8,128)(2,1)} %refs_3_.1), custom_call_target="tpu_custom_call" | custom-call | tf_op jit(solution)/shard_map/first_parts/pallas_call | solution.py:92
  1.8 0.5 collective-permute-start
  2.3 1.6 %first_parts.3 = (bf16[2,2,128,256]{3,2,1,0:T(8,128)(2,1)S(1)}, bf16[2,2,128,256]{3,2,1,0:T(8,128)(2,1)S(1)}, bf16[4,2,128,256]{3,2,1,0:T(8,128)(2,1)S(1)}, bf16[4,2,128,256]{3,2,1,0:T(8,128)(2,1)S(1)}) custom-call(bf16[128,2048]{1,0:T(8,128)(2,1)} %refs_4_.1, bf16[128,2048]{1,0:T(8,128)(2,1)} %refs_5_.1, bf16[128,2048]{1,0:T(8,128)(2,1)} %refs_2_.1, ...), custom_call_target="tpu_custom_call" | custom-call | tf_op jit(solution)/shard_map/first_parts/pallas_call | solution.py:92
  3.9 0.1 collective-permute-start.2
  4.1 0.5 collective-permute-start.5
  4.5 0.1 pad_dynamic-slice_fusion
  4.6 0.2 head_parts.9
  4.8 2.6 %collective-permute-start.1 = (bf16[2,2,128,256]{3,2,1,0:T(8,128)(2,1)S(1)}, bf16[2,2,128,256]{3,2,1,0:T(8,128)(2,1)S(1)}, u32[]{:S(2)}, u32[]{:S(2)}) collective-permute-start(bf16[2,2,128,256]{3,2,1,0:T(8,128)(2,1)S(1)} %head_parts.9), channel_id=1, source_target_pairs={{0,2},{2,0},{1,3},{3,1},{4,6},{6,4},{5,7},{7,5},{8,10},{10,8},{9,1... | collective-permute-start | bytes 786440 | tf_op jit(solution)/shard_map/ppermute | solution.py:32
  7.5 0.1 near_keys.1
  7.6 1.6 %collective-permute-start.3 = (bf16[2,2,128,512]{3,2,1,0:T(8,128)(2,1)S(1)}, bf16[2,2,128,512]{3,2,1,0:T(8,128)(2,1)S(1)}, u32[]{:S(2)}, u32[]{:S(2)}) collective-permute-start(bf16[2,2,128,512]{3,2,1,0:T(8,128)(2,1)S(1)} %near_keys.1), channel_id=1, source_target_pairs={{0,4},{4,8},{8,12},{12,0},{1,5},{5,9},{9,13},{13,1},{2,6},{6,10},{... | collective-permute-start | bytes 1572872 | tf_op jit(solution)/shard_map/ppermute | solution.py:27
  9.2 5.2 %collective-permute-done.1.refs_0_.refs_2_ = bf16[2,2,128,256]{3,2,1,0:T(8,128)(2,1)S(1)} collective-permute-done((bf16[2,2,128,256]{3,2,1,0:T(8,128)(2,1)S(1)}, bf16[2,2,128,256]{3,2,1,0:T(8,128)(2,1)S(1)}, u32[]{:S(2)}, u32[]{:S(2)}) %collective-permute-start.1) | collective-permute-done | bytes 262176 | tf_op jit(solution)/shard_map/ppermute | solution.py:32
  14.4 0.2 head_parts.11
  14.5 1.8 %collective-permute-start.6 = (bf16[2,2,128,256]{3,2,1,0:T(8,128)(2,1)S(1)}, bf16[2,2,128,256]{3,2,1,0:T(8,128)(2,1)S(1)}, u32[]{:S(2)}, u32[]{:S(2)}) collective-permute-start(bf16[2,2,128,256]{3,2,1,0:T(8,128)(2,1)S(1)} %head_parts.11), channel_id=1, source_target_pairs={{0,2},{2,0},{1,3},{3,1},{4,6},{6,4},{5,7},{7,5},{8,10},{10,8},{9,1... | collective-permute-start | bytes 786440 | tf_op jit(solution)/shard_map/ppermute | solution.py:32
  16.4 0.2 head_parts.13
  16.5 0.3 collective-permute-start.10
  16.9 1.8 %collective-permute-start.4 = (bf16[2,2,128,256]{3,2,1,0:T(8,128)(2,1)S(1)}, bf16[2,2,128,256]{3,2,1,0:T(8,128)(2,1)S(1)}, u32[]{:S(2)}, u32[]{:S(2)}) collective-permute-start(bf16[2,2,128,256]{3,2,1,0:T(8,128)(2,1)S(1)} %collective-permute-done.1.refs_0_.refs_2_), channel_id=1, source_target_pairs={{0,4},{4,8},{8,12},{12,0},{1,5},{5,9},{9,13},{13,1},{2,6},{6,10},{... | collective-permute-start | bytes 786440 | tf_op jit(solution)/shard_map/ppermute | solution.py:27
  18.7 0.7 and_select_fusion
  19.4 0.1 pad_maximum_fusion.refs_0_
  19.5 0.2 head_parts.8.refs_1_
  19.7 0.2 head_parts.10.refs_5_
  19.9 8.4 %collective-permute-done.10.refs_0_.refs_2_ = bf16[2,2,128,256]{3,2,1,0:T(8,128)(2,1)S(1)} collective-permute-done((bf16[2,2,128,256]{3,2,1,0:T(8,128)(2,1)S(1)}, bf16[2,2,128,256]{3,2,1,0:T(8,128)(2,1)S(1)}, u32[]{:S(2)}, u32[]{:S(2)}) %collective-permute-start.10) | collective-permute-done | bytes 262176 | tf_op jit(solution)/shard_map/ppermute | solution.py:32
  28.3 0.2 head_parts.15
  28.5 1.6 %collective-permute-start.12 = (bf16[2,2,128,256]{3,2,1,0:T(8,128)(2,1)S(1)}, bf16[2,2,128,256]{3,2,1,0:T(8,128)(2,1)S(1)}, u32[]{:S(2)}, u32[]{:S(2)}) collective-permute-start(bf16[2,2,128,256]{3,2,1,0:T(8,128)(2,1)S(1)} %head_parts.15), channel_id=1, source_target_pairs={{0,2},{2,0},{1,3},{3,1},{4,6},{6,4},{5,7},{7,5},{8,10},{10,8},{9,1... | collective-permute-start | bytes 786440 | tf_op jit(solution)/shard_map/ppermute | solution.py:32
  30.1 1.6 %collective-permute-start.11 = (bf16[2,2,128,256]{3,2,1,0:T(8,128)(2,1)S(1)}, bf16[2,2,128,256]{3,2,1,0:T(8,128)(2,1)S(1)}, u32[]{:S(2)}, u32[]{:S(2)}) collective-permute-start(bf16[2,2,128,256]{3,2,1,0:T(8,128)(2,1)S(1)} %collective-permute-done.10.refs_0_.refs_2_), channel_id=1, source_target_pairs={{0,4},{4,8},{8,12},{12,0},{1,5},{5,9},{9,13},{13,1},{2,6},{6,10},{... | collective-permute-start | bytes 786440 | tf_op jit(solution)/shard_map/ppermute | solution.py:27
  31.7 3.6 %attention_grads.2 = (f32[2,2,2,128,256]{4,3,2,1,0:T(8,128)S(1)}, bf16[2,128,256]{2,1,0:T(8,128)(2,1)S(1)}, bf16[2,128,256]{2,1,0:T(8,128)(2,1)S(1)}, bf16[2,2,2,128,256]{4,3,2,1,0:T(8,128)(2,1)S(1)}) custom-call(f32[2,768,256]{2,1,0:T(8,128)S(1)} %pad_maximum_fusion.refs_0_, bf16[2,2,128,256]{3,2,1,0:T(8,128)(2,1)S(1)} %head_parts.8.refs_1_, ...), custom_call_target="tpu_custom_call" | custom-call | flops 1006632960 | bytes 5242880 | tf_op jit(solution)/shard_map/attention_grads/pallas_call | solution.py:51
  35.3 1.3 %collective-permute-start.8 = (bf16[2,2,2,128,256]{4,3,2,1,0:T(8,128)(2,1)S(1)}, bf16[2,2,2,128,256]{4,3,2,1,0:T(8,128)(2,1)S(1)}, u32[]{:S(2)}, u32[]{:S(2)}) collective-permute-start(bf16[2,2,2,128,256]{4,3,2,1,0:T(8,128)(2,1)S(1)} %get-tuple-element.33), channel_id=1, source_target_pairs={{4,0},{8,4},{12,8},{5,1},{9,5},{13,9},{6,2},{10,6},{14,10},{7,3},{... | collective-permute-start | bytes 1572872 | tf_op jit(solution)/shard_map/ppermute | solution.py:27
  36.6 0.2 head_parts.12.refs_1_
  36.8 0.2 head_parts.14.refs_5_
  37.0 1.7 %collective-permute-done.11.refs_4_ = bf16[2,2,128,256]{3,2,1,0:T(8,128)(2,1)S(1)} collective-permute-done((bf16[2,2,128,256]{3,2,1,0:T(8,128)(2,1)S(1)}, bf16[2,2,128,256]{3,2,1,0:T(8,128)(2,1)S(1)}, u32[]{:S(2)}, u32[]{:S(2)}) %collective-permute-start.11) | collective-permute-done | bytes 262176 | tf_op jit(solution)/shard_map/ppermute | solution.py:27
  38.7 3.5 %attention_grads.3 = (f32[2,2,2,128,256]{4,3,2,1,0:T(8,128)S(1)}, bf16[2,128,256]{2,1,0:T(8,128)(2,1)S(1)}, bf16[2,128,256]{2,1,0:T(8,128)(2,1)S(1)}, bf16[2,2,1...) custom-call(f32[2,768,256]{2,1,0:T(8,128)S(1)} %pad_maximum_fusion.refs_0_, ...), custom_call_target="tpu_custom_call" | custom-call | flops 1006632960 | bytes 5242880 | tf_op jit(solution)/shard_map/attention_grads/pallas_call | solution.py:51
  42.3 1.3 %collective-permute-start.15 = (bf16[2,2,128,256]{3,2,1,0:T(8,128)(2,1)S(1)}, bf16[2,2,128,256]{3,2,1,0:T(8,128)(2,1)S(1)}, u32[]{:S(2)}, u32[]{:S(2)}) collective-permute-start(bf16[2,2,128,256]{3,2,1,0:T(8,128)(2,1)S(1)} %get-tuple-element.41), channel_id=1, source_target_pairs={{4,0},{8,4},{12,8},{5,1},{9,5},{13,9},{6,2},{10,6},{14,10},{7,3},{... | collective-permute-start | bytes 786440 | tf_op jit(solution)/shard_map/ppermute | solution.py:27
  43.6 0.7 %collective-permute-start.7 = (bf16[2,128,256]{2,1,0:T(8,128)(2,1)S(1)}, bf16[2,128,256]{2,1,0:T(8,128)(2,1)S(1)}, u32[]{:S(2)}, u32[]{:S(2)}) collective-permute-start(bf16[2,128,256]{2,1,0:T(8,128)(2,1)S(1)} %get-tuple-element.31), channel_id=1, source_target_pairs={{0,2},{2,0},{1,3},{3,1},{4,6},{6,4},{5,7},{7,5},{8,10},{10,8},{9,1... | collective-permute-start | bytes 393224 | tf_op jit(solution)/shard_map/ppermute | solution.py:32
  44.3 1.4 %collective-permute-start.13 = (bf16[2,128,256]{2,1,0:T(8,128)(2,1)S(1)}, bf16[2,128,256]{2,1,0:T(8,128)(2,1)S(1)}, u32[]{:S(2)}, u32[]{:S(2)}) collective-permute-start(bf16[2,128,256]{2,1,0:T(8,128)(2,1)S(1)} %get-tuple-element.38), channel_id=1, source_target_pairs={{0,2},{2,0},{1,3},{3,1},{4,6},{6,4},{5,7},{7,5},{8,10},{10,8},{9,1... | collective-permute-start | bytes 393224 | tf_op jit(solution)/shard_map/ppermute | solution.py:32
  45.7 1.3 %collective-permute-start.14 = (bf16[2,2,128,256]{3,2,1,0:T(8,128)(2,1)S(1)}, bf16[2,2,128,256]{3,2,1,0:T(8,128)(2,1)S(1)}, u32[]{:S(2)}, u32[]{:S(2)}) collective-permute-start(bf16[2,2,128,256]{3,2,1,0:T(8,128)(2,1)S(1)} %get-tuple-element.40), channel_id=1, source_target_pairs={{4,0},{8,4},{12,8},{5,1},{9,5},{13,9},{6,2},{10,6},{14,10},{7,3},{... | collective-permute-start | bytes 786440 | tf_op jit(solution)/shard_map/ppermute | solution.py:27
  47.0 1.7 %collective-permute-done.7.refs_1_ = bf16[2,128,256]{2,1,0:T(8,128)(2,1)S(1)} collective-permute-done((bf16[2,128,256]{2,1,0:T(8,128)(2,1)S(1)}, bf16[2,128,256]{2,1,0:T(8,128)(2,1)S(1)}, u32[]{:S(2)}, u32[]{:S(2)}) %collective-permute-start.7) | collective-permute-done | bytes 131104 | tf_op jit(solution)/shard_map/ppermute | solution.py:32
  48.6 3.4 %collective-permute-done.8.refs_0_ = bf16[2,2,2,128,256]{4,3,2,1,0:T(8,128)(2,1)S(1)} collective-permute-done((bf16[2,2,2,128,256]{4,3,2,1,0:T(8,128)(2,1)S(1)}, bf16[2,2,2,128,256]{4,3,2,1,0:T(8,128)(2,1)S(1)}, u32[]{:S(2)}, u32[]{:S(2)}) %collective-permute-start.8) | collective-permute-done | bytes 524320 | tf_op jit(solution)/shard_map/ppermute | solution.py:27
  52.0 0.1 summed.3
  52.1 0.6 collective-permute-start.9
  52.7 4.9 %collective-permute-done.15.refs_0_ = bf16[2,2,128,256]{3,2,1,0:T(8,128)(2,1)S(1)} collective-permute-done((bf16[2,2,128,256]{3,2,1,0:T(8,128)(2,1)S(1)}, bf16[2,2,128,256]{3,2,1,0:T(8,128)(2,1)S(1)}, u32[]{:S(2)}, u32[]{:S(2)}) %collective-permute-start.15) | collective-permute-done | bytes 262176 | tf_op jit(solution)/shard_map/ppermute | solution.py:27
  57.7 0.6 collective-permute-start.16
  58.3 2.8 %collective-permute-done.14.refs_0_ = bf16[2,2,128,256]{3,2,1,0:T(8,128)(2,1)S(1)} collective-permute-done((bf16[2,2,128,256]{3,2,1,0:T(8,128)(2,1)S(1)}, bf16[2,2,128,256]{3,2,1,0:T(8,128)(2,1)S(1)}, u32[]{:S(2)}, u32[]{:S(2)}) %collective-permute-start.14) | collective-permute-done | bytes 262176 | tf_op jit(solution)/shard_map/ppermute | solution.py:27
  61.2 0.1 rows_for_pair.2
  61.3 0.1 collective-permute-start.17
  61.3 2.8 %collective-permute-done.16.refs_3_ = bf16[2,2,128,256]{3,2,1,0:T(8,128)(2,1)S(1)} collective-permute-done((bf16[2,2,128,256]{3,2,1,0:T(8,128)(2,1)S(1)}, bf16[2,2,128,256]{3,2,1,0:T(8,128)(2,1)S(1)}, u32[]{:S(2)}, u32[]{:S(2)}) %collective-permute-start.16) | collective-permute-done | bytes 262176 | tf_op jit(solution)/shard_map/ppermute | solution.py:32
  64.2 0.1 rows_for_pair.3
  64.2 0.1 collective-permute-start.18
  64.3 1.7 %collective-permute-done.18.refs_3_ = bf16[3,2,128,256]{3,2,1,0:T(8,128)(2,1)S(1)} collective-permute-done((bf16[3,2,128,256]{3,2,1,0:T(8,128)(2,1)S(1)}, bf16[3,2,128,256]{3,2,1,0:T(8,128)(2,1)S(1)}, u32[]{:S(2)}, u32[]{:S(2)}) %collective-permute-start.18) | collective-permute-done | bytes 393248 | tf_op jit(solution)/shard_map/ppermute | solution.py:36
  66.0 1.3 %laid_out.1 = (bf16[128,2048]{1,0:T(8,128)(2,1)}, bf16[128,2048]{1,0:T(8,128)(2,1)}, bf16[128,2048]{1,0:T(8,128)(2,1)}) custom-call(bf16[3,2,128,256]{3,2,1,0:T(8,128)(2,1)S(1)} %get-tuple-element.36.refs_0_, bf16[3,2,128,256]{3,2,1,0:T(8,128)(2,1)S(1)} %get-tuple-element.42.refs_1_, bf16[3,2,128,256]{3,2,1,0:T(8,128)(2,1)S(1)} %collective-permute-done.17.refs_2_, ...), custom_call_target="tpu_custom_call" | custom-call | bytes 3145728 | tf_op jit(solution)/shard_map/laid_out/pallas_call | solution.py:51
  (20 shorter events, 0.2 us)
Async XLA Ops:
  1.8 2.9 %collective-permute-start = (bf16[2,2,128,256]{3,2,1,0:T(8,128)(2,1)S(1)}, bf16[2,2,128,256]{3,2,1,0:T(8,128)(2,1)S(1)}, u32[]{:S(2)}, u32[]{:S(2)}) collective-permute-start(bf16[2,2,128,256]{3,2,1,0:T(8,128)(2,1)S(1)} %get-tuple-element.25), channel_id=1, source_target_pairs={{0,1},{1,0},{2,3},{3,2},{4,5},{5,4},{6,7},{7,6},{8,9},{9,8},{10,11... | collective-permute-start | bytes 786440 | tf_op jit(solution)/shard_map/ppermute | solution.py:36
  2.3 2.2 %copy-start = (s32[2048]{0:T(1024)S(1)}, s32[2048]{0:T(1024)}, u32[]{:S(2)}) copy-start(s32[2048]{0:T(1024)} %param.9) | copy-start | bytes 24580
  3.9 3.5 %collective-permute-start.2 = (bf16[4,2,128,256]{3,2,1,0:T(8,128)(2,1)S(1)}, bf16[4,2,128,256]{3,2,1,0:T(8,128)(2,1)S(1)}, u32[]{:S(2)}, u32[]{:S(2)}) collective-permute-start(bf16[4,2,128,256]{3,2,1,0:T(8,128)(2,1)S(1)} %get-tuple-element.27), channel_id=1, source_target_pairs={{0,1},{1,0},{2,3},{3,2},{4,5},{5,4},{6,7},{7,6},{8,9},{9,8},{10,11... | collective-permute-start | bytes 1572872 | tf_op jit(solution)/shard_map/ppermute | solution.py:36
  4.1 5.1 %collective-permute-start.5 = (bf16[2,2,128,256]{3,2,1,0:T(8,128)(2,1)S(1)}, bf16[2,2,128,256]{3,2,1,0:T(8,128)(2,1)S(1)}, u32[]{:S(2)}, u32[]{:S(2)}) collective-permute-start(bf16[2,2,128,256]{3,2,1,0:T(8,128)(2,1)S(1)} %get-tuple-element.29), channel_id=1, source_target_pairs={{0,1},{1,0},{2,3},{3,2},{4,5},{5,4},{6,7},{7,6},{8,9},{9,8},{10,11... | collective-permute-start | bytes 786440 | tf_op jit(solution)/shard_map/ppermute | solution.py:36
  4.8 9.5 %collective-permute-start.1 = (bf16[2,2,128,256]{3,2,1,0:T(8,128)(2,1)S(1)}, bf16[2,2,128,256]{3,2,1,0:T(8,128)(2,1)S(1)}, u32[]{:S(2)}, u32[]{:S(2)}) collective-permute-start(bf16[2,2,128,256]{3,2,1,0:T(8,128)(2,1)S(1)} %head_parts.9), channel_id=1, source_target_pairs={{0,2},{2,0},{1,3},{3,1},{4,6},{6,4},{5,7},{7,5},{8,10},{10,8},{9,1... | collective-permute-start | bytes 786440 | tf_op jit(solution)/shard_map/ppermute | solution.py:32
  7.6 24.1 %collective-permute-start.3 = (bf16[2,2,128,512]{3,2,1,0:T(8,128)(2,1)S(1)}, bf16[2,2,128,512]{3,2,1,0:T(8,128)(2,1)S(1)}, u32[]{:S(2)}, u32[]{:S(2)}) collective-permute-start(bf16[2,2,128,512]{3,2,1,0:T(8,128)(2,1)S(1)} %near_keys.1), channel_id=1, source_target_pairs={{0,4},{4,8},{8,12},{12,0},{1,5},{5,9},{9,13},{13,1},{2,6},{6,10},{... | collective-permute-start | bytes 1572872 | tf_op jit(solution)/shard_map/ppermute | solution.py:27
  14.5 17.1 %collective-permute-start.6 = (bf16[2,2,128,256]{3,2,1,0:T(8,128)(2,1)S(1)}, bf16[2,2,128,256]{3,2,1,0:T(8,128)(2,1)S(1)}, u32[]{:S(2)}, u32[]{:S(2)}) collective-permute-start(bf16[2,2,128,256]{3,2,1,0:T(8,128)(2,1)S(1)} %head_parts.11), channel_id=1, source_target_pairs={{0,2},{2,0},{1,3},{3,1},{4,6},{6,4},{5,7},{7,5},{8,10},{10,8},{9,1... | collective-permute-start | bytes 786440 | tf_op jit(solution)/shard_map/ppermute | solution.py:32
  16.5 11.7 %collective-permute-start.10 = (bf16[2,2,128,256]{3,2,1,0:T(8,128)(2,1)S(1)}, bf16[2,2,128,256]{3,2,1,0:T(8,128)(2,1)S(1)}, u32[]{:S(2)}, u32[]{:S(2)}) collective-permute-start(bf16[2,2,128,256]{3,2,1,0:T(8,128)(2,1)S(1)} %head_parts.13), channel_id=1, source_target_pairs={{0,2},{2,0},{1,3},{3,1},{4,6},{6,4},{5,7},{7,5},{8,10},{10,8},{9,1... | collective-permute-start | bytes 786440 | tf_op jit(solution)/shard_map/ppermute | solution.py:32
  16.9 14.8 %collective-permute-start.4 = (bf16[2,2,128,256]{3,2,1,0:T(8,128)(2,1)S(1)}, bf16[2,2,128,256]{3,2,1,0:T(8,128)(2,1)S(1)}, u32[]{:S(2)}, u32[]{:S(2)}) collective-permute-start(bf16[2,2,128,256]{3,2,1,0:T(8,128)(2,1)S(1)} %collective-permute-done.1.refs_0_.refs_2_), channel_id=1, source_target_pairs={{0,4},{4,8},{8,12},{12,0},{1,5},{5,9},{9,13},{13,1},{2,6},{6,10},{... | collective-permute-start | bytes 786440 | tf_op jit(solution)/shard_map/ppermute | solution.py:27
  28.5 10.3 %collective-permute-start.12 = (bf16[2,2,128,256]{3,2,1,0:T(8,128)(2,1)S(1)}, bf16[2,2,128,256]{3,2,1,0:T(8,128)(2,1)S(1)}, u32[]{:S(2)}, u32[]{:S(2)}) collective-permute-start(bf16[2,2,128,256]{3,2,1,0:T(8,128)(2,1)S(1)} %head_parts.15), channel_id=1, source_target_pairs={{0,2},{2,0},{1,3},{3,1},{4,6},{6,4},{5,7},{7,5},{8,10},{10,8},{9,1... | collective-permute-start | bytes 786440 | tf_op jit(solution)/shard_map/ppermute | solution.py:32
  30.1 8.6 %collective-permute-start.11 = (bf16[2,2,128,256]{3,2,1,0:T(8,128)(2,1)S(1)}, bf16[2,2,128,256]{3,2,1,0:T(8,128)(2,1)S(1)}, u32[]{:S(2)}, u32[]{:S(2)}) collective-permute-start(bf16[2,2,128,256]{3,2,1,0:T(8,128)(2,1)S(1)} %collective-permute-done.10.refs_0_.refs_2_), channel_id=1, source_target_pairs={{0,4},{4,8},{8,12},{12,0},{1,5},{5,9},{9,13},{13,1},{2,6},{6,10},{... | collective-permute-start | bytes 786440 | tf_op jit(solution)/shard_map/ppermute | solution.py:27
  35.3 16.8 %collective-permute-start.8 = (bf16[2,2,2,128,256]{4,3,2,1,0:T(8,128)(2,1)S(1)}, bf16[2,2,2,128,256]{4,3,2,1,0:T(8,128)(2,1)S(1)}, u32[]{:S(2)}, u32[]{:S(2)}) collective-permute-start(bf16[2,2,2,128,256]{4,3,2,1,0:T(8,128)(2,1)S(1)} %get-tuple-element.33), channel_id=1, source_target_pairs={{4,0},{8,4},{12,8},{5,1},{9,5},{13,9},{6,2},{10,6},{14,10},{7,3},{... | collective-permute-start | bytes 1572872 | tf_op jit(solution)/shard_map/ppermute | solution.py:27
  42.3 15.3 %collective-permute-start.15 = (bf16[2,2,128,256]{3,2,1,0:T(8,128)(2,1)S(1)}, bf16[2,2,128,256]{3,2,1,0:T(8,128)(2,1)S(1)}, u32[]{:S(2)}, u32[]{:S(2)}) collective-permute-start(bf16[2,2,128,256]{3,2,1,0:T(8,128)(2,1)S(1)} %get-tuple-element.41), channel_id=1, source_target_pairs={{4,0},{8,4},{12,8},{5,1},{9,5},{13,9},{6,2},{10,6},{14,10},{7,3},{... | collective-permute-start | bytes 786440 | tf_op jit(solution)/shard_map/ppermute | solution.py:27
  43.6 5.0 %collective-permute-start.7 = (bf16[2,128,256]{2,1,0:T(8,128)(2,1)S(1)}, bf16[2,128,256]{2,1,0:T(8,128)(2,1)S(1)}, u32[]{:S(2)}, u32[]{:S(2)}) collective-permute-start(bf16[2,128,256]{2,1,0:T(8,128)(2,1)S(1)} %get-tuple-element.31), channel_id=1, source_target_pairs={{0,2},{2,0},{1,3},{3,1},{4,6},{6,4},{5,7},{7,5},{8,10},{10,8},{9,1... | collective-permute-start | bytes 393224 | tf_op jit(solution)/shard_map/ppermute | solution.py:32
  44.3 8.4 %collective-permute-start.13 = (bf16[2,128,256]{2,1,0:T(8,128)(2,1)S(1)}, bf16[2,128,256]{2,1,0:T(8,128)(2,1)S(1)}, u32[]{:S(2)}, u32[]{:S(2)}) collective-permute-start(bf16[2,128,256]{2,1,0:T(8,128)(2,1)S(1)} %get-tuple-element.38), channel_id=1, source_target_pairs={{0,2},{2,0},{1,3},{3,1},{4,6},{6,4},{5,7},{7,5},{8,10},{10,8},{9,1... | collective-permute-start | bytes 393224 | tf_op jit(solution)/shard_map/ppermute | solution.py:32
  45.7 15.5 %collective-permute-start.14 = (bf16[2,2,128,256]{3,2,1,0:T(8,128)(2,1)S(1)}, bf16[2,2,128,256]{3,2,1,0:T(8,128)(2,1)S(1)}, u32[]{:S(2)}, u32[]{:S(2)}) collective-permute-start(bf16[2,2,128,256]{3,2,1,0:T(8,128)(2,1)S(1)} %get-tuple-element.40), channel_id=1, source_target_pairs={{4,0},{8,4},{12,8},{5,1},{9,5},{13,9},{6,2},{10,6},{14,10},{7,3},{... | collective-permute-start | bytes 786440 | tf_op jit(solution)/shard_map/ppermute | solution.py:27
  52.1 9.1 %collective-permute-start.9 = (bf16[2,2,128,256]{3,2,1,0:T(8,128)(2,1)S(1)}, bf16[2,2,128,256]{3,2,1,0:T(8,128)(2,1)S(1)}, u32[]{:S(2)}, u32[]{:S(2)}) collective-permute-start(bf16[2,2,128,256]{3,2,1,0:T(8,128)(2,1)S(1)} %get-tuple-element.35), channel_id=1, source_target_pairs={{0,2},{2,0},{1,3},{3,1},{4,6},{6,4},{5,7},{7,5},{8,10},{10,8},{9,1... | collective-permute-start | bytes 786440 | tf_op jit(solution)/shard_map/ppermute | solution.py:32
  57.7 6.5 %collective-permute-start.16 = (bf16[2,2,128,256]{3,2,1,0:T(8,128)(2,1)S(1)}, bf16[2,2,128,256]{3,2,1,0:T(8,128)(2,1)S(1)}, u32[]{:S(2)}, u32[]{:S(2)}) collective-permute-start(bf16[2,2,128,256]{3,2,1,0:T(8,128)(2,1)S(1)} %summed.4.refs_1_), channel_id=1, source_target_pairs={{0,2},{2,0},{1,3},{3,1},{4,6},{6,4},{5,7},{7,5},{8,10},{10,8},{9,1... | collective-permute-start | bytes 786440 | tf_op jit(solution)/shard_map/ppermute | solution.py:32
  61.3 3.0 %collective-permute-start.17 = (bf16[3,2,128,256]{3,2,1,0:T(8,128)(2,1)S(1)}, bf16[3,2,128,256]{3,2,1,0:T(8,128)(2,1)S(1)}, u32[]{:S(2)}, u32[]{:S(2)}) collective-permute-start(bf16[3,2,128,256]{3,2,1,0:T(8,128)(2,1)S(1)} %get-tuple-element.43), channel_id=1, source_target_pairs={{0,1},{1,0},{2,3},{3,2},{4,5},{5,4},{6,7},{7,6},{8,9},{9,8},{10,11... | collective-permute-start | bytes 1179656 | tf_op jit(solution)/shard_map/ppermute | solution.py:36
  64.2 1.8 %collective-permute-start.18 = (bf16[3,2,128,256]{3,2,1,0:T(8,128)(2,1)S(1)}, bf16[3,2,128,256]{3,2,1,0:T(8,128)(2,1)S(1)}, u32[]{:S(2)}, u32[]{:S(2)}) collective-permute-start(bf16[3,2,128,256]{3,2,1,0:T(8,128)(2,1)S(1)} %get-tuple-element.44), channel_id=1, source_target_pairs={{0,1},{1,0},{2,3},{3,2},{4,5},{5,4},{6,7},{7,6},{8,9},{9,8},{10,11... | collective-permute-start | bytes 1179656 | tf_op jit(solution)/shard_map/ppermute | solution.py:36

commit v11 on v9

--- a/solution.py
+++ b/solution.py
@@ -338,9 +338,9 @@
         first_dq = dq[0]
         dq = [dq[0]] + [round_sub(dq[by], by) for by in others]
         if last:
-            later = [along_blocks(value, -1, False) for value in early[1:]]
+            later = [along_blocks(value, -1, True) for value in early[1:]]
             dkv = summed(grads, later, others, dq[1:])
-            near = along_blocks(relayed(early[0], dkv), -1, False)
+            near = along_blocks(relayed(early[0], dkv), -1, True)
             dkv = summed(grads, [near], [0], []) + [round_sub(value, by) for by, value in zip(others, dkv)]
         else:
             dkv = summed(grads, [along_blocks(early[0], -1, False)], [0] + others, dq[1:])

time: 62.4 us -> 65.1 us (1.043)
  waiting for transfers between devices: 24.9 us -> 26.7 us
  starting transfers between devices: 22.3 us -> 23.3 us
    ppermute x7, starting transfers between devices: 10.4 us -> 13.2 us  [along_blocks(): return lax.ppermute(value, 'blk', pairs)]
    ppermute x8, waiting for transfers between devices: 12.3 us -> 14.6 us  [round_sub(): lax.ppermute(value, 'sub', [(i, (i + by) % peers) for i in range(peers)])]
    ppermute x8, starting transfers between devices: 10.6 us -> 8.83 us  [round_sub(): lax.ppermute(value, 'sub', [(i, (i + by) % peers) for i in range(peers)])]
  transfers between devices with their start and end apart: 20 -> 20, of which waited for: 10 -> 9; matrix products, arithmetic and copies ran while one was open for 1% -> 1% of each run, Pallas kernels for 17% -> 16%
where the time goes in v11:
time: 65.1 us; the launch traced here: 64.9 us
  waiting for transfers between devices  26.7 us (41%)
  starting transfers between devices  23.3 us (36%)
  Pallas kernels  13.1 us (20%)
  between operations  0.88 us (1%)
  other arithmetic  0.79 us (1%)
    ppermute x8, waiting for transfers between devices, round_sub(): lax.ppermute(value, 'sub', [(i, (i + by) % peers) for i in range(peers)])  14.6 us
    ppermute x7, starting transfers between devices, along_blocks(): return lax.ppermute(value, 'blk', pairs)  13.2 us
    ppermute x7, waiting for transfers between devices, along_blocks(): return lax.ppermute(value, 'blk', pairs)  10.4 us
    pallas_call x18, Pallas kernels, call(): pl.pallas_call(kernel, out_shape=outs, in_specs=[spec] * len(ins), out_sp...  10.3 us
    ppermute x8, starting transfers between devices, round_sub(): lax.ppermute(value, 'sub', [(i, (i + by) % peers) for i in range(peers)])  8.83 us
    pallas_call x2, Pallas kernels, first_parts(): pl.pallas_call(kernel, out_shape=outs, in_specs=[spec] * (len(held) + len...  2.78 us
    ppermute x5, waiting for transfers between devices, swapped(): return lax.ppermute(value, 'pair', [(0, 1), (1, 0)])  1.71 us
  transfers between devices with their start and end apart: 20, of which 9 were waited for; matrix products, arithmetic and copies ran while one was open for 1% of the time, Pallas kernels for 16%

profile of v11, /device:TPU:0, one launch (start us, length us, event | category | flops | bytes accessed | tf_op | source)
XLA Modules:
  0.0 64.9 jit_solution(8521724920240645318)
XLA Ops:
  0.6 1.1 %first_parts.2 = (bf16[2,2,128,256]{3,2,1,0:T(8,128)(2,1)S(1)}, bf16[2,2,128,256]{3,2,1,0:T(8,128)(2,1)S(1)}) custom-call(bf16[128,2048]{1,0:T(8,128)(2,1)} %refs_2_.1, bf16[128,2048]{1,0:T(8,128)(2,1)} %refs_3_.1), custom_call_target="tpu_custom_call" | custom-call | tf_op jit(solution)/shard_map/first_parts/pallas_call | solution.py:92
  1.8 0.5 collective-permute-start
  2.3 1.6 %first_parts.3 = (bf16[2,2,128,256]{3,2,1,0:T(8,128)(2,1)S(1)}, bf16[2,2,128,256]{3,2,1,0:T(8,128)(2,1)S(1)}, bf16[4,2,128,256]{3,2,1,0:T(8,128)(2,1)S(1)}, bf16[4,2,128,256]{3,2,1,0:T(8,128)(2,1)S(1)}) custom-call(bf16[128,2048]{1,0:T(8,128)(2,1)} %refs_4_.1, bf16[128,2048]{1,0:T(8,128)(2,1)} %refs_5_.1, bf16[128,2048]{1,0:T(8,128)(2,1)} %refs_2_.1, ...), custom_call_target="tpu_custom_call" | custom-call | tf_op jit(solution)/shard_map/first_parts/pallas_call | solution.py:92
  3.9 0.1 collective-permute-start.4
  4.1 0.5 collective-permute-start.9
  4.6 0.1 pad_dynamic-slice_fusion
  4.7 0.2 head_parts.9
  4.8 2.6 %collective-permute-start.1 = (bf16[2,2,128,256]{3,2,1,0:T(8,128)(2,1)S(1)}, bf16[2,2,128,256]{3,2,1,0:T(8,128)(2,1)S(1)}, u32[]{:S(2)}, u32[]{:S(2)}) collective-permute-start(bf16[2,2,128,256]{3,2,1,0:T(8,128)(2,1)S(1)} %head_parts.9), channel_id=1, source_target_pairs={{0,2},{2,0},{1,3},{3,1},{4,6},{6,4},{5,7},{7,5},{8,10},{10,8},{9,1... | collective-permute-start | bytes 786440 | tf_op jit(solution)/shard_map/ppermute | solution.py:32
  7.5 0.2 head_parts.8.refs_1_
  7.7 1.6 %collective-permute-start.2 = (bf16[2,2,128,256]{3,2,1,0:T(8,128)(2,1)S(1)}, bf16[2,2,128,256]{3,2,1,0:T(8,128)(2,1)S(1)}, u32[]{:S(2)}, u32[]{:S(2)}) collective-permute-start(bf16[2,2,128,256]{3,2,1,0:T(8,128)(2,1)S(1)} %head_parts.8.refs_1_), channel_id=1, source_target_pairs={{0,4},{4,8},{8,12},{12,0},{1,5},{5,9},{9,13},{13,1},{2,6},{6,10},{... | collective-permute-start | bytes 786440 | tf_op jit(solution)/shard_map/ppermute | solution.py:27
  9.3 0.2 head_parts.11
  9.5 0.6 collective-permute-start.5
  10.1 4.5 %collective-permute-done.1.refs_2_.refs_0_ = bf16[2,2,128,256]{3,2,1,0:T(8,128)(2,1)S(1)} collective-permute-done((bf16[2,2,128,256]{3,2,1,0:T(8,128)(2,1)S(1)}, bf16[2,2,128,256]{3,2,1,0:T(8,128)(2,1)S(1)}, u32[]{:S(2)}, u32[]{:S(2)}) %collective-permute-start.1) | collective-permute-done | bytes 262176 | tf_op jit(solution)/shard_map/ppermute | solution.py:32
  14.6 0.2 head_parts.13
  14.8 2.0 %collective-permute-start.10 = (bf16[2,2,128,256]{3,2,1,0:T(8,128)(2,1)S(1)}, bf16[2,2,128,256]{3,2,1,0:T(8,128)(2,1)S(1)}, u32[]{:S(2)}, u32[]{:S(2)}) collective-permute-start(bf16[2,2,128,256]{3,2,1,0:T(8,128)(2,1)S(1)} %head_parts.13), channel_id=1, source_target_pairs={{0,2},{2,0},{1,3},{3,1},{4,6},{6,4},{5,7},{7,5},{8,10},{10,8},{9,1... | collective-permute-start | bytes 786440 | tf_op jit(solution)/shard_map/ppermute | solution.py:32
  16.8 1.6 %collective-permute-start.3 = (bf16[2,2,128,256]{3,2,1,0:T(8,128)(2,1)S(1)}, bf16[2,2,128,256]{3,2,1,0:T(8,128)(2,1)S(1)}, u32[]{:S(2)}, u32[]{:S(2)}) collective-permute-start(bf16[2,2,128,256]{3,2,1,0:T(8,128)(2,1)S(1)} %collective-permute-done.1.refs_2_.refs_0_), channel_id=1, source_target_pairs={{0,4},{4,8},{8,12},{12,0},{1,5},{5,9},{9,13},{13,1},{2,6},{6,10},{... | collective-permute-start | bytes 786440 | tf_op jit(solution)/shard_map/ppermute | solution.py:27
  18.4 0.7 %and_select_fusion = (f32[1,768,256]{2,1,0:T(8,128)S(1)}, f32[1,768,256]{2,1,0:T(8,128)S(1)}) fusion(s32[256]{0:T(256)S(1)} %get-tuple-element.54, s32[256]{0:T(256)S(1)} %get-tuple-element.52, s32[768]{0:T(1024)S(1)} %get-tuple-element.50, s32[768]{0:T(1024)S(1)} %get-tuple-element.48, pred[768]{0:T(1024)(128)(4,1)S(1)} %get-tuple-element.46, ...), kind=kLoop, calls=%fused_computation.1 | loop fusion | flops 1966080 | bytes 1590784 | tf_op jit(solution)/shard_map/jit(_where)/select_n | solution.py:299
  19.1 0.1 pad_maximum_fusion.refs_0_
  19.2 0.2 head_parts.10.refs_5_
  19.4 0.2 head_parts.12.refs_1_
  19.6 1.6 %collective-permute-start.11 = (bf16[2,2,128,256]{3,2,1,0:T(8,128)(2,1)S(1)}, bf16[2,2,128,256]{3,2,1,0:T(8,128)(2,1)S(1)}, u32[]{:S(2)}, u32[]{:S(2)}) collective-permute-start(bf16[2,2,128,256]{3,2,1,0:T(8,128)(2,1)S(1)} %head_parts.12.refs_1_), channel_id=1, source_target_pairs={{0,4},{4,8},{8,12},{12,0},{1,5},{5,9},{9,13},{13,1},{2,6},{6,10},{... | collective-permute-start | bytes 786440 | tf_op jit(solution)/shard_map/ppermute | solution.py:27
  21.3 0.2 head_parts.15
  21.4 1.0 %collective-permute-start.13 = (bf16[2,2,128,256]{3,2,1,0:T(8,128)(2,1)S(1)}, bf16[2,2,128,256]{3,2,1,0:T(8,128)(2,1)S(1)}, u32[]{:S(2)}, u32[]{:S(2)}) collective-permute-start(bf16[2,2,128,256]{3,2,1,0:T(8,128)(2,1)S(1)} %head_parts.15), channel_id=1, source_target_pairs={{0,2},{2,0},{1,3},{3,1},{4,6},{6,4},{5,7},{7,5},{8,10},{10,8},{9,1... | collective-permute-start | bytes 786440 | tf_op jit(solution)/shard_map/ppermute | solution.py:32
  22.4 5.4 %collective-permute-done.3.refs_4_ = bf16[2,2,128,256]{3,2,1,0:T(8,128)(2,1)S(1)} collective-permute-done((bf16[2,2,128,256]{3,2,1,0:T(8,128)(2,1)S(1)}, bf16[2,2,128,256]{3,2,1,0:T(8,128)(2,1)S(1)}, u32[]{:S(2)}, u32[]{:S(2)}) %collective-permute-start.3) | collective-permute-done | bytes 262176 | tf_op jit(solution)/shard_map/ppermute | solution.py:27
  27.9 3.5 %attention_grads.2 = (f32[2,2,2,128,256]{4,3,2,1,0:T(8,128)S(1)}, bf16[2,128,256]{2,1,0:T(8,128)(2,1)S(1)}, bf16[2,128,256]{2,1,0:T(8,128)(2,1)S(1)}, bf16[2,2,2,128,256]{4,3,2,1,0:T(8,128)(2,1)S(1)}) custom-call(f32[2,768,256]{2,1,0:T(8,128)S(1)} %pad_maximum_fusion.refs_0_, bf16[2,2,128,256]{3,2,1,0:T(8,128)(2,1)S(1)} %head_parts.8.refs_1_, ...), custom_call_target="tpu_custom_call" | custom-call | flops 1006632960 | bytes 4980736 | tf_op jit(solution)/shard_map/attention_grads/pallas_call | solution.py:51
  31.5 1.7 %collective-permute-start.12 = (bf16[2,2,128,256]{3,2,1,0:T(8,128)(2,1)S(1)}, bf16[2,2,128,256]{3,2,1,0:T(8,128)(2,1)S(1)}, u32[]{:S(2)}, u32[]{:S(2)}) collective-permute-start(bf16[2,2,128,256]{3,2,1,0:T(8,128)(2,1)S(1)} %relayed.2), channel_id=1, source_target_pairs={{0,4},{4,8},{8,12},{1,5},{5,9},{9,13},{2,6},{6,10},{10,14},{3,7},{... | collective-permute-start | bytes 786440 | tf_op jit(solution)/shard_map/ppermute | solution.py:27
  33.2 1.3 %collective-permute-start.7 = (bf16[2,2,2,128,256]{4,3,2,1,0:T(8,128)(2,1)S(1)}, bf16[2,2,2,128,256]{4,3,2,1,0:T(8,128)(2,1)S(1)}, u32[]{:S(2)}, u32[]{:S(2)}) collective-permute-start(bf16[2,2,2,128,256]{4,3,2,1,0:T(8,128)(2,1)S(1)} %get-tuple-element.31), channel_id=1, source_target_pairs={{4,0},{8,4},{12,8},{5,1},{9,5},{13,9},{6,2},{10,6},{14,10},{7,3},{... | collective-permute-start | bytes 1572872 | tf_op jit(solution)/shard_map/ppermute | solution.py:27
  34.5 0.2 head_parts.14.refs_5_
  34.7 2.3 %collective-permute-done.12.refs_4_ = bf16[2,2,128,256]{3,2,1,0:T(8,128)(2,1)S(1)} collective-permute-done((bf16[2,2,128,256]{3,2,1,0:T(8,128)(2,1)S(1)}, bf16[2,2,128,256]{3,2,1,0:T(8,128)(2,1)S(1)}, u32[]{:S(2)}, u32[]{:S(2)}) %collective-permute-start.12) | collective-permute-done | bytes 262176 | tf_op jit(solution)/shard_map/ppermute | solution.py:27
  37.0 3.5 %attention_grads.3 = (f32[2,2,2,128,256]{4,3,2,1,0:T(8,128)S(1)}, bf16[2,128,256]{2,1,0:T(8,128)(2,1)S(1)}, bf16[2,128,256]{2,1,0:T(8,128)(2,1)S(1)}, bf16[2,2,1...) custom-call(f32[2,768,256]{2,1,0:T(8,128)S(1)} %pad_maximum_fusion.refs_0_, ...), custom_call_target="tpu_custom_call" | custom-call | flops 1006632960 | bytes 4980736 | tf_op jit(solution)/shard_map/attention_grads/pallas_call | solution.py:51
  40.6 4.6 %collective-permute-start.15 = (bf16[2,2,128,256]{3,2,1,0:T(8,128)(2,1)S(1)}, bf16[2,2,128,256]{3,2,1,0:T(8,128)(2,1)S(1)}, u32[]{:S(2)}, u32[]{:S(2)}) collective-permute-start(bf16[2,2,128,256]{3,2,1,0:T(8,128)(2,1)S(1)} %get-tuple-element.41), channel_id=1, source_target_pairs={{0,12},{4,0},{8,4},{12,8},{1,13},{5,1},{9,5},{13,9},{2,14},{6,2},{... | collective-permute-start | bytes 786440 | tf_op jit(solution)/shard_map/ppermute | solution.py:27
  45.1 0.5 collective-permute-start.6
  45.7 1.5 %collective-permute-start.14 = (bf16[2,128,256]{2,1,0:T(8,128)(2,1)S(1)}, bf16[2,128,256]{2,1,0:T(8,128)(2,1)S(1)}, u32[]{:S(2)}, u32[]{:S(2)}) collective-permute-start(bf16[2,128,256]{2,1,0:T(8,128)(2,1)S(1)} %get-tuple-element.38), channel_id=1, source_target_pairs={{0,2},{2,0},{1,3},{3,1},{4,6},{6,4},{5,7},{7,5},{8,10},{10,8},{9,1... | collective-permute-start | bytes 393224 | tf_op jit(solution)/shard_map/ppermute | solution.py:32
  47.2 4.4 %collective-permute-done.6.refs_1_ = bf16[2,128,256]{2,1,0:T(8,128)(2,1)S(1)} collective-permute-done((bf16[2,128,256]{2,1,0:T(8,128)(2,1)S(1)}, bf16[2,128,256]{2,1,0:T(8,128)(2,1)S(1)}, u32[]{:S(2)}, u32[]{:S(2)}) %collective-permute-start.6) | collective-permute-done | bytes 131104 | tf_op jit(solution)/shard_map/ppermute | solution.py:32
  51.6 0.1 summed.3
  51.7 0.6 collective-permute-start.8
  52.2 2.1 %collective-permute-done.14.refs_1_ = bf16[2,128,256]{2,1,0:T(8,128)(2,1)S(1)} collective-permute-done((bf16[2,128,256]{2,1,0:T(8,128)(2,1)S(1)}, bf16[2,128,256]{2,1,0:T(8,128)(2,1)S(1)}, u32[]{:S(2)}, u32[]{:S(2)}) %collective-permute-start.14) | collective-permute-done | bytes 131104 | tf_op jit(solution)/shard_map/ppermute | solution.py:32
  54.4 0.1 summed.4.refs_0_
  54.5 0.8 %collective-permute-start.16 = (bf16[2,2,128,256]{3,2,1,0:T(8,128)(2,1)S(1)}, bf16[2,2,128,256]{3,2,1,0:T(8,128)(2,1)S(1)}, u32[]{:S(2)}, u32[]{:S(2)}) collective-permute-start(bf16[2,2,128,256]{3,2,1,0:T(8,128)(2,1)S(1)} %relayed.3), channel_id=1, source_target_pairs={{0,12},{4,0},{8,4},{12,8},{1,13},{5,1},{9,5},{13,9},{2,14},{6,2},{... | collective-permute-start | bytes 786440 | tf_op jit(solution)/shard_map/ppermute | solution.py:27
  55.3 2.8 %collective-permute-done.8.refs_3_ = bf16[2,2,128,256]{3,2,1,0:T(8,128)(2,1)S(1)} collective-permute-done((bf16[2,2,128,256]{3,2,1,0:T(8,128)(2,1)S(1)}, bf16[2,2,128,256]{3,2,1,0:T(8,128)(2,1)S(1)}, u32[]{:S(2)}, u32[]{:S(2)}) %collective-permute-start.8) | collective-permute-done | bytes 262176 | tf_op jit(solution)/shard_map/ppermute | solution.py:32
  58.1 0.1 rows_for_pair.2
  58.2 0.1 collective-permute-start.18
  58.2 2.7 %collective-permute-done.16.refs_0_ = bf16[2,2,128,256]{3,2,1,0:T(8,128)(2,1)S(1)} collective-permute-done((bf16[2,2,128,256]{3,2,1,0:T(8,128)(2,1)S(1)}, bf16[2,2,128,256]{3,2,1,0:T(8,128)(2,1)S(1)}, u32[]{:S(2)}, u32[]{:S(2)}) %collective-permute-start.16) | collective-permute-done | bytes 262176 | tf_op jit(solution)/shard_map/ppermute | solution.py:27
  61.0 0.7 %collective-permute-done.17.refs_3_ = bf16[2,2,128,256]{3,2,1,0:T(8,128)(2,1)S(1)} collective-permute-done((bf16[2,2,128,256]{3,2,1,0:T(8,128)(2,1)S(1)}, bf16[2,2,128,256]{3,2,1,0:T(8,128)(2,1)S(1)}, u32[]{:S(2)}, u32[]{:S(2)}) %collective-permute-start.17) | collective-permute-done | bytes 262176 | tf_op jit(solution)/shard_map/ppermute | solution.py:32
  61.7 0.1 rows_for_pair.3
  61.7 0.1 collective-permute-start.19
  61.8 1.7 %collective-permute-done.19.refs_3_ = bf16[3,2,128,256]{3,2,1,0:T(8,128)(2,1)S(1)} collective-permute-done((bf16[3,2,128,256]{3,2,1,0:T(8,128)(2,1)S(1)}, bf16[3,2,128,256]{3,2,1,0:T(8,128)(2,1)S(1)}, u32[]{:S(2)}, u32[]{:S(2)}) %collective-permute-start.19) | collective-permute-done | bytes 393248 | tf_op jit(solution)/shard_map/ppermute | solution.py:36
  63.5 1.3 %laid_out.1 = (bf16[128,2048]{1,0:T(8,128)(2,1)}, bf16[128,2048]{1,0:T(8,128)(2,1)}, bf16[128,2048]{1,0:T(8,128)(2,1)}) custom-call(bf16[3,2,128,256]{3,2,1,0:T(8,128)(2,1)S(1)} %get-tuple-element.34.refs_0_, bf16[3,2,128,256]{3,2,1,0:T(8,128)(2,1)S(1)} %get-tuple-element.42.refs_1_, bf16[3,2,128,256]{3,2,1,0:T(8,128)(2,1)S(1)} %collective-permute-done.18.refs_2_, ...), custom_call_target="tpu_custom_call" | custom-call | bytes 3145728 | tf_op jit(solution)/shard_map/laid_out/pallas_call | solution.py:51
  (23 shorter events, 0.2 us)
Async XLA Ops:
  1.8 2.9 %collective-permute-start = (bf16[2,2,128,256]{3,2,1,0:T(8,128)(2,1)S(1)}, bf16[2,2,128,256]{3,2,1,0:T(8,128)(2,1)S(1)}, u32[]{:S(2)}, u32[]{:S(2)}) collective-permute-start(bf16[2,2,128,256]{3,2,1,0:T(8,128)(2,1)S(1)} %get-tuple-element.25), channel_id=1, source_target_pairs={{0,1},{1,0},{2,3},{3,2},{4,5},{5,4},{6,7},{7,6},{8,9},{9,8},{10,11... | collective-permute-start | bytes 786440 | tf_op jit(solution)/shard_map/ppermute | solution.py:36
  2.3 2.3 %copy-start = (s32[2048]{0:T(1024)S(1)}, s32[2048]{0:T(1024)}, u32[]{:S(2)}) copy-start(s32[2048]{0:T(1024)} %param.9) | copy-start | bytes 24580
  3.9 5.3 %collective-permute-start.4 = (bf16[2,2,128,256]{3,2,1,0:T(8,128)(2,1)S(1)}, bf16[2,2,128,256]{3,2,1,0:T(8,128)(2,1)S(1)}, u32[]{:S(2)}, u32[]{:S(2)}) collective-permute-start(bf16[2,2,128,256]{3,2,1,0:T(8,128)(2,1)S(1)} %get-tuple-element.27), channel_id=1, source_target_pairs={{0,1},{1,0},{2,3},{3,2},{4,5},{5,4},{6,7},{7,6},{8,9},{9,8},{10,11... | collective-permute-start | bytes 786440 | tf_op jit(solution)/shard_map/ppermute | solution.py:36
  4.1 10.6 %collective-permute-start.9 = (bf16[4,2,128,256]{3,2,1,0:T(8,128)(2,1)S(1)}, bf16[4,2,128,256]{3,2,1,0:T(8,128)(2,1)S(1)}, u32[]{:S(2)}, u32[]{:S(2)}) collective-permute-start(bf16[4,2,128,256]{3,2,1,0:T(8,128)(2,1)S(1)} %get-tuple-element.36), channel_id=1, source_target_pairs={{0,1},{1,0},{2,3},{3,2},{4,5},{5,4},{6,7},{7,6},{8,9},{9,8},{10,11... | collective-permute-start | bytes 1572872 | tf_op jit(solution)/shard_map/ppermute | solution.py:36
  4.8 9.8 %collective-permute-start.1 = (bf16[2,2,128,256]{3,2,1,0:T(8,128)(2,1)S(1)}, bf16[2,2,128,256]{3,2,1,0:T(8,128)(2,1)S(1)}, u32[]{:S(2)}, u32[]{:S(2)}) collective-permute-start(bf16[2,2,128,256]{3,2,1,0:T(8,128)(2,1)S(1)} %head_parts.9), channel_id=1, source_target_pairs={{0,2},{2,0},{1,3},{3,1},{4,6},{6,4},{5,7},{7,5},{8,10},{10,8},{9,1... | collective-permute-start | bytes 786440 | tf_op jit(solution)/shard_map/ppermute | solution.py:32
  7.7 11.7 %collective-permute-start.2 = (bf16[2,2,128,256]{3,2,1,0:T(8,128)(2,1)S(1)}, bf16[2,2,128,256]{3,2,1,0:T(8,128)(2,1)S(1)}, u32[]{:S(2)}, u32[]{:S(2)}) collective-permute-start(bf16[2,2,128,256]{3,2,1,0:T(8,128)(2,1)S(1)} %head_parts.8.refs_1_), channel_id=1, source_target_pairs={{0,4},{4,8},{8,12},{12,0},{1,5},{5,9},{9,13},{13,1},{2,6},{6,10},{... | collective-permute-start | bytes 786440 | tf_op jit(solution)/shard_map/ppermute | solution.py:27
  9.5 11.8 %collective-permute-start.5 = (bf16[2,2,128,256]{3,2,1,0:T(8,128)(2,1)S(1)}, bf16[2,2,128,256]{3,2,1,0:T(8,128)(2,1)S(1)}, u32[]{:S(2)}, u32[]{:S(2)}) collective-permute-start(bf16[2,2,128,256]{3,2,1,0:T(8,128)(2,1)S(1)} %head_parts.11), channel_id=1, source_target_pairs={{0,2},{2,0},{1,3},{3,1},{4,6},{6,4},{5,7},{7,5},{8,10},{10,8},{9,1... | collective-permute-start | bytes 786440 | tf_op jit(solution)/shard_map/ppermute | solution.py:32
  14.8 16.6 %collective-permute-start.10 = (bf16[2,2,128,256]{3,2,1,0:T(8,128)(2,1)S(1)}, bf16[2,2,128,256]{3,2,1,0:T(8,128)(2,1)S(1)}, u32[]{:S(2)}, u32[]{:S(2)}) collective-permute-start(bf16[2,2,128,256]{3,2,1,0:T(8,128)(2,1)S(1)} %head_parts.13), channel_id=1, source_target_pairs={{0,2},{2,0},{1,3},{3,1},{4,6},{6,4},{5,7},{7,5},{8,10},{10,8},{9,1... | collective-permute-start | bytes 786440 | tf_op jit(solution)/shard_map/ppermute | solution.py:32
  16.8 11.0 %collective-permute-start.3 = (bf16[2,2,128,256]{3,2,1,0:T(8,128)(2,1)S(1)}, bf16[2,2,128,256]{3,2,1,0:T(8,128)(2,1)S(1)}, u32[]{:S(2)}, u32[]{:S(2)}) collective-permute-start(bf16[2,2,128,256]{3,2,1,0:T(8,128)(2,1)S(1)} %collective-permute-done.1.refs_2_.refs_0_), channel_id=1, source_target_pairs={{0,4},{4,8},{8,12},{12,0},{1,5},{5,9},{9,13},{13,1},{2,6},{6,10},{... | collective-permute-start | bytes 786440 | tf_op jit(solution)/shard_map/ppermute | solution.py:27
  19.6 15.1 %collective-permute-start.11 = (bf16[2,2,128,256]{3,2,1,0:T(8,128)(2,1)S(1)}, bf16[2,2,128,256]{3,2,1,0:T(8,128)(2,1)S(1)}, u32[]{:S(2)}, u32[]{:S(2)}) collective-permute-start(bf16[2,2,128,256]{3,2,1,0:T(8,128)(2,1)S(1)} %head_parts.12.refs_1_), channel_id=1, source_target_pairs={{0,4},{4,8},{8,12},{12,0},{1,5},{5,9},{9,13},{13,1},{2,6},{6,10},{... | collective-permute-start | bytes 786440 | tf_op jit(solution)/shard_map/ppermute | solution.py:27
  21.4 13.2 %collective-permute-start.13 = (bf16[2,2,128,256]{3,2,1,0:T(8,128)(2,1)S(1)}, bf16[2,2,128,256]{3,2,1,0:T(8,128)(2,1)S(1)}, u32[]{:S(2)}, u32[]{:S(2)}) collective-permute-start(bf16[2,2,128,256]{3,2,1,0:T(8,128)(2,1)S(1)} %head_parts.15), channel_id=1, source_target_pairs={{0,2},{2,0},{1,3},{3,1},{4,6},{6,4},{5,7},{7,5},{8,10},{10,8},{9,1... | collective-permute-start | bytes 786440 | tf_op jit(solution)/shard_map/ppermute | solution.py:32
  31.5 5.6 %collective-permute-start.12 = (bf16[2,2,128,256]{3,2,1,0:T(8,128)(2,1)S(1)}, bf16[2,2,128,256]{3,2,1,0:T(8,128)(2,1)S(1)}, u32[]{:S(2)}, u32[]{:S(2)}) collective-permute-start(bf16[2,2,128,256]{3,2,1,0:T(8,128)(2,1)S(1)} %relayed.2), channel_id=1, source_target_pairs={{0,4},{4,8},{8,12},{1,5},{5,9},{9,13},{2,6},{6,10},{10,14},{3,7},{... | collective-permute-start | bytes 786440 | tf_op jit(solution)/shard_map/ppermute | solution.py:27
  33.2 18.4 %collective-permute-start.7 = (bf16[2,2,2,128,256]{4,3,2,1,0:T(8,128)(2,1)S(1)}, bf16[2,2,2,128,256]{4,3,2,1,0:T(8,128)(2,1)S(1)}, u32[]{:S(2)}, u32[]{:S(2)}) collective-permute-start(bf16[2,2,2,128,256]{4,3,2,1,0:T(8,128)(2,1)S(1)} %get-tuple-element.31), channel_id=1, source_target_pairs={{4,0},{8,4},{12,8},{5,1},{9,5},{13,9},{6,2},{10,6},{14,10},{7,3},{... | collective-permute-start | bytes 1572872 | tf_op jit(solution)/shard_map/ppermute | solution.py:27
  40.6 13.8 %collective-permute-start.15 = (bf16[2,2,128,256]{3,2,1,0:T(8,128)(2,1)S(1)}, bf16[2,2,128,256]{3,2,1,0:T(8,128)(2,1)S(1)}, u32[]{:S(2)}, u32[]{:S(2)}) collective-permute-start(bf16[2,2,128,256]{3,2,1,0:T(8,128)(2,1)S(1)} %get-tuple-element.41), channel_id=1, source_target_pairs={{0,12},{4,0},{8,4},{12,8},{1,13},{5,1},{9,5},{13,9},{2,14},{6,2},{... | collective-permute-start | bytes 786440 | tf_op jit(solution)/shard_map/ppermute | solution.py:27
  45.1 6.4 %collective-permute-start.6 = (bf16[2,128,256]{2,1,0:T(8,128)(2,1)S(1)}, bf16[2,128,256]{2,1,0:T(8,128)(2,1)S(1)}, u32[]{:S(2)}, u32[]{:S(2)}) collective-permute-start(bf16[2,128,256]{2,1,0:T(8,128)(2,1)S(1)} %get-tuple-element.29), channel_id=1, source_target_pairs={{0,2},{2,0},{1,3},{3,1},{4,6},{6,4},{5,7},{7,5},{8,10},{10,8},{9,1... | collective-permute-start | bytes 393224 | tf_op jit(solution)/shard_map/ppermute | solution.py:32
  45.7 8.7 %collective-permute-start.14 = (bf16[2,128,256]{2,1,0:T(8,128)(2,1)S(1)}, bf16[2,128,256]{2,1,0:T(8,128)(2,1)S(1)}, u32[]{:S(2)}, u32[]{:S(2)}) collective-permute-start(bf16[2,128,256]{2,1,0:T(8,128)(2,1)S(1)} %get-tuple-element.38), channel_id=1, source_target_pairs={{0,2},{2,0},{1,3},{3,1},{4,6},{6,4},{5,7},{7,5},{8,10},{10,8},{9,1... | collective-permute-start | bytes 393224 | tf_op jit(solution)/shard_map/ppermute | solution.py:32
  51.7 6.4 %collective-permute-start.8 = (bf16[2,2,128,256]{3,2,1,0:T(8,128)(2,1)S(1)}, bf16[2,2,128,256]{3,2,1,0:T(8,128)(2,1)S(1)}, u32[]{:S(2)}, u32[]{:S(2)}) collective-permute-start(bf16[2,2,128,256]{3,2,1,0:T(8,128)(2,1)S(1)} %get-tuple-element.33), channel_id=1, source_target_pairs={{0,2},{2,0},{1,3},{3,1},{4,6},{6,4},{5,7},{7,5},{8,10},{10,8},{9,1... | collective-permute-start | bytes 786440 | tf_op jit(solution)/shard_map/ppermute | solution.py:32
  54.5 6.4 %collective-permute-start.16 = (bf16[2,2,128,256]{3,2,1,0:T(8,128)(2,1)S(1)}, bf16[2,2,128,256]{3,2,1,0:T(8,128)(2,1)S(1)}, u32[]{:S(2)}, u32[]{:S(2)}) collective-permute-start(bf16[2,2,128,256]{3,2,1,0:T(8,128)(2,1)S(1)} %relayed.3), channel_id=1, source_target_pairs={{0,12},{4,0},{8,4},{12,8},{1,13},{5,1},{9,5},{13,9},{2,14},{6,2},{... | collective-permute-start | bytes 786440 | tf_op jit(solution)/shard_map/ppermute | solution.py:27
  55.3 6.4 %collective-permute-start.17 = (bf16[2,2,128,256]{3,2,1,0:T(8,128)(2,1)S(1)}, bf16[2,2,128,256]{3,2,1,0:T(8,128)(2,1)S(1)}, u32[]{:S(2)}, u32[]{:S(2)}) collective-permute-start(bf16[2,2,128,256]{3,2,1,0:T(8,128)(2,1)S(1)} %summed.4.refs_0_), channel_id=1, source_target_pairs={{0,2},{2,0},{1,3},{3,1},{4,6},{6,4},{5,7},{7,5},{8,10},{10,8},{9,1... | collective-permute-start | bytes 786440 | tf_op jit(solution)/shard_map/ppermute | solution.py:32
  58.2 3.7 %collective-permute-start.18 = (bf16[3,2,128,256]{3,2,1,0:T(8,128)(2,1)S(1)}, bf16[3,2,128,256]{3,2,1,0:T(8,128)(2,1)S(1)}, u32[]{:S(2)}, u32[]{:S(2)}) collective-permute-start(bf16[3,2,128,256]{3,2,1,0:T(8,128)(2,1)S(1)} %get-tuple-element.43), channel_id=1, source_target_pairs={{0,1},{1,0},{2,3},{3,2},{4,5},{5,4},{6,7},{7,6},{8,9},{9,8},{10,11... | collective-permute-start | bytes 1179656 | tf_op jit(solution)/shard_map/ppermute | solution.py:36
  61.7 1.8 %collective-permute-start.19 = (bf16[3,2,128,256]{3,2,1,0:T(8,128)(2,1)S(1)}, bf16[3,2,128,256]{3,2,1,0:T(8,128)(2,1)S(1)}, u32[]{:S(2)}, u32[]{:S(2)}) collective-permute-start(bf16[3,2,128,256]{3,2,1,0:T(8,128)(2,1)S(1)} %get-tuple-element.44), channel_id=1, source_target_pairs={{0,1},{1,0},{2,3},{3,2},{4,5},{5,4},{6,7},{7,6},{8,9},{9,8},{10,11... | collective-permute-start | bytes 1179656 | tf_op jit(solution)/shard_map/ppermute | solution.py:36

commit v12 on v9

--- a/solution.py
+++ b/solution.py
@@ -101,6 +101,71 @@
     return [(parts[2 * i], parts[2 * i + 1]) for i in range(len(groups))]
 
 
+def first_keys(arrays, low, high):
+    rows, width = arrays[0].shape
+    half = width // 2
+    peers = lax.axis_size("sub")
+    part = half // peers
+    cut = high - low
+
+    def kernel(*refs):
+        ins, far, (send, keep), sems = refs[:2], refs[2:1 + peers], refs[1 + peers:-1], refs[-1]
+        p, s = lax.axis_index("pair"), lax.axis_index("sub")
+        moves = []
+        for i, ref in enumerate(ins):
+            for by in range(1, peers):
+                for side in range(2):
+                    start = pl.multiple_of(side * half + lax.rem(s + by, peers) * part + low, HD)
+                    moves.append((ref.at[:, pl.ds(start, cut)], far[by - 1].at[i, side]))
+            for out, side in ((send, 1 - p), (keep, p)):
+                start = pl.multiple_of(side * half + s * part + low, HD)
+                moves.append((ref.at[:, pl.ds(start, cut)], out.at[i]))
+        run_moves(moves, sems)
+
+    spec = pl.BlockSpec(memory_space=pl.ANY)
+    outs = [pltpu.VMEM((2, 2, rows, cut), LOW)] * (peers - 1) + [pltpu.VMEM((2, rows, cut), LOW)] * 2
+    parts = pl.pallas_call(
+        kernel,
+        out_shape=outs,
+        in_specs=[spec] * 2,
+        out_specs=[spec] * len(outs),
+        scratch_shapes=[pltpu.SemaphoreType.DMA((4 * peers,))],
+        name="first_keys",
+        compiler_params=pltpu.CompilerParams(vmem_limit_bytes=8 * MIB),
+    )(*[pltpu.with_memory_space_constraint(array, pltpu.HBM) for array in arrays])
+    return list(parts[:-2]), parts[-2], parts[-1]
+
+
+def other_side(received):
+    count = len(received)
+
+    def kernel(*refs):
+        p = lax.axis_index("pair")
+        run_moves([(ref.at[:, 1 - p], refs[-2].at[by]) for by, ref in enumerate(refs[:count])], refs[-1])
+
+    _, _, rows, cut = received[0].shape
+    scratch = [pltpu.SemaphoreType.DMA((count,))]
+    return call(kernel, received, [shape(count, 2, rows, cut)], scratch, "other_side")[0]
+
+
+def both_rows(mine, theirs):
+    count = len(mine)
+    _, _, rows, cut = theirs.shape
+
+    def kernel(*refs):
+        ins, theirs_ref, outs, sems = refs[:count], refs[count], refs[count + 1:-1], refs[-1]
+        p = lax.axis_index("pair")
+        moves = []
+        for by, (ref, out) in enumerate(zip(ins, outs)):
+            source = ref.at[:, p] if len(ref.shape) == 4 else ref
+            moves += [(source, out.at[:, p]), (theirs_ref.at[by], out.at[:, 1 - p])]
+        run_moves(moves, sems)
+
+    outs = [shape(2, 2, rows, cut)] * count
+    scratch = [pltpu.SemaphoreType.DMA((2 * count,))]
+    return call(kernel, mine + [theirs], outs, scratch, "both_rows")
+
+
 def head_parts(own, paired, which, turns, after):
     _, peers, rows, cut = own.shape
     chosen = pl.ds(which, 2)
@@ -310,10 +375,12 @@
         spans.append((at, at + heads * HD))
         at += heads * HD
     bias = allowed_bias(session, queries.shape[0])
-    (kv_send, kv_first), = first_parts([([keys, values], *spans[0])], [])
+    kv_far, near_send, near_keep = first_keys([keys, values], *spans[0])
+    kv_far = [round_sub(value, by) for by, value in zip(others, kv_far)]
     rest = [([queries, out_grad], *spans[0])] + [([keys, values, queries, out_grad], *span) for span in spans[1:]]
-    rest = first_parts(rest, [kv_first])
-    kv_parts = [(kv_first, swapped(kv_send), 0)]
+    rest = first_parts(rest, [near_keep])
+    near_theirs = swapped(near_send)
+    kv_parts = [None]
     qg_parts = [(rest[0][1], swapped(rest[0][0]), 0)]
     for send, own in rest[1:]:
         paired = swapped(send)
@@ -322,9 +389,14 @@
     count = len(spans)
     kv_sends, qg_sends, kv, qg, kv_own, own_earlier = [], [], [], [], [], []
     for index in range(count):
-        kv_sends.append(head_parts(*kv_parts[index], others, kv[index - 1] if index else []))
-        kv.append([round_sub(value, by) for by, value in zip(others, kv_sends[index])])
-        kv_own.append(head_parts(*kv_parts[index], [0], own_earlier[index - 1:index]))
+        if index:
+            kv_sends.append(head_parts(*kv_parts[index], others, kv[index - 1] + own_earlier[index - 1:index]))
+            kv.append([round_sub(value, by) for by, value in zip(others, kv_sends[index])])
+            kv_own.append(head_parts(*kv_parts[index], [0], own_earlier[index - 1:index]))
+        else:
+            kv_sends.append([])
+            kv_own.append(both_rows([near_keep], near_theirs.reshape(1, *near_theirs.shape)))
+            kv.append(both_rows(kv_far, swapped(other_side(kv_far))))
         own_earlier.append(along_blocks(kv_own[index][0], 1, True))
         qg_sends.append(head_parts(*qg_parts[index], others, qg[index - 1] if index else []))
         qg.append([round_sub(value, by) for by, value in zip(others, qg_sends[index])])

time: 62.4 us -> 63.2 us (1.013)
    ppermute x7, waiting for transfers between devices: 10.9 us -> 15.4 us  [along_blocks(): return lax.ppermute(value, 'blk', pairs)]
    ppermute x8, waiting for transfers between devices: 12.3 us -> 8.08 us  [round_sub(): lax.ppermute(value, 'sub', [(i, (i + by) % peers) for i in range(peers)])]
    ppermute x8, starting transfers between devices: 10.6 us -> 12 us  [round_sub(): lax.ppermute(value, 'sub', [(i, (i + by) % peers) for i in range(peers)])]
    pallas_call x0 -> x1, Pallas kernels: none -> 1.15 us  [first_keys(): pl.pallas_call(kernel, out_shape=outs, in_specs=[spec] * 2, out_specs=[sp...]
    pallas_call x2 -> x1, Pallas kernels: 2.78 us -> 1.64 us  [first_parts(): pl.pallas_call(kernel, out_shape=outs, in_specs=[spec] * (len(held) + len...]
    ppermute x7, starting transfers between devices: 10.4 us -> 9.36 us  [along_blocks(): return lax.ppermute(value, 'blk', pairs)]
    pallas_call x18 -> x19, Pallas kernels: 10.3 us -> 10.4 us  [call(): pl.pallas_call(kernel, out_shape=outs, in_specs=[spec] * len(ins), out_sp...]
    ppermute x5 -> x6, starting transfers between devices: 1.24 us -> 1.31 us  [swapped(): return lax.ppermute(value, 'pair', [(0, 1), (1, 0)])]
  transfers between devices with their start and end apart: 20 -> 21, of which waited for: 10 -> 12; matrix products, arithmetic and copies ran while one was open for 1% -> 1% of each run, Pallas kernels for 17% -> 17%
where the time goes in v12:
time: 63.2 us; the launch traced here: 62.8 us
  waiting for transfers between devices  25.2 us (40%)
  starting transfers between devices  22.7 us (36%)
  Pallas kernels  13.2 us (21%)
  between operations  0.91 us (1%)
  other arithmetic  0.79 us (1%)
    ppermute x7, waiting for transfers between devices, along_blocks(): return lax.ppermute(value, 'blk', pairs)  15.4 us
    ppermute x8, starting transfers between devices, round_sub(): lax.ppermute(value, 'sub', [(i, (i + by) % peers) for i in range(peers)])  12 us
    pallas_call x19, Pallas kernels, call(): pl.pallas_call(kernel, out_shape=outs, in_specs=[spec] * len(ins), out_sp...  10.4 us
    ppermute x7, starting transfers between devices, along_blocks(): return lax.ppermute(value, 'blk', pairs)  9.36 us
    ppermute x8, waiting for transfers between devices, round_sub(): lax.ppermute(value, 'sub', [(i, (i + by) % peers) for i in range(peers)])  8.08 us
    ppermute x6, waiting for transfers between devices, swapped(): return lax.ppermute(value, 'pair', [(0, 1), (1, 0)])  1.71 us
    pallas_call x1, Pallas kernels, first_parts(): pl.pallas_call(kernel, out_shape=outs, in_specs=[spec] * (len(held) + len...  1.64 us
    ppermute x6, starting transfers between devices, swapped(): return lax.ppermute(value, 'pair', [(0, 1), (1, 0)])  1.31 us
  transfers between devices with their start and end apart: 21, of which 12 were waited for; matrix products, arithmetic and copies ran while one was open for 1% of the time, Pallas kernels for 17%

profile of v12, /device:TPU:0, one launch (start us, length us, event | category | flops | bytes accessed | tf_op | source)
XLA Modules:
  0.0 62.8 jit_solution(13093077684689046086)
XLA Ops:
  0.6 1.2 %first_keys.1 = (bf16[2,2,128,256]{3,2,1,0:T(8,128)(2,1)S(1)}, bf16[2,128,256]{2,1,0:T(8,128)(2,1)S(1)}, bf16[2,128,256]{2,1,0:T(8,128)(2,1)S(1)}) custom-call(bf16[128,2048]{1,0:T(8,128)(2,1)} %refs_2_.1, bf16[128,2048]{1,0:T(8,128)(2,1)} %refs_3_.1), custom_call_target="tpu_custom_call" | custom-call | tf_op jit(solution)/shard_map/first_keys/pallas_call | solution.py:127
  1.8 0.5 collective-permute-start
  2.3 2.6 %collective-permute-start.1 = (bf16[2,2,128,256]{3,2,1,0:T(8,128)(2,1)S(1)}, bf16[2,2,128,256]{3,2,1,0:T(8,128)(2,1)S(1)}, u32[]{:S(2)}, u32[]{:S(2)}) collective-permute-start(bf16[2,2,128,256]{3,2,1,0:T(8,128)(2,1)S(1)} %get-tuple-element.27), channel_id=1, source_target_pairs={{0,2},{2,0},{1,3},{3,1},{4,6},{6,4},{5,7},{7,5},{8,10},{10,8},{9,1... | collective-permute-start | bytes 786440 | tf_op jit(solution)/shard_map/ppermute | solution.py:32
  4.9 1.6 %first_parts.1 = (bf16[2,2,128,256]{3,2,1,0:T(8,128)(2,1)S(1)}, bf16[2,2,128,256]{3,2,1,0:T(8,128)(2,1)S(1)}, bf16[4,2,128,256]{3,2,1,0:T(8,128)(2,1)S(1)}, bf16[4,2,128,256]{3,2,1,0:T(8,128)(2,1)S(1)}) custom-call(bf16[128,2048]{1,0:T(8,128)(2,1)} %refs_4_.1, bf16[128,2048]{1,0:T(8,128)(2,1)} %refs_5_.1, bf16[128,2048]{1,0:T(8,128)(2,1)} %refs_2_.1, ...), custom_call_target="tpu_custom_call" | custom-call | tf_op jit(solution)/shard_map/first_parts/pallas_call | solution.py:92
  6.5 0.2 collective-permute-start.5
  6.7 0.3 collective-permute-start.10
  7.1 0.1 pad_dynamic-slice_fusion
  7.2 0.2 both_rows.2.refs_1_
  7.4 1.6 %collective-permute-start.3 = (bf16[2,2,128,256]{3,2,1,0:T(8,128)(2,1)S(1)}, bf16[2,2,128,256]{3,2,1,0:T(8,128)(2,1)S(1)}, u32[]{:S(2)}, u32[]{:S(2)}) collective-permute-start(bf16[2,2,128,256]{3,2,1,0:T(8,128)(2,1)S(1)} %both_rows.2.refs_1_), channel_id=1, source_target_pairs={{0,4},{4,8},{8,12},{12,0},{1,5},{5,9},{9,13},{13,1},{2,6},{6,10},{... | collective-permute-start | bytes 786440 | tf_op jit(solution)/shard_map/ppermute | solution.py:27
  9.0 2.7 %collective-permute-done.1.refs_0_ = bf16[2,2,128,256]{3,2,1,0:T(8,128)(2,1)S(1)} collective-permute-done((bf16[2,2,128,256]{3,2,1,0:T(8,128)(2,1)S(1)}, bf16[2,2,128,256]{3,2,1,0:T(8,128)(2,1)S(1)}, u32[]{:S(2)}, u32[]{:S(2)}) %collective-permute-start.1) | collective-permute-done | bytes 262176 | tf_op jit(solution)/shard_map/ppermute | solution.py:32
  11.8 0.1 other_side.1
  12.0 0.2 head_parts.7
  12.2 1.8 %collective-permute-start.6 = (bf16[2,2,128,256]{3,2,1,0:T(8,128)(2,1)S(1)}, bf16[2,2,128,256]{3,2,1,0:T(8,128)(2,1)S(1)}, u32[]{:S(2)}, u32[]{:S(2)}) collective-permute-start(bf16[2,2,128,256]{3,2,1,0:T(8,128)(2,1)S(1)} %head_parts.7), channel_id=1, source_target_pairs={{0,2},{2,0},{1,3},{3,1},{4,6},{6,4},{5,7},{7,5},{8,10},{10,8},{9,1... | collective-permute-start | bytes 786440 | tf_op jit(solution)/shard_map/ppermute | solution.py:32
  14.0 0.2 both_rows.3.refs_2_.refs_0_
  14.2 1.6 %collective-permute-start.4 = (bf16[2,2,128,256]{3,2,1,0:T(8,128)(2,1)S(1)}, bf16[2,2,128,256]{3,2,1,0:T(8,128)(2,1)S(1)}, u32[]{:S(2)}, u32[]{:S(2)}) collective-permute-start(bf16[2,2,128,256]{3,2,1,0:T(8,128)(2,1)S(1)} %both_rows.3.refs_2_.refs_0_), channel_id=1, source_target_pairs={{0,4},{4,8},{8,12},{12,0},{1,5},{5,9},{9,13},{13,1},{2,6},{6,10},{... | collective-permute-start | bytes 786440 | tf_op jit(solution)/shard_map/ppermute | solution.py:27
  15.8 1.9 %collective-permute-done.3.refs_3_.refs_0_.refs_1_ = bf16[2,2,128,256]{3,2,1,0:T(8,128)(2,1)S(1)} collective-permute-done((bf16[2,2,128,256]{3,2,1,0:T(8,128)(2,1)S(1)}, bf16[2,2,128,256]{3,2,1,0:T(8,128)(2,1)S(1)}, u32[]{:S(2)}, u32[]{:S(2)}) %collective-permute-start.3) | collective-permute-done | bytes 262176 | tf_op jit(solution)/shard_map/ppermute | solution.py:27
  17.7 0.2 head_parts.9
  17.9 0.6 collective-permute-start.11
  18.5 0.7 %and_select_fusion = (f32[1,768,256]{2,1,0:T(8,128)S(1)}, f32[1,768,256]{2,1,0:T(8,128)S(1)}) fusion(s32[256]{0:T(256)S(1)} %get-tuple-element.56, s32[256]{0:T(256)S(1)} %get-tuple-element.54, s32[768]{0:T(1024)S(1)} %get-tuple-element.52, s32[768]{0:T(1024)S(1)} %get-tuple-element.50, pred[768]{0:T(1024)(128)(4,1)S(1)} %get-tuple-element.48, ...), kind=kLoop, calls=%fused_computation.1 | loop fusion | flops 1966080 | bytes 1590784 | tf_op jit(solution)/shard_map/jit(_where)/select_n | solution.py:364
  19.2 0.1 pad_maximum_fusion.refs_0_
  19.3 0.2 head_parts.6.refs_5_
  19.5 0.2 head_parts.8.refs_1_
  19.7 0.2 collective-permute-start.12
  19.9 1.4 %collective-permute-done.6.refs_6_.refs_0_ = bf16[2,2,128,256]{3,2,1,0:T(8,128)(2,1)S(1)} collective-permute-done((bf16[2,2,128,256]{3,2,1,0:T(8,128)(2,1)S(1)}, bf16[2,2,128,256]{3,2,1,0:T(8,128)(2,1)S(1)}, u32[]{:S(2)}, u32[]{:S(2)}) %collective-permute-start.6) | collective-permute-done | bytes 262176 | tf_op jit(solution)/shard_map/ppermute | solution.py:32
  21.3 0.2 head_parts.11
  21.5 1.8 %collective-permute-start.14 = (bf16[2,2,128,256]{3,2,1,0:T(8,128)(2,1)S(1)}, bf16[2,2,128,256]{3,2,1,0:T(8,128)(2,1)S(1)}, u32[]{:S(2)}, u32[]{:S(2)}) collective-permute-start(bf16[2,2,128,256]{3,2,1,0:T(8,128)(2,1)S(1)} %head_parts.11), channel_id=1, source_target_pairs={{0,2},{2,0},{1,3},{3,1},{4,6},{6,4},{5,7},{7,5},{8,10},{10,8},{9,1... | collective-permute-start | bytes 786440 | tf_op jit(solution)/shard_map/ppermute | solution.py:32
  23.3 1.8 %collective-permute-done.4.refs_4_ = bf16[2,2,128,256]{3,2,1,0:T(8,128)(2,1)S(1)} collective-permute-done((bf16[2,2,128,256]{3,2,1,0:T(8,128)(2,1)S(1)}, bf16[2,2,128,256]{3,2,1,0:T(8,128)(2,1)S(1)}, u32[]{:S(2)}, u32[]{:S(2)}) %collective-permute-start.4) | collective-permute-done | bytes 262176 | tf_op jit(solution)/shard_map/ppermute | solution.py:27
  25.2 3.5 %attention_grads.2 = (f32[2,2,2,128,256]{4,3,2,1,0:T(8,128)S(1)}, bf16[2,128,256]{2,1,0:T(8,128)(2,1)S(1)}, bf16[2,128,256]{2,1,0:T(8,128)(2,1)S(1)}, bf16[2,2,2,128,256]{4,3,2,1,0:T(8,128)(2,1)S(1)}) custom-call(f32[2,768,256]{2,1,0:T(8,128)S(1)} %pad_maximum_fusion.refs_0_, bf16[2,2,128,256]{3,2,1,0:T(8,128)(2,1)S(1)} %both_rows.2.refs_1_, ...), custom_call_target="tpu_custom_call" | custom-call | flops 1006632960 | bytes 4980736 | tf_op jit(solution)/shard_map/attention_grads/pallas_call | solution.py:51
  28.8 2.0 %collective-permute-start.13 = (bf16[2,2,128,256]{3,2,1,0:T(8,128)(2,1)S(1)}, bf16[2,2,128,256]{3,2,1,0:T(8,128)(2,1)S(1)}, u32[]{:S(2)}, u32[]{:S(2)}) collective-permute-start(bf16[2,2,128,256]{3,2,1,0:T(8,128)(2,1)S(1)} %relayed.2), channel_id=1, source_target_pairs={{0,4},{4,8},{8,12},{1,5},{5,9},{9,13},{2,6},{6,10},{10,14},{3,7},{... | collective-permute-start | bytes 786440 | tf_op jit(solution)/shard_map/ppermute | solution.py:27
  30.8 1.3 %collective-permute-start.8 = (bf16[2,2,2,128,256]{4,3,2,1,0:T(8,128)(2,1)S(1)}, bf16[2,2,2,128,256]{4,3,2,1,0:T(8,128)(2,1)S(1)}, u32[]{:S(2)}, u32[]{:S(2)}) collective-permute-start(bf16[2,2,2,128,256]{4,3,2,1,0:T(8,128)(2,1)S(1)} %get-tuple-element.33), channel_id=1, source_target_pairs={{4,0},{8,4},{12,8},{5,1},{9,5},{13,9},{6,2},{10,6},{14,10},{7,3},{... | collective-permute-start | bytes 1572872 | tf_op jit(solution)/shard_map/ppermute | solution.py:27
  32.1 0.2 head_parts.10.refs_5_
  32.3 3.5 %collective-permute-done.13.refs_4_ = bf16[2,2,128,256]{3,2,1,0:T(8,128)(2,1)S(1)} collective-permute-done((bf16[2,2,128,256]{3,2,1,0:T(8,128)(2,1)S(1)}, bf16[2,2,128,256]{3,2,1,0:T(8,128)(2,1)S(1)}, u32[]{:S(2)}, u32[]{:S(2)}) %collective-permute-start.13) | collective-permute-done | bytes 262176 | tf_op jit(solution)/shard_map/ppermute | solution.py:27
  35.8 3.5 %attention_grads.3 = (f32[2,2,2,128,256]{4,3,2,1,0:T(8,128)S(1)}, bf16[2,128,256]{2,1,0:T(8,128)(2,1)S(1)}, bf16[2,128,256]{2,1,0:T(8,128)(2,1)S(1)}, bf16[2,2,1...) custom-call(f32[2,768,256]{2,1,0:T(8,128)S(1)} %pad_maximum_fusion.refs_0_, ...), custom_call_target="tpu_custom_call" | custom-call | flops 1006632960 | bytes 4980736 | tf_op jit(solution)/shard_map/attention_grads/pallas_call | solution.py:51
  39.3 1.3 %collective-permute-start.16 = (bf16[2,2,128,256]{3,2,1,0:T(8,128)(2,1)S(1)}, bf16[2,2,128,256]{3,2,1,0:T(8,128)(2,1)S(1)}, u32[]{:S(2)}, u32[]{:S(2)}) collective-permute-start(bf16[2,2,128,256]{3,2,1,0:T(8,128)(2,1)S(1)} %get-tuple-element.43), channel_id=1, source_target_pairs={{4,0},{8,4},{12,8},{5,1},{9,5},{13,9},{6,2},{10,6},{14,10},{7,3},{... | collective-permute-start | bytes 786440 | tf_op jit(solution)/shard_map/ppermute | solution.py:27
  40.6 1.6 %collective-permute-start.7 = (bf16[2,128,256]{2,1,0:T(8,128)(2,1)S(1)}, bf16[2,128,256]{2,1,0:T(8,128)(2,1)S(1)}, u32[]{:S(2)}, u32[]{:S(2)}) collective-permute-start(bf16[2,128,256]{2,1,0:T(8,128)(2,1)S(1)} %get-tuple-element.31), channel_id=1, source_target_pairs={{0,2},{2,0},{1,3},{3,1},{4,6},{6,4},{5,7},{7,5},{8,10},{10,8},{9,1... | collective-permute-start | bytes 393224 | tf_op jit(solution)/shard_map/ppermute | solution.py:32
  42.2 0.5 collective-permute-start.15
  42.7 3.2 %collective-permute-done.7.refs_1_ = bf16[2,128,256]{2,1,0:T(8,128)(2,1)S(1)} collective-permute-done((bf16[2,128,256]{2,1,0:T(8,128)(2,1)S(1)}, bf16[2,128,256]{2,1,0:T(8,128)(2,1)S(1)}, u32[]{:S(2)}, u32[]{:S(2)}) %collective-permute-start.7) | collective-permute-done | bytes 131104 | tf_op jit(solution)/shard_map/ppermute | solution.py:32
  45.9 1.7 %collective-permute-done.8.refs_0_ = bf16[2,2,2,128,256]{4,3,2,1,0:T(8,128)(2,1)S(1)} collective-permute-done((bf16[2,2,2,128,256]{4,3,2,1,0:T(8,128)(2,1)S(1)}, bf16[2,2,2,128,256]{4,3,2,1,0:T(8,128)(2,1)S(1)}, u32[]{:S(2)}, u32[]{:S(2)}) %collective-permute-start.8) | collective-permute-done | bytes 524320 | tf_op jit(solution)/shard_map/ppermute | solution.py:27
  47.5 0.1 summed.3
  47.6 1.6 %collective-permute-start.9 = (bf16[2,2,128,256]{3,2,1,0:T(8,128)(2,1)S(1)}, bf16[2,2,128,256]{3,2,1,0:T(8,128)(2,1)S(1)}, u32[]{:S(2)}, u32[]{:S(2)}) collective-permute-start(bf16[2,2,128,256]{3,2,1,0:T(8,128)(2,1)S(1)} %get-tuple-element.35), channel_id=1, source_target_pairs={{0,2},{2,0},{1,3},{3,1},{4,6},{6,4},{5,7},{7,5},{8,10},{10,8},{9,1... | collective-permute-start | bytes 786440 | tf_op jit(solution)/shard_map/ppermute | solution.py:32
  49.2 2.0 %collective-permute-done.16.refs_0_ = bf16[2,2,128,256]{3,2,1,0:T(8,128)(2,1)S(1)} collective-permute-done((bf16[2,2,128,256]{3,2,1,0:T(8,128)(2,1)S(1)}, bf16[2,2,128,256]{3,2,1,0:T(8,128)(2,1)S(1)}, u32[]{:S(2)}, u32[]{:S(2)}) %collective-permute-start.16) | collective-permute-done | bytes 262176 | tf_op jit(solution)/shard_map/ppermute | solution.py:27
  51.2 1.3 %collective-permute-start.17 = (bf16[2,2,128,256]{3,2,1,0:T(8,128)(2,1)S(1)}, bf16[2,2,128,256]{3,2,1,0:T(8,128)(2,1)S(1)}, u32[]{:S(2)}, u32[]{:S(2)}) collective-permute-start(bf16[2,2,128,256]{3,2,1,0:T(8,128)(2,1)S(1)} %relayed.3), channel_id=1, source_target_pairs={{4,0},{8,4},{12,8},{5,1},{9,5},{13,9},{6,2},{10,6},{14,10},{7,3},{... | collective-permute-start | bytes 786440 | tf_op jit(solution)/shard_map/ppermute | solution.py:27
  52.5 1.6 %collective-permute-start.18 = (bf16[2,2,128,256]{3,2,1,0:T(8,128)(2,1)S(1)}, bf16[2,2,128,256]{3,2,1,0:T(8,128)(2,1)S(1)}, u32[]{:S(2)}, u32[]{:S(2)}) collective-permute-start(bf16[2,2,128,256]{3,2,1,0:T(8,128)(2,1)S(1)} %summed.4.refs_0_), channel_id=1, source_target_pairs={{0,2},{2,0},{1,3},{3,1},{4,6},{6,4},{5,7},{7,5},{8,10},{10,8},{9,1... | collective-permute-start | bytes 786440 | tf_op jit(solution)/shard_map/ppermute | solution.py:32
  54.1 0.7 %collective-permute-done.9.refs_3_ = bf16[2,2,128,256]{3,2,1,0:T(8,128)(2,1)S(1)} collective-permute-done((bf16[2,2,128,256]{3,2,1,0:T(8,128)(2,1)S(1)}, bf16[2,2,128,256]{3,2,1,0:T(8,128)(2,1)S(1)}, u32[]{:S(2)}, u32[]{:S(2)}) %collective-permute-start.9) | collective-permute-done | bytes 262176 | tf_op jit(solution)/shard_map/ppermute | solution.py:32
  54.9 4.6 %collective-permute-done.17.refs_0_ = bf16[2,2,128,256]{3,2,1,0:T(8,128)(2,1)S(1)} collective-permute-done((bf16[2,2,128,256]{3,2,1,0:T(8,128)(2,1)S(1)}, bf16[2,2,128,256]{3,2,1,0:T(8,128)(2,1)S(1)}, u32[]{:S(2)}, u32[]{:S(2)}) %collective-permute-start.17) | collective-permute-done | bytes 262176 | tf_op jit(solution)/shard_map/ppermute | solution.py:27
  59.5 0.1 collective-permute-done.18.refs_3_
  59.8 1.7 %collective-permute-done.20.refs_3_ = bf16[3,2,128,256]{3,2,1,0:T(8,128)(2,1)S(1)} collective-permute-done((bf16[3,2,128,256]{3,2,1,0:T(8,128)(2,1)S(1)}, bf16[3,2,128,256]{3,2,1,0:T(8,128)(2,1)S(1)}, u32[]{:S(2)}, u32[]{:S(2)}) %collective-permute-start.20) | collective-permute-done | bytes 393248 | tf_op jit(solution)/shard_map/ppermute | solution.py:36
  61.5 1.3 %laid_out.1 = (bf16[128,2048]{1,0:T(8,128)(2,1)}, bf16[128,2048]{1,0:T(8,128)(2,1)}, bf16[128,2048]{1,0:T(8,128)(2,1)}) custom-call(bf16[3,2,128,256]{3,2,1,0:T(8,128)(2,1)S(1)} %get-tuple-element.36.refs_0_, bf16[3,2,128,256]{3,2,1,0:T(8,128)(2,1)S(1)} %get-tuple-element.44.refs_1_, bf16[3,2,128,256]{3,2,1,0:T(8,128)(2,1)S(1)} %collective-permute-done.19.refs_2_, ...), custom_call_target="tpu_custom_call" | custom-call | bytes 3145728 | tf_op jit(solution)/shard_map/laid_out/pallas_call | solution.py:51
  (26 shorter events, 0.6 us)
Async XLA Ops:
  1.8 5.4 %collective-permute-start = (bf16[2,128,256]{2,1,0:T(8,128)(2,1)S(1)}, bf16[2,128,256]{2,1,0:T(8,128)(2,1)S(1)}, u32[]{:S(2)}, u32[]{:S(2)}) collective-permute-start(bf16[2,128,256]{2,1,0:T(8,128)(2,1)S(1)} %get-tuple-element.26), channel_id=1, source_target_pairs={{0,1},{1,0},{2,3},{3,2},{4,5},{5,4},{6,7},{7,6},{8,9},{9,8},{10,11... | collective-permute-start | bytes 393224 | tf_op jit(solution)/shard_map/ppermute | solution.py:36
  2.3 9.5 %collective-permute-start.1 = (bf16[2,2,128,256]{3,2,1,0:T(8,128)(2,1)S(1)}, bf16[2,2,128,256]{3,2,1,0:T(8,128)(2,1)S(1)}, u32[]{:S(2)}, u32[]{:S(2)}) collective-permute-start(bf16[2,2,128,256]{3,2,1,0:T(8,128)(2,1)S(1)} %get-tuple-element.27), channel_id=1, source_target_pairs={{0,2},{2,0},{1,3},{3,1},{4,6},{6,4},{5,7},{7,5},{8,10},{10,8},{9,1... | collective-permute-start | bytes 786440 | tf_op jit(solution)/shard_map/ppermute | solution.py:32
  4.9 2.2 %copy-start = (s32[2048]{0:T(1024)S(1)}, s32[2048]{0:T(1024)}, u32[]{:S(2)}) copy-start(s32[2048]{0:T(1024)} %param.9) | copy-start | bytes 24580
  6.5 5.4 %collective-permute-start.5 = (bf16[2,2,128,256]{3,2,1,0:T(8,128)(2,1)S(1)}, bf16[2,2,128,256]{3,2,1,0:T(8,128)(2,1)S(1)}, u32[]{:S(2)}, u32[]{:S(2)}) collective-permute-start(bf16[2,2,128,256]{3,2,1,0:T(8,128)(2,1)S(1)} %get-tuple-element.29), channel_id=1, source_target_pairs={{0,1},{1,0},{2,3},{3,2},{4,5},{5,4},{6,7},{7,6},{8,9},{9,8},{10,11... | collective-permute-start | bytes 786440 | tf_op jit(solution)/shard_map/ppermute | solution.py:36
  6.7 11.0 %collective-permute-start.10 = (bf16[4,2,128,256]{3,2,1,0:T(8,128)(2,1)S(1)}, bf16[4,2,128,256]{3,2,1,0:T(8,128)(2,1)S(1)}, u32[]{:S(2)}, u32[]{:S(2)}) collective-permute-start(bf16[4,2,128,256]{3,2,1,0:T(8,128)(2,1)S(1)} %get-tuple-element.38), channel_id=1, source_target_pairs={{0,1},{1,0},{2,3},{3,2},{4,5},{5,4},{6,7},{7,6},{8,9},{9,8},{10,11... | collective-permute-start | bytes 1572872 | tf_op jit(solution)/shard_map/ppermute | solution.py:36
  7.4 10.3 %collective-permute-start.3 = (bf16[2,2,128,256]{3,2,1,0:T(8,128)(2,1)S(1)}, bf16[2,2,128,256]{3,2,1,0:T(8,128)(2,1)S(1)}, u32[]{:S(2)}, u32[]{:S(2)}) collective-permute-start(bf16[2,2,128,256]{3,2,1,0:T(8,128)(2,1)S(1)} %both_rows.2.refs_1_), channel_id=1, source_target_pairs={{0,4},{4,8},{8,12},{12,0},{1,5},{5,9},{9,13},{13,1},{2,6},{6,10},{... | collective-permute-start | bytes 786440 | tf_op jit(solution)/shard_map/ppermute | solution.py:27
  11.9 2.1 %collective-permute-start.2 = (bf16[1,2,128,256]{3,2,1,0:T(8,128)(2,1)S(1)}, bf16[1,2,128,256]{3,2,1,0:T(8,128)(2,1)S(1)}, u32[]{:S(2)}, u32[]{:S(2)}) collective-permute-start(bf16[1,2,128,256]{3,2,1,0:T(8,128)(2,1)S(1)} %other_side.1), channel_id=1, source_target_pairs={{0,1},{1,0},{2,3},{3,2},{4,5},{5,4},{6,7},{7,6},{8,9},{9,8},{10,11... | collective-permute-start | bytes 393224 | tf_op jit(solution)/shard_map/ppermute | solution.py:36
  12.2 9.2 %collective-permute-start.6 = (bf16[2,2,128,256]{3,2,1,0:T(8,128)(2,1)S(1)}, bf16[2,2,128,256]{3,2,1,0:T(8,128)(2,1)S(1)}, u32[]{:S(2)}, u32[]{:S(2)}) collective-permute-start(bf16[2,2,128,256]{3,2,1,0:T(8,128)(2,1)S(1)} %head_parts.7), channel_id=1, source_target_pairs={{0,2},{2,0},{1,3},{3,1},{4,6},{6,4},{5,7},{7,5},{8,10},{10,8},{9,1... | collective-permute-start | bytes 786440 | tf_op jit(solution)/shard_map/ppermute | solution.py:32
  14.2 11.0 %collective-permute-start.4 = (bf16[2,2,128,256]{3,2,1,0:T(8,128)(2,1)S(1)}, bf16[2,2,128,256]{3,2,1,0:T(8,128)(2,1)S(1)}, u32[]{:S(2)}, u32[]{:S(2)}) collective-permute-start(bf16[2,2,128,256]{3,2,1,0:T(8,128)(2,1)S(1)} %both_rows.3.refs_2_.refs_0_), channel_id=1, source_target_pairs={{0,4},{4,8},{8,12},{12,0},{1,5},{5,9},{9,13},{13,1},{2,6},{6,10},{... | collective-permute-start | bytes 786440 | tf_op jit(solution)/shard_map/ppermute | solution.py:27
  17.9 10.8 %collective-permute-start.11 = (bf16[2,2,128,256]{3,2,1,0:T(8,128)(2,1)S(1)}, bf16[2,2,128,256]{3,2,1,0:T(8,128)(2,1)S(1)}, u32[]{:S(2)}, u32[]{:S(2)}) collective-permute-start(bf16[2,2,128,256]{3,2,1,0:T(8,128)(2,1)S(1)} %head_parts.9), channel_id=1, source_target_pairs={{0,2},{2,0},{1,3},{3,1},{4,6},{6,4},{5,7},{7,5},{8,10},{10,8},{9,1... | collective-permute-start | bytes 786440 | tf_op jit(solution)/shard_map/ppermute | solution.py:32
  19.7 12.6 %collective-permute-start.12 = (bf16[2,2,128,256]{3,2,1,0:T(8,128)(2,1)S(1)}, bf16[2,2,128,256]{3,2,1,0:T(8,128)(2,1)S(1)}, u32[]{:S(2)}, u32[]{:S(2)}) collective-permute-start(bf16[2,2,128,256]{3,2,1,0:T(8,128)(2,1)S(1)} %head_parts.8.refs_1_), channel_id=1, source_target_pairs={{0,4},{4,8},{8,12},{12,0},{1,5},{5,9},{9,13},{13,1},{2,6},{6,10},{... | collective-permute-start | bytes 786440 | tf_op jit(solution)/shard_map/ppermute | solution.py:27
  21.5 10.8 %collective-permute-start.14 = (bf16[2,2,128,256]{3,2,1,0:T(8,128)(2,1)S(1)}, bf16[2,2,128,256]{3,2,1,0:T(8,128)(2,1)S(1)}, u32[]{:S(2)}, u32[]{:S(2)}) collective-permute-start(bf16[2,2,128,256]{3,2,1,0:T(8,128)(2,1)S(1)} %head_parts.11), channel_id=1, source_target_pairs={{0,2},{2,0},{1,3},{3,1},{4,6},{6,4},{5,7},{7,5},{8,10},{10,8},{9,1... | collective-permute-start | bytes 786440 | tf_op jit(solution)/shard_map/ppermute | solution.py:32
  28.8 7.0 %collective-permute-start.13 = (bf16[2,2,128,256]{3,2,1,0:T(8,128)(2,1)S(1)}, bf16[2,2,128,256]{3,2,1,0:T(8,128)(2,1)S(1)}, u32[]{:S(2)}, u32[]{:S(2)}) collective-permute-start(bf16[2,2,128,256]{3,2,1,0:T(8,128)(2,1)S(1)} %relayed.2), channel_id=1, source_target_pairs={{0,4},{4,8},{8,12},{1,5},{5,9},{9,13},{2,6},{6,10},{10,14},{3,7},{... | collective-permute-start | bytes 786440 | tf_op jit(solution)/shard_map/ppermute | solution.py:27
  30.8 16.8 %collective-permute-start.8 = (bf16[2,2,2,128,256]{4,3,2,1,0:T(8,128)(2,1)S(1)}, bf16[2,2,2,128,256]{4,3,2,1,0:T(8,128)(2,1)S(1)}, u32[]{:S(2)}, u32[]{:S(2)}) collective-permute-start(bf16[2,2,2,128,256]{4,3,2,1,0:T(8,128)(2,1)S(1)} %get-tuple-element.33), channel_id=1, source_target_pairs={{4,0},{8,4},{12,8},{5,1},{9,5},{13,9},{6,2},{10,6},{14,10},{7,3},{... | collective-permute-start | bytes 1572872 | tf_op jit(solution)/shard_map/ppermute | solution.py:27
  39.3 11.8 %collective-permute-start.16 = (bf16[2,2,128,256]{3,2,1,0:T(8,128)(2,1)S(1)}, bf16[2,2,128,256]{3,2,1,0:T(8,128)(2,1)S(1)}, u32[]{:S(2)}, u32[]{:S(2)}) collective-permute-start(bf16[2,2,128,256]{3,2,1,0:T(8,128)(2,1)S(1)} %get-tuple-element.43), channel_id=1, source_target_pairs={{4,0},{8,4},{12,8},{5,1},{9,5},{13,9},{6,2},{10,6},{14,10},{7,3},{... | collective-permute-start | bytes 786440 | tf_op jit(solution)/shard_map/ppermute | solution.py:27
  40.6 5.3 %collective-permute-start.7 = (bf16[2,128,256]{2,1,0:T(8,128)(2,1)S(1)}, bf16[2,128,256]{2,1,0:T(8,128)(2,1)S(1)}, u32[]{:S(2)}, u32[]{:S(2)}) collective-permute-start(bf16[2,128,256]{2,1,0:T(8,128)(2,1)S(1)} %get-tuple-element.31), channel_id=1, source_target_pairs={{0,2},{2,0},{1,3},{3,1},{4,6},{6,4},{5,7},{7,5},{8,10},{10,8},{9,1... | collective-permute-start | bytes 393224 | tf_op jit(solution)/shard_map/ppermute | solution.py:32
  42.2 7.0 %collective-permute-start.15 = (bf16[2,128,256]{2,1,0:T(8,128)(2,1)S(1)}, bf16[2,128,256]{2,1,0:T(8,128)(2,1)S(1)}, u32[]{:S(2)}, u32[]{:S(2)}) collective-permute-start(bf16[2,128,256]{2,1,0:T(8,128)(2,1)S(1)} %get-tuple-element.40), channel_id=1, source_target_pairs={{0,2},{2,0},{1,3},{3,1},{4,6},{6,4},{5,7},{7,5},{8,10},{10,8},{9,1... | collective-permute-start | bytes 393224 | tf_op jit(solution)/shard_map/ppermute | solution.py:32
  47.6 7.1 %collective-permute-start.9 = (bf16[2,2,128,256]{3,2,1,0:T(8,128)(2,1)S(1)}, bf16[2,2,128,256]{3,2,1,0:T(8,128)(2,1)S(1)}, u32[]{:S(2)}, u32[]{:S(2)}) collective-permute-start(bf16[2,2,128,256]{3,2,1,0:T(8,128)(2,1)S(1)} %get-tuple-element.35), channel_id=1, source_target_pairs={{0,2},{2,0},{1,3},{3,1},{4,6},{6,4},{5,7},{7,5},{8,10},{10,8},{9,1... | collective-permute-start | bytes 786440 | tf_op jit(solution)/shard_map/ppermute | solution.py:32
  51.2 8.3 %collective-permute-start.17 = (bf16[2,2,128,256]{3,2,1,0:T(8,128)(2,1)S(1)}, bf16[2,2,128,256]{3,2,1,0:T(8,128)(2,1)S(1)}, u32[]{:S(2)}, u32[]{:S(2)}) collective-permute-start(bf16[2,2,128,256]{3,2,1,0:T(8,128)(2,1)S(1)} %relayed.3), channel_id=1, source_target_pairs={{4,0},{8,4},{12,8},{5,1},{9,5},{13,9},{6,2},{10,6},{14,10},{7,3},{... | collective-permute-start | bytes 786440 | tf_op jit(solution)/shard_map/ppermute | solution.py:27
  52.5 7.1 %collective-permute-start.18 = (bf16[2,2,128,256]{3,2,1,0:T(8,128)(2,1)S(1)}, bf16[2,2,128,256]{3,2,1,0:T(8,128)(2,1)S(1)}, u32[]{:S(2)}, u32[]{:S(2)}) collective-permute-start(bf16[2,2,128,256]{3,2,1,0:T(8,128)(2,1)S(1)} %summed.4.refs_0_), channel_id=1, source_target_pairs={{0,2},{2,0},{1,3},{3,1},{4,6},{6,4},{5,7},{7,5},{8,10},{10,8},{9,1... | collective-permute-start | bytes 786440 | tf_op jit(solution)/shard_map/ppermute | solution.py:32
  54.8 5.0 %collective-permute-start.19 = (bf16[3,2,128,256]{3,2,1,0:T(8,128)(2,1)S(1)}, bf16[3,2,128,256]{3,2,1,0:T(8,128)(2,1)S(1)}, u32[]{:S(2)}, u32[]{:S(2)}) collective-permute-start(bf16[3,2,128,256]{3,2,1,0:T(8,128)(2,1)S(1)} %get-tuple-element.45), channel_id=1, source_target_pairs={{0,1},{1,0},{2,3},{3,2},{4,5},{5,4},{6,7},{7,6},{8,9},{9,8},{10,11... | collective-permute-start | bytes 1179656 | tf_op jit(solution)/shard_map/ppermute | solution.py:36
  59.7 1.8 %collective-permute-start.20 = (bf16[3,2,128,256]{3,2,1,0:T(8,128)(2,1)S(1)}, bf16[3,2,128,256]{3,2,1,0:T(8,128)(2,1)S(1)}, u32[]{:S(2)}, u32[]{:S(2)}) collective-permute-start(bf16[3,2,128,256]{3,2,1,0:T(8,128)(2,1)S(1)} %get-tuple-element.46), channel_id=1, source_target_pairs={{0,1},{1,0},{2,3},{3,2},{4,5},{5,4},{6,7},{7,6},{8,9},{9,8},{10,11... | collective-permute-start | bytes 1179656 | tf_op jit(solution)/shard_map/ppermute | solution.py:36

commit v13 on v12

--- a/solution.py
+++ b/solution.py
@@ -390,7 +390,7 @@
     kv_sends, qg_sends, kv, qg, kv_own, own_earlier = [], [], [], [], [], []
     for index in range(count):
         if index:
-            kv_sends.append(head_parts(*kv_parts[index], others, kv[index - 1] + own_earlier[index - 1:index]))
+            kv_sends.append(head_parts(*kv_parts[index], others, kv_far))
             kv.append([round_sub(value, by) for by, value in zip(others, kv_sends[index])])
             kv_own.append(head_parts(*kv_parts[index], [0], own_earlier[index - 1:index]))
         else:
@@ -398,16 +398,16 @@
             kv_own.append(both_rows([near_keep], near_theirs.reshape(1, *near_theirs.shape)))
             kv.append(both_rows(kv_far, swapped(other_side(kv_far))))
         own_earlier.append(along_blocks(kv_own[index][0], 1, True))
-        qg_sends.append(head_parts(*qg_parts[index], others, qg[index - 1] if index else []))
+    for index in range(count):
+        turn = kv[index] if index else kv_sends[-1] + own_earlier[:1]
+        qg_sends.append(head_parts(*qg_parts[index], others, turn))
         qg.append([round_sub(value, by) for by, value in zip(others, qg_sends[index])])
     kept, paired = [], []
     for index in range(count):
         last = index == count - 1
-        forward = [relayed(value, [first_dq]) if index else value for value in kv[index]]
-        earlier = [own_earlier[index]] + [along_blocks(value, 1, not last) for value in forward]
+        earlier = [own_earlier[index]] + [along_blocks(value, 1, not last) for value in kv[index]]
         qg_all = head_parts(*qg_parts[index], [0], []) + qg[index]
         grads, dq, early = attention_grads(bias, kv_own[index] + kv[index], earlier, qg_all, last, [])
-        first_dq = dq[0]
         dq = [dq[0]] + [round_sub(dq[by], by) for by in others]
         if last:
             later = [along_blocks(value, -1, False) for value in early[1:]]

time: 63.2 us -> 66 us (1.044)
  starting transfers between devices: 22.7 us -> 24.7 us
  waiting for transfers between devices: 25.2 us -> 26 us
    ppermute x7, waiting for transfers between devices: 15.4 us -> 8.31 us  [along_blocks(): return lax.ppermute(value, 'blk', pairs)]
    ppermute x8, waiting for transfers between devices: 8.08 us -> 14.7 us  [round_sub(): lax.ppermute(value, 'sub', [(i, (i + by) % peers) for i in range(peers)])]
    ppermute x7, starting transfers between devices: 9.36 us -> 11.9 us  [along_blocks(): return lax.ppermute(value, 'blk', pairs)]
    ppermute x6, waiting for transfers between devices: 1.71 us -> 3.03 us  [swapped(): return lax.ppermute(value, 'pair', [(0, 1), (1, 0)])]
    pallas_call x19 -> x18, Pallas kernels: 10.4 us -> 10.4 us  [call(): pl.pallas_call(kernel, out_shape=outs, in_specs=[spec] * len(ins), out_sp...]
  transfers between devices with their start and end apart: 21 -> 21, of which waited for: 12 -> 12; matrix products, arithmetic and copies ran while one was open for 1% -> 1% of each run, Pallas kernels for 17% -> 16%
where the time goes in v13:
time: 66 us; the launch traced here: 65.7 us
  waiting for transfers between devices  26 us (39%)
  starting transfers between devices  24.7 us (37%)
  Pallas kernels  13.1 us (20%)
  between operations  0.9 us (1%)
  other arithmetic  0.79 us (1%)
    ppermute x8, waiting for transfers between devices, round_sub(): lax.ppermute(value, 'sub', [(i, (i + by) % peers) for i in range(peers)])  14.7 us
    ppermute x7, starting transfers between devices, along_blocks(): return lax.ppermute(value, 'blk', pairs)  11.9 us
    ppermute x8, starting transfers between devices, round_sub(): lax.ppermute(value, 'sub', [(i, (i + by) % peers) for i in range(peers)])  11.5 us
    pallas_call x18, Pallas kernels, call(): pl.pallas_call(kernel, out_shape=outs, in_specs=[spec] * len(ins), out_sp...  10.4 us
    ppermute x7, waiting for transfers between devices, along_blocks(): return lax.ppermute(value, 'blk', pairs)  8.31 us
    ppermute x6, waiting for transfers between devices, swapped(): return lax.ppermute(value, 'pair', [(0, 1), (1, 0)])  3.03 us
    pallas_call x1, Pallas kernels, first_parts(): pl.pallas_call(kernel, out_shape=outs, in_specs=[spec] * (len(held) + len...  1.64 us
  transfers between devices with their start and end apart: 21, of which 12 were waited for; matrix products, arithmetic and copies ran while one was open for 1% of the time, Pallas kernels for 16%

profile of v13, /device:TPU:0, one launch (start us, length us, event | category | flops | bytes accessed | tf_op | source)
XLA Modules:
  0.0 65.7 jit_solution(12768093127124528758)
XLA Ops:
  0.6 1.2 %first_keys.1 = (bf16[2,2,128,256]{3,2,1,0:T(8,128)(2,1)S(1)}, bf16[2,128,256]{2,1,0:T(8,128)(2,1)S(1)}, bf16[2,128,256]{2,1,0:T(8,128)(2,1)S(1)}) custom-call(bf16[128,2048]{1,0:T(8,128)(2,1)} %refs_2_.1, bf16[128,2048]{1,0:T(8,128)(2,1)} %refs_3_.1), custom_call_target="tpu_custom_call" | custom-call | tf_op jit(solution)/shard_map/first_keys/pallas_call | solution.py:127
  1.8 0.5 collective-permute-start
  2.3 2.6 %collective-permute-start.1 = (bf16[2,2,128,256]{3,2,1,0:T(8,128)(2,1)S(1)}, bf16[2,2,128,256]{3,2,1,0:T(8,128)(2,1)S(1)}, u32[]{:S(2)}, u32[]{:S(2)}) collective-permute-start(bf16[2,2,128,256]{3,2,1,0:T(8,128)(2,1)S(1)} %get-tuple-element.27), channel_id=1, source_target_pairs={{0,2},{2,0},{1,3},{3,1},{4,6},{6,4},{5,7},{7,5},{8,10},{10,8},{9,1... | collective-permute-start | bytes 786440 | tf_op jit(solution)/shard_map/ppermute | solution.py:32
  4.9 1.6 %first_parts.1 = (bf16[2,2,128,256]{3,2,1,0:T(8,128)(2,1)S(1)}, bf16[2,2,128,256]{3,2,1,0:T(8,128)(2,1)S(1)}, bf16[4,2,128,256]{3,2,1,0:T(8,128)(2,1)S(1)}, bf16[4,2,128,256]{3,2,1,0:T(8,128)(2,1)S(1)}) custom-call(bf16[128,2048]{1,0:T(8,128)(2,1)} %refs_4_.1, bf16[128,2048]{1,0:T(8,128)(2,1)} %refs_5_.1, bf16[128,2048]{1,0:T(8,128)(2,1)} %refs_2_.1, ...), custom_call_target="tpu_custom_call" | custom-call | tf_op jit(solution)/shard_map/first_parts/pallas_call | solution.py:92
  6.5 0.2 collective-permute-start.5
  6.7 0.3 collective-permute-start.6
  7.1 0.1 pad_dynamic-slice_fusion
  7.2 0.2 both_rows.2.refs_1_
  7.4 1.6 %collective-permute-start.3 = (bf16[2,2,128,256]{3,2,1,0:T(8,128)(2,1)S(1)}, bf16[2,2,128,256]{3,2,1,0:T(8,128)(2,1)S(1)}, u32[]{:S(2)}, u32[]{:S(2)}) collective-permute-start(bf16[2,2,128,256]{3,2,1,0:T(8,128)(2,1)S(1)} %both_rows.2.refs_1_), channel_id=1, source_target_pairs={{0,4},{4,8},{8,12},{12,0},{1,5},{5,9},{9,13},{13,1},{2,6},{6,10},{... | collective-permute-start | bytes 786440 | tf_op jit(solution)/shard_map/ppermute | solution.py:27
  9.0 2.7 %collective-permute-done.1.refs_0_ = bf16[2,2,128,256]{3,2,1,0:T(8,128)(2,1)S(1)} collective-permute-done((bf16[2,2,128,256]{3,2,1,0:T(8,128)(2,1)S(1)}, bf16[2,2,128,256]{3,2,1,0:T(8,128)(2,1)S(1)}, u32[]{:S(2)}, u32[]{:S(2)}) %collective-permute-start.1) | collective-permute-done | bytes 262176 | tf_op jit(solution)/shard_map/ppermute | solution.py:32
  11.8 0.1 other_side.1
  11.9 1.3 %collective-permute-done.2.refs_1_ = bf16[1,2,128,256]{3,2,1,0:T(8,128)(2,1)S(1)} collective-permute-done((bf16[1,2,128,256]{3,2,1,0:T(8,128)(2,1)S(1)}, bf16[1,2,128,256]{3,2,1,0:T(8,128)(2,1)S(1)}, u32[]{:S(2)}, u32[]{:S(2)}) %collective-permute-start.2) | collective-permute-done | bytes 131104 | tf_op jit(solution)/shard_map/ppermute | solution.py:36
  13.3 0.2 both_rows.3.refs_2_
  13.4 1.9 %collective-permute-start.4 = (bf16[2,2,128,256]{3,2,1,0:T(8,128)(2,1)S(1)}, bf16[2,2,128,256]{3,2,1,0:T(8,128)(2,1)S(1)}, u32[]{:S(2)}, u32[]{:S(2)}) collective-permute-start(bf16[2,2,128,256]{3,2,1,0:T(8,128)(2,1)S(1)} %both_rows.3.refs_2_), channel_id=1, source_target_pairs={{0,4},{4,8},{8,12},{12,0},{1,5},{5,9},{9,13},{13,1},{2,6},{6,10},{... | collective-permute-start | bytes 786440 | tf_op jit(solution)/shard_map/ppermute | solution.py:27
  15.3 0.2 head_parts.7.refs_0_
  15.5 1.6 %collective-permute-start.11 = (bf16[2,2,128,256]{3,2,1,0:T(8,128)(2,1)S(1)}, bf16[2,2,128,256]{3,2,1,0:T(8,128)(2,1)S(1)}, u32[]{:S(2)}, u32[]{:S(2)}) collective-permute-start(bf16[2,2,128,256]{3,2,1,0:T(8,128)(2,1)S(1)} %head_parts.7.refs_0_), channel_id=1, source_target_pairs={{0,2},{2,0},{1,3},{3,1},{4,6},{6,4},{5,7},{7,5},{8,10},{10,8},{9,1... | collective-permute-start | bytes 786440 | tf_op jit(solution)/shard_map/ppermute | solution.py:32
  17.1 0.6 collective-permute-done.3.refs_1_.refs_3_.refs_0_
  17.7 0.2 head_parts.8
  17.9 0.6 collective-permute-start.7
  18.5 0.7 %and_select_fusion = (f32[1,768,256]{2,1,0:T(8,128)S(1)}, f32[1,768,256]{2,1,0:T(8,128)S(1)}) fusion(s32[256]{0:T(256)S(1)} %get-tuple-element.56, s32[256]{0:T(256)S(1)} %get-tuple-element.54, s32[768]{0:T(1024)S(1)} %get-tuple-element.52, s32[768]{0:T(1024)S(1)} %get-tuple-element.50, pred[768]{0:T(1024)(128)(4,1)S(1)} %get-tuple-element.48, ...), kind=kLoop, calls=%fused_computation.1 | loop fusion | flops 1966080 | bytes 1590784 | tf_op jit(solution)/shard_map/jit(_where)/select_n | solution.py:364
  19.2 0.1 pad_maximum_fusion.refs_0_
  19.3 0.2 head_parts.6.refs_5_
  19.5 0.2 head_parts.9.refs_1_
  19.7 1.0 %collective-permute-start.12 = (bf16[2,2,128,256]{3,2,1,0:T(8,128)(2,1)S(1)}, bf16[2,2,128,256]{3,2,1,0:T(8,128)(2,1)S(1)}, u32[]{:S(2)}, u32[]{:S(2)}) collective-permute-start(bf16[2,2,128,256]{3,2,1,0:T(8,128)(2,1)S(1)} %head_parts.9.refs_1_), channel_id=1, source_target_pairs={{0,4},{4,8},{8,12},{12,0},{1,5},{5,9},{9,13},{13,1},{2,6},{6,10},{... | collective-permute-start | bytes 786440 | tf_op jit(solution)/shard_map/ppermute | solution.py:27
  20.7 4.1 %collective-permute-done.11.refs_0_.refs_2_ = bf16[2,2,128,256]{3,2,1,0:T(8,128)(2,1)S(1)} collective-permute-done((bf16[2,2,128,256]{3,2,1,0:T(8,128)(2,1)S(1)}, bf16[2,2,128,256]{3,2,1,0:T(8,128)(2,1)S(1)}, u32[]{:S(2)}, u32[]{:S(2)}) %collective-permute-start.11) | collective-permute-done | bytes 262176 | tf_op jit(solution)/shard_map/ppermute | solution.py:32
  24.8 0.2 head_parts.11
  25.0 1.6 %collective-permute-start.14 = (bf16[2,2,128,256]{3,2,1,0:T(8,128)(2,1)S(1)}, bf16[2,2,128,256]{3,2,1,0:T(8,128)(2,1)S(1)}, u32[]{:S(2)}, u32[]{:S(2)}) collective-permute-start(bf16[2,2,128,256]{3,2,1,0:T(8,128)(2,1)S(1)} %head_parts.11), channel_id=1, source_target_pairs={{0,2},{2,0},{1,3},{3,1},{4,6},{6,4},{5,7},{7,5},{8,10},{10,8},{9,1... | collective-permute-start | bytes 786440 | tf_op jit(solution)/shard_map/ppermute | solution.py:32
  26.5 3.5 %collective-permute-start.13 = (bf16[2,2,128,256]{3,2,1,0:T(8,128)(2,1)S(1)}, bf16[2,2,128,256]{3,2,1,0:T(8,128)(2,1)S(1)}, u32[]{:S(2)}, u32[]{:S(2)}) collective-permute-start(bf16[2,2,128,256]{3,2,1,0:T(8,128)(2,1)S(1)} %collective-permute-done.11.refs_0_.refs_2_), channel_id=1, source_target_pairs={{0,4},{4,8},{8,12},{1,5},{5,9},{9,13},{2,6},{6,10},{10,14},{3,7},{... | collective-permute-start | bytes 786440 | tf_op jit(solution)/shard_map/ppermute | solution.py:27
  30.1 0.4 collective-permute-done.7.refs_6_
  30.4 3.5 %attention_grads.2 = (f32[2,2,2,128,256]{4,3,2,1,0:T(8,128)S(1)}, bf16[2,128,256]{2,1,0:T(8,128)(2,1)S(1)}, bf16[2,128,256]{2,1,0:T(8,128)(2,1)S(1)}, bf16[2,2,2,128,256]{4,3,2,1,0:T(8,128)(2,1)S(1)}) custom-call(f32[2,768,256]{2,1,0:T(8,128)S(1)} %pad_maximum_fusion.refs_0_, bf16[2,2,128,256]{3,2,1,0:T(8,128)(2,1)S(1)} %both_rows.2.refs_1_, ...), custom_call_target="tpu_custom_call" | custom-call | flops 1006632960 | bytes 4980736 | tf_op jit(solution)/shard_map/attention_grads/pallas_call | solution.py:51
  34.0 1.3 %collective-permute-start.9 = (bf16[2,2,2,128,256]{4,3,2,1,0:T(8,128)(2,1)S(1)}, bf16[2,2,2,128,256]{4,3,2,1,0:T(8,128)(2,1)S(1)}, u32[]{:S(2)}, u32[]{:S(2)}) collective-permute-start(bf16[2,2,2,128,256]{4,3,2,1,0:T(8,128)(2,1)S(1)} %get-tuple-element.35), channel_id=1, source_target_pairs={{4,0},{8,4},{12,8},{5,1},{9,5},{13,9},{6,2},{10,6},{14,10},{7,3},{... | collective-permute-start | bytes 1572872 | tf_op jit(solution)/shard_map/ppermute | solution.py:27
  35.3 0.2 head_parts.10.refs_5_
  35.5 3.6 %attention_grads.3 = (f32[2,2,2,128,256]{4,3,2,1,0:T(8,128)S(1)}, bf16[2,128,256]{2,1,0:T(8,128)(2,1)S(1)}, bf16[2,128,256]{2,1,0:T(8,128)(2,1)S(1)}, bf16[2,2,1...) custom-call(f32[2,768,256]{2,1,0:T(8,128)S(1)} %pad_maximum_fusion.refs_0_, ...), custom_call_target="tpu_custom_call" | custom-call | flops 1006632960 | bytes 4980736 | tf_op jit(solution)/shard_map/attention_grads/pallas_call | solution.py:51
  39.1 1.3 %collective-permute-start.16 = (bf16[2,2,128,256]{3,2,1,0:T(8,128)(2,1)S(1)}, bf16[2,2,128,256]{3,2,1,0:T(8,128)(2,1)S(1)}, u32[]{:S(2)}, u32[]{:S(2)}) collective-permute-start(bf16[2,2,128,256]{3,2,1,0:T(8,128)(2,1)S(1)} %get-tuple-element.43), channel_id=1, source_target_pairs={{4,0},{8,4},{12,8},{5,1},{9,5},{13,9},{6,2},{10,6},{14,10},{7,3},{... | collective-permute-start | bytes 786440 | tf_op jit(solution)/shard_map/ppermute | solution.py:27
  40.4 1.6 %collective-permute-start.8 = (bf16[2,128,256]{2,1,0:T(8,128)(2,1)S(1)}, bf16[2,128,256]{2,1,0:T(8,128)(2,1)S(1)}, u32[]{:S(2)}, u32[]{:S(2)}) collective-permute-start(bf16[2,128,256]{2,1,0:T(8,128)(2,1)S(1)} %get-tuple-element.33), channel_id=1, source_target_pairs={{0,2},{2,0},{1,3},{3,1},{4,6},{6,4},{5,7},{7,5},{8,10},{10,8},{9,1... | collective-permute-start | bytes 393224 | tf_op jit(solution)/shard_map/ppermute | solution.py:32
  41.9 0.5 collective-permute-start.15
  42.5 3.2 %collective-permute-done.8.refs_1_ = bf16[2,128,256]{2,1,0:T(8,128)(2,1)S(1)} collective-permute-done((bf16[2,128,256]{2,1,0:T(8,128)(2,1)S(1)}, bf16[2,128,256]{2,1,0:T(8,128)(2,1)S(1)}, u32[]{:S(2)}, u32[]{:S(2)}) %collective-permute-start.8) | collective-permute-done | bytes 131104 | tf_op jit(solution)/shard_map/ppermute | solution.py:32
  45.6 4.7 %collective-permute-done.9.refs_0_ = bf16[2,2,2,128,256]{4,3,2,1,0:T(8,128)(2,1)S(1)} collective-permute-done((bf16[2,2,2,128,256]{4,3,2,1,0:T(8,128)(2,1)S(1)}, bf16[2,2,2,128,256]{4,3,2,1,0:T(8,128)(2,1)S(1)}, u32[]{:S(2)}, u32[]{:S(2)}) %collective-permute-start.9) | collective-permute-done | bytes 524320 | tf_op jit(solution)/shard_map/ppermute | solution.py:27
  50.4 0.1 summed.3
  50.5 1.6 %collective-permute-start.10 = (bf16[2,2,128,256]{3,2,1,0:T(8,128)(2,1)S(1)}, bf16[2,2,128,256]{3,2,1,0:T(8,128)(2,1)S(1)}, u32[]{:S(2)}, u32[]{:S(2)}) collective-permute-start(bf16[2,2,128,256]{3,2,1,0:T(8,128)(2,1)S(1)} %get-tuple-element.37), channel_id=1, source_target_pairs={{0,2},{2,0},{1,3},{3,1},{4,6},{6,4},{5,7},{7,5},{8,10},{10,8},{9,1... | collective-permute-start | bytes 786440 | tf_op jit(solution)/shard_map/ppermute | solution.py:32
  52.0 1.2 %collective-permute-done.16.refs_0_ = bf16[2,2,128,256]{3,2,1,0:T(8,128)(2,1)S(1)} collective-permute-done((bf16[2,2,128,256]{3,2,1,0:T(8,128)(2,1)S(1)}, bf16[2,2,128,256]{3,2,1,0:T(8,128)(2,1)S(1)}, u32[]{:S(2)}, u32[]{:S(2)}) %collective-permute-start.16) | collective-permute-done | bytes 262176 | tf_op jit(solution)/shard_map/ppermute | solution.py:27
  53.3 1.3 %collective-permute-start.17 = (bf16[2,2,128,256]{3,2,1,0:T(8,128)(2,1)S(1)}, bf16[2,2,128,256]{3,2,1,0:T(8,128)(2,1)S(1)}, u32[]{:S(2)}, u32[]{:S(2)}) collective-permute-start(bf16[2,2,128,256]{3,2,1,0:T(8,128)(2,1)S(1)} %relayed.1), channel_id=1, source_target_pairs={{4,0},{8,4},{12,8},{5,1},{9,5},{13,9},{6,2},{10,6},{14,10},{7,3},{... | collective-permute-start | bytes 786440 | tf_op jit(solution)/shard_map/ppermute | solution.py:27
  54.6 1.6 %collective-permute-start.18 = (bf16[2,2,128,256]{3,2,1,0:T(8,128)(2,1)S(1)}, bf16[2,2,128,256]{3,2,1,0:T(8,128)(2,1)S(1)}, u32[]{:S(2)}, u32[]{:S(2)}) collective-permute-start(bf16[2,2,128,256]{3,2,1,0:T(8,128)(2,1)S(1)} %summed.4.refs_0_), channel_id=1, source_target_pairs={{0,2},{2,0},{1,3},{3,1},{4,6},{6,4},{5,7},{7,5},{8,10},{10,8},{9,1... | collective-permute-start | bytes 786440 | tf_op jit(solution)/shard_map/ppermute | solution.py:32
  56.1 3.5 %collective-permute-done.10.refs_3_ = bf16[2,2,128,256]{3,2,1,0:T(8,128)(2,1)S(1)} collective-permute-done((bf16[2,2,128,256]{3,2,1,0:T(8,128)(2,1)S(1)}, bf16[2,2,128,256]{3,2,1,0:T(8,128)(2,1)S(1)}, u32[]{:S(2)}, u32[]{:S(2)}) %collective-permute-start.10) | collective-permute-done | bytes 262176 | tf_op jit(solution)/shard_map/ppermute | solution.py:32
  59.7 1.8 %collective-permute-done.17.refs_0_ = bf16[2,2,128,256]{3,2,1,0:T(8,128)(2,1)S(1)} collective-permute-done((bf16[2,2,128,256]{3,2,1,0:T(8,128)(2,1)S(1)}, bf16[2,2,128,256]{3,2,1,0:T(8,128)(2,1)S(1)}, u32[]{:S(2)}, u32[]{:S(2)}) %collective-permute-start.17) | collective-permute-done | bytes 262176 | tf_op jit(solution)/shard_map/ppermute | solution.py:27
  61.6 0.9 %collective-permute-done.18.refs_3_ = bf16[2,2,128,256]{3,2,1,0:T(8,128)(2,1)S(1)} collective-permute-done((bf16[2,2,128,256]{3,2,1,0:T(8,128)(2,1)S(1)}, bf16[2,2,128,256]{3,2,1,0:T(8,128)(2,1)S(1)}, u32[]{:S(2)}, u32[]{:S(2)}) %collective-permute-start.18) | collective-permute-done | bytes 262176 | tf_op jit(solution)/shard_map/ppermute | solution.py:32
  62.7 1.7 %collective-permute-done.20.refs_3_ = bf16[3,2,128,256]{3,2,1,0:T(8,128)(2,1)S(1)} collective-permute-done((bf16[3,2,128,256]{3,2,1,0:T(8,128)(2,1)S(1)}, bf16[3,2,128,256]{3,2,1,0:T(8,128)(2,1)S(1)}, u32[]{:S(2)}, u32[]{:S(2)}) %collective-permute-start.20) | collective-permute-done | bytes 393248 | tf_op jit(solution)/shard_map/ppermute | solution.py:36
  64.4 1.3 %laid_out.1 = (bf16[128,2048]{1,0:T(8,128)(2,1)}, bf16[128,2048]{1,0:T(8,128)(2,1)}, bf16[128,2048]{1,0:T(8,128)(2,1)}) custom-call(bf16[3,2,128,256]{3,2,1,0:T(8,128)(2,1)S(1)} %get-tuple-element.38.refs_0_, bf16[3,2,128,256]{3,2,1,0:T(8,128)(2,1)S(1)} %get-tuple-element.44.refs_1_, bf16[3,2,128,256]{3,2,1,0:T(8,128)(2,1)S(1)} %collective-permute-done.19.refs_2_, ...), custom_call_target="tpu_custom_call" | custom-call | bytes 3145728 | tf_op jit(solution)/shard_map/laid_out/pallas_call | solution.py:51
  (25 shorter events, 0.5 us)
Async XLA Ops:
  1.8 5.4 %collective-permute-start = (bf16[2,128,256]{2,1,0:T(8,128)(2,1)S(1)}, bf16[2,128,256]{2,1,0:T(8,128)(2,1)S(1)}, u32[]{:S(2)}, u32[]{:S(2)}) collective-permute-start(bf16[2,128,256]{2,1,0:T(8,128)(2,1)S(1)} %get-tuple-element.26), channel_id=1, source_target_pairs={{0,1},{1,0},{2,3},{3,2},{4,5},{5,4},{6,7},{7,6},{8,9},{9,8},{10,11... | collective-permute-start | bytes 393224 | tf_op jit(solution)/shard_map/ppermute | solution.py:36
  2.3 9.5 %collective-permute-start.1 = (bf16[2,2,128,256]{3,2,1,0:T(8,128)(2,1)S(1)}, bf16[2,2,128,256]{3,2,1,0:T(8,128)(2,1)S(1)}, u32[]{:S(2)}, u32[]{:S(2)}) collective-permute-start(bf16[2,2,128,256]{3,2,1,0:T(8,128)(2,1)S(1)} %get-tuple-element.27), channel_id=1, source_target_pairs={{0,2},{2,0},{1,3},{3,1},{4,6},{6,4},{5,7},{7,5},{8,10},{10,8},{9,1... | collective-permute-start | bytes 786440 | tf_op jit(solution)/shard_map/ppermute | solution.py:32
  4.9 2.2 %copy-start = (s32[2048]{0:T(1024)S(1)}, s32[2048]{0:T(1024)}, u32[]{:S(2)}) copy-start(s32[2048]{0:T(1024)} %param.9) | copy-start | bytes 24580
  6.5 10.6 %collective-permute-start.5 = (bf16[2,2,128,256]{3,2,1,0:T(8,128)(2,1)S(1)}, bf16[2,2,128,256]{3,2,1,0:T(8,128)(2,1)S(1)}, u32[]{:S(2)}, u32[]{:S(2)}) collective-permute-start(bf16[2,2,128,256]{3,2,1,0:T(8,128)(2,1)S(1)} %get-tuple-element.29), channel_id=1, source_target_pairs={{0,1},{1,0},{2,3},{3,2},{4,5},{5,4},{6,7},{7,6},{8,9},{9,8},{10,11... | collective-permute-start | bytes 786440 | tf_op jit(solution)/shard_map/ppermute | solution.py:36
  6.7 8.6 %collective-permute-start.6 = (bf16[4,2,128,256]{3,2,1,0:T(8,128)(2,1)S(1)}, bf16[4,2,128,256]{3,2,1,0:T(8,128)(2,1)S(1)}, u32[]{:S(2)}, u32[]{:S(2)}) collective-permute-start(bf16[4,2,128,256]{3,2,1,0:T(8,128)(2,1)S(1)} %get-tuple-element.31), channel_id=1, source_target_pairs={{0,1},{1,0},{2,3},{3,2},{4,5},{5,4},{6,7},{7,6},{8,9},{9,8},{10,11... | collective-permute-start | bytes 1572872 | tf_op jit(solution)/shard_map/ppermute | solution.py:36
  7.4 10.3 %collective-permute-start.3 = (bf16[2,2,128,256]{3,2,1,0:T(8,128)(2,1)S(1)}, bf16[2,2,128,256]{3,2,1,0:T(8,128)(2,1)S(1)}, u32[]{:S(2)}, u32[]{:S(2)}) collective-permute-start(bf16[2,2,128,256]{3,2,1,0:T(8,128)(2,1)S(1)} %both_rows.2.refs_1_), channel_id=1, source_target_pairs={{0,4},{4,8},{8,12},{12,0},{1,5},{5,9},{9,13},{13,1},{2,6},{6,10},{... | collective-permute-start | bytes 786440 | tf_op jit(solution)/shard_map/ppermute | solution.py:27
  11.9 1.4 %collective-permute-start.2 = (bf16[1,2,128,256]{3,2,1,0:T(8,128)(2,1)S(1)}, bf16[1,2,128,256]{3,2,1,0:T(8,128)(2,1)S(1)}, u32[]{:S(2)}, u32[]{:S(2)}) collective-permute-start(bf16[1,2,128,256]{3,2,1,0:T(8,128)(2,1)S(1)} %other_side.1), channel_id=1, source_target_pairs={{0,1},{1,0},{2,3},{3,2},{4,5},{5,4},{6,7},{7,6},{8,9},{9,8},{10,11... | collective-permute-start | bytes 393224 | tf_op jit(solution)/shard_map/ppermute | solution.py:36
  13.4 16.6 %collective-permute-start.4 = (bf16[2,2,128,256]{3,2,1,0:T(8,128)(2,1)S(1)}, bf16[2,2,128,256]{3,2,1,0:T(8,128)(2,1)S(1)}, u32[]{:S(2)}, u32[]{:S(2)}) collective-permute-start(bf16[2,2,128,256]{3,2,1,0:T(8,128)(2,1)S(1)} %both_rows.3.refs_2_), channel_id=1, source_target_pairs={{0,4},{4,8},{8,12},{12,0},{1,5},{5,9},{9,13},{13,1},{2,6},{6,10},{... | collective-permute-start | bytes 786440 | tf_op jit(solution)/shard_map/ppermute | solution.py:27
  15.5 9.3 %collective-permute-start.11 = (bf16[2,2,128,256]{3,2,1,0:T(8,128)(2,1)S(1)}, bf16[2,2,128,256]{3,2,1,0:T(8,128)(2,1)S(1)}, u32[]{:S(2)}, u32[]{:S(2)}) collective-permute-start(bf16[2,2,128,256]{3,2,1,0:T(8,128)(2,1)S(1)} %head_parts.7.refs_0_), channel_id=1, source_target_pairs={{0,2},{2,0},{1,3},{3,1},{4,6},{6,4},{5,7},{7,5},{8,10},{10,8},{9,1... | collective-permute-start | bytes 786440 | tf_op jit(solution)/shard_map/ppermute | solution.py:32
  17.9 12.5 %collective-permute-start.7 = (bf16[2,2,128,256]{3,2,1,0:T(8,128)(2,1)S(1)}, bf16[2,2,128,256]{3,2,1,0:T(8,128)(2,1)S(1)}, u32[]{:S(2)}, u32[]{:S(2)}) collective-permute-start(bf16[2,2,128,256]{3,2,1,0:T(8,128)(2,1)S(1)} %head_parts.8), channel_id=1, source_target_pairs={{0,2},{2,0},{1,3},{3,1},{4,6},{6,4},{5,7},{7,5},{8,10},{10,8},{9,1... | collective-permute-start | bytes 786440 | tf_op jit(solution)/shard_map/ppermute | solution.py:32
  19.7 15.8 %collective-permute-start.12 = (bf16[2,2,128,256]{3,2,1,0:T(8,128)(2,1)S(1)}, bf16[2,2,128,256]{3,2,1,0:T(8,128)(2,1)S(1)}, u32[]{:S(2)}, u32[]{:S(2)}) collective-permute-start(bf16[2,2,128,256]{3,2,1,0:T(8,128)(2,1)S(1)} %head_parts.9.refs_1_), channel_id=1, source_target_pairs={{0,4},{4,8},{8,12},{12,0},{1,5},{5,9},{9,13},{13,1},{2,6},{6,10},{... | collective-permute-start | bytes 786440 | tf_op jit(solution)/shard_map/ppermute | solution.py:27
  25.0 10.5 %collective-permute-start.14 = (bf16[2,2,128,256]{3,2,1,0:T(8,128)(2,1)S(1)}, bf16[2,2,128,256]{3,2,1,0:T(8,128)(2,1)S(1)}, u32[]{:S(2)}, u32[]{:S(2)}) collective-permute-start(bf16[2,2,128,256]{3,2,1,0:T(8,128)(2,1)S(1)} %head_parts.11), channel_id=1, source_target_pairs={{0,2},{2,0},{1,3},{3,1},{4,6},{6,4},{5,7},{7,5},{8,10},{10,8},{9,1... | collective-permute-start | bytes 786440 | tf_op jit(solution)/shard_map/ppermute | solution.py:32
  26.5 9.0 %collective-permute-start.13 = (bf16[2,2,128,256]{3,2,1,0:T(8,128)(2,1)S(1)}, bf16[2,2,128,256]{3,2,1,0:T(8,128)(2,1)S(1)}, u32[]{:S(2)}, u32[]{:S(2)}) collective-permute-start(bf16[2,2,128,256]{3,2,1,0:T(8,128)(2,1)S(1)} %collective-permute-done.11.refs_0_.refs_2_), channel_id=1, source_target_pairs={{0,4},{4,8},{8,12},{1,5},{5,9},{9,13},{2,6},{6,10},{10,14},{3,7},{... | collective-permute-start | bytes 786440 | tf_op jit(solution)/shard_map/ppermute | solution.py:27
  34.0 16.4 %collective-permute-start.9 = (bf16[2,2,2,128,256]{4,3,2,1,0:T(8,128)(2,1)S(1)}, bf16[2,2,2,128,256]{4,3,2,1,0:T(8,128)(2,1)S(1)}, u32[]{:S(2)}, u32[]{:S(2)}) collective-permute-start(bf16[2,2,2,128,256]{4,3,2,1,0:T(8,128)(2,1)S(1)} %get-tuple-element.35), channel_id=1, source_target_pairs={{4,0},{8,4},{12,8},{5,1},{9,5},{13,9},{6,2},{10,6},{14,10},{7,3},{... | collective-permute-start | bytes 1572872 | tf_op jit(solution)/shard_map/ppermute | solution.py:27
  39.1 14.1 %collective-permute-start.16 = (bf16[2,2,128,256]{3,2,1,0:T(8,128)(2,1)S(1)}, bf16[2,2,128,256]{3,2,1,0:T(8,128)(2,1)S(1)}, u32[]{:S(2)}, u32[]{:S(2)}) collective-permute-start(bf16[2,2,128,256]{3,2,1,0:T(8,128)(2,1)S(1)} %get-tuple-element.43), channel_id=1, source_target_pairs={{4,0},{8,4},{12,8},{5,1},{9,5},{13,9},{6,2},{10,6},{14,10},{7,3},{... | collective-permute-start | bytes 786440 | tf_op jit(solution)/shard_map/ppermute | solution.py:27
  40.4 5.3 %collective-permute-start.8 = (bf16[2,128,256]{2,1,0:T(8,128)(2,1)S(1)}, bf16[2,128,256]{2,1,0:T(8,128)(2,1)S(1)}, u32[]{:S(2)}, u32[]{:S(2)}) collective-permute-start(bf16[2,128,256]{2,1,0:T(8,128)(2,1)S(1)} %get-tuple-element.33), channel_id=1, source_target_pairs={{0,2},{2,0},{1,3},{3,1},{4,6},{6,4},{5,7},{7,5},{8,10},{10,8},{9,1... | collective-permute-start | bytes 393224 | tf_op jit(solution)/shard_map/ppermute | solution.py:32
  41.9 10.1 %collective-permute-start.15 = (bf16[2,128,256]{2,1,0:T(8,128)(2,1)S(1)}, bf16[2,128,256]{2,1,0:T(8,128)(2,1)S(1)}, u32[]{:S(2)}, u32[]{:S(2)}) collective-permute-start(bf16[2,128,256]{2,1,0:T(8,128)(2,1)S(1)} %get-tuple-element.40), channel_id=1, source_target_pairs={{0,2},{2,0},{1,3},{3,1},{4,6},{6,4},{5,7},{7,5},{8,10},{10,8},{9,1... | collective-permute-start | bytes 393224 | tf_op jit(solution)/shard_map/ppermute | solution.py:32
  50.5 9.1 %collective-permute-start.10 = (bf16[2,2,128,256]{3,2,1,0:T(8,128)(2,1)S(1)}, bf16[2,2,128,256]{3,2,1,0:T(8,128)(2,1)S(1)}, u32[]{:S(2)}, u32[]{:S(2)}) collective-permute-start(bf16[2,2,128,256]{3,2,1,0:T(8,128)(2,1)S(1)} %get-tuple-element.37), channel_id=1, source_target_pairs={{0,2},{2,0},{1,3},{3,1},{4,6},{6,4},{5,7},{7,5},{8,10},{10,8},{9,1... | collective-permute-start | bytes 786440 | tf_op jit(solution)/shard_map/ppermute | solution.py:32
  53.3 8.3 %collective-permute-start.17 = (bf16[2,2,128,256]{3,2,1,0:T(8,128)(2,1)S(1)}, bf16[2,2,128,256]{3,2,1,0:T(8,128)(2,1)S(1)}, u32[]{:S(2)}, u32[]{:S(2)}) collective-permute-start(bf16[2,2,128,256]{3,2,1,0:T(8,128)(2,1)S(1)} %relayed.1), channel_id=1, source_target_pairs={{4,0},{8,4},{12,8},{5,1},{9,5},{13,9},{6,2},{10,6},{14,10},{7,3},{... | collective-permute-start | bytes 786440 | tf_op jit(solution)/shard_map/ppermute | solution.py:27
  54.6 7.9 %collective-permute-start.18 = (bf16[2,2,128,256]{3,2,1,0:T(8,128)(2,1)S(1)}, bf16[2,2,128,256]{3,2,1,0:T(8,128)(2,1)S(1)}, u32[]{:S(2)}, u32[]{:S(2)}) collective-permute-start(bf16[2,2,128,256]{3,2,1,0:T(8,128)(2,1)S(1)} %summed.4.refs_0_), channel_id=1, source_target_pairs={{0,2},{2,0},{1,3},{3,1},{4,6},{6,4},{5,7},{7,5},{8,10},{10,8},{9,1... | collective-permute-start | bytes 786440 | tf_op jit(solution)/shard_map/ppermute | solution.py:32
  59.7 3.0 %collective-permute-start.19 = (bf16[3,2,128,256]{3,2,1,0:T(8,128)(2,1)S(1)}, bf16[3,2,128,256]{3,2,1,0:T(8,128)(2,1)S(1)}, u32[]{:S(2)}, u32[]{:S(2)}) collective-permute-start(bf16[3,2,128,256]{3,2,1,0:T(8,128)(2,1)S(1)} %get-tuple-element.45), channel_id=1, source_target_pairs={{0,1},{1,0},{2,3},{3,2},{4,5},{5,4},{6,7},{7,6},{8,9},{9,8},{10,11... | collective-permute-start | bytes 1179656 | tf_op jit(solution)/shard_map/ppermute | solution.py:36
  62.6 1.8 %collective-permute-start.20 = (bf16[3,2,128,256]{3,2,1,0:T(8,128)(2,1)S(1)}, bf16[3,2,128,256]{3,2,1,0:T(8,128)(2,1)S(1)}, u32[]{:S(2)}, u32[]{:S(2)}) collective-permute-start(bf16[3,2,128,256]{3,2,1,0:T(8,128)(2,1)S(1)} %get-tuple-element.46), channel_id=1, source_target_pairs={{0,1},{1,0},{2,3},{3,2},{4,5},{5,4},{6,7},{7,6},{8,9},{9,8},{10,11... | collective-permute-start | bytes 1179656 | tf_op jit(solution)/shard_map/ppermute | solution.py:36

commit v14 on v12

--- a/solution.py
+++ b/solution.py
@@ -192,10 +192,10 @@
     return call(kernel, [value] + after, [shape(*value.shape)], scratch, "relayed")[0]
 
 
-def attention_grads(bias, kv, kv_earlier, qg, split, after):
+def attention_grads(bias, kv, kv_earlier, qg, split, first, heads, after):
     peers = len(kv)
-    _, _, rows, cut = kv[0].shape
-    heads = cut // HD
+    rows, cut = kv[0].shape[2], heads * HD
+    chosen = pl.ds(first * HD, cut)
     strip = rows * peers
     early_count = peers if split else 1
 
@@ -210,9 +210,9 @@
         for by in range(peers):
             at = lax.rem(s - by + peers, peers)
             moves += [
-                (early_in[by], kv_all.at[:, 0:2, at]),
-                (kv_in[by], kv_all.at[:, 2:4, at]),
-                (qg_in[by], qg_all.at[:, :, at]),
+                (early_in[by].at[:, :, :, chosen], kv_all.at[:, 0:2, at]),
+                (kv_in[by].at[:, :, :, chosen], kv_all.at[:, 2:4, at]),
+                (qg_in[by].at[:, :, :, chosen], qg_all.at[:, :, at]),
             ]
         run_moves(moves, sems)
         strips = [(head, tile) for head in range(heads) for tile in range(2)]
@@ -292,21 +292,43 @@
 
 
 def summed(own, later, turns, after):
-    _, _, peers, rows, cut = own.shape
-    split = len(later) > 1 or later[0].ndim == 4
-
-    def kernel(own_ref, *refs):
-        later_refs, outs = refs[:len(later)], refs[len(later) + len(after):]
+    _, _, peers, rows, _ = own[0].shape
+    widths = [array.shape[-1] for array in own]
+    split = later[0].ndim == 4
+
+    def kernel(*refs):
+        own_refs, later_refs = refs[:len(own)], refs[len(own):len(own) + len(later)]
+        outs = refs[len(own) + len(later) + len(after):]
         s = lax.axis_index("sub")
         for place, (by, out) in enumerate(zip(turns, outs)):
             at = lax.rem(s + by, peers)
-            for which in range(2):
-                for row in range(2):
-                    term = later_refs[place][which, row] if split else later_refs[0][which, row, at]
-                    out[which, row] = (own_ref[which, row, at] + term.astype(WIDE)).astype(LOW)
-
-    outs = [shape(2, 2, rows, cut)] * len(turns)
-    return call(kernel, [own] + later + after, outs, [], "summed", whole=True)
+            start = 0
+            for group, width in enumerate(widths):
+                for which in range(2):
+                    for row in range(2):
+                        term = later_refs[place][which, row] if split else later_refs[group][which, row, at]
+                        total = own_refs[group][which, row, at] + term.astype(WIDE)
+                        out[which, row, :, pl.ds(start, width)] = total.astype(LOW)
+                start += width
+
+    outs = [shape(2, 2, rows, sum(widths))] * len(turns)
+    return call(kernel, own + later + after, outs, [], "summed", whole=True)
+
+
+def side_by_side(groups):
+    count, peers = len(groups), len(groups[0])
+    _, rows, _ = groups[0][0].shape
+    widths = [group[0].shape[-1] for group in groups]
+
+    def kernel(*refs):
+        for by in range(peers):
+            start = 0
+            for group, width in enumerate(widths):
+                refs[count * peers + by][:, :, pl.ds(start, width)] = refs[group * peers + by][...]
+                start += width
+
+    ins = [array for group in groups for array in group]
+    return call(kernel, ins, [shape(2, rows, sum(widths))] * peers, [], "side_by_side", whole=True)
 
 
 def rows_for_pair(dq, dkv):
@@ -400,22 +422,32 @@
         own_earlier.append(along_blocks(kv_own[index][0], 1, True))
         qg_sends.append(head_parts(*qg_parts[index], others, qg[index - 1] if index else []))
         qg.append([round_sub(value, by) for by, value in zip(others, qg_sends[index])])
-    kept, paired = [], []
-    for index in range(count):
+    kept, paired, first_dq, back = [], [], [], []
+    for index, (low, high) in enumerate(spans):
         last = index == count - 1
-        forward = [relayed(value, [first_dq]) if index else value for value in kv[index]]
+        forward = [relayed(value, first_dq) if index else value for value in kv[index]]
         earlier = [own_earlier[index]] + [along_blocks(value, 1, not last) for value in forward]
         qg_all = head_parts(*qg_parts[index], [0], []) + qg[index]
-        grads, dq, early = attention_grads(bias, kv_own[index] + kv[index], earlier, qg_all, last, [])
-        first_dq = dq[0]
-        dq = [dq[0]] + [round_sub(dq[by], by) for by in others]
+        kv_all = kv_own[index] + kv[index]
+        heads = (high - low) // HD
         if last:
+            grads, dq, early = attention_grads(bias, kv_all, earlier, qg_all, True, 0, heads, back)
+            dq = [dq[0]] + [round_sub(dq[by], by) for by in others]
             later = [along_blocks(value, -1, False) for value in early[1:]]
-            dkv = summed(grads, later, others, dq[1:])
-            near = along_blocks(relayed(early[0], dkv), -1, False)
-            dkv = summed(grads, [near], [0], []) + [round_sub(value, by) for by, value in zip(others, dkv)]
+            dkv = summed([grads], later, others, dq[1:])
+            near = along_blocks(relayed(early[0], dq[1:]), -1, False)
+            dkv = summed([grads], [near], [0], []) + [round_sub(value, by) for by, value in zip(others, dkv)]
         else:
-            dkv = summed(grads, [along_blocks(early[0], -1, False)], [0] + others, dq[1:])
+            groups, turn = [], []
+            for head in range(heads):
+                groups.append(attention_grads(bias, kv_all, earlier, qg_all, False, head, 1, turn))
+                turn = groups[-1][1][:1]
+                first_dq = first_dq or turn
+            later = [along_blocks(early[0], -1, False) for _, _, early in groups]
+            back = later[:1]
+            dq = side_by_side([dq for _, dq, _ in groups]) if heads > 1 else groups[0][1]
+            dq = [dq[0]] + [round_sub(dq[by], by) for by in others]
+            dkv = summed([grads for grads, _, _ in groups], later, [0] + others, dq[1:])
             dkv = [dkv[0]] + [round_sub(dkv[by], by) for by in others]
         send, keep = rows_for_pair(dq, dkv)
         kept.append(keep)

time: 63.2 us -> 64.6 us (1.022)
  starting transfers between devices: 22.7 us -> 25.4 us
  waiting for transfers between devices: 25.2 us -> 22.5 us
  Pallas kernels: 13.2 us -> 13.9 us
    ppermute x7 -> x8, waiting for transfers between devices: 15.4 us -> 7.34 us  [along_blocks(): return lax.ppermute(value, 'blk', pairs)]
    ppermute x8, waiting for transfers between devices: 8.08 us -> 13.4 us  [round_sub(): lax.ppermute(value, 'sub', [(i, (i + by) % peers) for i in range(peers)])]
    ppermute x7 -> x8, starting transfers between devices: 9.36 us -> 13.2 us  [along_blocks(): return lax.ppermute(value, 'blk', pairs)]
    ppermute x8, starting transfers between devices: 12 us -> 10.8 us  [round_sub(): lax.ppermute(value, 'sub', [(i, (i + by) % peers) for i in range(peers)])]
    pallas_call x19 -> x21, Pallas kernels: 10.4 us -> 11.2 us  [call(): pl.pallas_call(kernel, out_shape=outs, in_specs=[spec] * len(ins), out_sp...]
  transfers between devices with their start and end apart: 21 -> 22, of which waited for: 12 -> 10; matrix products, arithmetic and copies ran while one was open for 1% -> 1% of each run, Pallas kernels for 17% -> 18%
where the time goes in v14:
time: 64.6 us; the launch traced here: 63.6 us
  starting transfers between devices  25.4 us (39%)
  waiting for transfers between devices  22.5 us (35%)
  Pallas kernels  13.9 us (22%)
  between operations  0.96 us (1%)
  other arithmetic  0.79 us (1%)
    ppermute x8, waiting for transfers between devices, round_sub(): lax.ppermute(value, 'sub', [(i, (i + by) % peers) for i in range(peers)])  13.4 us
    ppermute x8, starting transfers between devices, along_blocks(): return lax.ppermute(value, 'blk', pairs)  13.2 us
    pallas_call x21, Pallas kernels, call(): pl.pallas_call(kernel, out_shape=outs, in_specs=[spec] * len(ins), out_sp...  11.2 us
    ppermute x8, starting transfers between devices, round_sub(): lax.ppermute(value, 'sub', [(i, (i + by) % peers) for i in range(peers)])  10.8 us
    ppermute x8, waiting for transfers between devices, along_blocks(): return lax.ppermute(value, 'blk', pairs)  7.34 us
    ppermute x6, waiting for transfers between devices, swapped(): return lax.ppermute(value, 'pair', [(0, 1), (1, 0)])  1.71 us
    pallas_call x1, Pallas kernels, first_parts(): pl.pallas_call(kernel, out_shape=outs, in_specs=[spec] * (len(held) + len...  1.64 us
    ppermute x6, starting transfers between devices, swapped(): return lax.ppermute(value, 'pair', [(0, 1), (1, 0)])  1.31 us
  transfers between devices with their start and end apart: 22, of which 10 were waited for; matrix products, arithmetic and copies ran while one was open for 1% of the time, Pallas kernels for 18%

profile of v14, /device:TPU:0, one launch (start us, length us, event | category | flops | bytes accessed | tf_op | source)
XLA Modules:
  0.0 63.6 jit_solution(6807062049150966109)
XLA Ops:
  0.6 1.2 %first_keys.1 = (bf16[2,2,128,256]{3,2,1,0:T(8,128)(2,1)S(1)}, bf16[2,128,256]{2,1,0:T(8,128)(2,1)S(1)}, bf16[2,128,256]{2,1,0:T(8,128)(2,1)S(1)}) custom-call(bf16[128,2048]{1,0:T(8,128)(2,1)} %refs_2_.1, bf16[128,2048]{1,0:T(8,128)(2,1)} %refs_3_.1), custom_call_target="tpu_custom_call" | custom-call | tf_op jit(solution)/shard_map/first_keys/pallas_call | solution.py:127
  1.8 0.5 collective-permute-start
  2.3 2.6 %collective-permute-start.1 = (bf16[2,2,128,256]{3,2,1,0:T(8,128)(2,1)S(1)}, bf16[2,2,128,256]{3,2,1,0:T(8,128)(2,1)S(1)}, u32[]{:S(2)}, u32[]{:S(2)}) collective-permute-start(bf16[2,2,128,256]{3,2,1,0:T(8,128)(2,1)S(1)} %get-tuple-element.33), channel_id=1, source_target_pairs={{0,2},{2,0},{1,3},{3,1},{4,6},{6,4},{5,7},{7,5},{8,10},{10,8},{9,1... | collective-permute-start | bytes 786440 | tf_op jit(solution)/shard_map/ppermute | solution.py:32
  4.9 1.6 %first_parts.1 = (bf16[2,2,128,256]{3,2,1,0:T(8,128)(2,1)S(1)}, bf16[2,2,128,256]{3,2,1,0:T(8,128)(2,1)S(1)}, bf16[4,2,128,256]{3,2,1,0:T(8,128)(2,1)S(1)}, bf16[4,2,128,256]{3,2,1,0:T(8,128)(2,1)S(1)}) custom-call(bf16[128,2048]{1,0:T(8,128)(2,1)} %refs_4_.1, bf16[128,2048]{1,0:T(8,128)(2,1)} %refs_5_.1, bf16[128,2048]{1,0:T(8,128)(2,1)} %refs_2_.1, ...), custom_call_target="tpu_custom_call" | custom-call | tf_op jit(solution)/shard_map/first_parts/pallas_call | solution.py:92
  6.5 0.2 collective-permute-start.5
  6.7 0.3 collective-permute-start.11
  7.1 0.1 pad_dynamic-slice_fusion
  7.2 0.2 both_rows.2.refs_1_
  7.4 1.6 %collective-permute-start.3 = (bf16[2,2,128,256]{3,2,1,0:T(8,128)(2,1)S(1)}, bf16[2,2,128,256]{3,2,1,0:T(8,128)(2,1)S(1)}, u32[]{:S(2)}, u32[]{:S(2)}) collective-permute-start(bf16[2,2,128,256]{3,2,1,0:T(8,128)(2,1)S(1)} %both_rows.2.refs_1_), channel_id=1, source_target_pairs={{0,4},{4,8},{8,12},{12,0},{1,5},{5,9},{9,13},{13,1},{2,6},{6,10},{... | collective-permute-start | bytes 786440 | tf_op jit(solution)/shard_map/ppermute | solution.py:27
  9.0 2.7 %collective-permute-done.1.refs_0_ = bf16[2,2,128,256]{3,2,1,0:T(8,128)(2,1)S(1)} collective-permute-done((bf16[2,2,128,256]{3,2,1,0:T(8,128)(2,1)S(1)}, bf16[2,2,128,256]{3,2,1,0:T(8,128)(2,1)S(1)}, u32[]{:S(2)}, u32[]{:S(2)}) %collective-permute-start.1) | collective-permute-done | bytes 262176 | tf_op jit(solution)/shard_map/ppermute | solution.py:32
  11.8 0.1 other_side.1
  12.0 0.2 head_parts.7
  12.2 1.8 %collective-permute-start.6 = (bf16[2,2,128,256]{3,2,1,0:T(8,128)(2,1)S(1)}, bf16[2,2,128,256]{3,2,1,0:T(8,128)(2,1)S(1)}, u32[]{:S(2)}, u32[]{:S(2)}) collective-permute-start(bf16[2,2,128,256]{3,2,1,0:T(8,128)(2,1)S(1)} %head_parts.7), channel_id=1, source_target_pairs={{0,2},{2,0},{1,3},{3,1},{4,6},{6,4},{5,7},{7,5},{8,10},{10,8},{9,1... | collective-permute-start | bytes 786440 | tf_op jit(solution)/shard_map/ppermute | solution.py:32
  14.0 0.2 both_rows.3.refs_2_.refs_0_
  14.2 1.6 %collective-permute-start.4 = (bf16[2,2,128,256]{3,2,1,0:T(8,128)(2,1)S(1)}, bf16[2,2,128,256]{3,2,1,0:T(8,128)(2,1)S(1)}, u32[]{:S(2)}, u32[]{:S(2)}) collective-permute-start(bf16[2,2,128,256]{3,2,1,0:T(8,128)(2,1)S(1)} %both_rows.3.refs_2_.refs_0_), channel_id=1, source_target_pairs={{0,4},{4,8},{8,12},{12,0},{1,5},{5,9},{9,13},{13,1},{2,6},{6,10},{... | collective-permute-start | bytes 786440 | tf_op jit(solution)/shard_map/ppermute | solution.py:27
  15.8 1.9 %collective-permute-done.3.refs_3_.refs_0_.refs_1_ = bf16[2,2,128,256]{3,2,1,0:T(8,128)(2,1)S(1)} collective-permute-done((bf16[2,2,128,256]{3,2,1,0:T(8,128)(2,1)S(1)}, bf16[2,2,128,256]{3,2,1,0:T(8,128)(2,1)S(1)}, u32[]{:S(2)}, u32[]{:S(2)}) %collective-permute-start.3) | collective-permute-done | bytes 262176 | tf_op jit(solution)/shard_map/ppermute | solution.py:27
  17.7 0.2 head_parts.9
  17.9 0.6 collective-permute-start.12
  18.5 0.7 %and_select_fusion = (f32[1,768,256]{2,1,0:T(8,128)S(1)}, f32[1,768,256]{2,1,0:T(8,128)S(1)}) fusion(s32[256]{0:T(256)S(1)} %get-tuple-element.68, s32[256]{0:T(256)S(1)} %get-tuple-element.66, s32[768]{0:T(1024)S(1)} %get-tuple-element.64, s32[768]{0:T(1024)S(1)} %get-tuple-element.62, pred[768]{0:T(1024)(128)(4,1)S(1)} %get-tuple-element.60, ...), kind=kLoop, calls=%fused_computation.1 | loop fusion | flops 1966080 | bytes 1590784 | tf_op jit(solution)/shard_map/jit(_where)/select_n | solution.py:386
  19.2 0.1 pad_maximum_fusion.refs_0_
  19.3 0.2 head_parts.6.refs_5_
  19.5 0.2 head_parts.8.refs_1_
  19.7 0.2 collective-permute-start.13
  19.9 1.4 %collective-permute-done.6.refs_6_.refs_0_ = bf16[2,2,128,256]{3,2,1,0:T(8,128)(2,1)S(1)} collective-permute-done((bf16[2,2,128,256]{3,2,1,0:T(8,128)(2,1)S(1)}, bf16[2,2,128,256]{3,2,1,0:T(8,128)(2,1)S(1)}, u32[]{:S(2)}, u32[]{:S(2)}) %collective-permute-start.6) | collective-permute-done | bytes 262176 | tf_op jit(solution)/shard_map/ppermute | solution.py:32
  21.3 0.2 head_parts.11
  21.5 1.8 %collective-permute-start.15 = (bf16[2,2,128,256]{3,2,1,0:T(8,128)(2,1)S(1)}, bf16[2,2,128,256]{3,2,1,0:T(8,128)(2,1)S(1)}, u32[]{:S(2)}, u32[]{:S(2)}) collective-permute-start(bf16[2,2,128,256]{3,2,1,0:T(8,128)(2,1)S(1)} %head_parts.11), channel_id=1, source_target_pairs={{0,2},{2,0},{1,3},{3,1},{4,6},{6,4},{5,7},{7,5},{8,10},{10,8},{9,1... | collective-permute-start | bytes 786440 | tf_op jit(solution)/shard_map/ppermute | solution.py:32
  23.3 1.8 %collective-permute-done.4.refs_4_ = bf16[2,2,128,256]{3,2,1,0:T(8,128)(2,1)S(1)} collective-permute-done((bf16[2,2,128,256]{3,2,1,0:T(8,128)(2,1)S(1)}, bf16[2,2,128,256]{3,2,1,0:T(8,128)(2,1)S(1)}, u32[]{:S(2)}, u32[]{:S(2)}) %collective-permute-start.4) | collective-permute-done | bytes 262176 | tf_op jit(solution)/shard_map/ppermute | solution.py:27
  25.2 2.1 %attention_grads.3 = (f32[2,2,2,128,128]{4,3,2,1,0:T(8,128)S(1)}, bf16[2,128,128]{2,1,0:T(8,128)(2,1)S(1)}, bf16[2,128,128]{2,1,0:T(8,128)(2,1)S(1)}, bf16[2,2,2,128,128]{4,3,2,1,0:T(8,128)(2,1)S(1)}) custom-call(f32[2,768,256]{2,1,0:T(8,128)S(1)} %pad_maximum_fusion.refs_0_, bf16[2,2,128,256]{3,2,1,0:T(8,128)(2,1)S(1)} %both_rows.2.refs_1_, ...), custom_call_target="tpu_custom_call" | custom-call | flops 503316480 | bytes 4063232 | tf_op jit(solution)/shard_map/attention_grads/pallas_call | solution.py:51
  27.3 1.3 %collective-permute-start.8 = (bf16[2,2,2,128,128]{4,3,2,1,0:T(8,128)(2,1)S(1)}, bf16[2,2,2,128,128]{4,3,2,1,0:T(8,128)(2,1)S(1)}, u32[]{:S(2)}, u32[]{:S(2)}) collective-permute-start(bf16[2,2,2,128,128]{4,3,2,1,0:T(8,128)(2,1)S(1)} %get-tuple-element.44), channel_id=1, source_target_pairs={{4,0},{8,4},{12,8},{5,1},{9,5},{13,9},{6,2},{10,6},{14,10},{7,3},{... | collective-permute-start | bytes 786440 | tf_op jit(solution)/shard_map/ppermute | solution.py:27
  28.6 4.6 %collective-permute-start.14 = (bf16[2,2,128,256]{3,2,1,0:T(8,128)(2,1)S(1)}, bf16[2,2,128,256]{3,2,1,0:T(8,128)(2,1)S(1)}, u32[]{:S(2)}, u32[]{:S(2)}) collective-permute-start(bf16[2,2,128,256]{3,2,1,0:T(8,128)(2,1)S(1)} %relayed.2), channel_id=1, source_target_pairs={{0,4},{4,8},{8,12},{1,5},{5,9},{9,13},{2,6},{6,10},{10,14},{3,7},{... | collective-permute-start | bytes 786440 | tf_op jit(solution)/shard_map/ppermute | solution.py:27
  33.2 0.2 head_parts.10.refs_5_
  33.4 2.1 %attention_grads.4 = (f32[2,2,2,128,128]{4,3,2,1,0:T(8,128)S(1)}, bf16[2,128,128]{2,1,0:T(8,128)(2,1)S(1)}, bf16[2,128,128]{2,1,0:T(8,128)(2,1)S(1)}, bf16[2,2,2,128,128]{4,3,2,1,0:T(8,128)(2,1)S(1)}) custom-call(f32[2,768,256]{2,1,0:T(8,128)S(1)} %pad_maximum_fusion.refs_0_, bf16[2,2,128,256]{3,2,1,0:T(8,128)(2,1)S(1)} %both_rows.2.refs_1_, ...), custom_call_target="tpu_custom_call" | custom-call | flops 503316480 | bytes 4128768 | tf_op jit(solution)/shard_map/attention_grads/pallas_call | solution.py:51
  35.5 1.3 %collective-permute-start.9 = (bf16[2,2,2,128,128]{4,3,2,1,0:T(8,128)(2,1)S(1)}, bf16[2,2,2,128,128]{4,3,2,1,0:T(8,128)(2,1)S(1)}, u32[]{:S(2)}, u32[]{:S(2)}) collective-permute-start(bf16[2,2,2,128,128]{4,3,2,1,0:T(8,128)(2,1)S(1)} %get-tuple-element.45), channel_id=1, source_target_pairs={{4,0},{8,4},{12,8},{5,1},{9,5},{13,9},{6,2},{10,6},{14,10},{7,3},{... | collective-permute-start | bytes 786440 | tf_op jit(solution)/shard_map/ppermute | solution.py:27
  36.9 0.5 collective-permute-done.14.refs_4_
  37.4 3.5 %attention_grads.5 = (f32[2,2,2,128,256]{4,3,2,1,0:T(8,128)S(1)}, bf16[2,128,256]{2,1,0:T(8,128)(2,1)S(1)}, bf16[2,128,256]{2,1,0:T(8,128)(2,1)S(1)}, bf16[2,2,1...) custom-call(f32[2,768,256]{2,1,0:T(8,128)S(1)} %pad_maximum_fusion.refs_0_, ...), custom_call_target="tpu_custom_call" | custom-call | flops 1006632960 | bytes 5242880 | tf_op jit(solution)/shard_map/attention_grads/pallas_call | solution.py:51
  41.0 1.3 %collective-permute-start.18 = (bf16[2,2,128,256]{3,2,1,0:T(8,128)(2,1)S(1)}, bf16[2,2,128,256]{3,2,1,0:T(8,128)(2,1)S(1)}, u32[]{:S(2)}, u32[]{:S(2)}) collective-permute-start(bf16[2,2,128,256]{3,2,1,0:T(8,128)(2,1)S(1)} %get-tuple-element.55), channel_id=1, source_target_pairs={{4,0},{8,4},{12,8},{5,1},{9,5},{13,9},{6,2},{10,6},{14,10},{7,3},{... | collective-permute-start | bytes 786440 | tf_op jit(solution)/shard_map/ppermute | solution.py:27
  42.3 1.0 %collective-permute-start.7 = (bf16[2,128,256]{2,1,0:T(8,128)(2,1)S(1)}, bf16[2,128,256]{2,1,0:T(8,128)(2,1)S(1)}, u32[]{:S(2)}, u32[]{:S(2)}) collective-permute-start(bf16[2,128,256]{2,1,0:T(8,128)(2,1)S(1)} %get-tuple-element.41), channel_id=1, source_target_pairs={{0,2},{2,0},{1,3},{3,1},{4,6},{6,4},{5,7},{7,5},{8,10},{10,8},{9,1... | collective-permute-start | bytes 393224 | tf_op jit(solution)/shard_map/ppermute | solution.py:32
  43.3 1.1 %collective-permute-start.16 = (bf16[2,128,256]{2,1,0:T(8,128)(2,1)S(1)}, bf16[2,128,256]{2,1,0:T(8,128)(2,1)S(1)}, u32[]{:S(2)}, u32[]{:S(2)}) collective-permute-start(bf16[2,128,256]{2,1,0:T(8,128)(2,1)S(1)} %get-tuple-element.52), channel_id=1, source_target_pairs={{0,2},{2,0},{1,3},{3,1},{4,6},{6,4},{5,7},{7,5},{8,10},{10,8},{9,1... | collective-permute-start | bytes 393224 | tf_op jit(solution)/shard_map/ppermute | solution.py:32
  44.4 3.5 %collective-permute-done.7.refs_4_.refs_1_ = bf16[2,128,256]{2,1,0:T(8,128)(2,1)S(1)} collective-permute-done((bf16[2,128,256]{2,1,0:T(8,128)(2,1)S(1)}, bf16[2,128,256]{2,1,0:T(8,128)(2,1)S(1)}, u32[]{:S(2)}, u32[]{:S(2)}) %collective-permute-start.7) | collective-permute-done | bytes 131104 | tf_op jit(solution)/shard_map/ppermute | solution.py:32
  48.0 0.1 summed.3
  48.1 1.0 %collective-permute-start.10 = (bf16[2,2,128,256]{3,2,1,0:T(8,128)(2,1)S(1)}, bf16[2,2,128,256]{3,2,1,0:T(8,128)(2,1)S(1)}, u32[]{:S(2)}, u32[]{:S(2)}) collective-permute-start(bf16[2,2,128,256]{3,2,1,0:T(8,128)(2,1)S(1)} %get-tuple-element.47), channel_id=1, source_target_pairs={{0,2},{2,0},{1,3},{3,1},{4,6},{6,4},{5,7},{7,5},{8,10},{10,8},{9,1... | collective-permute-start | bytes 786440 | tf_op jit(solution)/shard_map/ppermute | solution.py:32
  49.0 1.7 %collective-permute-done.16.refs_0_.refs_2_.refs_1_ = bf16[2,128,256]{2,1,0:T(8,128)(2,1)S(1)} collective-permute-done((bf16[2,128,256]{2,1,0:T(8,128)(2,1)S(1)}, bf16[2,128,256]{2,1,0:T(8,128)(2,1)S(1)}, u32[]{:S(2)}, u32[]{:S(2)}) %collective-permute-start.16) | collective-permute-done | bytes 131104 | tf_op jit(solution)/shard_map/ppermute | solution.py:32
  50.8 1.3 %collective-permute-start.17 = (bf16[2,2,128,256]{3,2,1,0:T(8,128)(2,1)S(1)}, bf16[2,2,128,256]{3,2,1,0:T(8,128)(2,1)S(1)}, u32[]{:S(2)}, u32[]{:S(2)}) collective-permute-start(bf16[2,2,128,256]{3,2,1,0:T(8,128)(2,1)S(1)} %relayed.3), channel_id=1, source_target_pairs={{4,0},{8,4},{12,8},{5,1},{9,5},{13,9},{6,2},{10,6},{14,10},{7,3},{... | collective-permute-start | bytes 786440 | tf_op jit(solution)/shard_map/ppermute | solution.py:27
  52.2 1.0 %collective-permute-start.19 = (bf16[2,2,128,256]{3,2,1,0:T(8,128)(2,1)S(1)}, bf16[2,2,128,256]{3,2,1,0:T(8,128)(2,1)S(1)}, u32[]{:S(2)}, u32[]{:S(2)}) collective-permute-start(bf16[2,2,128,256]{3,2,1,0:T(8,128)(2,1)S(1)} %summed.5), channel_id=1, source_target_pairs={{0,2},{2,0},{1,3},{3,1},{4,6},{6,4},{5,7},{7,5},{8,10},{10,8},{9,1... | collective-permute-start | bytes 786440 | tf_op jit(solution)/shard_map/ppermute | solution.py:32
  53.1 4.0 %collective-permute-done.10.refs_3_ = bf16[2,2,128,256]{3,2,1,0:T(8,128)(2,1)S(1)} collective-permute-done((bf16[2,2,128,256]{3,2,1,0:T(8,128)(2,1)S(1)}, bf16[2,2,128,256]{3,2,1,0:T(8,128)(2,1)S(1)}, u32[]{:S(2)}, u32[]{:S(2)}) %collective-permute-start.10) | collective-permute-done | bytes 262176 | tf_op jit(solution)/shard_map/ppermute | solution.py:32
  57.3 3.1 %collective-permute-done.17.refs_1_ = bf16[2,2,128,256]{3,2,1,0:T(8,128)(2,1)S(1)} collective-permute-done((bf16[2,2,128,256]{3,2,1,0:T(8,128)(2,1)S(1)}, bf16[2,2,128,256]{3,2,1,0:T(8,128)(2,1)S(1)}, u32[]{:S(2)}, u32[]{:S(2)}) %collective-permute-start.17) | collective-permute-done | bytes 262176 | tf_op jit(solution)/shard_map/ppermute | solution.py:27
  60.6 1.7 %collective-permute-done.21.refs_3_ = bf16[3,2,128,256]{3,2,1,0:T(8,128)(2,1)S(1)} collective-permute-done((bf16[3,2,128,256]{3,2,1,0:T(8,128)(2,1)S(1)}, bf16[3,2,128,256]{3,2,1,0:T(8,128)(2,1)S(1)}, u32[]{:S(2)}, u32[]{:S(2)}) %collective-permute-start.21) | collective-permute-done | bytes 393248 | tf_op jit(solution)/shard_map/ppermute | solution.py:36
  62.3 1.3 %laid_out.1 = (bf16[128,2048]{1,0:T(8,128)(2,1)}, bf16[128,2048]{1,0:T(8,128)(2,1)}, bf16[128,2048]{1,0:T(8,128)(2,1)}) custom-call(bf16[3,2,128,256]{3,2,1,0:T(8,128)(2,1)S(1)} %get-tuple-element.48.refs_0_, bf16[3,2,128,256]{3,2,1,0:T(8,128)(2,1)S(1)} %get-tuple-element.56.refs_1_, bf16[3,2,128,256]{3,2,1,0:T(8,128)(2,1)S(1)} %collective-permute-done.20.refs_2_, ...), custom_call_target="tpu_custom_call" | custom-call | bytes 3145728 | tf_op jit(solution)/shard_map/laid_out/pallas_call | solution.py:51
  (30 shorter events, 0.6 us)
Async XLA Ops:
  1.8 5.4 %collective-permute-start = (bf16[2,128,256]{2,1,0:T(8,128)(2,1)S(1)}, bf16[2,128,256]{2,1,0:T(8,128)(2,1)S(1)}, u32[]{:S(2)}, u32[]{:S(2)}) collective-permute-start(bf16[2,128,256]{2,1,0:T(8,128)(2,1)S(1)} %get-tuple-element.32), channel_id=1, source_target_pairs={{0,1},{1,0},{2,3},{3,2},{4,5},{5,4},{6,7},{7,6},{8,9},{9,8},{10,11... | collective-permute-start | bytes 393224 | tf_op jit(solution)/shard_map/ppermute | solution.py:36
  2.3 9.5 %collective-permute-start.1 = (bf16[2,2,128,256]{3,2,1,0:T(8,128)(2,1)S(1)}, bf16[2,2,128,256]{3,2,1,0:T(8,128)(2,1)S(1)}, u32[]{:S(2)}, u32[]{:S(2)}) collective-permute-start(bf16[2,2,128,256]{3,2,1,0:T(8,128)(2,1)S(1)} %get-tuple-element.33), channel_id=1, source_target_pairs={{0,2},{2,0},{1,3},{3,1},{4,6},{6,4},{5,7},{7,5},{8,10},{10,8},{9,1... | collective-permute-start | bytes 786440 | tf_op jit(solution)/shard_map/ppermute | solution.py:32
  4.9 2.2 %copy-start = (s32[2048]{0:T(1024)S(1)}, s32[2048]{0:T(1024)}, u32[]{:S(2)}) copy-start(s32[2048]{0:T(1024)} %param.9) | copy-start | bytes 24580
  6.5 5.4 %collective-permute-start.5 = (bf16[2,2,128,256]{3,2,1,0:T(8,128)(2,1)S(1)}, bf16[2,2,128,256]{3,2,1,0:T(8,128)(2,1)S(1)}, u32[]{:S(2)}, u32[]{:S(2)}) collective-permute-start(bf16[2,2,128,256]{3,2,1,0:T(8,128)(2,1)S(1)} %get-tuple-element.35), channel_id=1, source_target_pairs={{0,1},{1,0},{2,3},{3,2},{4,5},{5,4},{6,7},{7,6},{8,9},{9,8},{10,11... | collective-permute-start | bytes 786440 | tf_op jit(solution)/shard_map/ppermute | solution.py:36
  6.7 11.0 %collective-permute-start.11 = (bf16[4,2,128,256]{3,2,1,0:T(8,128)(2,1)S(1)}, bf16[4,2,128,256]{3,2,1,0:T(8,128)(2,1)S(1)}, u32[]{:S(2)}, u32[]{:S(2)}) collective-permute-start(bf16[4,2,128,256]{3,2,1,0:T(8,128)(2,1)S(1)} %get-tuple-element.50), channel_id=1, source_target_pairs={{0,1},{1,0},{2,3},{3,2},{4,5},{5,4},{6,7},{7,6},{8,9},{9,8},{10,11... | collective-permute-start | bytes 1572872 | tf_op jit(solution)/shard_map/ppermute | solution.py:36
  7.4 10.3 %collective-permute-start.3 = (bf16[2,2,128,256]{3,2,1,0:T(8,128)(2,1)S(1)}, bf16[2,2,128,256]{3,2,1,0:T(8,128)(2,1)S(1)}, u32[]{:S(2)}, u32[]{:S(2)}) collective-permute-start(bf16[2,2,128,256]{3,2,1,0:T(8,128)(2,1)S(1)} %both_rows.2.refs_1_), channel_id=1, source_target_pairs={{0,4},{4,8},{8,12},{12,0},{1,5},{5,9},{9,13},{13,1},{2,6},{6,10},{... | collective-permute-start | bytes 786440 | tf_op jit(solution)/shard_map/ppermute | solution.py:27
  11.9 2.1 %collective-permute-start.2 = (bf16[1,2,128,256]{3,2,1,0:T(8,128)(2,1)S(1)}, bf16[1,2,128,256]{3,2,1,0:T(8,128)(2,1)S(1)}, u32[]{:S(2)}, u32[]{:S(2)}) collective-permute-start(bf16[1,2,128,256]{3,2,1,0:T(8,128)(2,1)S(1)} %other_side.1), channel_id=1, source_target_pairs={{0,1},{1,0},{2,3},{3,2},{4,5},{5,4},{6,7},{7,6},{8,9},{9,8},{10,11... | collective-permute-start | bytes 393224 | tf_op jit(solution)/shard_map/ppermute | solution.py:36
  12.2 9.2 %collective-permute-start.6 = (bf16[2,2,128,256]{3,2,1,0:T(8,128)(2,1)S(1)}, bf16[2,2,128,256]{3,2,1,0:T(8,128)(2,1)S(1)}, u32[]{:S(2)}, u32[]{:S(2)}) collective-permute-start(bf16[2,2,128,256]{3,2,1,0:T(8,128)(2,1)S(1)} %head_parts.7), channel_id=1, source_target_pairs={{0,2},{2,0},{1,3},{3,1},{4,6},{6,4},{5,7},{7,5},{8,10},{10,8},{9,1... | collective-permute-start | bytes 786440 | tf_op jit(solution)/shard_map/ppermute | solution.py:32
  14.2 11.0 %collective-permute-start.4 = (bf16[2,2,128,256]{3,2,1,0:T(8,128)(2,1)S(1)}, bf16[2,2,128,256]{3,2,1,0:T(8,128)(2,1)S(1)}, u32[]{:S(2)}, u32[]{:S(2)}) collective-permute-start(bf16[2,2,128,256]{3,2,1,0:T(8,128)(2,1)S(1)} %both_rows.3.refs_2_.refs_0_), channel_id=1, source_target_pairs={{0,4},{4,8},{8,12},{12,0},{1,5},{5,9},{9,13},{13,1},{2,6},{6,10},{... | collective-permute-start | bytes 786440 | tf_op jit(solution)/shard_map/ppermute | solution.py:27
  17.9 10.7 %collective-permute-start.12 = (bf16[2,2,128,256]{3,2,1,0:T(8,128)(2,1)S(1)}, bf16[2,2,128,256]{3,2,1,0:T(8,128)(2,1)S(1)}, u32[]{:S(2)}, u32[]{:S(2)}) collective-permute-start(bf16[2,2,128,256]{3,2,1,0:T(8,128)(2,1)S(1)} %head_parts.9), channel_id=1, source_target_pairs={{0,2},{2,0},{1,3},{3,1},{4,6},{6,4},{5,7},{7,5},{8,10},{10,8},{9,1... | collective-permute-start | bytes 786440 | tf_op jit(solution)/shard_map/ppermute | solution.py:32
  19.7 17.1 %collective-permute-start.13 = (bf16[2,2,128,256]{3,2,1,0:T(8,128)(2,1)S(1)}, bf16[2,2,128,256]{3,2,1,0:T(8,128)(2,1)S(1)}, u32[]{:S(2)}, u32[]{:S(2)}) collective-permute-start(bf16[2,2,128,256]{3,2,1,0:T(8,128)(2,1)S(1)} %head_parts.8.refs_1_), channel_id=1, source_target_pairs={{0,4},{4,8},{8,12},{12,0},{1,5},{5,9},{9,13},{13,1},{2,6},{6,10},{... | collective-permute-start | bytes 786440 | tf_op jit(solution)/shard_map/ppermute | solution.py:27
  21.5 15.3 %collective-permute-start.15 = (bf16[2,2,128,256]{3,2,1,0:T(8,128)(2,1)S(1)}, bf16[2,2,128,256]{3,2,1,0:T(8,128)(2,1)S(1)}, u32[]{:S(2)}, u32[]{:S(2)}) collective-permute-start(bf16[2,2,128,256]{3,2,1,0:T(8,128)(2,1)S(1)} %head_parts.11), channel_id=1, source_target_pairs={{0,2},{2,0},{1,3},{3,1},{4,6},{6,4},{5,7},{7,5},{8,10},{10,8},{9,1... | collective-permute-start | bytes 786440 | tf_op jit(solution)/shard_map/ppermute | solution.py:32
  27.3 9.6 %collective-permute-start.8 = (bf16[2,2,2,128,128]{4,3,2,1,0:T(8,128)(2,1)S(1)}, bf16[2,2,2,128,128]{4,3,2,1,0:T(8,128)(2,1)S(1)}, u32[]{:S(2)}, u32[]{:S(2)}) collective-permute-start(bf16[2,2,2,128,128]{4,3,2,1,0:T(8,128)(2,1)S(1)} %get-tuple-element.44), channel_id=1, source_target_pairs={{4,0},{8,4},{12,8},{5,1},{9,5},{13,9},{6,2},{10,6},{14,10},{7,3},{... | collective-permute-start | bytes 786440 | tf_op jit(solution)/shard_map/ppermute | solution.py:27
  28.6 8.8 %collective-permute-start.14 = (bf16[2,2,128,256]{3,2,1,0:T(8,128)(2,1)S(1)}, bf16[2,2,128,256]{3,2,1,0:T(8,128)(2,1)S(1)}, u32[]{:S(2)}, u32[]{:S(2)}) collective-permute-start(bf16[2,2,128,256]{3,2,1,0:T(8,128)(2,1)S(1)} %relayed.2), channel_id=1, source_target_pairs={{0,4},{4,8},{8,12},{1,5},{5,9},{9,13},{2,6},{6,10},{10,14},{3,7},{... | collective-permute-start | bytes 786440 | tf_op jit(solution)/shard_map/ppermute | solution.py:27
  35.5 12.4 %collective-permute-start.9 = (bf16[2,2,2,128,128]{4,3,2,1,0:T(8,128)(2,1)S(1)}, bf16[2,2,2,128,128]{4,3,2,1,0:T(8,128)(2,1)S(1)}, u32[]{:S(2)}, u32[]{:S(2)}) collective-permute-start(bf16[2,2,2,128,128]{4,3,2,1,0:T(8,128)(2,1)S(1)} %get-tuple-element.45), channel_id=1, source_target_pairs={{4,0},{8,4},{12,8},{5,1},{9,5},{13,9},{6,2},{10,6},{14,10},{7,3},{... | collective-permute-start | bytes 786440 | tf_op jit(solution)/shard_map/ppermute | solution.py:27
  41.0 11.1 %collective-permute-start.18 = (bf16[2,2,128,256]{3,2,1,0:T(8,128)(2,1)S(1)}, bf16[2,2,128,256]{3,2,1,0:T(8,128)(2,1)S(1)}, u32[]{:S(2)}, u32[]{:S(2)}) collective-permute-start(bf16[2,2,128,256]{3,2,1,0:T(8,128)(2,1)S(1)} %get-tuple-element.55), channel_id=1, source_target_pairs={{4,0},{8,4},{12,8},{5,1},{9,5},{13,9},{6,2},{10,6},{14,10},{7,3},{... | collective-permute-start | bytes 786440 | tf_op jit(solution)/shard_map/ppermute | solution.py:27
  42.3 5.6 %collective-permute-start.7 = (bf16[2,128,256]{2,1,0:T(8,128)(2,1)S(1)}, bf16[2,128,256]{2,1,0:T(8,128)(2,1)S(1)}, u32[]{:S(2)}, u32[]{:S(2)}) collective-permute-start(bf16[2,128,256]{2,1,0:T(8,128)(2,1)S(1)} %get-tuple-element.41), channel_id=1, source_target_pairs={{0,2},{2,0},{1,3},{3,1},{4,6},{6,4},{5,7},{7,5},{8,10},{10,8},{9,1... | collective-permute-start | bytes 393224 | tf_op jit(solution)/shard_map/ppermute | solution.py:32
  43.3 7.5 %collective-permute-start.16 = (bf16[2,128,256]{2,1,0:T(8,128)(2,1)S(1)}, bf16[2,128,256]{2,1,0:T(8,128)(2,1)S(1)}, u32[]{:S(2)}, u32[]{:S(2)}) collective-permute-start(bf16[2,128,256]{2,1,0:T(8,128)(2,1)S(1)} %get-tuple-element.52), channel_id=1, source_target_pairs={{0,2},{2,0},{1,3},{3,1},{4,6},{6,4},{5,7},{7,5},{8,10},{10,8},{9,1... | collective-permute-start | bytes 393224 | tf_op jit(solution)/shard_map/ppermute | solution.py:32
  48.1 9.1 %collective-permute-start.10 = (bf16[2,2,128,256]{3,2,1,0:T(8,128)(2,1)S(1)}, bf16[2,2,128,256]{3,2,1,0:T(8,128)(2,1)S(1)}, u32[]{:S(2)}, u32[]{:S(2)}) collective-permute-start(bf16[2,2,128,256]{3,2,1,0:T(8,128)(2,1)S(1)} %get-tuple-element.47), channel_id=1, source_target_pairs={{0,2},{2,0},{1,3},{3,1},{4,6},{6,4},{5,7},{7,5},{8,10},{10,8},{9,1... | collective-permute-start | bytes 786440 | tf_op jit(solution)/shard_map/ppermute | solution.py:32
  50.8 9.6 %collective-permute-start.17 = (bf16[2,2,128,256]{3,2,1,0:T(8,128)(2,1)S(1)}, bf16[2,2,128,256]{3,2,1,0:T(8,128)(2,1)S(1)}, u32[]{:S(2)}, u32[]{:S(2)}) collective-permute-start(bf16[2,2,128,256]{3,2,1,0:T(8,128)(2,1)S(1)} %relayed.3), channel_id=1, source_target_pairs={{4,0},{8,4},{12,8},{5,1},{9,5},{13,9},{6,2},{10,6},{14,10},{7,3},{... | collective-permute-start | bytes 786440 | tf_op jit(solution)/shard_map/ppermute | solution.py:27
  52.2 8.3 %collective-permute-start.19 = (bf16[2,2,128,256]{3,2,1,0:T(8,128)(2,1)S(1)}, bf16[2,2,128,256]{3,2,1,0:T(8,128)(2,1)S(1)}, u32[]{:S(2)}, u32[]{:S(2)}) collective-permute-start(bf16[2,2,128,256]{3,2,1,0:T(8,128)(2,1)S(1)} %summed.5), channel_id=1, source_target_pairs={{0,2},{2,0},{1,3},{3,1},{4,6},{6,4},{5,7},{7,5},{8,10},{10,8},{9,1... | collective-permute-start | bytes 786440 | tf_op jit(solution)/shard_map/ppermute | solution.py:32
  57.2 3.4 %collective-permute-start.20 = (bf16[3,2,128,256]{3,2,1,0:T(8,128)(2,1)S(1)}, bf16[3,2,128,256]{3,2,1,0:T(8,128)(2,1)S(1)}, u32[]{:S(2)}, u32[]{:S(2)}) collective-permute-start(bf16[3,2,128,256]{3,2,1,0:T(8,128)(2,1)S(1)} %get-tuple-element.57), channel_id=1, source_target_pairs={{0,1},{1,0},{2,3},{3,2},{4,5},{5,4},{6,7},{7,6},{8,9},{9,8},{10,11... | collective-permute-start | bytes 1179656 | tf_op jit(solution)/shard_map/ppermute | solution.py:36
  60.5 1.8 %collective-permute-start.21 = (bf16[3,2,128,256]{3,2,1,0:T(8,128)(2,1)S(1)}, bf16[3,2,128,256]{3,2,1,0:T(8,128)(2,1)S(1)}, u32[]{:S(2)}, u32[]{:S(2)}) collective-permute-start(bf16[3,2,128,256]{3,2,1,0:T(8,128)(2,1)S(1)} %get-tuple-element.58), channel_id=1, source_target_pairs={{0,1},{1,0},{2,3},{3,2},{4,5},{5,4},{6,7},{7,6},{8,9},{9,8},{10,11... | collective-permute-start | bytes 1179656 | tf_op jit(solution)/shard_map/ppermute | solution.py:36

commit v15 on v14

--- a/solution.py
+++ b/solution.py
@@ -444,9 +444,9 @@
                 turn = groups[-1][1][:1]
                 first_dq = first_dq or turn
             later = [along_blocks(early[0], -1, False) for _, _, early in groups]
-            back = later[:1]
             dq = side_by_side([dq for _, dq, _ in groups]) if heads > 1 else groups[0][1]
             dq = [dq[0]] + [round_sub(dq[by], by) for by in others]
+            back = later[:1] + dq[1:]
             dkv = summed([grads for grads, _, _ in groups], later, [0] + others, dq[1:])
             dkv = [dkv[0]] + [round_sub(dkv[by], by) for by in others]
         send, keep = rows_for_pair(dq, dkv)

time: 64.6 us -> 63 us (0.975)
  waiting for transfers between devices: 22.5 us -> 21.4 us
    ppermute x8, waiting for transfers between devices: 13.4 us -> 11.7 us  [round_sub(): lax.ppermute(value, 'sub', [(i, (i + by) % peers) for i in range(peers)])]
    ppermute x8, waiting for transfers between devices: 7.34 us -> 7.99 us  [along_blocks(): return lax.ppermute(value, 'blk', pairs)]
  transfers between devices with their start and end apart: 22 -> 22, of which waited for: 10 -> 11; matrix products, arithmetic and copies ran while one was open for 1% -> 1% of each run, Pallas kernels for 18% -> 18%
where the time goes in v15:
time: 63 us; the launch traced here: 62.7 us
  starting transfers between devices  25.5 us (40%)
  waiting for transfers between devices  21.4 us (34%)
  Pallas kernels  13.9 us (22%)
  between operations  0.93 us (1%)
  other arithmetic  0.79 us (1%)
    ppermute x8, starting transfers between devices, along_blocks(): return lax.ppermute(value, 'blk', pairs)  13.2 us
    ppermute x8, waiting for transfers between devices, round_sub(): lax.ppermute(value, 'sub', [(i, (i + by) % peers) for i in range(peers)])  11.7 us
    pallas_call x21, Pallas kernels, call(): pl.pallas_call(kernel, out_shape=outs, in_specs=[spec] * len(ins), out_sp...  11.1 us
    ppermute x8, starting transfers between devices, round_sub(): lax.ppermute(value, 'sub', [(i, (i + by) % peers) for i in range(peers)])  11 us
    ppermute x8, waiting for transfers between devices, along_blocks(): return lax.ppermute(value, 'blk', pairs)  7.99 us
    ppermute x6, waiting for transfers between devices, swapped(): return lax.ppermute(value, 'pair', [(0, 1), (1, 0)])  1.71 us
    pallas_call x1, Pallas kernels, first_parts(): pl.pallas_call(kernel, out_shape=outs, in_specs=[spec] * (len(held) + len...  1.64 us
    ppermute x6, starting transfers between devices, swapped(): return lax.ppermute(value, 'pair', [(0, 1), (1, 0)])  1.31 us
  transfers between devices with their start and end apart: 22, of which 11 were waited for; matrix products, arithmetic and copies ran while one was open for 1% of the time, Pallas kernels for 18%

profile of v15, /device:TPU:0, one launch (start us, length us, event | category | flops | bytes accessed | tf_op | source)
XLA Modules:
  0.0 62.7 jit_solution(17938909236451514519)
XLA Ops:
  0.6 1.2 %first_keys.1 = (bf16[2,2,128,256]{3,2,1,0:T(8,128)(2,1)S(1)}, bf16[2,128,256]{2,1,0:T(8,128)(2,1)S(1)}, bf16[2,128,256]{2,1,0:T(8,128)(2,1)S(1)}) custom-call(bf16[128,2048]{1,0:T(8,128)(2,1)} %refs_2_.1, bf16[128,2048]{1,0:T(8,128)(2,1)} %refs_3_.1), custom_call_target="tpu_custom_call" | custom-call | tf_op jit(solution)/shard_map/first_keys/pallas_call | solution.py:127
  1.8 0.5 collective-permute-start
  2.3 2.6 %collective-permute-start.1 = (bf16[2,2,128,256]{3,2,1,0:T(8,128)(2,1)S(1)}, bf16[2,2,128,256]{3,2,1,0:T(8,128)(2,1)S(1)}, u32[]{:S(2)}, u32[]{:S(2)}) collective-permute-start(bf16[2,2,128,256]{3,2,1,0:T(8,128)(2,1)S(1)} %get-tuple-element.33), channel_id=1, source_target_pairs={{0,2},{2,0},{1,3},{3,1},{4,6},{6,4},{5,7},{7,5},{8,10},{10,8},{9,1... | collective-permute-start | bytes 786440 | tf_op jit(solution)/shard_map/ppermute | solution.py:32
  4.9 1.6 %first_parts.1 = (bf16[2,2,128,256]{3,2,1,0:T(8,128)(2,1)S(1)}, bf16[2,2,128,256]{3,2,1,0:T(8,128)(2,1)S(1)}, bf16[4,2,128,256]{3,2,1,0:T(8,128)(2,1)S(1)}, bf16[4,2,128,256]{3,2,1,0:T(8,128)(2,1)S(1)}) custom-call(bf16[128,2048]{1,0:T(8,128)(2,1)} %refs_4_.1, bf16[128,2048]{1,0:T(8,128)(2,1)} %refs_5_.1, bf16[128,2048]{1,0:T(8,128)(2,1)} %refs_2_.1, ...), custom_call_target="tpu_custom_call" | custom-call | tf_op jit(solution)/shard_map/first_parts/pallas_call | solution.py:92
  6.5 0.2 collective-permute-start.5
  6.7 0.3 collective-permute-start.11
  7.1 0.1 pad_dynamic-slice_fusion
  7.2 0.2 both_rows.2.refs_1_
  7.4 1.6 %collective-permute-start.3 = (bf16[2,2,128,256]{3,2,1,0:T(8,128)(2,1)S(1)}, bf16[2,2,128,256]{3,2,1,0:T(8,128)(2,1)S(1)}, u32[]{:S(2)}, u32[]{:S(2)}) collective-permute-start(bf16[2,2,128,256]{3,2,1,0:T(8,128)(2,1)S(1)} %both_rows.2.refs_1_), channel_id=1, source_target_pairs={{0,4},{4,8},{8,12},{12,0},{1,5},{5,9},{9,13},{13,1},{2,6},{6,10},{... | collective-permute-start | bytes 786440 | tf_op jit(solution)/shard_map/ppermute | solution.py:27
  9.0 2.7 %collective-permute-done.1.refs_0_ = bf16[2,2,128,256]{3,2,1,0:T(8,128)(2,1)S(1)} collective-permute-done((bf16[2,2,128,256]{3,2,1,0:T(8,128)(2,1)S(1)}, bf16[2,2,128,256]{3,2,1,0:T(8,128)(2,1)S(1)}, u32[]{:S(2)}, u32[]{:S(2)}) %collective-permute-start.1) | collective-permute-done | bytes 262176 | tf_op jit(solution)/shard_map/ppermute | solution.py:32
  12.0 0.2 head_parts.7
  12.2 1.8 %collective-permute-start.6 = (bf16[2,2,128,256]{3,2,1,0:T(8,128)(2,1)S(1)}, bf16[2,2,128,256]{3,2,1,0:T(8,128)(2,1)S(1)}, u32[]{:S(2)}, u32[]{:S(2)}) collective-permute-start(bf16[2,2,128,256]{3,2,1,0:T(8,128)(2,1)S(1)} %head_parts.7), channel_id=1, source_target_pairs={{0,2},{2,0},{1,3},{3,1},{4,6},{6,4},{5,7},{7,5},{8,10},{10,8},{9,1... | collective-permute-start | bytes 786440 | tf_op jit(solution)/shard_map/ppermute | solution.py:32
  14.0 0.2 both_rows.3.refs_2_.refs_0_
  14.2 1.6 %collective-permute-start.4 = (bf16[2,2,128,256]{3,2,1,0:T(8,128)(2,1)S(1)}, bf16[2,2,128,256]{3,2,1,0:T(8,128)(2,1)S(1)}, u32[]{:S(2)}, u32[]{:S(2)}) collective-permute-start(bf16[2,2,128,256]{3,2,1,0:T(8,128)(2,1)S(1)} %both_rows.3.refs_2_.refs_0_), channel_id=1, source_target_pairs={{0,4},{4,8},{8,12},{12,0},{1,5},{5,9},{9,13},{13,1},{2,6},{6,10},{... | collective-permute-start | bytes 786440 | tf_op jit(solution)/shard_map/ppermute | solution.py:27
  15.8 1.9 %collective-permute-done.3.refs_3_.refs_0_.refs_1_ = bf16[2,2,128,256]{3,2,1,0:T(8,128)(2,1)S(1)} collective-permute-done((bf16[2,2,128,256]{3,2,1,0:T(8,128)(2,1)S(1)}, bf16[2,2,128,256]{3,2,1,0:T(8,128)(2,1)S(1)}, u32[]{:S(2)}, u32[]{:S(2)}) %collective-permute-start.3) | collective-permute-done | bytes 262176 | tf_op jit(solution)/shard_map/ppermute | solution.py:27
  17.7 0.2 head_parts.9
  17.9 0.6 collective-permute-start.12
  18.5 0.7 %and_select_fusion = (f32[1,768,256]{2,1,0:T(8,128)S(1)}, f32[1,768,256]{2,1,0:T(8,128)S(1)}) fusion(s32[256]{0:T(256)S(1)} %get-tuple-element.68, s32[256]{0:T(256)S(1)} %get-tuple-element.66, s32[768]{0:T(1024)S(1)} %get-tuple-element.64, s32[768]{0:T(1024)S(1)} %get-tuple-element.62, pred[768]{0:T(1024)(128)(4,1)S(1)} %get-tuple-element.60, ...), kind=kLoop, calls=%fused_computation.1 | loop fusion | flops 1966080 | bytes 1590784 | tf_op jit(solution)/shard_map/jit(_where)/select_n | solution.py:386
  19.2 0.1 pad_maximum_fusion.refs_0_
  19.3 0.2 head_parts.6.refs_5_
  19.5 0.2 head_parts.8.refs_1_
  19.7 0.2 collective-permute-start.13
  19.9 1.4 %collective-permute-done.6.refs_6_.refs_0_ = bf16[2,2,128,256]{3,2,1,0:T(8,128)(2,1)S(1)} collective-permute-done((bf16[2,2,128,256]{3,2,1,0:T(8,128)(2,1)S(1)}, bf16[2,2,128,256]{3,2,1,0:T(8,128)(2,1)S(1)}, u32[]{:S(2)}, u32[]{:S(2)}) %collective-permute-start.6) | collective-permute-done | bytes 262176 | tf_op jit(solution)/shard_map/ppermute | solution.py:32
  21.3 0.2 head_parts.11
  21.5 1.8 %collective-permute-start.15 = (bf16[2,2,128,256]{3,2,1,0:T(8,128)(2,1)S(1)}, bf16[2,2,128,256]{3,2,1,0:T(8,128)(2,1)S(1)}, u32[]{:S(2)}, u32[]{:S(2)}) collective-permute-start(bf16[2,2,128,256]{3,2,1,0:T(8,128)(2,1)S(1)} %head_parts.11), channel_id=1, source_target_pairs={{0,2},{2,0},{1,3},{3,1},{4,6},{6,4},{5,7},{7,5},{8,10},{10,8},{9,1... | collective-permute-start | bytes 786440 | tf_op jit(solution)/shard_map/ppermute | solution.py:32
  23.3 1.8 %collective-permute-done.4.refs_4_ = bf16[2,2,128,256]{3,2,1,0:T(8,128)(2,1)S(1)} collective-permute-done((bf16[2,2,128,256]{3,2,1,0:T(8,128)(2,1)S(1)}, bf16[2,2,128,256]{3,2,1,0:T(8,128)(2,1)S(1)}, u32[]{:S(2)}, u32[]{:S(2)}) %collective-permute-start.4) | collective-permute-done | bytes 262176 | tf_op jit(solution)/shard_map/ppermute | solution.py:27
  25.2 2.1 %attention_grads.3 = (f32[2,2,2,128,128]{4,3,2,1,0:T(8,128)S(1)}, bf16[2,128,128]{2,1,0:T(8,128)(2,1)S(1)}, bf16[2,128,128]{2,1,0:T(8,128)(2,1)S(1)}, bf16[2,2,2,128,128]{4,3,2,1,0:T(8,128)(2,1)S(1)}) custom-call(f32[2,768,256]{2,1,0:T(8,128)S(1)} %pad_maximum_fusion.refs_0_, bf16[2,2,128,256]{3,2,1,0:T(8,128)(2,1)S(1)} %both_rows.2.refs_1_, ...), custom_call_target="tpu_custom_call" | custom-call | flops 503316480 | bytes 4063232 | tf_op jit(solution)/shard_map/attention_grads/pallas_call | solution.py:51
  27.3 1.3 %collective-permute-start.8 = (bf16[2,2,2,128,128]{4,3,2,1,0:T(8,128)(2,1)S(1)}, bf16[2,2,2,128,128]{4,3,2,1,0:T(8,128)(2,1)S(1)}, u32[]{:S(2)}, u32[]{:S(2)}) collective-permute-start(bf16[2,2,2,128,128]{4,3,2,1,0:T(8,128)(2,1)S(1)} %get-tuple-element.44), channel_id=1, source_target_pairs={{4,0},{8,4},{12,8},{5,1},{9,5},{13,9},{6,2},{10,6},{14,10},{7,3},{... | collective-permute-start | bytes 786440 | tf_op jit(solution)/shard_map/ppermute | solution.py:27
  28.6 4.6 %collective-permute-start.14 = (bf16[2,2,128,256]{3,2,1,0:T(8,128)(2,1)S(1)}, bf16[2,2,128,256]{3,2,1,0:T(8,128)(2,1)S(1)}, u32[]{:S(2)}, u32[]{:S(2)}) collective-permute-start(bf16[2,2,128,256]{3,2,1,0:T(8,128)(2,1)S(1)} %relayed.2), channel_id=1, source_target_pairs={{0,4},{4,8},{8,12},{1,5},{5,9},{9,13},{2,6},{6,10},{10,14},{3,7},{... | collective-permute-start | bytes 786440 | tf_op jit(solution)/shard_map/ppermute | solution.py:27
  33.2 2.1 %attention_grads.4 = (f32[2,2,2,128,128]{4,3,2,1,0:T(8,128)S(1)}, bf16[2,128,128]{2,1,0:T(8,128)(2,1)S(1)}, bf16[2,128,128]{2,1,0:T(8,128)(2,1)S(1)}, bf16[2,2,2,128,128]{4,3,2,1,0:T(8,128)(2,1)S(1)}) custom-call(f32[2,768,256]{2,1,0:T(8,128)S(1)} %pad_maximum_fusion.refs_0_, bf16[2,2,128,256]{3,2,1,0:T(8,128)(2,1)S(1)} %both_rows.2.refs_1_, ...), custom_call_target="tpu_custom_call" | custom-call | flops 503316480 | bytes 4128768 | tf_op jit(solution)/shard_map/attention_grads/pallas_call | solution.py:51
  35.4 1.0 %collective-permute-start.7 = (bf16[2,128,256]{2,1,0:T(8,128)(2,1)S(1)}, bf16[2,128,256]{2,1,0:T(8,128)(2,1)S(1)}, u32[]{:S(2)}, u32[]{:S(2)}) collective-permute-start(bf16[2,128,256]{2,1,0:T(8,128)(2,1)S(1)} %get-tuple-element.41), channel_id=1, source_target_pairs={{0,2},{2,0},{1,3},{3,1},{4,6},{6,4},{5,7},{7,5},{8,10},{10,8},{9,1... | collective-permute-start | bytes 393224 | tf_op jit(solution)/shard_map/ppermute | solution.py:32
  36.4 0.2 head_parts.10.refs_5_
  36.6 1.3 %collective-permute-start.9 = (bf16[2,2,2,128,128]{4,3,2,1,0:T(8,128)(2,1)S(1)}, bf16[2,2,2,128,128]{4,3,2,1,0:T(8,128)(2,1)S(1)}, u32[]{:S(2)}, u32[]{:S(2)}) collective-permute-start(bf16[2,2,2,128,128]{4,3,2,1,0:T(8,128)(2,1)S(1)} %get-tuple-element.45), channel_id=1, source_target_pairs={{4,0},{8,4},{12,8},{5,1},{9,5},{13,9},{6,2},{10,6},{14,10},{7,3},{... | collective-permute-start | bytes 786440 | tf_op jit(solution)/shard_map/ppermute | solution.py:27
  37.9 2.5 %collective-permute-done.7.refs_4_.refs_1_.refs_8_ = bf16[2,128,256]{2,1,0:T(8,128)(2,1)S(1)} collective-permute-done((bf16[2,128,256]{2,1,0:T(8,128)(2,1)S(1)}, bf16[2,128,256]{2,1,0:T(8,128)(2,1)S(1)}, u32[]{:S(2)}, u32[]{:S(2)}) %collective-permute-start.7) | collective-permute-done | bytes 131104 | tf_op jit(solution)/shard_map/ppermute | solution.py:32
  40.4 3.5 %attention_grads.5 = (f32[2,2,2,128,256]{4,3,2,1,0:T(8,128)S(1)}, bf16[2,128,256]{2,1,0:T(8,128)(2,1)S(1)}, bf16[2,128,256]{2,1,0:T(8,128)(2,1)S(1)}, bf16[2,2,1...) custom-call(f32[2,768,256]{2,1,0:T(8,128)S(1)} %pad_maximum_fusion.refs_0_, ...), custom_call_target="tpu_custom_call" | custom-call | flops 1006632960 | bytes 5373952 | tf_op jit(solution)/shard_map/attention_grads/pallas_call | solution.py:51
  44.0 1.3 %collective-permute-start.18 = (bf16[2,2,128,256]{3,2,1,0:T(8,128)(2,1)S(1)}, bf16[2,2,128,256]{3,2,1,0:T(8,128)(2,1)S(1)}, u32[]{:S(2)}, u32[]{:S(2)}) collective-permute-start(bf16[2,2,128,256]{3,2,1,0:T(8,128)(2,1)S(1)} %get-tuple-element.55), channel_id=1, source_target_pairs={{4,0},{8,4},{12,8},{5,1},{9,5},{13,9},{6,2},{10,6},{14,10},{7,3},{... | collective-permute-start | bytes 786440 | tf_op jit(solution)/shard_map/ppermute | solution.py:27
  45.3 1.0 %collective-permute-start.16 = (bf16[2,128,256]{2,1,0:T(8,128)(2,1)S(1)}, bf16[2,128,256]{2,1,0:T(8,128)(2,1)S(1)}, u32[]{:S(2)}, u32[]{:S(2)}) collective-permute-start(bf16[2,128,256]{2,1,0:T(8,128)(2,1)S(1)} %get-tuple-element.52), channel_id=1, source_target_pairs={{0,2},{2,0},{1,3},{3,1},{4,6},{6,4},{5,7},{7,5},{8,10},{10,8},{9,1... | collective-permute-start | bytes 393224 | tf_op jit(solution)/shard_map/ppermute | solution.py:32
  46.3 0.1 summed.3
  46.4 1.2 %collective-permute-start.10 = (bf16[2,2,128,256]{3,2,1,0:T(8,128)(2,1)S(1)}, bf16[2,2,128,256]{3,2,1,0:T(8,128)(2,1)S(1)}, u32[]{:S(2)}, u32[]{:S(2)}) collective-permute-start(bf16[2,2,128,256]{3,2,1,0:T(8,128)(2,1)S(1)} %get-tuple-element.47), channel_id=1, source_target_pairs={{0,2},{2,0},{1,3},{3,1},{4,6},{6,4},{5,7},{7,5},{8,10},{10,8},{9,1... | collective-permute-start | bytes 786440 | tf_op jit(solution)/shard_map/ppermute | solution.py:32
  47.5 3.1 %collective-permute-done.16.refs_0_.refs_2_.refs_1_ = bf16[2,128,256]{2,1,0:T(8,128)(2,1)S(1)} collective-permute-done((bf16[2,128,256]{2,1,0:T(8,128)(2,1)S(1)}, bf16[2,128,256]{2,1,0:T(8,128)(2,1)S(1)}, u32[]{:S(2)}, u32[]{:S(2)}) %collective-permute-start.16) | collective-permute-done | bytes 131104 | tf_op jit(solution)/shard_map/ppermute | solution.py:32
  50.7 1.3 %collective-permute-start.17 = (bf16[2,2,128,256]{3,2,1,0:T(8,128)(2,1)S(1)}, bf16[2,2,128,256]{3,2,1,0:T(8,128)(2,1)S(1)}, u32[]{:S(2)}, u32[]{:S(2)}) collective-permute-start(bf16[2,2,128,256]{3,2,1,0:T(8,128)(2,1)S(1)} %relayed.3), channel_id=1, source_target_pairs={{4,0},{8,4},{12,8},{5,1},{9,5},{13,9},{6,2},{10,6},{14,10},{7,3},{... | collective-permute-start | bytes 786440 | tf_op jit(solution)/shard_map/ppermute | solution.py:27
  52.0 1.0 %collective-permute-done.18.refs_1_ = bf16[2,2,128,256]{3,2,1,0:T(8,128)(2,1)S(1)} collective-permute-done((bf16[2,2,128,256]{3,2,1,0:T(8,128)(2,1)S(1)}, bf16[2,2,128,256]{3,2,1,0:T(8,128)(2,1)S(1)}, u32[]{:S(2)}, u32[]{:S(2)}) %collective-permute-start.18) | collective-permute-done | bytes 262176 | tf_op jit(solution)/shard_map/ppermute | solution.py:27
  53.1 1.0 %collective-permute-start.19 = (bf16[2,2,128,256]{3,2,1,0:T(8,128)(2,1)S(1)}, bf16[2,2,128,256]{3,2,1,0:T(8,128)(2,1)S(1)}, u32[]{:S(2)}, u32[]{:S(2)}) collective-permute-start(bf16[2,2,128,256]{3,2,1,0:T(8,128)(2,1)S(1)} %summed.5), channel_id=1, source_target_pairs={{0,2},{2,0},{1,3},{3,1},{4,6},{6,4},{5,7},{7,5},{8,10},{10,8},{9,1... | collective-permute-start | bytes 786440 | tf_op jit(solution)/shard_map/ppermute | solution.py:32
  54.1 1.8 %collective-permute-done.10.refs_3_ = bf16[2,2,128,256]{3,2,1,0:T(8,128)(2,1)S(1)} collective-permute-done((bf16[2,2,128,256]{3,2,1,0:T(8,128)(2,1)S(1)}, bf16[2,2,128,256]{3,2,1,0:T(8,128)(2,1)S(1)}, u32[]{:S(2)}, u32[]{:S(2)}) %collective-permute-start.10) | collective-permute-done | bytes 262176 | tf_op jit(solution)/shard_map/ppermute | solution.py:32
  56.1 3.2 %collective-permute-done.17.refs_1_ = bf16[2,2,128,256]{3,2,1,0:T(8,128)(2,1)S(1)} collective-permute-done((bf16[2,2,128,256]{3,2,1,0:T(8,128)(2,1)S(1)}, bf16[2,2,128,256]{3,2,1,0:T(8,128)(2,1)S(1)}, u32[]{:S(2)}, u32[]{:S(2)}) %collective-permute-start.17) | collective-permute-done | bytes 262176 | tf_op jit(solution)/shard_map/ppermute | solution.py:27
  59.3 0.2 collective-permute-done.19.refs_3_
  59.7 1.7 %collective-permute-done.21.refs_3_ = bf16[3,2,128,256]{3,2,1,0:T(8,128)(2,1)S(1)} collective-permute-done((bf16[3,2,128,256]{3,2,1,0:T(8,128)(2,1)S(1)}, bf16[3,2,128,256]{3,2,1,0:T(8,128)(2,1)S(1)}, u32[]{:S(2)}, u32[]{:S(2)}) %collective-permute-start.21) | collective-permute-done | bytes 393248 | tf_op jit(solution)/shard_map/ppermute | solution.py:36
  61.4 1.3 %laid_out.1 = (bf16[128,2048]{1,0:T(8,128)(2,1)}, bf16[128,2048]{1,0:T(8,128)(2,1)}, bf16[128,2048]{1,0:T(8,128)(2,1)}) custom-call(bf16[3,2,128,256]{3,2,1,0:T(8,128)(2,1)S(1)} %get-tuple-element.48.refs_0_, bf16[3,2,128,256]{3,2,1,0:T(8,128)(2,1)S(1)} %get-tuple-element.56.refs_1_, bf16[3,2,128,256]{3,2,1,0:T(8,128)(2,1)S(1)} %collective-permute-done.20.refs_2_, ...), custom_call_target="tpu_custom_call" | custom-call | bytes 3145728 | tf_op jit(solution)/shard_map/laid_out/pallas_call | solution.py:51
  (30 shorter events, 0.7 us)
Async XLA Ops:
  1.8 5.4 %collective-permute-start = (bf16[2,128,256]{2,1,0:T(8,128)(2,1)S(1)}, bf16[2,128,256]{2,1,0:T(8,128)(2,1)S(1)}, u32[]{:S(2)}, u32[]{:S(2)}) collective-permute-start(bf16[2,128,256]{2,1,0:T(8,128)(2,1)S(1)} %get-tuple-element.32), channel_id=1, source_target_pairs={{0,1},{1,0},{2,3},{3,2},{4,5},{5,4},{6,7},{7,6},{8,9},{9,8},{10,11... | collective-permute-start | bytes 393224 | tf_op jit(solution)/shard_map/ppermute | solution.py:36
  2.3 9.5 %collective-permute-start.1 = (bf16[2,2,128,256]{3,2,1,0:T(8,128)(2,1)S(1)}, bf16[2,2,128,256]{3,2,1,0:T(8,128)(2,1)S(1)}, u32[]{:S(2)}, u32[]{:S(2)}) collective-permute-start(bf16[2,2,128,256]{3,2,1,0:T(8,128)(2,1)S(1)} %get-tuple-element.33), channel_id=1, source_target_pairs={{0,2},{2,0},{1,3},{3,1},{4,6},{6,4},{5,7},{7,5},{8,10},{10,8},{9,1... | collective-permute-start | bytes 786440 | tf_op jit(solution)/shard_map/ppermute | solution.py:32
  4.9 2.2 %copy-start = (s32[2048]{0:T(1024)S(1)}, s32[2048]{0:T(1024)}, u32[]{:S(2)}) copy-start(s32[2048]{0:T(1024)} %param.9) | copy-start | bytes 24580
  6.5 5.4 %collective-permute-start.5 = (bf16[2,2,128,256]{3,2,1,0:T(8,128)(2,1)S(1)}, bf16[2,2,128,256]{3,2,1,0:T(8,128)(2,1)S(1)}, u32[]{:S(2)}, u32[]{:S(2)}) collective-permute-start(bf16[2,2,128,256]{3,2,1,0:T(8,128)(2,1)S(1)} %get-tuple-element.35), channel_id=1, source_target_pairs={{0,1},{1,0},{2,3},{3,2},{4,5},{5,4},{6,7},{7,6},{8,9},{9,8},{10,11... | collective-permute-start | bytes 786440 | tf_op jit(solution)/shard_map/ppermute | solution.py:36
  6.7 11.0 %collective-permute-start.11 = (bf16[4,2,128,256]{3,2,1,0:T(8,128)(2,1)S(1)}, bf16[4,2,128,256]{3,2,1,0:T(8,128)(2,1)S(1)}, u32[]{:S(2)}, u32[]{:S(2)}) collective-permute-start(bf16[4,2,128,256]{3,2,1,0:T(8,128)(2,1)S(1)} %get-tuple-element.50), channel_id=1, source_target_pairs={{0,1},{1,0},{2,3},{3,2},{4,5},{5,4},{6,7},{7,6},{8,9},{9,8},{10,11... | collective-permute-start | bytes 1572872 | tf_op jit(solution)/shard_map/ppermute | solution.py:36
  7.4 10.3 %collective-permute-start.3 = (bf16[2,2,128,256]{3,2,1,0:T(8,128)(2,1)S(1)}, bf16[2,2,128,256]{3,2,1,0:T(8,128)(2,1)S(1)}, u32[]{:S(2)}, u32[]{:S(2)}) collective-permute-start(bf16[2,2,128,256]{3,2,1,0:T(8,128)(2,1)S(1)} %both_rows.2.refs_1_), channel_id=1, source_target_pairs={{0,4},{4,8},{8,12},{12,0},{1,5},{5,9},{9,13},{13,1},{2,6},{6,10},{... | collective-permute-start | bytes 786440 | tf_op jit(solution)/shard_map/ppermute | solution.py:27
  11.9 2.1 %collective-permute-start.2 = (bf16[1,2,128,256]{3,2,1,0:T(8,128)(2,1)S(1)}, bf16[1,2,128,256]{3,2,1,0:T(8,128)(2,1)S(1)}, u32[]{:S(2)}, u32[]{:S(2)}) collective-permute-start(bf16[1,2,128,256]{3,2,1,0:T(8,128)(2,1)S(1)} %other_side.1), channel_id=1, source_target_pairs={{0,1},{1,0},{2,3},{3,2},{4,5},{5,4},{6,7},{7,6},{8,9},{9,8},{10,11... | collective-permute-start | bytes 393224 | tf_op jit(solution)/shard_map/ppermute | solution.py:36
  12.2 9.2 %collective-permute-start.6 = (bf16[2,2,128,256]{3,2,1,0:T(8,128)(2,1)S(1)}, bf16[2,2,128,256]{3,2,1,0:T(8,128)(2,1)S(1)}, u32[]{:S(2)}, u32[]{:S(2)}) collective-permute-start(bf16[2,2,128,256]{3,2,1,0:T(8,128)(2,1)S(1)} %head_parts.7), channel_id=1, source_target_pairs={{0,2},{2,0},{1,3},{3,1},{4,6},{6,4},{5,7},{7,5},{8,10},{10,8},{9,1... | collective-permute-start | bytes 786440 | tf_op jit(solution)/shard_map/ppermute | solution.py:32
  14.2 11.0 %collective-permute-start.4 = (bf16[2,2,128,256]{3,2,1,0:T(8,128)(2,1)S(1)}, bf16[2,2,128,256]{3,2,1,0:T(8,128)(2,1)S(1)}, u32[]{:S(2)}, u32[]{:S(2)}) collective-permute-start(bf16[2,2,128,256]{3,2,1,0:T(8,128)(2,1)S(1)} %both_rows.3.refs_2_.refs_0_), channel_id=1, source_target_pairs={{0,4},{4,8},{8,12},{12,0},{1,5},{5,9},{9,13},{13,1},{2,6},{6,10},{... | collective-permute-start | bytes 786440 | tf_op jit(solution)/shard_map/ppermute | solution.py:27
  17.9 10.7 %collective-permute-start.12 = (bf16[2,2,128,256]{3,2,1,0:T(8,128)(2,1)S(1)}, bf16[2,2,128,256]{3,2,1,0:T(8,128)(2,1)S(1)}, u32[]{:S(2)}, u32[]{:S(2)}) collective-permute-start(bf16[2,2,128,256]{3,2,1,0:T(8,128)(2,1)S(1)} %head_parts.9), channel_id=1, source_target_pairs={{0,2},{2,0},{1,3},{3,1},{4,6},{6,4},{5,7},{7,5},{8,10},{10,8},{9,1... | collective-permute-start | bytes 786440 | tf_op jit(solution)/shard_map/ppermute | solution.py:32
  19.7 16.8 %collective-permute-start.13 = (bf16[2,2,128,256]{3,2,1,0:T(8,128)(2,1)S(1)}, bf16[2,2,128,256]{3,2,1,0:T(8,128)(2,1)S(1)}, u32[]{:S(2)}, u32[]{:S(2)}) collective-permute-start(bf16[2,2,128,256]{3,2,1,0:T(8,128)(2,1)S(1)} %head_parts.8.refs_1_), channel_id=1, source_target_pairs={{0,4},{4,8},{8,12},{12,0},{1,5},{5,9},{9,13},{13,1},{2,6},{6,10},{... | collective-permute-start | bytes 786440 | tf_op jit(solution)/shard_map/ppermute | solution.py:27
  21.5 16.3 %collective-permute-start.15 = (bf16[2,2,128,256]{3,2,1,0:T(8,128)(2,1)S(1)}, bf16[2,2,128,256]{3,2,1,0:T(8,128)(2,1)S(1)}, u32[]{:S(2)}, u32[]{:S(2)}) collective-permute-start(bf16[2,2,128,256]{3,2,1,0:T(8,128)(2,1)S(1)} %head_parts.11), channel_id=1, source_target_pairs={{0,2},{2,0},{1,3},{3,1},{4,6},{6,4},{5,7},{7,5},{8,10},{10,8},{9,1... | collective-permute-start | bytes 786440 | tf_op jit(solution)/shard_map/ppermute | solution.py:32
  27.3 13.1 %collective-permute-start.8 = (bf16[2,2,2,128,128]{4,3,2,1,0:T(8,128)(2,1)S(1)}, bf16[2,2,2,128,128]{4,3,2,1,0:T(8,128)(2,1)S(1)}, u32[]{:S(2)}, u32[]{:S(2)}) collective-permute-start(bf16[2,2,2,128,128]{4,3,2,1,0:T(8,128)(2,1)S(1)} %get-tuple-element.44), channel_id=1, source_target_pairs={{4,0},{8,4},{12,8},{5,1},{9,5},{13,9},{6,2},{10,6},{14,10},{7,3},{... | collective-permute-start | bytes 786440 | tf_op jit(solution)/shard_map/ppermute | solution.py:27
  28.6 11.8 %collective-permute-start.14 = (bf16[2,2,128,256]{3,2,1,0:T(8,128)(2,1)S(1)}, bf16[2,2,128,256]{3,2,1,0:T(8,128)(2,1)S(1)}, u32[]{:S(2)}, u32[]{:S(2)}) collective-permute-start(bf16[2,2,128,256]{3,2,1,0:T(8,128)(2,1)S(1)} %relayed.2), channel_id=1, source_target_pairs={{0,4},{4,8},{8,12},{1,5},{5,9},{9,13},{2,6},{6,10},{10,14},{3,7},{... | collective-permute-start | bytes 786440 | tf_op jit(solution)/shard_map/ppermute | solution.py:27
  35.4 5.0 %collective-permute-start.7 = (bf16[2,128,256]{2,1,0:T(8,128)(2,1)S(1)}, bf16[2,128,256]{2,1,0:T(8,128)(2,1)S(1)}, u32[]{:S(2)}, u32[]{:S(2)}) collective-permute-start(bf16[2,128,256]{2,1,0:T(8,128)(2,1)S(1)} %get-tuple-element.41), channel_id=1, source_target_pairs={{0,2},{2,0},{1,3},{3,1},{4,6},{6,4},{5,7},{7,5},{8,10},{10,8},{9,1... | collective-permute-start | bytes 393224 | tf_op jit(solution)/shard_map/ppermute | solution.py:32
  36.6 9.7 %collective-permute-start.9 = (bf16[2,2,2,128,128]{4,3,2,1,0:T(8,128)(2,1)S(1)}, bf16[2,2,2,128,128]{4,3,2,1,0:T(8,128)(2,1)S(1)}, u32[]{:S(2)}, u32[]{:S(2)}) collective-permute-start(bf16[2,2,2,128,128]{4,3,2,1,0:T(8,128)(2,1)S(1)} %get-tuple-element.45), channel_id=1, source_target_pairs={{4,0},{8,4},{12,8},{5,1},{9,5},{13,9},{6,2},{10,6},{14,10},{7,3},{... | collective-permute-start | bytes 786440 | tf_op jit(solution)/shard_map/ppermute | solution.py:27
  44.0 9.0 %collective-permute-start.18 = (bf16[2,2,128,256]{3,2,1,0:T(8,128)(2,1)S(1)}, bf16[2,2,128,256]{3,2,1,0:T(8,128)(2,1)S(1)}, u32[]{:S(2)}, u32[]{:S(2)}) collective-permute-start(bf16[2,2,128,256]{3,2,1,0:T(8,128)(2,1)S(1)} %get-tuple-element.55), channel_id=1, source_target_pairs={{4,0},{8,4},{12,8},{5,1},{9,5},{13,9},{6,2},{10,6},{14,10},{7,3},{... | collective-permute-start | bytes 786440 | tf_op jit(solution)/shard_map/ppermute | solution.py:27
  45.3 5.4 %collective-permute-start.16 = (bf16[2,128,256]{2,1,0:T(8,128)(2,1)S(1)}, bf16[2,128,256]{2,1,0:T(8,128)(2,1)S(1)}, u32[]{:S(2)}, u32[]{:S(2)}) collective-permute-start(bf16[2,128,256]{2,1,0:T(8,128)(2,1)S(1)} %get-tuple-element.52), channel_id=1, source_target_pairs={{0,2},{2,0},{1,3},{3,1},{4,6},{6,4},{5,7},{7,5},{8,10},{10,8},{9,1... | collective-permute-start | bytes 393224 | tf_op jit(solution)/shard_map/ppermute | solution.py:32
  46.4 9.5 %collective-permute-start.10 = (bf16[2,2,128,256]{3,2,1,0:T(8,128)(2,1)S(1)}, bf16[2,2,128,256]{3,2,1,0:T(8,128)(2,1)S(1)}, u32[]{:S(2)}, u32[]{:S(2)}) collective-permute-start(bf16[2,2,128,256]{3,2,1,0:T(8,128)(2,1)S(1)} %get-tuple-element.47), channel_id=1, source_target_pairs={{0,2},{2,0},{1,3},{3,1},{4,6},{6,4},{5,7},{7,5},{8,10},{10,8},{9,1... | collective-permute-start | bytes 786440 | tf_op jit(solution)/shard_map/ppermute | solution.py:32
  50.7 8.6 %collective-permute-start.17 = (bf16[2,2,128,256]{3,2,1,0:T(8,128)(2,1)S(1)}, bf16[2,2,128,256]{3,2,1,0:T(8,128)(2,1)S(1)}, u32[]{:S(2)}, u32[]{:S(2)}) collective-permute-start(bf16[2,2,128,256]{3,2,1,0:T(8,128)(2,1)S(1)} %relayed.3), channel_id=1, source_target_pairs={{4,0},{8,4},{12,8},{5,1},{9,5},{13,9},{6,2},{10,6},{14,10},{7,3},{... | collective-permute-start | bytes 786440 | tf_op jit(solution)/shard_map/ppermute | solution.py:27
  53.1 6.4 %collective-permute-start.19 = (bf16[2,2,128,256]{3,2,1,0:T(8,128)(2,1)S(1)}, bf16[2,2,128,256]{3,2,1,0:T(8,128)(2,1)S(1)}, u32[]{:S(2)}, u32[]{:S(2)}) collective-permute-start(bf16[2,2,128,256]{3,2,1,0:T(8,128)(2,1)S(1)} %summed.5), channel_id=1, source_target_pairs={{0,2},{2,0},{1,3},{3,1},{4,6},{6,4},{5,7},{7,5},{8,10},{10,8},{9,1... | collective-permute-start | bytes 786440 | tf_op jit(solution)/shard_map/ppermute | solution.py:32
  56.0 3.7 %collective-permute-start.20 = (bf16[3,2,128,256]{3,2,1,0:T(8,128)(2,1)S(1)}, bf16[3,2,128,256]{3,2,1,0:T(8,128)(2,1)S(1)}, u32[]{:S(2)}, u32[]{:S(2)}) collective-permute-start(bf16[3,2,128,256]{3,2,1,0:T(8,128)(2,1)S(1)} %get-tuple-element.57), channel_id=1, source_target_pairs={{0,1},{1,0},{2,3},{3,2},{4,5},{5,4},{6,7},{7,6},{8,9},{9,8},{10,11... | collective-permute-start | bytes 1179656 | tf_op jit(solution)/shard_map/ppermute | solution.py:36
  59.6 1.8 %collective-permute-start.21 = (bf16[3,2,128,256]{3,2,1,0:T(8,128)(2,1)S(1)}, bf16[3,2,128,256]{3,2,1,0:T(8,128)(2,1)S(1)}, u32[]{:S(2)}, u32[]{:S(2)}) collective-permute-start(bf16[3,2,128,256]{3,2,1,0:T(8,128)(2,1)S(1)} %get-tuple-element.58), channel_id=1, source_target_pairs={{0,1},{1,0},{2,3},{3,2},{4,5},{5,4},{6,7},{7,6},{8,9},{9,8},{10,11... | collective-permute-start | bytes 1179656 | tf_op jit(solution)/shard_map/ppermute | solution.py:36

commit v16 on v15

--- a/solution.py
+++ b/solution.py
@@ -313,22 +313,6 @@
 
     outs = [shape(2, 2, rows, sum(widths))] * len(turns)
     return call(kernel, own + later + after, outs, [], "summed", whole=True)
-
-
-def side_by_side(groups):
-    count, peers = len(groups), len(groups[0])
-    _, rows, _ = groups[0][0].shape
-    widths = [group[0].shape[-1] for group in groups]
-
-    def kernel(*refs):
-        for by in range(peers):
-            start = 0
-            for group, width in enumerate(widths):
-                refs[count * peers + by][:, :, pl.ds(start, width)] = refs[group * peers + by][...]
-                start += width
-
-    ins = [array for group in groups for array in group]
-    return call(kernel, ins, [shape(2, rows, sum(widths))] * peers, [], "side_by_side", whole=True)
 
 
 def rows_for_pair(dq, dkv):
@@ -422,7 +406,7 @@
         own_earlier.append(along_blocks(kv_own[index][0], 1, True))
         qg_sends.append(head_parts(*qg_parts[index], others, qg[index - 1] if index else []))
         qg.append([round_sub(value, by) for by, value in zip(others, qg_sends[index])])
-    kept, paired, first_dq, back = [], [], [], []
+    kept, paired, first_dq, back, release = [], [], [], [], []
     for index, (low, high) in enumerate(spans):
         last = index == count - 1
         forward = [relayed(value, first_dq) if index else value for value in kv[index]]
@@ -435,19 +419,15 @@
             dq = [dq[0]] + [round_sub(dq[by], by) for by in others]
             later = [along_blocks(value, -1, False) for value in early[1:]]
             dkv = summed([grads], later, others, dq[1:])
-            near = along_blocks(relayed(early[0], dq[1:]), -1, False)
+            near = along_blocks(relayed(early[0], release), -1, False)
             dkv = summed([grads], [near], [0], []) + [round_sub(value, by) for by, value in zip(others, dkv)]
         else:
-            groups, turn = [], []
-            for head in range(heads):
-                groups.append(attention_grads(bias, kv_all, earlier, qg_all, False, head, 1, turn))
-                turn = groups[-1][1][:1]
-                first_dq = first_dq or turn
-            later = [along_blocks(early[0], -1, False) for _, _, early in groups]
-            dq = side_by_side([dq for _, dq, _ in groups]) if heads > 1 else groups[0][1]
+            grads, dq, early = attention_grads(bias, kv_all, earlier, qg_all, False, 0, heads, [])
+            first_dq = dq[:1]
             dq = [dq[0]] + [round_sub(dq[by], by) for by in others]
-            back = later[:1] + dq[1:]
-            dkv = summed([grads for grads, _, _ in groups], later, [0] + others, dq[1:])
+            back = dq[1:]
+            dkv = summed([grads], [along_blocks(early[0], -1, False)], [0] + others, dq[1:])
+            release = dkv[:1]
             dkv = [dkv[0]] + [round_sub(dkv[by], by) for by in others]
         send, keep = rows_for_pair(dq, dkv)
         kept.append(keep)

time: 63 us -> 62.7 us (level)
  waiting for transfers between devices: 21.4 us -> 23.7 us
  starting transfers between devices: 25.5 us -> 23.7 us
  Pallas kernels: 13.9 us -> 13.1 us
    ppermute x8 -> x7, waiting for transfers between devices: 7.99 us -> 12.1 us  [along_blocks(): return lax.ppermute(value, 'blk', pairs)]
    ppermute x8 -> x7, starting transfers between devices: 13.2 us -> 9.36 us  [along_blocks(): return lax.ppermute(value, 'blk', pairs)]
    ppermute x8, starting transfers between devices: 11 us -> 13 us  [round_sub(): lax.ppermute(value, 'sub', [(i, (i + by) % peers) for i in range(peers)])]
    ppermute x8, waiting for transfers between devices: 11.7 us -> 9.87 us  [round_sub(): lax.ppermute(value, 'sub', [(i, (i + by) % peers) for i in range(peers)])]
    pallas_call x21 -> x19, Pallas kernels: 11.1 us -> 10.4 us  [call(): pl.pallas_call(kernel, out_shape=outs, in_specs=[spec] * len(ins), out_sp...]
  transfers between devices with their start and end apart: 22 -> 21, of which waited for: 11 -> 11; matrix products, arithmetic and copies ran while one was open for 1% -> 1% of each run, Pallas kernels for 18% -> 17%
where the time goes in v16:
time: 62.7 us; the launch traced here: 62.3 us
  starting transfers between devices  23.7 us (38%)
  waiting for transfers between devices  23.7 us (38%)
  Pallas kernels  13.1 us (21%)
  between operations  0.91 us (1%)
  other arithmetic  0.79 us (1%)
    ppermute x8, starting transfers between devices, round_sub(): lax.ppermute(value, 'sub', [(i, (i + by) % peers) for i in range(peers)])  13 us
    ppermute x7, waiting for transfers between devices, along_blocks(): return lax.ppermute(value, 'blk', pairs)  12.1 us
    pallas_call x19, Pallas kernels, call(): pl.pallas_call(kernel, out_shape=outs, in_specs=[spec] * len(ins), out_sp...  10.4 us
    ppermute x8, waiting for transfers between devices, round_sub(): lax.ppermute(value, 'sub', [(i, (i + by) % peers) for i in range(peers)])  9.87 us
    ppermute x7, starting transfers between devices, along_blocks(): return lax.ppermute(value, 'blk', pairs)  9.36 us
    ppermute x6, waiting for transfers between devices, swapped(): return lax.ppermute(value, 'pair', [(0, 1), (1, 0)])  1.71 us
    pallas_call x1, Pallas kernels, first_parts(): pl.pallas_call(kernel, out_shape=outs, in_specs=[spec] * (len(held) + len...  1.64 us
    ppermute x6, starting transfers between devices, swapped(): return lax.ppermute(value, 'pair', [(0, 1), (1, 0)])  1.31 us
  transfers between devices with their start and end apart: 21, of which 11 were waited for; matrix products, arithmetic and copies ran while one was open for 1% of the time, Pallas kernels for 17%

profile of v16, /device:TPU:0, one launch (start us, length us, event | category | flops | bytes accessed | tf_op | source)
XLA Modules:
  0.0 62.3 jit_solution(5448745810159460699)
XLA Ops:
  0.6 1.2 %first_keys.1 = (bf16[2,2,128,256]{3,2,1,0:T(8,128)(2,1)S(1)}, bf16[2,128,256]{2,1,0:T(8,128)(2,1)S(1)}, bf16[2,128,256]{2,1,0:T(8,128)(2,1)S(1)}) custom-call(bf16[128,2048]{1,0:T(8,128)(2,1)} %refs_2_.1, bf16[128,2048]{1,0:T(8,128)(2,1)} %refs_3_.1), custom_call_target="tpu_custom_call" | custom-call | tf_op jit(solution)/shard_map/first_keys/pallas_call | solution.py:127
  1.8 0.5 collective-permute-start
  2.3 2.6 %collective-permute-start.1 = (bf16[2,2,128,256]{3,2,1,0:T(8,128)(2,1)S(1)}, bf16[2,2,128,256]{3,2,1,0:T(8,128)(2,1)S(1)}, u32[]{:S(2)}, u32[]{:S(2)}) collective-permute-start(bf16[2,2,128,256]{3,2,1,0:T(8,128)(2,1)S(1)} %get-tuple-element.27), channel_id=1, source_target_pairs={{0,2},{2,0},{1,3},{3,1},{4,6},{6,4},{5,7},{7,5},{8,10},{10,8},{9,1... | collective-permute-start | bytes 786440 | tf_op jit(solution)/shard_map/ppermute | solution.py:32
  4.9 1.6 %first_parts.1 = (bf16[2,2,128,256]{3,2,1,0:T(8,128)(2,1)S(1)}, bf16[2,2,128,256]{3,2,1,0:T(8,128)(2,1)S(1)}, bf16[4,2,128,256]{3,2,1,0:T(8,128)(2,1)S(1)}, bf16[4,2,128,256]{3,2,1,0:T(8,128)(2,1)S(1)}) custom-call(bf16[128,2048]{1,0:T(8,128)(2,1)} %refs_4_.1, bf16[128,2048]{1,0:T(8,128)(2,1)} %refs_5_.1, bf16[128,2048]{1,0:T(8,128)(2,1)} %refs_2_.1, ...), custom_call_target="tpu_custom_call" | custom-call | tf_op jit(solution)/shard_map/first_parts/pallas_call | solution.py:92
  6.5 0.2 collective-permute-start.5
  6.7 0.3 collective-permute-start.10
  7.1 0.1 pad_dynamic-slice_fusion
  7.2 0.2 both_rows.2.refs_1_
  7.4 1.6 %collective-permute-start.3 = (bf16[2,2,128,256]{3,2,1,0:T(8,128)(2,1)S(1)}, bf16[2,2,128,256]{3,2,1,0:T(8,128)(2,1)S(1)}, u32[]{:S(2)}, u32[]{:S(2)}) collective-permute-start(bf16[2,2,128,256]{3,2,1,0:T(8,128)(2,1)S(1)} %both_rows.2.refs_1_), channel_id=1, source_target_pairs={{0,4},{4,8},{8,12},{12,0},{1,5},{5,9},{9,13},{13,1},{2,6},{6,10},{... | collective-permute-start | bytes 786440 | tf_op jit(solution)/shard_map/ppermute | solution.py:27
  9.0 2.7 %collective-permute-done.1.refs_0_ = bf16[2,2,128,256]{3,2,1,0:T(8,128)(2,1)S(1)} collective-permute-done((bf16[2,2,128,256]{3,2,1,0:T(8,128)(2,1)S(1)}, bf16[2,2,128,256]{3,2,1,0:T(8,128)(2,1)S(1)}, u32[]{:S(2)}, u32[]{:S(2)}) %collective-permute-start.1) | collective-permute-done | bytes 262176 | tf_op jit(solution)/shard_map/ppermute | solution.py:32
  11.8 0.1 other_side.1
  12.0 0.2 head_parts.7
  12.2 1.8 %collective-permute-start.6 = (bf16[2,2,128,256]{3,2,1,0:T(8,128)(2,1)S(1)}, bf16[2,2,128,256]{3,2,1,0:T(8,128)(2,1)S(1)}, u32[]{:S(2)}, u32[]{:S(2)}) collective-permute-start(bf16[2,2,128,256]{3,2,1,0:T(8,128)(2,1)S(1)} %head_parts.7), channel_id=1, source_target_pairs={{0,2},{2,0},{1,3},{3,1},{4,6},{6,4},{5,7},{7,5},{8,10},{10,8},{9,1... | collective-permute-start | bytes 786440 | tf_op jit(solution)/shard_map/ppermute | solution.py:32
  14.0 0.2 both_rows.3.refs_2_.refs_0_
  14.2 1.6 %collective-permute-start.4 = (bf16[2,2,128,256]{3,2,1,0:T(8,128)(2,1)S(1)}, bf16[2,2,128,256]{3,2,1,0:T(8,128)(2,1)S(1)}, u32[]{:S(2)}, u32[]{:S(2)}) collective-permute-start(bf16[2,2,128,256]{3,2,1,0:T(8,128)(2,1)S(1)} %both_rows.3.refs_2_.refs_0_), channel_id=1, source_target_pairs={{0,4},{4,8},{8,12},{12,0},{1,5},{5,9},{9,13},{13,1},{2,6},{6,10},{... | collective-permute-start | bytes 786440 | tf_op jit(solution)/shard_map/ppermute | solution.py:27
  15.8 1.9 %collective-permute-done.3.refs_3_.refs_0_.refs_1_ = bf16[2,2,128,256]{3,2,1,0:T(8,128)(2,1)S(1)} collective-permute-done((bf16[2,2,128,256]{3,2,1,0:T(8,128)(2,1)S(1)}, bf16[2,2,128,256]{3,2,1,0:T(8,128)(2,1)S(1)}, u32[]{:S(2)}, u32[]{:S(2)}) %collective-permute-start.3) | collective-permute-done | bytes 262176 | tf_op jit(solution)/shard_map/ppermute | solution.py:27
  17.7 0.2 head_parts.9
  17.9 0.6 collective-permute-start.11
  18.5 0.7 %and_select_fusion = (f32[1,768,256]{2,1,0:T(8,128)S(1)}, f32[1,768,256]{2,1,0:T(8,128)S(1)}) fusion(s32[256]{0:T(256)S(1)} %get-tuple-element.56, s32[256]{0:T(256)S(1)} %get-tuple-element.54, s32[768]{0:T(1024)S(1)} %get-tuple-element.52, s32[768]{0:T(1024)S(1)} %get-tuple-element.50, pred[768]{0:T(1024)(128)(4,1)S(1)} %get-tuple-element.48, ...), kind=kLoop, calls=%fused_computation.1 | loop fusion | flops 1966080 | bytes 1590784 | tf_op jit(solution)/shard_map/jit(_where)/select_n | solution.py:370
  19.2 0.1 pad_maximum_fusion.refs_0_
  19.3 0.2 head_parts.6.refs_5_
  19.5 0.2 head_parts.8.refs_1_
  19.7 0.2 collective-permute-start.12
  19.9 1.4 %collective-permute-done.6.refs_6_.refs_0_ = bf16[2,2,128,256]{3,2,1,0:T(8,128)(2,1)S(1)} collective-permute-done((bf16[2,2,128,256]{3,2,1,0:T(8,128)(2,1)S(1)}, bf16[2,2,128,256]{3,2,1,0:T(8,128)(2,1)S(1)}, u32[]{:S(2)}, u32[]{:S(2)}) %collective-permute-start.6) | collective-permute-done | bytes 262176 | tf_op jit(solution)/shard_map/ppermute | solution.py:32
  21.3 0.2 head_parts.11
  21.5 1.8 %collective-permute-start.14 = (bf16[2,2,128,256]{3,2,1,0:T(8,128)(2,1)S(1)}, bf16[2,2,128,256]{3,2,1,0:T(8,128)(2,1)S(1)}, u32[]{:S(2)}, u32[]{:S(2)}) collective-permute-start(bf16[2,2,128,256]{3,2,1,0:T(8,128)(2,1)S(1)} %head_parts.11), channel_id=1, source_target_pairs={{0,2},{2,0},{1,3},{3,1},{4,6},{6,4},{5,7},{7,5},{8,10},{10,8},{9,1... | collective-permute-start | bytes 786440 | tf_op jit(solution)/shard_map/ppermute | solution.py:32
  23.3 1.8 %collective-permute-done.4.refs_4_ = bf16[2,2,128,256]{3,2,1,0:T(8,128)(2,1)S(1)} collective-permute-done((bf16[2,2,128,256]{3,2,1,0:T(8,128)(2,1)S(1)}, bf16[2,2,128,256]{3,2,1,0:T(8,128)(2,1)S(1)}, u32[]{:S(2)}, u32[]{:S(2)}) %collective-permute-start.4) | collective-permute-done | bytes 262176 | tf_op jit(solution)/shard_map/ppermute | solution.py:27
  25.2 3.5 %attention_grads.2 = (f32[2,2,2,128,256]{4,3,2,1,0:T(8,128)S(1)}, bf16[2,128,256]{2,1,0:T(8,128)(2,1)S(1)}, bf16[2,128,256]{2,1,0:T(8,128)(2,1)S(1)}, bf16[2,2,2,128,256]{4,3,2,1,0:T(8,128)(2,1)S(1)}) custom-call(f32[2,768,256]{2,1,0:T(8,128)S(1)} %pad_maximum_fusion.refs_0_, bf16[2,2,128,256]{3,2,1,0:T(8,128)(2,1)S(1)} %both_rows.2.refs_1_, ...), custom_call_target="tpu_custom_call" | custom-call | flops 1006632960 | bytes 4980736 | tf_op jit(solution)/shard_map/attention_grads/pallas_call | solution.py:51
  28.8 2.0 %collective-permute-start.13 = (bf16[2,2,128,256]{3,2,1,0:T(8,128)(2,1)S(1)}, bf16[2,2,128,256]{3,2,1,0:T(8,128)(2,1)S(1)}, u32[]{:S(2)}, u32[]{:S(2)}) collective-permute-start(bf16[2,2,128,256]{3,2,1,0:T(8,128)(2,1)S(1)} %relayed.2), channel_id=1, source_target_pairs={{0,4},{4,8},{8,12},{1,5},{5,9},{9,13},{2,6},{6,10},{10,14},{3,7},{... | collective-permute-start | bytes 786440 | tf_op jit(solution)/shard_map/ppermute | solution.py:27
  30.8 1.3 %collective-permute-start.8 = (bf16[2,2,2,128,256]{4,3,2,1,0:T(8,128)(2,1)S(1)}, bf16[2,2,2,128,256]{4,3,2,1,0:T(8,128)(2,1)S(1)}, u32[]{:S(2)}, u32[]{:S(2)}) collective-permute-start(bf16[2,2,2,128,256]{4,3,2,1,0:T(8,128)(2,1)S(1)} %get-tuple-element.33), channel_id=1, source_target_pairs={{4,0},{8,4},{12,8},{5,1},{9,5},{13,9},{6,2},{10,6},{14,10},{7,3},{... | collective-permute-start | bytes 1572872 | tf_op jit(solution)/shard_map/ppermute | solution.py:27
  32.1 1.6 %collective-permute-start.7 = (bf16[2,128,256]{2,1,0:T(8,128)(2,1)S(1)}, bf16[2,128,256]{2,1,0:T(8,128)(2,1)S(1)}, u32[]{:S(2)}, u32[]{:S(2)}) collective-permute-start(bf16[2,128,256]{2,1,0:T(8,128)(2,1)S(1)} %get-tuple-element.31), channel_id=1, source_target_pairs={{0,2},{2,0},{1,3},{3,1},{4,6},{6,4},{5,7},{7,5},{8,10},{10,8},{9,1... | collective-permute-start | bytes 393224 | tf_op jit(solution)/shard_map/ppermute | solution.py:32
  33.6 0.2 head_parts.10.refs_5_
  33.8 3.3 %collective-permute-done.7.refs_2_.refs_1_.refs_7_ = bf16[2,128,256]{2,1,0:T(8,128)(2,1)S(1)} collective-permute-done((bf16[2,128,256]{2,1,0:T(8,128)(2,1)S(1)}, bf16[2,128,256]{2,1,0:T(8,128)(2,1)S(1)}, u32[]{:S(2)}, u32[]{:S(2)}) %collective-permute-start.7) | collective-permute-done | bytes 131104 | tf_op jit(solution)/shard_map/ppermute | solution.py:32
  37.1 3.5 %attention_grads.3 = (f32[2,2,2,128,256]{4,3,2,1,0:T(8,128)S(1)}, bf16[2,128,256]{2,1,0:T(8,128)(2,1)S(1)}, bf16[2,128,256]{2,1,0:T(8,128)(2,1)S(1)}, bf16[2,2,1...) custom-call(f32[2,768,256]{2,1,0:T(8,128)S(1)} %pad_maximum_fusion.refs_0_, ...), custom_call_target="tpu_custom_call" | custom-call | flops 1006632960 | bytes 5111808 | tf_op jit(solution)/shard_map/attention_grads/pallas_call | solution.py:51
  40.6 1.3 %collective-permute-start.17 = (bf16[2,2,128,256]{3,2,1,0:T(8,128)(2,1)S(1)}, bf16[2,2,128,256]{3,2,1,0:T(8,128)(2,1)S(1)}, u32[]{:S(2)}, u32[]{:S(2)}) collective-permute-start(bf16[2,2,128,256]{3,2,1,0:T(8,128)(2,1)S(1)} %get-tuple-element.43), channel_id=1, source_target_pairs={{4,0},{8,4},{12,8},{5,1},{9,5},{13,9},{6,2},{10,6},{14,10},{7,3},{... | collective-permute-start | bytes 786440 | tf_op jit(solution)/shard_map/ppermute | solution.py:27
  41.9 1.6 %collective-permute-start.15 = (bf16[2,128,256]{2,1,0:T(8,128)(2,1)S(1)}, bf16[2,128,256]{2,1,0:T(8,128)(2,1)S(1)}, u32[]{:S(2)}, u32[]{:S(2)}) collective-permute-start(bf16[2,128,256]{2,1,0:T(8,128)(2,1)S(1)} %get-tuple-element.40), channel_id=1, source_target_pairs={{0,2},{2,0},{1,3},{3,1},{4,6},{6,4},{5,7},{7,5},{8,10},{10,8},{9,1... | collective-permute-start | bytes 393224 | tf_op jit(solution)/shard_map/ppermute | solution.py:32
  43.5 3.5 %collective-permute-done.8.refs_1_ = bf16[2,2,2,128,256]{4,3,2,1,0:T(8,128)(2,1)S(1)} collective-permute-done((bf16[2,2,2,128,256]{4,3,2,1,0:T(8,128)(2,1)S(1)}, bf16[2,2,2,128,256]{4,3,2,1,0:T(8,128)(2,1)S(1)}, u32[]{:S(2)}, u32[]{:S(2)}) %collective-permute-start.8) | collective-permute-done | bytes 524320 | tf_op jit(solution)/shard_map/ppermute | solution.py:27
  47.0 0.1 summed.3
  47.1 1.6 %collective-permute-start.9 = (bf16[2,2,128,256]{3,2,1,0:T(8,128)(2,1)S(1)}, bf16[2,2,128,256]{3,2,1,0:T(8,128)(2,1)S(1)}, u32[]{:S(2)}, u32[]{:S(2)}) collective-permute-start(bf16[2,2,128,256]{3,2,1,0:T(8,128)(2,1)S(1)} %get-tuple-element.35), channel_id=1, source_target_pairs={{0,2},{2,0},{1,3},{3,1},{4,6},{6,4},{5,7},{7,5},{8,10},{10,8},{9,1... | collective-permute-start | bytes 786440 | tf_op jit(solution)/shard_map/ppermute | solution.py:32
  48.7 1.3 %collective-permute-start.16 = (bf16[2,2,128,256]{3,2,1,0:T(8,128)(2,1)S(1)}, bf16[2,2,128,256]{3,2,1,0:T(8,128)(2,1)S(1)}, u32[]{:S(2)}, u32[]{:S(2)}) collective-permute-start(bf16[2,2,128,256]{3,2,1,0:T(8,128)(2,1)S(1)} %relayed.3), channel_id=1, source_target_pairs={{4,0},{8,4},{12,8},{5,1},{9,5},{13,9},{6,2},{10,6},{14,10},{7,3},{... | collective-permute-start | bytes 786440 | tf_op jit(solution)/shard_map/ppermute | solution.py:27
  50.0 2.6 %collective-permute-done.17.refs_1_ = bf16[2,2,128,256]{3,2,1,0:T(8,128)(2,1)S(1)} collective-permute-done((bf16[2,2,128,256]{3,2,1,0:T(8,128)(2,1)S(1)}, bf16[2,2,128,256]{3,2,1,0:T(8,128)(2,1)S(1)}, u32[]{:S(2)}, u32[]{:S(2)}) %collective-permute-start.17) | collective-permute-done | bytes 262176 | tf_op jit(solution)/shard_map/ppermute | solution.py:27
  52.7 1.6 %collective-permute-start.18 = (bf16[2,2,128,256]{3,2,1,0:T(8,128)(2,1)S(1)}, bf16[2,2,128,256]{3,2,1,0:T(8,128)(2,1)S(1)}, u32[]{:S(2)}, u32[]{:S(2)}) collective-permute-start(bf16[2,2,128,256]{3,2,1,0:T(8,128)(2,1)S(1)} %summed.5), channel_id=1, source_target_pairs={{0,2},{2,0},{1,3},{3,1},{4,6},{6,4},{5,7},{7,5},{8,10},{10,8},{9,1... | collective-permute-start | bytes 786440 | tf_op jit(solution)/shard_map/ppermute | solution.py:32
  54.2 0.3 collective-permute-done.9.refs_3_
  54.6 0.1 collective-permute-start.19
  54.7 2.3 %collective-permute-done.16.refs_1_ = bf16[2,2,128,256]{3,2,1,0:T(8,128)(2,1)S(1)} collective-permute-done((bf16[2,2,128,256]{3,2,1,0:T(8,128)(2,1)S(1)}, bf16[2,2,128,256]{3,2,1,0:T(8,128)(2,1)S(1)}, u32[]{:S(2)}, u32[]{:S(2)}) %collective-permute-start.16) | collective-permute-done | bytes 262176 | tf_op jit(solution)/shard_map/ppermute | solution.py:27
  57.0 2.1 %collective-permute-done.18.refs_3_ = bf16[2,2,128,256]{3,2,1,0:T(8,128)(2,1)S(1)} collective-permute-done((bf16[2,2,128,256]{3,2,1,0:T(8,128)(2,1)S(1)}, bf16[2,2,128,256]{3,2,1,0:T(8,128)(2,1)S(1)}, u32[]{:S(2)}, u32[]{:S(2)}) %collective-permute-start.18) | collective-permute-done | bytes 262176 | tf_op jit(solution)/shard_map/ppermute | solution.py:32
  59.3 1.7 %collective-permute-done.20.refs_3_ = bf16[3,2,128,256]{3,2,1,0:T(8,128)(2,1)S(1)} collective-permute-done((bf16[3,2,128,256]{3,2,1,0:T(8,128)(2,1)S(1)}, bf16[3,2,128,256]{3,2,1,0:T(8,128)(2,1)S(1)}, u32[]{:S(2)}, u32[]{:S(2)}) %collective-permute-start.20) | collective-permute-done | bytes 393248 | tf_op jit(solution)/shard_map/ppermute | solution.py:36
  61.0 1.3 %laid_out.1 = (bf16[128,2048]{1,0:T(8,128)(2,1)}, bf16[128,2048]{1,0:T(8,128)(2,1)}, bf16[128,2048]{1,0:T(8,128)(2,1)}) custom-call(bf16[3,2,128,256]{3,2,1,0:T(8,128)(2,1)S(1)} %get-tuple-element.36.refs_0_, bf16[3,2,128,256]{3,2,1,0:T(8,128)(2,1)S(1)} %get-tuple-element.44.refs_1_, bf16[3,2,128,256]{3,2,1,0:T(8,128)(2,1)S(1)} %collective-permute-done.19.refs_2_, ...), custom_call_target="tpu_custom_call" | custom-call | bytes 3145728 | tf_op jit(solution)/shard_map/laid_out/pallas_call | solution.py:51
  (26 shorter events, 0.5 us)
Async XLA Ops:
  1.8 5.4 %collective-permute-start = (bf16[2,128,256]{2,1,0:T(8,128)(2,1)S(1)}, bf16[2,128,256]{2,1,0:T(8,128)(2,1)S(1)}, u32[]{:S(2)}, u32[]{:S(2)}) collective-permute-start(bf16[2,128,256]{2,1,0:T(8,128)(2,1)S(1)} %get-tuple-element.26), channel_id=1, source_target_pairs={{0,1},{1,0},{2,3},{3,2},{4,5},{5,4},{6,7},{7,6},{8,9},{9,8},{10,11... | collective-permute-start | bytes 393224 | tf_op jit(solution)/shard_map/ppermute | solution.py:36
  2.3 9.5 %collective-permute-start.1 = (bf16[2,2,128,256]{3,2,1,0:T(8,128)(2,1)S(1)}, bf16[2,2,128,256]{3,2,1,0:T(8,128)(2,1)S(1)}, u32[]{:S(2)}, u32[]{:S(2)}) collective-permute-start(bf16[2,2,128,256]{3,2,1,0:T(8,128)(2,1)S(1)} %get-tuple-element.27), channel_id=1, source_target_pairs={{0,2},{2,0},{1,3},{3,1},{4,6},{6,4},{5,7},{7,5},{8,10},{10,8},{9,1... | collective-permute-start | bytes 786440 | tf_op jit(solution)/shard_map/ppermute | solution.py:32
  4.9 2.2 %copy-start = (s32[2048]{0:T(1024)S(1)}, s32[2048]{0:T(1024)}, u32[]{:S(2)}) copy-start(s32[2048]{0:T(1024)} %param.9) | copy-start | bytes 24580
  6.5 5.4 %collective-permute-start.5 = (bf16[2,2,128,256]{3,2,1,0:T(8,128)(2,1)S(1)}, bf16[2,2,128,256]{3,2,1,0:T(8,128)(2,1)S(1)}, u32[]{:S(2)}, u32[]{:S(2)}) collective-permute-start(bf16[2,2,128,256]{3,2,1,0:T(8,128)(2,1)S(1)} %get-tuple-element.29), channel_id=1, source_target_pairs={{0,1},{1,0},{2,3},{3,2},{4,5},{5,4},{6,7},{7,6},{8,9},{9,8},{10,11... | collective-permute-start | bytes 786440 | tf_op jit(solution)/shard_map/ppermute | solution.py:36
  6.7 11.0 %collective-permute-start.10 = (bf16[4,2,128,256]{3,2,1,0:T(8,128)(2,1)S(1)}, bf16[4,2,128,256]{3,2,1,0:T(8,128)(2,1)S(1)}, u32[]{:S(2)}, u32[]{:S(2)}) collective-permute-start(bf16[4,2,128,256]{3,2,1,0:T(8,128)(2,1)S(1)} %get-tuple-element.38), channel_id=1, source_target_pairs={{0,1},{1,0},{2,3},{3,2},{4,5},{5,4},{6,7},{7,6},{8,9},{9,8},{10,11... | collective-permute-start | bytes 1572872 | tf_op jit(solution)/shard_map/ppermute | solution.py:36
  7.4 10.3 %collective-permute-start.3 = (bf16[2,2,128,256]{3,2,1,0:T(8,128)(2,1)S(1)}, bf16[2,2,128,256]{3,2,1,0:T(8,128)(2,1)S(1)}, u32[]{:S(2)}, u32[]{:S(2)}) collective-permute-start(bf16[2,2,128,256]{3,2,1,0:T(8,128)(2,1)S(1)} %both_rows.2.refs_1_), channel_id=1, source_target_pairs={{0,4},{4,8},{8,12},{12,0},{1,5},{5,9},{9,13},{13,1},{2,6},{6,10},{... | collective-permute-start | bytes 786440 | tf_op jit(solution)/shard_map/ppermute | solution.py:27
  11.9 2.1 %collective-permute-start.2 = (bf16[1,2,128,256]{3,2,1,0:T(8,128)(2,1)S(1)}, bf16[1,2,128,256]{3,2,1,0:T(8,128)(2,1)S(1)}, u32[]{:S(2)}, u32[]{:S(2)}) collective-permute-start(bf16[1,2,128,256]{3,2,1,0:T(8,128)(2,1)S(1)} %other_side.1), channel_id=1, source_target_pairs={{0,1},{1,0},{2,3},{3,2},{4,5},{5,4},{6,7},{7,6},{8,9},{9,8},{10,11... | collective-permute-start | bytes 393224 | tf_op jit(solution)/shard_map/ppermute | solution.py:36
  12.2 9.2 %collective-permute-start.6 = (bf16[2,2,128,256]{3,2,1,0:T(8,128)(2,1)S(1)}, bf16[2,2,128,256]{3,2,1,0:T(8,128)(2,1)S(1)}, u32[]{:S(2)}, u32[]{:S(2)}) collective-permute-start(bf16[2,2,128,256]{3,2,1,0:T(8,128)(2,1)S(1)} %head_parts.7), channel_id=1, source_target_pairs={{0,2},{2,0},{1,3},{3,1},{4,6},{6,4},{5,7},{7,5},{8,10},{10,8},{9,1... | collective-permute-start | bytes 786440 | tf_op jit(solution)/shard_map/ppermute | solution.py:32
  14.2 11.0 %collective-permute-start.4 = (bf16[2,2,128,256]{3,2,1,0:T(8,128)(2,1)S(1)}, bf16[2,2,128,256]{3,2,1,0:T(8,128)(2,1)S(1)}, u32[]{:S(2)}, u32[]{:S(2)}) collective-permute-start(bf16[2,2,128,256]{3,2,1,0:T(8,128)(2,1)S(1)} %both_rows.3.refs_2_.refs_0_), channel_id=1, source_target_pairs={{0,4},{4,8},{8,12},{12,0},{1,5},{5,9},{9,13},{13,1},{2,6},{6,10},{... | collective-permute-start | bytes 786440 | tf_op jit(solution)/shard_map/ppermute | solution.py:27
  17.9 10.8 %collective-permute-start.11 = (bf16[2,2,128,256]{3,2,1,0:T(8,128)(2,1)S(1)}, bf16[2,2,128,256]{3,2,1,0:T(8,128)(2,1)S(1)}, u32[]{:S(2)}, u32[]{:S(2)}) collective-permute-start(bf16[2,2,128,256]{3,2,1,0:T(8,128)(2,1)S(1)} %head_parts.9), channel_id=1, source_target_pairs={{0,2},{2,0},{1,3},{3,1},{4,6},{6,4},{5,7},{7,5},{8,10},{10,8},{9,1... | collective-permute-start | bytes 786440 | tf_op jit(solution)/shard_map/ppermute | solution.py:32
  19.7 14.1 %collective-permute-start.12 = (bf16[2,2,128,256]{3,2,1,0:T(8,128)(2,1)S(1)}, bf16[2,2,128,256]{3,2,1,0:T(8,128)(2,1)S(1)}, u32[]{:S(2)}, u32[]{:S(2)}) collective-permute-start(bf16[2,2,128,256]{3,2,1,0:T(8,128)(2,1)S(1)} %head_parts.8.refs_1_), channel_id=1, source_target_pairs={{0,4},{4,8},{8,12},{12,0},{1,5},{5,9},{9,13},{13,1},{2,6},{6,10},{... | collective-permute-start | bytes 786440 | tf_op jit(solution)/shard_map/ppermute | solution.py:27
  21.5 12.3 %collective-permute-start.14 = (bf16[2,2,128,256]{3,2,1,0:T(8,128)(2,1)S(1)}, bf16[2,2,128,256]{3,2,1,0:T(8,128)(2,1)S(1)}, u32[]{:S(2)}, u32[]{:S(2)}) collective-permute-start(bf16[2,2,128,256]{3,2,1,0:T(8,128)(2,1)S(1)} %head_parts.11), channel_id=1, source_target_pairs={{0,2},{2,0},{1,3},{3,1},{4,6},{6,4},{5,7},{7,5},{8,10},{10,8},{9,1... | collective-permute-start | bytes 786440 | tf_op jit(solution)/shard_map/ppermute | solution.py:32
  28.8 8.3 %collective-permute-start.13 = (bf16[2,2,128,256]{3,2,1,0:T(8,128)(2,1)S(1)}, bf16[2,2,128,256]{3,2,1,0:T(8,128)(2,1)S(1)}, u32[]{:S(2)}, u32[]{:S(2)}) collective-permute-start(bf16[2,2,128,256]{3,2,1,0:T(8,128)(2,1)S(1)} %relayed.2), channel_id=1, source_target_pairs={{0,4},{4,8},{8,12},{1,5},{5,9},{9,13},{2,6},{6,10},{10,14},{3,7},{... | collective-permute-start | bytes 786440 | tf_op jit(solution)/shard_map/ppermute | solution.py:27
  30.8 16.2 %collective-permute-start.8 = (bf16[2,2,2,128,256]{4,3,2,1,0:T(8,128)(2,1)S(1)}, bf16[2,2,2,128,256]{4,3,2,1,0:T(8,128)(2,1)S(1)}, u32[]{:S(2)}, u32[]{:S(2)}) collective-permute-start(bf16[2,2,2,128,256]{4,3,2,1,0:T(8,128)(2,1)S(1)} %get-tuple-element.33), channel_id=1, source_target_pairs={{4,0},{8,4},{12,8},{5,1},{9,5},{13,9},{6,2},{10,6},{14,10},{7,3},{... | collective-permute-start | bytes 1572872 | tf_op jit(solution)/shard_map/ppermute | solution.py:27
  32.1 5.0 %collective-permute-start.7 = (bf16[2,128,256]{2,1,0:T(8,128)(2,1)S(1)}, bf16[2,128,256]{2,1,0:T(8,128)(2,1)S(1)}, u32[]{:S(2)}, u32[]{:S(2)}) collective-permute-start(bf16[2,128,256]{2,1,0:T(8,128)(2,1)S(1)} %get-tuple-element.31), channel_id=1, source_target_pairs={{0,2},{2,0},{1,3},{3,1},{4,6},{6,4},{5,7},{7,5},{8,10},{10,8},{9,1... | collective-permute-start | bytes 393224 | tf_op jit(solution)/shard_map/ppermute | solution.py:32
  40.6 12.0 %collective-permute-start.17 = (bf16[2,2,128,256]{3,2,1,0:T(8,128)(2,1)S(1)}, bf16[2,2,128,256]{3,2,1,0:T(8,128)(2,1)S(1)}, u32[]{:S(2)}, u32[]{:S(2)}) collective-permute-start(bf16[2,2,128,256]{3,2,1,0:T(8,128)(2,1)S(1)} %get-tuple-element.43), channel_id=1, source_target_pairs={{4,0},{8,4},{12,8},{5,1},{9,5},{13,9},{6,2},{10,6},{14,10},{7,3},{... | collective-permute-start | bytes 786440 | tf_op jit(solution)/shard_map/ppermute | solution.py:27
  41.9 8.1 %collective-permute-start.15 = (bf16[2,128,256]{2,1,0:T(8,128)(2,1)S(1)}, bf16[2,128,256]{2,1,0:T(8,128)(2,1)S(1)}, u32[]{:S(2)}, u32[]{:S(2)}) collective-permute-start(bf16[2,128,256]{2,1,0:T(8,128)(2,1)S(1)} %get-tuple-element.40), channel_id=1, source_target_pairs={{0,2},{2,0},{1,3},{3,1},{4,6},{6,4},{5,7},{7,5},{8,10},{10,8},{9,1... | collective-permute-start | bytes 393224 | tf_op jit(solution)/shard_map/ppermute | solution.py:32
  47.1 7.5 %collective-permute-start.9 = (bf16[2,2,128,256]{3,2,1,0:T(8,128)(2,1)S(1)}, bf16[2,2,128,256]{3,2,1,0:T(8,128)(2,1)S(1)}, u32[]{:S(2)}, u32[]{:S(2)}) collective-permute-start(bf16[2,2,128,256]{3,2,1,0:T(8,128)(2,1)S(1)} %get-tuple-element.35), channel_id=1, source_target_pairs={{0,2},{2,0},{1,3},{3,1},{4,6},{6,4},{5,7},{7,5},{8,10},{10,8},{9,1... | collective-permute-start | bytes 786440 | tf_op jit(solution)/shard_map/ppermute | solution.py:32
  48.7 8.3 %collective-permute-start.16 = (bf16[2,2,128,256]{3,2,1,0:T(8,128)(2,1)S(1)}, bf16[2,2,128,256]{3,2,1,0:T(8,128)(2,1)S(1)}, u32[]{:S(2)}, u32[]{:S(2)}) collective-permute-start(bf16[2,2,128,256]{3,2,1,0:T(8,128)(2,1)S(1)} %relayed.3), channel_id=1, source_target_pairs={{4,0},{8,4},{12,8},{5,1},{9,5},{13,9},{6,2},{10,6},{14,10},{7,3},{... | collective-permute-start | bytes 786440 | tf_op jit(solution)/shard_map/ppermute | solution.py:27
  52.7 6.5 %collective-permute-start.18 = (bf16[2,2,128,256]{3,2,1,0:T(8,128)(2,1)S(1)}, bf16[2,2,128,256]{3,2,1,0:T(8,128)(2,1)S(1)}, u32[]{:S(2)}, u32[]{:S(2)}) collective-permute-start(bf16[2,2,128,256]{3,2,1,0:T(8,128)(2,1)S(1)} %summed.5), channel_id=1, source_target_pairs={{0,2},{2,0},{1,3},{3,1},{4,6},{6,4},{5,7},{7,5},{8,10},{10,8},{9,1... | collective-permute-start | bytes 786440 | tf_op jit(solution)/shard_map/ppermute | solution.py:32
  54.6 4.7 %collective-permute-start.19 = (bf16[3,2,128,256]{3,2,1,0:T(8,128)(2,1)S(1)}, bf16[3,2,128,256]{3,2,1,0:T(8,128)(2,1)S(1)}, u32[]{:S(2)}, u32[]{:S(2)}) collective-permute-start(bf16[3,2,128,256]{3,2,1,0:T(8,128)(2,1)S(1)} %get-tuple-element.45), channel_id=1, source_target_pairs={{0,1},{1,0},{2,3},{3,2},{4,5},{5,4},{6,7},{7,6},{8,9},{9,8},{10,11... | collective-permute-start | bytes 1179656 | tf_op jit(solution)/shard_map/ppermute | solution.py:36
  59.2 1.8 %collective-permute-start.20 = (bf16[3,2,128,256]{3,2,1,0:T(8,128)(2,1)S(1)}, bf16[3,2,128,256]{3,2,1,0:T(8,128)(2,1)S(1)}, u32[]{:S(2)}, u32[]{:S(2)}) collective-permute-start(bf16[3,2,128,256]{3,2,1,0:T(8,128)(2,1)S(1)} %get-tuple-element.46), channel_id=1, source_target_pairs={{0,1},{1,0},{2,3},{3,2},{4,5},{5,4},{6,7},{7,6},{8,9},{9,8},{10,11... | collective-permute-start | bytes 1179656 | tf_op jit(solution)/shard_map/ppermute | solution.py:36

commit v17 on v16

--- a/solution.py
+++ b/solution.py
@@ -415,9 +415,9 @@
         kv_all = kv_own[index] + kv[index]
         heads = (high - low) // HD
         if last:
-            grads, dq, early = attention_grads(bias, kv_all, earlier, qg_all, True, 0, heads, back)
+            grads, dq, early = attention_grads(bias, kv_all, earlier, qg_all, True, 0, heads, [])
             dq = [dq[0]] + [round_sub(dq[by], by) for by in others]
-            later = [along_blocks(value, -1, False) for value in early[1:]]
+            later = [along_blocks(relayed(value, back), -1, False) for value in early[1:]]
             dkv = summed([grads], later, others, dq[1:])
             near = along_blocks(relayed(early[0], release), -1, False)
             dkv = summed([grads], [near], [0], []) + [round_sub(value, by) for by, value in zip(others, dkv)]

time: 62.7 us -> 63.2 us (level)
    ppermute x7, waiting for transfers between devices: 12.1 us -> 14.3 us  [along_blocks(): return lax.ppermute(value, 'blk', pairs)]
    ppermute x8, waiting for transfers between devices: 9.87 us -> 7.71 us  [round_sub(): lax.ppermute(value, 'sub', [(i, (i + by) % peers) for i in range(peers)])]
    pallas_call x19 -> x20, Pallas kernels: 10.4 us -> 10.4 us  [call(): pl.pallas_call(kernel, out_shape=outs, in_specs=[spec] * len(ins), out_sp...]
where the time goes in v17:
time: 63.2 us; the launch traced here: 62.8 us
  starting transfers between devices  24.2 us (38%)
  waiting for transfers between devices  23.7 us (38%)
  Pallas kernels  13.2 us (21%)
  between operations  0.93 us (1%)
  other arithmetic  0.79 us (1%)
    ppermute x7, waiting for transfers between devices, along_blocks(): return lax.ppermute(value, 'blk', pairs)  14.3 us
    ppermute x8, starting transfers between devices, round_sub(): lax.ppermute(value, 'sub', [(i, (i + by) % peers) for i in range(peers)])  13.5 us
    pallas_call x20, Pallas kernels, call(): pl.pallas_call(kernel, out_shape=outs, in_specs=[spec] * len(ins), out_sp...  10.4 us
    ppermute x7, starting transfers between devices, along_blocks(): return lax.ppermute(value, 'blk', pairs)  9.36 us
    ppermute x8, waiting for transfers between devices, round_sub(): lax.ppermute(value, 'sub', [(i, (i + by) % peers) for i in range(peers)])  7.71 us
    ppermute x6, waiting for transfers between devices, swapped(): return lax.ppermute(value, 'pair', [(0, 1), (1, 0)])  1.71 us
    pallas_call x1, Pallas kernels, first_parts(): pl.pallas_call(kernel, out_shape=outs, in_specs=[spec] * (len(held) + len...  1.64 us
    ppermute x6, starting transfers between devices, swapped(): return lax.ppermute(value, 'pair', [(0, 1), (1, 0)])  1.31 us
  transfers between devices with their start and end apart: 21, of which 11 were waited for; matrix products, arithmetic and copies ran while one was open for 1% of the time, Pallas kernels for 17%

profile of v17, /device:TPU:0, one launch (start us, length us, event | category | flops | bytes accessed | tf_op | source)
XLA Modules:
  0.0 62.8 jit_solution(7644315076773487291)
XLA Ops:
  0.6 1.2 %first_keys.1 = (bf16[2,2,128,256]{3,2,1,0:T(8,128)(2,1)S(1)}, bf16[2,128,256]{2,1,0:T(8,128)(2,1)S(1)}, bf16[2,128,256]{2,1,0:T(8,128)(2,1)S(1)}) custom-call(bf16[128,2048]{1,0:T(8,128)(2,1)} %refs_2_.1, bf16[128,2048]{1,0:T(8,128)(2,1)} %refs_3_.1), custom_call_target="tpu_custom_call" | custom-call | tf_op jit(solution)/shard_map/first_keys/pallas_call | solution.py:127
  1.8 0.5 collective-permute-start
  2.3 2.6 %collective-permute-start.1 = (bf16[2,2,128,256]{3,2,1,0:T(8,128)(2,1)S(1)}, bf16[2,2,128,256]{3,2,1,0:T(8,128)(2,1)S(1)}, u32[]{:S(2)}, u32[]{:S(2)}) collective-permute-start(bf16[2,2,128,256]{3,2,1,0:T(8,128)(2,1)S(1)} %get-tuple-element.27), channel_id=1, source_target_pairs={{0,2},{2,0},{1,3},{3,1},{4,6},{6,4},{5,7},{7,5},{8,10},{10,8},{9,1... | collective-permute-start | bytes 786440 | tf_op jit(solution)/shard_map/ppermute | solution.py:32
  4.9 1.6 %first_parts.1 = (bf16[2,2,128,256]{3,2,1,0:T(8,128)(2,1)S(1)}, bf16[2,2,128,256]{3,2,1,0:T(8,128)(2,1)S(1)}, bf16[4,2,128,256]{3,2,1,0:T(8,128)(2,1)S(1)}, bf16[4,2,128,256]{3,2,1,0:T(8,128)(2,1)S(1)}) custom-call(bf16[128,2048]{1,0:T(8,128)(2,1)} %refs_4_.1, bf16[128,2048]{1,0:T(8,128)(2,1)} %refs_5_.1, bf16[128,2048]{1,0:T(8,128)(2,1)} %refs_2_.1, ...), custom_call_target="tpu_custom_call" | custom-call | tf_op jit(solution)/shard_map/first_parts/pallas_call | solution.py:92
  6.5 0.2 collective-permute-start.5
  6.7 0.3 collective-permute-start.10
  7.1 0.1 pad_dynamic-slice_fusion
  7.2 0.2 both_rows.2.refs_1_
  7.4 1.6 %collective-permute-start.3 = (bf16[2,2,128,256]{3,2,1,0:T(8,128)(2,1)S(1)}, bf16[2,2,128,256]{3,2,1,0:T(8,128)(2,1)S(1)}, u32[]{:S(2)}, u32[]{:S(2)}) collective-permute-start(bf16[2,2,128,256]{3,2,1,0:T(8,128)(2,1)S(1)} %both_rows.2.refs_1_), channel_id=1, source_target_pairs={{0,4},{4,8},{8,12},{12,0},{1,5},{5,9},{9,13},{13,1},{2,6},{6,10},{... | collective-permute-start | bytes 786440 | tf_op jit(solution)/shard_map/ppermute | solution.py:27
  9.0 2.7 %collective-permute-done.1.refs_0_ = bf16[2,2,128,256]{3,2,1,0:T(8,128)(2,1)S(1)} collective-permute-done((bf16[2,2,128,256]{3,2,1,0:T(8,128)(2,1)S(1)}, bf16[2,2,128,256]{3,2,1,0:T(8,128)(2,1)S(1)}, u32[]{:S(2)}, u32[]{:S(2)}) %collective-permute-start.1) | collective-permute-done | bytes 262176 | tf_op jit(solution)/shard_map/ppermute | solution.py:32
  11.8 0.1 other_side.1
  11.9 0.1 collective-permute-start.2
  12.0 0.2 head_parts.7
  12.2 1.8 %collective-permute-start.6 = (bf16[2,2,128,256]{3,2,1,0:T(8,128)(2,1)S(1)}, bf16[2,2,128,256]{3,2,1,0:T(8,128)(2,1)S(1)}, u32[]{:S(2)}, u32[]{:S(2)}) collective-permute-start(bf16[2,2,128,256]{3,2,1,0:T(8,128)(2,1)S(1)} %head_parts.7), channel_id=1, source_target_pairs={{0,2},{2,0},{1,3},{3,1},{4,6},{6,4},{5,7},{7,5},{8,10},{10,8},{9,1... | collective-permute-start | bytes 786440 | tf_op jit(solution)/shard_map/ppermute | solution.py:32
  14.0 0.2 both_rows.3.refs_2_.refs_0_
  14.2 1.6 %collective-permute-start.4 = (bf16[2,2,128,256]{3,2,1,0:T(8,128)(2,1)S(1)}, bf16[2,2,128,256]{3,2,1,0:T(8,128)(2,1)S(1)}, u32[]{:S(2)}, u32[]{:S(2)}) collective-permute-start(bf16[2,2,128,256]{3,2,1,0:T(8,128)(2,1)S(1)} %both_rows.3.refs_2_.refs_0_), channel_id=1, source_target_pairs={{0,4},{4,8},{8,12},{12,0},{1,5},{5,9},{9,13},{13,1},{2,6},{6,10},{... | collective-permute-start | bytes 786440 | tf_op jit(solution)/shard_map/ppermute | solution.py:27
  15.8 1.9 %collective-permute-done.3.refs_3_.refs_0_.refs_1_ = bf16[2,2,128,256]{3,2,1,0:T(8,128)(2,1)S(1)} collective-permute-done((bf16[2,2,128,256]{3,2,1,0:T(8,128)(2,1)S(1)}, bf16[2,2,128,256]{3,2,1,0:T(8,128)(2,1)S(1)}, u32[]{:S(2)}, u32[]{:S(2)}) %collective-permute-start.3) | collective-permute-done | bytes 262176 | tf_op jit(solution)/shard_map/ppermute | solution.py:27
  17.7 0.2 head_parts.9
  17.9 0.6 collective-permute-start.11
  18.5 0.7 %and_select_fusion = (f32[1,768,256]{2,1,0:T(8,128)S(1)}, f32[1,768,256]{2,1,0:T(8,128)S(1)}) fusion(s32[256]{0:T(256)S(1)} %get-tuple-element.56, s32[256]{0:T(256)S(1)} %get-tuple-element.54, s32[768]{0:T(1024)S(1)} %get-tuple-element.52, s32[768]{0:T(1024)S(1)} %get-tuple-element.50, pred[768]{0:T(1024)(128)(4,1)S(1)} %get-tuple-element.48, ...), kind=kLoop, calls=%fused_computation.1 | loop fusion | flops 1966080 | bytes 1590784 | tf_op jit(solution)/shard_map/jit(_where)/select_n | solution.py:370
  19.2 0.1 pad_maximum_fusion.refs_0_
  19.3 0.2 head_parts.6.refs_5_
  19.5 0.2 head_parts.8.refs_1_
  19.7 0.2 collective-permute-start.12
  19.9 1.4 %collective-permute-done.6.refs_6_.refs_0_ = bf16[2,2,128,256]{3,2,1,0:T(8,128)(2,1)S(1)} collective-permute-done((bf16[2,2,128,256]{3,2,1,0:T(8,128)(2,1)S(1)}, bf16[2,2,128,256]{3,2,1,0:T(8,128)(2,1)S(1)}, u32[]{:S(2)}, u32[]{:S(2)}) %collective-permute-start.6) | collective-permute-done | bytes 262176 | tf_op jit(solution)/shard_map/ppermute | solution.py:32
  21.3 0.2 head_parts.11
  21.5 1.8 %collective-permute-start.14 = (bf16[2,2,128,256]{3,2,1,0:T(8,128)(2,1)S(1)}, bf16[2,2,128,256]{3,2,1,0:T(8,128)(2,1)S(1)}, u32[]{:S(2)}, u32[]{:S(2)}) collective-permute-start(bf16[2,2,128,256]{3,2,1,0:T(8,128)(2,1)S(1)} %head_parts.11), channel_id=1, source_target_pairs={{0,2},{2,0},{1,3},{3,1},{4,6},{6,4},{5,7},{7,5},{8,10},{10,8},{9,1... | collective-permute-start | bytes 786440 | tf_op jit(solution)/shard_map/ppermute | solution.py:32
  23.3 1.8 %collective-permute-done.4.refs_4_ = bf16[2,2,128,256]{3,2,1,0:T(8,128)(2,1)S(1)} collective-permute-done((bf16[2,2,128,256]{3,2,1,0:T(8,128)(2,1)S(1)}, bf16[2,2,128,256]{3,2,1,0:T(8,128)(2,1)S(1)}, u32[]{:S(2)}, u32[]{:S(2)}) %collective-permute-start.4) | collective-permute-done | bytes 262176 | tf_op jit(solution)/shard_map/ppermute | solution.py:27
  25.2 3.5 %attention_grads.2 = (f32[2,2,2,128,256]{4,3,2,1,0:T(8,128)S(1)}, bf16[2,128,256]{2,1,0:T(8,128)(2,1)S(1)}, bf16[2,128,256]{2,1,0:T(8,128)(2,1)S(1)}, bf16[2,2,2,128,256]{4,3,2,1,0:T(8,128)(2,1)S(1)}) custom-call(f32[2,768,256]{2,1,0:T(8,128)S(1)} %pad_maximum_fusion.refs_0_, bf16[2,2,128,256]{3,2,1,0:T(8,128)(2,1)S(1)} %both_rows.2.refs_1_, ...), custom_call_target="tpu_custom_call" | custom-call | flops 1006632960 | bytes 4980736 | tf_op jit(solution)/shard_map/attention_grads/pallas_call | solution.py:51
  28.8 2.0 %collective-permute-start.13 = (bf16[2,2,128,256]{3,2,1,0:T(8,128)(2,1)S(1)}, bf16[2,2,128,256]{3,2,1,0:T(8,128)(2,1)S(1)}, u32[]{:S(2)}, u32[]{:S(2)}) collective-permute-start(bf16[2,2,128,256]{3,2,1,0:T(8,128)(2,1)S(1)} %relayed.3), channel_id=1, source_target_pairs={{0,4},{4,8},{8,12},{1,5},{5,9},{9,13},{2,6},{6,10},{10,14},{3,7},{... | collective-permute-start | bytes 786440 | tf_op jit(solution)/shard_map/ppermute | solution.py:27
  30.8 1.3 %collective-permute-start.8 = (bf16[2,2,2,128,256]{4,3,2,1,0:T(8,128)(2,1)S(1)}, bf16[2,2,2,128,256]{4,3,2,1,0:T(8,128)(2,1)S(1)}, u32[]{:S(2)}, u32[]{:S(2)}) collective-permute-start(bf16[2,2,2,128,256]{4,3,2,1,0:T(8,128)(2,1)S(1)} %get-tuple-element.33), channel_id=1, source_target_pairs={{4,0},{8,4},{12,8},{5,1},{9,5},{13,9},{6,2},{10,6},{14,10},{7,3},{... | collective-permute-start | bytes 1572872 | tf_op jit(solution)/shard_map/ppermute | solution.py:27
  32.1 1.6 %collective-permute-start.7 = (bf16[2,128,256]{2,1,0:T(8,128)(2,1)S(1)}, bf16[2,128,256]{2,1,0:T(8,128)(2,1)S(1)}, u32[]{:S(2)}, u32[]{:S(2)}) collective-permute-start(bf16[2,128,256]{2,1,0:T(8,128)(2,1)S(1)} %get-tuple-element.31), channel_id=1, source_target_pairs={{0,2},{2,0},{1,3},{3,1},{4,6},{6,4},{5,7},{7,5},{8,10},{10,8},{9,1... | collective-permute-start | bytes 393224 | tf_op jit(solution)/shard_map/ppermute | solution.py:32
  33.6 0.2 head_parts.10.refs_5_
  33.8 1.9 %collective-permute-done.13.refs_4_ = bf16[2,2,128,256]{3,2,1,0:T(8,128)(2,1)S(1)} collective-permute-done((bf16[2,2,128,256]{3,2,1,0:T(8,128)(2,1)S(1)}, bf16[2,2,128,256]{3,2,1,0:T(8,128)(2,1)S(1)}, u32[]{:S(2)}, u32[]{:S(2)}) %collective-permute-start.13) | collective-permute-done | bytes 262176 | tf_op jit(solution)/shard_map/ppermute | solution.py:27
  35.8 3.5 %attention_grads.3 = (f32[2,2,2,128,256]{4,3,2,1,0:T(8,128)S(1)}, bf16[2,128,256]{2,1,0:T(8,128)(2,1)S(1)}, bf16[2,128,256]{2,1,0:T(8,128)(2,1)S(1)}, bf16[2,2,1...) custom-call(f32[2,768,256]{2,1,0:T(8,128)S(1)} %pad_maximum_fusion.refs_0_, ...), custom_call_target="tpu_custom_call" | custom-call | flops 1006632960 | bytes 4980736 | tf_op jit(solution)/shard_map/attention_grads/pallas_call | solution.py:51
  39.4 1.3 %collective-permute-start.17 = (bf16[2,2,128,256]{3,2,1,0:T(8,128)(2,1)S(1)}, bf16[2,2,128,256]{3,2,1,0:T(8,128)(2,1)S(1)}, u32[]{:S(2)}, u32[]{:S(2)}) collective-permute-start(bf16[2,2,128,256]{3,2,1,0:T(8,128)(2,1)S(1)} %relayed.5), channel_id=1, source_target_pairs={{4,0},{8,4},{12,8},{5,1},{9,5},{13,9},{6,2},{10,6},{14,10},{7,3},{... | collective-permute-start | bytes 786440 | tf_op jit(solution)/shard_map/ppermute | solution.py:27
  40.7 1.6 %collective-permute-start.15 = (bf16[2,128,256]{2,1,0:T(8,128)(2,1)S(1)}, bf16[2,128,256]{2,1,0:T(8,128)(2,1)S(1)}, u32[]{:S(2)}, u32[]{:S(2)}) collective-permute-start(bf16[2,128,256]{2,1,0:T(8,128)(2,1)S(1)} %get-tuple-element.40), channel_id=1, source_target_pairs={{0,2},{2,0},{1,3},{3,1},{4,6},{6,4},{5,7},{7,5},{8,10},{10,8},{9,1... | collective-permute-start | bytes 393224 | tf_op jit(solution)/shard_map/ppermute | solution.py:32
  42.2 5.3 %collective-permute-done.8.refs_1_ = bf16[2,2,2,128,256]{4,3,2,1,0:T(8,128)(2,1)S(1)} collective-permute-done((bf16[2,2,2,128,256]{4,3,2,1,0:T(8,128)(2,1)S(1)}, bf16[2,2,2,128,256]{4,3,2,1,0:T(8,128)(2,1)S(1)}, u32[]{:S(2)}, u32[]{:S(2)}) %collective-permute-start.8) | collective-permute-done | bytes 524320 | tf_op jit(solution)/shard_map/ppermute | solution.py:27
  47.5 0.1 summed.3
  47.6 1.6 %collective-permute-start.9 = (bf16[2,2,128,256]{3,2,1,0:T(8,128)(2,1)S(1)}, bf16[2,2,128,256]{3,2,1,0:T(8,128)(2,1)S(1)}, u32[]{:S(2)}, u32[]{:S(2)}) collective-permute-start(bf16[2,2,128,256]{3,2,1,0:T(8,128)(2,1)S(1)} %get-tuple-element.35), channel_id=1, source_target_pairs={{0,2},{2,0},{1,3},{3,1},{4,6},{6,4},{5,7},{7,5},{8,10},{10,8},{9,1... | collective-permute-start | bytes 786440 | tf_op jit(solution)/shard_map/ppermute | solution.py:32
  49.2 1.3 %collective-permute-start.16 = (bf16[2,2,128,256]{3,2,1,0:T(8,128)(2,1)S(1)}, bf16[2,2,128,256]{3,2,1,0:T(8,128)(2,1)S(1)}, u32[]{:S(2)}, u32[]{:S(2)}) collective-permute-start(bf16[2,2,128,256]{3,2,1,0:T(8,128)(2,1)S(1)} %relayed.4), channel_id=1, source_target_pairs={{4,0},{8,4},{12,8},{5,1},{9,5},{13,9},{6,2},{10,6},{14,10},{7,3},{... | collective-permute-start | bytes 786440 | tf_op jit(solution)/shard_map/ppermute | solution.py:27
  50.5 2.2 %collective-permute-done.17.refs_1_ = bf16[2,2,128,256]{3,2,1,0:T(8,128)(2,1)S(1)} collective-permute-done((bf16[2,2,128,256]{3,2,1,0:T(8,128)(2,1)S(1)}, bf16[2,2,128,256]{3,2,1,0:T(8,128)(2,1)S(1)}, u32[]{:S(2)}, u32[]{:S(2)}) %collective-permute-start.17) | collective-permute-done | bytes 262176 | tf_op jit(solution)/shard_map/ppermute | solution.py:27
  52.7 2.0 %collective-permute-start.18 = (bf16[2,2,128,256]{3,2,1,0:T(8,128)(2,1)S(1)}, bf16[2,2,128,256]{3,2,1,0:T(8,128)(2,1)S(1)}, u32[]{:S(2)}, u32[]{:S(2)}) collective-permute-start(bf16[2,2,128,256]{3,2,1,0:T(8,128)(2,1)S(1)} %summed.5), channel_id=1, source_target_pairs={{0,2},{2,0},{1,3},{3,1},{4,6},{6,4},{5,7},{7,5},{8,10},{10,8},{9,1... | collective-permute-start | bytes 786440 | tf_op jit(solution)/shard_map/ppermute | solution.py:32
  54.8 1.4 %collective-permute-done.9.refs_3_ = bf16[2,2,128,256]{3,2,1,0:T(8,128)(2,1)S(1)} collective-permute-done((bf16[2,2,128,256]{3,2,1,0:T(8,128)(2,1)S(1)}, bf16[2,2,128,256]{3,2,1,0:T(8,128)(2,1)S(1)}, u32[]{:S(2)}, u32[]{:S(2)}) %collective-permute-start.9) | collective-permute-done | bytes 262176 | tf_op jit(solution)/shard_map/ppermute | solution.py:32
  56.3 1.1 %collective-permute-done.16.refs_1_ = bf16[2,2,128,256]{3,2,1,0:T(8,128)(2,1)S(1)} collective-permute-done((bf16[2,2,128,256]{3,2,1,0:T(8,128)(2,1)S(1)}, bf16[2,2,128,256]{3,2,1,0:T(8,128)(2,1)S(1)}, u32[]{:S(2)}, u32[]{:S(2)}) %collective-permute-start.16) | collective-permute-done | bytes 262176 | tf_op jit(solution)/shard_map/ppermute | solution.py:27
  57.5 2.1 %collective-permute-done.18.refs_3_ = bf16[2,2,128,256]{3,2,1,0:T(8,128)(2,1)S(1)} collective-permute-done((bf16[2,2,128,256]{3,2,1,0:T(8,128)(2,1)S(1)}, bf16[2,2,128,256]{3,2,1,0:T(8,128)(2,1)S(1)}, u32[]{:S(2)}, u32[]{:S(2)}) %collective-permute-start.18) | collective-permute-done | bytes 262176 | tf_op jit(solution)/shard_map/ppermute | solution.py:32
  59.8 1.7 %collective-permute-done.20.refs_3_ = bf16[3,2,128,256]{3,2,1,0:T(8,128)(2,1)S(1)} collective-permute-done((bf16[3,2,128,256]{3,2,1,0:T(8,128)(2,1)S(1)}, bf16[3,2,128,256]{3,2,1,0:T(8,128)(2,1)S(1)}, u32[]{:S(2)}, u32[]{:S(2)}) %collective-permute-start.20) | collective-permute-done | bytes 393248 | tf_op jit(solution)/shard_map/ppermute | solution.py:36
  61.5 1.3 %laid_out.1 = (bf16[128,2048]{1,0:T(8,128)(2,1)}, bf16[128,2048]{1,0:T(8,128)(2,1)}, bf16[128,2048]{1,0:T(8,128)(2,1)}) custom-call(bf16[3,2,128,256]{3,2,1,0:T(8,128)(2,1)S(1)} %get-tuple-element.36.refs_0_, bf16[3,2,128,256]{3,2,1,0:T(8,128)(2,1)S(1)} %get-tuple-element.44.refs_1_, bf16[3,2,128,256]{3,2,1,0:T(8,128)(2,1)S(1)} %collective-permute-done.19.refs_2_, ...), custom_call_target="tpu_custom_call" | custom-call | bytes 3145728 | tf_op jit(solution)/shard_map/laid_out/pallas_call | solution.py:51
  (27 shorter events, 0.5 us)
Async XLA Ops:
  1.8 5.4 %collective-permute-start = (bf16[2,128,256]{2,1,0:T(8,128)(2,1)S(1)}, bf16[2,128,256]{2,1,0:T(8,128)(2,1)S(1)}, u32[]{:S(2)}, u32[]{:S(2)}) collective-permute-start(bf16[2,128,256]{2,1,0:T(8,128)(2,1)S(1)} %get-tuple-element.26), channel_id=1, source_target_pairs={{0,1},{1,0},{2,3},{3,2},{4,5},{5,4},{6,7},{7,6},{8,9},{9,8},{10,11... | collective-permute-start | bytes 393224 | tf_op jit(solution)/shard_map/ppermute | solution.py:36
  2.3 9.5 %collective-permute-start.1 = (bf16[2,2,128,256]{3,2,1,0:T(8,128)(2,1)S(1)}, bf16[2,2,128,256]{3,2,1,0:T(8,128)(2,1)S(1)}, u32[]{:S(2)}, u32[]{:S(2)}) collective-permute-start(bf16[2,2,128,256]{3,2,1,0:T(8,128)(2,1)S(1)} %get-tuple-element.27), channel_id=1, source_target_pairs={{0,2},{2,0},{1,3},{3,1},{4,6},{6,4},{5,7},{7,5},{8,10},{10,8},{9,1... | collective-permute-start | bytes 786440 | tf_op jit(solution)/shard_map/ppermute | solution.py:32
  4.9 2.2 %copy-start = (s32[2048]{0:T(1024)S(1)}, s32[2048]{0:T(1024)}, u32[]{:S(2)}) copy-start(s32[2048]{0:T(1024)} %param.9) | copy-start | bytes 24580
  6.5 5.4 %collective-permute-start.5 = (bf16[2,2,128,256]{3,2,1,0:T(8,128)(2,1)S(1)}, bf16[2,2,128,256]{3,2,1,0:T(8,128)(2,1)S(1)}, u32[]{:S(2)}, u32[]{:S(2)}) collective-permute-start(bf16[2,2,128,256]{3,2,1,0:T(8,128)(2,1)S(1)} %get-tuple-element.29), channel_id=1, source_target_pairs={{0,1},{1,0},{2,3},{3,2},{4,5},{5,4},{6,7},{7,6},{8,9},{9,8},{10,11... | collective-permute-start | bytes 786440 | tf_op jit(solution)/shard_map/ppermute | solution.py:36
  6.7 11.0 %collective-permute-start.10 = (bf16[4,2,128,256]{3,2,1,0:T(8,128)(2,1)S(1)}, bf16[4,2,128,256]{3,2,1,0:T(8,128)(2,1)S(1)}, u32[]{:S(2)}, u32[]{:S(2)}) collective-permute-start(bf16[4,2,128,256]{3,2,1,0:T(8,128)(2,1)S(1)} %get-tuple-element.38), channel_id=1, source_target_pairs={{0,1},{1,0},{2,3},{3,2},{4,5},{5,4},{6,7},{7,6},{8,9},{9,8},{10,11... | collective-permute-start | bytes 1572872 | tf_op jit(solution)/shard_map/ppermute | solution.py:36
  7.4 10.3 %collective-permute-start.3 = (bf16[2,2,128,256]{3,2,1,0:T(8,128)(2,1)S(1)}, bf16[2,2,128,256]{3,2,1,0:T(8,128)(2,1)S(1)}, u32[]{:S(2)}, u32[]{:S(2)}) collective-permute-start(bf16[2,2,128,256]{3,2,1,0:T(8,128)(2,1)S(1)} %both_rows.2.refs_1_), channel_id=1, source_target_pairs={{0,4},{4,8},{8,12},{12,0},{1,5},{5,9},{9,13},{13,1},{2,6},{6,10},{... | collective-permute-start | bytes 786440 | tf_op jit(solution)/shard_map/ppermute | solution.py:27
  11.9 2.1 %collective-permute-start.2 = (bf16[1,2,128,256]{3,2,1,0:T(8,128)(2,1)S(1)}, bf16[1,2,128,256]{3,2,1,0:T(8,128)(2,1)S(1)}, u32[]{:S(2)}, u32[]{:S(2)}) collective-permute-start(bf16[1,2,128,256]{3,2,1,0:T(8,128)(2,1)S(1)} %other_side.1), channel_id=1, source_target_pairs={{0,1},{1,0},{2,3},{3,2},{4,5},{5,4},{6,7},{7,6},{8,9},{9,8},{10,11... | collective-permute-start | bytes 393224 | tf_op jit(solution)/shard_map/ppermute | solution.py:36
  12.2 9.2 %collective-permute-start.6 = (bf16[2,2,128,256]{3,2,1,0:T(8,128)(2,1)S(1)}, bf16[2,2,128,256]{3,2,1,0:T(8,128)(2,1)S(1)}, u32[]{:S(2)}, u32[]{:S(2)}) collective-permute-start(bf16[2,2,128,256]{3,2,1,0:T(8,128)(2,1)S(1)} %head_parts.7), channel_id=1, source_target_pairs={{0,2},{2,0},{1,3},{3,1},{4,6},{6,4},{5,7},{7,5},{8,10},{10,8},{9,1... | collective-permute-start | bytes 786440 | tf_op jit(solution)/shard_map/ppermute | solution.py:32
  14.2 11.0 %collective-permute-start.4 = (bf16[2,2,128,256]{3,2,1,0:T(8,128)(2,1)S(1)}, bf16[2,2,128,256]{3,2,1,0:T(8,128)(2,1)S(1)}, u32[]{:S(2)}, u32[]{:S(2)}) collective-permute-start(bf16[2,2,128,256]{3,2,1,0:T(8,128)(2,1)S(1)} %both_rows.3.refs_2_.refs_0_), channel_id=1, source_target_pairs={{0,4},{4,8},{8,12},{12,0},{1,5},{5,9},{9,13},{13,1},{2,6},{6,10},{... | collective-permute-start | bytes 786440 | tf_op jit(solution)/shard_map/ppermute | solution.py:27
  17.9 10.8 %collective-permute-start.11 = (bf16[2,2,128,256]{3,2,1,0:T(8,128)(2,1)S(1)}, bf16[2,2,128,256]{3,2,1,0:T(8,128)(2,1)S(1)}, u32[]{:S(2)}, u32[]{:S(2)}) collective-permute-start(bf16[2,2,128,256]{3,2,1,0:T(8,128)(2,1)S(1)} %head_parts.9), channel_id=1, source_target_pairs={{0,2},{2,0},{1,3},{3,1},{4,6},{6,4},{5,7},{7,5},{8,10},{10,8},{9,1... | collective-permute-start | bytes 786440 | tf_op jit(solution)/shard_map/ppermute | solution.py:32
  19.7 14.1 %collective-permute-start.12 = (bf16[2,2,128,256]{3,2,1,0:T(8,128)(2,1)S(1)}, bf16[2,2,128,256]{3,2,1,0:T(8,128)(2,1)S(1)}, u32[]{:S(2)}, u32[]{:S(2)}) collective-permute-start(bf16[2,2,128,256]{3,2,1,0:T(8,128)(2,1)S(1)} %head_parts.8.refs_1_), channel_id=1, source_target_pairs={{0,4},{4,8},{8,12},{12,0},{1,5},{5,9},{9,13},{13,1},{2,6},{6,10},{... | collective-permute-start | bytes 786440 | tf_op jit(solution)/shard_map/ppermute | solution.py:27
  21.5 12.3 %collective-permute-start.14 = (bf16[2,2,128,256]{3,2,1,0:T(8,128)(2,1)S(1)}, bf16[2,2,128,256]{3,2,1,0:T(8,128)(2,1)S(1)}, u32[]{:S(2)}, u32[]{:S(2)}) collective-permute-start(bf16[2,2,128,256]{3,2,1,0:T(8,128)(2,1)S(1)} %head_parts.11), channel_id=1, source_target_pairs={{0,2},{2,0},{1,3},{3,1},{4,6},{6,4},{5,7},{7,5},{8,10},{10,8},{9,1... | collective-permute-start | bytes 786440 | tf_op jit(solution)/shard_map/ppermute | solution.py:32
  28.8 7.0 %collective-permute-start.13 = (bf16[2,2,128,256]{3,2,1,0:T(8,128)(2,1)S(1)}, bf16[2,2,128,256]{3,2,1,0:T(8,128)(2,1)S(1)}, u32[]{:S(2)}, u32[]{:S(2)}) collective-permute-start(bf16[2,2,128,256]{3,2,1,0:T(8,128)(2,1)S(1)} %relayed.3), channel_id=1, source_target_pairs={{0,4},{4,8},{8,12},{1,5},{5,9},{9,13},{2,6},{6,10},{10,14},{3,7},{... | collective-permute-start | bytes 786440 | tf_op jit(solution)/shard_map/ppermute | solution.py:27
  30.8 16.8 %collective-permute-start.8 = (bf16[2,2,2,128,256]{4,3,2,1,0:T(8,128)(2,1)S(1)}, bf16[2,2,2,128,256]{4,3,2,1,0:T(8,128)(2,1)S(1)}, u32[]{:S(2)}, u32[]{:S(2)}) collective-permute-start(bf16[2,2,2,128,256]{4,3,2,1,0:T(8,128)(2,1)S(1)} %get-tuple-element.33), channel_id=1, source_target_pairs={{4,0},{8,4},{12,8},{5,1},{9,5},{13,9},{6,2},{10,6},{14,10},{7,3},{... | collective-permute-start | bytes 1572872 | tf_op jit(solution)/shard_map/ppermute | solution.py:27
  32.1 7.2 %collective-permute-start.7 = (bf16[2,128,256]{2,1,0:T(8,128)(2,1)S(1)}, bf16[2,128,256]{2,1,0:T(8,128)(2,1)S(1)}, u32[]{:S(2)}, u32[]{:S(2)}) collective-permute-start(bf16[2,128,256]{2,1,0:T(8,128)(2,1)S(1)} %get-tuple-element.31), channel_id=1, source_target_pairs={{0,2},{2,0},{1,3},{3,1},{4,6},{6,4},{5,7},{7,5},{8,10},{10,8},{9,1... | collective-permute-start | bytes 393224 | tf_op jit(solution)/shard_map/ppermute | solution.py:32
  39.4 13.3 %collective-permute-start.17 = (bf16[2,2,128,256]{3,2,1,0:T(8,128)(2,1)S(1)}, bf16[2,2,128,256]{3,2,1,0:T(8,128)(2,1)S(1)}, u32[]{:S(2)}, u32[]{:S(2)}) collective-permute-start(bf16[2,2,128,256]{3,2,1,0:T(8,128)(2,1)S(1)} %relayed.5), channel_id=1, source_target_pairs={{4,0},{8,4},{12,8},{5,1},{9,5},{13,9},{6,2},{10,6},{14,10},{7,3},{... | collective-permute-start | bytes 786440 | tf_op jit(solution)/shard_map/ppermute | solution.py:27
  40.7 9.9 %collective-permute-start.15 = (bf16[2,128,256]{2,1,0:T(8,128)(2,1)S(1)}, bf16[2,128,256]{2,1,0:T(8,128)(2,1)S(1)}, u32[]{:S(2)}, u32[]{:S(2)}) collective-permute-start(bf16[2,128,256]{2,1,0:T(8,128)(2,1)S(1)} %get-tuple-element.40), channel_id=1, source_target_pairs={{0,2},{2,0},{1,3},{3,1},{4,6},{6,4},{5,7},{7,5},{8,10},{10,8},{9,1... | collective-permute-start | bytes 393224 | tf_op jit(solution)/shard_map/ppermute | solution.py:32
  47.6 8.6 %collective-permute-start.9 = (bf16[2,2,128,256]{3,2,1,0:T(8,128)(2,1)S(1)}, bf16[2,2,128,256]{3,2,1,0:T(8,128)(2,1)S(1)}, u32[]{:S(2)}, u32[]{:S(2)}) collective-permute-start(bf16[2,2,128,256]{3,2,1,0:T(8,128)(2,1)S(1)} %get-tuple-element.35), channel_id=1, source_target_pairs={{0,2},{2,0},{1,3},{3,1},{4,6},{6,4},{5,7},{7,5},{8,10},{10,8},{9,1... | collective-permute-start | bytes 786440 | tf_op jit(solution)/shard_map/ppermute | solution.py:32
  49.2 8.3 %collective-permute-start.16 = (bf16[2,2,128,256]{3,2,1,0:T(8,128)(2,1)S(1)}, bf16[2,2,128,256]{3,2,1,0:T(8,128)(2,1)S(1)}, u32[]{:S(2)}, u32[]{:S(2)}) collective-permute-start(bf16[2,2,128,256]{3,2,1,0:T(8,128)(2,1)S(1)} %relayed.4), channel_id=1, source_target_pairs={{4,0},{8,4},{12,8},{5,1},{9,5},{13,9},{6,2},{10,6},{14,10},{7,3},{... | collective-permute-start | bytes 786440 | tf_op jit(solution)/shard_map/ppermute | solution.py:27
  52.7 6.9 %collective-permute-start.18 = (bf16[2,2,128,256]{3,2,1,0:T(8,128)(2,1)S(1)}, bf16[2,2,128,256]{3,2,1,0:T(8,128)(2,1)S(1)}, u32[]{:S(2)}, u32[]{:S(2)}) collective-permute-start(bf16[2,2,128,256]{3,2,1,0:T(8,128)(2,1)S(1)} %summed.5), channel_id=1, source_target_pairs={{0,2},{2,0},{1,3},{3,1},{4,6},{6,4},{5,7},{7,5},{8,10},{10,8},{9,1... | collective-permute-start | bytes 786440 | tf_op jit(solution)/shard_map/ppermute | solution.py:32
  56.3 3.5 %collective-permute-start.19 = (bf16[3,2,128,256]{3,2,1,0:T(8,128)(2,1)S(1)}, bf16[3,2,128,256]{3,2,1,0:T(8,128)(2,1)S(1)}, u32[]{:S(2)}, u32[]{:S(2)}) collective-permute-start(bf16[3,2,128,256]{3,2,1,0:T(8,128)(2,1)S(1)} %get-tuple-element.45), channel_id=1, source_target_pairs={{0,1},{1,0},{2,3},{3,2},{4,5},{5,4},{6,7},{7,6},{8,9},{9,8},{10,11... | collective-permute-start | bytes 1179656 | tf_op jit(solution)/shard_map/ppermute | solution.py:36
  59.7 1.8 %collective-permute-start.20 = (bf16[3,2,128,256]{3,2,1,0:T(8,128)(2,1)S(1)}, bf16[3,2,128,256]{3,2,1,0:T(8,128)(2,1)S(1)}, u32[]{:S(2)}, u32[]{:S(2)}) collective-permute-start(bf16[3,2,128,256]{3,2,1,0:T(8,128)(2,1)S(1)} %get-tuple-element.46), channel_id=1, source_target_pairs={{0,1},{1,0},{2,3},{3,2},{4,5},{5,4},{6,7},{7,6},{8,9},{9,8},{10,11... | collective-permute-start | bytes 1179656 | tf_op jit(solution)/shard_map/ppermute | solution.py:36

commit v18 on v17

--- a/solution.py
+++ b/solution.py
@@ -30,6 +30,12 @@
 def round_sub(value, by):
     peers = lax.axis_size("sub")
     return lax.ppermute(value, "sub", [(i, (i + by) % peers) for i in range(peers)])
+
+
+def cross_sub(value, by):
+    peers = lax.axis_size("sub")
+    pairs = [(2 * s + p, 2 * ((s + by) % peers) + 1 - p) for p in range(2) for s in range(peers)]
+    return lax.ppermute(value, ("sub", "pair"), pairs)
 
 
 def swapped(value):
@@ -101,7 +107,7 @@
     return [(parts[2 * i], parts[2 * i + 1]) for i in range(len(groups))]
 
 
-def first_keys(arrays, low, high):
+def first_keys(arrays, low, high, after):
     rows, width = arrays[0].shape
     half = width // 2
     peers = lax.axis_size("sub")
@@ -109,7 +115,7 @@
     cut = high - low
 
     def kernel(*refs):
-        ins, far, (send, keep), sems = refs[:2], refs[2:1 + peers], refs[1 + peers:-1], refs[-1]
+        ins, far, (send, keep), sems = refs[:2], refs[2 + len(after):1 + peers + len(after)], refs[-3:-1], refs[-1]
         p, s = lax.axis_index("pair"), lax.axis_index("sub")
         moves = []
         for i, ref in enumerate(ins):
@@ -127,12 +133,12 @@
     parts = pl.pallas_call(
         kernel,
         out_shape=outs,
-        in_specs=[spec] * 2,
+        in_specs=[spec] * (2 + len(after)),
         out_specs=[spec] * len(outs),
         scratch_shapes=[pltpu.SemaphoreType.DMA((4 * peers,))],
         name="first_keys",
         compiler_params=pltpu.CompilerParams(vmem_limit_bytes=8 * MIB),
-    )(*[pltpu.with_memory_space_constraint(array, pltpu.HBM) for array in arrays])
+    )(*[pltpu.with_memory_space_constraint(array, pltpu.HBM) for array in arrays], *after)
     return list(parts[:-2]), parts[-2], parts[-1]
 
 
@@ -333,25 +339,96 @@
     return call(kernel, dq + dkv, outs, [], "rows_for_pair", whole=True)
 
 
-def laid_out(kept, paired, spans):
-    _, peers, rows, _ = kept[0].shape
+def last_sums(own, later, after):
+    _, _, peers, rows, cut = own.shape
+
+    def kernel(own_ref, *refs):
+        later_refs, outs = refs[:peers - 1], refs[len(later) + len(after):]
+        p, s = lax.axis_index("pair"), lax.axis_index("sub")
+        for by in range(1, peers):
+            at = lax.rem(s + by, peers)
+            for out, row in ((outs[2 * by - 2], p), (outs[2 * by - 1], 1 - p)):
+                for which in range(2):
+                    total = own_ref[which, row, at] + later_refs[by - 1][which, row].astype(WIDE)
+                    out[which] = total.astype(LOW)
+
+    return call(kernel, [own] + later + after, [shape(2, rows, cut)] * (2 * peers - 2), [], "last_sums", whole=True)
+
+
+def last_rows(own, later):
+    _, _, peers, rows, cut = own.shape
+
+    def kernel(own_ref, later_ref, send_k, send_v, keep):
+        p, s = lax.axis_index("pair"), lax.axis_index("sub")
+        for which, send in enumerate((send_k, send_v)):
+            for out, at, row in ((send, 0, 1 - p), (keep, which, p)):
+                out[at] = (own_ref[which, row, s] + later_ref[which, row].astype(WIDE)).astype(LOW)
+
+    outs = [shape(1, rows, cut), shape(1, rows, cut), shape(2, rows, cut)]
+    return call(kernel, [own, later], outs, [], "last_rows", whole=True)
+
+
+def query_rows(dq):
+    peers = len(dq)
+    _, rows, cut = dq[0].shape
+
+    def kernel(*refs):
+        p = lax.axis_index("pair")
+        for out, row in zip(refs[peers:], (1 - p, p)):
+            for by in range(peers):
+                out[by] = refs[by][row]
+
+    return call(kernel, dq, [shape(peers, rows, cut)] * 2, [], "query_rows", whole=True)
+
+
+def stacked(parts):
+    _, rows, cut = parts[0].shape
+
+    def kernel(*refs):
+        at = 0
+        for ref in refs[:-1]:
+            for i in range(ref.shape[0]):
+                refs[-1][at + i] = ref[i]
+            at += ref.shape[0]
+
+    outs = [shape(sum(part.shape[0] for part in parts), rows, cut)]
+    return call(kernel, parts, outs, [], "stacked", whole=True)[0]
+
+
+def laid_out(whole, last, straight, crossed, spans):
+    peers = lax.axis_size("sub")
+    rows = last[0].shape[1]
     part = spans[-1][1]
     half = part * peers
-    count = len(spans)
-
-    def kernel(*refs):
-        keep, rec, outs, sems = refs[:count], refs[count:2 * count], refs[2 * count:-1], refs[-1]
-        p = lax.axis_index("pair")
+    ins = [array for both in whole for array in both] + list(last) + straight + crossed
+
+    def kernel(*refs):
+        outs, sems = refs[len(ins):-1], refs[-1]
+        p, s = lax.axis_index("pair"), lax.axis_index("sub")
         moves = []
-        for mine, theirs, (low, high) in zip(keep, rec, spans):
-            for source, side in ((mine, p), (theirs, 1 - p)):
+
+        def place(source, which, side, at, span):
+            columns = pl.ds(pl.multiple_of(side * half + at * part + span[0], HD), span[1] - span[0])
+            moves.append((source, outs[which].at[:, columns]))
+
+        for i, side in enumerate((p, 1 - p)):
+            for chunk in range(len(whole)):
                 for at in range(peers):
-                    columns = pl.ds(pl.multiple_of(side * half + at * part + low, HD), high - low)
-                    moves += [(source.at[which, at], out.at[:, columns]) for which, out in enumerate(outs)]
+                    for which in range(3):
+                        place(refs[2 * chunk + i].at[which, at], which, side, at, spans[chunk])
+            ours = refs[2 * len(whole) + i]
+            far = refs[2 * len(whole) + 2 + i * (peers - 1):]
+            for by in range(peers):
+                at = lax.rem(s - by + peers, peers)
+                place(ours.at[2 + by], 0, side, at, spans[-1])
+                for which in range(2):
+                    source = ours.at[which] if by == 0 else far[by - 1].at[which]
+                    place(source, 1 + which, side, at, spans[-1])
         run_moves(moves, sems)
 
     outs = [shape(rows, 2 * half)] * 3
-    return call(kernel, kept + paired, outs, [pltpu.SemaphoreType.DMA((6 * count * peers,))], "laid_out")
+    scratch = [pltpu.SemaphoreType.DMA((6 * len(spans) * peers,))]
+    return call(kernel, ins, outs, scratch, "laid_out")
 
 
 def allowed_bias(session, rows):
@@ -381,19 +458,16 @@
         spans.append((at, at + heads * HD))
         at += heads * HD
     bias = allowed_bias(session, queries.shape[0])
-    kv_far, near_send, near_keep = first_keys([keys, values], *spans[0])
+    kv_far, near_send, near_keep = first_keys([keys, values], *spans[0], [])
     kv_far = [round_sub(value, by) for by, value in zip(others, kv_far)]
-    rest = [([queries, out_grad], *spans[0])] + [([keys, values, queries, out_grad], *span) for span in spans[1:]]
+    rest = [([queries, out_grad], *spans[0])] + [([keys, values], *span) for span in spans[1:]]
     rest = first_parts(rest, [near_keep])
     near_theirs = swapped(near_send)
-    kv_parts = [None]
-    qg_parts = [(rest[0][1], swapped(rest[0][0]), 0)]
-    for send, own in rest[1:]:
-        paired = swapped(send)
-        kv_parts.append((own, paired, 0))
-        qg_parts.append((own, paired, 2))
+    paired = [(own, swapped(send), 0) for send, own in rest]
+    qg_parts, kv_parts = paired[:1], [None] + paired[1:]
+    later_reads = [first_keys([queries, out_grad], *span, [rest[0][1]]) for span in spans[1:]]
     count = len(spans)
-    kv_sends, qg_sends, kv, qg, kv_own, own_earlier = [], [], [], [], [], []
+    kv_sends, qg_own, kv, qg, kv_own, own_earlier = [], [], [], [], [], []
     for index in range(count):
         if index:
             kv_sends.append(head_parts(*kv_parts[index], others, kv[index - 1] + own_earlier[index - 1:index]))
@@ -404,35 +478,46 @@
             kv_own.append(both_rows([near_keep], near_theirs.reshape(1, *near_theirs.shape)))
             kv.append(both_rows(kv_far, swapped(other_side(kv_far))))
         own_earlier.append(along_blocks(kv_own[index][0], 1, True))
-        qg_sends.append(head_parts(*qg_parts[index], others, qg[index - 1] if index else []))
-        qg.append([round_sub(value, by) for by, value in zip(others, qg_sends[index])])
-    kept, paired, first_dq, back, release = [], [], [], [], []
+        if index:
+            far, send, keep = later_reads[index - 1]
+            far = [round_sub(relayed(value, qg[index - 1]), by) for by, value in zip(others, far)]
+            qg.append(both_rows(far, swapped(other_side(far))))
+            qg_own.append(both_rows([keep], swapped(send).reshape(1, *send.shape)))
+        else:
+            sends = head_parts(*qg_parts[index], others, [])
+            qg.append([round_sub(value, by) for by, value in zip(others, sends)])
+            qg_own.append(head_parts(*qg_parts[index], [0], []))
+    done, first_dq = [], []
     for index, (low, high) in enumerate(spans):
         last = index == count - 1
         forward = [relayed(value, first_dq) if index else value for value in kv[index]]
         earlier = [own_earlier[index]] + [along_blocks(value, 1, not last) for value in forward]
-        qg_all = head_parts(*qg_parts[index], [0], []) + qg[index]
-        kv_all = kv_own[index] + kv[index]
-        heads = (high - low) // HD
-        if last:
-            grads, dq, early = attention_grads(bias, kv_all, earlier, qg_all, True, 0, heads, [])
-            dq = [dq[0]] + [round_sub(dq[by], by) for by in others]
+        qg_all = qg_own[index] + qg[index]
+        after = [] if last else own_earlier[index + 1:index + 2] + [later_reads[index][2]]
+        done.append(attention_grads(bias, kv_own[index] + kv[index], earlier, qg_all, last, 0, (high - low) // HD, after))
+        first_dq = done[-1][1][:1]
+    whole, back, release = [], [], []
+    for index, (grads, dq, early) in enumerate(done):
+        near_dq = dq[:1]
+        dq = near_dq + [round_sub(dq[by], by) for by in others]
+        if index == count - 1:
             later = [along_blocks(relayed(value, back), -1, False) for value in early[1:]]
-            dkv = summed([grads], later, others, dq[1:])
-            near = along_blocks(relayed(early[0], release), -1, False)
-            dkv = summed([grads], [near], [0], []) + [round_sub(value, by) for by, value in zip(others, dkv)]
+            sums = last_sums(grads, later, dq[1:])
+            straight = [round_sub(sums[2 * by - 2], by) for by in others]
+            crossed = [cross_sub(sums[2 * by - 1], by) for by in others]
+            near = along_blocks(relayed(early[0], sums[:1]), -1, False)
+            send_k, send_v, keep = last_rows(grads, near)
+            send, keep_dq = query_rows(dq)
+            theirs = [swapped(send_k), swapped(send_v), swapped(send)]
+            ours = (stacked([keep, keep_dq]), stacked(theirs))
         else:
-            grads, dq, early = attention_grads(bias, kv_all, earlier, qg_all, False, 0, heads, [])
-            first_dq = dq[:1]
-            dq = [dq[0]] + [round_sub(dq[by], by) for by in others]
             back = dq[1:]
-            dkv = summed([grads], [along_blocks(early[0], -1, False)], [0] + others, dq[1:])
+            dkv = summed([grads], [along_blocks(early[0], -1, False)], [0] + others, dq[1:] + first_dq)
             release = dkv[:1]
             dkv = [dkv[0]] + [round_sub(dkv[by], by) for by in others]
-        send, keep = rows_for_pair(dq, dkv)
-        kept.append(keep)
-        paired.append(swapped(send))
-    return tuple(laid_out(kept, paired, spans))
+            send, keep = rows_for_pair(dq, dkv)
+            whole.append((keep, swapped(send)))
+    return tuple(laid_out(whole, ours, straight, crossed, spans))
 
 
 def solution(mesh):

time: 63.2 us -> 73 us (1.16)
  waiting for transfers between devices: 23.7 us -> 31 us
  starting transfers between devices: 24.2 us -> 25.5 us
  Pallas kernels: 13.2 us -> 14.2 us
    ppermute x8, waiting for transfers between devices: 7.71 us -> 12.1 us  [round_sub(): lax.ppermute(value, 'sub', [(i, (i + by) % peers) for i in range(peers)])]
    ppermute x7, waiting for transfers between devices: 14.3 us -> 17.9 us  [along_blocks(): return lax.ppermute(value, 'blk', pairs)]
    ppermute x8, starting transfers between devices: 13.5 us -> 10.6 us  [round_sub(): lax.ppermute(value, 'sub', [(i, (i + by) % peers) for i in range(peers)])]
    ppermute x7, starting transfers between devices: 9.36 us -> 11.8 us  [along_blocks(): return lax.ppermute(value, 'blk', pairs)]
    ppermute x0 -> x1, starting transfers between devices: none -> 1.19 us  [cross_sub(): return lax.ppermute(value, ('sub', 'pair'), pairs)]
    pallas_call x1 -> x2, Pallas kernels: 1.15 us -> 2.31 us  [first_keys(): pl.pallas_call(kernel, out_shape=outs, in_specs=[spec] * (2 + len(after))...]
    ppermute x6 -> x10, starting transfers between devices: 1.31 us -> 2.01 us  [swapped(): return lax.ppermute(value, 'pair', [(0, 1), (1, 0)])]
    ppermute x6 -> x10, waiting for transfers between devices: 1.71 us -> 1.03 us  [swapped(): return lax.ppermute(value, 'pair', [(0, 1), (1, 0)])]
  transfers between devices with their start and end apart: 21 -> 26, of which waited for: 11 -> 13; matrix products, arithmetic and copies ran while one was open for 1% -> 1% of each run, Pallas kernels for 17% -> 16%
where the time goes in v18:
time: 73 us; the launch traced here: 72.6 us
  waiting for transfers between devices  31 us (42%)
  starting transfers between devices  25.5 us (35%)
  Pallas kernels  14.2 us (19%)
  between operations  1 us (1%)
  other arithmetic  0.79 us (1%)
    ppermute x7, waiting for transfers between devices, along_blocks(): return lax.ppermute(value, 'blk', pairs)  17.9 us
    ppermute x8, waiting for transfers between devices, round_sub(): lax.ppermute(value, 'sub', [(i, (i + by) % peers) for i in range(peers)])  12.1 us
    ppermute x7, starting transfers between devices, along_blocks(): return lax.ppermute(value, 'blk', pairs)  11.8 us
    ppermute x8, starting transfers between devices, round_sub(): lax.ppermute(value, 'sub', [(i, (i + by) % peers) for i in range(peers)])  10.6 us
    pallas_call x24, Pallas kernels, call(): pl.pallas_call(kernel, out_shape=outs, in_specs=[spec] * len(ins), out_sp...  10.5 us
    pallas_call x2, Pallas kernels, first_keys(): pl.pallas_call(kernel, out_shape=outs, in_specs=[spec] * (2 + len(after))...  2.31 us
    ppermute x10, starting transfers between devices, swapped(): return lax.ppermute(value, 'pair', [(0, 1), (1, 0)])  2.01 us
  transfers between devices with their start and end apart: 26, of which 13 were waited for; matrix products, arithmetic and copies ran while one was open for 1% of the time, Pallas kernels for 16%

profile of v18, /device:TPU:0, one launch (start us, length us, event | category | flops | bytes accessed | tf_op | source)
XLA Modules:
  0.0 72.6 jit_solution(6350888433669870661)
XLA Ops:
  0.6 1.2 %first_keys.2 = (bf16[2,2,128,256]{3,2,1,0:T(8,128)(2,1)S(1)}, bf16[2,128,256]{2,1,0:T(8,128)(2,1)S(1)}, bf16[2,128,256]{2,1,0:T(8,128)(2,1)S(1)}) custom-call(bf16[128,2048]{1,0:T(8,128)(2,1)} %refs_2_.1, bf16[128,2048]{1,0:T(8,128)(2,1)} %refs_3_.1), custom_call_target="tpu_custom_call" | custom-call | tf_op jit(solution)/shard_map/first_keys/pallas_call | solution.py:133
  1.8 0.5 collective-permute-start
  2.3 2.6 %collective-permute-start.1 = (bf16[2,2,128,256]{3,2,1,0:T(8,128)(2,1)S(1)}, bf16[2,2,128,256]{3,2,1,0:T(8,128)(2,1)S(1)}, u32[]{:S(2)}, u32[]{:S(2)}) collective-permute-start(bf16[2,2,128,256]{3,2,1,0:T(8,128)(2,1)S(1)} %get-tuple-element.35), channel_id=1, source_target_pairs={{0,2},{2,0},{1,3},{3,1},{4,6},{6,4},{5,7},{7,5},{8,10},{10,8},{9,1... | collective-permute-start | bytes 786440 | tf_op jit(solution)/shard_map/ppermute | solution.py:32
  4.9 1.4 %first_parts.1 = (bf16[2,2,128,256]{3,2,1,0:T(8,128)(2,1)S(1)}, bf16[2,2,128,256]{3,2,1,0:T(8,128)(2,1)S(1)}, bf16[2,2,128,256]{3,2,1,0:T(8,128)(2,1)S(1)}, bf16[2,2,128,256]{3,2,1,0:T(8,128)(2,1)S(1)}) custom-call(bf16[128,2048]{1,0:T(8,128)(2,1)} %refs_0_.5, bf16[128,2048]{1,0:T(8,128)(2,1)} %refs_1_.5, bf16[128,2048]{1,0:T(8,128)(2,1)} %refs_2_.1, ...), custom_call_target="tpu_custom_call" | custom-call | tf_op jit(solution)/shard_map/first_parts/pallas_call | solution.py:98
  6.3 0.2 collective-permute-start.5
  6.5 0.3 collective-permute-start.7
  7.0 0.2 both_rows.4.refs_1_
  7.2 1.6 %collective-permute-start.3 = (bf16[2,2,128,256]{3,2,1,0:T(8,128)(2,1)S(1)}, bf16[2,2,128,256]{3,2,1,0:T(8,128)(2,1)S(1)}, u32[]{:S(2)}, u32[]{:S(2)}) collective-permute-start(bf16[2,2,128,256]{3,2,1,0:T(8,128)(2,1)S(1)} %both_rows.4.refs_1_), channel_id=1, source_target_pairs={{0,4},{4,8},{8,12},{12,0},{1,5},{5,9},{9,13},{13,1},{2,6},{6,10},{... | collective-permute-start | bytes 786440 | tf_op jit(solution)/shard_map/ppermute | solution.py:27
  8.8 3.0 %collective-permute-done.1.refs_0_ = bf16[2,2,128,256]{3,2,1,0:T(8,128)(2,1)S(1)} collective-permute-done((bf16[2,2,128,256]{3,2,1,0:T(8,128)(2,1)S(1)}, bf16[2,2,128,256]{3,2,1,0:T(8,128)(2,1)S(1)}, u32[]{:S(2)}, u32[]{:S(2)}) %collective-permute-start.1) | collective-permute-done | bytes 262176 | tf_op jit(solution)/shard_map/ppermute | solution.py:32
  12.0 0.2 head_parts.5
  12.2 1.8 %collective-permute-start.6 = (bf16[2,2,128,256]{3,2,1,0:T(8,128)(2,1)S(1)}, bf16[2,2,128,256]{3,2,1,0:T(8,128)(2,1)S(1)}, u32[]{:S(2)}, u32[]{:S(2)}) collective-permute-start(bf16[2,2,128,256]{3,2,1,0:T(8,128)(2,1)S(1)} %head_parts.5), channel_id=1, source_target_pairs={{0,2},{2,0},{1,3},{3,1},{4,6},{6,4},{5,7},{7,5},{8,10},{10,8},{9,1... | collective-permute-start | bytes 786440 | tf_op jit(solution)/shard_map/ppermute | solution.py:32
  14.0 0.2 both_rows.5.refs_2_.refs_0_
  14.2 1.6 %collective-permute-start.4 = (bf16[2,2,128,256]{3,2,1,0:T(8,128)(2,1)S(1)}, bf16[2,2,128,256]{3,2,1,0:T(8,128)(2,1)S(1)}, u32[]{:S(2)}, u32[]{:S(2)}) collective-permute-start(bf16[2,2,128,256]{3,2,1,0:T(8,128)(2,1)S(1)} %both_rows.5.refs_2_.refs_0_), channel_id=1, source_target_pairs={{0,4},{4,8},{8,12},{12,0},{1,5},{5,9},{9,13},{13,1},{2,6},{6,10},{... | collective-permute-start | bytes 786440 | tf_op jit(solution)/shard_map/ppermute | solution.py:27
  15.8 1.6 %collective-permute-done.3.refs_0_.refs_3_.refs_1_ = bf16[2,2,128,256]{3,2,1,0:T(8,128)(2,1)S(1)} collective-permute-done((bf16[2,2,128,256]{3,2,1,0:T(8,128)(2,1)S(1)}, bf16[2,2,128,256]{3,2,1,0:T(8,128)(2,1)S(1)}, u32[]{:S(2)}, u32[]{:S(2)}) %collective-permute-start.3) | collective-permute-done | bytes 262176 | tf_op jit(solution)/shard_map/ppermute | solution.py:27
  17.5 0.2 head_parts.6.refs_1_
  17.7 0.7 and_select_fusion
  18.4 1.2 %first_keys.3 = (bf16[2,2,128,256]{3,2,1,0:T(8,128)(2,1)S(1)}, bf16[2,128,256]{2,1,0:T(8,128)(2,1)S(1)}, bf16[2,128,256]{2,1,0:T(8,128)(2,1)S(1)}) custom-call(bf16[128,2048]{1,0:T(8,128)(2,1)} %refs_0_.5, bf16[128,2048]{1,0:T(8,128)(2,1)} %refs_1_.5, bf16[2,2,128,256]{3,2,1,0:T(8,128)(2,1)S(1)} %get-tuple-element.36.own_ref.refs_2_), custom_call_target="tpu_custom_call" | custom-call | tf_op jit(solution)/shard_map/first_keys/pallas_call | solution.py:133
  19.6 0.1 pad_maximum_fusion.refs_0_
  19.7 0.2 head_parts.4.refs_5_
  19.9 0.2 head_parts.7
  20.1 1.0 %collective-permute-start.11 = (bf16[2,2,128,256]{3,2,1,0:T(8,128)(2,1)S(1)}, bf16[2,2,128,256]{3,2,1,0:T(8,128)(2,1)S(1)}, u32[]{:S(2)}, u32[]{:S(2)}) collective-permute-start(bf16[2,2,128,256]{3,2,1,0:T(8,128)(2,1)S(1)} %head_parts.7), channel_id=1, source_target_pairs={{0,2},{2,0},{1,3},{3,1},{4,6},{6,4},{5,7},{7,5},{8,10},{10,8},{9,1... | collective-permute-start | bytes 786440 | tf_op jit(solution)/shard_map/ppermute | solution.py:32
  21.1 4.1 %collective-permute-done.4.refs_4_ = bf16[2,2,128,256]{3,2,1,0:T(8,128)(2,1)S(1)} collective-permute-done((bf16[2,2,128,256]{3,2,1,0:T(8,128)(2,1)S(1)}, bf16[2,2,128,256]{3,2,1,0:T(8,128)(2,1)S(1)}, u32[]{:S(2)}, u32[]{:S(2)}) %collective-permute-start.4) | collective-permute-done | bytes 262176 | tf_op jit(solution)/shard_map/ppermute | solution.py:27
  25.2 4.9 %collective-permute-done.8.refs_7_.refs_3_ = bf16[2,2,128,256]{3,2,1,0:T(8,128)(2,1)S(1)} collective-permute-done((bf16[2,2,128,256]{3,2,1,0:T(8,128)(2,1)S(1)}, bf16[2,2,128,256]{3,2,1,0:T(8,128)(2,1)S(1)}, u32[]{:S(2)}, u32[]{:S(2)}) %collective-permute-start.8) | collective-permute-done | bytes 262176 | tf_op jit(solution)/shard_map/ppermute | solution.py:27
  30.1 3.5 %attention_grads.2 = (f32[2,2,2,128,256]{4,3,2,1,0:T(8,128)S(1)}, bf16[2,128,256]{2,1,0:T(8,128)(2,1)S(1)}, bf16[2,128,256]{2,1,0:T(8,128)(2,1)S(1)}, bf16[2,2,2,128,256]{4,3,2,1,0:T(8,128)(2,1)S(1)}) custom-call(f32[2,768,256]{2,1,0:T(8,128)S(1)} %pad_maximum_fusion.refs_0_, bf16[2,2,128,256]{3,2,1,0:T(8,128)(2,1)S(1)} %both_rows.4.refs_1_, ...), custom_call_target="tpu_custom_call" | custom-call | flops 1006632960 | bytes 5373952 | tf_op jit(solution)/shard_map/attention_grads/pallas_call | solution.py:57
  33.7 1.3 %collective-permute-start.10 = (bf16[2,2,2,128,256]{4,3,2,1,0:T(8,128)(2,1)S(1)}, bf16[2,2,2,128,256]{4,3,2,1,0:T(8,128)(2,1)S(1)}, u32[]{:S(2)}, u32[]{:S(2)}) collective-permute-start(bf16[2,2,2,128,256]{4,3,2,1,0:T(8,128)(2,1)S(1)} %get-tuple-element.44), channel_id=1, source_target_pairs={{4,0},{8,4},{12,8},{5,1},{9,5},{13,9},{6,2},{10,6},{14,10},{7,3},{... | collective-permute-start | bytes 1572872 | tf_op jit(solution)/shard_map/ppermute | solution.py:27
  35.0 1.1 %collective-permute-start.14 = (bf16[2,2,128,256]{3,2,1,0:T(8,128)(2,1)S(1)}, bf16[2,2,128,256]{3,2,1,0:T(8,128)(2,1)S(1)}, u32[]{:S(2)}, u32[]{:S(2)}) collective-permute-start(bf16[2,2,128,256]{3,2,1,0:T(8,128)(2,1)S(1)} %relayed.5), channel_id=1, source_target_pairs={{0,2},{2,0},{1,3},{3,1},{4,6},{6,4},{5,7},{7,5},{8,10},{10,8},{9,1... | collective-permute-start | bytes 786440 | tf_op jit(solution)/shard_map/ppermute | solution.py:32
  36.1 4.6 %collective-permute-start.12 = (bf16[2,2,128,256]{3,2,1,0:T(8,128)(2,1)S(1)}, bf16[2,2,128,256]{3,2,1,0:T(8,128)(2,1)S(1)}, u32[]{:S(2)}, u32[]{:S(2)}) collective-permute-start(bf16[2,2,128,256]{3,2,1,0:T(8,128)(2,1)S(1)} %relayed.4), channel_id=1, source_target_pairs={{0,4},{4,8},{8,12},{1,5},{5,9},{9,13},{2,6},{6,10},{10,14},{3,7},{... | collective-permute-start | bytes 786440 | tf_op jit(solution)/shard_map/ppermute | solution.py:27
  40.7 2.0 %collective-permute-done.14.refs_0_ = bf16[2,2,128,256]{3,2,1,0:T(8,128)(2,1)S(1)} collective-permute-done((bf16[2,2,128,256]{3,2,1,0:T(8,128)(2,1)S(1)}, bf16[2,2,128,256]{3,2,1,0:T(8,128)(2,1)S(1)}, u32[]{:S(2)}, u32[]{:S(2)}) %collective-permute-start.14) | collective-permute-done | bytes 262176 | tf_op jit(solution)/shard_map/ppermute | solution.py:32
  42.9 1.0 %collective-permute-start.9 = (bf16[2,128,256]{2,1,0:T(8,128)(2,1)S(1)}, bf16[2,128,256]{2,1,0:T(8,128)(2,1)S(1)}, u32[]{:S(2)}, u32[]{:S(2)}) collective-permute-start(bf16[2,128,256]{2,1,0:T(8,128)(2,1)S(1)} %get-tuple-element.42), channel_id=1, source_target_pairs={{0,2},{2,0},{1,3},{3,1},{4,6},{6,4},{5,7},{7,5},{8,10},{10,8},{9,1... | collective-permute-start | bytes 393224 | tf_op jit(solution)/shard_map/ppermute | solution.py:32
  43.9 0.2 both_rows.6.refs_5_
  44.1 0.1 collective-permute-done.15.refs_1_
  44.2 0.2 both_rows.7.refs_6_
  44.4 0.8 %collective-permute-done.12.refs_4_ = bf16[2,2,128,256]{3,2,1,0:T(8,128)(2,1)S(1)} collective-permute-done((bf16[2,2,128,256]{3,2,1,0:T(8,128)(2,1)S(1)}, bf16[2,2,128,256]{3,2,1,0:T(8,128)(2,1)S(1)}, u32[]{:S(2)}, u32[]{:S(2)}) %collective-permute-start.12) | collective-permute-done | bytes 262176 | tf_op jit(solution)/shard_map/ppermute | solution.py:27
  45.2 3.5 %attention_grads.3 = (f32[2,2,2,128,256]{4,3,2,1,0:T(8,128)S(1)}, bf16[2,128,256]{2,1,0:T(8,128)(2,1)S(1)}, bf16[2,128,256]{2,1,0:T(8,128)(2,1)S(1)}, bf16[2,2,1...) custom-call(f32[2,768,256]{2,1,0:T(8,128)S(1)} %pad_maximum_fusion.refs_0_, ...), custom_call_target="tpu_custom_call" | custom-call | flops 1006632960 | bytes 4980736 | tf_op jit(solution)/shard_map/attention_grads/pallas_call | solution.py:57
  48.9 1.1 %collective-permute-start.16 = (bf16[2,2,128,256]{3,2,1,0:T(8,128)(2,1)S(1)}, bf16[2,2,128,256]{3,2,1,0:T(8,128)(2,1)S(1)}, u32[]{:S(2)}, u32[]{:S(2)}) collective-permute-start(bf16[2,2,128,256]{3,2,1,0:T(8,128)(2,1)S(1)} %get-tuple-element.49), channel_id=1, source_target_pairs={{0,2},{2,0},{1,3},{3,1},{4,6},{6,4},{5,7},{7,5},{8,10},{10,8},{9,1... | collective-permute-start | bytes 786440 | tf_op jit(solution)/shard_map/ppermute | solution.py:32
  50.0 1.3 %collective-permute-start.18 = (bf16[2,2,128,256]{3,2,1,0:T(8,128)(2,1)S(1)}, bf16[2,2,128,256]{3,2,1,0:T(8,128)(2,1)S(1)}, u32[]{:S(2)}, u32[]{:S(2)}) collective-permute-start(bf16[2,2,128,256]{3,2,1,0:T(8,128)(2,1)S(1)} %relayed.6), channel_id=1, source_target_pairs={{4,0},{8,4},{12,8},{5,1},{9,5},{13,9},{6,2},{10,6},{14,10},{7,3},{... | collective-permute-start | bytes 786440 | tf_op jit(solution)/shard_map/ppermute | solution.py:27
  51.3 1.1 %collective-permute-start.19 = (bf16[2,128,256]{2,1,0:T(8,128)(2,1)S(1)}, bf16[2,128,256]{2,1,0:T(8,128)(2,1)S(1)}, u32[]{:S(2)}, u32[]{:S(2)}) collective-permute-start(bf16[2,128,256]{2,1,0:T(8,128)(2,1)S(1)} %get-tuple-element.55), channel_id=1, source_target_pairs={{0,2},{2,0},{1,3},{3,1},{4,6},{6,4},{5,7},{7,5},{8,10},{10,8},{9,1... | collective-permute-start | bytes 393224 | tf_op jit(solution)/shard_map/ppermute | solution.py:32
  52.4 5.8 %collective-permute-done.16.refs_3_ = bf16[2,2,128,256]{3,2,1,0:T(8,128)(2,1)S(1)} collective-permute-done((bf16[2,2,128,256]{3,2,1,0:T(8,128)(2,1)S(1)}, bf16[2,2,128,256]{3,2,1,0:T(8,128)(2,1)S(1)}, u32[]{:S(2)}, u32[]{:S(2)}) %collective-permute-start.16) | collective-permute-done | bytes 262176 | tf_op jit(solution)/shard_map/ppermute | solution.py:32
  58.3 1.3 %collective-permute-done.19.refs_1_ = bf16[2,128,256]{2,1,0:T(8,128)(2,1)S(1)} collective-permute-done((bf16[2,128,256]{2,1,0:T(8,128)(2,1)S(1)}, bf16[2,128,256]{2,1,0:T(8,128)(2,1)S(1)}, u32[]{:S(2)}, u32[]{:S(2)}) %collective-permute-start.19) | collective-permute-done | bytes 131104 | tf_op jit(solution)/shard_map/ppermute | solution.py:32
  59.6 0.4 collective-permute-done.18.refs_0_
  60.1 1.3 %collective-permute-start.20 = (bf16[2,2,128,256]{3,2,1,0:T(8,128)(2,1)S(1)}, bf16[2,2,128,256]{3,2,1,0:T(8,128)(2,1)S(1)}, u32[]{:S(2)}, u32[]{:S(2)}) collective-permute-start(bf16[2,2,128,256]{3,2,1,0:T(8,128)(2,1)S(1)} %relayed.7), channel_id=1, source_target_pairs={{4,0},{8,4},{12,8},{5,1},{9,5},{13,9},{6,2},{10,6},{14,10},{7,3},{... | collective-permute-start | bytes 786440 | tf_op jit(solution)/shard_map/ppermute | solution.py:27
  61.5 1.2 %collective-permute-start.25 = (bf16[2,128,256]{2,1,0:T(8,128)(2,1)S(1)}, bf16[2,128,256]{2,1,0:T(8,128)(2,1)S(1)}, u32[]{:S(2)}, u32[]{:S(2)}) collective-permute-start(bf16[2,128,256]{2,1,0:T(8,128)(2,1)S(1)} %get-tuple-element.62), channel_id=1, source_target_pairs={{0,3},{2,1},{1,2},{3,0},{4,7},{6,5},{5,6},{7,4},{8,11},{10,9},{9,1... | collective-permute-start | bytes 393224 | tf_op jit(solution)/shard_map/ppermute | solution.py:38
  62.7 0.9 %collective-permute-start.24 = (bf16[2,128,256]{2,1,0:T(8,128)(2,1)S(1)}, bf16[2,128,256]{2,1,0:T(8,128)(2,1)S(1)}, u32[]{:S(2)}, u32[]{:S(2)}) collective-permute-start(bf16[2,128,256]{2,1,0:T(8,128)(2,1)S(1)} %get-tuple-element.56.refs_0_), channel_id=1, source_target_pairs={{0,2},{2,0},{1,3},{3,1},{4,6},{6,4},{5,7},{7,5},{8,10},{10,8},{9,1... | collective-permute-start | bytes 393224 | tf_op jit(solution)/shard_map/ppermute | solution.py:32
  63.7 6.0 %collective-permute-done.20.later_ref = bf16[2,2,128,256]{3,2,1,0:T(8,128)(2,1)S(1)} collective-permute-done((bf16[2,2,128,256]{3,2,1,0:T(8,128)(2,1)S(1)}, bf16[2,2,128,256]{3,2,1,0:T(8,128)(2,1)S(1)}, u32[]{:S(2)}, u32[]{:S(2)}) %collective-permute-start.20) | collective-permute-done | bytes 262176 | tf_op jit(solution)/shard_map/ppermute | solution.py:27
  69.8 0.5 collective-permute-start.22
  70.3 0.7 collective-permute-done.21.refs_0_
  71.1 0.2 collective-permute-done.22.refs_1_
  71.3 1.3 %laid_out.1 = (bf16[128,2048]{1,0:T(8,128)(2,1)}, bf16[128,2048]{1,0:T(8,128)(2,1)}, bf16[128,2048]{1,0:T(8,128)(2,1)}) custom-call(bf16[3,2,128,256]{3,2,1,0:T(8,128)(2,1)S(1)} %get-tuple-element.50.refs_0_, bf16[3,2,128,256]{3,2,1,0:T(8,128)(2,1)S(1)} %collective-permute-done.17.refs_1_, bf16[4,128,256]{2,1,0:T(8,128)(2,1)S(1)} %stacked.2.refs_2_, ...), custom_call_target="tpu_custom_call" | custom-call | bytes 3145728 | tf_op jit(solution)/shard_map/laid_out/pallas_call | solution.py:57
  (42 shorter events, 1.3 us)
Async XLA Ops:
  0.6 6.2 %copy-start = (s32[2048]{0:T(1024)S(1)}, s32[2048]{0:T(1024)}, u32[]{:S(2)}) copy-start(s32[2048]{0:T(1024)} %param.9) | copy-start | bytes 24580
  1.8 5.2 %collective-permute-start = (bf16[2,128,256]{2,1,0:T(8,128)(2,1)S(1)}, bf16[2,128,256]{2,1,0:T(8,128)(2,1)S(1)}, u32[]{:S(2)}, u32[]{:S(2)}) collective-permute-start(bf16[2,128,256]{2,1,0:T(8,128)(2,1)S(1)} %get-tuple-element.34), channel_id=1, source_target_pairs={{0,1},{1,0},{2,3},{3,2},{4,5},{5,4},{6,7},{7,6},{8,9},{9,8},{10,11... | collective-permute-start | bytes 393224 | tf_op jit(solution)/shard_map/ppermute | solution.py:42
  2.3 9.5 %collective-permute-start.1 = (bf16[2,2,128,256]{3,2,1,0:T(8,128)(2,1)S(1)}, bf16[2,2,128,256]{3,2,1,0:T(8,128)(2,1)S(1)}, u32[]{:S(2)}, u32[]{:S(2)}) collective-permute-start(bf16[2,2,128,256]{3,2,1,0:T(8,128)(2,1)S(1)} %get-tuple-element.35), channel_id=1, source_target_pairs={{0,2},{2,0},{1,3},{3,1},{4,6},{6,4},{5,7},{7,5},{8,10},{10,8},{9,1... | collective-permute-start | bytes 786440 | tf_op jit(solution)/shard_map/ppermute | solution.py:32
  6.3 5.7 %collective-permute-start.5 = (bf16[2,2,128,256]{3,2,1,0:T(8,128)(2,1)S(1)}, bf16[2,2,128,256]{3,2,1,0:T(8,128)(2,1)S(1)}, u32[]{:S(2)}, u32[]{:S(2)}) collective-permute-start(bf16[2,2,128,256]{3,2,1,0:T(8,128)(2,1)S(1)} %get-tuple-element.37), channel_id=1, source_target_pairs={{0,1},{1,0},{2,3},{3,2},{4,5},{5,4},{6,7},{7,6},{8,9},{9,8},{10,11... | collective-permute-start | bytes 786440 | tf_op jit(solution)/shard_map/ppermute | solution.py:42
  6.5 9.3 %collective-permute-start.7 = (bf16[2,2,128,256]{3,2,1,0:T(8,128)(2,1)S(1)}, bf16[2,2,128,256]{3,2,1,0:T(8,128)(2,1)S(1)}, u32[]{:S(2)}, u32[]{:S(2)}) collective-permute-start(bf16[2,2,128,256]{3,2,1,0:T(8,128)(2,1)S(1)} %get-tuple-element.39), channel_id=1, source_target_pairs={{0,1},{1,0},{2,3},{3,2},{4,5},{5,4},{6,7},{7,6},{8,9},{9,8},{10,11... | collective-permute-start | bytes 786440 | tf_op jit(solution)/shard_map/ppermute | solution.py:42
  7.2 10.3 %collective-permute-start.3 = (bf16[2,2,128,256]{3,2,1,0:T(8,128)(2,1)S(1)}, bf16[2,2,128,256]{3,2,1,0:T(8,128)(2,1)S(1)}, u32[]{:S(2)}, u32[]{:S(2)}) collective-permute-start(bf16[2,2,128,256]{3,2,1,0:T(8,128)(2,1)S(1)} %both_rows.4.refs_1_), channel_id=1, source_target_pairs={{0,4},{4,8},{8,12},{12,0},{1,5},{5,9},{9,13},{13,1},{2,6},{6,10},{... | collective-permute-start | bytes 786440 | tf_op jit(solution)/shard_map/ppermute | solution.py:27
  11.9 2.1 %collective-permute-start.2 = (bf16[1,2,128,256]{3,2,1,0:T(8,128)(2,1)S(1)}, bf16[1,2,128,256]{3,2,1,0:T(8,128)(2,1)S(1)}, u32[]{:S(2)}, u32[]{:S(2)}) collective-permute-start(bf16[1,2,128,256]{3,2,1,0:T(8,128)(2,1)S(1)} %other_side.2), channel_id=1, source_target_pairs={{0,1},{1,0},{2,3},{3,2},{4,5},{5,4},{6,7},{7,6},{8,9},{9,8},{10,11... | collective-permute-start | bytes 393224 | tf_op jit(solution)/shard_map/ppermute | solution.py:42
  12.2 8.9 %collective-permute-start.6 = (bf16[2,2,128,256]{3,2,1,0:T(8,128)(2,1)S(1)}, bf16[2,2,128,256]{3,2,1,0:T(8,128)(2,1)S(1)}, u32[]{:S(2)}, u32[]{:S(2)}) collective-permute-start(bf16[2,2,128,256]{3,2,1,0:T(8,128)(2,1)S(1)} %head_parts.5), channel_id=1, source_target_pairs={{0,2},{2,0},{1,3},{3,1},{4,6},{6,4},{5,7},{7,5},{8,10},{10,8},{9,1... | collective-permute-start | bytes 786440 | tf_op jit(solution)/shard_map/ppermute | solution.py:32
  14.2 11.0 %collective-permute-start.4 = (bf16[2,2,128,256]{3,2,1,0:T(8,128)(2,1)S(1)}, bf16[2,2,128,256]{3,2,1,0:T(8,128)(2,1)S(1)}, u32[]{:S(2)}, u32[]{:S(2)}) collective-permute-start(bf16[2,2,128,256]{3,2,1,0:T(8,128)(2,1)S(1)} %both_rows.5.refs_2_.refs_0_), channel_id=1, source_target_pairs={{0,4},{4,8},{8,12},{12,0},{1,5},{5,9},{9,13},{13,1},{2,6},{6,10},{... | collective-permute-start | bytes 786440 | tf_op jit(solution)/shard_map/ppermute | solution.py:27
  17.6 12.5 %collective-permute-start.8 = (bf16[2,2,128,256]{3,2,1,0:T(8,128)(2,1)S(1)}, bf16[2,2,128,256]{3,2,1,0:T(8,128)(2,1)S(1)}, u32[]{:S(2)}, u32[]{:S(2)}) collective-permute-start(bf16[2,2,128,256]{3,2,1,0:T(8,128)(2,1)S(1)} %head_parts.6.refs_1_), channel_id=1, source_target_pairs={{0,4},{4,8},{8,12},{12,0},{1,5},{5,9},{9,13},{13,1},{2,6},{6,10},{... | collective-permute-start | bytes 786440 | tf_op jit(solution)/shard_map/ppermute | solution.py:27
  20.1 16.0 %collective-permute-start.11 = (bf16[2,2,128,256]{3,2,1,0:T(8,128)(2,1)S(1)}, bf16[2,2,128,256]{3,2,1,0:T(8,128)(2,1)S(1)}, u32[]{:S(2)}, u32[]{:S(2)}) collective-permute-start(bf16[2,2,128,256]{3,2,1,0:T(8,128)(2,1)S(1)} %head_parts.7), channel_id=1, source_target_pairs={{0,2},{2,0},{1,3},{3,1},{4,6},{6,4},{5,7},{7,5},{8,10},{10,8},{9,1... | collective-permute-start | bytes 786440 | tf_op jit(solution)/shard_map/ppermute | solution.py:32
  33.7 15.1 %collective-permute-start.10 = (bf16[2,2,2,128,256]{4,3,2,1,0:T(8,128)(2,1)S(1)}, bf16[2,2,2,128,256]{4,3,2,1,0:T(8,128)(2,1)S(1)}, u32[]{:S(2)}, u32[]{:S(2)}) collective-permute-start(bf16[2,2,2,128,256]{4,3,2,1,0:T(8,128)(2,1)S(1)} %get-tuple-element.44), channel_id=1, source_target_pairs={{4,0},{8,4},{12,8},{5,1},{9,5},{13,9},{6,2},{10,6},{14,10},{7,3},{... | collective-permute-start | bytes 1572872 | tf_op jit(solution)/shard_map/ppermute | solution.py:27
  35.0 7.7 %collective-permute-start.14 = (bf16[2,2,128,256]{3,2,1,0:T(8,128)(2,1)S(1)}, bf16[2,2,128,256]{3,2,1,0:T(8,128)(2,1)S(1)}, u32[]{:S(2)}, u32[]{:S(2)}) collective-permute-start(bf16[2,2,128,256]{3,2,1,0:T(8,128)(2,1)S(1)} %relayed.5), channel_id=1, source_target_pairs={{0,2},{2,0},{1,3},{3,1},{4,6},{6,4},{5,7},{7,5},{8,10},{10,8},{9,1... | collective-permute-start | bytes 786440 | tf_op jit(solution)/shard_map/ppermute | solution.py:32
  36.1 9.1 %collective-permute-start.12 = (bf16[2,2,128,256]{3,2,1,0:T(8,128)(2,1)S(1)}, bf16[2,2,128,256]{3,2,1,0:T(8,128)(2,1)S(1)}, u32[]{:S(2)}, u32[]{:S(2)}) collective-permute-start(bf16[2,2,128,256]{3,2,1,0:T(8,128)(2,1)S(1)} %relayed.4), channel_id=1, source_target_pairs={{0,4},{4,8},{8,12},{1,5},{5,9},{9,13},{2,6},{6,10},{10,14},{3,7},{... | collective-permute-start | bytes 786440 | tf_op jit(solution)/shard_map/ppermute | solution.py:27
  40.7 3.2 %collective-permute-start.13 = (bf16[2,128,256]{2,1,0:T(8,128)(2,1)S(1)}, bf16[2,128,256]{2,1,0:T(8,128)(2,1)S(1)}, u32[]{:S(2)}, u32[]{:S(2)}) collective-permute-start(bf16[2,128,256]{2,1,0:T(8,128)(2,1)S(1)} %get-tuple-element.45), channel_id=1, source_target_pairs={{0,1},{1,0},{2,3},{3,2},{4,5},{5,4},{6,7},{7,6},{8,9},{9,8},{10,11... | collective-permute-start | bytes 393224 | tf_op jit(solution)/shard_map/ppermute | solution.py:42
  42.8 1.4 %collective-permute-start.15 = (bf16[1,2,128,256]{3,2,1,0:T(8,128)(2,1)S(1)}, bf16[1,2,128,256]{3,2,1,0:T(8,128)(2,1)S(1)}, u32[]{:S(2)}, u32[]{:S(2)}) collective-permute-start(bf16[1,2,128,256]{3,2,1,0:T(8,128)(2,1)S(1)} %other_side.3), channel_id=1, source_target_pairs={{0,1},{1,0},{2,3},{3,2},{4,5},{5,4},{6,7},{7,6},{8,9},{9,8},{10,11... | collective-permute-start | bytes 393224 | tf_op jit(solution)/shard_map/ppermute | solution.py:42
  42.9 5.9 %collective-permute-start.9 = (bf16[2,128,256]{2,1,0:T(8,128)(2,1)S(1)}, bf16[2,128,256]{2,1,0:T(8,128)(2,1)S(1)}, u32[]{:S(2)}, u32[]{:S(2)}) collective-permute-start(bf16[2,128,256]{2,1,0:T(8,128)(2,1)S(1)} %get-tuple-element.42), channel_id=1, source_target_pairs={{0,2},{2,0},{1,3},{3,1},{4,6},{6,4},{5,7},{7,5},{8,10},{10,8},{9,1... | collective-permute-start | bytes 393224 | tf_op jit(solution)/shard_map/ppermute | solution.py:32
  48.9 9.3 %collective-permute-start.16 = (bf16[2,2,128,256]{3,2,1,0:T(8,128)(2,1)S(1)}, bf16[2,2,128,256]{3,2,1,0:T(8,128)(2,1)S(1)}, u32[]{:S(2)}, u32[]{:S(2)}) collective-permute-start(bf16[2,2,128,256]{3,2,1,0:T(8,128)(2,1)S(1)} %get-tuple-element.49), channel_id=1, source_target_pairs={{0,2},{2,0},{1,3},{3,1},{4,6},{6,4},{5,7},{7,5},{8,10},{10,8},{9,1... | collective-permute-start | bytes 786440 | tf_op jit(solution)/shard_map/ppermute | solution.py:32
  50.0 10.0 %collective-permute-start.18 = (bf16[2,2,128,256]{3,2,1,0:T(8,128)(2,1)S(1)}, bf16[2,2,128,256]{3,2,1,0:T(8,128)(2,1)S(1)}, u32[]{:S(2)}, u32[]{:S(2)}) collective-permute-start(bf16[2,2,128,256]{3,2,1,0:T(8,128)(2,1)S(1)} %relayed.6), channel_id=1, source_target_pairs={{4,0},{8,4},{12,8},{5,1},{9,5},{13,9},{6,2},{10,6},{14,10},{7,3},{... | collective-permute-start | bytes 786440 | tf_op jit(solution)/shard_map/ppermute | solution.py:27
  51.3 8.3 %collective-permute-start.19 = (bf16[2,128,256]{2,1,0:T(8,128)(2,1)S(1)}, bf16[2,128,256]{2,1,0:T(8,128)(2,1)S(1)}, u32[]{:S(2)}, u32[]{:S(2)}) collective-permute-start(bf16[2,128,256]{2,1,0:T(8,128)(2,1)S(1)} %get-tuple-element.55), channel_id=1, source_target_pairs={{0,2},{2,0},{1,3},{3,1},{4,6},{6,4},{5,7},{7,5},{8,10},{10,8},{9,1... | collective-permute-start | bytes 393224 | tf_op jit(solution)/shard_map/ppermute | solution.py:32
  58.2 13.0 %collective-permute-start.17 = (bf16[3,2,128,256]{3,2,1,0:T(8,128)(2,1)S(1)}, bf16[3,2,128,256]{3,2,1,0:T(8,128)(2,1)S(1)}, u32[]{:S(2)}, u32[]{:S(2)}) collective-permute-start(bf16[3,2,128,256]{3,2,1,0:T(8,128)(2,1)S(1)} %get-tuple-element.51), channel_id=1, source_target_pairs={{0,1},{1,0},{2,3},{3,2},{4,5},{5,4},{6,7},{7,6},{8,9},{9,8},{10,11... | collective-permute-start | bytes 1179656 | tf_op jit(solution)/shard_map/ppermute | solution.py:42
  60.1 9.6 %collective-permute-start.20 = (bf16[2,2,128,256]{3,2,1,0:T(8,128)(2,1)S(1)}, bf16[2,2,128,256]{3,2,1,0:T(8,128)(2,1)S(1)}, u32[]{:S(2)}, u32[]{:S(2)}) collective-permute-start(bf16[2,2,128,256]{3,2,1,0:T(8,128)(2,1)S(1)} %relayed.7), channel_id=1, source_target_pairs={{4,0},{8,4},{12,8},{5,1},{9,5},{13,9},{6,2},{10,6},{14,10},{7,3},{... | collective-permute-start | bytes 786440 | tf_op jit(solution)/shard_map/ppermute | solution.py:27
  61.5 8.3 %collective-permute-start.23 = (bf16[2,128,256]{2,1,0:T(8,128)(2,1)S(1)}, bf16[2,128,256]{2,1,0:T(8,128)(2,1)S(1)}, u32[]{:S(2)}, u32[]{:S(2)}) collective-permute-start(bf16[2,128,256]{2,1,0:T(8,128)(2,1)S(1)} %get-tuple-element.61), channel_id=1, source_target_pairs={{0,1},{1,0},{2,3},{3,2},{4,5},{5,4},{6,7},{7,6},{8,9},{9,8},{10,11... | collective-permute-start | bytes 393224 | tf_op jit(solution)/shard_map/ppermute | solution.py:42
  61.5 9.7 %collective-permute-start.25 = (bf16[2,128,256]{2,1,0:T(8,128)(2,1)S(1)}, bf16[2,128,256]{2,1,0:T(8,128)(2,1)S(1)}, u32[]{:S(2)}, u32[]{:S(2)}) collective-permute-start(bf16[2,128,256]{2,1,0:T(8,128)(2,1)S(1)} %get-tuple-element.62), channel_id=1, source_target_pairs={{0,3},{2,1},{1,2},{3,0},{4,7},{6,5},{5,6},{7,4},{8,11},{10,9},{9,1... | collective-permute-start | bytes 393224 | tf_op jit(solution)/shard_map/ppermute | solution.py:38
  62.7 8.5 %collective-permute-start.24 = (bf16[2,128,256]{2,1,0:T(8,128)(2,1)S(1)}, bf16[2,128,256]{2,1,0:T(8,128)(2,1)S(1)}, u32[]{:S(2)}, u32[]{:S(2)}) collective-permute-start(bf16[2,128,256]{2,1,0:T(8,128)(2,1)S(1)} %get-tuple-element.56.refs_0_), channel_id=1, source_target_pairs={{0,2},{2,0},{1,3},{3,1},{4,6},{6,4},{5,7},{7,5},{8,10},{10,8},{9,1... | collective-permute-start | bytes 393224 | tf_op jit(solution)/shard_map/ppermute | solution.py:32
  69.7 1.3 %collective-permute-start.21 = (bf16[1,128,256]{2,1,0:T(8,128)(2,1)S(1)}, bf16[1,128,256]{2,1,0:T(8,128)(2,1)S(1)}, u32[]{:S(2)}, u32[]{:S(2)}) collective-permute-start(bf16[1,128,256]{2,1,0:T(8,128)(2,1)S(1)} %get-tuple-element.59), channel_id=1, source_target_pairs={{0,1},{1,0},{2,3},{3,2},{4,5},{5,4},{6,7},{7,6},{8,9},{9,8},{10,11... | collective-permute-start | bytes 196616 | tf_op jit(solution)/shard_map/ppermute | solution.py:42
  69.8 1.4 %collective-permute-start.22 = (bf16[1,128,256]{2,1,0:T(8,128)(2,1)S(1)}, bf16[1,128,256]{2,1,0:T(8,128)(2,1)S(1)}, u32[]{:S(2)}, u32[]{:S(2)}) collective-permute-start(bf16[1,128,256]{2,1,0:T(8,128)(2,1)S(1)} %get-tuple-element.60), channel_id=1, source_target_pairs={{0,1},{1,0},{2,3},{3,2},{4,5},{5,4},{6,7},{7,6},{8,9},{9,8},{10,11... | collective-permute-start | bytes 196616 | tf_op jit(solution)/shard_map/ppermute | solution.py:42

commit v19 on v17

--- a/solution.py
+++ b/solution.py
@@ -315,43 +315,90 @@
     return call(kernel, own + later + after, outs, [], "summed", whole=True)
 
 
-def rows_for_pair(dq, dkv):
+def last_rows(own, later):
+    _, _, peers, rows, cut = own.shape
+
+    def kernel(own_ref, later_ref, send_k, send_v, keep):
+        p, s = lax.axis_index("pair"), lax.axis_index("sub")
+        for which, send in enumerate((send_k, send_v)):
+            for out, at, row in ((send, 0, 1 - p), (keep, which, p)):
+                out[at] = (own_ref[which, row, s] + later_ref[which, row].astype(WIDE)).astype(LOW)
+
+    outs = [shape(1, rows, cut), shape(1, rows, cut), shape(2, rows, cut)]
+    return call(kernel, [own, later], outs, [], "last_rows", whole=True)
+
+
+def query_rows(dq):
     peers = len(dq)
     _, rows, cut = dq[0].shape
 
     def kernel(*refs):
-        dq_refs, dkv_refs, (send, keep) = refs[:peers], refs[peers:2 * peers], refs[-2:]
-        p, s = lax.axis_index("pair"), lax.axis_index("sub")
-        for by in range(peers):
-            at = lax.rem(s - by + peers, peers)
-            for out, row in ((send, 1 - p), (keep, p)):
-                out[0, at] = dq_refs[by][row]
+        p = lax.axis_index("pair")
+        for out, row in zip(refs[peers:], (1 - p, p)):
+            for by in range(peers):
+                out[by] = refs[by][row]
+
+    return call(kernel, dq, [shape(peers, rows, cut)] * 2, [], "query_rows", whole=True)
+
+
+def stacked(parts):
+    _, rows, cut = parts[0].shape
+
+    def kernel(*refs):
+        at = 0
+        for ref in refs[:-1]:
+            for i in range(ref.shape[0]):
+                refs[-1][at + i] = ref[i]
+            at += ref.shape[0]
+
+    outs = [shape(sum(part.shape[0] for part in parts), rows, cut)]
+    return call(kernel, parts, outs, [], "stacked", whole=True)[0]
+
+
+def far_rows(received):
+    peers = len(received) + 1
+    _, _, rows, cut = received[0].shape
+
+    def kernel(*refs):
+        p = lax.axis_index("pair")
+        for out, row in zip(refs[-2:], (1 - p, p)):
+            for by in range(peers - 1):
                 for which in range(2):
-                    out[1 + which, at] = dkv_refs[by][which, row]
-
-    outs = [shape(3, peers, rows, cut)] * 2
-    return call(kernel, dq + dkv, outs, [], "rows_for_pair", whole=True)
-
-
-def laid_out(kept, paired, spans):
-    _, peers, rows, _ = kept[0].shape
+                    out[which, by] = refs[by][which, row]
+
+    return call(kernel, received, [shape(2, peers - 1, rows, cut)] * 2, [], "far_rows", whole=True)
+
+
+def laid_out(chunks, spans):
+    peers = lax.axis_size("sub")
+    rows = chunks[0][0].shape[1]
     part = spans[-1][1]
     half = part * peers
-    count = len(spans)
-
-    def kernel(*refs):
-        keep, rec, outs, sems = refs[:count], refs[count:2 * count], refs[2 * count:-1], refs[-1]
-        p = lax.axis_index("pair")
-        moves = []
-        for mine, theirs, (low, high) in zip(keep, rec, spans):
-            for source, side in ((mine, p), (theirs, 1 - p)):
-                for at in range(peers):
-                    columns = pl.ds(pl.multiple_of(side * half + at * part + low, HD), high - low)
-                    moves += [(source.at[which, at], out.at[:, columns]) for which, out in enumerate(outs)]
+    ins = [array for chunk in chunks for array in chunk]
+
+    def kernel(*refs):
+        outs, sems = refs[len(ins):-1], refs[-1]
+        p, s = lax.axis_index("pair"), lax.axis_index("sub")
+        moves = []
+
+        def place(source, which, side, at, span):
+            columns = pl.ds(pl.multiple_of(side * half + at * part + span[0], HD), span[1] - span[0])
+            moves.append((source, outs[which].at[:, columns]))
+
+        for chunk, span in enumerate(spans):
+            for i, side in enumerate((p, 1 - p)):
+                near_ref, far_ref = refs[4 * chunk + i], refs[4 * chunk + 2 + i]
+                for by in range(peers):
+                    at = lax.rem(s - by + peers, peers)
+                    place(near_ref.at[2 + by], 0, side, at, span)
+                    for which in range(2):
+                        source = far_ref.at[which, by - 1] if by else near_ref.at[which]
+                        place(source, 1 + which, side, at, span)
         run_moves(moves, sems)
 
     outs = [shape(rows, 2 * half)] * 3
-    return call(kernel, kept + paired, outs, [pltpu.SemaphoreType.DMA((6 * count * peers,))], "laid_out")
+    scratch = [pltpu.SemaphoreType.DMA((6 * len(spans) * peers,))]
+    return call(kernel, ins, outs, scratch, "laid_out")
 
 
 def allowed_bias(session, rows):
@@ -406,7 +453,7 @@
         own_earlier.append(along_blocks(kv_own[index][0], 1, True))
         qg_sends.append(head_parts(*qg_parts[index], others, qg[index - 1] if index else []))
         qg.append([round_sub(value, by) for by, value in zip(others, qg_sends[index])])
-    kept, paired, first_dq, back, release = [], [], [], [], []
+    chunks, first_dq, back = [], [], []
     for index, (low, high) in enumerate(spans):
         last = index == count - 1
         forward = [relayed(value, first_dq) if index else value for value in kv[index]]
@@ -419,20 +466,25 @@
             dq = [dq[0]] + [round_sub(dq[by], by) for by in others]
             later = [along_blocks(relayed(value, back), -1, False) for value in early[1:]]
             dkv = summed([grads], later, others, dq[1:])
-            near = along_blocks(relayed(early[0], release), -1, False)
-            dkv = summed([grads], [near], [0], []) + [round_sub(value, by) for by, value in zip(others, dkv)]
+            own_later = along_blocks(relayed(early[0], dkv), -1, False)
+            send_k, send_v, keep = last_rows(grads, own_later)
+            send, keep_dq = query_rows(dq)
+            theirs = [swapped(send_k), swapped(send_v), swapped(send)]
+            near = [stacked([keep, keep_dq]), stacked(theirs)]
         else:
             grads, dq, early = attention_grads(bias, kv_all, earlier, qg_all, False, 0, heads, [])
             first_dq = dq[:1]
             dq = [dq[0]] + [round_sub(dq[by], by) for by in others]
             back = dq[1:]
             dkv = summed([grads], [along_blocks(early[0], -1, False)], [0] + others, dq[1:])
-            release = dkv[:1]
-            dkv = [dkv[0]] + [round_sub(dkv[by], by) for by in others]
-        send, keep = rows_for_pair(dq, dkv)
-        kept.append(keep)
-        paired.append(swapped(send))
-    return tuple(laid_out(kept, paired, spans))
+            send, keep = far_rows(dkv[:1])
+            send_dq, keep_dq = query_rows(dq)
+            two = (2,) + keep.shape[2:]
+            near = [stacked([keep.reshape(two), keep_dq]), stacked([swapped(send).reshape(two), swapped(send_dq)])]
+            dkv = dkv[1:]
+        send, keep = far_rows([round_sub(value, by) for by, value in zip(others, dkv)])
+        chunks.append(near + [keep, swapped(send)])
+    return tuple(laid_out(chunks, spans))
 
 
 def solution(mesh):

time: 63.2 us -> 64.7 us (1.024)
    ppermute x8, waiting for transfers between devices: 7.71 us -> 8.98 us  [round_sub(): lax.ppermute(value, 'sub', [(i, (i + by) % peers) for i in range(peers)])]
    ppermute x6 -> x11, starting transfers between devices: 1.31 us -> 2.45 us  [swapped(): return lax.ppermute(value, 'pair', [(0, 1), (1, 0)])]
    ppermute x6 -> x11, waiting for transfers between devices: 1.71 us -> 1.11 us  [swapped(): return lax.ppermute(value, 'pair', [(0, 1), (1, 0)])]
    pallas_call x20 -> x27, Pallas kernels: 10.4 us -> 10.5 us  [call(): pl.pallas_call(kernel, out_shape=outs, in_specs=[spec] * len(ins), out_sp...]
  transfers between devices with their start and end apart: 21 -> 26, of which waited for: 11 -> 12; matrix products, arithmetic and copies ran while one was open for 1% -> 1% of each run, Pallas kernels for 17% -> 17%
where the time goes in v19:
time: 64.7 us; the launch traced here: 64.3 us
  starting transfers between devices  24.8 us (38%)
  waiting for transfers between devices  24.3 us (38%)
  Pallas kernels  13.3 us (21%)
  between operations  0.98 us (2%)
  other arithmetic  0.79 us (1%)
    ppermute x7, waiting for transfers between devices, along_blocks(): return lax.ppermute(value, 'blk', pairs)  14.3 us
    ppermute x8, starting transfers between devices, round_sub(): lax.ppermute(value, 'sub', [(i, (i + by) % peers) for i in range(peers)])  13 us
    pallas_call x27, Pallas kernels, call(): pl.pallas_call(kernel, out_shape=outs, in_specs=[spec] * len(ins), out_sp...  10.5 us
    ppermute x7, starting transfers between devices, along_blocks(): return lax.ppermute(value, 'blk', pairs)  9.36 us
    ppermute x8, waiting for transfers between devices, round_sub(): lax.ppermute(value, 'sub', [(i, (i + by) % peers) for i in range(peers)])  8.98 us
    ppermute x11, starting transfers between devices, swapped(): return lax.ppermute(value, 'pair', [(0, 1), (1, 0)])  2.45 us
    pallas_call x1, Pallas kernels, first_parts(): pl.pallas_call(kernel, out_shape=outs, in_specs=[spec] * (len(held) + len...  1.64 us
  transfers between devices with their start and end apart: 26, of which 12 were waited for; matrix products, arithmetic and copies ran while one was open for 1% of the time, Pallas kernels for 17%

profile of v19, /device:TPU:0, one launch (start us, length us, event | category | flops | bytes accessed | tf_op | source)
XLA Modules:
  0.0 64.3 jit_solution(1664447713087658430)
XLA Ops:
  0.6 1.2 %first_keys.1 = (bf16[2,2,128,256]{3,2,1,0:T(8,128)(2,1)S(1)}, bf16[2,128,256]{2,1,0:T(8,128)(2,1)S(1)}, bf16[2,128,256]{2,1,0:T(8,128)(2,1)S(1)}) custom-call(bf16[128,2048]{1,0:T(8,128)(2,1)} %refs_2_.1, bf16[128,2048]{1,0:T(8,128)(2,1)} %refs_3_.1), custom_call_target="tpu_custom_call" | custom-call | tf_op jit(solution)/shard_map/first_keys/pallas_call | solution.py:127
  1.8 0.5 collective-permute-start
  2.3 2.6 %collective-permute-start.1 = (bf16[2,2,128,256]{3,2,1,0:T(8,128)(2,1)S(1)}, bf16[2,2,128,256]{3,2,1,0:T(8,128)(2,1)S(1)}, u32[]{:S(2)}, u32[]{:S(2)}) collective-permute-start(bf16[2,2,128,256]{3,2,1,0:T(8,128)(2,1)S(1)} %get-tuple-element.36), channel_id=1, source_target_pairs={{0,2},{2,0},{1,3},{3,1},{4,6},{6,4},{5,7},{7,5},{8,10},{10,8},{9,1... | collective-permute-start | bytes 786440 | tf_op jit(solution)/shard_map/ppermute | solution.py:32
  4.9 1.6 %first_parts.1 = (bf16[2,2,128,256]{3,2,1,0:T(8,128)(2,1)S(1)}, bf16[2,2,128,256]{3,2,1,0:T(8,128)(2,1)S(1)}, bf16[4,2,128,256]{3,2,1,0:T(8,128)(2,1)S(1)}, bf16[4,2,128,256]{3,2,1,0:T(8,128)(2,1)S(1)}) custom-call(bf16[128,2048]{1,0:T(8,128)(2,1)} %refs_4_.1, bf16[128,2048]{1,0:T(8,128)(2,1)} %refs_5_.1, bf16[128,2048]{1,0:T(8,128)(2,1)} %refs_2_.1, ...), custom_call_target="tpu_custom_call" | custom-call | tf_op jit(solution)/shard_map/first_parts/pallas_call | solution.py:92
  6.5 0.2 collective-permute-start.5
  6.7 0.3 collective-permute-start.13
  7.2 0.2 both_rows.2.refs_1_
  7.4 1.6 %collective-permute-start.3 = (bf16[2,2,128,256]{3,2,1,0:T(8,128)(2,1)S(1)}, bf16[2,2,128,256]{3,2,1,0:T(8,128)(2,1)S(1)}, u32[]{:S(2)}, u32[]{:S(2)}) collective-permute-start(bf16[2,2,128,256]{3,2,1,0:T(8,128)(2,1)S(1)} %both_rows.2.refs_1_), channel_id=1, source_target_pairs={{0,4},{4,8},{8,12},{12,0},{1,5},{5,9},{9,13},{13,1},{2,6},{6,10},{... | collective-permute-start | bytes 786440 | tf_op jit(solution)/shard_map/ppermute | solution.py:27
  9.0 2.7 %collective-permute-done.1.refs_0_ = bf16[2,2,128,256]{3,2,1,0:T(8,128)(2,1)S(1)} collective-permute-done((bf16[2,2,128,256]{3,2,1,0:T(8,128)(2,1)S(1)}, bf16[2,2,128,256]{3,2,1,0:T(8,128)(2,1)S(1)}, u32[]{:S(2)}, u32[]{:S(2)}) %collective-permute-start.1) | collective-permute-done | bytes 262176 | tf_op jit(solution)/shard_map/ppermute | solution.py:32
  12.0 0.2 head_parts.7
  12.2 1.8 %collective-permute-start.6 = (bf16[2,2,128,256]{3,2,1,0:T(8,128)(2,1)S(1)}, bf16[2,2,128,256]{3,2,1,0:T(8,128)(2,1)S(1)}, u32[]{:S(2)}, u32[]{:S(2)}) collective-permute-start(bf16[2,2,128,256]{3,2,1,0:T(8,128)(2,1)S(1)} %head_parts.7), channel_id=1, source_target_pairs={{0,2},{2,0},{1,3},{3,1},{4,6},{6,4},{5,7},{7,5},{8,10},{10,8},{9,1... | collective-permute-start | bytes 786440 | tf_op jit(solution)/shard_map/ppermute | solution.py:32
  14.0 0.2 both_rows.3.refs_2_.refs_0_
  14.2 1.6 %collective-permute-start.4 = (bf16[2,2,128,256]{3,2,1,0:T(8,128)(2,1)S(1)}, bf16[2,2,128,256]{3,2,1,0:T(8,128)(2,1)S(1)}, u32[]{:S(2)}, u32[]{:S(2)}) collective-permute-start(bf16[2,2,128,256]{3,2,1,0:T(8,128)(2,1)S(1)} %both_rows.3.refs_2_.refs_0_), channel_id=1, source_target_pairs={{0,4},{4,8},{8,12},{12,0},{1,5},{5,9},{9,13},{13,1},{2,6},{6,10},{... | collective-permute-start | bytes 786440 | tf_op jit(solution)/shard_map/ppermute | solution.py:27
  15.8 1.9 %collective-permute-done.3.refs_3_.refs_0_.refs_1_ = bf16[2,2,128,256]{3,2,1,0:T(8,128)(2,1)S(1)} collective-permute-done((bf16[2,2,128,256]{3,2,1,0:T(8,128)(2,1)S(1)}, bf16[2,2,128,256]{3,2,1,0:T(8,128)(2,1)S(1)}, u32[]{:S(2)}, u32[]{:S(2)}) %collective-permute-start.3) | collective-permute-done | bytes 262176 | tf_op jit(solution)/shard_map/ppermute | solution.py:27
  17.7 0.2 head_parts.9
  17.9 0.6 collective-permute-start.14
  18.5 0.7 %and_select_fusion = (f32[1,768,256]{2,1,0:T(8,128)S(1)}, f32[1,768,256]{2,1,0:T(8,128)S(1)}) fusion(s32[256]{0:T(256)S(1)} %get-tuple-element.74, s32[256]{0:T(256)S(1)} %get-tuple-element.72, s32[768]{0:T(1024)S(1)} %get-tuple-element.70, s32[768]{0:T(1024)S(1)} %get-tuple-element.68, pred[768]{0:T(1024)(128)(4,1)S(1)} %get-tuple-element.66, ...), kind=kLoop, calls=%fused_computation.1 | loop fusion | flops 1966080 | bytes 1590784 | tf_op jit(solution)/shard_map/jit(_where)/select_n | solution.py:417
  19.2 0.1 pad_maximum_fusion.refs_0_
  19.3 0.2 head_parts.6.refs_5_
  19.5 0.2 head_parts.8.refs_1_
  19.7 0.2 collective-permute-start.15
  19.9 1.4 %collective-permute-done.6.refs_6_.refs_0_ = bf16[2,2,128,256]{3,2,1,0:T(8,128)(2,1)S(1)} collective-permute-done((bf16[2,2,128,256]{3,2,1,0:T(8,128)(2,1)S(1)}, bf16[2,2,128,256]{3,2,1,0:T(8,128)(2,1)S(1)}, u32[]{:S(2)}, u32[]{:S(2)}) %collective-permute-start.6) | collective-permute-done | bytes 262176 | tf_op jit(solution)/shard_map/ppermute | solution.py:32
  21.3 0.2 head_parts.11
  21.5 1.8 %collective-permute-start.17 = (bf16[2,2,128,256]{3,2,1,0:T(8,128)(2,1)S(1)}, bf16[2,2,128,256]{3,2,1,0:T(8,128)(2,1)S(1)}, u32[]{:S(2)}, u32[]{:S(2)}) collective-permute-start(bf16[2,2,128,256]{3,2,1,0:T(8,128)(2,1)S(1)} %head_parts.11), channel_id=1, source_target_pairs={{0,2},{2,0},{1,3},{3,1},{4,6},{6,4},{5,7},{7,5},{8,10},{10,8},{9,1... | collective-permute-start | bytes 786440 | tf_op jit(solution)/shard_map/ppermute | solution.py:32
  23.3 1.8 %collective-permute-done.4.refs_4_ = bf16[2,2,128,256]{3,2,1,0:T(8,128)(2,1)S(1)} collective-permute-done((bf16[2,2,128,256]{3,2,1,0:T(8,128)(2,1)S(1)}, bf16[2,2,128,256]{3,2,1,0:T(8,128)(2,1)S(1)}, u32[]{:S(2)}, u32[]{:S(2)}) %collective-permute-start.4) | collective-permute-done | bytes 262176 | tf_op jit(solution)/shard_map/ppermute | solution.py:27
  25.2 3.5 %attention_grads.2 = (f32[2,2,2,128,256]{4,3,2,1,0:T(8,128)S(1)}, bf16[2,128,256]{2,1,0:T(8,128)(2,1)S(1)}, bf16[2,128,256]{2,1,0:T(8,128)(2,1)S(1)}, bf16[2,2,2,128,256]{4,3,2,1,0:T(8,128)(2,1)S(1)}) custom-call(f32[2,768,256]{2,1,0:T(8,128)S(1)} %pad_maximum_fusion.refs_0_, bf16[2,2,128,256]{3,2,1,0:T(8,128)(2,1)S(1)} %both_rows.2.refs_1_, ...), custom_call_target="tpu_custom_call" | custom-call | flops 1006632960 | bytes 4980736 | tf_op jit(solution)/shard_map/attention_grads/pallas_call | solution.py:51
  28.8 2.0 %collective-permute-start.16 = (bf16[2,2,128,256]{3,2,1,0:T(8,128)(2,1)S(1)}, bf16[2,2,128,256]{3,2,1,0:T(8,128)(2,1)S(1)}, u32[]{:S(2)}, u32[]{:S(2)}) collective-permute-start(bf16[2,2,128,256]{3,2,1,0:T(8,128)(2,1)S(1)} %relayed.3), channel_id=1, source_target_pairs={{0,4},{4,8},{8,12},{1,5},{5,9},{9,13},{2,6},{6,10},{10,14},{3,7},{... | collective-permute-start | bytes 786440 | tf_op jit(solution)/shard_map/ppermute | solution.py:27
  30.8 1.3 %collective-permute-start.7 = (bf16[2,2,2,128,256]{4,3,2,1,0:T(8,128)(2,1)S(1)}, bf16[2,2,2,128,256]{4,3,2,1,0:T(8,128)(2,1)S(1)}, u32[]{:S(2)}, u32[]{:S(2)}) collective-permute-start(bf16[2,2,2,128,256]{4,3,2,1,0:T(8,128)(2,1)S(1)} %get-tuple-element.40), channel_id=1, source_target_pairs={{4,0},{8,4},{12,8},{5,1},{9,5},{13,9},{6,2},{10,6},{14,10},{7,3},{... | collective-permute-start | bytes 1572872 | tf_op jit(solution)/shard_map/ppermute | solution.py:27
  32.1 1.6 %collective-permute-start.8 = (bf16[2,128,256]{2,1,0:T(8,128)(2,1)S(1)}, bf16[2,128,256]{2,1,0:T(8,128)(2,1)S(1)}, u32[]{:S(2)}, u32[]{:S(2)}) collective-permute-start(bf16[2,128,256]{2,1,0:T(8,128)(2,1)S(1)} %get-tuple-element.41), channel_id=1, source_target_pairs={{0,2},{2,0},{1,3},{3,1},{4,6},{6,4},{5,7},{7,5},{8,10},{10,8},{9,1... | collective-permute-start | bytes 393224 | tf_op jit(solution)/shard_map/ppermute | solution.py:32
  33.6 0.2 head_parts.10.refs_5_
  33.8 1.9 %collective-permute-done.16.refs_4_ = bf16[2,2,128,256]{3,2,1,0:T(8,128)(2,1)S(1)} collective-permute-done((bf16[2,2,128,256]{3,2,1,0:T(8,128)(2,1)S(1)}, bf16[2,2,128,256]{3,2,1,0:T(8,128)(2,1)S(1)}, u32[]{:S(2)}, u32[]{:S(2)}) %collective-permute-start.16) | collective-permute-done | bytes 262176 | tf_op jit(solution)/shard_map/ppermute | solution.py:27
  35.8 3.5 %attention_grads.3 = (f32[2,2,2,128,256]{4,3,2,1,0:T(8,128)S(1)}, bf16[2,128,256]{2,1,0:T(8,128)(2,1)S(1)}, bf16[2,128,256]{2,1,0:T(8,128)(2,1)S(1)}, bf16[2,2,1...) custom-call(f32[2,768,256]{2,1,0:T(8,128)S(1)} %pad_maximum_fusion.refs_0_, ...), custom_call_target="tpu_custom_call" | custom-call | flops 1006632960 | bytes 4980736 | tf_op jit(solution)/shard_map/attention_grads/pallas_call | solution.py:51
  39.4 1.3 %collective-permute-start.18 = (bf16[2,2,128,256]{3,2,1,0:T(8,128)(2,1)S(1)}, bf16[2,2,128,256]{3,2,1,0:T(8,128)(2,1)S(1)}, u32[]{:S(2)}, u32[]{:S(2)}) collective-permute-start(bf16[2,2,128,256]{3,2,1,0:T(8,128)(2,1)S(1)} %relayed.4), channel_id=1, source_target_pairs={{4,0},{8,4},{12,8},{5,1},{9,5},{13,9},{6,2},{10,6},{14,10},{7,3},{... | collective-permute-start | bytes 786440 | tf_op jit(solution)/shard_map/ppermute | solution.py:27
  40.7 1.6 %collective-permute-start.19 = (bf16[2,128,256]{2,1,0:T(8,128)(2,1)S(1)}, bf16[2,128,256]{2,1,0:T(8,128)(2,1)S(1)}, u32[]{:S(2)}, u32[]{:S(2)}) collective-permute-start(bf16[2,128,256]{2,1,0:T(8,128)(2,1)S(1)} %get-tuple-element.56), channel_id=1, source_target_pairs={{0,2},{2,0},{1,3},{3,1},{4,6},{6,4},{5,7},{7,5},{8,10},{10,8},{9,1... | collective-permute-start | bytes 393224 | tf_op jit(solution)/shard_map/ppermute | solution.py:32
  42.2 5.3 %collective-permute-done.7.refs_1_ = bf16[2,2,2,128,256]{4,3,2,1,0:T(8,128)(2,1)S(1)} collective-permute-done((bf16[2,2,2,128,256]{4,3,2,1,0:T(8,128)(2,1)S(1)}, bf16[2,2,2,128,256]{4,3,2,1,0:T(8,128)(2,1)S(1)}, u32[]{:S(2)}, u32[]{:S(2)}) %collective-permute-start.7) | collective-permute-done | bytes 524320 | tf_op jit(solution)/shard_map/ppermute | solution.py:27
  47.5 0.1 summed.2
  47.6 1.6 %collective-permute-start.11 = (bf16[2,2,128,256]{3,2,1,0:T(8,128)(2,1)S(1)}, bf16[2,2,128,256]{3,2,1,0:T(8,128)(2,1)S(1)}, u32[]{:S(2)}, u32[]{:S(2)}) collective-permute-start(bf16[2,2,128,256]{3,2,1,0:T(8,128)(2,1)S(1)} %get-tuple-element.48), channel_id=1, source_target_pairs={{0,2},{2,0},{1,3},{3,1},{4,6},{6,4},{5,7},{7,5},{8,10},{10,8},{9,1... | collective-permute-start | bytes 786440 | tf_op jit(solution)/shard_map/ppermute | solution.py:32
  49.2 2.0 %collective-permute-done.18.refs_1_ = bf16[2,2,128,256]{3,2,1,0:T(8,128)(2,1)S(1)} collective-permute-done((bf16[2,2,128,256]{3,2,1,0:T(8,128)(2,1)S(1)}, bf16[2,2,128,256]{3,2,1,0:T(8,128)(2,1)S(1)}, u32[]{:S(2)}, u32[]{:S(2)}) %collective-permute-start.18) | collective-permute-done | bytes 262176 | tf_op jit(solution)/shard_map/ppermute | solution.py:27
  51.2 1.6 %collective-permute-start.24 = (bf16[2,2,128,256]{3,2,1,0:T(8,128)(2,1)S(1)}, bf16[2,2,128,256]{3,2,1,0:T(8,128)(2,1)S(1)}, u32[]{:S(2)}, u32[]{:S(2)}) collective-permute-start(bf16[2,2,128,256]{3,2,1,0:T(8,128)(2,1)S(1)} %summed.3.refs_0_), channel_id=1, source_target_pairs={{0,2},{2,0},{1,3},{3,1},{4,6},{6,4},{5,7},{7,5},{8,10},{10,8},{9,1... | collective-permute-start | bytes 786440 | tf_op jit(solution)/shard_map/ppermute | solution.py:32
  52.8 1.3 %collective-permute-start.20 = (bf16[2,2,128,256]{3,2,1,0:T(8,128)(2,1)S(1)}, bf16[2,2,128,256]{3,2,1,0:T(8,128)(2,1)S(1)}, u32[]{:S(2)}, u32[]{:S(2)}) collective-permute-start(bf16[2,2,128,256]{3,2,1,0:T(8,128)(2,1)S(1)} %relayed.5), channel_id=1, source_target_pairs={{4,0},{8,4},{12,8},{5,1},{9,5},{13,9},{6,2},{10,6},{14,10},{7,3},{... | collective-permute-start | bytes 786440 | tf_op jit(solution)/shard_map/ppermute | solution.py:27
  54.2 0.5 collective-permute-start.9
  54.8 1.4 %collective-permute-done.11.refs_0_ = bf16[2,2,128,256]{3,2,1,0:T(8,128)(2,1)S(1)} collective-permute-done((bf16[2,2,128,256]{3,2,1,0:T(8,128)(2,1)S(1)}, bf16[2,2,128,256]{3,2,1,0:T(8,128)(2,1)S(1)}, u32[]{:S(2)}, u32[]{:S(2)}) %collective-permute-start.11) | collective-permute-done | bytes 262176 | tf_op jit(solution)/shard_map/ppermute | solution.py:32
  56.2 3.4 %collective-permute-done.24.refs_0_ = bf16[2,2,128,256]{3,2,1,0:T(8,128)(2,1)S(1)} collective-permute-done((bf16[2,2,128,256]{3,2,1,0:T(8,128)(2,1)S(1)}, bf16[2,2,128,256]{3,2,1,0:T(8,128)(2,1)S(1)}, u32[]{:S(2)}, u32[]{:S(2)}) %collective-permute-start.24) | collective-permute-done | bytes 262176 | tf_op jit(solution)/shard_map/ppermute | solution.py:32
  59.7 1.3 %collective-permute-done.20.later_ref = bf16[2,2,128,256]{3,2,1,0:T(8,128)(2,1)S(1)} collective-permute-done((bf16[2,2,128,256]{3,2,1,0:T(8,128)(2,1)S(1)}, bf16[2,2,128,256]{3,2,1,0:T(8,128)(2,1)S(1)}, u32[]{:S(2)}, u32[]{:S(2)}) %collective-permute-start.20) | collective-permute-done | bytes 262176 | tf_op jit(solution)/shard_map/ppermute | solution.py:27
  61.1 0.6 collective-permute-start.21
  61.9 0.7 %collective-permute-done.21.refs_0_ = bf16[1,128,256]{2,1,0:T(8,128)(2,1)S(1)} collective-permute-done((bf16[1,128,256]{2,1,0:T(8,128)(2,1)S(1)}, bf16[1,128,256]{2,1,0:T(8,128)(2,1)S(1)}, u32[]{:S(2)}, u32[]{:S(2)}) %collective-permute-start.21) | collective-permute-done | bytes 65568 | tf_op jit(solution)/shard_map/ppermute | solution.py:36
  62.6 0.4 collective-permute-done.22.refs_1_
  63.0 1.3 %laid_out.1 = (bf16[128,2048]{1,0:T(8,128)(2,1)}, bf16[128,2048]{1,0:T(8,128)(2,1)}, bf16[128,2048]{1,0:T(8,128)(2,1)}) custom-call(bf16[4,128,256]{2,1,0:T(8,128)(2,1)S(1)} %stacked.4.refs_0_, bf16[4,128,256]{2,1,0:T(8,128)(2,1)S(1)} %stacked.5.refs_1_, bf16[2,1,128,256]{3,2,1,0:T(8,128)(2,1)S(1)} %get-tuple-element.49.refs_2_, ...), custom_call_target="tpu_custom_call" | custom-call | bytes 3145728 | tf_op jit(solution)/shard_map/laid_out/pallas_call | solution.py:51
  (44 shorter events, 0.8 us)
Async XLA Ops:
  1.8 5.4 %collective-permute-start = (bf16[2,128,256]{2,1,0:T(8,128)(2,1)S(1)}, bf16[2,128,256]{2,1,0:T(8,128)(2,1)S(1)}, u32[]{:S(2)}, u32[]{:S(2)}) collective-permute-start(bf16[2,128,256]{2,1,0:T(8,128)(2,1)S(1)} %get-tuple-element.35), channel_id=1, source_target_pairs={{0,1},{1,0},{2,3},{3,2},{4,5},{5,4},{6,7},{7,6},{8,9},{9,8},{10,11... | collective-permute-start | bytes 393224 | tf_op jit(solution)/shard_map/ppermute | solution.py:36
  2.3 9.5 %collective-permute-start.1 = (bf16[2,2,128,256]{3,2,1,0:T(8,128)(2,1)S(1)}, bf16[2,2,128,256]{3,2,1,0:T(8,128)(2,1)S(1)}, u32[]{:S(2)}, u32[]{:S(2)}) collective-permute-start(bf16[2,2,128,256]{3,2,1,0:T(8,128)(2,1)S(1)} %get-tuple-element.36), channel_id=1, source_target_pairs={{0,2},{2,0},{1,3},{3,1},{4,6},{6,4},{5,7},{7,5},{8,10},{10,8},{9,1... | collective-permute-start | bytes 786440 | tf_op jit(solution)/shard_map/ppermute | solution.py:32
  4.9 2.2 %copy-start = (s32[2048]{0:T(1024)S(1)}, s32[2048]{0:T(1024)}, u32[]{:S(2)}) copy-start(s32[2048]{0:T(1024)} %param.9) | copy-start | bytes 24580
  6.5 5.4 %collective-permute-start.5 = (bf16[2,2,128,256]{3,2,1,0:T(8,128)(2,1)S(1)}, bf16[2,2,128,256]{3,2,1,0:T(8,128)(2,1)S(1)}, u32[]{:S(2)}, u32[]{:S(2)}) collective-permute-start(bf16[2,2,128,256]{3,2,1,0:T(8,128)(2,1)S(1)} %get-tuple-element.38), channel_id=1, source_target_pairs={{0,1},{1,0},{2,3},{3,2},{4,5},{5,4},{6,7},{7,6},{8,9},{9,8},{10,11... | collective-permute-start | bytes 786440 | tf_op jit(solution)/shard_map/ppermute | solution.py:36
  6.7 11.0 %collective-permute-start.13 = (bf16[4,2,128,256]{3,2,1,0:T(8,128)(2,1)S(1)}, bf16[4,2,128,256]{3,2,1,0:T(8,128)(2,1)S(1)}, u32[]{:S(2)}, u32[]{:S(2)}) collective-permute-start(bf16[4,2,128,256]{3,2,1,0:T(8,128)(2,1)S(1)} %get-tuple-element.52), channel_id=1, source_target_pairs={{0,1},{1,0},{2,3},{3,2},{4,5},{5,4},{6,7},{7,6},{8,9},{9,8},{10,11... | collective-permute-start | bytes 1572872 | tf_op jit(solution)/shard_map/ppermute | solution.py:36
  7.4 10.3 %collective-permute-start.3 = (bf16[2,2,128,256]{3,2,1,0:T(8,128)(2,1)S(1)}, bf16[2,2,128,256]{3,2,1,0:T(8,128)(2,1)S(1)}, u32[]{:S(2)}, u32[]{:S(2)}) collective-permute-start(bf16[2,2,128,256]{3,2,1,0:T(8,128)(2,1)S(1)} %both_rows.2.refs_1_), channel_id=1, source_target_pairs={{0,4},{4,8},{8,12},{12,0},{1,5},{5,9},{9,13},{13,1},{2,6},{6,10},{... | collective-permute-start | bytes 786440 | tf_op jit(solution)/shard_map/ppermute | solution.py:27
  11.9 2.1 %collective-permute-start.2 = (bf16[1,2,128,256]{3,2,1,0:T(8,128)(2,1)S(1)}, bf16[1,2,128,256]{3,2,1,0:T(8,128)(2,1)S(1)}, u32[]{:S(2)}, u32[]{:S(2)}) collective-permute-start(bf16[1,2,128,256]{3,2,1,0:T(8,128)(2,1)S(1)} %other_side.1), channel_id=1, source_target_pairs={{0,1},{1,0},{2,3},{3,2},{4,5},{5,4},{6,7},{7,6},{8,9},{9,8},{10,11... | collective-permute-start | bytes 393224 | tf_op jit(solution)/shard_map/ppermute | solution.py:36
  12.2 9.2 %collective-permute-start.6 = (bf16[2,2,128,256]{3,2,1,0:T(8,128)(2,1)S(1)}, bf16[2,2,128,256]{3,2,1,0:T(8,128)(2,1)S(1)}, u32[]{:S(2)}, u32[]{:S(2)}) collective-permute-start(bf16[2,2,128,256]{3,2,1,0:T(8,128)(2,1)S(1)} %head_parts.7), channel_id=1, source_target_pairs={{0,2},{2,0},{1,3},{3,1},{4,6},{6,4},{5,7},{7,5},{8,10},{10,8},{9,1... | collective-permute-start | bytes 786440 | tf_op jit(solution)/shard_map/ppermute | solution.py:32
  14.2 11.0 %collective-permute-start.4 = (bf16[2,2,128,256]{3,2,1,0:T(8,128)(2,1)S(1)}, bf16[2,2,128,256]{3,2,1,0:T(8,128)(2,1)S(1)}, u32[]{:S(2)}, u32[]{:S(2)}) collective-permute-start(bf16[2,2,128,256]{3,2,1,0:T(8,128)(2,1)S(1)} %both_rows.3.refs_2_.refs_0_), channel_id=1, source_target_pairs={{0,4},{4,8},{8,12},{12,0},{1,5},{5,9},{9,13},{13,1},{2,6},{6,10},{... | collective-permute-start | bytes 786440 | tf_op jit(solution)/shard_map/ppermute | solution.py:27
  17.9 10.8 %collective-permute-start.14 = (bf16[2,2,128,256]{3,2,1,0:T(8,128)(2,1)S(1)}, bf16[2,2,128,256]{3,2,1,0:T(8,128)(2,1)S(1)}, u32[]{:S(2)}, u32[]{:S(2)}) collective-permute-start(bf16[2,2,128,256]{3,2,1,0:T(8,128)(2,1)S(1)} %head_parts.9), channel_id=1, source_target_pairs={{0,2},{2,0},{1,3},{3,1},{4,6},{6,4},{5,7},{7,5},{8,10},{10,8},{9,1... | collective-permute-start | bytes 786440 | tf_op jit(solution)/shard_map/ppermute | solution.py:32
  19.7 14.1 %collective-permute-start.15 = (bf16[2,2,128,256]{3,2,1,0:T(8,128)(2,1)S(1)}, bf16[2,2,128,256]{3,2,1,0:T(8,128)(2,1)S(1)}, u32[]{:S(2)}, u32[]{:S(2)}) collective-permute-start(bf16[2,2,128,256]{3,2,1,0:T(8,128)(2,1)S(1)} %head_parts.8.refs_1_), channel_id=1, source_target_pairs={{0,4},{4,8},{8,12},{12,0},{1,5},{5,9},{9,13},{13,1},{2,6},{6,10},{... | collective-permute-start | bytes 786440 | tf_op jit(solution)/shard_map/ppermute | solution.py:27
  21.5 12.3 %collective-permute-start.17 = (bf16[2,2,128,256]{3,2,1,0:T(8,128)(2,1)S(1)}, bf16[2,2,128,256]{3,2,1,0:T(8,128)(2,1)S(1)}, u32[]{:S(2)}, u32[]{:S(2)}) collective-permute-start(bf16[2,2,128,256]{3,2,1,0:T(8,128)(2,1)S(1)} %head_parts.11), channel_id=1, source_target_pairs={{0,2},{2,0},{1,3},{3,1},{4,6},{6,4},{5,7},{7,5},{8,10},{10,8},{9,1... | collective-permute-start | bytes 786440 | tf_op jit(solution)/shard_map/ppermute | solution.py:32
  28.8 7.0 %collective-permute-start.16 = (bf16[2,2,128,256]{3,2,1,0:T(8,128)(2,1)S(1)}, bf16[2,2,128,256]{3,2,1,0:T(8,128)(2,1)S(1)}, u32[]{:S(2)}, u32[]{:S(2)}) collective-permute-start(bf16[2,2,128,256]{3,2,1,0:T(8,128)(2,1)S(1)} %relayed.3), channel_id=1, source_target_pairs={{0,4},{4,8},{8,12},{1,5},{5,9},{9,13},{2,6},{6,10},{10,14},{3,7},{... | collective-permute-start | bytes 786440 | tf_op jit(solution)/shard_map/ppermute | solution.py:27
  30.8 16.8 %collective-permute-start.7 = (bf16[2,2,2,128,256]{4,3,2,1,0:T(8,128)(2,1)S(1)}, bf16[2,2,2,128,256]{4,3,2,1,0:T(8,128)(2,1)S(1)}, u32[]{:S(2)}, u32[]{:S(2)}) collective-permute-start(bf16[2,2,2,128,256]{4,3,2,1,0:T(8,128)(2,1)S(1)} %get-tuple-element.40), channel_id=1, source_target_pairs={{4,0},{8,4},{12,8},{5,1},{9,5},{13,9},{6,2},{10,6},{14,10},{7,3},{... | collective-permute-start | bytes 1572872 | tf_op jit(solution)/shard_map/ppermute | solution.py:27
  32.1 7.2 %collective-permute-start.8 = (bf16[2,128,256]{2,1,0:T(8,128)(2,1)S(1)}, bf16[2,128,256]{2,1,0:T(8,128)(2,1)S(1)}, u32[]{:S(2)}, u32[]{:S(2)}) collective-permute-start(bf16[2,128,256]{2,1,0:T(8,128)(2,1)S(1)} %get-tuple-element.41), channel_id=1, source_target_pairs={{0,2},{2,0},{1,3},{3,1},{4,6},{6,4},{5,7},{7,5},{8,10},{10,8},{9,1... | collective-permute-start | bytes 393224 | tf_op jit(solution)/shard_map/ppermute | solution.py:32
  39.4 11.8 %collective-permute-start.18 = (bf16[2,2,128,256]{3,2,1,0:T(8,128)(2,1)S(1)}, bf16[2,2,128,256]{3,2,1,0:T(8,128)(2,1)S(1)}, u32[]{:S(2)}, u32[]{:S(2)}) collective-permute-start(bf16[2,2,128,256]{3,2,1,0:T(8,128)(2,1)S(1)} %relayed.4), channel_id=1, source_target_pairs={{4,0},{8,4},{12,8},{5,1},{9,5},{13,9},{6,2},{10,6},{14,10},{7,3},{... | collective-permute-start | bytes 786440 | tf_op jit(solution)/shard_map/ppermute | solution.py:27
  40.7 8.5 %collective-permute-start.19 = (bf16[2,128,256]{2,1,0:T(8,128)(2,1)S(1)}, bf16[2,128,256]{2,1,0:T(8,128)(2,1)S(1)}, u32[]{:S(2)}, u32[]{:S(2)}) collective-permute-start(bf16[2,128,256]{2,1,0:T(8,128)(2,1)S(1)} %get-tuple-element.56), channel_id=1, source_target_pairs={{0,2},{2,0},{1,3},{3,1},{4,6},{6,4},{5,7},{7,5},{8,10},{10,8},{9,1... | collective-permute-start | bytes 393224 | tf_op jit(solution)/shard_map/ppermute | solution.py:32
  47.6 8.6 %collective-permute-start.11 = (bf16[2,2,128,256]{3,2,1,0:T(8,128)(2,1)S(1)}, bf16[2,2,128,256]{3,2,1,0:T(8,128)(2,1)S(1)}, u32[]{:S(2)}, u32[]{:S(2)}) collective-permute-start(bf16[2,2,128,256]{3,2,1,0:T(8,128)(2,1)S(1)} %get-tuple-element.48), channel_id=1, source_target_pairs={{0,2},{2,0},{1,3},{3,1},{4,6},{6,4},{5,7},{7,5},{8,10},{10,8},{9,1... | collective-permute-start | bytes 786440 | tf_op jit(solution)/shard_map/ppermute | solution.py:32
  51.2 8.5 %collective-permute-start.24 = (bf16[2,2,128,256]{3,2,1,0:T(8,128)(2,1)S(1)}, bf16[2,2,128,256]{3,2,1,0:T(8,128)(2,1)S(1)}, u32[]{:S(2)}, u32[]{:S(2)}) collective-permute-start(bf16[2,2,128,256]{3,2,1,0:T(8,128)(2,1)S(1)} %summed.3.refs_0_), channel_id=1, source_target_pairs={{0,2},{2,0},{1,3},{3,1},{4,6},{6,4},{5,7},{7,5},{8,10},{10,8},{9,1... | collective-permute-start | bytes 786440 | tf_op jit(solution)/shard_map/ppermute | solution.py:32
  52.8 8.3 %collective-permute-start.20 = (bf16[2,2,128,256]{3,2,1,0:T(8,128)(2,1)S(1)}, bf16[2,2,128,256]{3,2,1,0:T(8,128)(2,1)S(1)}, u32[]{:S(2)}, u32[]{:S(2)}) collective-permute-start(bf16[2,2,128,256]{3,2,1,0:T(8,128)(2,1)S(1)} %relayed.5), channel_id=1, source_target_pairs={{4,0},{8,4},{12,8},{5,1},{9,5},{13,9},{6,2},{10,6},{14,10},{7,3},{... | collective-permute-start | bytes 786440 | tf_op jit(solution)/shard_map/ppermute | solution.py:27
  54.1 7.0 %collective-permute-start.10 = (bf16[2,128,256]{2,1,0:T(8,128)(2,1)S(1)}, bf16[2,128,256]{2,1,0:T(8,128)(2,1)S(1)}, u32[]{:S(2)}, u32[]{:S(2)}) collective-permute-start(bf16[2,128,256]{2,1,0:T(8,128)(2,1)S(1)} %get-tuple-element.47), channel_id=1, source_target_pairs={{0,1},{1,0},{2,3},{3,2},{4,5},{5,4},{6,7},{7,6},{8,9},{9,8},{10,11... | collective-permute-start | bytes 393224 | tf_op jit(solution)/shard_map/ppermute | solution.py:36
  54.2 7.5 %collective-permute-start.9 = (bf16[2,1,128,256]{3,2,0,1:T(8,128)(2,1)S(1)}, bf16[2,1,128,256]{3,2,0,1:T(8,128)(2,1)S(1)}, u32[]{:S(2)}, u32[]{:S(2)}) collective-permute-start(bf16[2,1,128,256]{3,2,0,1:T(8,128)(2,1)S(1)} %bitcast.7), channel_id=1, source_target_pairs={{0,1},{1,0},{2,3},{3,2},{4,5},{5,4},{6,7},{7,6},{8,9},{9,8},{10,11... | collective-permute-start | bytes 393224 | tf_op jit(solution)/shard_map/ppermute | solution.py:36
  56.2 5.6 %collective-permute-start.23 = (bf16[2,128,256]{2,1,0:T(8,128)(2,1)S(1)}, bf16[2,128,256]{2,1,0:T(8,128)(2,1)S(1)}, u32[]{:S(2)}, u32[]{:S(2)}) collective-permute-start(bf16[2,128,256]{2,1,0:T(8,128)(2,1)S(1)} %get-tuple-element.62), channel_id=1, source_target_pairs={{0,1},{1,0},{2,3},{3,2},{4,5},{5,4},{6,7},{7,6},{8,9},{9,8},{10,11... | collective-permute-start | bytes 393224 | tf_op jit(solution)/shard_map/ppermute | solution.py:36
  59.7 3.3 %collective-permute-start.12 = (bf16[2,1,128,256]{3,2,1,0:T(8,128)(2,1)S(1)}, bf16[2,1,128,256]{3,2,1,0:T(8,128)(2,1)S(1)}, u32[]{:S(2)}, u32[]{:S(2)}) collective-permute-start(bf16[2,1,128,256]{3,2,1,0:T(8,128)(2,1)S(1)} %get-tuple-element.50), channel_id=1, source_target_pairs={{0,1},{1,0},{2,3},{3,2},{4,5},{5,4},{6,7},{7,6},{8,9},{9,8},{10,11... | collective-permute-start | bytes 393224 | tf_op jit(solution)/shard_map/ppermute | solution.py:36
  61.0 1.9 %collective-permute-start.25 = (bf16[2,1,128,256]{3,2,1,0:T(8,128)(2,1)S(1)}, bf16[2,1,128,256]{3,2,1,0:T(8,128)(2,1)S(1)}, u32[]{:S(2)}, u32[]{:S(2)}) collective-permute-start(bf16[2,1,128,256]{3,2,1,0:T(8,128)(2,1)S(1)} %get-tuple-element.64), channel_id=1, source_target_pairs={{0,1},{1,0},{2,3},{3,2},{4,5},{5,4},{6,7},{7,6},{8,9},{9,8},{10,11... | collective-permute-start | bytes 393224 | tf_op jit(solution)/shard_map/ppermute | solution.py:36
  61.1 1.5 %collective-permute-start.21 = (bf16[1,128,256]{2,1,0:T(8,128)(2,1)S(1)}, bf16[1,128,256]{2,1,0:T(8,128)(2,1)S(1)}, u32[]{:S(2)}, u32[]{:S(2)}) collective-permute-start(bf16[1,128,256]{2,1,0:T(8,128)(2,1)S(1)} %get-tuple-element.60), channel_id=1, source_target_pairs={{0,1},{1,0},{2,3},{3,2},{4,5},{5,4},{6,7},{7,6},{8,9},{9,8},{10,11... | collective-permute-start | bytes 196616 | tf_op jit(solution)/shard_map/ppermute | solution.py:36
  61.7 1.3 %collective-permute-start.22 = (bf16[1,128,256]{2,1,0:T(8,128)(2,1)S(1)}, bf16[1,128,256]{2,1,0:T(8,128)(2,1)S(1)}, u32[]{:S(2)}, u32[]{:S(2)}) collective-permute-start(bf16[1,128,256]{2,1,0:T(8,128)(2,1)S(1)} %get-tuple-element.61), channel_id=1, source_target_pairs={{0,1},{1,0},{2,3},{3,2},{4,5},{5,4},{6,7},{7,6},{8,9},{9,8},{10,11... | collective-permute-start | bytes 196616 | tf_op jit(solution)/shard_map/ppermute | solution.py:36

commit v20 on v19

--- a/solution.py
+++ b/solution.py
@@ -315,17 +315,20 @@
     return call(kernel, own + later + after, outs, [], "summed", whole=True)
 
 
-def last_rows(own, later):
-    _, _, peers, rows, cut = own.shape
-
-    def kernel(own_ref, later_ref, send_k, send_v, keep):
+def last_rows(own, later, dq):
+    _, _, _, rows, cut = own.shape
+
+    def kernel(own_ref, later_ref, *refs):
+        dq_refs, outs = refs[:len(dq)], refs[len(dq):]
         p, s = lax.axis_index("pair"), lax.axis_index("sub")
-        for which, send in enumerate((send_k, send_v)):
-            for out, at, row in ((send, 0, 1 - p), (keep, which, p)):
-                out[at] = (own_ref[which, row, s] + later_ref[which, row].astype(WIDE)).astype(LOW)
-
-    outs = [shape(1, rows, cut), shape(1, rows, cut), shape(2, rows, cut)]
-    return call(kernel, [own, later], outs, [], "last_rows", whole=True)
+        for out, row in zip(outs, (1 - p, p)):
+            for which in range(2):
+                total = own_ref[which, row, s] + later_ref[which, row].astype(WIDE)
+                out[which] = total.astype(LOW)
+            for by in range(len(dq)):
+                out[2 + by] = dq_refs[by][row]
+
+    return call(kernel, [own, later] + dq, [shape(2 + len(dq), rows, cut)] * 2, [], "last_rows", whole=True)
 
 
 def query_rows(dq):
@@ -453,7 +456,7 @@
         own_earlier.append(along_blocks(kv_own[index][0], 1, True))
         qg_sends.append(head_parts(*qg_parts[index], others, qg[index - 1] if index else []))
         qg.append([round_sub(value, by) for by, value in zip(others, qg_sends[index])])
-    chunks, first_dq, back = [], [], []
+    chunks, first_dq, back, release = [], [], [], []
     for index, (low, high) in enumerate(spans):
         last = index == count - 1
         forward = [relayed(value, first_dq) if index else value for value in kv[index]]
@@ -466,17 +469,17 @@
             dq = [dq[0]] + [round_sub(dq[by], by) for by in others]
             later = [along_blocks(relayed(value, back), -1, False) for value in early[1:]]
             dkv = summed([grads], later, others, dq[1:])
-            own_later = along_blocks(relayed(early[0], dkv), -1, False)
-            send_k, send_v, keep = last_rows(grads, own_later)
-            send, keep_dq = query_rows(dq)
-            theirs = [swapped(send_k), swapped(send_v), swapped(send)]
-            near = [stacked([keep, keep_dq]), stacked(theirs)]
+            own_later = along_blocks(relayed(early[0], release), -1, False)
+            send, keep = last_rows(grads, own_later, [])
+            send_dq, keep_dq = query_rows(dq)
+            near = [stacked([keep, keep_dq]), stacked([swapped(send), swapped(send_dq)])]
         else:
             grads, dq, early = attention_grads(bias, kv_all, earlier, qg_all, False, 0, heads, [])
             first_dq = dq[:1]
             dq = [dq[0]] + [round_sub(dq[by], by) for by in others]
             back = dq[1:]
             dkv = summed([grads], [along_blocks(early[0], -1, False)], [0] + others, dq[1:])
+            release = dkv[:1]
             send, keep = far_rows(dkv[:1])
             send_dq, keep_dq = query_rows(dq)
             two = (2,) + keep.shape[2:]

time: 64.7 us -> 62.9 us (0.972)
  waiting for transfers between devices: 24.3 us -> 22.3 us
    ppermute x8, waiting for transfers between devices: 8.98 us -> 7.01 us  [round_sub(): lax.ppermute(value, 'sub', [(i, (i + by) % peers) for i in range(peers)])]
    ppermute x11 -> x10, starting transfers between devices: 2.45 us -> 2.36 us  [swapped(): return lax.ppermute(value, 'pair', [(0, 1), (1, 0)])]
  transfers between devices with their start and end apart: 26 -> 25, of which waited for: 12 -> 12; matrix products, arithmetic and copies ran while one was open for 1% -> 1% of each run, Pallas kernels for 17% -> 17%
where the time goes in v20:
time: 62.9 us; the launch traced here: 62.6 us
  starting transfers between devices  25.2 us (40%)
  waiting for transfers between devices  22.3 us (35%)
  Pallas kernels  13.2 us (21%)
  between operations  0.98 us (2%)
  other arithmetic  0.79 us (1%)
    ppermute x7, waiting for transfers between devices, along_blocks(): return lax.ppermute(value, 'blk', pairs)  14.4 us
    ppermute x8, starting transfers between devices, round_sub(): lax.ppermute(value, 'sub', [(i, (i + by) % peers) for i in range(peers)])  13.5 us
    pallas_call x27, Pallas kernels, call(): pl.pallas_call(kernel, out_shape=outs, in_specs=[spec] * len(ins), out_sp...  10.4 us
    ppermute x7, starting transfers between devices, along_blocks(): return lax.ppermute(value, 'blk', pairs)  9.36 us
    ppermute x8, waiting for transfers between devices, round_sub(): lax.ppermute(value, 'sub', [(i, (i + by) % peers) for i in range(peers)])  7.01 us
    ppermute x10, starting transfers between devices, swapped(): return lax.ppermute(value, 'pair', [(0, 1), (1, 0)])  2.36 us
    pallas_call x1, Pallas kernels, first_parts(): pl.pallas_call(kernel, out_shape=outs, in_specs=[spec] * (len(held) + len...  1.64 us
  transfers between devices with their start and end apart: 25, of which 12 were waited for; matrix products, arithmetic and copies ran while one was open for 1% of the time, Pallas kernels for 17%

profile of v20, /device:TPU:0, one launch (start us, length us, event | category | flops | bytes accessed | tf_op | source)
XLA Modules:
  0.0 62.6 jit_solution(7616498282802461007)
XLA Ops:
  0.6 1.2 %first_keys.1 = (bf16[2,2,128,256]{3,2,1,0:T(8,128)(2,1)S(1)}, bf16[2,128,256]{2,1,0:T(8,128)(2,1)S(1)}, bf16[2,128,256]{2,1,0:T(8,128)(2,1)S(1)}) custom-call(bf16[128,2048]{1,0:T(8,128)(2,1)} %refs_2_.1, bf16[128,2048]{1,0:T(8,128)(2,1)} %refs_3_.1), custom_call_target="tpu_custom_call" | custom-call | tf_op jit(solution)/shard_map/first_keys/pallas_call | solution.py:127
  1.8 0.5 collective-permute-start
  2.3 2.6 %collective-permute-start.1 = (bf16[2,2,128,256]{3,2,1,0:T(8,128)(2,1)S(1)}, bf16[2,2,128,256]{3,2,1,0:T(8,128)(2,1)S(1)}, u32[]{:S(2)}, u32[]{:S(2)}) collective-permute-start(bf16[2,2,128,256]{3,2,1,0:T(8,128)(2,1)S(1)} %get-tuple-element.35), channel_id=1, source_target_pairs={{0,2},{2,0},{1,3},{3,1},{4,6},{6,4},{5,7},{7,5},{8,10},{10,8},{9,1... | collective-permute-start | bytes 786440 | tf_op jit(solution)/shard_map/ppermute | solution.py:32
  4.9 1.6 %first_parts.1 = (bf16[2,2,128,256]{3,2,1,0:T(8,128)(2,1)S(1)}, bf16[2,2,128,256]{3,2,1,0:T(8,128)(2,1)S(1)}, bf16[4,2,128,256]{3,2,1,0:T(8,128)(2,1)S(1)}, bf16[4,2,128,256]{3,2,1,0:T(8,128)(2,1)S(1)}) custom-call(bf16[128,2048]{1,0:T(8,128)(2,1)} %refs_4_.1, bf16[128,2048]{1,0:T(8,128)(2,1)} %refs_5_.1, bf16[128,2048]{1,0:T(8,128)(2,1)} %refs_2_.1, ...), custom_call_target="tpu_custom_call" | custom-call | tf_op jit(solution)/shard_map/first_parts/pallas_call | solution.py:92
  6.5 0.2 collective-permute-start.5
  6.7 0.3 collective-permute-start.13
  7.2 0.2 both_rows.2.refs_1_
  7.4 1.6 %collective-permute-start.3 = (bf16[2,2,128,256]{3,2,1,0:T(8,128)(2,1)S(1)}, bf16[2,2,128,256]{3,2,1,0:T(8,128)(2,1)S(1)}, u32[]{:S(2)}, u32[]{:S(2)}) collective-permute-start(bf16[2,2,128,256]{3,2,1,0:T(8,128)(2,1)S(1)} %both_rows.2.refs_1_), channel_id=1, source_target_pairs={{0,4},{4,8},{8,12},{12,0},{1,5},{5,9},{9,13},{13,1},{2,6},{6,10},{... | collective-permute-start | bytes 786440 | tf_op jit(solution)/shard_map/ppermute | solution.py:27
  9.0 2.7 %collective-permute-done.1.refs_0_ = bf16[2,2,128,256]{3,2,1,0:T(8,128)(2,1)S(1)} collective-permute-done((bf16[2,2,128,256]{3,2,1,0:T(8,128)(2,1)S(1)}, bf16[2,2,128,256]{3,2,1,0:T(8,128)(2,1)S(1)}, u32[]{:S(2)}, u32[]{:S(2)}) %collective-permute-start.1) | collective-permute-done | bytes 262176 | tf_op jit(solution)/shard_map/ppermute | solution.py:32
  12.0 0.2 head_parts.7
  12.2 1.8 %collective-permute-start.6 = (bf16[2,2,128,256]{3,2,1,0:T(8,128)(2,1)S(1)}, bf16[2,2,128,256]{3,2,1,0:T(8,128)(2,1)S(1)}, u32[]{:S(2)}, u32[]{:S(2)}) collective-permute-start(bf16[2,2,128,256]{3,2,1,0:T(8,128)(2,1)S(1)} %head_parts.7), channel_id=1, source_target_pairs={{0,2},{2,0},{1,3},{3,1},{4,6},{6,4},{5,7},{7,5},{8,10},{10,8},{9,1... | collective-permute-start | bytes 786440 | tf_op jit(solution)/shard_map/ppermute | solution.py:32
  14.0 0.2 both_rows.3.refs_2_.refs_0_
  14.2 1.6 %collective-permute-start.4 = (bf16[2,2,128,256]{3,2,1,0:T(8,128)(2,1)S(1)}, bf16[2,2,128,256]{3,2,1,0:T(8,128)(2,1)S(1)}, u32[]{:S(2)}, u32[]{:S(2)}) collective-permute-start(bf16[2,2,128,256]{3,2,1,0:T(8,128)(2,1)S(1)} %both_rows.3.refs_2_.refs_0_), channel_id=1, source_target_pairs={{0,4},{4,8},{8,12},{12,0},{1,5},{5,9},{9,13},{13,1},{2,6},{6,10},{... | collective-permute-start | bytes 786440 | tf_op jit(solution)/shard_map/ppermute | solution.py:27
  15.8 1.9 %collective-permute-done.3.refs_3_.refs_0_.refs_1_ = bf16[2,2,128,256]{3,2,1,0:T(8,128)(2,1)S(1)} collective-permute-done((bf16[2,2,128,256]{3,2,1,0:T(8,128)(2,1)S(1)}, bf16[2,2,128,256]{3,2,1,0:T(8,128)(2,1)S(1)}, u32[]{:S(2)}, u32[]{:S(2)}) %collective-permute-start.3) | collective-permute-done | bytes 262176 | tf_op jit(solution)/shard_map/ppermute | solution.py:27
  17.7 0.2 head_parts.9
  17.9 0.6 collective-permute-start.14
  18.5 0.7 %and_select_fusion = (f32[1,768,256]{2,1,0:T(8,128)S(1)}, f32[1,768,256]{2,1,0:T(8,128)S(1)}) fusion(s32[256]{0:T(256)S(1)} %get-tuple-element.72, s32[256]{0:T(256)S(1)} %get-tuple-element.70, s32[768]{0:T(1024)S(1)} %get-tuple-element.68, s32[768]{0:T(1024)S(1)} %get-tuple-element.66, pred[768]{0:T(1024)(128)(4,1)S(1)} %get-tuple-element.64, ...), kind=kLoop, calls=%fused_computation.1 | loop fusion | flops 1966080 | bytes 1590784 | tf_op jit(solution)/shard_map/jit(_where)/select_n | solution.py:420
  19.2 0.1 pad_maximum_fusion.refs_0_
  19.3 0.2 head_parts.6.refs_5_
  19.5 0.2 head_parts.8.refs_1_
  19.7 0.2 collective-permute-start.15
  19.9 1.4 %collective-permute-done.6.refs_6_.refs_0_ = bf16[2,2,128,256]{3,2,1,0:T(8,128)(2,1)S(1)} collective-permute-done((bf16[2,2,128,256]{3,2,1,0:T(8,128)(2,1)S(1)}, bf16[2,2,128,256]{3,2,1,0:T(8,128)(2,1)S(1)}, u32[]{:S(2)}, u32[]{:S(2)}) %collective-permute-start.6) | collective-permute-done | bytes 262176 | tf_op jit(solution)/shard_map/ppermute | solution.py:32
  21.3 0.2 head_parts.11
  21.5 1.8 %collective-permute-start.17 = (bf16[2,2,128,256]{3,2,1,0:T(8,128)(2,1)S(1)}, bf16[2,2,128,256]{3,2,1,0:T(8,128)(2,1)S(1)}, u32[]{:S(2)}, u32[]{:S(2)}) collective-permute-start(bf16[2,2,128,256]{3,2,1,0:T(8,128)(2,1)S(1)} %head_parts.11), channel_id=1, source_target_pairs={{0,2},{2,0},{1,3},{3,1},{4,6},{6,4},{5,7},{7,5},{8,10},{10,8},{9,1... | collective-permute-start | bytes 786440 | tf_op jit(solution)/shard_map/ppermute | solution.py:32
  23.3 1.8 %collective-permute-done.4.refs_4_ = bf16[2,2,128,256]{3,2,1,0:T(8,128)(2,1)S(1)} collective-permute-done((bf16[2,2,128,256]{3,2,1,0:T(8,128)(2,1)S(1)}, bf16[2,2,128,256]{3,2,1,0:T(8,128)(2,1)S(1)}, u32[]{:S(2)}, u32[]{:S(2)}) %collective-permute-start.4) | collective-permute-done | bytes 262176 | tf_op jit(solution)/shard_map/ppermute | solution.py:27
  25.2 3.5 %attention_grads.2 = (f32[2,2,2,128,256]{4,3,2,1,0:T(8,128)S(1)}, bf16[2,128,256]{2,1,0:T(8,128)(2,1)S(1)}, bf16[2,128,256]{2,1,0:T(8,128)(2,1)S(1)}, bf16[2,2,2,128,256]{4,3,2,1,0:T(8,128)(2,1)S(1)}) custom-call(f32[2,768,256]{2,1,0:T(8,128)S(1)} %pad_maximum_fusion.refs_0_, bf16[2,2,128,256]{3,2,1,0:T(8,128)(2,1)S(1)} %both_rows.2.refs_1_, ...), custom_call_target="tpu_custom_call" | custom-call | flops 1006632960 | bytes 4980736 | tf_op jit(solution)/shard_map/attention_grads/pallas_call | solution.py:51
  28.8 2.0 %collective-permute-start.16 = (bf16[2,2,128,256]{3,2,1,0:T(8,128)(2,1)S(1)}, bf16[2,2,128,256]{3,2,1,0:T(8,128)(2,1)S(1)}, u32[]{:S(2)}, u32[]{:S(2)}) collective-permute-start(bf16[2,2,128,256]{3,2,1,0:T(8,128)(2,1)S(1)} %relayed.3), channel_id=1, source_target_pairs={{0,4},{4,8},{8,12},{1,5},{5,9},{9,13},{2,6},{6,10},{10,14},{3,7},{... | collective-permute-start | bytes 786440 | tf_op jit(solution)/shard_map/ppermute | solution.py:27
  30.8 1.3 %collective-permute-start.7 = (bf16[2,2,2,128,256]{4,3,2,1,0:T(8,128)(2,1)S(1)}, bf16[2,2,2,128,256]{4,3,2,1,0:T(8,128)(2,1)S(1)}, u32[]{:S(2)}, u32[]{:S(2)}) collective-permute-start(bf16[2,2,2,128,256]{4,3,2,1,0:T(8,128)(2,1)S(1)} %get-tuple-element.39), channel_id=1, source_target_pairs={{4,0},{8,4},{12,8},{5,1},{9,5},{13,9},{6,2},{10,6},{14,10},{7,3},{... | collective-permute-start | bytes 1572872 | tf_op jit(solution)/shard_map/ppermute | solution.py:27
  32.1 1.6 %collective-permute-start.8 = (bf16[2,128,256]{2,1,0:T(8,128)(2,1)S(1)}, bf16[2,128,256]{2,1,0:T(8,128)(2,1)S(1)}, u32[]{:S(2)}, u32[]{:S(2)}) collective-permute-start(bf16[2,128,256]{2,1,0:T(8,128)(2,1)S(1)} %get-tuple-element.40), channel_id=1, source_target_pairs={{0,2},{2,0},{1,3},{3,1},{4,6},{6,4},{5,7},{7,5},{8,10},{10,8},{9,1... | collective-permute-start | bytes 393224 | tf_op jit(solution)/shard_map/ppermute | solution.py:32
  33.6 0.2 head_parts.10.refs_5_
  33.8 1.9 %collective-permute-done.16.refs_4_ = bf16[2,2,128,256]{3,2,1,0:T(8,128)(2,1)S(1)} collective-permute-done((bf16[2,2,128,256]{3,2,1,0:T(8,128)(2,1)S(1)}, bf16[2,2,128,256]{3,2,1,0:T(8,128)(2,1)S(1)}, u32[]{:S(2)}, u32[]{:S(2)}) %collective-permute-start.16) | collective-permute-done | bytes 262176 | tf_op jit(solution)/shard_map/ppermute | solution.py:27
  35.8 3.5 %attention_grads.3 = (f32[2,2,2,128,256]{4,3,2,1,0:T(8,128)S(1)}, bf16[2,128,256]{2,1,0:T(8,128)(2,1)S(1)}, bf16[2,128,256]{2,1,0:T(8,128)(2,1)S(1)}, bf16[2,2,1...) custom-call(f32[2,768,256]{2,1,0:T(8,128)S(1)} %pad_maximum_fusion.refs_0_, ...), custom_call_target="tpu_custom_call" | custom-call | flops 1006632960 | bytes 4980736 | tf_op jit(solution)/shard_map/attention_grads/pallas_call | solution.py:51
  39.4 1.3 %collective-permute-start.22 = (bf16[2,2,128,256]{3,2,1,0:T(8,128)(2,1)S(1)}, bf16[2,2,128,256]{3,2,1,0:T(8,128)(2,1)S(1)}, u32[]{:S(2)}, u32[]{:S(2)}) collective-permute-start(bf16[2,2,128,256]{3,2,1,0:T(8,128)(2,1)S(1)} %relayed.5), channel_id=1, source_target_pairs={{4,0},{8,4},{12,8},{5,1},{9,5},{13,9},{6,2},{10,6},{14,10},{7,3},{... | collective-permute-start | bytes 786440 | tf_op jit(solution)/shard_map/ppermute | solution.py:27
  40.7 1.6 %collective-permute-start.19 = (bf16[2,128,256]{2,1,0:T(8,128)(2,1)S(1)}, bf16[2,128,256]{2,1,0:T(8,128)(2,1)S(1)}, u32[]{:S(2)}, u32[]{:S(2)}) collective-permute-start(bf16[2,128,256]{2,1,0:T(8,128)(2,1)S(1)} %get-tuple-element.56), channel_id=1, source_target_pairs={{0,2},{2,0},{1,3},{3,1},{4,6},{6,4},{5,7},{7,5},{8,10},{10,8},{9,1... | collective-permute-start | bytes 393224 | tf_op jit(solution)/shard_map/ppermute | solution.py:32
  42.2 5.3 %collective-permute-done.7.refs_1_ = bf16[2,2,2,128,256]{4,3,2,1,0:T(8,128)(2,1)S(1)} collective-permute-done((bf16[2,2,2,128,256]{4,3,2,1,0:T(8,128)(2,1)S(1)}, bf16[2,2,2,128,256]{4,3,2,1,0:T(8,128)(2,1)S(1)}, u32[]{:S(2)}, u32[]{:S(2)}) %collective-permute-start.7) | collective-permute-done | bytes 524320 | tf_op jit(solution)/shard_map/ppermute | solution.py:27
  47.5 0.1 summed.2
  47.6 1.6 %collective-permute-start.11 = (bf16[2,2,128,256]{3,2,1,0:T(8,128)(2,1)S(1)}, bf16[2,2,128,256]{3,2,1,0:T(8,128)(2,1)S(1)}, u32[]{:S(2)}, u32[]{:S(2)}) collective-permute-start(bf16[2,2,128,256]{3,2,1,0:T(8,128)(2,1)S(1)} %get-tuple-element.47), channel_id=1, source_target_pairs={{0,2},{2,0},{1,3},{3,1},{4,6},{6,4},{5,7},{7,5},{8,10},{10,8},{9,1... | collective-permute-start | bytes 786440 | tf_op jit(solution)/shard_map/ppermute | solution.py:32
  49.2 1.3 %collective-permute-start.18 = (bf16[2,2,128,256]{3,2,1,0:T(8,128)(2,1)S(1)}, bf16[2,2,128,256]{3,2,1,0:T(8,128)(2,1)S(1)}, u32[]{:S(2)}, u32[]{:S(2)}) collective-permute-start(bf16[2,2,128,256]{3,2,1,0:T(8,128)(2,1)S(1)} %relayed.4), channel_id=1, source_target_pairs={{4,0},{8,4},{12,8},{5,1},{9,5},{13,9},{6,2},{10,6},{14,10},{7,3},{... | collective-permute-start | bytes 786440 | tf_op jit(solution)/shard_map/ppermute | solution.py:27
  50.5 2.2 %collective-permute-done.22.refs_1_ = bf16[2,2,128,256]{3,2,1,0:T(8,128)(2,1)S(1)} collective-permute-done((bf16[2,2,128,256]{3,2,1,0:T(8,128)(2,1)S(1)}, bf16[2,2,128,256]{3,2,1,0:T(8,128)(2,1)S(1)}, u32[]{:S(2)}, u32[]{:S(2)}) %collective-permute-start.22) | collective-permute-done | bytes 262176 | tf_op jit(solution)/shard_map/ppermute | solution.py:27
  52.7 2.0 %collective-permute-start.23 = (bf16[2,2,128,256]{3,2,1,0:T(8,128)(2,1)S(1)}, bf16[2,2,128,256]{3,2,1,0:T(8,128)(2,1)S(1)}, u32[]{:S(2)}, u32[]{:S(2)}) collective-permute-start(bf16[2,2,128,256]{3,2,1,0:T(8,128)(2,1)S(1)} %summed.3), channel_id=1, source_target_pairs={{0,2},{2,0},{1,3},{3,1},{4,6},{6,4},{5,7},{7,5},{8,10},{10,8},{9,1... | collective-permute-start | bytes 786440 | tf_op jit(solution)/shard_map/ppermute | solution.py:32
  54.9 0.5 collective-permute-start.9
  55.5 0.7 %collective-permute-done.11.refs_0_ = bf16[2,2,128,256]{3,2,1,0:T(8,128)(2,1)S(1)} collective-permute-done((bf16[2,2,128,256]{3,2,1,0:T(8,128)(2,1)S(1)}, bf16[2,2,128,256]{3,2,1,0:T(8,128)(2,1)S(1)}, u32[]{:S(2)}, u32[]{:S(2)}) %collective-permute-start.11) | collective-permute-done | bytes 262176 | tf_op jit(solution)/shard_map/ppermute | solution.py:32
  56.2 1.2 %collective-permute-done.18.later_ref = bf16[2,2,128,256]{3,2,1,0:T(8,128)(2,1)S(1)} collective-permute-done((bf16[2,2,128,256]{3,2,1,0:T(8,128)(2,1)S(1)}, bf16[2,2,128,256]{3,2,1,0:T(8,128)(2,1)S(1)}, u32[]{:S(2)}, u32[]{:S(2)}) %collective-permute-start.18) | collective-permute-done | bytes 262176 | tf_op jit(solution)/shard_map/ppermute | solution.py:27
  57.5 2.1 %collective-permute-done.23.refs_0_ = bf16[2,2,128,256]{3,2,1,0:T(8,128)(2,1)S(1)} collective-permute-done((bf16[2,2,128,256]{3,2,1,0:T(8,128)(2,1)S(1)}, bf16[2,2,128,256]{3,2,1,0:T(8,128)(2,1)S(1)}, u32[]{:S(2)}, u32[]{:S(2)}) %collective-permute-start.23) | collective-permute-done | bytes 262176 | tf_op jit(solution)/shard_map/ppermute | solution.py:32
  59.7 0.6 collective-permute-start.24
  60.4 0.6 %collective-permute-done.20.refs_0_ = bf16[2,128,256]{2,1,0:T(8,128)(2,1)S(1)} collective-permute-done((bf16[2,128,256]{2,1,0:T(8,128)(2,1)S(1)}, bf16[2,128,256]{2,1,0:T(8,128)(2,1)S(1)}, u32[]{:S(2)}, u32[]{:S(2)}) %collective-permute-start.20) | collective-permute-done | bytes 131104 | tf_op jit(solution)/shard_map/ppermute | solution.py:36
  61.0 0.2 collective-permute-done.24.refs_7_
  61.3 1.3 %laid_out.1 = (bf16[128,2048]{1,0:T(8,128)(2,1)}, bf16[128,2048]{1,0:T(8,128)(2,1)}, bf16[128,2048]{1,0:T(8,128)(2,1)}) custom-call(bf16[4,128,256]{2,1,0:T(8,128)(2,1)S(1)} %stacked.4.refs_0_, bf16[4,128,256]{2,1,0:T(8,128)(2,1)S(1)} %stacked.5.refs_1_, bf16[2,1,128,256]{3,2,1,0:T(8,128)(2,1)S(1)} %get-tuple-element.48.refs_2_, ...), custom_call_target="tpu_custom_call" | custom-call | bytes 3145728 | tf_op jit(solution)/shard_map/laid_out/pallas_call | solution.py:51
  (42 shorter events, 0.7 us)
Async XLA Ops:
  1.8 5.4 %collective-permute-start = (bf16[2,128,256]{2,1,0:T(8,128)(2,1)S(1)}, bf16[2,128,256]{2,1,0:T(8,128)(2,1)S(1)}, u32[]{:S(2)}, u32[]{:S(2)}) collective-permute-start(bf16[2,128,256]{2,1,0:T(8,128)(2,1)S(1)} %get-tuple-element.34), channel_id=1, source_target_pairs={{0,1},{1,0},{2,3},{3,2},{4,5},{5,4},{6,7},{7,6},{8,9},{9,8},{10,11... | collective-permute-start | bytes 393224 | tf_op jit(solution)/shard_map/ppermute | solution.py:36
  2.3 9.5 %collective-permute-start.1 = (bf16[2,2,128,256]{3,2,1,0:T(8,128)(2,1)S(1)}, bf16[2,2,128,256]{3,2,1,0:T(8,128)(2,1)S(1)}, u32[]{:S(2)}, u32[]{:S(2)}) collective-permute-start(bf16[2,2,128,256]{3,2,1,0:T(8,128)(2,1)S(1)} %get-tuple-element.35), channel_id=1, source_target_pairs={{0,2},{2,0},{1,3},{3,1},{4,6},{6,4},{5,7},{7,5},{8,10},{10,8},{9,1... | collective-permute-start | bytes 786440 | tf_op jit(solution)/shard_map/ppermute | solution.py:32
  4.9 2.2 %copy-start = (s32[2048]{0:T(1024)S(1)}, s32[2048]{0:T(1024)}, u32[]{:S(2)}) copy-start(s32[2048]{0:T(1024)} %param.9) | copy-start | bytes 24580
  6.5 5.4 %collective-permute-start.5 = (bf16[2,2,128,256]{3,2,1,0:T(8,128)(2,1)S(1)}, bf16[2,2,128,256]{3,2,1,0:T(8,128)(2,1)S(1)}, u32[]{:S(2)}, u32[]{:S(2)}) collective-permute-start(bf16[2,2,128,256]{3,2,1,0:T(8,128)(2,1)S(1)} %get-tuple-element.37), channel_id=1, source_target_pairs={{0,1},{1,0},{2,3},{3,2},{4,5},{5,4},{6,7},{7,6},{8,9},{9,8},{10,11... | collective-permute-start | bytes 786440 | tf_op jit(solution)/shard_map/ppermute | solution.py:36
  6.7 11.0 %collective-permute-start.13 = (bf16[4,2,128,256]{3,2,1,0:T(8,128)(2,1)S(1)}, bf16[4,2,128,256]{3,2,1,0:T(8,128)(2,1)S(1)}, u32[]{:S(2)}, u32[]{:S(2)}) collective-permute-start(bf16[4,2,128,256]{3,2,1,0:T(8,128)(2,1)S(1)} %get-tuple-element.51), channel_id=1, source_target_pairs={{0,1},{1,0},{2,3},{3,2},{4,5},{5,4},{6,7},{7,6},{8,9},{9,8},{10,11... | collective-permute-start | bytes 1572872 | tf_op jit(solution)/shard_map/ppermute | solution.py:36
  7.4 10.3 %collective-permute-start.3 = (bf16[2,2,128,256]{3,2,1,0:T(8,128)(2,1)S(1)}, bf16[2,2,128,256]{3,2,1,0:T(8,128)(2,1)S(1)}, u32[]{:S(2)}, u32[]{:S(2)}) collective-permute-start(bf16[2,2,128,256]{3,2,1,0:T(8,128)(2,1)S(1)} %both_rows.2.refs_1_), channel_id=1, source_target_pairs={{0,4},{4,8},{8,12},{12,0},{1,5},{5,9},{9,13},{13,1},{2,6},{6,10},{... | collective-permute-start | bytes 786440 | tf_op jit(solution)/shard_map/ppermute | solution.py:27
  11.9 2.1 %collective-permute-start.2 = (bf16[1,2,128,256]{3,2,1,0:T(8,128)(2,1)S(1)}, bf16[1,2,128,256]{3,2,1,0:T(8,128)(2,1)S(1)}, u32[]{:S(2)}, u32[]{:S(2)}) collective-permute-start(bf16[1,2,128,256]{3,2,1,0:T(8,128)(2,1)S(1)} %other_side.1), channel_id=1, source_target_pairs={{0,1},{1,0},{2,3},{3,2},{4,5},{5,4},{6,7},{7,6},{8,9},{9,8},{10,11... | collective-permute-start | bytes 393224 | tf_op jit(solution)/shard_map/ppermute | solution.py:36
  12.2 9.2 %collective-permute-start.6 = (bf16[2,2,128,256]{3,2,1,0:T(8,128)(2,1)S(1)}, bf16[2,2,128,256]{3,2,1,0:T(8,128)(2,1)S(1)}, u32[]{:S(2)}, u32[]{:S(2)}) collective-permute-start(bf16[2,2,128,256]{3,2,1,0:T(8,128)(2,1)S(1)} %head_parts.7), channel_id=1, source_target_pairs={{0,2},{2,0},{1,3},{3,1},{4,6},{6,4},{5,7},{7,5},{8,10},{10,8},{9,1... | collective-permute-start | bytes 786440 | tf_op jit(solution)/shard_map/ppermute | solution.py:32
  14.2 11.0 %collective-permute-start.4 = (bf16[2,2,128,256]{3,2,1,0:T(8,128)(2,1)S(1)}, bf16[2,2,128,256]{3,2,1,0:T(8,128)(2,1)S(1)}, u32[]{:S(2)}, u32[]{:S(2)}) collective-permute-start(bf16[2,2,128,256]{3,2,1,0:T(8,128)(2,1)S(1)} %both_rows.3.refs_2_.refs_0_), channel_id=1, source_target_pairs={{0,4},{4,8},{8,12},{12,0},{1,5},{5,9},{9,13},{13,1},{2,6},{6,10},{... | collective-permute-start | bytes 786440 | tf_op jit(solution)/shard_map/ppermute | solution.py:27
  17.9 10.8 %collective-permute-start.14 = (bf16[2,2,128,256]{3,2,1,0:T(8,128)(2,1)S(1)}, bf16[2,2,128,256]{3,2,1,0:T(8,128)(2,1)S(1)}, u32[]{:S(2)}, u32[]{:S(2)}) collective-permute-start(bf16[2,2,128,256]{3,2,1,0:T(8,128)(2,1)S(1)} %head_parts.9), channel_id=1, source_target_pairs={{0,2},{2,0},{1,3},{3,1},{4,6},{6,4},{5,7},{7,5},{8,10},{10,8},{9,1... | collective-permute-start | bytes 786440 | tf_op jit(solution)/shard_map/ppermute | solution.py:32
  19.7 14.1 %collective-permute-start.15 = (bf16[2,2,128,256]{3,2,1,0:T(8,128)(2,1)S(1)}, bf16[2,2,128,256]{3,2,1,0:T(8,128)(2,1)S(1)}, u32[]{:S(2)}, u32[]{:S(2)}) collective-permute-start(bf16[2,2,128,256]{3,2,1,0:T(8,128)(2,1)S(1)} %head_parts.8.refs_1_), channel_id=1, source_target_pairs={{0,4},{4,8},{8,12},{12,0},{1,5},{5,9},{9,13},{13,1},{2,6},{6,10},{... | collective-permute-start | bytes 786440 | tf_op jit(solution)/shard_map/ppermute | solution.py:27
  21.5 12.3 %collective-permute-start.17 = (bf16[2,2,128,256]{3,2,1,0:T(8,128)(2,1)S(1)}, bf16[2,2,128,256]{3,2,1,0:T(8,128)(2,1)S(1)}, u32[]{:S(2)}, u32[]{:S(2)}) collective-permute-start(bf16[2,2,128,256]{3,2,1,0:T(8,128)(2,1)S(1)} %head_parts.11), channel_id=1, source_target_pairs={{0,2},{2,0},{1,3},{3,1},{4,6},{6,4},{5,7},{7,5},{8,10},{10,8},{9,1... | collective-permute-start | bytes 786440 | tf_op jit(solution)/shard_map/ppermute | solution.py:32
  28.8 7.0 %collective-permute-start.16 = (bf16[2,2,128,256]{3,2,1,0:T(8,128)(2,1)S(1)}, bf16[2,2,128,256]{3,2,1,0:T(8,128)(2,1)S(1)}, u32[]{:S(2)}, u32[]{:S(2)}) collective-permute-start(bf16[2,2,128,256]{3,2,1,0:T(8,128)(2,1)S(1)} %relayed.3), channel_id=1, source_target_pairs={{0,4},{4,8},{8,12},{1,5},{5,9},{9,13},{2,6},{6,10},{10,14},{3,7},{... | collective-permute-start | bytes 786440 | tf_op jit(solution)/shard_map/ppermute | solution.py:27
  30.8 16.8 %collective-permute-start.7 = (bf16[2,2,2,128,256]{4,3,2,1,0:T(8,128)(2,1)S(1)}, bf16[2,2,2,128,256]{4,3,2,1,0:T(8,128)(2,1)S(1)}, u32[]{:S(2)}, u32[]{:S(2)}) collective-permute-start(bf16[2,2,2,128,256]{4,3,2,1,0:T(8,128)(2,1)S(1)} %get-tuple-element.39), channel_id=1, source_target_pairs={{4,0},{8,4},{12,8},{5,1},{9,5},{13,9},{6,2},{10,6},{14,10},{7,3},{... | collective-permute-start | bytes 1572872 | tf_op jit(solution)/shard_map/ppermute | solution.py:27
  32.1 7.2 %collective-permute-start.8 = (bf16[2,128,256]{2,1,0:T(8,128)(2,1)S(1)}, bf16[2,128,256]{2,1,0:T(8,128)(2,1)S(1)}, u32[]{:S(2)}, u32[]{:S(2)}) collective-permute-start(bf16[2,128,256]{2,1,0:T(8,128)(2,1)S(1)} %get-tuple-element.40), channel_id=1, source_target_pairs={{0,2},{2,0},{1,3},{3,1},{4,6},{6,4},{5,7},{7,5},{8,10},{10,8},{9,1... | collective-permute-start | bytes 393224 | tf_op jit(solution)/shard_map/ppermute | solution.py:32
  39.4 13.3 %collective-permute-start.22 = (bf16[2,2,128,256]{3,2,1,0:T(8,128)(2,1)S(1)}, bf16[2,2,128,256]{3,2,1,0:T(8,128)(2,1)S(1)}, u32[]{:S(2)}, u32[]{:S(2)}) collective-permute-start(bf16[2,2,128,256]{3,2,1,0:T(8,128)(2,1)S(1)} %relayed.5), channel_id=1, source_target_pairs={{4,0},{8,4},{12,8},{5,1},{9,5},{13,9},{6,2},{10,6},{14,10},{7,3},{... | collective-permute-start | bytes 786440 | tf_op jit(solution)/shard_map/ppermute | solution.py:27
  40.7 9.9 %collective-permute-start.19 = (bf16[2,128,256]{2,1,0:T(8,128)(2,1)S(1)}, bf16[2,128,256]{2,1,0:T(8,128)(2,1)S(1)}, u32[]{:S(2)}, u32[]{:S(2)}) collective-permute-start(bf16[2,128,256]{2,1,0:T(8,128)(2,1)S(1)} %get-tuple-element.56), channel_id=1, source_target_pairs={{0,2},{2,0},{1,3},{3,1},{4,6},{6,4},{5,7},{7,5},{8,10},{10,8},{9,1... | collective-permute-start | bytes 393224 | tf_op jit(solution)/shard_map/ppermute | solution.py:32
  47.6 8.6 %collective-permute-start.11 = (bf16[2,2,128,256]{3,2,1,0:T(8,128)(2,1)S(1)}, bf16[2,2,128,256]{3,2,1,0:T(8,128)(2,1)S(1)}, u32[]{:S(2)}, u32[]{:S(2)}) collective-permute-start(bf16[2,2,128,256]{3,2,1,0:T(8,128)(2,1)S(1)} %get-tuple-element.47), channel_id=1, source_target_pairs={{0,2},{2,0},{1,3},{3,1},{4,6},{6,4},{5,7},{7,5},{8,10},{10,8},{9,1... | collective-permute-start | bytes 786440 | tf_op jit(solution)/shard_map/ppermute | solution.py:32
  49.2 8.3 %collective-permute-start.18 = (bf16[2,2,128,256]{3,2,1,0:T(8,128)(2,1)S(1)}, bf16[2,2,128,256]{3,2,1,0:T(8,128)(2,1)S(1)}, u32[]{:S(2)}, u32[]{:S(2)}) collective-permute-start(bf16[2,2,128,256]{3,2,1,0:T(8,128)(2,1)S(1)} %relayed.4), channel_id=1, source_target_pairs={{4,0},{8,4},{12,8},{5,1},{9,5},{13,9},{6,2},{10,6},{14,10},{7,3},{... | collective-permute-start | bytes 786440 | tf_op jit(solution)/shard_map/ppermute | solution.py:27
  52.7 6.9 %collective-permute-start.23 = (bf16[2,2,128,256]{3,2,1,0:T(8,128)(2,1)S(1)}, bf16[2,2,128,256]{3,2,1,0:T(8,128)(2,1)S(1)}, u32[]{:S(2)}, u32[]{:S(2)}) collective-permute-start(bf16[2,2,128,256]{3,2,1,0:T(8,128)(2,1)S(1)} %summed.3), channel_id=1, source_target_pairs={{0,2},{2,0},{1,3},{3,1},{4,6},{6,4},{5,7},{7,5},{8,10},{10,8},{9,1... | collective-permute-start | bytes 786440 | tf_op jit(solution)/shard_map/ppermute | solution.py:32
  54.8 4.9 %collective-permute-start.10 = (bf16[2,128,256]{2,1,0:T(8,128)(2,1)S(1)}, bf16[2,128,256]{2,1,0:T(8,128)(2,1)S(1)}, u32[]{:S(2)}, u32[]{:S(2)}) collective-permute-start(bf16[2,128,256]{2,1,0:T(8,128)(2,1)S(1)} %get-tuple-element.46), channel_id=1, source_target_pairs={{0,1},{1,0},{2,3},{3,2},{4,5},{5,4},{6,7},{7,6},{8,9},{9,8},{10,11... | collective-permute-start | bytes 393224 | tf_op jit(solution)/shard_map/ppermute | solution.py:36
  54.9 5.4 %collective-permute-start.9 = (bf16[2,1,128,256]{3,2,0,1:T(8,128)(2,1)S(1)}, bf16[2,1,128,256]{3,2,0,1:T(8,128)(2,1)S(1)}, u32[]{:S(2)}, u32[]{:S(2)}) collective-permute-start(bf16[2,1,128,256]{3,2,0,1:T(8,128)(2,1)S(1)} %bitcast.7), channel_id=1, source_target_pairs={{0,1},{1,0},{2,3},{3,2},{4,5},{5,4},{6,7},{7,6},{8,9},{9,8},{10,11... | collective-permute-start | bytes 393224 | tf_op jit(solution)/shard_map/ppermute | solution.py:36
  56.2 4.2 %collective-permute-start.21 = (bf16[2,128,256]{2,1,0:T(8,128)(2,1)S(1)}, bf16[2,128,256]{2,1,0:T(8,128)(2,1)S(1)}, u32[]{:S(2)}, u32[]{:S(2)}) collective-permute-start(bf16[2,128,256]{2,1,0:T(8,128)(2,1)S(1)} %get-tuple-element.59), channel_id=1, source_target_pairs={{0,1},{1,0},{2,3},{3,2},{4,5},{5,4},{6,7},{7,6},{8,9},{9,8},{10,11... | collective-permute-start | bytes 393224 | tf_op jit(solution)/shard_map/ppermute | solution.py:36
  57.5 3.6 %collective-permute-start.12 = (bf16[2,1,128,256]{3,2,1,0:T(8,128)(2,1)S(1)}, bf16[2,1,128,256]{3,2,1,0:T(8,128)(2,1)S(1)}, u32[]{:S(2)}, u32[]{:S(2)}) collective-permute-start(bf16[2,1,128,256]{3,2,1,0:T(8,128)(2,1)S(1)} %get-tuple-element.49), channel_id=1, source_target_pairs={{0,1},{1,0},{2,3},{3,2},{4,5},{5,4},{6,7},{7,6},{8,9},{9,8},{10,11... | collective-permute-start | bytes 393224 | tf_op jit(solution)/shard_map/ppermute | solution.py:36
  59.7 1.3 %collective-permute-start.20 = (bf16[2,128,256]{2,1,0:T(8,128)(2,1)S(1)}, bf16[2,128,256]{2,1,0:T(8,128)(2,1)S(1)}, u32[]{:S(2)}, u32[]{:S(2)}) collective-permute-start(bf16[2,128,256]{2,1,0:T(8,128)(2,1)S(1)} %get-tuple-element.58), channel_id=1, source_target_pairs={{0,1},{1,0},{2,3},{3,2},{4,5},{5,4},{6,7},{7,6},{8,9},{9,8},{10,11... | collective-permute-start | bytes 393224 | tf_op jit(solution)/shard_map/ppermute | solution.py:36
  59.7 1.6 %collective-permute-start.24 = (bf16[2,1,128,256]{3,2,1,0:T(8,128)(2,1)S(1)}, bf16[2,1,128,256]{3,2,1,0:T(8,128)(2,1)S(1)}, u32[]{:S(2)}, u32[]{:S(2)}) collective-permute-start(bf16[2,1,128,256]{3,2,1,0:T(8,128)(2,1)S(1)} %get-tuple-element.62), channel_id=1, source_target_pairs={{0,1},{1,0},{2,3},{3,2},{4,5},{5,4},{6,7},{7,6},{8,9},{9,8},{10,11... | collective-permute-start | bytes 393224 | tf_op jit(solution)/shard_map/ppermute | solution.py:36

commit v21 on v11

--- a/solution.py
+++ b/solution.py
@@ -328,7 +328,7 @@
         own_earlier.append(along_blocks(kv_own[index][0], 1, True))
         qg_sends.append(head_parts(*qg_parts[index], others, qg[index - 1] if index else []))
         qg.append([round_sub(value, by) for by, value in zip(others, qg_sends[index])])
-    kept, paired = [], []
+    kept, paired, back, release = [], [], [], []
     for index in range(count):
         last = index == count - 1
         forward = [relayed(value, [first_dq]) if index else value for value in kv[index]]
@@ -338,12 +338,14 @@
         first_dq = dq[0]
         dq = [dq[0]] + [round_sub(dq[by], by) for by in others]
         if last:
-            later = [along_blocks(value, -1, True) for value in early[1:]]
+            later = [along_blocks(relayed(value, back), -1, False) for value in early[1:]]
             dkv = summed(grads, later, others, dq[1:])
-            near = along_blocks(relayed(early[0], dkv), -1, True)
+            near = along_blocks(relayed(early[0], release), -1, False)
             dkv = summed(grads, [near], [0], []) + [round_sub(value, by) for by, value in zip(others, dkv)]
         else:
+            back = dq[1:]
             dkv = summed(grads, [along_blocks(early[0], -1, False)], [0] + others, dq[1:])
+            release = dkv[:1]
             dkv = [dkv[0]] + [round_sub(dkv[by], by) for by in others]
         send, keep = rows_for_pair(dq, dkv)
         kept.append(keep)

time: 65.1 us -> 63 us (0.968)
  starting transfers between devices: 23.3 us -> 22.1 us
  waiting for transfers between devices: 26.7 us -> 25.6 us
    ppermute x8, waiting for transfers between devices: 14.6 us -> 5.99 us  [round_sub(): lax.ppermute(value, 'sub', [(i, (i + by) % peers) for i in range(peers)])]
    ppermute x7, waiting for transfers between devices: 10.4 us -> 17.9 us  [along_blocks(): return lax.ppermute(value, 'blk', pairs)]
    ppermute x7, starting transfers between devices: 13.2 us -> 10.4 us  [along_blocks(): return lax.ppermute(value, 'blk', pairs)]
    ppermute x8, starting transfers between devices: 8.83 us -> 10.5 us  [round_sub(): lax.ppermute(value, 'sub', [(i, (i + by) % peers) for i in range(peers)])]
    pallas_call x18 -> x19, Pallas kernels: 10.3 us -> 10.3 us  [call(): pl.pallas_call(kernel, out_shape=outs, in_specs=[spec] * len(ins), out_sp...]
  transfers between devices with their start and end apart: 20 -> 20, of which waited for: 9 -> 9; matrix products, arithmetic and copies ran while one was open for 1% -> 1% of each run, Pallas kernels for 16% -> 17%
where the time goes in v21:
time: 63 us; the launch traced here: 62.6 us
  waiting for transfers between devices  25.6 us (41%)
  starting transfers between devices  22.1 us (35%)
  Pallas kernels  13.1 us (21%)
  between operations  0.92 us (1%)
  other arithmetic  0.79 us (1%)
    ppermute x7, waiting for transfers between devices, along_blocks(): return lax.ppermute(value, 'blk', pairs)  17.9 us
    ppermute x8, starting transfers between devices, round_sub(): lax.ppermute(value, 'sub', [(i, (i + by) % peers) for i in range(peers)])  10.5 us
    ppermute x7, starting transfers between devices, along_blocks(): return lax.ppermute(value, 'blk', pairs)  10.4 us
    pallas_call x19, Pallas kernels, call(): pl.pallas_call(kernel, out_shape=outs, in_specs=[spec] * len(ins), out_sp...  10.3 us
    ppermute x8, waiting for transfers between devices, round_sub(): lax.ppermute(value, 'sub', [(i, (i + by) % peers) for i in range(peers)])  5.99 us
    pallas_call x2, Pallas kernels, first_parts(): pl.pallas_call(kernel, out_shape=outs, in_specs=[spec] * (len(held) + len...  2.78 us
    ppermute x5, waiting for transfers between devices, swapped(): return lax.ppermute(value, 'pair', [(0, 1), (1, 0)])  1.71 us
  transfers between devices with their start and end apart: 20, of which 9 were waited for; matrix products, arithmetic and copies ran while one was open for 1% of the time, Pallas kernels for 17%

profile of v21, /device:TPU:0, one launch (start us, length us, event | category | flops | bytes accessed | tf_op | source)
XLA Modules:
  0.0 62.6 jit_solution(15848407192809496525)
XLA Ops:
  0.6 1.1 %first_parts.2 = (bf16[2,2,128,256]{3,2,1,0:T(8,128)(2,1)S(1)}, bf16[2,2,128,256]{3,2,1,0:T(8,128)(2,1)S(1)}) custom-call(bf16[128,2048]{1,0:T(8,128)(2,1)} %refs_2_.1, bf16[128,2048]{1,0:T(8,128)(2,1)} %refs_3_.1), custom_call_target="tpu_custom_call" | custom-call | tf_op jit(solution)/shard_map/first_parts/pallas_call | solution.py:92
  1.8 0.5 collective-permute-start
  2.3 1.6 %first_parts.3 = (bf16[2,2,128,256]{3,2,1,0:T(8,128)(2,1)S(1)}, bf16[2,2,128,256]{3,2,1,0:T(8,128)(2,1)S(1)}, bf16[4,2,128,256]{3,2,1,0:T(8,128)(2,1)S(1)}, bf16[4,2,128,256]{3,2,1,0:T(8,128)(2,1)S(1)}) custom-call(bf16[128,2048]{1,0:T(8,128)(2,1)} %refs_4_.1, bf16[128,2048]{1,0:T(8,128)(2,1)} %refs_5_.1, bf16[128,2048]{1,0:T(8,128)(2,1)} %refs_2_.1, ...), custom_call_target="tpu_custom_call" | custom-call | tf_op jit(solution)/shard_map/first_parts/pallas_call | solution.py:92
  3.9 0.1 collective-permute-start.4
  4.1 0.5 collective-permute-start.9
  4.6 0.1 pad_dynamic-slice_fusion
  4.7 0.2 head_parts.9
  4.8 2.6 %collective-permute-start.1 = (bf16[2,2,128,256]{3,2,1,0:T(8,128)(2,1)S(1)}, bf16[2,2,128,256]{3,2,1,0:T(8,128)(2,1)S(1)}, u32[]{:S(2)}, u32[]{:S(2)}) collective-permute-start(bf16[2,2,128,256]{3,2,1,0:T(8,128)(2,1)S(1)} %head_parts.9), channel_id=1, source_target_pairs={{0,2},{2,0},{1,3},{3,1},{4,6},{6,4},{5,7},{7,5},{8,10},{10,8},{9,1... | collective-permute-start | bytes 786440 | tf_op jit(solution)/shard_map/ppermute | solution.py:32
  7.5 0.2 head_parts.8.refs_1_
  7.7 1.6 %collective-permute-start.2 = (bf16[2,2,128,256]{3,2,1,0:T(8,128)(2,1)S(1)}, bf16[2,2,128,256]{3,2,1,0:T(8,128)(2,1)S(1)}, u32[]{:S(2)}, u32[]{:S(2)}) collective-permute-start(bf16[2,2,128,256]{3,2,1,0:T(8,128)(2,1)S(1)} %head_parts.8.refs_1_), channel_id=1, source_target_pairs={{0,4},{4,8},{8,12},{12,0},{1,5},{5,9},{9,13},{13,1},{2,6},{6,10},{... | collective-permute-start | bytes 786440 | tf_op jit(solution)/shard_map/ppermute | solution.py:27
  9.3 0.2 head_parts.11
  9.5 0.6 collective-permute-start.5
  10.1 4.5 %collective-permute-done.1.refs_2_.refs_0_ = bf16[2,2,128,256]{3,2,1,0:T(8,128)(2,1)S(1)} collective-permute-done((bf16[2,2,128,256]{3,2,1,0:T(8,128)(2,1)S(1)}, bf16[2,2,128,256]{3,2,1,0:T(8,128)(2,1)S(1)}, u32[]{:S(2)}, u32[]{:S(2)}) %collective-permute-start.1) | collective-permute-done | bytes 262176 | tf_op jit(solution)/shard_map/ppermute | solution.py:32
  14.6 0.2 head_parts.13
  14.8 2.0 %collective-permute-start.10 = (bf16[2,2,128,256]{3,2,1,0:T(8,128)(2,1)S(1)}, bf16[2,2,128,256]{3,2,1,0:T(8,128)(2,1)S(1)}, u32[]{:S(2)}, u32[]{:S(2)}) collective-permute-start(bf16[2,2,128,256]{3,2,1,0:T(8,128)(2,1)S(1)} %head_parts.13), channel_id=1, source_target_pairs={{0,2},{2,0},{1,3},{3,1},{4,6},{6,4},{5,7},{7,5},{8,10},{10,8},{9,1... | collective-permute-start | bytes 786440 | tf_op jit(solution)/shard_map/ppermute | solution.py:32
  16.8 1.6 %collective-permute-start.3 = (bf16[2,2,128,256]{3,2,1,0:T(8,128)(2,1)S(1)}, bf16[2,2,128,256]{3,2,1,0:T(8,128)(2,1)S(1)}, u32[]{:S(2)}, u32[]{:S(2)}) collective-permute-start(bf16[2,2,128,256]{3,2,1,0:T(8,128)(2,1)S(1)} %collective-permute-done.1.refs_2_.refs_0_), channel_id=1, source_target_pairs={{0,4},{4,8},{8,12},{12,0},{1,5},{5,9},{9,13},{13,1},{2,6},{6,10},{... | collective-permute-start | bytes 786440 | tf_op jit(solution)/shard_map/ppermute | solution.py:27
  18.4 0.7 %and_select_fusion = (f32[1,768,256]{2,1,0:T(8,128)S(1)}, f32[1,768,256]{2,1,0:T(8,128)S(1)}) fusion(s32[256]{0:T(256)S(1)} %get-tuple-element.54, s32[256]{0:T(256)S(1)} %get-tuple-element.52, s32[768]{0:T(1024)S(1)} %get-tuple-element.50, s32[768]{0:T(1024)S(1)} %get-tuple-element.48, pred[768]{0:T(1024)(128)(4,1)S(1)} %get-tuple-element.46, ...), kind=kLoop, calls=%fused_computation.1 | loop fusion | flops 1966080 | bytes 1590784 | tf_op jit(solution)/shard_map/jit(_where)/select_n | solution.py:299
  19.1 0.1 pad_maximum_fusion.refs_0_
  19.2 0.2 head_parts.10.refs_5_
  19.4 0.2 head_parts.12.refs_1_
  19.6 1.6 %collective-permute-start.11 = (bf16[2,2,128,256]{3,2,1,0:T(8,128)(2,1)S(1)}, bf16[2,2,128,256]{3,2,1,0:T(8,128)(2,1)S(1)}, u32[]{:S(2)}, u32[]{:S(2)}) collective-permute-start(bf16[2,2,128,256]{3,2,1,0:T(8,128)(2,1)S(1)} %head_parts.12.refs_1_), channel_id=1, source_target_pairs={{0,4},{4,8},{8,12},{12,0},{1,5},{5,9},{9,13},{13,1},{2,6},{6,10},{... | collective-permute-start | bytes 786440 | tf_op jit(solution)/shard_map/ppermute | solution.py:27
  21.3 0.2 head_parts.15
  21.4 1.0 %collective-permute-start.13 = (bf16[2,2,128,256]{3,2,1,0:T(8,128)(2,1)S(1)}, bf16[2,2,128,256]{3,2,1,0:T(8,128)(2,1)S(1)}, u32[]{:S(2)}, u32[]{:S(2)}) collective-permute-start(bf16[2,2,128,256]{3,2,1,0:T(8,128)(2,1)S(1)} %head_parts.15), channel_id=1, source_target_pairs={{0,2},{2,0},{1,3},{3,1},{4,6},{6,4},{5,7},{7,5},{8,10},{10,8},{9,1... | collective-permute-start | bytes 786440 | tf_op jit(solution)/shard_map/ppermute | solution.py:32
  22.4 5.4 %collective-permute-done.3.refs_4_ = bf16[2,2,128,256]{3,2,1,0:T(8,128)(2,1)S(1)} collective-permute-done((bf16[2,2,128,256]{3,2,1,0:T(8,128)(2,1)S(1)}, bf16[2,2,128,256]{3,2,1,0:T(8,128)(2,1)S(1)}, u32[]{:S(2)}, u32[]{:S(2)}) %collective-permute-start.3) | collective-permute-done | bytes 262176 | tf_op jit(solution)/shard_map/ppermute | solution.py:27
  27.9 3.5 %attention_grads.2 = (f32[2,2,2,128,256]{4,3,2,1,0:T(8,128)S(1)}, bf16[2,128,256]{2,1,0:T(8,128)(2,1)S(1)}, bf16[2,128,256]{2,1,0:T(8,128)(2,1)S(1)}, bf16[2,2,2,128,256]{4,3,2,1,0:T(8,128)(2,1)S(1)}) custom-call(f32[2,768,256]{2,1,0:T(8,128)S(1)} %pad_maximum_fusion.refs_0_, bf16[2,2,128,256]{3,2,1,0:T(8,128)(2,1)S(1)} %head_parts.8.refs_1_, ...), custom_call_target="tpu_custom_call" | custom-call | flops 1006632960 | bytes 4980736 | tf_op jit(solution)/shard_map/attention_grads/pallas_call | solution.py:51
  31.5 1.7 %collective-permute-start.12 = (bf16[2,2,128,256]{3,2,1,0:T(8,128)(2,1)S(1)}, bf16[2,2,128,256]{3,2,1,0:T(8,128)(2,1)S(1)}, u32[]{:S(2)}, u32[]{:S(2)}) collective-permute-start(bf16[2,2,128,256]{3,2,1,0:T(8,128)(2,1)S(1)} %relayed.3), channel_id=1, source_target_pairs={{0,4},{4,8},{8,12},{1,5},{5,9},{9,13},{2,6},{6,10},{10,14},{3,7},{... | collective-permute-start | bytes 786440 | tf_op jit(solution)/shard_map/ppermute | solution.py:27
  33.2 1.3 %collective-permute-start.7 = (bf16[2,2,2,128,256]{4,3,2,1,0:T(8,128)(2,1)S(1)}, bf16[2,2,2,128,256]{4,3,2,1,0:T(8,128)(2,1)S(1)}, u32[]{:S(2)}, u32[]{:S(2)}) collective-permute-start(bf16[2,2,2,128,256]{4,3,2,1,0:T(8,128)(2,1)S(1)} %get-tuple-element.31), channel_id=1, source_target_pairs={{4,0},{8,4},{12,8},{5,1},{9,5},{13,9},{6,2},{10,6},{14,10},{7,3},{... | collective-permute-start | bytes 1572872 | tf_op jit(solution)/shard_map/ppermute | solution.py:27
  34.5 0.6 collective-permute-start.6
  35.1 0.2 head_parts.14.refs_5_
  35.3 1.8 %collective-permute-done.12.refs_4_ = bf16[2,2,128,256]{3,2,1,0:T(8,128)(2,1)S(1)} collective-permute-done((bf16[2,2,128,256]{3,2,1,0:T(8,128)(2,1)S(1)}, bf16[2,2,128,256]{3,2,1,0:T(8,128)(2,1)S(1)}, u32[]{:S(2)}, u32[]{:S(2)}) %collective-permute-start.12) | collective-permute-done | bytes 262176 | tf_op jit(solution)/shard_map/ppermute | solution.py:27
  37.0 3.5 %attention_grads.3 = (f32[2,2,2,128,256]{4,3,2,1,0:T(8,128)S(1)}, bf16[2,128,256]{2,1,0:T(8,128)(2,1)S(1)}, bf16[2,128,256]{2,1,0:T(8,128)(2,1)S(1)}, bf16[2,2,1...) custom-call(f32[2,768,256]{2,1,0:T(8,128)S(1)} %pad_maximum_fusion.refs_0_, ...), custom_call_target="tpu_custom_call" | custom-call | flops 1006632960 | bytes 4980736 | tf_op jit(solution)/shard_map/attention_grads/pallas_call | solution.py:51
  40.6 1.3 %collective-permute-start.16 = (bf16[2,2,128,256]{3,2,1,0:T(8,128)(2,1)S(1)}, bf16[2,2,128,256]{3,2,1,0:T(8,128)(2,1)S(1)}, u32[]{:S(2)}, u32[]{:S(2)}) collective-permute-start(bf16[2,2,128,256]{3,2,1,0:T(8,128)(2,1)S(1)} %relayed.5), channel_id=1, source_target_pairs={{4,0},{8,4},{12,8},{5,1},{9,5},{13,9},{6,2},{10,6},{14,10},{7,3},{... | collective-permute-start | bytes 786440 | tf_op jit(solution)/shard_map/ppermute | solution.py:27
  41.9 0.6 collective-permute-start.14
  42.5 5.8 %collective-permute-done.7.refs_0_ = bf16[2,2,2,128,256]{4,3,2,1,0:T(8,128)(2,1)S(1)} collective-permute-done((bf16[2,2,2,128,256]{4,3,2,1,0:T(8,128)(2,1)S(1)}, bf16[2,2,2,128,256]{4,3,2,1,0:T(8,128)(2,1)S(1)}, u32[]{:S(2)}, u32[]{:S(2)}) %collective-permute-start.7) | collective-permute-done | bytes 524320 | tf_op jit(solution)/shard_map/ppermute | solution.py:27
  48.4 0.1 summed.3
  48.5 1.5 %collective-permute-start.8 = (bf16[2,2,128,256]{3,2,1,0:T(8,128)(2,1)S(1)}, bf16[2,2,128,256]{3,2,1,0:T(8,128)(2,1)S(1)}, u32[]{:S(2)}, u32[]{:S(2)}) collective-permute-start(bf16[2,2,128,256]{3,2,1,0:T(8,128)(2,1)S(1)} %get-tuple-element.33), channel_id=1, source_target_pairs={{0,2},{2,0},{1,3},{3,1},{4,6},{6,4},{5,7},{7,5},{8,10},{10,8},{9,1... | collective-permute-start | bytes 786440 | tf_op jit(solution)/shard_map/ppermute | solution.py:32
  50.0 1.3 %collective-permute-start.15 = (bf16[2,2,128,256]{3,2,1,0:T(8,128)(2,1)S(1)}, bf16[2,2,128,256]{3,2,1,0:T(8,128)(2,1)S(1)}, u32[]{:S(2)}, u32[]{:S(2)}) collective-permute-start(bf16[2,2,128,256]{3,2,1,0:T(8,128)(2,1)S(1)} %relayed.4), channel_id=1, source_target_pairs={{4,0},{8,4},{12,8},{5,1},{9,5},{13,9},{6,2},{10,6},{14,10},{7,3},{... | collective-permute-start | bytes 786440 | tf_op jit(solution)/shard_map/ppermute | solution.py:27
  51.3 1.6 %collective-permute-done.16.refs_0_ = bf16[2,2,128,256]{3,2,1,0:T(8,128)(2,1)S(1)} collective-permute-done((bf16[2,2,128,256]{3,2,1,0:T(8,128)(2,1)S(1)}, bf16[2,2,128,256]{3,2,1,0:T(8,128)(2,1)S(1)}, u32[]{:S(2)}, u32[]{:S(2)}) %collective-permute-start.16) | collective-permute-done | bytes 262176 | tf_op jit(solution)/shard_map/ppermute | solution.py:27
  53.0 1.5 %collective-permute-start.17 = (bf16[2,2,128,256]{3,2,1,0:T(8,128)(2,1)S(1)}, bf16[2,2,128,256]{3,2,1,0:T(8,128)(2,1)S(1)}, u32[]{:S(2)}, u32[]{:S(2)}) collective-permute-start(bf16[2,2,128,256]{3,2,1,0:T(8,128)(2,1)S(1)} %summed.5), channel_id=1, source_target_pairs={{0,2},{2,0},{1,3},{3,1},{4,6},{6,4},{5,7},{7,5},{8,10},{10,8},{9,1... | collective-permute-start | bytes 786440 | tf_op jit(solution)/shard_map/ppermute | solution.py:32
  54.6 0.3 collective-permute-done.8.refs_3_
  54.9 0.1 rows_for_pair.2
  55.0 0.1 collective-permute-start.18
  55.0 3.3 %collective-permute-done.15.refs_0_ = bf16[2,2,128,256]{3,2,1,0:T(8,128)(2,1)S(1)} collective-permute-done((bf16[2,2,128,256]{3,2,1,0:T(8,128)(2,1)S(1)}, bf16[2,2,128,256]{3,2,1,0:T(8,128)(2,1)S(1)}, u32[]{:S(2)}, u32[]{:S(2)}) %collective-permute-start.15) | collective-permute-done | bytes 262176 | tf_op jit(solution)/shard_map/ppermute | solution.py:27
  58.4 1.1 %collective-permute-done.17.refs_3_ = bf16[2,2,128,256]{3,2,1,0:T(8,128)(2,1)S(1)} collective-permute-done((bf16[2,2,128,256]{3,2,1,0:T(8,128)(2,1)S(1)}, bf16[2,2,128,256]{3,2,1,0:T(8,128)(2,1)S(1)}, u32[]{:S(2)}, u32[]{:S(2)}) %collective-permute-start.17) | collective-permute-done | bytes 262176 | tf_op jit(solution)/shard_map/ppermute | solution.py:32
  59.5 0.1 rows_for_pair.3
  59.5 0.1 collective-permute-start.19
  59.6 1.7 %collective-permute-done.19.refs_3_ = bf16[3,2,128,256]{3,2,1,0:T(8,128)(2,1)S(1)} collective-permute-done((bf16[3,2,128,256]{3,2,1,0:T(8,128)(2,1)S(1)}, bf16[3,2,128,256]{3,2,1,0:T(8,128)(2,1)S(1)}, u32[]{:S(2)}, u32[]{:S(2)}) %collective-permute-start.19) | collective-permute-done | bytes 393248 | tf_op jit(solution)/shard_map/ppermute | solution.py:36
  61.3 1.3 %laid_out.1 = (bf16[128,2048]{1,0:T(8,128)(2,1)}, bf16[128,2048]{1,0:T(8,128)(2,1)}, bf16[128,2048]{1,0:T(8,128)(2,1)}) custom-call(bf16[3,2,128,256]{3,2,1,0:T(8,128)(2,1)S(1)} %get-tuple-element.34.refs_0_, bf16[3,2,128,256]{3,2,1,0:T(8,128)(2,1)S(1)} %get-tuple-element.42.refs_1_, bf16[3,2,128,256]{3,2,1,0:T(8,128)(2,1)S(1)} %collective-permute-done.18.refs_2_, ...), custom_call_target="tpu_custom_call" | custom-call | bytes 3145728 | tf_op jit(solution)/shard_map/laid_out/pallas_call | solution.py:51
  (24 shorter events, 0.3 us)
Async XLA Ops:
  1.8 2.9 %collective-permute-start = (bf16[2,2,128,256]{3,2,1,0:T(8,128)(2,1)S(1)}, bf16[2,2,128,256]{3,2,1,0:T(8,128)(2,1)S(1)}, u32[]{:S(2)}, u32[]{:S(2)}) collective-permute-start(bf16[2,2,128,256]{3,2,1,0:T(8,128)(2,1)S(1)} %get-tuple-element.25), channel_id=1, source_target_pairs={{0,1},{1,0},{2,3},{3,2},{4,5},{5,4},{6,7},{7,6},{8,9},{9,8},{10,11... | collective-permute-start | bytes 786440 | tf_op jit(solution)/shard_map/ppermute | solution.py:36
  2.3 2.3 %copy-start = (s32[2048]{0:T(1024)S(1)}, s32[2048]{0:T(1024)}, u32[]{:S(2)}) copy-start(s32[2048]{0:T(1024)} %param.9) | copy-start | bytes 24580
  3.9 5.3 %collective-permute-start.4 = (bf16[2,2,128,256]{3,2,1,0:T(8,128)(2,1)S(1)}, bf16[2,2,128,256]{3,2,1,0:T(8,128)(2,1)S(1)}, u32[]{:S(2)}, u32[]{:S(2)}) collective-permute-start(bf16[2,2,128,256]{3,2,1,0:T(8,128)(2,1)S(1)} %get-tuple-element.27), channel_id=1, source_target_pairs={{0,1},{1,0},{2,3},{3,2},{4,5},{5,4},{6,7},{7,6},{8,9},{9,8},{10,11... | collective-permute-start | bytes 786440 | tf_op jit(solution)/shard_map/ppermute | solution.py:36
  4.1 10.6 %collective-permute-start.9 = (bf16[4,2,128,256]{3,2,1,0:T(8,128)(2,1)S(1)}, bf16[4,2,128,256]{3,2,1,0:T(8,128)(2,1)S(1)}, u32[]{:S(2)}, u32[]{:S(2)}) collective-permute-start(bf16[4,2,128,256]{3,2,1,0:T(8,128)(2,1)S(1)} %get-tuple-element.36), channel_id=1, source_target_pairs={{0,1},{1,0},{2,3},{3,2},{4,5},{5,4},{6,7},{7,6},{8,9},{9,8},{10,11... | collective-permute-start | bytes 1572872 | tf_op jit(solution)/shard_map/ppermute | solution.py:36
  4.8 9.8 %collective-permute-start.1 = (bf16[2,2,128,256]{3,2,1,0:T(8,128)(2,1)S(1)}, bf16[2,2,128,256]{3,2,1,0:T(8,128)(2,1)S(1)}, u32[]{:S(2)}, u32[]{:S(2)}) collective-permute-start(bf16[2,2,128,256]{3,2,1,0:T(8,128)(2,1)S(1)} %head_parts.9), channel_id=1, source_target_pairs={{0,2},{2,0},{1,3},{3,1},{4,6},{6,4},{5,7},{7,5},{8,10},{10,8},{9,1... | collective-permute-start | bytes 786440 | tf_op jit(solution)/shard_map/ppermute | solution.py:32
  7.7 11.7 %collective-permute-start.2 = (bf16[2,2,128,256]{3,2,1,0:T(8,128)(2,1)S(1)}, bf16[2,2,128,256]{3,2,1,0:T(8,128)(2,1)S(1)}, u32[]{:S(2)}, u32[]{:S(2)}) collective-permute-start(bf16[2,2,128,256]{3,2,1,0:T(8,128)(2,1)S(1)} %head_parts.8.refs_1_), channel_id=1, source_target_pairs={{0,4},{4,8},{8,12},{12,0},{1,5},{5,9},{9,13},{13,1},{2,6},{6,10},{... | collective-permute-start | bytes 786440 | tf_op jit(solution)/shard_map/ppermute | solution.py:27
  9.5 11.8 %collective-permute-start.5 = (bf16[2,2,128,256]{3,2,1,0:T(8,128)(2,1)S(1)}, bf16[2,2,128,256]{3,2,1,0:T(8,128)(2,1)S(1)}, u32[]{:S(2)}, u32[]{:S(2)}) collective-permute-start(bf16[2,2,128,256]{3,2,1,0:T(8,128)(2,1)S(1)} %head_parts.11), channel_id=1, source_target_pairs={{0,2},{2,0},{1,3},{3,1},{4,6},{6,4},{5,7},{7,5},{8,10},{10,8},{9,1... | collective-permute-start | bytes 786440 | tf_op jit(solution)/shard_map/ppermute | solution.py:32
  14.8 16.6 %collective-permute-start.10 = (bf16[2,2,128,256]{3,2,1,0:T(8,128)(2,1)S(1)}, bf16[2,2,128,256]{3,2,1,0:T(8,128)(2,1)S(1)}, u32[]{:S(2)}, u32[]{:S(2)}) collective-permute-start(bf16[2,2,128,256]{3,2,1,0:T(8,128)(2,1)S(1)} %head_parts.13), channel_id=1, source_target_pairs={{0,2},{2,0},{1,3},{3,1},{4,6},{6,4},{5,7},{7,5},{8,10},{10,8},{9,1... | collective-permute-start | bytes 786440 | tf_op jit(solution)/shard_map/ppermute | solution.py:32
  16.8 11.0 %collective-permute-start.3 = (bf16[2,2,128,256]{3,2,1,0:T(8,128)(2,1)S(1)}, bf16[2,2,128,256]{3,2,1,0:T(8,128)(2,1)S(1)}, u32[]{:S(2)}, u32[]{:S(2)}) collective-permute-start(bf16[2,2,128,256]{3,2,1,0:T(8,128)(2,1)S(1)} %collective-permute-done.1.refs_2_.refs_0_), channel_id=1, source_target_pairs={{0,4},{4,8},{8,12},{12,0},{1,5},{5,9},{9,13},{13,1},{2,6},{6,10},{... | collective-permute-start | bytes 786440 | tf_op jit(solution)/shard_map/ppermute | solution.py:27
  19.6 15.6 %collective-permute-start.11 = (bf16[2,2,128,256]{3,2,1,0:T(8,128)(2,1)S(1)}, bf16[2,2,128,256]{3,2,1,0:T(8,128)(2,1)S(1)}, u32[]{:S(2)}, u32[]{:S(2)}) collective-permute-start(bf16[2,2,128,256]{3,2,1,0:T(8,128)(2,1)S(1)} %head_parts.12.refs_1_), channel_id=1, source_target_pairs={{0,4},{4,8},{8,12},{12,0},{1,5},{5,9},{9,13},{13,1},{2,6},{6,10},{... | collective-permute-start | bytes 786440 | tf_op jit(solution)/shard_map/ppermute | solution.py:27
  21.4 13.8 %collective-permute-start.13 = (bf16[2,2,128,256]{3,2,1,0:T(8,128)(2,1)S(1)}, bf16[2,2,128,256]{3,2,1,0:T(8,128)(2,1)S(1)}, u32[]{:S(2)}, u32[]{:S(2)}) collective-permute-start(bf16[2,2,128,256]{3,2,1,0:T(8,128)(2,1)S(1)} %head_parts.15), channel_id=1, source_target_pairs={{0,2},{2,0},{1,3},{3,1},{4,6},{6,4},{5,7},{7,5},{8,10},{10,8},{9,1... | collective-permute-start | bytes 786440 | tf_op jit(solution)/shard_map/ppermute | solution.py:32
  31.5 5.6 %collective-permute-start.12 = (bf16[2,2,128,256]{3,2,1,0:T(8,128)(2,1)S(1)}, bf16[2,2,128,256]{3,2,1,0:T(8,128)(2,1)S(1)}, u32[]{:S(2)}, u32[]{:S(2)}) collective-permute-start(bf16[2,2,128,256]{3,2,1,0:T(8,128)(2,1)S(1)} %relayed.3), channel_id=1, source_target_pairs={{0,4},{4,8},{8,12},{1,5},{5,9},{9,13},{2,6},{6,10},{10,14},{3,7},{... | collective-permute-start | bytes 786440 | tf_op jit(solution)/shard_map/ppermute | solution.py:27
  33.2 15.2 %collective-permute-start.7 = (bf16[2,2,2,128,256]{4,3,2,1,0:T(8,128)(2,1)S(1)}, bf16[2,2,2,128,256]{4,3,2,1,0:T(8,128)(2,1)S(1)}, u32[]{:S(2)}, u32[]{:S(2)}) collective-permute-start(bf16[2,2,2,128,256]{4,3,2,1,0:T(8,128)(2,1)S(1)} %get-tuple-element.31), channel_id=1, source_target_pairs={{4,0},{8,4},{12,8},{5,1},{9,5},{13,9},{6,2},{10,6},{14,10},{7,3},{... | collective-permute-start | bytes 1572872 | tf_op jit(solution)/shard_map/ppermute | solution.py:27
  34.5 6.1 %collective-permute-start.6 = (bf16[2,128,256]{2,1,0:T(8,128)(2,1)S(1)}, bf16[2,128,256]{2,1,0:T(8,128)(2,1)S(1)}, u32[]{:S(2)}, u32[]{:S(2)}) collective-permute-start(bf16[2,128,256]{2,1,0:T(8,128)(2,1)S(1)} %get-tuple-element.29), channel_id=1, source_target_pairs={{0,2},{2,0},{1,3},{3,1},{4,6},{6,4},{5,7},{7,5},{8,10},{10,8},{9,1... | collective-permute-start | bytes 393224 | tf_op jit(solution)/shard_map/ppermute | solution.py:32
  40.6 12.3 %collective-permute-start.16 = (bf16[2,2,128,256]{3,2,1,0:T(8,128)(2,1)S(1)}, bf16[2,2,128,256]{3,2,1,0:T(8,128)(2,1)S(1)}, u32[]{:S(2)}, u32[]{:S(2)}) collective-permute-start(bf16[2,2,128,256]{3,2,1,0:T(8,128)(2,1)S(1)} %relayed.5), channel_id=1, source_target_pairs={{4,0},{8,4},{12,8},{5,1},{9,5},{13,9},{6,2},{10,6},{14,10},{7,3},{... | collective-permute-start | bytes 786440 | tf_op jit(solution)/shard_map/ppermute | solution.py:27
  41.9 9.4 %collective-permute-start.14 = (bf16[2,128,256]{2,1,0:T(8,128)(2,1)S(1)}, bf16[2,128,256]{2,1,0:T(8,128)(2,1)S(1)}, u32[]{:S(2)}, u32[]{:S(2)}) collective-permute-start(bf16[2,128,256]{2,1,0:T(8,128)(2,1)S(1)} %get-tuple-element.38), channel_id=1, source_target_pairs={{0,2},{2,0},{1,3},{3,1},{4,6},{6,4},{5,7},{7,5},{8,10},{10,8},{9,1... | collective-permute-start | bytes 393224 | tf_op jit(solution)/shard_map/ppermute | solution.py:32
  48.5 6.4 %collective-permute-start.8 = (bf16[2,2,128,256]{3,2,1,0:T(8,128)(2,1)S(1)}, bf16[2,2,128,256]{3,2,1,0:T(8,128)(2,1)S(1)}, u32[]{:S(2)}, u32[]{:S(2)}) collective-permute-start(bf16[2,2,128,256]{3,2,1,0:T(8,128)(2,1)S(1)} %get-tuple-element.33), channel_id=1, source_target_pairs={{0,2},{2,0},{1,3},{3,1},{4,6},{6,4},{5,7},{7,5},{8,10},{10,8},{9,1... | collective-permute-start | bytes 786440 | tf_op jit(solution)/shard_map/ppermute | solution.py:32
  50.0 8.3 %collective-permute-start.15 = (bf16[2,2,128,256]{3,2,1,0:T(8,128)(2,1)S(1)}, bf16[2,2,128,256]{3,2,1,0:T(8,128)(2,1)S(1)}, u32[]{:S(2)}, u32[]{:S(2)}) collective-permute-start(bf16[2,2,128,256]{3,2,1,0:T(8,128)(2,1)S(1)} %relayed.4), channel_id=1, source_target_pairs={{4,0},{8,4},{12,8},{5,1},{9,5},{13,9},{6,2},{10,6},{14,10},{7,3},{... | collective-permute-start | bytes 786440 | tf_op jit(solution)/shard_map/ppermute | solution.py:27
  53.0 6.4 %collective-permute-start.17 = (bf16[2,2,128,256]{3,2,1,0:T(8,128)(2,1)S(1)}, bf16[2,2,128,256]{3,2,1,0:T(8,128)(2,1)S(1)}, u32[]{:S(2)}, u32[]{:S(2)}) collective-permute-start(bf16[2,2,128,256]{3,2,1,0:T(8,128)(2,1)S(1)} %summed.5), channel_id=1, source_target_pairs={{0,2},{2,0},{1,3},{3,1},{4,6},{6,4},{5,7},{7,5},{8,10},{10,8},{9,1... | collective-permute-start | bytes 786440 | tf_op jit(solution)/shard_map/ppermute | solution.py:32
  55.0 4.6 %collective-permute-start.18 = (bf16[3,2,128,256]{3,2,1,0:T(8,128)(2,1)S(1)}, bf16[3,2,128,256]{3,2,1,0:T(8,128)(2,1)S(1)}, u32[]{:S(2)}, u32[]{:S(2)}) collective-permute-start(bf16[3,2,128,256]{3,2,1,0:T(8,128)(2,1)S(1)} %get-tuple-element.43), channel_id=1, source_target_pairs={{0,1},{1,0},{2,3},{3,2},{4,5},{5,4},{6,7},{7,6},{8,9},{9,8},{10,11... | collective-permute-start | bytes 1179656 | tf_op jit(solution)/shard_map/ppermute | solution.py:36
  59.5 1.8 %collective-permute-start.19 = (bf16[3,2,128,256]{3,2,1,0:T(8,128)(2,1)S(1)}, bf16[3,2,128,256]{3,2,1,0:T(8,128)(2,1)S(1)}, u32[]{:S(2)}, u32[]{:S(2)}) collective-permute-start(bf16[3,2,128,256]{3,2,1,0:T(8,128)(2,1)S(1)} %get-tuple-element.44), channel_id=1, source_target_pairs={{0,1},{1,0},{2,3},{3,2},{4,5},{5,4},{6,7},{7,6},{8,9},{9,8},{10,11... | collective-permute-start | bytes 1179656 | tf_op jit(solution)/shard_map/ppermute | solution.py:36

commit v22 on v9

--- a/solution.py
+++ b/solution.py
@@ -1,3 +1,4 @@
+import functools
 import math
 
 import jax
@@ -167,13 +168,17 @@
 
         def finish(head, tile):
             q, g, k, scores, grad_prob = products.pop((head, tile))
-            scores = scores * TO_BITS + bias_ref[tile]
-            peak = jnp.max(scores, axis=0, keepdims=True)
-            weight = jnp.exp2(scores - peak)
-            prob = weight * (1.0 / jnp.sum(weight, axis=0, keepdims=True))
-            prob_low = prob.astype(LOW)
-            row_dot = jnp.sum(prob_low.astype(WIDE) * grad_prob, axis=0, keepdims=True)
-            score_low = (prob * (grad_prob - row_dot)).astype(LOW)
+            cuts = [slice(at, at + HD) for at in range(0, 3 * strip, HD)]
+            scaled = [scores[cut] * TO_BITS + bias_ref[tile, cut] for cut in cuts]
+            peak = jnp.max(functools.reduce(jnp.maximum, scaled), axis=0, keepdims=True)
+            weight = [jnp.exp2(piece - peak) for piece in scaled]
+            inverse = 1.0 / jnp.sum(functools.reduce(jnp.add, weight), axis=0, keepdims=True)
+            prob = [piece * inverse for piece in weight]
+            low = [piece.astype(LOW) for piece in prob]
+            dots = [piece.astype(WIDE) * grad_prob[cut] for piece, cut in zip(low, cuts)]
+            row_dot = jnp.sum(functools.reduce(jnp.add, dots), axis=0, keepdims=True)
+            score_low = [(piece * (grad_prob[cut] - row_dot)).astype(LOW) for piece, cut in zip(prob, cuts)]
+            prob_low, score_low = jnp.concatenate(low, axis=0), jnp.concatenate(score_low, axis=0)
             dq = jnp.dot(k.T, score_low, preferred_element_type=WIDE) * SCALE
             dq_all[tile, :, :, pl.ds(head * HD, HD)] = dq.T.astype(LOW).reshape(peers, rows, HD)
             dk = jnp.dot(score_low, q, preferred_element_type=WIDE) * SCALE

time: 62.4 us -> 62.3 us (level)
  no operation moved by 1% of the time
where the time goes in v22:
time: 62.3 us; the launch traced here: 62 us
  waiting for transfers between devices  24.8 us (40%)
  starting transfers between devices  22.4 us (36%)
  Pallas kernels  13 us (21%)
  between operations  0.9 us (1%)
  other arithmetic  0.79 us (1%)
    ppermute x8, waiting for transfers between devices, round_sub(): lax.ppermute(value, 'sub', [(i, (i + by) % peers) for i in range(peers)])  12.2 us
    ppermute x7, waiting for transfers between devices, along_blocks(): return lax.ppermute(value, 'blk', pairs)  11 us
    ppermute x8, starting transfers between devices, round_sub(): lax.ppermute(value, 'sub', [(i, (i + by) % peers) for i in range(peers)])  10.7 us
    ppermute x7, starting transfers between devices, along_blocks(): return lax.ppermute(value, 'blk', pairs)  10.4 us
    pallas_call x18, Pallas kernels, call(): pl.pallas_call(kernel, out_shape=outs, in_specs=[spec] * len(ins), out_sp...  10.2 us
    pallas_call x2, Pallas kernels, first_parts(): pl.pallas_call(kernel, out_shape=outs, in_specs=[spec] * (len(held) + len...  2.78 us
    ppermute x5, waiting for transfers between devices, swapped(): return lax.ppermute(value, 'pair', [(0, 1), (1, 0)])  1.71 us
  transfers between devices with their start and end apart: 20, of which 10 were waited for; matrix products, arithmetic and copies ran while one was open for 1% of the time, Pallas kernels for 17%

profile of v22, /device:TPU:0, one launch (start us, length us, event | category | flops | bytes accessed | tf_op | source)
XLA Modules:
  0.0 62.0 jit_solution(11708686693769855362)
XLA Ops:
  0.6 1.1 %first_parts.2 = (bf16[2,2,128,256]{3,2,1,0:T(8,128)(2,1)S(1)}, bf16[2,2,128,256]{3,2,1,0:T(8,128)(2,1)S(1)}) custom-call(bf16[128,2048]{1,0:T(8,128)(2,1)} %refs_2_.1, bf16[128,2048]{1,0:T(8,128)(2,1)} %refs_3_.1), custom_call_target="tpu_custom_call" | custom-call | tf_op jit(solution)/shard_map/first_parts/pallas_call | solution.py:93
  1.8 0.5 collective-permute-start
  2.3 1.6 %first_parts.3 = (bf16[2,2,128,256]{3,2,1,0:T(8,128)(2,1)S(1)}, bf16[2,2,128,256]{3,2,1,0:T(8,128)(2,1)S(1)}, bf16[4,2,128,256]{3,2,1,0:T(8,128)(2,1)S(1)}, bf16[4,2,128,256]{3,2,1,0:T(8,128)(2,1)S(1)}) custom-call(bf16[128,2048]{1,0:T(8,128)(2,1)} %refs_4_.1, bf16[128,2048]{1,0:T(8,128)(2,1)} %refs_5_.1, bf16[128,2048]{1,0:T(8,128)(2,1)} %refs_2_.1, ...), custom_call_target="tpu_custom_call" | custom-call | tf_op jit(solution)/shard_map/first_parts/pallas_call | solution.py:93
  3.9 0.1 collective-permute-start.4
  4.1 0.5 collective-permute-start.9
  4.6 0.1 pad_dynamic-slice_fusion
  4.7 0.2 head_parts.9
  4.8 2.6 %collective-permute-start.1 = (bf16[2,2,128,256]{3,2,1,0:T(8,128)(2,1)S(1)}, bf16[2,2,128,256]{3,2,1,0:T(8,128)(2,1)S(1)}, u32[]{:S(2)}, u32[]{:S(2)}) collective-permute-start(bf16[2,2,128,256]{3,2,1,0:T(8,128)(2,1)S(1)} %head_parts.9), channel_id=1, source_target_pairs={{0,2},{2,0},{1,3},{3,1},{4,6},{6,4},{5,7},{7,5},{8,10},{10,8},{9,1... | collective-permute-start | bytes 786440 | tf_op jit(solution)/shard_map/ppermute | solution.py:33
  7.5 0.2 head_parts.8.refs_1_
  7.7 1.6 %collective-permute-start.2 = (bf16[2,2,128,256]{3,2,1,0:T(8,128)(2,1)S(1)}, bf16[2,2,128,256]{3,2,1,0:T(8,128)(2,1)S(1)}, u32[]{:S(2)}, u32[]{:S(2)}) collective-permute-start(bf16[2,2,128,256]{3,2,1,0:T(8,128)(2,1)S(1)} %head_parts.8.refs_1_), channel_id=1, source_target_pairs={{0,4},{4,8},{8,12},{12,0},{1,5},{5,9},{9,13},{13,1},{2,6},{6,10},{... | collective-permute-start | bytes 786440 | tf_op jit(solution)/shard_map/ppermute | solution.py:28
  9.3 0.2 head_parts.11
  9.5 0.6 collective-permute-start.5
  10.1 4.5 %collective-permute-done.1.refs_2_.refs_0_ = bf16[2,2,128,256]{3,2,1,0:T(8,128)(2,1)S(1)} collective-permute-done((bf16[2,2,128,256]{3,2,1,0:T(8,128)(2,1)S(1)}, bf16[2,2,128,256]{3,2,1,0:T(8,128)(2,1)S(1)}, u32[]{:S(2)}, u32[]{:S(2)}) %collective-permute-start.1) | collective-permute-done | bytes 262176 | tf_op jit(solution)/shard_map/ppermute | solution.py:33
  14.6 0.2 head_parts.13
  14.8 2.0 %collective-permute-start.10 = (bf16[2,2,128,256]{3,2,1,0:T(8,128)(2,1)S(1)}, bf16[2,2,128,256]{3,2,1,0:T(8,128)(2,1)S(1)}, u32[]{:S(2)}, u32[]{:S(2)}) collective-permute-start(bf16[2,2,128,256]{3,2,1,0:T(8,128)(2,1)S(1)} %head_parts.13), channel_id=1, source_target_pairs={{0,2},{2,0},{1,3},{3,1},{4,6},{6,4},{5,7},{7,5},{8,10},{10,8},{9,1... | collective-permute-start | bytes 786440 | tf_op jit(solution)/shard_map/ppermute | solution.py:33
  16.8 1.6 %collective-permute-start.3 = (bf16[2,2,128,256]{3,2,1,0:T(8,128)(2,1)S(1)}, bf16[2,2,128,256]{3,2,1,0:T(8,128)(2,1)S(1)}, u32[]{:S(2)}, u32[]{:S(2)}) collective-permute-start(bf16[2,2,128,256]{3,2,1,0:T(8,128)(2,1)S(1)} %collective-permute-done.1.refs_2_.refs_0_), channel_id=1, source_target_pairs={{0,4},{4,8},{8,12},{12,0},{1,5},{5,9},{9,13},{13,1},{2,6},{6,10},{... | collective-permute-start | bytes 786440 | tf_op jit(solution)/shard_map/ppermute | solution.py:28
  18.4 0.7 %and_select_fusion = (f32[1,768,256]{2,1,0:T(8,128)S(1)}, f32[1,768,256]{2,1,0:T(8,128)S(1)}) fusion(s32[256]{0:T(256)S(1)} %get-tuple-element.54, s32[256]{0:T(256)S(1)} %get-tuple-element.52, s32[768]{0:T(1024)S(1)} %get-tuple-element.50, s32[768]{0:T(1024)S(1)} %get-tuple-element.48, pred[768]{0:T(1024)(128)(4,1)S(1)} %get-tuple-element.46, ...), kind=kLoop, calls=%fused_computation.1 | loop fusion | flops 1966080 | bytes 1590784 | tf_op jit(solution)/shard_map/jit(_where)/select_n | solution.py:304
  19.1 0.1 pad_maximum_fusion.refs_0_
  19.2 0.2 head_parts.10.refs_5_
  19.4 0.2 head_parts.12.refs_1_
  19.6 1.6 %collective-permute-start.11 = (bf16[2,2,128,256]{3,2,1,0:T(8,128)(2,1)S(1)}, bf16[2,2,128,256]{3,2,1,0:T(8,128)(2,1)S(1)}, u32[]{:S(2)}, u32[]{:S(2)}) collective-permute-start(bf16[2,2,128,256]{3,2,1,0:T(8,128)(2,1)S(1)} %head_parts.12.refs_1_), channel_id=1, source_target_pairs={{0,4},{4,8},{8,12},{12,0},{1,5},{5,9},{9,13},{13,1},{2,6},{6,10},{... | collective-permute-start | bytes 786440 | tf_op jit(solution)/shard_map/ppermute | solution.py:28
  21.3 0.2 head_parts.15
  21.4 1.0 %collective-permute-start.13 = (bf16[2,2,128,256]{3,2,1,0:T(8,128)(2,1)S(1)}, bf16[2,2,128,256]{3,2,1,0:T(8,128)(2,1)S(1)}, u32[]{:S(2)}, u32[]{:S(2)}) collective-permute-start(bf16[2,2,128,256]{3,2,1,0:T(8,128)(2,1)S(1)} %head_parts.15), channel_id=1, source_target_pairs={{0,2},{2,0},{1,3},{3,1},{4,6},{6,4},{5,7},{7,5},{8,10},{10,8},{9,1... | collective-permute-start | bytes 786440 | tf_op jit(solution)/shard_map/ppermute | solution.py:33
  22.4 5.4 %collective-permute-done.3.refs_4_ = bf16[2,2,128,256]{3,2,1,0:T(8,128)(2,1)S(1)} collective-permute-done((bf16[2,2,128,256]{3,2,1,0:T(8,128)(2,1)S(1)}, bf16[2,2,128,256]{3,2,1,0:T(8,128)(2,1)S(1)}, u32[]{:S(2)}, u32[]{:S(2)}) %collective-permute-start.3) | collective-permute-done | bytes 262176 | tf_op jit(solution)/shard_map/ppermute | solution.py:28
  27.9 3.5 %attention_grads.2 = (f32[2,2,2,128,256]{4,3,2,1,0:T(8,128)S(1)}, bf16[2,128,256]{2,1,0:T(8,128)(2,1)S(1)}, bf16[2,128,256]{2,1,0:T(8,128)(2,1)S(1)}, bf16[2,2,2,128,256]{4,3,2,1,0:T(8,128)(2,1)S(1)}) custom-call(f32[2,768,256]{2,1,0:T(8,128)S(1)} %pad_maximum_fusion.refs_0_, bf16[2,2,128,256]{3,2,1,0:T(8,128)(2,1)S(1)} %head_parts.8.refs_1_, ...), custom_call_target="tpu_custom_call" | custom-call | flops 1006632960 | bytes 4980736 | tf_op jit(solution)/shard_map/attention_grads/pallas_call | solution.py:52
  31.4 1.7 %collective-permute-start.12 = (bf16[2,2,128,256]{3,2,1,0:T(8,128)(2,1)S(1)}, bf16[2,2,128,256]{3,2,1,0:T(8,128)(2,1)S(1)}, u32[]{:S(2)}, u32[]{:S(2)}) collective-permute-start(bf16[2,2,128,256]{3,2,1,0:T(8,128)(2,1)S(1)} %relayed.2), channel_id=1, source_target_pairs={{0,4},{4,8},{8,12},{1,5},{5,9},{9,13},{2,6},{6,10},{10,14},{3,7},{... | collective-permute-start | bytes 786440 | tf_op jit(solution)/shard_map/ppermute | solution.py:28
  33.1 1.3 %collective-permute-start.7 = (bf16[2,2,2,128,256]{4,3,2,1,0:T(8,128)(2,1)S(1)}, bf16[2,2,2,128,256]{4,3,2,1,0:T(8,128)(2,1)S(1)}, u32[]{:S(2)}, u32[]{:S(2)}) collective-permute-start(bf16[2,2,2,128,256]{4,3,2,1,0:T(8,128)(2,1)S(1)} %get-tuple-element.31), channel_id=1, source_target_pairs={{4,0},{8,4},{12,8},{5,1},{9,5},{13,9},{6,2},{10,6},{14,10},{7,3},{... | collective-permute-start | bytes 1572872 | tf_op jit(solution)/shard_map/ppermute | solution.py:28
  34.4 0.2 head_parts.14.refs_5_
  34.6 2.3 %collective-permute-done.12.refs_4_ = bf16[2,2,128,256]{3,2,1,0:T(8,128)(2,1)S(1)} collective-permute-done((bf16[2,2,128,256]{3,2,1,0:T(8,128)(2,1)S(1)}, bf16[2,2,128,256]{3,2,1,0:T(8,128)(2,1)S(1)}, u32[]{:S(2)}, u32[]{:S(2)}) %collective-permute-start.12) | collective-permute-done | bytes 262176 | tf_op jit(solution)/shard_map/ppermute | solution.py:28
  37.0 3.5 %attention_grads.3 = (f32[2,2,2,128,256]{4,3,2,1,0:T(8,128)S(1)}, bf16[2,128,256]{2,1,0:T(8,128)(2,1)S(1)}, bf16[2,128,256]{2,1,0:T(8,128)(2,1)S(1)}, bf16[2,2,1...) custom-call(f32[2,768,256]{2,1,0:T(8,128)S(1)} %pad_maximum_fusion.refs_0_, ...), custom_call_target="tpu_custom_call" | custom-call | flops 1006632960 | bytes 4980736 | tf_op jit(solution)/shard_map/attention_grads/pallas_call | solution.py:52
  40.5 1.3 %collective-permute-start.15 = (bf16[2,2,128,256]{3,2,1,0:T(8,128)(2,1)S(1)}, bf16[2,2,128,256]{3,2,1,0:T(8,128)(2,1)S(1)}, u32[]{:S(2)}, u32[]{:S(2)}) collective-permute-start(bf16[2,2,128,256]{3,2,1,0:T(8,128)(2,1)S(1)} %get-tuple-element.41), channel_id=1, source_target_pairs={{4,0},{8,4},{12,8},{5,1},{9,5},{13,9},{6,2},{10,6},{14,10},{7,3},{... | collective-permute-start | bytes 786440 | tf_op jit(solution)/shard_map/ppermute | solution.py:28
  41.8 0.6 collective-permute-start.6
  42.4 1.5 %collective-permute-start.14 = (bf16[2,128,256]{2,1,0:T(8,128)(2,1)S(1)}, bf16[2,128,256]{2,1,0:T(8,128)(2,1)S(1)}, u32[]{:S(2)}, u32[]{:S(2)}) collective-permute-start(bf16[2,128,256]{2,1,0:T(8,128)(2,1)S(1)} %get-tuple-element.38), channel_id=1, source_target_pairs={{0,2},{2,0},{1,3},{3,1},{4,6},{6,4},{5,7},{7,5},{8,10},{10,8},{9,1... | collective-permute-start | bytes 393224 | tf_op jit(solution)/shard_map/ppermute | solution.py:33
  43.8 4.2 %collective-permute-done.6.refs_1_ = bf16[2,128,256]{2,1,0:T(8,128)(2,1)S(1)} collective-permute-done((bf16[2,128,256]{2,1,0:T(8,128)(2,1)S(1)}, bf16[2,128,256]{2,1,0:T(8,128)(2,1)S(1)}, u32[]{:S(2)}, u32[]{:S(2)}) %collective-permute-start.6) | collective-permute-done | bytes 131104 | tf_op jit(solution)/shard_map/ppermute | solution.py:33
  48.0 0.1 summed.3
  48.1 0.9 %collective-permute-start.8 = (bf16[2,2,128,256]{3,2,1,0:T(8,128)(2,1)S(1)}, bf16[2,2,128,256]{3,2,1,0:T(8,128)(2,1)S(1)}, u32[]{:S(2)}, u32[]{:S(2)}) collective-permute-start(bf16[2,2,128,256]{3,2,1,0:T(8,128)(2,1)S(1)} %get-tuple-element.33), channel_id=1, source_target_pairs={{0,2},{2,0},{1,3},{3,1},{4,6},{6,4},{5,7},{7,5},{8,10},{10,8},{9,1... | collective-permute-start | bytes 786440 | tf_op jit(solution)/shard_map/ppermute | solution.py:33
  49.0 0.4 collective-permute-done.14.refs_1_
  49.4 0.7 %collective-permute-done.15.refs_0_ = bf16[2,2,128,256]{3,2,1,0:T(8,128)(2,1)S(1)} collective-permute-done((bf16[2,2,128,256]{3,2,1,0:T(8,128)(2,1)S(1)}, bf16[2,2,128,256]{3,2,1,0:T(8,128)(2,1)S(1)}, u32[]{:S(2)}, u32[]{:S(2)}) %collective-permute-start.15) | collective-permute-done | bytes 262176 | tf_op jit(solution)/shard_map/ppermute | solution.py:28
  50.2 1.3 %collective-permute-start.16 = (bf16[2,2,128,256]{3,2,1,0:T(8,128)(2,1)S(1)}, bf16[2,2,128,256]{3,2,1,0:T(8,128)(2,1)S(1)}, u32[]{:S(2)}, u32[]{:S(2)}) collective-permute-start(bf16[2,2,128,256]{3,2,1,0:T(8,128)(2,1)S(1)} %relayed.3), channel_id=1, source_target_pairs={{4,0},{8,4},{12,8},{5,1},{9,5},{13,9},{6,2},{10,6},{14,10},{7,3},{... | collective-permute-start | bytes 786440 | tf_op jit(solution)/shard_map/ppermute | solution.py:28
  51.5 1.6 %collective-permute-start.17 = (bf16[2,2,128,256]{3,2,1,0:T(8,128)(2,1)S(1)}, bf16[2,2,128,256]{3,2,1,0:T(8,128)(2,1)S(1)}, u32[]{:S(2)}, u32[]{:S(2)}) collective-permute-start(bf16[2,2,128,256]{3,2,1,0:T(8,128)(2,1)S(1)} %summed.4.refs_0_), channel_id=1, source_target_pairs={{0,2},{2,0},{1,3},{3,1},{4,6},{6,4},{5,7},{7,5},{8,10},{10,8},{9,1... | collective-permute-start | bytes 786440 | tf_op jit(solution)/shard_map/ppermute | solution.py:33
  53.1 2.9 %collective-permute-done.8.refs_3_ = bf16[2,2,128,256]{3,2,1,0:T(8,128)(2,1)S(1)} collective-permute-done((bf16[2,2,128,256]{3,2,1,0:T(8,128)(2,1)S(1)}, bf16[2,2,128,256]{3,2,1,0:T(8,128)(2,1)S(1)}, u32[]{:S(2)}, u32[]{:S(2)}) %collective-permute-start.8) | collective-permute-done | bytes 262176 | tf_op jit(solution)/shard_map/ppermute | solution.py:33
  56.0 0.1 collective-permute-start.18
  56.1 2.5 %collective-permute-done.16.refs_0_ = bf16[2,2,128,256]{3,2,1,0:T(8,128)(2,1)S(1)} collective-permute-done((bf16[2,2,128,256]{3,2,1,0:T(8,128)(2,1)S(1)}, bf16[2,2,128,256]{3,2,1,0:T(8,128)(2,1)S(1)}, u32[]{:S(2)}, u32[]{:S(2)}) %collective-permute-start.16) | collective-permute-done | bytes 262176 | tf_op jit(solution)/shard_map/ppermute | solution.py:28
  58.6 0.1 collective-permute-done.17.refs_3_
  58.8 0.1 rows_for_pair.3
  58.8 0.1 collective-permute-start.19
  58.9 1.7 %collective-permute-done.19.refs_3_ = bf16[3,2,128,256]{3,2,1,0:T(8,128)(2,1)S(1)} collective-permute-done((bf16[3,2,128,256]{3,2,1,0:T(8,128)(2,1)S(1)}, bf16[3,2,128,256]{3,2,1,0:T(8,128)(2,1)S(1)}, u32[]{:S(2)}, u32[]{:S(2)}) %collective-permute-start.19) | collective-permute-done | bytes 393248 | tf_op jit(solution)/shard_map/ppermute | solution.py:37
  60.6 1.3 %laid_out.1 = (bf16[128,2048]{1,0:T(8,128)(2,1)}, bf16[128,2048]{1,0:T(8,128)(2,1)}, bf16[128,2048]{1,0:T(8,128)(2,1)}) custom-call(bf16[3,2,128,256]{3,2,1,0:T(8,128)(2,1)S(1)} %get-tuple-element.34.refs_0_, bf16[3,2,128,256]{3,2,1,0:T(8,128)(2,1)S(1)} %get-tuple-element.42.refs_1_, bf16[3,2,128,256]{3,2,1,0:T(8,128)(2,1)S(1)} %collective-permute-done.18.refs_2_, ...), custom_call_target="tpu_custom_call" | custom-call | bytes 3145728 | tf_op jit(solution)/shard_map/laid_out/pallas_call | solution.py:52
  (23 shorter events, 0.3 us)
Async XLA Ops:
  1.8 2.9 %collective-permute-start = (bf16[2,2,128,256]{3,2,1,0:T(8,128)(2,1)S(1)}, bf16[2,2,128,256]{3,2,1,0:T(8,128)(2,1)S(1)}, u32[]{:S(2)}, u32[]{:S(2)}) collective-permute-start(bf16[2,2,128,256]{3,2,1,0:T(8,128)(2,1)S(1)} %get-tuple-element.25), channel_id=1, source_target_pairs={{0,1},{1,0},{2,3},{3,2},{4,5},{5,4},{6,7},{7,6},{8,9},{9,8},{10,11... | collective-permute-start | bytes 786440 | tf_op jit(solution)/shard_map/ppermute | solution.py:37
  2.3 2.3 %copy-start = (s32[2048]{0:T(1024)S(1)}, s32[2048]{0:T(1024)}, u32[]{:S(2)}) copy-start(s32[2048]{0:T(1024)} %param.9) | copy-start | bytes 24580
  3.9 5.3 %collective-permute-start.4 = (bf16[2,2,128,256]{3,2,1,0:T(8,128)(2,1)S(1)}, bf16[2,2,128,256]{3,2,1,0:T(8,128)(2,1)S(1)}, u32[]{:S(2)}, u32[]{:S(2)}) collective-permute-start(bf16[2,2,128,256]{3,2,1,0:T(8,128)(2,1)S(1)} %get-tuple-element.27), channel_id=1, source_target_pairs={{0,1},{1,0},{2,3},{3,2},{4,5},{5,4},{6,7},{7,6},{8,9},{9,8},{10,11... | collective-permute-start | bytes 786440 | tf_op jit(solution)/shard_map/ppermute | solution.py:37
  4.1 10.6 %collective-permute-start.9 = (bf16[4,2,128,256]{3,2,1,0:T(8,128)(2,1)S(1)}, bf16[4,2,128,256]{3,2,1,0:T(8,128)(2,1)S(1)}, u32[]{:S(2)}, u32[]{:S(2)}) collective-permute-start(bf16[4,2,128,256]{3,2,1,0:T(8,128)(2,1)S(1)} %get-tuple-element.36), channel_id=1, source_target_pairs={{0,1},{1,0},{2,3},{3,2},{4,5},{5,4},{6,7},{7,6},{8,9},{9,8},{10,11... | collective-permute-start | bytes 1572872 | tf_op jit(solution)/shard_map/ppermute | solution.py:37
  4.8 9.8 %collective-permute-start.1 = (bf16[2,2,128,256]{3,2,1,0:T(8,128)(2,1)S(1)}, bf16[2,2,128,256]{3,2,1,0:T(8,128)(2,1)S(1)}, u32[]{:S(2)}, u32[]{:S(2)}) collective-permute-start(bf16[2,2,128,256]{3,2,1,0:T(8,128)(2,1)S(1)} %head_parts.9), channel_id=1, source_target_pairs={{0,2},{2,0},{1,3},{3,1},{4,6},{6,4},{5,7},{7,5},{8,10},{10,8},{9,1... | collective-permute-start | bytes 786440 | tf_op jit(solution)/shard_map/ppermute | solution.py:33
  7.7 11.7 %collective-permute-start.2 = (bf16[2,2,128,256]{3,2,1,0:T(8,128)(2,1)S(1)}, bf16[2,2,128,256]{3,2,1,0:T(8,128)(2,1)S(1)}, u32[]{:S(2)}, u32[]{:S(2)}) collective-permute-start(bf16[2,2,128,256]{3,2,1,0:T(8,128)(2,1)S(1)} %head_parts.8.refs_1_), channel_id=1, source_target_pairs={{0,4},{4,8},{8,12},{12,0},{1,5},{5,9},{9,13},{13,1},{2,6},{6,10},{... | collective-permute-start | bytes 786440 | tf_op jit(solution)/shard_map/ppermute | solution.py:28
  9.5 11.8 %collective-permute-start.5 = (bf16[2,2,128,256]{3,2,1,0:T(8,128)(2,1)S(1)}, bf16[2,2,128,256]{3,2,1,0:T(8,128)(2,1)S(1)}, u32[]{:S(2)}, u32[]{:S(2)}) collective-permute-start(bf16[2,2,128,256]{3,2,1,0:T(8,128)(2,1)S(1)} %head_parts.11), channel_id=1, source_target_pairs={{0,2},{2,0},{1,3},{3,1},{4,6},{6,4},{5,7},{7,5},{8,10},{10,8},{9,1... | collective-permute-start | bytes 786440 | tf_op jit(solution)/shard_map/ppermute | solution.py:33
  14.8 16.5 %collective-permute-start.10 = (bf16[2,2,128,256]{3,2,1,0:T(8,128)(2,1)S(1)}, bf16[2,2,128,256]{3,2,1,0:T(8,128)(2,1)S(1)}, u32[]{:S(2)}, u32[]{:S(2)}) collective-permute-start(bf16[2,2,128,256]{3,2,1,0:T(8,128)(2,1)S(1)} %head_parts.13), channel_id=1, source_target_pairs={{0,2},{2,0},{1,3},{3,1},{4,6},{6,4},{5,7},{7,5},{8,10},{10,8},{9,1... | collective-permute-start | bytes 786440 | tf_op jit(solution)/shard_map/ppermute | solution.py:33
  16.8 11.0 %collective-permute-start.3 = (bf16[2,2,128,256]{3,2,1,0:T(8,128)(2,1)S(1)}, bf16[2,2,128,256]{3,2,1,0:T(8,128)(2,1)S(1)}, u32[]{:S(2)}, u32[]{:S(2)}) collective-permute-start(bf16[2,2,128,256]{3,2,1,0:T(8,128)(2,1)S(1)} %collective-permute-done.1.refs_2_.refs_0_), channel_id=1, source_target_pairs={{0,4},{4,8},{8,12},{12,0},{1,5},{5,9},{9,13},{13,1},{2,6},{6,10},{... | collective-permute-start | bytes 786440 | tf_op jit(solution)/shard_map/ppermute | solution.py:28
  19.6 15.0 %collective-permute-start.11 = (bf16[2,2,128,256]{3,2,1,0:T(8,128)(2,1)S(1)}, bf16[2,2,128,256]{3,2,1,0:T(8,128)(2,1)S(1)}, u32[]{:S(2)}, u32[]{:S(2)}) collective-permute-start(bf16[2,2,128,256]{3,2,1,0:T(8,128)(2,1)S(1)} %head_parts.12.refs_1_), channel_id=1, source_target_pairs={{0,4},{4,8},{8,12},{12,0},{1,5},{5,9},{9,13},{13,1},{2,6},{6,10},{... | collective-permute-start | bytes 786440 | tf_op jit(solution)/shard_map/ppermute | solution.py:28
  21.4 13.2 %collective-permute-start.13 = (bf16[2,2,128,256]{3,2,1,0:T(8,128)(2,1)S(1)}, bf16[2,2,128,256]{3,2,1,0:T(8,128)(2,1)S(1)}, u32[]{:S(2)}, u32[]{:S(2)}) collective-permute-start(bf16[2,2,128,256]{3,2,1,0:T(8,128)(2,1)S(1)} %head_parts.15), channel_id=1, source_target_pairs={{0,2},{2,0},{1,3},{3,1},{4,6},{6,4},{5,7},{7,5},{8,10},{10,8},{9,1... | collective-permute-start | bytes 786440 | tf_op jit(solution)/shard_map/ppermute | solution.py:33
  31.4 5.6 %collective-permute-start.12 = (bf16[2,2,128,256]{3,2,1,0:T(8,128)(2,1)S(1)}, bf16[2,2,128,256]{3,2,1,0:T(8,128)(2,1)S(1)}, u32[]{:S(2)}, u32[]{:S(2)}) collective-permute-start(bf16[2,2,128,256]{3,2,1,0:T(8,128)(2,1)S(1)} %relayed.2), channel_id=1, source_target_pairs={{0,4},{4,8},{8,12},{1,5},{5,9},{9,13},{2,6},{6,10},{10,14},{3,7},{... | collective-permute-start | bytes 786440 | tf_op jit(solution)/shard_map/ppermute | solution.py:28
  33.1 14.9 %collective-permute-start.7 = (bf16[2,2,2,128,256]{4,3,2,1,0:T(8,128)(2,1)S(1)}, bf16[2,2,2,128,256]{4,3,2,1,0:T(8,128)(2,1)S(1)}, u32[]{:S(2)}, u32[]{:S(2)}) collective-permute-start(bf16[2,2,2,128,256]{4,3,2,1,0:T(8,128)(2,1)S(1)} %get-tuple-element.31), channel_id=1, source_target_pairs={{4,0},{8,4},{12,8},{5,1},{9,5},{13,9},{6,2},{10,6},{14,10},{7,3},{... | collective-permute-start | bytes 1572872 | tf_op jit(solution)/shard_map/ppermute | solution.py:28
  40.5 9.7 %collective-permute-start.15 = (bf16[2,2,128,256]{3,2,1,0:T(8,128)(2,1)S(1)}, bf16[2,2,128,256]{3,2,1,0:T(8,128)(2,1)S(1)}, u32[]{:S(2)}, u32[]{:S(2)}) collective-permute-start(bf16[2,2,128,256]{3,2,1,0:T(8,128)(2,1)S(1)} %get-tuple-element.41), channel_id=1, source_target_pairs={{4,0},{8,4},{12,8},{5,1},{9,5},{13,9},{6,2},{10,6},{14,10},{7,3},{... | collective-permute-start | bytes 786440 | tf_op jit(solution)/shard_map/ppermute | solution.py:28
  41.8 6.2 %collective-permute-start.6 = (bf16[2,128,256]{2,1,0:T(8,128)(2,1)S(1)}, bf16[2,128,256]{2,1,0:T(8,128)(2,1)S(1)}, u32[]{:S(2)}, u32[]{:S(2)}) collective-permute-start(bf16[2,128,256]{2,1,0:T(8,128)(2,1)S(1)} %get-tuple-element.29), channel_id=1, source_target_pairs={{0,2},{2,0},{1,3},{3,1},{4,6},{6,4},{5,7},{7,5},{8,10},{10,8},{9,1... | collective-permute-start | bytes 393224 | tf_op jit(solution)/shard_map/ppermute | solution.py:33
  42.4 7.1 %collective-permute-start.14 = (bf16[2,128,256]{2,1,0:T(8,128)(2,1)S(1)}, bf16[2,128,256]{2,1,0:T(8,128)(2,1)S(1)}, u32[]{:S(2)}, u32[]{:S(2)}) collective-permute-start(bf16[2,128,256]{2,1,0:T(8,128)(2,1)S(1)} %get-tuple-element.38), channel_id=1, source_target_pairs={{0,2},{2,0},{1,3},{3,1},{4,6},{6,4},{5,7},{7,5},{8,10},{10,8},{9,1... | collective-permute-start | bytes 393224 | tf_op jit(solution)/shard_map/ppermute | solution.py:33
  48.1 7.9 %collective-permute-start.8 = (bf16[2,2,128,256]{3,2,1,0:T(8,128)(2,1)S(1)}, bf16[2,2,128,256]{3,2,1,0:T(8,128)(2,1)S(1)}, u32[]{:S(2)}, u32[]{:S(2)}) collective-permute-start(bf16[2,2,128,256]{3,2,1,0:T(8,128)(2,1)S(1)} %get-tuple-element.33), channel_id=1, source_target_pairs={{0,2},{2,0},{1,3},{3,1},{4,6},{6,4},{5,7},{7,5},{8,10},{10,8},{9,1... | collective-permute-start | bytes 786440 | tf_op jit(solution)/shard_map/ppermute | solution.py:33
  50.2 8.4 %collective-permute-start.16 = (bf16[2,2,128,256]{3,2,1,0:T(8,128)(2,1)S(1)}, bf16[2,2,128,256]{3,2,1,0:T(8,128)(2,1)S(1)}, u32[]{:S(2)}, u32[]{:S(2)}) collective-permute-start(bf16[2,2,128,256]{3,2,1,0:T(8,128)(2,1)S(1)} %relayed.3), channel_id=1, source_target_pairs={{4,0},{8,4},{12,8},{5,1},{9,5},{13,9},{6,2},{10,6},{14,10},{7,3},{... | collective-permute-start | bytes 786440 | tf_op jit(solution)/shard_map/ppermute | solution.py:28
  51.5 7.3 %collective-permute-start.17 = (bf16[2,2,128,256]{3,2,1,0:T(8,128)(2,1)S(1)}, bf16[2,2,128,256]{3,2,1,0:T(8,128)(2,1)S(1)}, u32[]{:S(2)}, u32[]{:S(2)}) collective-permute-start(bf16[2,2,128,256]{3,2,1,0:T(8,128)(2,1)S(1)} %summed.4.refs_0_), channel_id=1, source_target_pairs={{0,2},{2,0},{1,3},{3,1},{4,6},{6,4},{5,7},{7,5},{8,10},{10,8},{9,1... | collective-permute-start | bytes 786440 | tf_op jit(solution)/shard_map/ppermute | solution.py:33
  56.0 2.9 %collective-permute-start.18 = (bf16[3,2,128,256]{3,2,1,0:T(8,128)(2,1)S(1)}, bf16[3,2,128,256]{3,2,1,0:T(8,128)(2,1)S(1)}, u32[]{:S(2)}, u32[]{:S(2)}) collective-permute-start(bf16[3,2,128,256]{3,2,1,0:T(8,128)(2,1)S(1)} %get-tuple-element.43), channel_id=1, source_target_pairs={{0,1},{1,0},{2,3},{3,2},{4,5},{5,4},{6,7},{7,6},{8,9},{9,8},{10,11... | collective-permute-start | bytes 1179656 | tf_op jit(solution)/shard_map/ppermute | solution.py:37
  58.8 1.8 %collective-permute-start.19 = (bf16[3,2,128,256]{3,2,1,0:T(8,128)(2,1)S(1)}, bf16[3,2,128,256]{3,2,1,0:T(8,128)(2,1)S(1)}, u32[]{:S(2)}, u32[]{:S(2)}) collective-permute-start(bf16[3,2,128,256]{3,2,1,0:T(8,128)(2,1)S(1)} %get-tuple-element.44), channel_id=1, source_target_pairs={{0,1},{1,0},{2,3},{3,2},{4,5},{5,4},{6,7},{7,6},{8,9},{9,8},{10,11... | collective-permute-start | bytes 1179656 | tf_op jit(solution)/shard_map/ppermute | solution.py:37

commit v23 on v22

--- a/solution.py
+++ b/solution.py
@@ -152,7 +152,7 @@
             ]
         run_moves(moves, sems)
         strips = [(head, tile) for head in range(heads) for tile in range(2)]
-        products, terms = {}, {}
+        products, terms, turned = {}, {}, {}
 
         def flat(ref, which, tiles, head):
             block = ref[which, tiles, :, :, pl.ds(head * HD, HD)]
@@ -179,7 +179,10 @@
             row_dot = jnp.sum(functools.reduce(jnp.add, dots), axis=0, keepdims=True)
             score_low = [(piece * (grad_prob[cut] - row_dot)).astype(LOW) for piece, cut in zip(prob, cuts)]
             prob_low, score_low = jnp.concatenate(low, axis=0), jnp.concatenate(score_low, axis=0)
-            dq = jnp.dot(k.T, score_low, preferred_element_type=WIDE) * SCALE
+            if tile == 0:
+                turned[head] = flat(kv_all, 0, pl.ds(0, 4), head).T
+            k_turned = turned[head][:, tile * strip:(tile + 3) * strip]
+            dq = jnp.dot(k_turned, score_low, preferred_element_type=WIDE) * SCALE
             dq_all[tile, :, :, pl.ds(head * HD, HD)] = dq.T.astype(LOW).reshape(peers, rows, HD)
             dk = jnp.dot(score_low, q, preferred_element_type=WIDE) * SCALE
             dv = jnp.dot(prob_low, g, preferred_element_type=WIDE)

time: 62.3 us -> 62.3 us (level)
  no operation moved by 1% of the time
where the time goes in v23:
time: 62.3 us; the launch traced here: 62 us
  waiting for transfers between devices  24.8 us (40%)
  starting transfers between devices  22.4 us (36%)
  Pallas kernels  13 us (21%)
  between operations  0.9 us (1%)
  other arithmetic  0.79 us (1%)
    ppermute x8, waiting for transfers between devices, round_sub(): lax.ppermute(value, 'sub', [(i, (i + by) % peers) for i in range(peers)])  12.2 us
    ppermute x7, waiting for transfers between devices, along_blocks(): return lax.ppermute(value, 'blk', pairs)  10.9 us
    ppermute x8, starting transfers between devices, round_sub(): lax.ppermute(value, 'sub', [(i, (i + by) % peers) for i in range(peers)])  10.7 us
    ppermute x7, starting transfers between devices, along_blocks(): return lax.ppermute(value, 'blk', pairs)  10.4 us
    pallas_call x18, Pallas kernels, call(): pl.pallas_call(kernel, out_shape=outs, in_specs=[spec] * len(ins), out_sp...  10.2 us
    pallas_call x2, Pallas kernels, first_parts(): pl.pallas_call(kernel, out_shape=outs, in_specs=[spec] * (len(held) + len...  2.78 us
    ppermute x5, waiting for transfers between devices, swapped(): return lax.ppermute(value, 'pair', [(0, 1), (1, 0)])  1.71 us
  transfers between devices with their start and end apart: 20, of which 10 were waited for; matrix products, arithmetic and copies ran while one was open for 1% of the time, Pallas kernels for 17%

profile of v23, /device:TPU:0, one launch (start us, length us, event | category | flops | bytes accessed | tf_op | source)
XLA Modules:
  0.0 62.0 jit_solution(4397909386375542948)
XLA Ops:
  0.6 1.1 %first_parts.2 = (bf16[2,2,128,256]{3,2,1,0:T(8,128)(2,1)S(1)}, bf16[2,2,128,256]{3,2,1,0:T(8,128)(2,1)S(1)}) custom-call(bf16[128,2048]{1,0:T(8,128)(2,1)} %refs_2_.1, bf16[128,2048]{1,0:T(8,128)(2,1)} %refs_3_.1), custom_call_target="tpu_custom_call" | custom-call | tf_op jit(solution)/shard_map/first_parts/pallas_call | solution.py:93
  1.8 0.5 collective-permute-start
  2.3 1.6 %first_parts.3 = (bf16[2,2,128,256]{3,2,1,0:T(8,128)(2,1)S(1)}, bf16[2,2,128,256]{3,2,1,0:T(8,128)(2,1)S(1)}, bf16[4,2,128,256]{3,2,1,0:T(8,128)(2,1)S(1)}, bf16[4,2,128,256]{3,2,1,0:T(8,128)(2,1)S(1)}) custom-call(bf16[128,2048]{1,0:T(8,128)(2,1)} %refs_4_.1, bf16[128,2048]{1,0:T(8,128)(2,1)} %refs_5_.1, bf16[128,2048]{1,0:T(8,128)(2,1)} %refs_2_.1, ...), custom_call_target="tpu_custom_call" | custom-call | tf_op jit(solution)/shard_map/first_parts/pallas_call | solution.py:93
  3.9 0.1 collective-permute-start.4
  4.1 0.5 collective-permute-start.9
  4.6 0.1 pad_dynamic-slice_fusion
  4.7 0.2 head_parts.9
  4.8 2.6 %collective-permute-start.1 = (bf16[2,2,128,256]{3,2,1,0:T(8,128)(2,1)S(1)}, bf16[2,2,128,256]{3,2,1,0:T(8,128)(2,1)S(1)}, u32[]{:S(2)}, u32[]{:S(2)}) collective-permute-start(bf16[2,2,128,256]{3,2,1,0:T(8,128)(2,1)S(1)} %head_parts.9), channel_id=1, source_target_pairs={{0,2},{2,0},{1,3},{3,1},{4,6},{6,4},{5,7},{7,5},{8,10},{10,8},{9,1... | collective-permute-start | bytes 786440 | tf_op jit(solution)/shard_map/ppermute | solution.py:33
  7.5 0.2 head_parts.8.refs_1_
  7.7 1.6 %collective-permute-start.2 = (bf16[2,2,128,256]{3,2,1,0:T(8,128)(2,1)S(1)}, bf16[2,2,128,256]{3,2,1,0:T(8,128)(2,1)S(1)}, u32[]{:S(2)}, u32[]{:S(2)}) collective-permute-start(bf16[2,2,128,256]{3,2,1,0:T(8,128)(2,1)S(1)} %head_parts.8.refs_1_), channel_id=1, source_target_pairs={{0,4},{4,8},{8,12},{12,0},{1,5},{5,9},{9,13},{13,1},{2,6},{6,10},{... | collective-permute-start | bytes 786440 | tf_op jit(solution)/shard_map/ppermute | solution.py:28
  9.3 0.2 head_parts.11
  9.5 0.6 collective-permute-start.5
  10.1 4.5 %collective-permute-done.1.refs_2_.refs_0_ = bf16[2,2,128,256]{3,2,1,0:T(8,128)(2,1)S(1)} collective-permute-done((bf16[2,2,128,256]{3,2,1,0:T(8,128)(2,1)S(1)}, bf16[2,2,128,256]{3,2,1,0:T(8,128)(2,1)S(1)}, u32[]{:S(2)}, u32[]{:S(2)}) %collective-permute-start.1) | collective-permute-done | bytes 262176 | tf_op jit(solution)/shard_map/ppermute | solution.py:33
  14.6 0.2 head_parts.13
  14.8 2.0 %collective-permute-start.10 = (bf16[2,2,128,256]{3,2,1,0:T(8,128)(2,1)S(1)}, bf16[2,2,128,256]{3,2,1,0:T(8,128)(2,1)S(1)}, u32[]{:S(2)}, u32[]{:S(2)}) collective-permute-start(bf16[2,2,128,256]{3,2,1,0:T(8,128)(2,1)S(1)} %head_parts.13), channel_id=1, source_target_pairs={{0,2},{2,0},{1,3},{3,1},{4,6},{6,4},{5,7},{7,5},{8,10},{10,8},{9,1... | collective-permute-start | bytes 786440 | tf_op jit(solution)/shard_map/ppermute | solution.py:33
  16.8 1.6 %collective-permute-start.3 = (bf16[2,2,128,256]{3,2,1,0:T(8,128)(2,1)S(1)}, bf16[2,2,128,256]{3,2,1,0:T(8,128)(2,1)S(1)}, u32[]{:S(2)}, u32[]{:S(2)}) collective-permute-start(bf16[2,2,128,256]{3,2,1,0:T(8,128)(2,1)S(1)} %collective-permute-done.1.refs_2_.refs_0_), channel_id=1, source_target_pairs={{0,4},{4,8},{8,12},{12,0},{1,5},{5,9},{9,13},{13,1},{2,6},{6,10},{... | collective-permute-start | bytes 786440 | tf_op jit(solution)/shard_map/ppermute | solution.py:28
  18.4 0.7 %and_select_fusion = (f32[1,768,256]{2,1,0:T(8,128)S(1)}, f32[1,768,256]{2,1,0:T(8,128)S(1)}) fusion(s32[256]{0:T(256)S(1)} %get-tuple-element.54, s32[256]{0:T(256)S(1)} %get-tuple-element.52, s32[768]{0:T(1024)S(1)} %get-tuple-element.50, s32[768]{0:T(1024)S(1)} %get-tuple-element.48, pred[768]{0:T(1024)(128)(4,1)S(1)} %get-tuple-element.46, ...), kind=kLoop, calls=%fused_computation.1 | loop fusion | flops 1966080 | bytes 1590784 | tf_op jit(solution)/shard_map/jit(_where)/select_n | solution.py:307
  19.1 0.1 pad_maximum_fusion.refs_0_
  19.2 0.2 head_parts.10.refs_5_
  19.4 0.2 head_parts.12.refs_1_
  19.6 1.6 %collective-permute-start.11 = (bf16[2,2,128,256]{3,2,1,0:T(8,128)(2,1)S(1)}, bf16[2,2,128,256]{3,2,1,0:T(8,128)(2,1)S(1)}, u32[]{:S(2)}, u32[]{:S(2)}) collective-permute-start(bf16[2,2,128,256]{3,2,1,0:T(8,128)(2,1)S(1)} %head_parts.12.refs_1_), channel_id=1, source_target_pairs={{0,4},{4,8},{8,12},{12,0},{1,5},{5,9},{9,13},{13,1},{2,6},{6,10},{... | collective-permute-start | bytes 786440 | tf_op jit(solution)/shard_map/ppermute | solution.py:28
  21.3 0.2 head_parts.15
  21.4 1.0 %collective-permute-start.13 = (bf16[2,2,128,256]{3,2,1,0:T(8,128)(2,1)S(1)}, bf16[2,2,128,256]{3,2,1,0:T(8,128)(2,1)S(1)}, u32[]{:S(2)}, u32[]{:S(2)}) collective-permute-start(bf16[2,2,128,256]{3,2,1,0:T(8,128)(2,1)S(1)} %head_parts.15), channel_id=1, source_target_pairs={{0,2},{2,0},{1,3},{3,1},{4,6},{6,4},{5,7},{7,5},{8,10},{10,8},{9,1... | collective-permute-start | bytes 786440 | tf_op jit(solution)/shard_map/ppermute | solution.py:33
  22.4 5.4 %collective-permute-done.3.refs_4_ = bf16[2,2,128,256]{3,2,1,0:T(8,128)(2,1)S(1)} collective-permute-done((bf16[2,2,128,256]{3,2,1,0:T(8,128)(2,1)S(1)}, bf16[2,2,128,256]{3,2,1,0:T(8,128)(2,1)S(1)}, u32[]{:S(2)}, u32[]{:S(2)}) %collective-permute-start.3) | collective-permute-done | bytes 262176 | tf_op jit(solution)/shard_map/ppermute | solution.py:28
  27.9 3.5 %attention_grads.2 = (f32[2,2,2,128,256]{4,3,2,1,0:T(8,128)S(1)}, bf16[2,128,256]{2,1,0:T(8,128)(2,1)S(1)}, bf16[2,128,256]{2,1,0:T(8,128)(2,1)S(1)}, bf16[2,2,2,128,256]{4,3,2,1,0:T(8,128)(2,1)S(1)}) custom-call(f32[2,768,256]{2,1,0:T(8,128)S(1)} %pad_maximum_fusion.refs_0_, bf16[2,2,128,256]{3,2,1,0:T(8,128)(2,1)S(1)} %head_parts.8.refs_1_, ...), custom_call_target="tpu_custom_call" | custom-call | flops 1006632960 | bytes 4980736 | tf_op jit(solution)/shard_map/attention_grads/pallas_call | solution.py:52
  31.4 1.7 %collective-permute-start.12 = (bf16[2,2,128,256]{3,2,1,0:T(8,128)(2,1)S(1)}, bf16[2,2,128,256]{3,2,1,0:T(8,128)(2,1)S(1)}, u32[]{:S(2)}, u32[]{:S(2)}) collective-permute-start(bf16[2,2,128,256]{3,2,1,0:T(8,128)(2,1)S(1)} %relayed.2), channel_id=1, source_target_pairs={{0,4},{4,8},{8,12},{1,5},{5,9},{9,13},{2,6},{6,10},{10,14},{3,7},{... | collective-permute-start | bytes 786440 | tf_op jit(solution)/shard_map/ppermute | solution.py:28
  33.1 1.3 %collective-permute-start.7 = (bf16[2,2,2,128,256]{4,3,2,1,0:T(8,128)(2,1)S(1)}, bf16[2,2,2,128,256]{4,3,2,1,0:T(8,128)(2,1)S(1)}, u32[]{:S(2)}, u32[]{:S(2)}) collective-permute-start(bf16[2,2,2,128,256]{4,3,2,1,0:T(8,128)(2,1)S(1)} %get-tuple-element.31), channel_id=1, source_target_pairs={{4,0},{8,4},{12,8},{5,1},{9,5},{13,9},{6,2},{10,6},{14,10},{7,3},{... | collective-permute-start | bytes 1572872 | tf_op jit(solution)/shard_map/ppermute | solution.py:28
  34.4 0.2 head_parts.14.refs_5_
  34.7 2.3 %collective-permute-done.12.refs_4_ = bf16[2,2,128,256]{3,2,1,0:T(8,128)(2,1)S(1)} collective-permute-done((bf16[2,2,128,256]{3,2,1,0:T(8,128)(2,1)S(1)}, bf16[2,2,128,256]{3,2,1,0:T(8,128)(2,1)S(1)}, u32[]{:S(2)}, u32[]{:S(2)}) %collective-permute-start.12) | collective-permute-done | bytes 262176 | tf_op jit(solution)/shard_map/ppermute | solution.py:28
  37.0 3.5 %attention_grads.3 = (f32[2,2,2,128,256]{4,3,2,1,0:T(8,128)S(1)}, bf16[2,128,256]{2,1,0:T(8,128)(2,1)S(1)}, bf16[2,128,256]{2,1,0:T(8,128)(2,1)S(1)}, bf16[2,2,1...) custom-call(f32[2,768,256]{2,1,0:T(8,128)S(1)} %pad_maximum_fusion.refs_0_, ...), custom_call_target="tpu_custom_call" | custom-call | flops 1006632960 | bytes 4980736 | tf_op jit(solution)/shard_map/attention_grads/pallas_call | solution.py:52
  40.5 1.3 %collective-permute-start.15 = (bf16[2,2,128,256]{3,2,1,0:T(8,128)(2,1)S(1)}, bf16[2,2,128,256]{3,2,1,0:T(8,128)(2,1)S(1)}, u32[]{:S(2)}, u32[]{:S(2)}) collective-permute-start(bf16[2,2,128,256]{3,2,1,0:T(8,128)(2,1)S(1)} %get-tuple-element.41), channel_id=1, source_target_pairs={{4,0},{8,4},{12,8},{5,1},{9,5},{13,9},{6,2},{10,6},{14,10},{7,3},{... | collective-permute-start | bytes 786440 | tf_op jit(solution)/shard_map/ppermute | solution.py:28
  41.8 0.6 collective-permute-start.6
  42.4 1.5 %collective-permute-start.14 = (bf16[2,128,256]{2,1,0:T(8,128)(2,1)S(1)}, bf16[2,128,256]{2,1,0:T(8,128)(2,1)S(1)}, u32[]{:S(2)}, u32[]{:S(2)}) collective-permute-start(bf16[2,128,256]{2,1,0:T(8,128)(2,1)S(1)} %get-tuple-element.38), channel_id=1, source_target_pairs={{0,2},{2,0},{1,3},{3,1},{4,6},{6,4},{5,7},{7,5},{8,10},{10,8},{9,1... | collective-permute-start | bytes 393224 | tf_op jit(solution)/shard_map/ppermute | solution.py:33
  43.9 4.1 %collective-permute-done.6.refs_1_ = bf16[2,128,256]{2,1,0:T(8,128)(2,1)S(1)} collective-permute-done((bf16[2,128,256]{2,1,0:T(8,128)(2,1)S(1)}, bf16[2,128,256]{2,1,0:T(8,128)(2,1)S(1)}, u32[]{:S(2)}, u32[]{:S(2)}) %collective-permute-start.6) | collective-permute-done | bytes 131104 | tf_op jit(solution)/shard_map/ppermute | solution.py:33
  48.0 0.1 summed.3
  48.1 0.9 %collective-permute-start.8 = (bf16[2,2,128,256]{3,2,1,0:T(8,128)(2,1)S(1)}, bf16[2,2,128,256]{3,2,1,0:T(8,128)(2,1)S(1)}, u32[]{:S(2)}, u32[]{:S(2)}) collective-permute-start(bf16[2,2,128,256]{3,2,1,0:T(8,128)(2,1)S(1)} %get-tuple-element.33), channel_id=1, source_target_pairs={{0,2},{2,0},{1,3},{3,1},{4,6},{6,4},{5,7},{7,5},{8,10},{10,8},{9,1... | collective-permute-start | bytes 786440 | tf_op jit(solution)/shard_map/ppermute | solution.py:33
  49.0 0.5 collective-permute-done.14.refs_1_
  49.4 0.7 %collective-permute-done.15.refs_0_ = bf16[2,2,128,256]{3,2,1,0:T(8,128)(2,1)S(1)} collective-permute-done((bf16[2,2,128,256]{3,2,1,0:T(8,128)(2,1)S(1)}, bf16[2,2,128,256]{3,2,1,0:T(8,128)(2,1)S(1)}, u32[]{:S(2)}, u32[]{:S(2)}) %collective-permute-start.15) | collective-permute-done | bytes 262176 | tf_op jit(solution)/shard_map/ppermute | solution.py:28
  50.2 1.3 %collective-permute-start.16 = (bf16[2,2,128,256]{3,2,1,0:T(8,128)(2,1)S(1)}, bf16[2,2,128,256]{3,2,1,0:T(8,128)(2,1)S(1)}, u32[]{:S(2)}, u32[]{:S(2)}) collective-permute-start(bf16[2,2,128,256]{3,2,1,0:T(8,128)(2,1)S(1)} %relayed.3), channel_id=1, source_target_pairs={{4,0},{8,4},{12,8},{5,1},{9,5},{13,9},{6,2},{10,6},{14,10},{7,3},{... | collective-permute-start | bytes 786440 | tf_op jit(solution)/shard_map/ppermute | solution.py:28
  51.5 1.6 %collective-permute-start.17 = (bf16[2,2,128,256]{3,2,1,0:T(8,128)(2,1)S(1)}, bf16[2,2,128,256]{3,2,1,0:T(8,128)(2,1)S(1)}, u32[]{:S(2)}, u32[]{:S(2)}) collective-permute-start(bf16[2,2,128,256]{3,2,1,0:T(8,128)(2,1)S(1)} %summed.4.refs_0_), channel_id=1, source_target_pairs={{0,2},{2,0},{1,3},{3,1},{4,6},{6,4},{5,7},{7,5},{8,10},{10,8},{9,1... | collective-permute-start | bytes 786440 | tf_op jit(solution)/shard_map/ppermute | solution.py:33
  53.1 2.9 %collective-permute-done.8.refs_3_ = bf16[2,2,128,256]{3,2,1,0:T(8,128)(2,1)S(1)} collective-permute-done((bf16[2,2,128,256]{3,2,1,0:T(8,128)(2,1)S(1)}, bf16[2,2,128,256]{3,2,1,0:T(8,128)(2,1)S(1)}, u32[]{:S(2)}, u32[]{:S(2)}) %collective-permute-start.8) | collective-permute-done | bytes 262176 | tf_op jit(solution)/shard_map/ppermute | solution.py:33
  56.0 0.1 rows_for_pair.2
  56.0 0.1 collective-permute-start.18
  56.1 2.5 %collective-permute-done.16.refs_0_ = bf16[2,2,128,256]{3,2,1,0:T(8,128)(2,1)S(1)} collective-permute-done((bf16[2,2,128,256]{3,2,1,0:T(8,128)(2,1)S(1)}, bf16[2,2,128,256]{3,2,1,0:T(8,128)(2,1)S(1)}, u32[]{:S(2)}, u32[]{:S(2)}) %collective-permute-start.16) | collective-permute-done | bytes 262176 | tf_op jit(solution)/shard_map/ppermute | solution.py:28
  58.7 0.1 collective-permute-done.17.refs_3_
  58.9 0.1 collective-permute-start.19
  58.9 1.7 %collective-permute-done.19.refs_3_ = bf16[3,2,128,256]{3,2,1,0:T(8,128)(2,1)S(1)} collective-permute-done((bf16[3,2,128,256]{3,2,1,0:T(8,128)(2,1)S(1)}, bf16[3,2,128,256]{3,2,1,0:T(8,128)(2,1)S(1)}, u32[]{:S(2)}, u32[]{:S(2)}) %collective-permute-start.19) | collective-permute-done | bytes 393248 | tf_op jit(solution)/shard_map/ppermute | solution.py:37
  60.6 1.3 %laid_out.1 = (bf16[128,2048]{1,0:T(8,128)(2,1)}, bf16[128,2048]{1,0:T(8,128)(2,1)}, bf16[128,2048]{1,0:T(8,128)(2,1)}) custom-call(bf16[3,2,128,256]{3,2,1,0:T(8,128)(2,1)S(1)} %get-tuple-element.34.refs_0_, bf16[3,2,128,256]{3,2,1,0:T(8,128)(2,1)S(1)} %get-tuple-element.42.refs_1_, bf16[3,2,128,256]{3,2,1,0:T(8,128)(2,1)S(1)} %collective-permute-done.18.refs_2_, ...), custom_call_target="tpu_custom_call" | custom-call | bytes 3145728 | tf_op jit(solution)/shard_map/laid_out/pallas_call | solution.py:52
  (23 shorter events, 0.3 us)
Async XLA Ops:
  1.8 2.9 %collective-permute-start = (bf16[2,2,128,256]{3,2,1,0:T(8,128)(2,1)S(1)}, bf16[2,2,128,256]{3,2,1,0:T(8,128)(2,1)S(1)}, u32[]{:S(2)}, u32[]{:S(2)}) collective-permute-start(bf16[2,2,128,256]{3,2,1,0:T(8,128)(2,1)S(1)} %get-tuple-element.25), channel_id=1, source_target_pairs={{0,1},{1,0},{2,3},{3,2},{4,5},{5,4},{6,7},{7,6},{8,9},{9,8},{10,11... | collective-permute-start | bytes 786440 | tf_op jit(solution)/shard_map/ppermute | solution.py:37
  2.3 2.3 %copy-start = (s32[2048]{0:T(1024)S(1)}, s32[2048]{0:T(1024)}, u32[]{:S(2)}) copy-start(s32[2048]{0:T(1024)} %param.9) | copy-start | bytes 24580
  3.9 5.3 %collective-permute-start.4 = (bf16[2,2,128,256]{3,2,1,0:T(8,128)(2,1)S(1)}, bf16[2,2,128,256]{3,2,1,0:T(8,128)(2,1)S(1)}, u32[]{:S(2)}, u32[]{:S(2)}) collective-permute-start(bf16[2,2,128,256]{3,2,1,0:T(8,128)(2,1)S(1)} %get-tuple-element.27), channel_id=1, source_target_pairs={{0,1},{1,0},{2,3},{3,2},{4,5},{5,4},{6,7},{7,6},{8,9},{9,8},{10,11... | collective-permute-start | bytes 786440 | tf_op jit(solution)/shard_map/ppermute | solution.py:37
  4.1 10.6 %collective-permute-start.9 = (bf16[4,2,128,256]{3,2,1,0:T(8,128)(2,1)S(1)}, bf16[4,2,128,256]{3,2,1,0:T(8,128)(2,1)S(1)}, u32[]{:S(2)}, u32[]{:S(2)}) collective-permute-start(bf16[4,2,128,256]{3,2,1,0:T(8,128)(2,1)S(1)} %get-tuple-element.36), channel_id=1, source_target_pairs={{0,1},{1,0},{2,3},{3,2},{4,5},{5,4},{6,7},{7,6},{8,9},{9,8},{10,11... | collective-permute-start | bytes 1572872 | tf_op jit(solution)/shard_map/ppermute | solution.py:37
  4.8 9.8 %collective-permute-start.1 = (bf16[2,2,128,256]{3,2,1,0:T(8,128)(2,1)S(1)}, bf16[2,2,128,256]{3,2,1,0:T(8,128)(2,1)S(1)}, u32[]{:S(2)}, u32[]{:S(2)}) collective-permute-start(bf16[2,2,128,256]{3,2,1,0:T(8,128)(2,1)S(1)} %head_parts.9), channel_id=1, source_target_pairs={{0,2},{2,0},{1,3},{3,1},{4,6},{6,4},{5,7},{7,5},{8,10},{10,8},{9,1... | collective-permute-start | bytes 786440 | tf_op jit(solution)/shard_map/ppermute | solution.py:33
  7.7 11.7 %collective-permute-start.2 = (bf16[2,2,128,256]{3,2,1,0:T(8,128)(2,1)S(1)}, bf16[2,2,128,256]{3,2,1,0:T(8,128)(2,1)S(1)}, u32[]{:S(2)}, u32[]{:S(2)}) collective-permute-start(bf16[2,2,128,256]{3,2,1,0:T(8,128)(2,1)S(1)} %head_parts.8.refs_1_), channel_id=1, source_target_pairs={{0,4},{4,8},{8,12},{12,0},{1,5},{5,9},{9,13},{13,1},{2,6},{6,10},{... | collective-permute-start | bytes 786440 | tf_op jit(solution)/shard_map/ppermute | solution.py:28
  9.5 11.8 %collective-permute-start.5 = (bf16[2,2,128,256]{3,2,1,0:T(8,128)(2,1)S(1)}, bf16[2,2,128,256]{3,2,1,0:T(8,128)(2,1)S(1)}, u32[]{:S(2)}, u32[]{:S(2)}) collective-permute-start(bf16[2,2,128,256]{3,2,1,0:T(8,128)(2,1)S(1)} %head_parts.11), channel_id=1, source_target_pairs={{0,2},{2,0},{1,3},{3,1},{4,6},{6,4},{5,7},{7,5},{8,10},{10,8},{9,1... | collective-permute-start | bytes 786440 | tf_op jit(solution)/shard_map/ppermute | solution.py:33
  14.8 16.6 %collective-permute-start.10 = (bf16[2,2,128,256]{3,2,1,0:T(8,128)(2,1)S(1)}, bf16[2,2,128,256]{3,2,1,0:T(8,128)(2,1)S(1)}, u32[]{:S(2)}, u32[]{:S(2)}) collective-permute-start(bf16[2,2,128,256]{3,2,1,0:T(8,128)(2,1)S(1)} %head_parts.13), channel_id=1, source_target_pairs={{0,2},{2,0},{1,3},{3,1},{4,6},{6,4},{5,7},{7,5},{8,10},{10,8},{9,1... | collective-permute-start | bytes 786440 | tf_op jit(solution)/shard_map/ppermute | solution.py:33
  16.8 11.0 %collective-permute-start.3 = (bf16[2,2,128,256]{3,2,1,0:T(8,128)(2,1)S(1)}, bf16[2,2,128,256]{3,2,1,0:T(8,128)(2,1)S(1)}, u32[]{:S(2)}, u32[]{:S(2)}) collective-permute-start(bf16[2,2,128,256]{3,2,1,0:T(8,128)(2,1)S(1)} %collective-permute-done.1.refs_2_.refs_0_), channel_id=1, source_target_pairs={{0,4},{4,8},{8,12},{12,0},{1,5},{5,9},{9,13},{13,1},{2,6},{6,10},{... | collective-permute-start | bytes 786440 | tf_op jit(solution)/shard_map/ppermute | solution.py:28
  19.6 15.0 %collective-permute-start.11 = (bf16[2,2,128,256]{3,2,1,0:T(8,128)(2,1)S(1)}, bf16[2,2,128,256]{3,2,1,0:T(8,128)(2,1)S(1)}, u32[]{:S(2)}, u32[]{:S(2)}) collective-permute-start(bf16[2,2,128,256]{3,2,1,0:T(8,128)(2,1)S(1)} %head_parts.12.refs_1_), channel_id=1, source_target_pairs={{0,4},{4,8},{8,12},{12,0},{1,5},{5,9},{9,13},{13,1},{2,6},{6,10},{... | collective-permute-start | bytes 786440 | tf_op jit(solution)/shard_map/ppermute | solution.py:28
  21.4 13.2 %collective-permute-start.13 = (bf16[2,2,128,256]{3,2,1,0:T(8,128)(2,1)S(1)}, bf16[2,2,128,256]{3,2,1,0:T(8,128)(2,1)S(1)}, u32[]{:S(2)}, u32[]{:S(2)}) collective-permute-start(bf16[2,2,128,256]{3,2,1,0:T(8,128)(2,1)S(1)} %head_parts.15), channel_id=1, source_target_pairs={{0,2},{2,0},{1,3},{3,1},{4,6},{6,4},{5,7},{7,5},{8,10},{10,8},{9,1... | collective-permute-start | bytes 786440 | tf_op jit(solution)/shard_map/ppermute | solution.py:33
  31.4 5.6 %collective-permute-start.12 = (bf16[2,2,128,256]{3,2,1,0:T(8,128)(2,1)S(1)}, bf16[2,2,128,256]{3,2,1,0:T(8,128)(2,1)S(1)}, u32[]{:S(2)}, u32[]{:S(2)}) collective-permute-start(bf16[2,2,128,256]{3,2,1,0:T(8,128)(2,1)S(1)} %relayed.2), channel_id=1, source_target_pairs={{0,4},{4,8},{8,12},{1,5},{5,9},{9,13},{2,6},{6,10},{10,14},{3,7},{... | collective-permute-start | bytes 786440 | tf_op jit(solution)/shard_map/ppermute | solution.py:28
  33.1 14.9 %collective-permute-start.7 = (bf16[2,2,2,128,256]{4,3,2,1,0:T(8,128)(2,1)S(1)}, bf16[2,2,2,128,256]{4,3,2,1,0:T(8,128)(2,1)S(1)}, u32[]{:S(2)}, u32[]{:S(2)}) collective-permute-start(bf16[2,2,2,128,256]{4,3,2,1,0:T(8,128)(2,1)S(1)} %get-tuple-element.31), channel_id=1, source_target_pairs={{4,0},{8,4},{12,8},{5,1},{9,5},{13,9},{6,2},{10,6},{14,10},{7,3},{... | collective-permute-start | bytes 1572872 | tf_op jit(solution)/shard_map/ppermute | solution.py:28
  40.5 9.6 %collective-permute-start.15 = (bf16[2,2,128,256]{3,2,1,0:T(8,128)(2,1)S(1)}, bf16[2,2,128,256]{3,2,1,0:T(8,128)(2,1)S(1)}, u32[]{:S(2)}, u32[]{:S(2)}) collective-permute-start(bf16[2,2,128,256]{3,2,1,0:T(8,128)(2,1)S(1)} %get-tuple-element.41), channel_id=1, source_target_pairs={{4,0},{8,4},{12,8},{5,1},{9,5},{13,9},{6,2},{10,6},{14,10},{7,3},{... | collective-permute-start | bytes 786440 | tf_op jit(solution)/shard_map/ppermute | solution.py:28
  41.8 6.2 %collective-permute-start.6 = (bf16[2,128,256]{2,1,0:T(8,128)(2,1)S(1)}, bf16[2,128,256]{2,1,0:T(8,128)(2,1)S(1)}, u32[]{:S(2)}, u32[]{:S(2)}) collective-permute-start(bf16[2,128,256]{2,1,0:T(8,128)(2,1)S(1)} %get-tuple-element.29), channel_id=1, source_target_pairs={{0,2},{2,0},{1,3},{3,1},{4,6},{6,4},{5,7},{7,5},{8,10},{10,8},{9,1... | collective-permute-start | bytes 393224 | tf_op jit(solution)/shard_map/ppermute | solution.py:33
  42.4 7.0 %collective-permute-start.14 = (bf16[2,128,256]{2,1,0:T(8,128)(2,1)S(1)}, bf16[2,128,256]{2,1,0:T(8,128)(2,1)S(1)}, u32[]{:S(2)}, u32[]{:S(2)}) collective-permute-start(bf16[2,128,256]{2,1,0:T(8,128)(2,1)S(1)} %get-tuple-element.38), channel_id=1, source_target_pairs={{0,2},{2,0},{1,3},{3,1},{4,6},{6,4},{5,7},{7,5},{8,10},{10,8},{9,1... | collective-permute-start | bytes 393224 | tf_op jit(solution)/shard_map/ppermute | solution.py:33
  48.1 7.9 %collective-permute-start.8 = (bf16[2,2,128,256]{3,2,1,0:T(8,128)(2,1)S(1)}, bf16[2,2,128,256]{3,2,1,0:T(8,128)(2,1)S(1)}, u32[]{:S(2)}, u32[]{:S(2)}) collective-permute-start(bf16[2,2,128,256]{3,2,1,0:T(8,128)(2,1)S(1)} %get-tuple-element.33), channel_id=1, source_target_pairs={{0,2},{2,0},{1,3},{3,1},{4,6},{6,4},{5,7},{7,5},{8,10},{10,8},{9,1... | collective-permute-start | bytes 786440 | tf_op jit(solution)/shard_map/ppermute | solution.py:33
  50.2 8.4 %collective-permute-start.16 = (bf16[2,2,128,256]{3,2,1,0:T(8,128)(2,1)S(1)}, bf16[2,2,128,256]{3,2,1,0:T(8,128)(2,1)S(1)}, u32[]{:S(2)}, u32[]{:S(2)}) collective-permute-start(bf16[2,2,128,256]{3,2,1,0:T(8,128)(2,1)S(1)} %relayed.3), channel_id=1, source_target_pairs={{4,0},{8,4},{12,8},{5,1},{9,5},{13,9},{6,2},{10,6},{14,10},{7,3},{... | collective-permute-start | bytes 786440 | tf_op jit(solution)/shard_map/ppermute | solution.py:28
  51.5 7.3 %collective-permute-start.17 = (bf16[2,2,128,256]{3,2,1,0:T(8,128)(2,1)S(1)}, bf16[2,2,128,256]{3,2,1,0:T(8,128)(2,1)S(1)}, u32[]{:S(2)}, u32[]{:S(2)}) collective-permute-start(bf16[2,2,128,256]{3,2,1,0:T(8,128)(2,1)S(1)} %summed.4.refs_0_), channel_id=1, source_target_pairs={{0,2},{2,0},{1,3},{3,1},{4,6},{6,4},{5,7},{7,5},{8,10},{10,8},{9,1... | collective-permute-start | bytes 786440 | tf_op jit(solution)/shard_map/ppermute | solution.py:33
  56.0 2.9 %collective-permute-start.18 = (bf16[3,2,128,256]{3,2,1,0:T(8,128)(2,1)S(1)}, bf16[3,2,128,256]{3,2,1,0:T(8,128)(2,1)S(1)}, u32[]{:S(2)}, u32[]{:S(2)}) collective-permute-start(bf16[3,2,128,256]{3,2,1,0:T(8,128)(2,1)S(1)} %get-tuple-element.43), channel_id=1, source_target_pairs={{0,1},{1,0},{2,3},{3,2},{4,5},{5,4},{6,7},{7,6},{8,9},{9,8},{10,11... | collective-permute-start | bytes 1179656 | tf_op jit(solution)/shard_map/ppermute | solution.py:37
  58.9 1.8 %collective-permute-start.19 = (bf16[3,2,128,256]{3,2,1,0:T(8,128)(2,1)S(1)}, bf16[3,2,128,256]{3,2,1,0:T(8,128)(2,1)S(1)}, u32[]{:S(2)}, u32[]{:S(2)}) collective-permute-start(bf16[3,2,128,256]{3,2,1,0:T(8,128)(2,1)S(1)} %get-tuple-element.44), channel_id=1, source_target_pairs={{0,1},{1,0},{2,3},{3,2},{4,5},{5,4},{6,7},{7,6},{8,9},{9,8},{10,11... | collective-permute-start | bytes 1179656 | tf_op jit(solution)/shard_map/ppermute | solution.py:37
